TPU v7x, 32 devices: a whole 2x2x4 slice. The times are simulated.
32 devices in a mesh: section: 4 (over y, x), dp: 4 (over z), cores: 2 (over core).
Axes of the slice: x: 2, y: 2, z: 4, core: 2. Of those that a mesh axis runs over, the one named last changes fastest.
Arguments:
- arrivals: bfloat16 [2, 384, 2048], P(None, 'dp'), may hold values from -6 to 6
- in_flight: bfloat16 [4, 384, 2048], P('section', 'dp'), may hold values from -6 to 6
- cotangent: bfloat16 [2, 384, 2048], P(None, 'dp'), may hold values from -6 to 6
- grad_flight: bfloat16 [4, 384, 2048], P('section', 'dp'), may hold values from -6 to 6
- stashed: bfloat16 [4, 2, 384, 2048], P('section', None, 'dp'), may hold values from -6 to 6
- in_weight: bfloat16 [4, 2048, 4096], P('section', 'dp', 'cores'), may hold values from -0.125 to 0.125
- out_weight: bfloat16 [4, 1024, 2048], P('section', 'cores', 'dp'), may hold values from -0.1875 to 0.1875
- forward_blocks: int32 [4, 5], P('dp'), may hold values from 1 to 4, 12 in all within a row
- backward_blocks: int32 [4, 5], P('dp'), may hold values from 1 to 4, 12 in all within a row
- forward_marks: int32 [4, 5, 4, 4], P('dp'), may hold values 0 or 1
- backward_marks: int32 [4, 5, 4, 4], P('dp'), may hold values 0 or 1
Outputs:
- activations: bfloat16 [4, 2, 384, 2048], P('section', None, ('dp', 'cores'))
- input_grads: bfloat16 [4, 2, 384, 2048], P('section', None, ('dp', 'cores'))
- weight_grads: float32 [4, 1024, 2048], P('section', 'cores', 'dp')
Inputs may be any that keep to these rules, and one draw needn't show every extreme that they name: `forward_blocks`: in each replica's row the 5 lengths add up to 12 blocks and the longest is 4. `backward_blocks`: in each replica's row the 5 lengths add up to 12 blocks and the longest is 4.
All inputs are finite; a program needn't handle non-finite values. No bound on the sum of `forward_marks` or of `backward_marks` on one device may be relied on, other than what follows from the above.
Results may differ from a plain program's by a relative error of at most 0.03.
Values may be sent and summed in bfloat16 or wider, within the bound.
No kernel may reach another device: no remote copies, remote signals or barrier semaphores. Data moves between devices by JAX's collectives and lax.ppermute only.
A program may use at most 64 MiB of HBM per device.

v0:
```python
import jax
import jax.numpy as jnp
from jax import lax
from jax.sharding import PartitionSpec as P

HEAD_DIM = 128
BLOCK = 24
BLOCKS = 4


EPSILON = 1e-06


def from_behind(x, axis, by):
    peers = lax.axis_size(axis)
    pairs = [(i, i + by) for i in range(peers) if 0 <= i + by < peers]
    return lax.ppermute(x, axis, pairs)


def block_keep(live_blocks, block_marks):
    length = BLOCKS * BLOCK
    places = jnp.arange(length, dtype=jnp.int32)
    owners = places // BLOCK
    onehot = (owners[:, None] == jnp.arange(BLOCKS, dtype=jnp.int32)[None, :]).astype(jnp.float32)
    spread = jnp.einsum("ia,rab,jb->rij", onehot, block_marks.astype(jnp.float32), onehot)
    allowed = (owners[:, None] == owners[None, :])[None] | (spread > 0.5)
    causal = (places[:, None] >= places[None, :])[None]
    tokens_live = live_blocks * BLOCK
    living = places[None, :] < tokens_live[:, None]
    keeping = causal & allowed & living[:, :, None] & living[:, None, :]
    return (keeping.astype(jnp.float32), 1.0 / tokens_live.astype(jnp.float32))


def choose_history(block_table, mark_table, history):
    histories = block_table.shape[1]
    matches = jnp.arange(histories, dtype=jnp.int32) == history
    blocks = jnp.sum(jnp.where(matches, block_table[0], 0))
    marked = jnp.sum(jnp.where(matches[:, None, None], mark_table[0], 0), axis=0)
    return block_keep(blocks[None], marked[None])


def norm_rows(values_f):
    return lax.rsqrt(jnp.mean(values_f * values_f, axis=-1, keepdims=True) + EPSILON)


def heads_forward(pre_act, keeping, inverse_count):
    scaling = HEAD_DIM ** (-0.5)
    active = jax.nn.silu(pre_act)
    gate_rows = active[:, :, :, 0]
    value_rows = active[:, :, :, 1].astype(jnp.bfloat16)
    query_rows = active[:, :, :, 2].astype(jnp.bfloat16)
    key_rows = active[:, :, :, 3].astype(jnp.bfloat16)
    scores = (
        jnp.einsum("rigd,rjgd->rgij", query_rows, key_rows, preferred_element_type=jnp.float32)
        * scaling
    )
    weights = keeping[:, None] * inverse_count[:, None, None, None]
    attention = (jax.nn.silu(scores) * weights).astype(jnp.bfloat16)
    mixed = jnp.einsum("rgij,rjgd->rigd", attention, value_rows, preferred_element_type=jnp.float32)
    root_scale = lax.rsqrt(jnp.mean(mixed * mixed, axis=-1, keepdims=True) + EPSILON)
    normed = mixed * root_scale
    gated = (normed * gate_rows).astype(jnp.bfloat16)
    return (
        gated,
        (
            gate_rows,
            value_rows,
            query_rows,
            key_rows,
            scores,
            weights,
            attention,
            root_scale,
            normed,
        ),
    )


def heads_backward(pre_act, saved, upstream):
    gate_rows, value_rows, query_rows, key_rows, scores, weights, attention, root_scale, normed = (
        saved
    )
    scaling = HEAD_DIM ** (-0.5)
    grad_gated = upstream.astype(jnp.float32)
    grad_normed = grad_gated * gate_rows
    grad_gate = grad_gated * normed
    grad_mixed = root_scale * (
        grad_normed - normed * jnp.mean(grad_normed * normed, axis=-1, keepdims=True)
    )
    mixed_low = grad_mixed.astype(jnp.bfloat16)
    grad_attention = jnp.einsum(
        "rigd,rjgd->rgij", mixed_low, value_rows, preferred_element_type=jnp.float32
    )
    grad_value = jnp.einsum(
        "rgij,rigd->rjgd", attention, mixed_low, preferred_element_type=jnp.float32
    )
    sigmoid_s = jax.nn.sigmoid(scores)
    grad_scores = (
        grad_attention * weights * sigmoid_s * (1.0 + scores * (1.0 - sigmoid_s)) * scaling
    ).astype(jnp.bfloat16)
    grad_query = jnp.einsum(
        "rgij,rjgd->rigd", grad_scores, key_rows, preferred_element_type=jnp.float32
    )
    grad_key = jnp.einsum(
        "rgij,rigd->rjgd", grad_scores, query_rows, preferred_element_type=jnp.float32
    )
    grad_active = jnp.stack([grad_gate, grad_value, grad_query, grad_key], axis=3)
    sigmoid_u = jax.nn.sigmoid(pre_act)
    return (grad_active * sigmoid_u * (1.0 + pre_act * (1.0 - sigmoid_u))).astype(jnp.bfloat16)


def per_device(
    arrivals,
    in_flight,
    cotangent,
    grad_flight,
    stashed,
    in_weight,
    out_weight,
    forward_blocks,
    backward_blocks,
    forward_marks,
    backward_marks,
):
    section_no = lax.axis_index("section")
    sections = lax.axis_size("section")
    core_no = lax.axis_index("cores")
    ticks = arrivals.shape[0]
    length = arrivals.shape[1]
    share = length // lax.axis_size("cores")
    row_start = core_no * share
    out_full = lax.all_gather(out_weight[0], "dp", axis=1, tiled=True)
    slab_rows = out_full.shape[0]
    groups = slab_rows // HEAD_DIM
    columns = in_weight.shape[2]
    in_full = None
    in_full = lax.all_gather(in_weight[0], "dp", axis=0, tiled=True)
    received = in_flight[0]
    returned = grad_flight[0]
    ahead_out = []
    back_out = []
    gated_list = []
    upstream_list = []
    for tick_no in range(ticks):
        if tick_no == 0:
            prior = in_flight[0]
            later = grad_flight[0]
        else:
            prior = received
            later = returned
        inputs = jnp.where(section_no == 0, arrivals[tick_no], prior)
        upstream = jnp.where(section_no == sections - 1, cotangent[tick_no], later)
        keep_ahead, count_ahead = choose_history(
            forward_blocks, forward_marks, tick_no - section_no + sections - 1
        )
        keep_back, count_back = choose_history(
            backward_blocks, backward_marks, tick_no + section_no
        )
        floats = inputs.astype(jnp.float32)
        saved_floats = stashed[0, tick_no].astype(jnp.float32)
        root_saved = norm_rows(saved_floats)
        scaled_saved = saved_floats * root_saved
        both_normed = jnp.concatenate(
            [(floats * norm_rows(floats)).astype(jnp.bfloat16), scaled_saved.astype(jnp.bfloat16)],
            axis=0,
        )
        pre_both = jnp.dot(both_normed, in_full, preferred_element_type=jnp.float32)
        pre_ahead = pre_both[:length].reshape(1, length, groups, 4, HEAD_DIM)
        pre_back = pre_both[length:].reshape(1, length, groups, 4, HEAD_DIM)
        gated_ahead, unused = heads_forward(pre_ahead, keep_ahead, count_ahead)
        partial_sum = jnp.dot(
            gated_ahead.reshape(length, slab_rows), out_full, preferred_element_type=jnp.float32
        )
        summed = lax.psum(partial_sum.astype(jnp.bfloat16), "cores").astype(jnp.float32)
        outgoing = (floats + summed).astype(jnp.bfloat16)
        ahead_out.append(lax.dynamic_slice_in_dim(outgoing, row_start, share, 0))
        if tick_no + 1 < ticks:
            received = from_behind(outgoing, "section", 1)
        gated_back, saved = heads_forward(pre_back, keep_back, count_back)
        grad_gated = (
            jnp.einsum("sd,fd->sf", upstream, out_full, preferred_element_type=jnp.float32)
            .astype(jnp.bfloat16)
            .reshape(1, length, groups, HEAD_DIM)
        )
        grad_pre = heads_backward(pre_back, saved, grad_gated).reshape(length, columns)
        grad_normed = jnp.einsum("sf,df->sd", grad_pre, in_full, preferred_element_type=jnp.float32)
        back_part = root_saved * (
            grad_normed
            - scaled_saved * jnp.mean(grad_normed * scaled_saved, axis=-1, keepdims=True)
        )
        back_sum = lax.psum(back_part.astype(jnp.bfloat16), "cores").astype(jnp.float32)
        grad_in = (upstream.astype(jnp.float32) + back_sum).astype(jnp.bfloat16)
        back_out.append(lax.dynamic_slice_in_dim(grad_in, row_start, share, 0))
        gated_list.append(gated_back.reshape(length, slab_rows))
        upstream_list.append(upstream)
        if tick_no + 1 < ticks:
            returned = from_behind(grad_in, "section", -1)
    stacked_gated = jnp.concatenate(gated_list, axis=0)
    stacked_upstream = jnp.concatenate(upstream_list, axis=0)
    product = lax.dot_general(
        stacked_gated,
        stacked_upstream,
        (((0,), (0,)), ((), ())),
        preferred_element_type=jnp.float32,
    )
    scaling = (ticks * length * lax.axis_size("dp")) ** (-0.5)
    grads_sum = (
        lax.psum_scatter(
            product.astype(jnp.bfloat16), "dp", scatter_dimension=1, tiled=True
        ).astype(jnp.float32)
        * scaling
    )
    return (jnp.stack(ahead_out)[None], jnp.stack(back_out)[None], grads_sum[None])


def solution(mesh):
    in_specs = (
        P(None, "dp", None),
        P("section", "dp", None),
        P(None, "dp", None),
        P("section", "dp", None),
        P("section", None, "dp", None),
        P("section", "dp", "cores"),
        P("section", "cores", "dp"),
        P("dp", None),
        P("dp", None),
        P("dp", None, None, None),
        P("dp", None, None, None),
    )
    out_specs = (
        P("section", None, ("dp", "cores"), None),
        P("section", None, ("dp", "cores"), None),
        P("section", "cores", "dp"),
    )
    return jax.shard_map(
        per_device, mesh=mesh, in_specs=in_specs, out_specs=out_specs, check_vma=False
    )
```

profile of v0, /device:TPU:5, one launch (start us, length us, event | category | flops | bytes accessed | tf_op | source)
XLA Modules:
  0.0 391.2 jit_solution(10865271771457832967)
XLA Ops:
  13.9 1.9 fusion.38
  15.8 1.9 fusion.48
  17.9 38.9 %all-gather.7.cloned.1.call-done = bf16[1,512,2048]{2,1,0:T(8,128)(2,1)} async-done(((bf16[1,512,512]{2,1,0:T(8,128)(2,1)}), bf16[1,512,2048]{2,1,0:T(8,128)(2,1)}) %all-gather.7.cloned.1.call-update) | async-done | bytes 2097168 | tf_op jit(solution)/shard_map/all_gather | solution.py:132
  56.8 2.4 fusion.31
  59.9 147.4 %all-gather.5.cloned.1.call-done = bf16[1,2048,2048]{2,1,0:T(8,128)(2,1)} async-done(((bf16[1,512,2048]{2,1,0:T(8,128)(2,1)}), bf16[1,2048,2048]{2,1,0:T(8,128)(2,1)}) %all-gather.5.cloned.1.call-update) | async-done | bytes 8388624 | tf_op jit(solution)/shard_map/all_gather | solution.py:137
  207.3 5.2 %fusion.6 = f32[192,2048]{1,0:T(8,128)S(1)} fusion(bf16[1,2048,2048]{2,1,0:T(8,128)(2,1)} %all-gather.5.cloned.1.call-done, bf16[96,2048]{1,0:T(8,128)(2,1)S(1)} %get-tuple-element.54, bf16[96,2048]{1,0:T(8,128)(2,1)S(1)} %get-tuple-element.55), kind=kOutput, calls=%fused_computation.6 | convolution fusion | flops 1612185600 | bytes 10747904 | tf_op jit(solution)/shard_map/dot_general | solution.py:167
  221.3 1.4 pad_maximum_fusion
  223.2 1.2 stack.60
  224.4 6.5 %fusion.68 = (f32[96]{0:T(128)S(1)}, f32[96]{0:T(128)S(1)}, f32[96,2048]{1,0:T(8,128)S(1)}) fusion(f32[96]{0:T(128)S(1)} %add_rsqrt_fusion.6, bf16[1,2,96,2048]{3,2,1,0:T(8,128)(2,1)S(1)} %copy-done.1, bf16[1,2048,2048]{2,1,0:T(8,128)(2,1)} %all-gather.5.cloned.1.call-done, f32[96,2048]{1,0:T(8,128)} %stack.60, f32[192,2048]{1,0:T(8,128)S(1)} %copy-done.10), kind=kOutput, calls=%fused_computation.87 | convolution fusion | flops 808451840 | bytes 11535616 | tf_op jit(solution)/shard_map/sf,df->sd/dot_general | solution.py:186
  232.8 1.2 convolution_convert_fusion.2
  236.3 15.9 %all-reduce.7.cloned.1.call-done = (bf16[96,2048]{1,0:T(8,128)(2,1)}, bf16[96,2048]{1,0:T(8,128)(2,1)}) async-done(((bf16[96,2048]{1,0:T(8,128)(2,1)}, bf16[96,2048]{1,0:T(8,128)(2,1)}), (bf16[96,2048]{1,0:T(8,128)(2,1)}, bf16[96,2048]{1,0:T(8,128)(2,1)})) %all-reduce.7.cloned.1.call-update) | async-done | bytes 786448 | tf_op jit(solution)/shard_map/psum | solution.py:174
  253.4 3.2 collective-permute-start
  256.6 1.8 add_convert_fusion
  258.5 3.3 collective-permute-start.1
  261.7 5.1 %collective-permute-done = bf16[96,2048]{1,0:T(8,128)(2,1)S(1)} collective-permute-done((bf16[96,2048]{1,0:T(8,128)(2,1)S(1)}, bf16[96,2048]{1,0:T(8,128)(2,1)S(1)}, u32[]{:S(2)}, u32[]{:S(2)}) %collective-permute-start) | collective-permute-done | bytes 393248 | tf_op jit(solution)/shard_map/ppermute | solution.py:17
  267.2 5.2 %fusion.4 = f32[192,2048]{1,0:T(8,128)S(1)} fusion(bf16[1,2048,2048]{2,1,0:T(8,128)(2,1)} %all-gather.5.cloned.1.call-done, bf16[96,2048]{1,0:T(8,128)(2,1)S(1)} %copy-done.22, bf16[96,2048]{1,0:T(8,128)(2,1)S(1)} %multiply_convert_fusion.2), kind=kOutput, calls=%fused_computation.4 | convolution fusion | flops 1612185600 | bytes 10747904 | tf_op jit(solution)/shard_map/dot_general | solution.py:167
  273.6 1.3 fusion.157
  274.9 2.6 reshape.826
  277.4 2.4 fusion.152
  282.7 1.4 fusion.28
  285.2 1.9 multiply_convert_fusion.5
  292.2 2.5 reshape.822
  294.8 2.5 fusion.153
  297.3 2.0 multiply_reduce_fusion.5
  302.3 1.4 copy.45
  303.7 2.4 stack.67
  306.0 6.8 %fusion.73 = (f32[96]{0:T(128)S(1)}, f32[96,2048]{1,0:T(8,128)S(1)}) fusion(f32[96]{0:T(128)S(1)} %add_rsqrt_fusion.4, bf16[1,2,96,2048]{3,2,1,0:T(8,128)(2,1)} %param.15, bf16[1,2048,2048]{2,1,0:T(8,128)(2,1)} %all-gather.5.cloned.1.call-done, f32[96,2048]{1,0:T(8,128)} %stack.67, f32[192,2048]{1,0:T(8,128)} %copy-done.8), kind=kOutput, calls=%fused_computation.92 | convolution fusion | flops 807862144 | bytes 11141888 | tf_op jit(solution)/shard_map/sf,df->sd/dot_general | solution.py:186
  313.8 1.2 convolution_convert_fusion.1
  315.3 3.1 convolution_convert_fusion
  319.5 16.7 %all-reduce.5.cloned.1.call-done = (bf16[96,2048]{1,0:T(8,128)(2,1)}, bf16[96,2048]{1,0:T(8,128)(2,1)}) async-done(((bf16[96,2048]{1,0:T(8,128)(2,1)}, bf16[96,2048]{1,0:T(8,128)(2,1)}), (bf16[96,2048]{1,0:T(8,128)(2,1)}, bf16[96,2048]{1,0:T(8,128)(2,1)})) %all-reduce.5.cloned.1.call-update) | async-done | bytes 786448 | tf_op jit(solution)/shard_map/psum | solution.py:174
  339.7 42.8 %reduce-scatter.2.cloned.1.call-done = bf16[512,512]{1,0:T(8,128)(2,1)} async-done(((bf16[512,2048]{1,0:T(8,128)(2,1)}), bf16[512,512]{1,0:T(8,128)(2,1)}) %reduce-scatter.2.cloned.1.call-update) | async-done | bytes 524304 | tf_op jit(solution)/shard_map/reduce_scatter | solution.py:208
  382.5 2.2 multiply_bitcast_fusion
  (160 shorter events, 38.6 us)
Async XLA Ops:
  7.2 5.3 %copy-start.29 = (s32[1,5,4,4]{1,3,2,0:T(4,128)S(1)}, s32[1,5,4,4]{1,3,2,0:T(4,128)}, u32[]{:S(2)}) copy-start(s32[1,5,4,4]{1,3,2,0:T(4,128)} %param.20) | copy-start | bytes 964
  7.2 5.5 %copy-start.30 = (s32[1,5,4,4]{1,3,2,0:T(4,128)S(1)}, s32[1,5,4,4]{1,3,2,0:T(4,128)}, u32[]{:S(2)}) copy-start(s32[1,5,4,4]{1,3,2,0:T(4,128)} %param.21) | copy-start | bytes 964
  7.2 6.3 %copy-start.1 = (bf16[1,2,96,2048]{3,2,1,0:T(8,128)(2,1)S(1)}, bf16[1,2,96,2048]{3,2,1,0:T(8,128)(2,1)}, u32[]{:S(2)}) copy-start(bf16[1,2,96,2048]{3,2,1,0:T(8,128)(2,1)} %param.15) | copy-start | bytes 2359300
  7.2 6.4 %copy-start.25 = (bf16[1,96,2048]{2,1,0:T(8,128)(2,1)S(1)}, bf16[1,96,2048]{2,1,0:T(8,128)(2,1)}, u32[]{:S(2)}) copy-start(bf16[1,96,2048]{2,1,0:T(8,128)(2,1)} %param.12) | copy-start | bytes 1179652
  7.2 6.4 %copy-start.16 = (bf16[2,96,2048]{2,1,0:T(8,128)(2,1)S(1)}, bf16[2,96,2048]{2,1,0:T(8,128)(2,1)}, u32[]{:S(2)}) copy-start(bf16[2,96,2048]{2,1,0:T(8,128)(2,1)} %param.11) | copy-start | bytes 2359300
  7.2 49.5 %all-gather.7.cloned.1.call-start = ((), (), s32[]{:S(2)}) async-start(), calls=%async_computation.3 | async-start | bytes 2621440 | tf_op jit(solution)/shard_map/all_gather | solution.py:132
  8.0 9.7 %copy-start.18 = (bf16[2,96,2048]{2,1,0:T(8,128)(2,1)S(1)}, bf16[2,96,2048]{2,1,0:T(8,128)(2,1)}, u32[]{:S(2)}) copy-start(bf16[2,96,2048]{2,1,0:T(8,128)(2,1)} %param.13) | copy-start | bytes 2359300
  8.0 9.7 %copy-start.26 = (bf16[1,96,2048]{2,1,0:T(8,128)(2,1)S(1)}, bf16[1,96,2048]{2,1,0:T(8,128)(2,1)}, u32[]{:S(2)}) copy-start(bf16[1,96,2048]{2,1,0:T(8,128)(2,1)} %param.14) | copy-start | bytes 1179652
  8.0 199.3 %all-gather.5.cloned.1.call-start = ((), (), s32[]{:S(2)}) async-start(), calls=%async_computation.2 | async-start | bytes 10485760 | tf_op jit(solution)/shard_map/all_gather | solution.py:137
  8.7 243.5 %all-reduce.7.cloned.1.call-start = ((), (), s32[]{:S(2)}) async-start(), calls=%async_computation.5 | async-start | bytes 1572864 | tf_op jit(solution)/shard_map/psum | solution.py:174
  13.9 45.3 %copy-start.5 = (bf16[1,96,2048]{2,1,0:T(8,128)(2,1)}, bf16[1,96,2048]{2,1,0:T(8,128)(2,1)S(1)}, u32[]{:S(2)}) copy-start(bf16[1,96,2048]{2,1,0:T(8,128)(2,1)S(1)} %get-tuple-element.28) | copy-start | bytes 1179652
  221.3 3.1 copy-start.10
  232.1 3.3 copy-start.33
  232.1 20.1 %copy-start.6 = (bf16[1,96,2048]{2,1,0:T(8,128)(2,1)S(1)}, bf16[1,96,2048]{2,1,0:T(8,128)(2,1)}, u32[]{:S(2)}) copy-start(bf16[1,96,2048]{2,1,0:T(8,128)(2,1)} %copy-done.5) | copy-start | bytes 1179652
  234.1 102.1 %all-reduce.5.cloned.1.call-start = ((), (), s32[]{:S(2)}) async-start(), calls=%async_computation.4 | async-start | bytes 1572864 | tf_op jit(solution)/shard_map/psum | solution.py:174
  236.3 43.7 %copy-start.34 = (f32[96,96]{1,0:T(8,128)}, f32[96,96]{1,0:T(8,128)S(1)}, u32[]{:S(2)}) copy-start(f32[96,96]{1,0:T(8,128)S(1)} %fusion.53) | copy-start | bytes 110596
  252.2 14.6 %copy-start.17 = (bf16[2,96,2048]{2,1,0:T(8,128)(2,1)S(1)}, bf16[2,96,2048]{2,1,0:T(8,128)(2,1)}, u32[]{:S(2)}) copy-start(bf16[2,96,2048]{2,1,0:T(8,128)(2,1)} %param.11) | copy-start | bytes 2359300
  253.4 8.4 %copy-start.13 = (bf16[96,2048]{1,0:T(8,128)(2,1)}, bf16[96,2048]{1,0:T(8,128)(2,1)S(1)}, u32[]{:S(2)}) copy-start(bf16[96,2048]{1,0:T(8,128)(2,1)S(1)} %fusion.80) | copy-start | bytes 1179652
  253.4 13.8 %copy-start.22 = (bf16[96,2048]{1,0:T(8,128)(2,1)S(1)}, bf16[96,2048]{1,0:T(8,128)(2,1)}, u32[]{:S(2)}) copy-start(bf16[96,2048]{1,0:T(8,128)(2,1)} %get-tuple-element.37) | copy-start | bytes 1179652
  253.4 13.4 %collective-permute-start = (bf16[96,2048]{1,0:T(8,128)(2,1)S(1)}, bf16[96,2048]{1,0:T(8,128)(2,1)S(1)}, u32[]{:S(2)}, u32[]{:S(2)}) collective-permute-start(bf16[96,2048]{1,0:T(8,128)(2,1)S(1)} %fusion.80), channel_id=1, source_target_pairs={{0,8},{8,16},{16,24},{1,9},{9,17},{17,25},{2,10},{10,18},{18,26},{... | collective-permute-start | bytes 1179656 | tf_op jit(solution)/shard_map/ppermute | solution.py:17
  258.5 22.4 %collective-permute-start.1 = (bf16[96,2048]{1,0:T(8,128)(2,1)}, bf16[96,2048]{1,0:T(8,128)(2,1)}, u32[]{:S(2)}, u32[]{:S(2)}) collective-permute-start(bf16[96,2048]{1,0:T(8,128)(2,1)} %add_convert_fusion), channel_id=1, source_target_pairs={{8,0},{16,8},{24,16},{9,1},{17,9},{25,17},{10,2},{18,10},{26,18},{... | collective-permute-start | bytes 1179656 | tf_op jit(solution)/shard_map/ppermute | solution.py:17
  277.4 3.5 copy-start.19
  285.2 4.4 %copy-start.12 = (bf16[1,96,4,4,128]{4,1,2,3,0:T(8,128)(2,1)S(1)}, bf16[1,96,4,4,128]{4,1,2,3,0:T(8,128)(2,1)}, u32[]{:S(2)}) copy-start(bf16[1,96,4,4,128]{4,1,2,3,0:T(8,128)(2,1)} %copy-done.11) | copy-start | bytes 1179652
  285.2 6.1 %copy-start.28 = (f32[4,96,96]{2,1,0:T(8,128)S(1)}, f32[4,96,96]{2,1,0:T(8,128)}, u32[]{:S(2)}) copy-start(f32[4,96,96]{2,1,0:T(8,128)} %copy-done.27) | copy-start | bytes 442372
  285.2 6.1 %copy-start.35 = (f32[96,96]{1,0:T(8,128)S(1)}, f32[96,96]{1,0:T(8,128)}, u32[]{:S(2)}) copy-start(f32[96,96]{1,0:T(8,128)} %copy-done.34) | copy-start | bytes 110596
  294.8 6.3 %copy-start.15 = (f32[1,96,4,1,128]{4,1,2,3,0:T(8,128)S(1)}, f32[1,96,4,1,128]{4,1,2,3,0:T(8,128)}, u32[]{:S(2)}) copy-start(f32[1,96,4,1,128]{4,1,2,3,0:T(8,128)} %get-tuple-element.39) | copy-start | bytes 589828
  306.0 6.8 %copy-start.2 = (bf16[1,2,96,2048]{3,2,1,0:T(8,128)(2,1)S(1)}, bf16[1,2,96,2048]{3,2,1,0:T(8,128)(2,1)}, u32[]{:S(2)}) copy-start(bf16[1,2,96,2048]{3,2,1,0:T(8,128)(2,1)} %param.15) | copy-start | bytes 2359300
  306.0 7.8 %copy-start.21 = (bf16[1,96,4,128]{3,2,1,0:T(4,128)(2,1)S(1)}, bf16[1,96,4,128]{3,2,1,0:T(4,128)(2,1)}, u32[]{:S(2)}) copy-start(bf16[1,96,4,128]{3,2,1,0:T(4,128)(2,1)} %copy.31) | copy-start | bytes 294916
  312.8 2.3 copy-start.23
  315.1 67.5 %reduce-scatter.2.cloned.1.call-start = ((), (), s32[]{:S(2)}) async-start(), calls=%async_computation.1 | async-start | bytes 2621440 | tf_op jit(solution)/shard_map/reduce_scatter | solution.py:208
  315.3 3.2 copy-start.14
  318.5 18.7 %copy-start.4 = (bf16[96,2048]{1,0:T(8,128)(2,1)S(1)}, bf16[96,2048]{1,0:T(8,128)(2,1)}, u32[]{:S(2)}) copy-start(bf16[96,2048]{1,0:T(8,128)(2,1)} %copy-done.3) | copy-start | bytes 1179652
  (13 other events, 17.2 us)
Sparse Core Ops, SparseCore 0:
  9.6 47.0 all-gather.6
  58.3 148.8 all-gather.4
  234.2 17.9 all-reduce.6
  315.2 20.9 all-reduce.4
  338.3 44.1 reduce-scatter.1
where the time goes:
time: 394 us; the launch traced here: 391 us
  waiting for transfers between devices  268 us (68%)
  matrix products  48.3 us (12%)
  other arithmetic  29.6 us (8%)
  local copies, waits for them, and re-layouts  21.3 us (5%)
  between operations  17.2 us (4%)
  starting transfers between devices  6.68 us (2%)
    all_gather x1, waiting for transfers between devices, per_device(): in_full = lax.all_gather(in_weight[0], 'dp', axis=0, tiled=True)  147 us
    reduce_scatter x1, waiting for transfers between devices, per_device(): lax.psum_scatter(product.astype(jnp.bfloat16), 'dp', scatter_dimension=1,...  42.8 us
    all_gather x1, waiting for transfers between devices, per_device(): out_full = lax.all_gather(out_weight[0], 'dp', axis=1, tiled=True)  38.9 us
    psum x2, waiting for transfers between devices, per_device(): lax.psum(partial_sum.astype(jnp.bfloat16), 'cores').astype(jnp.float32)  32.6 us
    dot_general x2, matrix products, per_device(): jnp.einsum('sf,df->sd', grad_pre, in_full, preferred_element_type=jnp.flo...  13.3 us
    dot_general x2, matrix products, per_device(): pre_both = jnp.dot(both_normed, in_full, preferred_element_type=jnp.float32)  10.4 us
  transfers between devices with their start and end apart: 7, of which 6 were waited for; matrix products, arithmetic and copies ran while one was open for 9% of the time, Pallas kernels for 0%

commit v1 on v0

v1 whole, which is shorter than its diff:
```python
import jax
import jax.numpy as jnp
from jax import lax
from jax.sharding import PartitionSpec as P

HEAD_DIM = 128
BLOCK = 24
BLOCKS = 4


EPSILON = 1e-06


def block_keep(live_blocks, block_marks):
    length = BLOCKS * BLOCK
    places = jnp.arange(length, dtype=jnp.int32)
    owners = places // BLOCK
    onehot = (owners[:, None] == jnp.arange(BLOCKS, dtype=jnp.int32)[None, :]).astype(jnp.float32)
    spread = jnp.einsum("ia,rab,jb->rij", onehot, block_marks.astype(jnp.float32), onehot)
    allowed = (owners[:, None] == owners[None, :])[None] | (spread > 0.5)
    causal = (places[:, None] >= places[None, :])[None]
    tokens_live = live_blocks * BLOCK
    living = places[None, :] < tokens_live[:, None]
    keeping = causal & allowed & living[:, :, None] & living[:, None, :]
    return (keeping.astype(jnp.float32), 1.0 / tokens_live.astype(jnp.float32))


def choose_history(tables, history):
    matches = jnp.arange(tables.shape[1], dtype=jnp.int32) == history
    chosen = jnp.sum(jnp.where(matches[None, :, None], tables, 0), axis=1)
    return block_keep(chosen[:, 0], chosen[:, 1:].reshape(-1, BLOCKS, BLOCKS))


def norm_rows(values_f):
    return lax.rsqrt(jnp.mean(values_f * values_f, axis=-1, keepdims=True) + EPSILON)


def heads_forward(pre_act, keeping, inverse_count):
    scaling = HEAD_DIM ** (-0.5)
    active = jax.nn.silu(pre_act)
    gate_rows = active[:, :, :, 0]
    value_rows = active[:, :, :, 1].astype(jnp.bfloat16)
    query_rows = active[:, :, :, 2].astype(jnp.bfloat16)
    key_rows = active[:, :, :, 3].astype(jnp.bfloat16)
    scores = (
        jnp.einsum("rigd,rjgd->rgij", query_rows, key_rows, preferred_element_type=jnp.float32)
        * scaling
    )
    weights = keeping[:, None] * inverse_count[:, None, None, None]
    attention = (jax.nn.silu(scores) * weights).astype(jnp.bfloat16)
    mixed = jnp.einsum("rgij,rjgd->rigd", attention, value_rows, preferred_element_type=jnp.float32)
    root_scale = lax.rsqrt(jnp.mean(mixed * mixed, axis=-1, keepdims=True) + EPSILON)
    normed = mixed * root_scale
    gated = (normed * gate_rows).astype(jnp.bfloat16)
    return (
        gated,
        (
            gate_rows,
            value_rows,
            query_rows,
            key_rows,
            scores,
            weights,
            attention,
            root_scale,
            normed,
        ),
    )


def heads_backward(pre_act, saved, upstream):
    gate_rows, value_rows, query_rows, key_rows, scores, weights, attention, root_scale, normed = (
        saved
    )
    scaling = HEAD_DIM ** (-0.5)
    grad_gated = upstream.astype(jnp.float32)
    grad_normed = grad_gated * gate_rows
    grad_gate = grad_gated * normed
    grad_mixed = root_scale * (
        grad_normed - normed * jnp.mean(grad_normed * normed, axis=-1, keepdims=True)
    )
    mixed_low = grad_mixed.astype(jnp.bfloat16)
    grad_attention = jnp.einsum(
        "rigd,rjgd->rgij", mixed_low, value_rows, preferred_element_type=jnp.float32
    )
    grad_value = jnp.einsum(
        "rgij,rigd->rjgd", attention, mixed_low, preferred_element_type=jnp.float32
    )
    sigmoid_s = jax.nn.sigmoid(scores)
    grad_scores = (
        grad_attention * weights * sigmoid_s * (1.0 + scores * (1.0 - sigmoid_s)) * scaling
    ).astype(jnp.bfloat16)
    grad_query = jnp.einsum(
        "rgij,rjgd->rigd", grad_scores, key_rows, preferred_element_type=jnp.float32
    )
    grad_key = jnp.einsum(
        "rgij,rigd->rjgd", grad_scores, query_rows, preferred_element_type=jnp.float32
    )
    grad_active = jnp.stack([grad_gate, grad_value, grad_query, grad_key], axis=3)
    sigmoid_u = jax.nn.sigmoid(pre_act)
    return (grad_active * sigmoid_u * (1.0 + pre_act * (1.0 - sigmoid_u))).astype(jnp.bfloat16)


def after(value, *earlier):
    return lax.optimization_barrier((value,) + earlier)[0]


def per_device(
    arrivals,
    in_flight,
    cotangent,
    grad_flight,
    stashed,
    in_weight,
    out_weight,
    forward_blocks,
    backward_blocks,
    forward_marks,
    backward_marks,
):
    section_no = lax.axis_index("section")
    sections = lax.axis_size("section")
    core_no = lax.axis_index("cores")
    cores = lax.axis_size("cores")
    dp_no = lax.axis_index("dp")
    dp_size = lax.axis_size("dp")
    ticks = arrivals.shape[0]
    length = arrivals.shape[1]
    width = arrivals.shape[2]
    share = length // cores
    row_start = core_no * share
    in_shard = in_weight[0]
    out_shard = out_weight[0]
    depth = in_shard.shape[0]
    slab_rows = out_shard.shape[0]
    groups = slab_rows // HEAD_DIM
    columns = in_shard.shape[1]

    hosts = [2 * k + 1 if 4 * k < dp_size - 2 else 2 * k for k in range(dp_size // 2)]
    is_host = jnp.any(dp_no == jnp.array(hosts, jnp.int32))

    def fetch(x, j):
        return lax.ppermute(x, "dp", [(h ^ j, h) for h in hosts])

    def give_back(x):
        return lax.ppermute(x, "dp", [(h, h ^ 1) for h in hosts])

    def swap_cores(x):
        return lax.ppermute(x, "cores", [(c, c ^ 1) for c in range(cores)])

    def along_sections(x, by):
        pairs = [(i, i + by) for i in range(sections) if 0 <= i + by < sections]
        return lax.ppermute(x, "section", pairs)

    first_section = section_no == 0
    last_section = section_no == sections - 1
    own = jnp.stack(
        [
            stashed[0, 0],
            stashed[0, 1],
            jnp.where(first_section, arrivals[0], in_flight[0]),
            jnp.where(last_section, cotangent[0], grad_flight[0]),
            jnp.where(first_section, arrivals[1], cotangent[1]),
        ]
    )
    tables = jnp.concatenate(
        [
            jnp.concatenate([b[..., None], m.reshape(m.shape[:2] + (-1,))], axis=-1)
            for b, m in ((forward_blocks, forward_marks), (backward_blocks, backward_marks))
        ],
        axis=0,
    )
    order = [j for j in range(dp_size - 1, 0, -1)]
    in_parts = {0: in_shard}
    out_parts = {0: out_shard}
    for j in order:
        in_parts[j] = fetch(in_shard, j)
    both = jnp.stack([own, fetch(own, 1)], axis=1)
    tables = jnp.stack([tables, fetch(tables, 1)], axis=1)
    out_late = after(out_shard, *[in_parts[j] for j in order])
    for j in order:
        out_parts[j] = fetch(out_late, j)

    def columns_of(x, j):
        return lax.dynamic_slice_in_dim(x, (dp_no ^ j) * depth, depth, axis=x.ndim - 1)

    def project(normed):
        total = 0.0
        for j in range(dp_size):
            total = total + jnp.dot(
                columns_of(normed, j), in_parts[j], preferred_element_type=jnp.float32
            )
        return total

    def by_columns(pieces):
        whole = jnp.zeros(pieces[0].shape[:-1] + (width,), pieces[0].dtype)
        for j in range(dp_size):
            whole = lax.dynamic_update_slice_in_dim(
                whole, pieces[j], (dp_no ^ j) * depth, axis=whole.ndim - 1
            )
        return whole

    def normed_of(x):
        floats = x.astype(jnp.float32)
        root = norm_rows(floats)
        scaled = floats * root
        return scaled.reshape(-1, width), root.reshape(-1, 1)

    def rows_of(x, core):
        return lax.dynamic_slice_in_dim(x, core * share, share, axis=1)

    def reduce_over_cores(part, residual):
        theirs = swap_cores(rows_of(part, 1 - core_no))
        mine = rows_of(part, core_no)
        total = (
            rows_of(residual, core_no).astype(jnp.float32)
            + mine.astype(jnp.float32)
            + theirs.astype(jnp.float32)
        )
        return total.astype(jnp.bfloat16)

    def gather_over_cores(mine):
        theirs = swap_cores(mine)
        low = jnp.where(core_no == 0, mine, theirs)
        high = jnp.where(core_no == 0, theirs, mine)
        return jnp.concatenate([low, high], axis=1)

    def forward(x, tick_no):
        keeping, count = choose_history(tables[0], tick_no - section_no + sections - 1)
        scaled, unused = normed_of(x)
        pre = project(scaled.astype(jnp.bfloat16)).reshape(2, length, groups, 4, HEAD_DIM)
        gated, unused = heads_forward(pre, keeping, count)
        gated = gated.reshape(2 * length, slab_rows)
        part = by_columns(
            [
                jnp.dot(gated, out_parts[j], preferred_element_type=jnp.float32).astype(
                    jnp.bfloat16
                )
                for j in range(dp_size)
            ]
        )
        return reduce_over_cores(part.reshape(2, length, width), x)

    def recompute(x, tick_no):
        keeping, count = choose_history(tables[1], tick_no + section_no)
        scaled, root = normed_of(x)
        pre = project(scaled.astype(jnp.bfloat16)).reshape(2, length, groups, 4, HEAD_DIM)
        gated, saved = heads_forward(pre, keeping, count)
        return gated.reshape(2 * length, slab_rows), (pre, saved, scaled, root)

    def backward(kept, upstream):
        pre, saved, scaled, root = kept
        flat = upstream.reshape(2 * length, width)
        total = 0.0
        for j in range(dp_size):
            total = total + lax.dot_general(
                columns_of(flat, j),
                out_parts[j],
                (((1,), (1,)), ((), ())),
                preferred_element_type=jnp.float32,
            )
        grad_gated = total.astype(jnp.bfloat16).reshape(2, length, groups, HEAD_DIM)
        grad_pre = heads_backward(pre, saved, grad_gated).reshape(2 * length, columns)
        grad_normed = by_columns(
            [
                lax.dot_general(
                    grad_pre,
                    in_parts[j],
                    (((1,), (1,)), ((), ())),
                    preferred_element_type=jnp.float32,
                )
                for j in range(dp_size)
            ]
        )
        part = root * (
            grad_normed - scaled * jnp.mean(grad_normed * scaled, axis=-1, keepdims=True)
        )
        return reduce_over_cores(part.astype(jnp.bfloat16).reshape(2, length, width), upstream)

    def term(gated, upstream):
        return lax.dot_general(
            gated,
            upstream.reshape(2 * length, width),
            (((0,), (0,)), ((), ())),
            preferred_element_type=jnp.float32,
        )

    gated_0, kept_0 = recompute(both[0], 0)
    gated_1, kept_1 = recompute(both[1], 1)
    ahead_0 = forward(both[2], 0)
    back_0 = backward(kept_0, both[3])
    ahead_in = along_sections(ahead_0, 1)
    back_in = along_sections(back_0, -1)
    x_1 = jnp.where(first_section, both[4], gather_over_cores(ahead_in))
    g_1 = jnp.where(last_section, both[4], gather_over_cores(back_in))
    ahead_1 = forward(x_1, 1)
    back_1 = backward(kept_1, g_1)
    product = (term(gated_0, both[3]) + term(gated_1, g_1)).astype(jnp.bfloat16)

    scaling = (ticks * length * dp_size) ** (-0.5)
    grads = 0.0
    for k in range(len(hosts)):
        mine = jnp.where(dp_no == hosts[k], columns_of(product, 0), 0)
        grads = grads + mine.astype(jnp.float32)
    for j in range(1, dp_size):
        landed = lax.ppermute(columns_of(product, j), "dp", [(h, h ^ j) for h in hosts])
        grads = grads + landed.astype(jnp.float32)
    grads = grads * scaling

    def placed(mine):
        landed = give_back(mine[1])
        return jnp.where(is_host, mine[0], landed)

    ahead = jnp.stack([placed(ahead_0), placed(ahead_1)])
    back = jnp.stack([placed(back_0), placed(back_1)])
    return (ahead[None], back[None], grads[None])


def solution(mesh):
    in_specs = (
        P(None, "dp", None),
        P("section", "dp", None),
        P(None, "dp", None),
        P("section", "dp", None),
        P("section", None, "dp", None),
        P("section", "dp", "cores"),
        P("section", "cores", "dp"),
        P("dp", None),
        P("dp", None),
        P("dp", None, None, None),
        P("dp", None, None, None),
    )
    out_specs = (
        P("section", None, ("dp", "cores"), None),
        P("section", None, ("dp", "cores"), None),
        P("section", "cores", "dp"),
    )
    return jax.shard_map(
        per_device, mesh=mesh, in_specs=in_specs, out_specs=out_specs, check_vma=False
    )
```

time: 394 us -> 373 us (0.947); the launches traced: 391 us -> 366 us
  waiting for transfers between devices: 268 us -> 133 us
  matrix products: 48.3 us -> 90.5 us
  starting transfers between devices: 6.68 us -> 43.2 us
  other arithmetic: 29.6 us -> 59.9 us
  local copies, waits for them, and re-layouts: 21.3 us -> 37 us
  between operations: 17.2 us -> 2.22 us
    all_gather x2 -> x0, waiting for transfers between devices: 186 us -> none  [the longest x1 147 us: per_device(): in_full = lax.all_gather(in_weight[0], 'dp', axis=0, tiled=True)]
    ppermute x2 -> x23, waiting for transfers between devices: 5.08 us -> 133 us  [the longest x8 116 us: fetch(): return lax.ppermute(x, 'dp', [(h ^ j, h) for h in hosts])]
    reduce_scatter x1 -> x0, waiting for transfers between devices: 42.8 us -> none  [per_device(): lax.psum_scatter(product.astype(jnp.bfloat16), 'dp', scatter_dimension=1,...]
    dot_general x9 -> x42, matrix products: 33.1 us -> 74.2 us  [the longest x16 36.2 us: project(): jnp.dot(columns_of(normed, j), in_parts[j], preferred_element_type=jnp.fl...]
    ppermute x2 -> x23, starting transfers between devices: 6.48 us -> 43.2 us  [the longest x8 22.9 us: fetch(): return lax.ppermute(x, 'dp', [(h ^ j, h) for h in hosts])]
    psum x2 -> x0, waiting for transfers between devices: 32.6 us -> none  [per_device(): lax.psum(partial_sum.astype(jnp.bfloat16), 'cores').astype(jnp.float32)]
    convert_element_type x6 -> x16, other arithmetic: 5.44 us -> 16.3 us  [the longest x2 4.86 us: heads_backward(): (grad_active * sigmoid_u * (1.0 + pre_act * (1.0 - sigmoid_u))).astype(jn...]
    another operation x8 -> x12, other arithmetic: 8.84 us -> 18.8 us
  transfers between devices with their start and end apart: 7 -> 23, of which waited for: 6 -> 7; matrix products, arithmetic and copies ran while one was open for 9% -> 41% of each run, Pallas kernels for 0% -> 0%
where the time goes in v1:
time: 373 us; the launch traced here: 366 us
  waiting for transfers between devices  133 us (36%)
  matrix products  90.5 us (24%)
  other arithmetic  59.9 us (16%)
  starting transfers between devices  43.2 us (12%)
  local copies, waits for them, and re-layouts  37 us (10%)
    ppermute x8, waiting for transfers between devices, fetch(): return lax.ppermute(x, 'dp', [(h ^ j, h) for h in hosts])  116 us
    dot_general x16, matrix products, project(): jnp.dot(columns_of(normed, j), in_parts[j], preferred_element_type=jnp.fl...  36.2 us
    ppermute x8, starting transfers between devices, fetch(): return lax.ppermute(x, 'dp', [(h ^ j, h) for h in hosts])  22.9 us
    dot_general x8, matrix products, backward(): lax.dot_general(grad_pre, in_parts[j], (((1,), (1,)), ((), ())), preferre...  16.6 us
    ppermute x4, waiting for transfers between devices, give_back(): return lax.ppermute(x, 'dp', [(h, h ^ 1) for h in hosts])  13.3 us
    another operation x4, other arithmetic  12.9 us
    dot_general x8, matrix products, backward(): lax.dot_general(columns_of(flat, j), out_parts[j], (((1,), (1,)), ((), ()...  11.4 us
    another operation x4, local copies, waits for them, and re-layouts, heads_backward(): jnp.stack([grad_gate, grad_value, grad_query, grad_key], axis=3)  9.97 us
  transfers between devices with their start and end apart: 23, of which 7 were waited for; matrix products, arithmetic and copies ran while one was open for 41% of the time, Pallas kernels for 0%

profile of v1, /device:TPU:5, one launch (start us, length us, event | category | flops | bytes accessed | tf_op | source)
XLA Modules:
  0.0 366.2 jit_solution(6289507863743735323)
XLA Ops:
  0.6 4.7 %collective-permute-start.1 = (bf16[512,2048]{1,0:T(8,128)(2,1)}, bf16[512,2048]{1,0:T(8,128)(2,1)}, u32[]{:S(2)}, u32[]{:S(2)}) collective-permute-start(bf16[512,2048]{1,0:T(8,128)(2,1)} %bitcast.357), channel_id=1, source_target_pairs={{0,2},{6,4},{1,3},{7,5},{8,10},{14,12},{9,11},{15,13},{16,18},{22,... | collective-permute-start | bytes 6291464 | tf_op jit(solution)/shard_map/ppermute | solution.py:143
  5.3 2.6 collective-permute-start.2
  14.6 2.6 collective-permute-start
  19.9 115.8 %collective-permute-done.4 = s32[2,5,17]{2,0,1:T(2,128)S(1)} collective-permute-done((s32[2,5,17]{2,0,1:T(2,128)S(1)}, s32[2,5,17]{2,0,1:T(2,128)S(1)}, u32[]{:S(2)}, u32[]{:S(2)}) %collective-permute-start.4) | collective-permute-done | bytes 712 | tf_op jit(solution)/shard_map/ppermute | solution.py:143
  142.0 4.0 %multiply_reduce_fusion.1 = (f32[2,96]{1,0:T(2,128)S(1)}, f32[1,2,96,2048]{3,2,1,0:T(8,128)}, f32[2,96]{1,0:T(2,128)S(1)}, bf16[1,2,96,2048]{3,2,1,0:T(8,128)(2,...) fusion(bf16[5,1,96,2048]{3,2,1,0:T(8,128)(2,1)} %bitcast.4, bf16[5,1,96,2048]{3,2,1,0:T(8,128)(2,1)S(1)} %bitcast.361), kind=kLoop, calls=%fused_computation.31 | loop fusion | flops 4718016 | bytes 7866624 | tf_op jit(solution)/shard_map/reduce_sum | solution.py:35
  146.0 3.2 fusion.206
  157.3 5.1 %collective-permute-start.5 = (bf16[512,512]{1,0:T(8,128)(2,1)S(1)}, bf16[512,512]{1,0:T(8,128)(2,1)}, u32[]{:S(2)}, u32[]{:S(2)}) collective-permute-start(bf16[512,512]{1,0:T(8,128)(2,1)S(1)} %bitcast.369), channel_id=1, source_target_pairs={{0,2},{6,4},{1,3},{7,5},{8,10},{14,12},{9,11},{15,13},{16,18},{22,... | collective-permute-start | bytes 1572872 | tf_op jit(solution)/shard_map/ppermute | solution.py:143
  163.8 3.1 collective-permute-start.6
  171.3 3.4 fusion.1
  174.8 3.2 reshape.552
  177.9 3.2 fusion.205
  187.7 3.5 fusion
  191.2 3.2 reshape.554
  194.3 3.2 fusion.208
  203.9 3.4 fusion.3
  207.4 3.5 reshape.544
  210.9 3.5 fusion.212
  236.7 2.8 stack.91
  243.0 2.4 convolution_dynamic-update-slice_fusion.6
  245.4 2.4 convolution_dynamic-update-slice_fusion.5
  247.9 2.6 convolution_dynamic-update-slice_fusion.4
  258.7 3.1 collective-permute-start.16
  266.9 3.0 collective-permute-done.15
  275.6 4.1 %collective-permute-done.10 = bf16[2,48,2048]{2,1,0:T(8,128)(2,1)} collective-permute-done((bf16[2,48,2048]{2,1,0:T(8,128)(2,1)S(1)}, bf16[2,48,2048]{2,1,0:T(8,128)(2,1)}, u32[]{:S(2)}, u32[]{:S(2)}) %collective-permute-start.10) | collective-permute-done | bytes 393248 | tf_op jit(solution)/shard_map/ppermute | solution.py:153
  308.7 2.8 stack.98
  315.0 2.4 convolution_dynamic-update-slice_fusion.2
  317.4 2.4 convolution_dynamic-update-slice_fusion.1
  319.9 2.6 convolution_dynamic-update-slice_fusion
  335.7 2.9 fusion.211
  351.7 2.9 multiply_bitcast_fusion
  354.6 5.8 %collective-permute-done.19 = bf16[48,2048]{1,0:T(8,128)(2,1)S(1)} collective-permute-done((bf16[48,2048]{1,0:T(8,128)(2,1)S(1)}, bf16[48,2048]{1,0:T(8,128)(2,1)S(1)}, u32[]{:S(2)}, u32[]{:S(2)}) %collective-permute-start.19) | collective-permute-done | bytes 196640 | tf_op jit(solution)/shard_map/ppermute | solution.py:146
  361.8 2.8 collective-permute-done.13
  (308 shorter events, 147.5 us)
Async XLA Ops:
  0.6 11.4 %copy-start.41 = (bf16[2,96,2048]{2,1,0:T(8,128)(2,1)S(1)}, bf16[2,96,2048]{2,1,0:T(8,128)(2,1)}, u32[]{:S(2)}) copy-start(bf16[2,96,2048]{2,1,0:T(8,128)(2,1)} %param.12) | copy-start | bytes 2359300
  0.6 11.4 %copy-start.48 = (bf16[1,96,2048]{2,1,0:T(8,128)(2,1)S(1)}, bf16[1,96,2048]{2,1,0:T(8,128)(2,1)}, u32[]{:S(2)}) copy-start(bf16[1,96,2048]{2,1,0:T(8,128)(2,1)} %param.13) | copy-start | bytes 1179652
  0.6 156.6 %collective-permute-start.1 = (bf16[512,2048]{1,0:T(8,128)(2,1)}, bf16[512,2048]{1,0:T(8,128)(2,1)}, u32[]{:S(2)}, u32[]{:S(2)}) collective-permute-start(bf16[512,2048]{1,0:T(8,128)(2,1)} %bitcast.357), channel_id=1, source_target_pairs={{0,2},{6,4},{1,3},{7,5},{8,10},{14,12},{9,11},{15,13},{16,18},{22,... | collective-permute-start | bytes 6291464 | tf_op jit(solution)/shard_map/ppermute | solution.py:143
  5.3 151.9 %collective-permute-start.2 = (bf16[512,2048]{1,0:T(8,128)(2,1)}, bf16[512,2048]{1,0:T(8,128)(2,1)}, u32[]{:S(2)}, u32[]{:S(2)}) collective-permute-start(bf16[512,2048]{1,0:T(8,128)(2,1)} %bitcast.358), channel_id=1, source_target_pairs={{6,2},{0,4},{7,3},{1,5},{14,10},{8,12},{15,11},{9,13},{22,18},{16,... | collective-permute-start | bytes 6291464 | tf_op jit(solution)/shard_map/ppermute | solution.py:143
  8.0 149.3 %collective-permute-start.3 = (bf16[512,2048]{1,0:T(8,128)(2,1)}, bf16[512,2048]{1,0:T(8,128)(2,1)}, u32[]{:S(2)}, u32[]{:S(2)}) collective-permute-start(bf16[512,2048]{1,0:T(8,128)(2,1)} %bitcast.359), channel_id=1, source_target_pairs={{4,2},{2,4},{5,3},{3,5},{12,10},{10,12},{13,11},{11,13},{20,18},{1... | collective-permute-start | bytes 6291464 | tf_op jit(solution)/shard_map/ppermute | solution.py:143
  12.1 5.4 %copy-start.50 = (s32[1,5,4,4]{1,3,2,0:T(4,128)S(1)}, s32[1,5,4,4]{1,3,2,0:T(4,128)}, u32[]{:S(2)}) copy-start(s32[1,5,4,4]{1,3,2,0:T(4,128)} %param.22) | copy-start | bytes 964
  12.1 7.1 %copy-start.53 = (s32[2]{0:T(128)S(1)}, s32[2]{0:T(128)}, u32[]{:S(2)}) copy-start(s32[2]{0:T(128)} %constant.106.clone) | copy-start | bytes 28
  14.6 127.4 %copy-start.1 = (bf16[5,96,2048]{2,1,0:T(8,128)(2,1)}, bf16[5,96,2048]{2,1,0:T(8,128)(2,1)S(1)}, u32[]{:S(2)}) copy-start(bf16[5,96,2048]{2,1,0:T(8,128)(2,1)S(1)} %select_dynamic-update-slice_fusion) | copy-start | bytes 5898244
  14.6 126.3 %collective-permute-start = (bf16[5,96,2048]{2,1,0:T(8,128)(2,1)S(1)}, bf16[5,96,2048]{2,1,0:T(8,128)(2,1)}, u32[]{:S(2)}, u32[]{:S(2)}) collective-permute-start(bf16[5,96,2048]{2,1,0:T(8,128)(2,1)S(1)} %select_dynamic-update-slice_fusion), channel_id=1, source_target_pairs={{0,2},{6,4},{1,3},{7,5},{8,10},{14,12},{9,11},{15,13},{16,18},{22,... | collective-permute-start | bytes 5898248 | tf_op jit(solution)/shard_map/ppermute | solution.py:143
  17.7 118.1 %collective-permute-start.4 = (s32[2,5,17]{2,0,1:T(2,128)S(1)}, s32[2,5,17]{2,0,1:T(2,128)S(1)}, u32[]{:S(2)}, u32[]{:S(2)}) collective-permute-start(s32[2,5,17]{2,0,1:T(2,128)S(1)} %add_add_fusion), channel_id=1, source_target_pairs={{0,2},{6,4},{1,3},{7,5},{8,10},{14,12},{9,11},{15,13},{16,18},{22,... | collective-permute-start | bytes 2048 | tf_op jit(solution)/shard_map/ppermute | solution.py:143
  142.0 116.6 %copy-start.5 = (bf16[1,2,96,2048]{3,2,1,0:T(8,128)(2,1)}, bf16[1,2,96,2048]{3,2,1,0:T(8,128)(2,1)S(1)}, u32[]{:S(2)}) copy-start(bf16[1,2,96,2048]{3,2,1,0:T(8,128)(2,1)S(1)} %fusion.59) | copy-start | bytes 2359300
  155.5 11.4 %copy-start.24 = (bf16[192,2048]{1,0:T(8,128)(2,1)S(1)}, bf16[192,2048]{1,0:T(8,128)(2,1)}, u32[]{:S(2)}) copy-start(bf16[192,2048]{1,0:T(8,128)(2,1)} %get-tuple-element.13) | copy-start | bytes 2359300
  157.3 67.0 %collective-permute-start.5 = (bf16[512,512]{1,0:T(8,128)(2,1)S(1)}, bf16[512,512]{1,0:T(8,128)(2,1)}, u32[]{:S(2)}, u32[]{:S(2)}) collective-permute-start(bf16[512,512]{1,0:T(8,128)(2,1)S(1)} %bitcast.369), channel_id=1, source_target_pairs={{0,2},{6,4},{1,3},{7,5},{8,10},{14,12},{9,11},{15,13},{16,18},{22,... | collective-permute-start | bytes 1572872 | tf_op jit(solution)/shard_map/ppermute | solution.py:143
  162.4 60.3 %collective-permute-start.7 = (bf16[512,512]{1,0:T(8,128)(2,1)S(1)}, bf16[512,512]{1,0:T(8,128)(2,1)}, u32[]{:S(2)}, u32[]{:S(2)}) collective-permute-start(bf16[512,512]{1,0:T(8,128)(2,1)S(1)} %bitcast.370), channel_id=1, source_target_pairs={{4,2},{2,4},{5,3},{3,5},{12,10},{10,12},{13,11},{11,13},{20,18},{1... | collective-permute-start | bytes 1572872 | tf_op jit(solution)/shard_map/ppermute | solution.py:143
  163.8 61.9 %collective-permute-start.6 = (bf16[512,512]{1,0:T(8,128)(2,1)S(1)}, bf16[512,512]{1,0:T(8,128)(2,1)}, u32[]{:S(2)}, u32[]{:S(2)}) collective-permute-start(bf16[512,512]{1,0:T(8,128)(2,1)S(1)} %bitcast.371), channel_id=1, source_target_pairs={{6,2},{0,4},{7,3},{1,5},{14,10},{8,12},{15,11},{9,13},{22,18},{16,... | collective-permute-start | bytes 1572872 | tf_op jit(solution)/shard_map/ppermute | solution.py:143
  251.1 7.4 %collective-permute-start.14 = (bf16[2,48,2048]{2,1,0:T(8,128)(2,1)S(1)}, bf16[2,48,2048]{2,1,0:T(8,128)(2,1)S(1)}, u32[]{:S(2)}, u32[]{:S(2)}) collective-permute-start(bf16[2,48,2048]{2,1,0:T(8,128)(2,1)S(1)} %constant_dynamic-slice_fusion.4), channel_id=1, source_target_pairs={{0,1},{1,0},{2,3},{3,2},{4,5},{5,4},{6,7},{7,6},{8,9},{9,8},{10,11... | collective-permute-start | bytes 1179656 | tf_op jit(solution)/shard_map/ppermute | solution.py:149
  258.0 5.1 %collective-permute-start.8 = (bf16[2,48,2048]{2,1,0:T(8,128)(2,1)S(1)}, bf16[2,48,2048]{2,1,0:T(8,128)(2,1)S(1)}, u32[]{:S(2)}, u32[]{:S(2)}) collective-permute-start(bf16[2,48,2048]{2,1,0:T(8,128)(2,1)S(1)} %constant_dynamic-slice_fusion.6), channel_id=1, source_target_pairs={{0,1},{1,0},{2,3},{3,2},{4,5},{5,4},{6,7},{7,6},{8,9},{9,8},{10,11... | collective-permute-start | bytes 1179656 | tf_op jit(solution)/shard_map/ppermute | solution.py:149
  258.7 12.6 %collective-permute-start.16 = (bf16[2,48,2048]{2,1,0:T(8,128)(2,1)S(1)}, bf16[2,48,2048]{2,1,0:T(8,128)(2,1)S(1)}, u32[]{:S(2)}, u32[]{:S(2)}) collective-permute-start(bf16[2,48,2048]{2,1,0:T(8,128)(2,1)S(1)} %fusion.62), channel_id=1, source_target_pairs={{8,0},{16,8},{24,16},{9,1},{17,9},{25,17},{10,2},{18,10},{26,18},{... | collective-permute-start | bytes 1179656 | tf_op jit(solution)/shard_map/ppermute | solution.py:153
  261.8 8.0 %collective-permute-start.15 = (bf16[48,2048]{1,0:T(8,128)(2,1)S(1)}, bf16[48,2048]{1,0:T(8,128)(2,1)S(1)}, u32[]{:S(2)}, u32[]{:S(2)}) collective-permute-start(bf16[48,2048]{1,0:T(8,128)(2,1)S(1)} %slice_bitcast_fusion.9), channel_id=1, source_target_pairs={{2,0},{4,6},{3,1},{5,7},{10,8},{12,14},{11,9},{13,15},{18,16},{20,... | collective-permute-start | bytes 589832 | tf_op jit(solution)/shard_map/ppermute | solution.py:146
  263.3 16.4 %collective-permute-start.10 = (bf16[2,48,2048]{2,1,0:T(8,128)(2,1)S(1)}, bf16[2,48,2048]{2,1,0:T(8,128)(2,1)}, u32[]{:S(2)}, u32[]{:S(2)}) collective-permute-start(bf16[2,48,2048]{2,1,0:T(8,128)(2,1)S(1)} %fusion.64), channel_id=1, source_target_pairs={{0,8},{8,16},{16,24},{1,9},{9,17},{17,25},{2,10},{10,18},{18,26},{... | collective-permute-start | bytes 1179656 | tf_op jit(solution)/shard_map/ppermute | solution.py:153
  265.6 8.8 %collective-permute-start.9 = (bf16[48,2048]{1,0:T(8,128)(2,1)S(1)}, bf16[48,2048]{1,0:T(8,128)(2,1)S(1)}, u32[]{:S(2)}, u32[]{:S(2)}) collective-permute-start(bf16[48,2048]{1,0:T(8,128)(2,1)S(1)} %slice_bitcast_fusion.24), channel_id=1, source_target_pairs={{2,0},{4,6},{3,1},{5,7},{10,8},{12,14},{11,9},{13,15},{18,16},{20,... | collective-permute-start | bytes 589832 | tf_op jit(solution)/shard_map/ppermute | solution.py:146
  271.3 9.3 %collective-permute-start.17 = (bf16[2,48,2048]{2,1,0:T(8,128)(2,1)S(1)}, bf16[2,48,2048]{2,1,0:T(8,128)(2,1)S(1)}, u32[]{:S(2)}, u32[]{:S(2)}) collective-permute-start(bf16[2,48,2048]{2,1,0:T(8,128)(2,1)S(1)} %collective-permute-done.16), channel_id=1, source_target_pairs={{0,1},{1,0},{2,3},{3,2},{4,5},{5,4},{6,7},{7,6},{8,9},{9,8},{10,11... | collective-permute-start | bytes 1179656 | tf_op jit(solution)/shard_map/ppermute | solution.py:149
  279.7 14.9 %collective-permute-start.11 = (bf16[2,48,2048]{2,1,0:T(8,128)(2,1)}, bf16[2,48,2048]{2,1,0:T(8,128)(2,1)}, u32[]{:S(2)}, u32[]{:S(2)}) collective-permute-start(bf16[2,48,2048]{2,1,0:T(8,128)(2,1)} %collective-permute-done.10), channel_id=1, source_target_pairs={{0,1},{1,0},{2,3},{3,2},{4,5},{5,4},{6,7},{7,6},{8,9},{9,8},{10,11... | collective-permute-start | bytes 1179656 | tf_op jit(solution)/shard_map/ppermute | solution.py:149
  302.2 49.5 %collective-permute-start.20 = (bf16[512,512]{1,0:T(8,128)(2,1)}, bf16[512,512]{1,0:T(8,128)(2,1)}, u32[]{:S(2)}, u32[]{:S(2)}) collective-permute-start(bf16[512,512]{1,0:T(8,128)(2,1)} %get-tuple-element.35), channel_id=1, source_target_pairs={{2,0},{4,6},{3,1},{5,7},{10,8},{12,14},{11,9},{13,15},{18,16},{20,... | collective-permute-start | bytes 1572872 | tf_op jit(solution)/shard_map/ppermute | solution.py:306
  303.5 48.2 %collective-permute-start.21 = (bf16[512,512]{1,0:T(8,128)(2,1)}, bf16[512,512]{1,0:T(8,128)(2,1)}, u32[]{:S(2)}, u32[]{:S(2)}) collective-permute-start(bf16[512,512]{1,0:T(8,128)(2,1)} %get-tuple-element.37), channel_id=1, source_target_pairs={{2,6},{4,0},{3,7},{5,1},{10,14},{12,8},{11,15},{13,9},{18,22},{20,... | collective-permute-start | bytes 1572872 | tf_op jit(solution)/shard_map/ppermute | solution.py:306
  304.8 46.9 %collective-permute-start.22 = (bf16[512,512]{1,0:T(8,128)(2,1)}, bf16[512,512]{1,0:T(8,128)(2,1)}, u32[]{:S(2)}, u32[]{:S(2)}) collective-permute-start(bf16[512,512]{1,0:T(8,128)(2,1)} %get-tuple-element.36), channel_id=1, source_target_pairs={{2,4},{4,2},{3,5},{5,3},{10,12},{12,10},{11,13},{13,11},{18,20},{2... | collective-permute-start | bytes 1572872 | tf_op jit(solution)/shard_map/ppermute | solution.py:306
  324.8 22.5 %collective-permute-start.18 = (bf16[2,48,2048]{2,1,0:T(8,128)(2,1)}, bf16[2,48,2048]{2,1,0:T(8,128)(2,1)}, u32[]{:S(2)}, u32[]{:S(2)}) collective-permute-start(bf16[2,48,2048]{2,1,0:T(8,128)(2,1)} %constant_dynamic-slice_fusion.3), channel_id=1, source_target_pairs={{0,1},{1,0},{2,3},{3,2},{4,5},{5,4},{6,7},{7,6},{8,9},{9,8},{10,11... | collective-permute-start | bytes 1179656 | tf_op jit(solution)/shard_map/ppermute | solution.py:149
  346.7 3.3 collective-permute-start.12
  348.7 11.7 %collective-permute-start.19 = (bf16[48,2048]{1,0:T(8,128)(2,1)S(1)}, bf16[48,2048]{1,0:T(8,128)(2,1)S(1)}, u32[]{:S(2)}, u32[]{:S(2)}) collective-permute-start(bf16[48,2048]{1,0:T(8,128)(2,1)S(1)} %slice_bitcast_fusion.4), channel_id=1, source_target_pairs={{2,0},{4,6},{3,1},{5,7},{10,8},{12,14},{11,9},{13,15},{18,16},{20,... | collective-permute-start | bytes 589832 | tf_op jit(solution)/shard_map/ppermute | solution.py:146
  350.2 10.8 %copy-start.42 = (bf16[1,48,2048]{2,1,0:T(8,128)(2,1)S(1)}, bf16[1,48,2048]{2,1,0:T(8,128)(2,1)}, u32[]{:S(2)}) copy-start(bf16[1,48,2048]{2,1,0:T(8,128)(2,1)} %fusion.89) | copy-start | bytes 589828
  350.2 14.4 %collective-permute-start.13 = (bf16[48,2048]{1,0:T(8,128)(2,1)S(1)}, bf16[48,2048]{1,0:T(8,128)(2,1)S(1)}, u32[]{:S(2)}, u32[]{:S(2)}) collective-permute-start(bf16[48,2048]{1,0:T(8,128)(2,1)S(1)} %slice_bitcast_fusion.14), channel_id=1, source_target_pairs={{2,0},{4,6},{3,1},{5,7},{10,8},{12,14},{11,9},{13,15},{18,16},{20,... | collective-permute-start | bytes 589832 | tf_op jit(solution)/shard_map/ppermute | solution.py:146
  354.6 10.6 %copy-start.43 = (bf16[1,48,2048]{2,1,0:T(8,128)(2,1)S(1)}, bf16[1,48,2048]{2,1,0:T(8,128)(2,1)}, u32[]{:S(2)}) copy-start(bf16[1,48,2048]{2,1,0:T(8,128)(2,1)} %fusion.93) | copy-start | bytes 589828
  (48 other events, 140.8 us)

commit v2 on v0

v2 whole, which is shorter than its diff:
```python
import functools

import jax
import jax.numpy as jnp
from jax import lax
from jax.experimental import pallas as pl
from jax.experimental.pallas import tpu as pltpu
from jax.sharding import PartitionSpec as P

HEAD_DIM = 128
BLOCK = 24
BLOCKS = 4
EPSILON = 1e-06
SCALING = HEAD_DIM ** (-0.5)
VMEM_BYTES = 50 * 1024 * 1024

F32 = jnp.float32
BF16 = jnp.bfloat16


def dot(a, b):
    return lax.dot_general(a, b, (((1,), (0,)), ((), ())), preferred_element_type=F32)


def dot_nt(a, b):
    return lax.dot_general(a, b, (((1,), (1,)), ((), ())), preferred_element_type=F32)


def dot_tn(a, b):
    return lax.dot_general(a, b, (((0,), (0,)), ((), ())), preferred_element_type=F32)


def row_root(floats):
    return lax.rsqrt(jnp.mean(floats * floats, axis=-1, keepdims=True) + EPSILON)


def sigmoid(x):
    return 1.0 / (1.0 + jnp.exp(-x))


def attend(pre, keep):
    sig = sigmoid(pre)
    active = pre * sig
    gate = active[:, :HEAD_DIM]
    vqk = active[:, HEAD_DIM:].astype(BF16)
    value = vqk[:, :HEAD_DIM]
    query = vqk[:, HEAD_DIM : 2 * HEAD_DIM]
    key = vqk[:, 2 * HEAD_DIM :]
    scores = dot_nt(query, key) * SCALING
    sig_s = sigmoid(scores)
    probs = (scores * sig_s * keep).astype(BF16)
    mixed = dot(probs, value)
    gated = (mixed * row_root(mixed) * gate).astype(BF16)
    return sig, gate, vqk, scores, sig_s, probs, mixed, gated


def project_kernel(n, places, offs, own, theirs, keep, *rest):
    weights = rest[:n]
    gated_out, gate_out, vqk_out, slope_out, mixed_out, probs_out, factor_out, normed = rest[n:]
    depth = weights[0].shape[0]
    length = own.shape[1]
    rows = 2 * length

    @pl.when(pl.program_id(0) == 0)
    def _():
        for i, place in enumerate(places):
            for r, source in enumerate((own, theirs)):
                floats = source[place].astype(F32)
                normed[pl.ds((2 * i + r) * length, length), :] = (
                    floats * row_root(floats)
                ).astype(BF16)

    pre_all = None
    for j in range(n):
        columns = pl.ds(pl.multiple_of(offs[j], depth), depth)
        term = dot(normed[:, columns], weights[j][...])
        pre_all = term if pre_all is None else pre_all + term
    for i in range(len(places)):
        pre = pre_all[i * rows : (i + 1) * rows]
        kept = keep[i]
        sig, gate, vqk, scores, sig_s, probs, mixed, gated = attend(pre, kept)
        gated_out[i] = gated
        if i > 0:
            gate_out[i - 1] = gate
            vqk_out[i - 1] = vqk
            slope_out[i - 1] = sig * (1.0 + pre * (1.0 - sig))
            mixed_out[i - 1] = mixed
            probs_out[i - 1, 0] = probs
            factor_out[i - 1, 0] = kept * sig_s * (1.0 + scores * (1.0 - sig_s)) * SCALING


def split_rows(core, part, send, keep):
    share = send.shape[1]
    cores = part.shape[0] // (2 * share)
    for r in range(2):
        base = r * cores * share
        mine = pl.multiple_of(base + core * share, share)
        other = pl.multiple_of(base + (cores - 1 - core) * share, share)
        send[r] = part[pl.ds(other, share), :]
        keep[r] = part[pl.ds(mine, share), :]


def out_kernel(n, core, offs, gated, *rest):
    weights = rest[:n]
    send, keep, part = rest[n:]
    depth = weights[0].shape[1]
    for j in range(n):
        columns = pl.ds(pl.multiple_of(offs[j], depth), depth)
        part[:, columns] = dot(gated[0], weights[j][...]).astype(BF16)
    split_rows(core[0], part, send, keep)


def assemble(core, fresh, mine, theirs, new_own, new_theirs, whole):
    share = mine.shape[1]
    length = new_own.shape[1]
    cores = length // share
    use_fresh = fresh != 0
    for r, source in enumerate((new_own, new_theirs)):
        for owner, landed in ((core, mine), (cores - 1 - core, theirs)):
            inside = pl.multiple_of(owner * share, share)
            rows = source[0, pl.ds(inside, share), :]
            at = pl.multiple_of(r * length + owner * share, share)
            whole[pl.ds(at, share), :] = jnp.where(use_fresh, rows, landed[r])


def forward_kernel(n, heads, core, offs, fresh, mine, theirs, new_own, new_theirs, keep, *rest):
    in_parts = rest[:n]
    out_parts = rest[n : 2 * n]
    send, kept, whole, normed, gated, part = rest[2 * n :]
    depth = in_parts[0].shape[0]
    head = pl.program_id(0)

    @pl.when(head == 0)
    def _():
        assemble(core[0], fresh[0], mine, theirs, new_own, new_theirs, whole)
        floats = whole[...].astype(F32)
        normed[...] = (floats * row_root(floats)).astype(BF16)

    pre = None
    for j in range(n):
        columns = pl.ds(pl.multiple_of(offs[j], depth), depth)
        term = dot(normed[:, columns], in_parts[j][...])
        pre = term if pre is None else pre + term
    gated[head] = attend(pre, keep[0])[-1]

    @pl.when(head == heads - 1)
    def _():
        for j in range(n):
            columns = pl.ds(pl.multiple_of(offs[j], depth), depth)
            total = None
            for h in range(heads):
                term = dot(gated[h], out_parts[j][pl.ds(h * HEAD_DIM, HEAD_DIM), :])
                total = term if total is None else total + term
            part[:, columns] = total.astype(BF16)
        split_rows(core[0], part, send, kept)


def backward_kernel(
    n, heads, core, offs, up_own, up_theirs, x_own, x_theirs, gate, vqk, slope, mixed, probs, factor, *rest
):
    out_parts = rest[:n]
    in_hbm = rest[n : 2 * n]
    send, keep, upstream, in_parts, grad_normed, part, sems = rest[2 * n :]
    depth = out_parts[0].shape[1]
    length = up_own.shape[1]
    wide = 4 * HEAD_DIM
    copies = [
        pltpu.make_async_copy(in_hbm[j], in_parts.at[j], sems.at[j]) for j in range(n)
    ]
    for copy in copies:
        copy.start()
    for r, source in enumerate((up_own, up_theirs)):
        upstream[pl.ds(r * length, length), :] = source[0]
    grad_gated = None
    for j in range(n):
        columns = pl.ds(pl.multiple_of(offs[j], depth), depth)
        term = dot_nt(upstream[:, columns], out_parts[j][...])
        grad_gated = term if grad_gated is None else grad_gated + term
    grad_gated = grad_gated.astype(BF16).astype(F32)
    grads_pre = []
    for h in range(heads):
        cut = slice(h * HEAD_DIM, (h + 1) * HEAD_DIM)
        up = grad_gated[:, cut]
        mixed_h = mixed[0, :, cut]
        root = row_root(mixed_h)
        normed = mixed_h * root
        grad_n = up * gate[0, :, cut]
        grad_gate = up * normed
        grad_mixed = root * (grad_n - normed * jnp.mean(grad_n * normed, axis=-1, keepdims=True))
        low = grad_mixed.astype(BF16)
        base = 3 * h * HEAD_DIM
        value = vqk[0, :, base : base + HEAD_DIM]
        query = vqk[0, :, base + HEAD_DIM : base + 2 * HEAD_DIM]
        key = vqk[0, :, base + 2 * HEAD_DIM : base + 3 * HEAD_DIM]
        grad_scores = (dot_nt(low, value) * factor[0, h]).astype(BF16)
        grad_value = dot_tn(probs[0, h], low)
        grad_query = dot(grad_scores, key)
        grad_key = dot_tn(grad_scores, query)
        grad_active = jnp.concatenate([grad_gate, grad_value, grad_query, grad_key], axis=1)
        grads_pre.append((grad_active * slope[0, :, h * wide : (h + 1) * wide]).astype(BF16))
    grad_pre = jnp.concatenate(grads_pre, axis=1)
    for j in range(n):
        columns = pl.ds(pl.multiple_of(offs[j], depth), depth)
        copies[j].wait()
        grad_normed[:, columns] = dot_nt(grad_pre, in_parts[j])
    for r, source in enumerate((x_own, x_theirs)):
        rows = pl.ds(r * length, length)
        floats = source[0].astype(F32)
        root = row_root(floats)
        scaled = floats * root
        grad_n = grad_normed[rows, :]
        part[rows, :] = (
            root * (grad_n - scaled * jnp.mean(grad_n * scaled, axis=-1, keepdims=True))
        ).astype(BF16)
    split_rows(core[0], part, send, keep)


def term_kernel(
    n, core, offs, fresh, mine, theirs, new_own, new_theirs, up_own, up_theirs, gated, *rest
):
    pieces = rest[:n]
    whole, upstream = rest[n:]
    depth = pieces[0].shape[1]
    length = up_own.shape[1]
    assemble(core[0], fresh[0], mine, theirs, new_own, new_theirs, whole)
    for r, source in enumerate((up_own, up_theirs)):
        upstream[pl.ds(r * length, length), :] = source[0]
    for j in range(n):
        columns = pl.ds(pl.multiple_of(offs[j], depth), depth)
        pieces[j][...] = (
            dot_tn(gated[1], upstream[:, columns]) + dot_tn(gated[2], whole[:, columns])
        ).astype(BF16)


def after(value, *earlier):
    return lax.optimization_barrier((value,) + earlier)[0]


def block_keep(live_blocks, block_marks):
    length = BLOCKS * BLOCK
    places = jnp.arange(length, dtype=jnp.int32)
    owners = places // BLOCK
    marked = jnp.repeat(jnp.repeat(block_marks, BLOCK, axis=-2), BLOCK, axis=-1) == 1
    allowed = (owners[:, None] == owners[None, :]) | marked
    causal = places[:, None] >= places[None, :]
    tokens = live_blocks[..., None, None] * BLOCK
    keeping = causal & allowed & (places[:, None] < tokens) & (places[None, :] < tokens)
    return jnp.where(keeping, 1.0 / jnp.maximum(tokens, 1).astype(F32), 0.0)


def per_device(
    arrivals,
    in_flight,
    cotangent,
    grad_flight,
    stashed,
    in_weight,
    out_weight,
    forward_blocks,
    backward_blocks,
    forward_marks,
    backward_marks,
):
    section_no = lax.axis_index("section")
    sections = lax.axis_size("section")
    core_no = lax.axis_index("cores")
    cores = lax.axis_size("cores")
    dp_no = lax.axis_index("dp")
    n = lax.axis_size("dp")
    ticks = arrivals.shape[0]
    length = arrivals.shape[1]
    width = arrivals.shape[2]
    rows = 2 * length
    share = length // cores
    in_shard = in_weight[0]
    out_shard = out_weight[0]
    depth = in_shard.shape[0]
    slab = out_shard.shape[0]
    heads = slab // HEAD_DIM
    wide = 4 * HEAD_DIM

    hosts = [2 * k + 1 if 4 * k < n - 2 else 2 * k for k in range(n // 2)]
    host_table = jnp.array(hosts, jnp.int32)
    is_host = dp_no == host_table[dp_no // 2]

    def from_partner(x):
        return lax.ppermute(x, "dp", [(h ^ 1, h) for h in hosts])

    def to_partner(x):
        return lax.ppermute(x, "dp", [(h, h ^ 1) for h in hosts])

    def from_host(x, m):
        return lax.ppermute(x, "dp", [(hosts[k ^ m], hosts[k]) for k in range(n // 2)])

    def swap_cores(x):
        return lax.ppermute(x, "cores", [(c, cores - 1 - c) for c in range(cores)])

    def along_sections(x, by):
        pairs = [(i, i + by) for i in range(sections) if 0 <= i + by < sections]
        return lax.ppermute(x, "section", pairs)

    first_section = section_no == 0
    last_section = section_no == sections - 1
    tables = jnp.concatenate(
        [
            jnp.concatenate([b[..., None], m.reshape(m.shape[:2] + (-1,))], axis=-1)
            for b, m in ((forward_blocks, forward_marks), (backward_blocks, backward_marks))
        ],
        axis=0,
    )
    own = jnp.stack(
        [
            jnp.where(first_section, arrivals[0], in_flight[0]),
            stashed[0, 0],
            stashed[0, 1],
            jnp.where(last_section, cotangent[0], grad_flight[0]),
            jnp.where(first_section, arrivals[1], cotangent[1]),
        ]
    )
    in_near = from_partner(in_shard)
    in_parts = [in_shard, in_near]
    in_parts += [from_host(in_shard, m) for m in range(1, n // 2)]
    near_tables = from_partner(tables)
    theirs = from_partner(after(own, near_tables))
    in_parts += [from_host(in_near, m) for m in range(1, n // 2)]
    out_own = after(out_shard, *in_parts[1 : 1 + n // 2])
    out_far = [from_host(out_own, m) for m in range(1, n // 2)]
    out_near = from_partner(after(out_shard, theirs))
    out_parts = [out_shard, out_near] + out_far
    out_parts += [from_host(out_near, m) for m in range(1, n // 2)]
    owners = [dp_no, dp_no ^ 1]
    owners += [host_table[(dp_no // 2) ^ m] for m in range(1, n // 2)]
    owners += [host_table[(dp_no // 2) ^ m] ^ 1 for m in range(1, n // 2)]
    offs = jnp.stack(owners).astype(jnp.int32) * depth
    core = jnp.reshape(core_no, (1,)).astype(jnp.int32)
    first_flag = jnp.reshape(first_section, (1,)).astype(jnp.int32)
    last_flag = jnp.reshape(last_section, (1,)).astype(jnp.int32)

    both_tables = jnp.stack([tables, near_tables], axis=1)
    ahead_at = sections - 1 - section_no
    chosen = jnp.stack(
        [
            lax.dynamic_index_in_dim(both_tables[way], at, axis=1, keepdims=False)
            for way, at in (
                (0, ahead_at),
                (1, section_no),
                (1, section_no + 1),
                (0, ahead_at + 1),
            )
        ]
    )
    kept = block_keep(chosen[..., 0], chosen[..., 1:].reshape(-1, 2, BLOCKS, BLOCKS))
    blank = jnp.zeros_like(kept[:, 0])
    keep = jnp.concatenate(
        [
            jnp.concatenate([kept[:, 0], blank], axis=2),
            jnp.concatenate([blank, kept[:, 1]], axis=2),
        ],
        axis=1,
    )

    smem = pl.BlockSpec(memory_space=pltpu.SMEM)
    params = pltpu.CompilerParams(vmem_limit_bytes=VMEM_BYTES)
    whole_of = lambda x: pl.BlockSpec(x.shape, lambda *_: (0,) * x.ndim)

    def row_of(x, i):
        return pl.BlockSpec((1,) + x.shape[1:], lambda *_: (i,) + (0,) * (x.ndim - 1))

    def struct(shape, dtype):
        return jax.ShapeDtypeStruct(shape, dtype)

    halves = [struct((2, share, width), BF16)] * 2
    half_specs = [pl.BlockSpec((2, share, width), lambda *_: (0, 0, 0))] * 2

    by_head = lambda lead, last: pl.BlockSpec(lead + (last,), lambda h: (0,) * len(lead) + (h,))
    square = pl.BlockSpec((2, 1, rows, rows), lambda h: (0, h, 0, 0))
    gated, gate, vqk, slope, mixed, probs, factor = pl.pallas_call(
        functools.partial(project_kernel, n, (0, 1, 2)),
        grid=(heads,),
        in_specs=[smem, whole_of(own), whole_of(theirs), pl.BlockSpec((3, rows, rows), lambda h: (0, 0, 0))]
        + [by_head((depth,), wide)] * n,
        out_specs=[
            by_head((3, rows), HEAD_DIM),
            by_head((2, rows), HEAD_DIM),
            by_head((2, rows), 3 * HEAD_DIM),
            by_head((2, rows), wide),
            by_head((2, rows), HEAD_DIM),
            square,
            square,
        ],
        out_shape=[
            struct((3, rows, slab), BF16),
            struct((2, rows, slab), F32),
            struct((2, rows, 3 * slab), BF16),
            struct((2, rows, 4 * slab), F32),
            struct((2, rows, slab), F32),
            struct((2, heads, rows, rows), BF16),
            struct((2, heads, rows, rows), F32),
        ],
        scratch_shapes=[pltpu.VMEM((3 * rows, width), BF16)],
        compiler_params=params,
        name="project",
    )(offs, own, theirs, keep, *in_parts)

    def backward(up_own, up_theirs, up_at, tick_no):
        saved = [gate, vqk, slope, mixed, probs, factor]
        return pl.pallas_call(
            functools.partial(backward_kernel, n, heads),
            grid=(1,),
            in_specs=[smem, smem, row_of(up_own, up_at[0]), row_of(up_theirs, up_at[1])]
            + [row_of(own, 1 + tick_no), row_of(theirs, 1 + tick_no)]
            + [row_of(x, tick_no) for x in saved]
            + [whole_of(out_shard)] * n
            + [pl.BlockSpec(memory_space=pl.ANY)] * n,
            out_specs=half_specs,
            out_shape=halves,
            scratch_shapes=[
                pltpu.VMEM((rows, width), BF16),
                pltpu.VMEM((n,) + in_shard.shape, BF16),
                pltpu.VMEM((rows, width), F32),
                pltpu.VMEM((rows, width), BF16),
                pltpu.SemaphoreType.DMA((n,)),
            ],
            compiler_params=params,
            name="backward",
        )(core, offs, up_own, up_theirs, own, theirs, *saved, *out_parts, *in_parts)

    def finish(residual, halves_of):
        send, mine = halves_of
        landed = swap_cores(send)
        return (residual.astype(F32) + mine.astype(F32) + landed.astype(F32)).astype(BF16)

    def own_rows(at):
        both = jnp.stack([own[at], theirs[at]])
        return lax.dynamic_slice_in_dim(both, core_no * share, share, axis=1)

    ahead_parts = pl.pallas_call(
        functools.partial(out_kernel, n),
        grid=(1,),
        in_specs=[smem, smem, row_of(gated, 0)] + [whole_of(out_shard)] * n,
        out_specs=half_specs,
        out_shape=halves,
        scratch_shapes=[pltpu.VMEM((rows, width), BF16)],
        compiler_params=params,
        name="out",
    )(core, offs, gated, *out_parts)
    ahead_0 = finish(own_rows(0), ahead_parts)
    ahead_in = along_sections(ahead_0, 1)
    back_0 = finish(own_rows(3), backward(own, theirs, (3, 3), 0))
    back_in = along_sections(back_0, -1)

    ahead_their = swap_cores(ahead_in)
    ahead_parts = pl.pallas_call(
        functools.partial(forward_kernel, n, heads),
        grid=(heads,),
        in_specs=[smem, smem, smem, whole_of(ahead_in), whole_of(ahead_their)]
        + [row_of(own, 4), row_of(theirs, 4), row_of(keep, 3)]
        + [by_head((depth,), wide)] * n
        + [whole_of(out_shard)] * n,
        out_specs=half_specs,
        out_shape=halves,
        scratch_shapes=[
            pltpu.VMEM((rows, width), BF16),
            pltpu.VMEM((rows, width), BF16),
            pltpu.VMEM((heads, rows, HEAD_DIM), BF16),
            pltpu.VMEM((rows, width), BF16),
        ],
        compiler_params=params,
        name="forward",
    )(core, offs, first_flag, ahead_in, ahead_their, own, theirs, keep, *in_parts, *out_parts)
    ahead_1 = finish(jnp.where(first_section, own_rows(4), ahead_in), ahead_parts)

    back_their = swap_cores(back_in)
    *pieces, up_1 = pl.pallas_call(
        functools.partial(term_kernel, n),
        grid=(1,),
        in_specs=[smem, smem, smem, whole_of(back_in), whole_of(back_their)]
        + [row_of(own, 4), row_of(theirs, 4), row_of(own, 3), row_of(theirs, 3), whole_of(gated)],
        out_specs=[pl.BlockSpec((slab, depth), lambda *_: (0, 0))] * n
        + [pl.BlockSpec((rows, width), lambda *_: (0, 0))],
        out_shape=[struct((slab, depth), BF16)] * n + [struct((rows, width), BF16)],
        scratch_shapes=[pltpu.VMEM((rows, width), BF16)],
        compiler_params=params,
        name="terms",
    )(core, offs, last_flag, back_in, back_their, own, theirs, own, theirs, gated)
    up_1 = up_1.reshape(2, length, width)
    back_1 = finish(
        jnp.where(last_section, own_rows(4), back_in), backward(up_1, up_1, (0, 1), 1)
    )

    scaling = (ticks * length * n) ** (-0.5)
    grads = jnp.where(is_host, pieces[0], 0).astype(F32)
    grads = grads + to_partner(pieces[1]).astype(F32)
    for m in range(1, n // 2):
        grads = grads + from_host(pieces[1 + m], m).astype(F32)
        beyond = pieces[n // 2 + m]
        landed = lax.ppermute(
            beyond, "dp", [(hosts[k ^ m], hosts[k] ^ 1) for k in range(n // 2)]
        )
        grads = grads + landed.astype(F32)
    grads = grads * scaling

    def placed(mine):
        return jnp.where(is_host, mine[0], to_partner(mine[1]))

    ahead = jnp.stack([placed(ahead_0), placed(ahead_1)])
    back = jnp.stack([placed(back_0), placed(back_1)])
    return (ahead[None], back[None], grads[None])


def solution(mesh):
    in_specs = (
        P(None, "dp", None),
        P("section", "dp", None),
        P(None, "dp", None),
        P("section", "dp", None),
        P("section", None, "dp", None),
        P("section", "dp", "cores"),
        P("section", "cores", "dp"),
        P("dp", None),
        P("dp", None),
        P("dp", None, None, None),
        P("dp", None, None, None),
    )
    out_specs = (
        P("section", None, ("dp", "cores"), None),
        P("section", None, ("dp", "cores"), None),
        P("section", "cores", "dp"),
    )
    return jax.shard_map(
        per_device, mesh=mesh, in_specs=in_specs, out_specs=out_specs, check_vma=False
    )
```

time: 394 us -> 225 us (0.57)
  waiting for transfers between devices: 268 us -> 117 us
  matrix products: 48.3 us -> 0 us
  Pallas kernels: 0 us -> 44.5 us
  starting transfers between devices: 6.68 us -> 37.6 us
  other arithmetic: 29.6 us -> 9.93 us
  between operations: 17.2 us -> 2.44 us
  local copies, waits for them, and re-layouts: 21.3 us -> 8.98 us
    all_gather x2 -> x0, waiting for transfers between devices: 186 us -> none  [the longest x1 147 us: per_device(): in_full = lax.all_gather(in_weight[0], 'dp', axis=0, tiled=True)]
    ppermute x2 -> x23, waiting for transfers between devices: 5.08 us -> 117 us  [the longest x4 78.2 us: from_partner(): return lax.ppermute(x, 'dp', [(h ^ 1, h) for h in hosts])]
    dot_general x27 -> x0, matrix products: 48.3 us -> none  [the longest x2 13.3 us: per_device(): jnp.einsum('sf,df->sd', grad_pre, in_full, preferred_element_type=jnp.flo...]
    pallas_call x0 -> x6, Pallas kernels: none -> 44.5 us  [the longest x2 17.9 us: backward(): pl.pallas_call(functools.partial(backward_kernel, n, heads), grid=(1,), i...]
    reduce_scatter x1 -> x0, waiting for transfers between devices: 42.8 us -> none  [per_device(): lax.psum_scatter(product.astype(jnp.bfloat16), 'dp', scatter_dimension=1,...]
    psum x2 -> x0, waiting for transfers between devices: 32.6 us -> none  [per_device(): lax.psum(partial_sum.astype(jnp.bfloat16), 'cores').astype(jnp.float32)]
    ppermute x2 -> x23, starting transfers between devices: 6.48 us -> 37.6 us  [the longest x4 11.4 us: from_partner(): return lax.ppermute(x, 'dp', [(h ^ 1, h) for h in hosts])]
    another operation x10 -> x9, other arithmetic: 11.4 us -> 1.44 us  [the longest x1 1.23 us: per_device(): jnp.stack([jnp.where(first_section, arrivals[0], in_flight[0]), stashed[0...]
  transfers between devices with their start and end apart: 7 -> 23, of which waited for: 6 -> 8; matrix products, arithmetic and copies ran while one was open for 9% -> 5% of each run, Pallas kernels for 0% -> 20%
where the time goes in v2:
time: 225 us; the launch traced here: 221 us
  waiting for transfers between devices  117 us (52%)
  Pallas kernels  44.5 us (20%)
  starting transfers between devices  37.6 us (17%)
  other arithmetic  9.93 us (4%)
  local copies, waits for them, and re-layouts  8.98 us (4%)
  between operations  2.44 us (1%)
    ppermute x4, waiting for transfers between devices, from_partner(): return lax.ppermute(x, 'dp', [(h ^ 1, h) for h in hosts])  78.2 us
    pallas_call x2, Pallas kernels, backward(): pl.pallas_call(functools.partial(backward_kernel, n, heads), grid=(1,), i...  17.9 us
    ppermute x5, waiting for transfers between devices, to_partner(): return lax.ppermute(x, 'dp', [(h, h ^ 1) for h in hosts])  15.5 us
    pallas_call x1, Pallas kernels, per_device(): pl.pallas_call(functools.partial(project_kernel, n, (0, 1, 2)), grid=(hea...  14.2 us
    ppermute x1, waiting for transfers between devices, per_device(): lax.ppermute(beyond, 'dp', [(hosts[k ^ m], hosts[k] ^ 1) for k in range(n...  14.2 us
    ppermute x4, starting transfers between devices, from_partner(): return lax.ppermute(x, 'dp', [(h ^ 1, h) for h in hosts])  11.4 us
    ppermute x2, waiting for transfers between devices, along_sections(): return lax.ppermute(x, 'section', pairs)  9.61 us
    pallas_call x1, Pallas kernels, per_device(): pl.pallas_call(functools.partial(forward_kernel, n, heads), grid=(heads,)...  8.21 us
  transfers between devices with their start and end apart: 23, of which 8 were waited for; matrix products, arithmetic and copies ran while one was open for 5% of the time, Pallas kernels for 20%

profile of v2, /device:TPU:5, one launch (start us, length us, event | category | flops | bytes accessed | tf_op | source)
XLA Modules:
  0.0 220.9 jit_solution(16574979529983017405)
XLA Ops:
  3.8 3.2 %collective-permute-start = (s32[2,5,17]{2,0,1:T(2,128)S(1)}, s32[2,5,17]{2,0,1:T(2,128)S(1)}, u32[]{:S(2)}, u32[]{:S(2)}) collective-permute-start(s32[2,5,17]{2,0,1:T(2,128)S(1)} %add_add_fusion), channel_id=1, source_target_pairs={{0,2},{6,4},{1,3},{7,5},{8,10},{14,12},{9,11},{15,13},{16,18},{22,... | collective-permute-start | bytes 2048 | tf_op jit(solution)/shard_map/ppermute | solution.py:287
  7.0 2.6 %collective-permute-start.2 = (bf16[512,2048]{1,0:T(8,128)(2,1)}, bf16[512,2048]{1,0:T(8,128)(2,1)}, u32[]{:S(2)}, u32[]{:S(2)}) collective-permute-start(bf16[512,2048]{1,0:T(8,128)(2,1)} %bitcast.23.rest_0_.rest_4_), channel_id=1, source_target_pairs={{0,2},{6,4},{1,3},{7,5},{8,10},{14,12},{9,11},{15,13},{16,18},{22,... | collective-permute-start | bytes 6291464 | tf_op jit(solution)/shard_map/ppermute | solution.py:287
  9.7 2.0 constant_dynamic-update-slice_fusion.2
  12.8 1.3 constant_dynamic-update-slice_fusion.1
  15.3 1.2 copy-done.8
  16.6 1.4 collective-permute-start.1
  18.0 2.0 collective-permute-start.3
  21.3 31.7 %collective-permute-done.2.rest_1_.rest_5_ = bf16[512,2048]{1,0:T(8,128)(2,1)} collective-permute-done((bf16[512,2048]{1,0:T(8,128)(2,1)}, bf16[512,2048]{1,0:T(8,128)(2,1)}, u32[]{:S(2)}, u32[]{:S(2)}) %collective-permute-start.2) | collective-permute-done | bytes 2097184 | tf_op jit(solution)/shard_map/ppermute | solution.py:287
  52.9 2.0 collective-permute-start.4
  57.4 37.7 %collective-permute-done.1.theirs.new_theirs.up_theirs.x_theirs = bf16[5,96,2048]{2,1,0:T(8,128)(2,1)S(1)} collective-permute-done((bf16[5,96,2048]{2,1,0:T(8,128)(2,1)}, bf16[5,96,2048]{2,1,0:T(8,128)(2,1)S(1)}, u32[]{:S(2)}, u32[]{:S(2)}) %collective-permute-start.1) | collective-permute-done | bytes 1966112 | tf_op jit(solution)/shard_map/ppermute | solution.py:287
  95.1 4.1 %collective-permute-start.5 = (bf16[512,512]{1,0:T(8,128)(2,1)S(1)}, bf16[512,512]{1,0:T(8,128)(2,1)S(1)}, u32[]{:S(2)}, u32[]{:S(2)}) collective-permute-start(bf16[512,512]{1,0:T(8,128)(2,1)S(1)} %bitcast.91), channel_id=1, source_target_pairs={{0,2},{6,4},{1,3},{7,5},{8,10},{14,12},{9,11},{15,13},{16,18},{22,... | collective-permute-start | bytes 1572872 | tf_op jit(solution)/shard_map/ppermute | solution.py:287
  100.1 8.8 %collective-permute-done.5.rest_1_.rest_5_ = bf16[512,512]{1,0:T(8,128)(2,1)S(1)} collective-permute-done((bf16[512,512]{1,0:T(8,128)(2,1)S(1)}, bf16[512,512]{1,0:T(8,128)(2,1)S(1)}, u32[]{:S(2)}, u32[]{:S(2)}) %collective-permute-start.5) | collective-permute-done | bytes 524320 | tf_op jit(solution)/shard_map/ppermute | solution.py:287
  110.0 14.2 %project.1 = (bf16[3,192,512]{2,1,0:T(8,128)(2,1)S(1)}, f32[2,192,512]{2,1,0:T(8,128)S(1)}, bf16[2,192,1536]{2,1,0:T(8,128)(2,1)}, f32[2,192,2048]{2,1,0:T(8,128...) custom-call(s32[4]{0:T(128)S(1)} %add_multiply_fusion.offs, ...), custom_call_target="tpu_custom_call" | custom-call | tf_op jit(solution)/shard_map/project/pallas_call | solution.py:377
  126.3 2.4 %collective-permute-start.8 = (bf16[2,48,2048]{2,1,0:T(8,128)(2,1)S(1)}, bf16[2,48,2048]{2,1,0:T(8,128)(2,1)S(1)}, u32[]{:S(2)}, u32[]{:S(2)}) collective-permute-start(bf16[2,48,2048]{2,1,0:T(8,128)(2,1)S(1)} %get-tuple-element.31), channel_id=1, source_target_pairs={{0,1},{1,0},{2,3},{3,2},{4,5},{5,4},{6,7},{7,6},{8,9},{9,8},{10,11... | collective-permute-start | bytes 1179656 | tf_op jit(solution)/shard_map/ppermute | solution.py:296
  128.9 9.4 %backward.2 = (bf16[2,48,2048]{2,1,0:T(8,128)(2,1)S(1)}, bf16[2,48,2048]{2,1,0:T(8,128)(2,1)S(1)}) custom-call(s32[1]{0:T(128)} %bitcast.7.core, s32[4]{0:T(128)S(1)} %add_multiply_fusion.offs, bf16[5,96,2048]{2,1,0:T(8,128)(2,1)} %copy-done.8, bf16[5,96,2048]{2,1,0:T(8,128)(2,1)} %copy-done.6, bf16[5,96,2048]{2,1,0:T(8,128)(2,1)} %copy-done.8, ...), custom_call_target="tpu_custom_call" | custom-call | tf_op jit(solution)/shard_map/backward/pallas_call | solution.py:407
  139.4 3.1 %collective-permute-start.10 = (bf16[2,48,2048]{2,1,0:T(8,128)(2,1)S(1)}, bf16[2,48,2048]{2,1,0:T(8,128)(2,1)S(1)}, u32[]{:S(2)}, u32[]{:S(2)}) collective-permute-start(bf16[2,48,2048]{2,1,0:T(8,128)(2,1)S(1)} %add_convert_fusion.3), channel_id=1, source_target_pairs={{0,8},{8,16},{16,24},{1,9},{9,17},{17,25},{2,10},{10,18},{18,26},{... | collective-permute-start | bytes 1179656 | tf_op jit(solution)/shard_map/ppermute | solution.py:300
  142.6 1.3 collective-permute-start.9
  144.0 3.0 %collective-permute-start.16 = (bf16[2,48,2048]{2,1,0:T(8,128)(2,1)S(1)}, bf16[2,48,2048]{2,1,0:T(8,128)(2,1)S(1)}, u32[]{:S(2)}, u32[]{:S(2)}) collective-permute-start(bf16[2,48,2048]{2,1,0:T(8,128)(2,1)S(1)} %add_convert_fusion.1), channel_id=1, source_target_pairs={{8,0},{16,8},{24,16},{9,1},{17,9},{25,17},{10,2},{18,10},{26,18},{... | collective-permute-start | bytes 1179656 | tf_op jit(solution)/shard_map/ppermute | solution.py:300
  147.1 1.5 collective-permute-start.15
  148.6 4.3 %collective-permute-done.10.mine = bf16[2,48,2048]{2,1,0:T(8,128)(2,1)S(1)} collective-permute-done((bf16[2,48,2048]{2,1,0:T(8,128)(2,1)S(1)}, bf16[2,48,2048]{2,1,0:T(8,128)(2,1)S(1)}, u32[]{:S(2)}, u32[]{:S(2)}) %collective-permute-start.10) | collective-permute-done | bytes 393248 | tf_op jit(solution)/shard_map/ppermute | solution.py:300
  154.2 5.3 %collective-permute-done.16.mine = bf16[2,48,2048]{2,1,0:T(8,128)(2,1)S(1)} collective-permute-done((bf16[2,48,2048]{2,1,0:T(8,128)(2,1)S(1)}, bf16[2,48,2048]{2,1,0:T(8,128)(2,1)S(1)}, u32[]{:S(2)}, u32[]{:S(2)}) %collective-permute-start.16) | collective-permute-done | bytes 393248 | tf_op jit(solution)/shard_map/ppermute | solution.py:300
  160.3 8.2 %forward.1 = (bf16[2,48,2048]{2,1,0:T(8,128)(2,1)S(1)}, bf16[2,48,2048]{2,1,0:T(8,128)(2,1)S(1)}) custom-call(s32[1]{0:T(128)} %bitcast.7.core, s32[4]{0:T(128)S(1)} %add_multiply_fusion.offs, s32[1]{0:T(128)} %bitcast.28.fresh, bf16[2,48,2048]{2,1,0:T(8,128)(2,1)S(1)} %collective-permute-done.10.mine, ...), custom_call_target="tpu_custom_call" | custom-call | tf_op jit(solution)/shard_map/forward/pallas_call | solution.py:453
  168.6 3.0 %terms.1 = (bf16[512,512]{1,0:T(8,128)(2,1)S(1)}, bf16[512,512]{1,0:T(8,128)(2,1)S(1)}, bf16[512,512]{1,0:T(8,128)(2,1)S(1)}, bf16[512,512]{1,0:T(8,128)(2,1)S(1)}, bf16[192,2048]{1,0:T(8,128)(2,1)}) custom-call(s32[1]{0:T(128)} %bitcast.7.core, s32[4]{0:T(128)S(1)} %add_multiply_fusion.offs, s32[1]{0:T(128)} %bitcast.36.fresh, ...), custom_call_target="tpu_custom_call" | custom-call | tf_op jit(solution)/shard_map/terms/pallas_call | solution.py:474
  172.8 8.5 %backward.3 = (bf16[2,48,2048]{2,1,0:T(8,128)(2,1)S(1)}, bf16[2,48,2048]{2,1,0:T(8,128)(2,1)S(1)}) custom-call(s32[1]{0:T(128)} %bitcast.7.core, s32[4]{0:T(128)S(1)} %add_multiply_fusion.offs, bf16[2,96,2048]{2,1,0:T(8,128)(2,1)S(1)} %bitcast.97, bf16[2,96,2048]{2,1,0:T(8,128)(2,1)S(1)} %bitcast.98, bf16[5,96,2048]{2,1,0:T(8,128)(2,1)} %copy-done.8, ...), custom_call_target="tpu_custom_call" | custom-call | tf_op jit(solution)/shard_map/backward/pallas_call | solution.py:407
  181.8 1.3 collective-permute-start.20
  183.8 1.3 collective-permute-start.22
  185.7 1.3 collective-permute-start.13
  187.0 1.3 collective-permute-start.19
  188.3 12.1 %collective-permute-done.20 = bf16[512,512]{1,0:T(8,128)(2,1)S(1)} collective-permute-done((bf16[512,512]{1,0:T(8,128)(2,1)S(1)}, bf16[512,512]{1,0:T(8,128)(2,1)S(1)}, u32[]{:S(2)}, u32[]{:S(2)}) %collective-permute-start.20) | collective-permute-done | bytes 524320 | tf_op jit(solution)/shard_map/ppermute | solution.py:290
  200.4 14.2 %collective-permute-done.22 = bf16[512,512]{1,0:T(8,128)(2,1)S(1)} collective-permute-done((bf16[512,512]{1,0:T(8,128)(2,1)S(1)}, bf16[512,512]{1,0:T(8,128)(2,1)S(1)}, u32[]{:S(2)}, u32[]{:S(2)}) %collective-permute-start.22) | collective-permute-done | bytes 524320 | tf_op jit(solution)/shard_map/ppermute | solution.py:497
  214.6 1.3 multiply_bitcast_fusion
  216.7 3.4 %collective-permute-done.19 = bf16[48,2048]{1,0:T(8,128)(2,1)S(1)} collective-permute-done((bf16[48,2048]{1,0:T(8,128)(2,1)S(1)}, bf16[48,2048]{1,0:T(8,128)(2,1)S(1)}, u32[]{:S(2)}, u32[]{:S(2)}) %collective-permute-start.19) | collective-permute-done | bytes 196640 | tf_op jit(solution)/shard_map/ppermute | solution.py:290
  (90 shorter events, 20.0 us)
Async XLA Ops:
  0.6 12.1 %copy-start.10 = (bf16[1,2,96,2048]{3,2,1,0:T(8,128)(2,1)S(1)}, bf16[1,2,96,2048]{3,2,1,0:T(8,128)(2,1)}, u32[]{:S(2)}) copy-start(bf16[1,2,96,2048]{3,2,1,0:T(8,128)(2,1)} %param.16) | copy-start | bytes 2359300
  3.8 11.5 %collective-permute-start = (s32[2,5,17]{2,0,1:T(2,128)S(1)}, s32[2,5,17]{2,0,1:T(2,128)S(1)}, u32[]{:S(2)}, u32[]{:S(2)}) collective-permute-start(s32[2,5,17]{2,0,1:T(2,128)S(1)} %add_add_fusion), channel_id=1, source_target_pairs={{0,2},{6,4},{1,3},{7,5},{8,10},{14,12},{9,11},{15,13},{16,18},{22,... | collective-permute-start | bytes 2048 | tf_op jit(solution)/shard_map/ppermute | solution.py:287
  7.0 45.9 %collective-permute-start.2 = (bf16[512,2048]{1,0:T(8,128)(2,1)}, bf16[512,2048]{1,0:T(8,128)(2,1)}, u32[]{:S(2)}, u32[]{:S(2)}) collective-permute-start(bf16[512,2048]{1,0:T(8,128)(2,1)} %bitcast.23.rest_0_.rest_4_), channel_id=1, source_target_pairs={{0,2},{6,4},{1,3},{7,5},{8,10},{14,12},{9,11},{15,13},{16,18},{22,... | collective-permute-start | bytes 6291464 | tf_op jit(solution)/shard_map/ppermute | solution.py:287
  12.7 7.3 %copy-start.11 = (s32[2]{0:T(128)S(1)}, s32[2]{0:T(128)}, u32[]{:S(2)}) copy-start(s32[2]{0:T(128)} %constant.87.clone) | copy-start | bytes 28
  12.7 82.3 %copy-start = (bf16[1,512,512]{2,1,0:T(8,128)(2,1)S(1)}, bf16[1,512,512]{2,1,0:T(8,128)(2,1)}, u32[]{:S(2)}) copy-start(bf16[1,512,512]{2,1,0:T(8,128)(2,1)} %param.18) | copy-start | bytes 1572868
  16.6 78.5 %collective-permute-start.1 = (bf16[5,96,2048]{2,1,0:T(8,128)(2,1)}, bf16[5,96,2048]{2,1,0:T(8,128)(2,1)S(1)}, u32[]{:S(2)}, u32[]{:S(2)}) collective-permute-start(bf16[5,96,2048]{2,1,0:T(8,128)(2,1)} %copy-done.8), channel_id=1, source_target_pairs={{0,2},{6,4},{1,3},{7,5},{8,10},{14,12},{9,11},{15,13},{16,18},{22,... | collective-permute-start | bytes 5898248 | tf_op jit(solution)/shard_map/ppermute | solution.py:287
  18.0 81.5 %collective-permute-start.3 = (bf16[512,2048]{1,0:T(8,128)(2,1)}, bf16[512,2048]{1,0:T(8,128)(2,1)}, u32[]{:S(2)}, u32[]{:S(2)}) collective-permute-start(bf16[512,2048]{1,0:T(8,128)(2,1)} %bitcast.23.rest_0_.rest_4_), channel_id=1, source_target_pairs={{4,2},{2,4},{5,3},{3,5},{12,10},{10,12},{13,11},{11,13},{20,18},{1... | collective-permute-start | bytes 6291464 | tf_op jit(solution)/shard_map/ppermute | solution.py:293
  52.9 57.1 %collective-permute-start.4 = (bf16[512,2048]{1,0:T(8,128)(2,1)}, bf16[512,2048]{1,0:T(8,128)(2,1)}, u32[]{:S(2)}, u32[]{:S(2)}) collective-permute-start(bf16[512,2048]{1,0:T(8,128)(2,1)} %collective-permute-done.2.rest_1_.rest_5_), channel_id=1, source_target_pairs={{4,2},{2,4},{5,3},{3,5},{12,10},{10,12},{13,11},{11,13},{20,18},{1... | collective-permute-start | bytes 6291464 | tf_op jit(solution)/shard_map/ppermute | solution.py:293
  95.1 15.0 %copy-start.6 = (bf16[5,96,2048]{2,1,0:T(8,128)(2,1)}, bf16[5,96,2048]{2,1,0:T(8,128)(2,1)S(1)}, u32[]{:S(2)}) copy-start(bf16[5,96,2048]{2,1,0:T(8,128)(2,1)S(1)} %collective-permute-done.1.theirs.new_theirs.up_theirs.x_theirs) | copy-start | bytes 5898244
  95.1 13.9 %collective-permute-start.5 = (bf16[512,512]{1,0:T(8,128)(2,1)S(1)}, bf16[512,512]{1,0:T(8,128)(2,1)S(1)}, u32[]{:S(2)}, u32[]{:S(2)}) collective-permute-start(bf16[512,512]{1,0:T(8,128)(2,1)S(1)} %bitcast.91), channel_id=1, source_target_pairs={{0,2},{6,4},{1,3},{7,5},{8,10},{14,12},{9,11},{15,13},{16,18},{22,... | collective-permute-start | bytes 1572872 | tf_op jit(solution)/shard_map/ppermute | solution.py:287
  99.4 25.7 %collective-permute-start.6 = (bf16[512,512]{1,0:T(8,128)(2,1)S(1)}, bf16[512,512]{1,0:T(8,128)(2,1)S(1)}, u32[]{:S(2)}, u32[]{:S(2)}) collective-permute-start(bf16[512,512]{1,0:T(8,128)(2,1)S(1)} %bitcast.92), channel_id=1, source_target_pairs={{4,2},{2,4},{5,3},{3,5},{12,10},{10,12},{13,11},{11,13},{20,18},{1... | collective-permute-start | bytes 1572872 | tf_op jit(solution)/shard_map/ppermute | solution.py:293
  108.9 16.2 %collective-permute-start.7 = (bf16[512,512]{1,0:T(8,128)(2,1)S(1)}, bf16[512,512]{1,0:T(8,128)(2,1)S(1)}, u32[]{:S(2)}, u32[]{:S(2)}) collective-permute-start(bf16[512,512]{1,0:T(8,128)(2,1)S(1)} %collective-permute-done.5.rest_1_.rest_5_), channel_id=1, source_target_pairs={{4,2},{2,4},{5,3},{3,5},{12,10},{10,12},{13,11},{11,13},{20,18},{1... | collective-permute-start | bytes 1572872 | tf_op jit(solution)/shard_map/ppermute | solution.py:293
  110.0 14.2 %copy-start.1 = (f32[4,192,192]{2,1,0:T(8,128)}, f32[4,192,192]{2,1,0:T(8,128)S(1)}, u32[]{:S(2)}) copy-start(f32[4,192,192]{2,1,0:T(8,128)S(1)} %select_maximum_fusion.keep) | copy-start | bytes 1769476
  125.1 3.7 %copy-start.4 = (bf16[2,4,192,192]{3,2,1,0:T(8,128)(2,1)}, bf16[2,4,192,192]{3,2,1,0:T(8,128)(2,1)S(1)}, u32[]{:S(2)}) copy-start(bf16[2,4,192,192]{3,2,1,0:T(8,128)(2,1)S(1)} %get-tuple-element.38.probs) | copy-start | bytes 1769476
  125.1 3.7 %copy-start.2 = (f32[2,192,512]{2,1,0:T(8,128)}, f32[2,192,512]{2,1,0:T(8,128)S(1)}, u32[]{:S(2)}) copy-start(f32[2,192,512]{2,1,0:T(8,128)S(1)} %get-tuple-element.34.gate) | copy-start | bytes 2359300
  125.1 3.6 %copy-start.7 = (bf16[5,96,2048]{2,1,0:T(8,128)(2,1)S(1)}, bf16[5,96,2048]{2,1,0:T(8,128)(2,1)}, u32[]{:S(2)}) copy-start(bf16[5,96,2048]{2,1,0:T(8,128)(2,1)} %copy-done.6) | copy-start | bytes 5898244
  126.3 12.9 %collective-permute-start.8 = (bf16[2,48,2048]{2,1,0:T(8,128)(2,1)S(1)}, bf16[2,48,2048]{2,1,0:T(8,128)(2,1)S(1)}, u32[]{:S(2)}, u32[]{:S(2)}) collective-permute-start(bf16[2,48,2048]{2,1,0:T(8,128)(2,1)S(1)} %get-tuple-element.31), channel_id=1, source_target_pairs={{0,1},{1,0},{2,3},{3,2},{4,5},{5,4},{6,7},{7,6},{8,9},{9,8},{10,11... | collective-permute-start | bytes 1179656 | tf_op jit(solution)/shard_map/ppermute | solution.py:296
  128.9 10.3 %copy-start.9 = (bf16[1,96,2048]{2,1,0:T(8,128)(2,1)S(1)}, bf16[1,96,2048]{2,1,0:T(8,128)(2,1)}, u32[]{:S(2)}) copy-start(bf16[1,96,2048]{2,1,0:T(8,128)(2,1)} %get-tuple-element.54) | copy-start | bytes 1179652
  138.3 5.5 %collective-permute-start.14 = (bf16[2,48,2048]{2,1,0:T(8,128)(2,1)S(1)}, bf16[2,48,2048]{2,1,0:T(8,128)(2,1)S(1)}, u32[]{:S(2)}, u32[]{:S(2)}) collective-permute-start(bf16[2,48,2048]{2,1,0:T(8,128)(2,1)S(1)} %get-tuple-element.41), channel_id=1, source_target_pairs={{0,1},{1,0},{2,3},{3,2},{4,5},{5,4},{6,7},{7,6},{8,9},{9,8},{10,11... | collective-permute-start | bytes 1179656 | tf_op jit(solution)/shard_map/ppermute | solution.py:296
  139.4 13.5 %collective-permute-start.10 = (bf16[2,48,2048]{2,1,0:T(8,128)(2,1)S(1)}, bf16[2,48,2048]{2,1,0:T(8,128)(2,1)S(1)}, u32[]{:S(2)}, u32[]{:S(2)}) collective-permute-start(bf16[2,48,2048]{2,1,0:T(8,128)(2,1)S(1)} %add_convert_fusion.3), channel_id=1, source_target_pairs={{0,8},{8,16},{16,24},{1,9},{9,17},{17,25},{2,10},{10,18},{18,26},{... | collective-permute-start | bytes 1179656 | tf_op jit(solution)/shard_map/ppermute | solution.py:300
  142.6 17.7 %collective-permute-start.9 = (bf16[48,2048]{1,0:T(8,128)(2,1)S(1)}, bf16[48,2048]{1,0:T(8,128)(2,1)S(1)}, u32[]{:S(2)}, u32[]{:S(2)}) collective-permute-start(bf16[48,2048]{1,0:T(8,128)(2,1)S(1)} %slice_bitcast_fusion.6), channel_id=1, source_target_pairs={{2,0},{4,6},{3,1},{5,7},{10,8},{12,14},{11,9},{13,15},{18,16},{20,... | collective-permute-start | bytes 589832 | tf_op jit(solution)/shard_map/ppermute | solution.py:290
  144.0 15.4 %collective-permute-start.16 = (bf16[2,48,2048]{2,1,0:T(8,128)(2,1)S(1)}, bf16[2,48,2048]{2,1,0:T(8,128)(2,1)S(1)}, u32[]{:S(2)}, u32[]{:S(2)}) collective-permute-start(bf16[2,48,2048]{2,1,0:T(8,128)(2,1)S(1)} %add_convert_fusion.1), channel_id=1, source_target_pairs={{8,0},{16,8},{24,16},{9,1},{17,9},{25,17},{10,2},{18,10},{26,18},{... | collective-permute-start | bytes 1179656 | tf_op jit(solution)/shard_map/ppermute | solution.py:300
  147.1 34.7 %collective-permute-start.15 = (bf16[48,2048]{1,0:T(8,128)(2,1)S(1)}, bf16[48,2048]{1,0:T(8,128)(2,1)S(1)}, u32[]{:S(2)}, u32[]{:S(2)}) collective-permute-start(bf16[48,2048]{1,0:T(8,128)(2,1)S(1)} %slice_bitcast_fusion.2), channel_id=1, source_target_pairs={{2,0},{4,6},{3,1},{5,7},{10,8},{12,14},{11,9},{13,15},{18,16},{20,... | collective-permute-start | bytes 589832 | tf_op jit(solution)/shard_map/ppermute | solution.py:290
  152.9 7.4 %collective-permute-start.11 = (bf16[2,48,2048]{2,1,0:T(8,128)(2,1)S(1)}, bf16[2,48,2048]{2,1,0:T(8,128)(2,1)S(1)}, u32[]{:S(2)}, u32[]{:S(2)}) collective-permute-start(bf16[2,48,2048]{2,1,0:T(8,128)(2,1)S(1)} %collective-permute-done.10.mine), channel_id=1, source_target_pairs={{0,1},{1,0},{2,3},{3,2},{4,5},{5,4},{6,7},{7,6},{8,9},{9,8},{10,11... | collective-permute-start | bytes 1179656 | tf_op jit(solution)/shard_map/ppermute | solution.py:296
  159.5 9.2 %collective-permute-start.17 = (bf16[2,48,2048]{2,1,0:T(8,128)(2,1)S(1)}, bf16[2,48,2048]{2,1,0:T(8,128)(2,1)S(1)}, u32[]{:S(2)}, u32[]{:S(2)}) collective-permute-start(bf16[2,48,2048]{2,1,0:T(8,128)(2,1)S(1)} %collective-permute-done.16.mine), channel_id=1, source_target_pairs={{0,1},{1,0},{2,3},{3,2},{4,5},{5,4},{6,7},{7,6},{8,9},{9,8},{10,11... | collective-permute-start | bytes 1179656 | tf_op jit(solution)/shard_map/ppermute | solution.py:296
  168.5 16.6 %collective-permute-start.12 = (bf16[2,48,2048]{2,1,0:T(8,128)(2,1)S(1)}, bf16[2,48,2048]{2,1,0:T(8,128)(2,1)S(1)}, u32[]{:S(2)}, u32[]{:S(2)}) collective-permute-start(bf16[2,48,2048]{2,1,0:T(8,128)(2,1)S(1)} %get-tuple-element.33), channel_id=1, source_target_pairs={{0,1},{1,0},{2,3},{3,2},{4,5},{5,4},{6,7},{7,6},{8,9},{9,8},{10,11... | collective-permute-start | bytes 1179656 | tf_op jit(solution)/shard_map/ppermute | solution.py:296
  181.3 3.9 %collective-permute-start.18 = (bf16[2,48,2048]{2,1,0:T(8,128)(2,1)S(1)}, bf16[2,48,2048]{2,1,0:T(8,128)(2,1)S(1)}, u32[]{:S(2)}, u32[]{:S(2)}) collective-permute-start(bf16[2,48,2048]{2,1,0:T(8,128)(2,1)S(1)} %get-tuple-element.44), channel_id=1, source_target_pairs={{0,1},{1,0},{2,3},{3,2},{4,5},{5,4},{6,7},{7,6},{8,9},{9,8},{10,11... | collective-permute-start | bytes 1179656 | tf_op jit(solution)/shard_map/ppermute | solution.py:296
  181.8 18.6 %collective-permute-start.20 = (bf16[512,512]{1,0:T(8,128)(2,1)S(1)}, bf16[512,512]{1,0:T(8,128)(2,1)S(1)}, u32[]{:S(2)}, u32[]{:S(2)}) collective-permute-start(bf16[512,512]{1,0:T(8,128)(2,1)S(1)} %get-tuple-element.46), channel_id=1, source_target_pairs={{2,0},{4,6},{3,1},{5,7},{10,8},{12,14},{11,9},{13,15},{18,16},{20,... | collective-permute-start | bytes 1572872 | tf_op jit(solution)/shard_map/ppermute | solution.py:290
  183.1 17.3 %collective-permute-start.21 = (bf16[512,512]{1,0:T(8,128)(2,1)S(1)}, bf16[512,512]{1,0:T(8,128)(2,1)S(1)}, u32[]{:S(2)}, u32[]{:S(2)}) collective-permute-start(bf16[512,512]{1,0:T(8,128)(2,1)S(1)} %get-tuple-element.47), channel_id=1, source_target_pairs={{4,2},{2,4},{5,3},{3,5},{12,10},{10,12},{13,11},{11,13},{20,18},{1... | collective-permute-start | bytes 1572872 | tf_op jit(solution)/shard_map/ppermute | solution.py:293
  183.8 30.8 %collective-permute-start.22 = (bf16[512,512]{1,0:T(8,128)(2,1)S(1)}, bf16[512,512]{1,0:T(8,128)(2,1)S(1)}, u32[]{:S(2)}, u32[]{:S(2)}) collective-permute-start(bf16[512,512]{1,0:T(8,128)(2,1)S(1)} %get-tuple-element.48), channel_id=1, source_target_pairs={{4,0},{2,6},{5,1},{3,7},{12,8},{10,14},{13,9},{11,15},{20,16},{18,... | collective-permute-start | bytes 1572872 | tf_op jit(solution)/shard_map/ppermute | solution.py:497
  185.7 30.2 %collective-permute-start.13 = (bf16[48,2048]{1,0:T(8,128)(2,1)S(1)}, bf16[48,2048]{1,0:T(8,128)(2,1)S(1)}, u32[]{:S(2)}, u32[]{:S(2)}) collective-permute-start(bf16[48,2048]{1,0:T(8,128)(2,1)S(1)} %slice_bitcast_fusion.4), channel_id=1, source_target_pairs={{2,0},{4,6},{3,1},{5,7},{10,8},{12,14},{11,9},{13,15},{18,16},{20,... | collective-permute-start | bytes 589832 | tf_op jit(solution)/shard_map/ppermute | solution.py:290
  187.0 33.0 %collective-permute-start.19 = (bf16[48,2048]{1,0:T(8,128)(2,1)S(1)}, bf16[48,2048]{1,0:T(8,128)(2,1)S(1)}, u32[]{:S(2)}, u32[]{:S(2)}) collective-permute-start(bf16[48,2048]{1,0:T(8,128)(2,1)S(1)} %slice_bitcast_fusion), channel_id=1, source_target_pairs={{2,0},{4,6},{3,1},{5,7},{10,8},{12,14},{11,9},{13,15},{18,16},{20,... | collective-permute-start | bytes 589832 | tf_op jit(solution)/shard_map/ppermute | solution.py:290
  (3 other events, 3.3 us)

commit v3 on v2

v3 whole, which is shorter than its diff:
```python
import functools

import jax
import jax.numpy as jnp
from jax import lax
from jax.experimental import pallas as pl
from jax.experimental.pallas import tpu as pltpu
from jax.sharding import PartitionSpec as P

HEAD_DIM = 128
BLOCK = 24
BLOCKS = 4
EPSILON = 1e-06
SCALING = HEAD_DIM ** (-0.5)
VMEM_BYTES = 24 * 1024 * 1024

F32 = jnp.float32
BF16 = jnp.bfloat16


def dot(a, b):
    return lax.dot_general(a, b, (((1,), (0,)), ((), ())), preferred_element_type=F32)


def dot_nt(a, b):
    return lax.dot_general(a, b, (((1,), (1,)), ((), ())), preferred_element_type=F32)


def dot_tn(a, b):
    return lax.dot_general(a, b, (((0,), (0,)), ((), ())), preferred_element_type=F32)


def row_root(floats):
    return lax.rsqrt(jnp.mean(floats * floats, axis=-1, keepdims=True) + EPSILON)


def sigmoid(x):
    return 1.0 / (1.0 + jnp.exp(-x))


def attend(pre, keep):
    sig = sigmoid(pre)
    active = pre * sig
    gate = active[:, :HEAD_DIM]
    vqk = active[:, HEAD_DIM:].astype(BF16)
    value = vqk[:, :HEAD_DIM]
    query = vqk[:, HEAD_DIM : 2 * HEAD_DIM]
    key = vqk[:, 2 * HEAD_DIM :]
    scores = dot_nt(query, key) * SCALING
    sig_s = sigmoid(scores)
    probs = (scores * sig_s * keep).astype(BF16)
    mixed = dot(probs, value)
    gated = (mixed * row_root(mixed) * gate).astype(BF16)
    return sig, gate, vqk, scores, sig_s, probs, mixed, gated


def project_kernel(n, heads, offs, x_own, x_theirs, stash_own, stash_theirs, keep, *rest):
    weights = rest[:n]
    gated_out, gate_out, vqk_out, slope_out, mixed_out, probs_out, factor_out, normed = rest[n:]
    depth = weights[0].shape[0]
    length = x_own.shape[0]
    rows = 2 * length
    wide = 4 * HEAD_DIM
    head = pl.program_id(0)

    @pl.when(head == 0)
    def _():
        sources = [x_own, x_theirs]
        for t in range(stash_own.shape[0]):
            sources += [stash_own.at[t], stash_theirs.at[t]]
        for i, source in enumerate(sources):
            floats = source[...].astype(F32)
            normed[pl.ds(i * length, length), :] = (floats * row_root(floats)).astype(BF16)

    here = pl.ds(pl.multiple_of(head * wide, wide), wide)
    pre_all = None
    for j in range(n):
        columns = pl.ds(pl.multiple_of(offs[j], depth), depth)
        term = dot(normed[:, columns], weights[j][:, here])
        pre_all = term if pre_all is None else pre_all + term
    for i in range(1 + stash_own.shape[0]):
        pre = pre_all[i * rows : (i + 1) * rows]
        kept = keep[i]
        sig, gate, vqk, scores, sig_s, probs, mixed, gated = attend(pre, kept)
        gated_out[i] = gated
        if i > 0:
            gate_out[i - 1] = gate
            vqk_out[i - 1] = vqk
            slope_out[i - 1] = sig * (1.0 + pre * (1.0 - sig))
            mixed_out[i - 1] = mixed
            probs_out[i - 1, 0] = probs
            factor_out[i - 1, 0] = kept * sig_s * (1.0 + scores * (1.0 - sig_s)) * SCALING


def split_rows(core, part, send, keep):
    share = send.shape[1]
    cores = part.shape[0] // (2 * share)
    for r in range(2):
        base = r * cores * share
        mine = pl.multiple_of(base + core * share, share)
        other = pl.multiple_of(base + (cores - 1 - core) * share, share)
        send[r] = part[pl.ds(other, share), :]
        keep[r] = part[pl.ds(mine, share), :]


def out_kernel(n, core, offs, gated, *rest):
    weights = rest[:n]
    send, keep, part = rest[n:]
    depth = weights[0].shape[1]
    for j in range(n):
        columns = pl.ds(pl.multiple_of(offs[j], depth), depth)
        part[:, columns] = dot(gated[0], weights[j][...]).astype(BF16)
    split_rows(core[0], part, send, keep)


def assemble(core, fresh, mine, theirs, new_own, new_theirs, whole):
    share = mine.shape[1]
    length = new_own.shape[0]
    cores = length // share
    use_fresh = fresh != 0
    for r, source in enumerate((new_own, new_theirs)):
        for owner, landed in ((core, mine), (cores - 1 - core, theirs)):
            inside = pl.multiple_of(owner * share, share)
            rows = source[pl.ds(inside, share), :]
            at = pl.multiple_of(r * length + owner * share, share)
            whole[pl.ds(at, share), :] = jnp.where(use_fresh, rows, landed[r])


def forward_kernel(n, heads, core, offs, fresh, mine, theirs, new_own, new_theirs, keep, *rest):
    in_parts = rest[:n]
    out_parts = rest[n : 2 * n]
    send, kept, whole, normed, gated, part = rest[2 * n :]
    depth = in_parts[0].shape[0]
    head = pl.program_id(0)

    @pl.when(head == 0)
    def _():
        assemble(core[0], fresh[0], mine, theirs, new_own, new_theirs, whole)
        floats = whole[...].astype(F32)
        normed[...] = (floats * row_root(floats)).astype(BF16)

    wide = 4 * HEAD_DIM
    here = pl.ds(pl.multiple_of(head * wide, wide), wide)
    pre = None
    for j in range(n):
        columns = pl.ds(pl.multiple_of(offs[j], depth), depth)
        term = dot(normed[:, columns], in_parts[j][:, here])
        pre = term if pre is None else pre + term
    gated[head] = attend(pre, keep[keep.shape[0] - 1])[-1]

    @pl.when(head == heads - 1)
    def _():
        for j in range(n):
            columns = pl.ds(pl.multiple_of(offs[j], depth), depth)
            total = None
            for h in range(heads):
                term = dot(gated[h], out_parts[j][pl.ds(h * HEAD_DIM, HEAD_DIM), :])
                total = term if total is None else total + term
            part[:, columns] = total.astype(BF16)
        split_rows(core[0], part, send, kept)


def backward_kernel(
    n, heads, tick, core, offs, ups, x_own, x_theirs, gate, vqk, slope, mixed, probs, factor, *rest
):
    out_parts = rest[:n]
    in_parts = rest[n : 2 * n]
    send, keep, grad_normed, part = rest[2 * n :]
    depth = out_parts[0].shape[1]
    length = x_own.shape[1]
    wide = 4 * HEAD_DIM
    grad_gated = None
    for j in range(n):
        columns = pl.ds(pl.multiple_of(offs[j], depth), depth)
        term = dot_nt(ups[:, columns], out_parts[j][...])
        grad_gated = term if grad_gated is None else grad_gated + term
    grad_gated = grad_gated.astype(BF16).astype(F32)
    grads_pre = []
    for h in range(heads):
        cut = slice(h * HEAD_DIM, (h + 1) * HEAD_DIM)
        up = grad_gated[:, cut]
        mixed_h = mixed[tick, :, cut]
        root = row_root(mixed_h)
        normed = mixed_h * root
        grad_n = up * gate[tick, :, cut]
        grad_gate = up * normed
        grad_mixed = root * (grad_n - normed * jnp.mean(grad_n * normed, axis=-1, keepdims=True))
        low = grad_mixed.astype(BF16)
        base = 3 * h * HEAD_DIM
        value = vqk[tick, :, base : base + HEAD_DIM]
        query = vqk[tick, :, base + HEAD_DIM : base + 2 * HEAD_DIM]
        key = vqk[tick, :, base + 2 * HEAD_DIM : base + 3 * HEAD_DIM]
        grad_scores = (dot_nt(low, value) * factor[tick, h]).astype(BF16)
        grad_value = dot_tn(probs[tick, h], low)
        grad_query = dot(grad_scores, key)
        grad_key = dot_tn(grad_scores, query)
        grad_active = jnp.concatenate([grad_gate, grad_value, grad_query, grad_key], axis=1)
        grads_pre.append((grad_active * slope[tick, :, h * wide : (h + 1) * wide]).astype(BF16))
    grad_pre = jnp.concatenate(grads_pre, axis=1)
    for j in range(n):
        columns = pl.ds(pl.multiple_of(offs[j], depth), depth)
        grad_normed[:, columns] = dot_nt(grad_pre, in_parts[j][...])
    for r, source in enumerate((x_own, x_theirs)):
        rows = pl.ds(r * length, length)
        floats = source[tick].astype(F32)
        root = row_root(floats)
        scaled = floats * root
        grad_n = grad_normed[rows, :]
        part[rows, :] = (
            root * (grad_n - scaled * jnp.mean(grad_n * scaled, axis=-1, keepdims=True))
        ).astype(BF16)
    split_rows(core[0], part, send, keep)


def pack_kernel(n, offs, gated, up_own, up_theirs, whole, *packs):
    depth = packs[0].shape[1] - 2 * gated.shape[2]
    slab = gated.shape[2]
    length = up_own.shape[0]
    whole[:length, :] = up_own[...]
    whole[length:, :] = up_theirs[...]
    for j in range(1, n):
        pack = packs[j - 1]
        columns = pl.ds(pl.multiple_of(offs[j], depth), depth)
        pack[:, :slab] = gated[1]
        pack[:, slab : 2 * slab] = gated[2]
        pack[:length, 2 * slab :] = up_own[:, columns]
        pack[length:, 2 * slab :] = up_theirs[:, columns]


def gather_kernel(n, core, offs, fresh, mine, theirs, new_own, new_theirs, whole, *pieces):
    assemble(core[0], fresh[0], mine, theirs, new_own, new_theirs, whole)
    depth = pieces[0].shape[1]
    for j in range(1, n):
        columns = pl.ds(pl.multiple_of(offs[j], depth), depth)
        pieces[j - 1][...] = whole[:, columns]


def grads_kernel(n, scaling, host, offs, gated, up_0, up_1, *rest):
    packs = rest[: n - 1]
    pieces = rest[n - 1 : 2 * n - 2]
    out = rest[2 * n - 2]
    slab = gated.shape[2]
    depth = out.shape[1]
    at_host = host[0] != 0
    columns = pl.ds(pl.multiple_of(offs[0], depth), depth)

    def product(first, second, third, fourth):
        return dot_tn(first, third) + dot_tn(second, fourth)

    total = product(
        jnp.where(at_host, gated[1], packs[0][:, :slab]),
        jnp.where(at_host, gated[2], packs[0][:, slab : 2 * slab]),
        jnp.where(at_host, up_0[:, columns], packs[0][:, 2 * slab :]),
        jnp.where(at_host, up_1[:, columns], pieces[0][...]),
    )
    for m in range(1, n // 2):
        near, beyond = m, n // 2 + m - 1
        pack = jnp.where(at_host, packs[near][...], packs[beyond][...])
        piece = jnp.where(at_host, pieces[near][...], pieces[beyond][...])
        total = total + product(
            pack[:, :slab], pack[:, slab : 2 * slab], pack[:, 2 * slab :], piece
        )
    out[...] = total * scaling


def after(value, *earlier):
    return lax.optimization_barrier((value,) + earlier)[0]


def block_keep(live_blocks, block_marks):
    length = BLOCKS * BLOCK
    places = jnp.arange(length, dtype=jnp.int32)
    owners = places // BLOCK
    marked = jnp.repeat(jnp.repeat(block_marks, BLOCK, axis=-2), BLOCK, axis=-1) == 1
    allowed = (owners[:, None] == owners[None, :]) | marked
    causal = places[:, None] >= places[None, :]
    tokens = live_blocks[..., None, None] * BLOCK
    keeping = causal & allowed & (places[:, None] < tokens) & (places[None, :] < tokens)
    return jnp.where(keeping, 1.0 / jnp.maximum(tokens, 1).astype(F32), 0.0)


def per_device(
    arrivals,
    in_flight,
    cotangent,
    grad_flight,
    stashed,
    in_weight,
    out_weight,
    forward_blocks,
    backward_blocks,
    forward_marks,
    backward_marks,
):
    section_no = lax.axis_index("section")
    sections = lax.axis_size("section")
    core_no = lax.axis_index("cores")
    cores = lax.axis_size("cores")
    dp_no = lax.axis_index("dp")
    n = lax.axis_size("dp")
    ticks = arrivals.shape[0]
    length = arrivals.shape[1]
    width = arrivals.shape[2]
    rows = 2 * length
    share = length // cores
    in_shard = in_weight[0]
    out_shard = out_weight[0]
    depth = in_shard.shape[0]
    slab = out_shard.shape[0]
    heads = slab // HEAD_DIM
    wide = 4 * HEAD_DIM

    hosts = [2 * k + 1 if 4 * k < n - 2 else 2 * k for k in range(n // 2)]
    host_table = jnp.array(hosts, jnp.int32)
    is_host = dp_no == host_table[dp_no // 2]

    def from_partner(x):
        return lax.ppermute(x, "dp", [(h ^ 1, h) for h in hosts])

    def to_partner(x):
        return lax.ppermute(x, "dp", [(h, h ^ 1) for h in hosts])

    def from_host(x, m):
        return lax.ppermute(x, "dp", [(hosts[k ^ m], hosts[k]) for k in range(n // 2)])

    def to_beyond(x, m):
        return lax.ppermute(
            x, "dp", [(hosts[k ^ m], hosts[k] ^ 1) for k in range(n // 2)]
        )

    def swap_cores(x):
        return lax.ppermute(x, "cores", [(c, cores - 1 - c) for c in range(cores)])

    def along_sections(x, by):
        pairs = [(i, i + by) for i in range(sections) if 0 <= i + by < sections]
        return lax.ppermute(x, "section", pairs)

    first_section = section_no == 0
    last_section = section_no == sections - 1
    between = range(1, n // 2)

    in_near = from_partner(in_shard)
    in_far = [from_host(in_shard, m) for m in between]
    in_near, in_far, rows_in, tables_in = lax.optimization_barrier(
        (
            in_near,
            in_far,
            (arrivals, in_flight, cotangent, grad_flight, stashed),
            (forward_blocks, forward_marks, backward_blocks, backward_marks),
        )
    )
    in_parts = [in_shard, in_near] + in_far + [from_host(in_near, m) for m in between]
    arrivals, in_flight, cotangent, grad_flight, stashed = rows_in
    tables = jnp.concatenate(
        [
            jnp.concatenate([b[..., None], m.reshape(m.shape[:2] + (-1,))], axis=-1)
            for b, m in (tables_in[:2], tables_in[2:])
        ],
        axis=0,
    )
    near_tables = from_partner(tables)
    stash_own = stashed[0]
    stash_theirs = from_partner(stash_own)
    x_own = jnp.where(first_section, arrivals[0], in_flight[0])
    x_theirs = from_partner(x_own)
    up_own = jnp.where(last_section, cotangent[0], grad_flight[0])
    new_own = jnp.where(first_section, arrivals[1], cotangent[1])
    out_late, up_late, new_late, stash_theirs, x_theirs = lax.optimization_barrier(
        (out_shard, up_own, new_own, stash_theirs, x_theirs)
    )
    out_near = from_partner(out_late)
    out_far = [from_host(out_late, m) for m in between]
    up_theirs = from_partner(up_late)
    new_theirs = from_partner(new_late)
    out_parts = [out_shard, out_near] + out_far + [from_host(out_near, m) for m in between]
    owners = [dp_no, dp_no ^ 1]
    owners += [host_table[(dp_no // 2) ^ m] for m in range(1, n // 2)]
    owners += [host_table[(dp_no // 2) ^ m] ^ 1 for m in range(1, n // 2)]
    offs = jnp.stack(owners).astype(jnp.int32) * depth
    core = jnp.reshape(core_no, (1,)).astype(jnp.int32)
    first_flag = jnp.reshape(first_section, (1,)).astype(jnp.int32)
    host_flag = jnp.reshape(is_host, (1,)).astype(jnp.int32)
    last_flag = jnp.reshape(last_section, (1,)).astype(jnp.int32)

    both_tables = jnp.stack([tables, near_tables], axis=1)
    ahead_at = sections - 1 - section_no
    chosen = jnp.stack(
        [
            lax.dynamic_index_in_dim(both_tables[way], at, axis=1, keepdims=False)
            for way, at in (
                (0, ahead_at),
                (1, section_no),
                (1, section_no + 1),
                (0, ahead_at + 1),
            )
        ]
    )
    kept = block_keep(chosen[..., 0], chosen[..., 1:].reshape(-1, 2, BLOCKS, BLOCKS))
    blank = jnp.zeros_like(kept[:, 0])
    keep = jnp.concatenate(
        [
            jnp.concatenate([kept[:, 0], blank], axis=2),
            jnp.concatenate([blank, kept[:, 1]], axis=2),
        ],
        axis=1,
    )

    smem = pl.BlockSpec(memory_space=pltpu.SMEM)
    vmem = pl.BlockSpec(memory_space=pltpu.VMEM)
    params = pltpu.CompilerParams(vmem_limit_bytes=VMEM_BYTES)

    def cost(multiply_adds, bytes_accessed):
        return pl.CostEstimate(
            flops=2 * multiply_adds, bytes_accessed=bytes_accessed, transcendentals=0
        )

    def struct(shape, dtype):
        return jax.ShapeDtypeStruct(shape, dtype)

    halves = [struct((2, share, width), BF16)] * 2
    matmul = rows * width * 4 * slab
    weight_bytes = 2 * width * 5 * slab

    by_head = lambda lead, last: pl.BlockSpec(lead + (last,), lambda h: (0,) * len(lead) + (h,))
    square = pl.BlockSpec((2, 1, rows, rows), lambda h: (0, h, 0, 0))
    gated, gate, vqk, slope, mixed, probs, factor = pl.pallas_call(
        functools.partial(project_kernel, n, heads),
        grid=(heads,),
        in_specs=[smem] + [vmem] * (5 + n),
        out_specs=[
            by_head((3, rows), HEAD_DIM),
            by_head((2, rows), HEAD_DIM),
            by_head((2, rows), 3 * HEAD_DIM),
            by_head((2, rows), wide),
            by_head((2, rows), HEAD_DIM),
            square,
            square,
        ],
        out_shape=[
            struct((3, rows, slab), BF16),
            struct((2, rows, slab), F32),
            struct((2, rows, 3 * slab), BF16),
            struct((2, rows, 4 * slab), F32),
            struct((2, rows, slab), F32),
            struct((2, heads, rows, rows), BF16),
            struct((2, heads, rows, rows), F32),
        ],
        scratch_shapes=[pltpu.VMEM((3 * rows, width), BF16)],
        compiler_params=params,
        cost_estimate=cost(3 * matmul, 2 * weight_bytes),
        name="project",
    )(offs, x_own, x_theirs, stash_own, stash_theirs, keep, *in_parts)

    def backward(ups, tick_no):
        saved = [gate, vqk, slope, mixed, probs, factor]
        return pl.pallas_call(
            functools.partial(backward_kernel, n, heads, tick_no),
            in_specs=[smem] * 2 + [vmem] * (3 + len(saved) + 2 * n),
            out_specs=[vmem] * 2,
            out_shape=halves,
            scratch_shapes=[
                pltpu.VMEM((rows, width), F32),
                pltpu.VMEM((rows, width), BF16),
            ],
            compiler_params=params,
            cost_estimate=cost(2 * matmul, 2 * weight_bytes),
            name="backward",
        )(core, offs, ups, stash_own, stash_theirs, *saved, *out_parts, *in_parts)

    gated, new_theirs = lax.optimization_barrier((gated, new_theirs))

    def summed(residual, mine, landed):
        return (residual.astype(F32) + mine.astype(F32) + landed.astype(F32)).astype(BF16)

    def own_rows(mine, others):
        return lax.dynamic_slice_in_dim(jnp.stack([mine, others]), core_no * share, share, axis=1)

    up_0, *packs = pl.pallas_call(
        functools.partial(pack_kernel, n),
        in_specs=[smem] + [vmem] * 3,
        out_specs=[vmem] * n,
        out_shape=[struct((rows, width), BF16)]
        + [struct((rows, 2 * slab + depth), BF16)] * (n - 1),
        compiler_params=params,
        name="pack",
    )(offs, gated, up_own, up_theirs)
    packs, out_parts = lax.optimization_barrier((packs, out_parts))

    ahead_send, ahead_keep = pl.pallas_call(
        functools.partial(out_kernel, n),
        in_specs=[smem] * 2 + [vmem] * (1 + n),
        out_specs=[vmem] * 2,
        out_shape=halves,
        scratch_shapes=[pltpu.VMEM((rows, width), BF16)],
        compiler_params=params,
        cost_estimate=cost(matmul // 4, weight_bytes // 4),
        name="out",
    )(core, offs, gated, *out_parts)
    ahead_0 = summed(own_rows(x_own, x_theirs), ahead_keep, swap_cores(ahead_send))
    ahead_in = along_sections(ahead_0, 1)
    packs_near = [to_partner(packs[0])] + [from_host(packs[m], m) for m in between]
    back_send, back_keep = backward(after(up_0, ahead_0), 0)
    back_send, back_keep, ahead_in, packs_near = lax.optimization_barrier(
        (back_send, back_keep, ahead_in, packs_near)
    )
    back_0 = summed(own_rows(up_own, up_theirs), back_keep, swap_cores(back_send))
    back_in = along_sections(back_0, -1)

    packs_beyond = [to_beyond(packs[n // 2 + m - 1], m) for m in between]
    ahead_their = swap_cores(ahead_in)
    ahead_send, ahead_keep = pl.pallas_call(
        functools.partial(forward_kernel, n, heads),
        grid=(heads,),
        in_specs=[smem] * 3 + [vmem] * (5 + 2 * n),
        out_specs=[vmem] * 2,
        out_shape=halves,
        scratch_shapes=[
            pltpu.VMEM((rows, width), BF16),
            pltpu.VMEM((rows, width), BF16),
            pltpu.VMEM((heads, rows, HEAD_DIM), BF16),
            pltpu.VMEM((rows, width), BF16),
        ],
        compiler_params=params,
        cost_estimate=cost(2 * matmul, 2 * weight_bytes),
        name="forward",
    )(
        core, offs, first_flag, ahead_in, ahead_their, new_own, new_theirs, keep, *in_parts, *out_parts
    )
    ahead_send, ahead_keep, back_in, packs_beyond = lax.optimization_barrier(
        (ahead_send, ahead_keep, back_in, packs_beyond)
    )
    new_rows = own_rows(new_own, new_theirs)
    ahead_1 = summed(
        jnp.where(first_section, new_rows, ahead_in), ahead_keep, swap_cores(ahead_send)
    )

    back_their = swap_cores(back_in)
    up_1, *pieces = pl.pallas_call(
        functools.partial(gather_kernel, n),
        in_specs=[smem] * 3 + [vmem] * 4,
        out_specs=[vmem] * n,
        out_shape=[struct((rows, width), BF16)] + [struct((rows, depth), BF16)] * (n - 1),
        compiler_params=params,
        name="gather",
    )(core, offs, last_flag, back_in, back_their, new_own, new_theirs)
    landed = [to_partner(pieces[0])] + [from_host(pieces[m], m) for m in between]
    landed += [to_beyond(pieces[n // 2 + m - 1], m) for m in between]
    back_send, back_keep = backward(up_1, 1)
    back_send, back_keep, landed = lax.optimization_barrier((back_send, back_keep, landed))
    back_1 = summed(
        jnp.where(last_section, new_rows, back_in), back_keep, swap_cores(back_send)
    )

    grads = pl.pallas_call(
        functools.partial(grads_kernel, n, (ticks * length * n) ** (-0.5)),
        in_specs=[smem] * 2 + [vmem] * (3 + 2 * (n - 1)),
        out_specs=vmem,
        out_shape=struct((slab, depth), F32),
        compiler_params=params,
        cost_estimate=cost(matmul // 4, weight_bytes // 4),
        name="grads",
    )(
        host_flag, offs, gated, up_0, up_1, *packs_near, *packs_beyond, *landed
    )

    first_pair = to_partner(jnp.stack([ahead_0[1], back_0[1]]))
    ahead = jnp.stack(
        [
            jnp.where(is_host, ahead_0[0], first_pair[0]),
            jnp.where(is_host, ahead_1[0], to_partner(ahead_1[1])),
        ]
    )
    back = jnp.stack(
        [
            jnp.where(is_host, back_0[0], first_pair[1]),
            jnp.where(is_host, back_1[0], to_partner(back_1[1])),
        ]
    )
    return (ahead[None], back[None], grads[None])


def solution(mesh):
    in_specs = (
        P(None, "dp", None),
        P("section", "dp", None),
        P(None, "dp", None),
        P("section", "dp", None),
        P("section", None, "dp", None),
        P("section", "dp", "cores"),
        P("section", "cores", "dp"),
        P("dp", None),
        P("dp", None),
        P("dp", None, None, None),
        P("dp", None, None, None),
    )
    out_specs = (
        P("section", None, ("dp", "cores"), None),
        P("section", None, ("dp", "cores"), None),
        P("section", "cores", "dp"),
    )
    return jax.shard_map(
        per_device, mesh=mesh, in_specs=in_specs, out_specs=out_specs, check_vma=False
    )
```

time: 225 us -> 248 us (1.10)
  local copies, waits for them, and re-layouts: 8.98 us -> 65.2 us
  waiting for transfers between devices: 117 us -> 69.4 us
  starting transfers between devices: 37.6 us -> 51.2 us
  other arithmetic: 9.93 us -> 14.9 us
    unnamed x26 -> x144, local copies, waits for them, and re-layouts: 4.35 us -> 51.2 us
    ppermute x4 -> x7, waiting for transfers between devices: 78.2 us -> 53.6 us  [from_partner(): return lax.ppermute(x, 'dp', [(h ^ 1, h) for h in hosts])]
    ppermute x1 -> x2, waiting for transfers between devices: 14.2 us -> 0.01 us  [to_beyond(): lax.ppermute(x, 'dp', [(hosts[k ^ m], hosts[k] ^ 1) for k in range(n // 2)])]
    ppermute x4 -> x7, starting transfers between devices: 11.4 us -> 24.6 us  [from_partner(): return lax.ppermute(x, 'dp', [(h ^ 1, h) for h in hosts])]
    ppermute x2, waiting for transfers between devices: 9.61 us -> 0.01 us  [along_sections(): return lax.ppermute(x, 'section', pairs)]
    eq x4, local copies, waits for them, and re-layouts: 0.55 us -> 5.83 us  [block_keep(): jnp.repeat(jnp.repeat(block_marks, BLOCK, axis=-2), BLOCK, axis=-1) == 1]
    select_n x0 -> x2, other arithmetic: none -> 3.63 us  [the longest x1 2.45 us: per_device(): new_own = jnp.where(first_section, arrivals[1], cotangent[1])]
    unnamed x2 -> x0, other arithmetic: 3.27 us -> none
  transfers between devices with their start and end apart: 23 -> 28, of which waited for: 8 -> 4; matrix products, arithmetic and copies ran while one was open for 5% -> 9% of each run, Pallas kernels for 20% -> 17%
where the time goes in v3:
time: 248 us; the launch traced here: 246 us
  waiting for transfers between devices  69.4 us (28%)
  local copies, waits for them, and re-layouts  65.2 us (26%)
  starting transfers between devices  51.2 us (21%)
  Pallas kernels  42.9 us (17%)
  other arithmetic  14.9 us (6%)
  between operations  2.68 us (1%)
    ppermute x7, waiting for transfers between devices, from_partner(): return lax.ppermute(x, 'dp', [(h ^ 1, h) for h in hosts])  53.6 us
    unnamed x144, local copies, waits for them, and re-layouts  51.2 us
    ppermute x7, starting transfers between devices, from_partner(): return lax.ppermute(x, 'dp', [(h ^ 1, h) for h in hosts])  24.6 us
    ppermute x5, waiting for transfers between devices, to_partner(): return lax.ppermute(x, 'dp', [(h, h ^ 1) for h in hosts])  15.7 us
    pallas_call x2, Pallas kernels, backward(): pl.pallas_call(functools.partial(backward_kernel, n, heads, tick_no), in_...  14.7 us
    pallas_call x1, Pallas kernels, per_device(): pl.pallas_call(functools.partial(project_kernel, n, heads), grid=(heads,)...  12.5 us
    pallas_call x1, Pallas kernels, per_device(): pl.pallas_call(functools.partial(forward_kernel, n, heads), grid=(heads,)...  8.15 us
    ppermute x5, starting transfers between devices, to_partner(): return lax.ppermute(x, 'dp', [(h, h ^ 1) for h in hosts])  6.57 us
  transfers between devices with their start and end apart: 28, of which 4 were waited for; matrix products, arithmetic and copies ran while one was open for 9% of the time, Pallas kernels for 17%

profile of v3, /device:TPU:5, one launch (start us, length us, event | category | flops | bytes accessed | tf_op | source)
XLA Modules:
  0.0 246.2 jit_solution(8840353427807655933)
XLA Ops:
  1.6 7.0 %collective-permute-start = (bf16[512,2048]{1,0:T(8,128)(2,1)}, bf16[512,2048]{1,0:T(8,128)(2,1)}, u32[]{:S(2)}, u32[]{:S(2)}) collective-permute-start(bf16[512,2048]{1,0:T(8,128)(2,1)} %bitcast.74), channel_id=1, source_target_pairs={{0,2},{6,4},{1,3},{7,5},{8,10},{14,12},{9,11},{15,13},{16,18},{22,... | collective-permute-start | bytes 6291464 | tf_op jit(solution)/shard_map/ppermute | solution.py:318
  13.3 38.1 %collective-permute-done.rest_1_.rest_5_ = bf16[512,2048]{1,0:T(8,128)(2,1)} collective-permute-done((bf16[512,2048]{1,0:T(8,128)(2,1)}, bf16[512,2048]{1,0:T(8,128)(2,1)}, u32[]{:S(2)}, u32[]{:S(2)}) %collective-permute-start) | collective-permute-done | bytes 2097184 | tf_op jit(solution)/shard_map/ppermute | solution.py:318
  54.7 4.1 %collective-permute-start.4 = (s32[2,5,17]{2,0,1:T(2,128)S(1)}, s32[2,5,17]{2,0,1:T(2,128)S(1)}, u32[]{:S(2)}, u32[]{:S(2)}) collective-permute-start(s32[2,5,17]{2,0,1:T(2,128)S(1)} %add_add_fusion), channel_id=1, source_target_pairs={{0,2},{6,4},{1,3},{7,5},{8,10},{14,12},{9,11},{15,13},{16,18},{22,... | collective-permute-start | bytes 2048 | tf_op jit(solution)/shard_map/ppermute | solution.py:318
  60.1 2.1 collective-permute-start.5
  62.2 2.5 slice_select_fusion
  64.7 1.4 collective-permute-start.3
  68.3 15.5 %collective-permute-done.3.x_theirs = bf16[96,2048]{1,0:T(8,128)(2,1)S(1)} collective-permute-done((bf16[96,2048]{1,0:T(8,128)(2,1)S(1)}, bf16[96,2048]{1,0:T(8,128)(2,1)S(1)}, u32[]{:S(2)}, u32[]{:S(2)}) %collective-permute-start.3) | collective-permute-done | bytes 393248 | tf_op jit(solution)/shard_map/ppermute | solution.py:318
  85.4 4.2 %collective-permute-start.8 = (bf16[512,512]{1,0:T(8,128)(2,1)S(1)}, bf16[512,512]{1,0:T(8,128)(2,1)S(1)}, u32[]{:S(2)}, u32[]{:S(2)}) collective-permute-start(bf16[512,512]{1,0:T(8,128)(2,1)S(1)} %bitcast.79), channel_id=1, source_target_pairs={{0,2},{6,4},{1,3},{7,5},{8,10},{14,12},{9,11},{15,13},{16,18},{22,... | collective-permute-start | bytes 1572872 | tf_op jit(solution)/shard_map/ppermute | solution.py:318
  97.2 1.7 copy.49
  101.7 5.2 %collective-permute-start.6 = (bf16[96,2048]{1,0:T(8,128)(2,1)S(1)}, bf16[96,2048]{1,0:T(8,128)(2,1)S(1)}, u32[]{:S(2)}, u32[]{:S(2)}) collective-permute-start(bf16[96,2048]{1,0:T(8,128)(2,1)S(1)} %bitcast.85), channel_id=1, source_target_pairs={{0,2},{6,4},{1,3},{7,5},{8,10},{14,12},{9,11},{15,13},{16,18},{22,... | collective-permute-start | bytes 1179656 | tf_op jit(solution)/shard_map/ppermute | solution.py:318
  108.2 1.6 copy-done.2
  113.1 12.5 %project.1 = (bf16[3,192,512]{2,1,0:T(8,128)(2,1)S(1)}, f32[2,192,512]{2,1,0:T(8,128)S(1)}, bf16[2,192,1536]{2,1,0:T(8,128)(2,1)S(1)}, f32[2,192,2048]{2,1,0:T(8...) custom-call(s32[4]{0:T(128)S(1)} %add_multiply_fusion.offs, ...), custom_call_target="tpu_custom_call" | custom-call | flops 4831838208 | bytes 20971520 | tf_op jit(solution)/shard_map/project/pallas_call | solution.py:426
  125.6 1.6 copy-done.6
  130.7 1.5 pack.1
  135.5 1.9 out.1
  139.0 3.5 %collective-permute-start.11 = (bf16[2,48,2048]{2,1,0:T(8,128)(2,1)}, bf16[2,48,2048]{2,1,0:T(8,128)(2,1)}, u32[]{:S(2)}, u32[]{:S(2)}) collective-permute-start(bf16[2,48,2048]{2,1,0:T(8,128)(2,1)} %get-tuple-element.92), channel_id=1, source_target_pairs={{0,1},{1,0},{2,3},{3,2},{4,5},{5,4},{6,7},{7,6},{8,9},{9,8},{10,11... | collective-permute-start | bytes 1179656 | tf_op jit(solution)/shard_map/ppermute | solution.py:332
  142.6 1.4 collective-permute-start.13
  146.1 3.1 %collective-permute-start.12 = (bf16[2,48,2048]{2,1,0:T(8,128)(2,1)S(1)}, bf16[2,48,2048]{2,1,0:T(8,128)(2,1)}, u32[]{:S(2)}, u32[]{:S(2)}) collective-permute-start(bf16[2,48,2048]{2,1,0:T(8,128)(2,1)S(1)} %add_convert_fusion.3), channel_id=1, source_target_pairs={{0,8},{8,16},{16,24},{1,9},{9,17},{17,25},{2,10},{10,18},{18,26},{... | collective-permute-start | bytes 1179656 | tf_op jit(solution)/shard_map/ppermute | solution.py:336
  149.3 1.6 copy-done.3
  150.9 1.9 copy-done.7
  152.8 1.4 copy-done.19
  161.1 7.3 %backward.2 = (bf16[2,48,2048]{2,1,0:T(8,128)(2,1)S(1)}, bf16[2,48,2048]{2,1,0:T(8,128)(2,1)S(1)}) custom-call(s32[1]{0:T(128)} %bitcast.8.core, s32[4]{0:T(128)S(1)} %add_multiply_fusion.offs, bf16[192,2048]{1,0:T(8,128)(2,1)S(1)} %copy-done.33, bf16[2,96,2048]{2,1,0:T(8,128)(2,1)S(1)} %bitcast.93, bf16[2,96,2048]{2,1,0:T(8,128)(2,1)S(1)} %copy-done.42, ...), custom_call_target="tpu_custom_call" | custom-call | flops 3221225472 | bytes 20971520 | tf_op jit(solution)/shard_map/backward/pallas_call | solution.py:456
  171.3 3.2 %collective-permute-start.18 = (bf16[2,48,2048]{2,1,0:T(8,128)(2,1)}, bf16[2,48,2048]{2,1,0:T(8,128)(2,1)}, u32[]{:S(2)}, u32[]{:S(2)}) collective-permute-start(bf16[2,48,2048]{2,1,0:T(8,128)(2,1)} %add_convert_fusion.2), channel_id=1, source_target_pairs={{8,0},{16,8},{24,16},{9,1},{17,9},{25,17},{10,2},{18,10},{26,18},{... | collective-permute-start | bytes 1179656 | tf_op jit(solution)/shard_map/ppermute | solution.py:336
  174.6 1.6 copy-done.4
  180.4 8.1 %forward.1 = (bf16[2,48,2048]{2,1,0:T(8,128)(2,1)S(1)}, bf16[2,48,2048]{2,1,0:T(8,128)(2,1)S(1)}) custom-call(s32[1]{0:T(128)} %bitcast.8.core, s32[4]{0:T(128)S(1)} %add_multiply_fusion.offs, s32[1]{0:T(128)} %bitcast.30.fresh, bf16[2,48,2048]{2,1,0:T(8,128)(2,1)} %collective-permute-done.12.mine, bf16[2,48,2048]{2,1,0:T(8,128)(2,1)} %collective-permute-done.17.theirs, ...), custom_call_target="tpu_custom_call" | custom-call | flops 3221225472 | bytes 20971520 | tf_op jit(solution)/shard_map/forward/pallas_call | solution.py:511
  200.1 1.6 copy-done.5
  201.7 1.9 copy-done.8
  212.6 7.4 %backward.3 = (bf16[2,48,2048]{2,1,0:T(8,128)(2,1)S(1)}, bf16[2,48,2048]{2,1,0:T(8,128)(2,1)S(1)}) custom-call(s32[1]{0:T(128)} %bitcast.8.core, s32[4]{0:T(128)S(1)} %add_multiply_fusion.offs, bf16[192,2048]{1,0:T(8,128)(2,1)S(1)} %get-tuple-element.115.ups.up_1, bf16[2,96,2048]{2,1,0:T(8,128)(2,1)S(1)} %bitcast.94, bf16[2,96,2048]{2,1,0:T(8,128)(2,1)S(1)} %copy-done.43, ...), custom_call_target="tpu_custom_call" | custom-call | flops 3221225472 | bytes 20971520 | tf_op jit(solution)/shard_map/backward/pallas_call | solution.py:456
  221.8 2.9 %grads.1 = f32[512,512]{1,0:T(8,128)} custom-call(s32[1]{0:T(128)} %bitcast.40.host, s32[4]{0:T(128)S(1)} %add_multiply_fusion.offs, bf16[3,192,512]{2,1,0:T(8,128)(2,1)S(1)} %copy-done.22, bf16[192,2048]{1,0:T(8,128)(2,1)S(1)} %copy-done.34, bf16[192,2048]{1,0:T(8,128)(2,1)S(1)} %get-tuple-element.115.ups.up_1, bf16[192,1536]{1,0:T(8,128)(2,1)S(1)} %copy-done.58, ...), custom_call_target="tpu_custom_call" | custom-call | flops 402653184 | bytes 2621440 | tf_op jit(solution)/shard_map/grads/pallas_call | solution.py:554
  224.7 1.6 add_convert_fusion
  228.9 12.3 %collective-permute-done.21 = bf16[48,2048]{1,0:T(8,128)(2,1)S(1)} collective-permute-done((bf16[48,2048]{1,0:T(8,128)(2,1)S(1)}, bf16[48,2048]{1,0:T(8,128)(2,1)S(1)}, u32[]{:S(2)}, u32[]{:S(2)}) %collective-permute-start.21) | collective-permute-done | bytes 196640 | tf_op jit(solution)/shard_map/ppermute | solution.py:321
  242.0 3.4 %collective-permute-done.27 = bf16[48,2048]{1,0:T(8,128)(2,1)S(1)} collective-permute-done((bf16[48,2048]{1,0:T(8,128)(2,1)S(1)}, bf16[48,2048]{1,0:T(8,128)(2,1)S(1)}, u32[]{:S(2)}, u32[]{:S(2)}) %collective-permute-start.27) | collective-permute-done | bytes 196640 | tf_op jit(solution)/shard_map/ppermute | solution.py:321
  (216 shorter events, 78.4 us)
Async XLA Ops:
  0.6 84.8 %copy-start.9 = (bf16[1,512,512]{2,1,0:T(8,128)(2,1)S(1)}, bf16[1,512,512]{2,1,0:T(8,128)(2,1)}, u32[]{:S(2)}) copy-start(bf16[1,512,512]{2,1,0:T(8,128)(2,1)} %param.18) | copy-start | bytes 1572868
  0.6 11.4 %collective-permute-start.1 = (bf16[512,2048]{1,0:T(8,128)(2,1)}, bf16[512,2048]{1,0:T(8,128)(2,1)S(1)}, u32[]{:S(2)}, u32[]{:S(2)}) collective-permute-start(bf16[512,2048]{1,0:T(8,128)(2,1)} %bitcast.73), channel_id=1, source_target_pairs={{4,2},{2,4},{5,3},{3,5},{12,10},{10,12},{13,11},{11,13},{20,18},{1... | collective-permute-start | bytes 6291464 | tf_op jit(solution)/shard_map/ppermute | solution.py:324
  1.6 49.9 %collective-permute-start = (bf16[512,2048]{1,0:T(8,128)(2,1)}, bf16[512,2048]{1,0:T(8,128)(2,1)}, u32[]{:S(2)}, u32[]{:S(2)}) collective-permute-start(bf16[512,2048]{1,0:T(8,128)(2,1)} %bitcast.74), channel_id=1, source_target_pairs={{0,2},{6,4},{1,3},{7,5},{8,10},{14,12},{9,11},{15,13},{16,18},{22,... | collective-permute-start | bytes 6291464 | tf_op jit(solution)/shard_map/ppermute | solution.py:318
  54.7 12.2 %collective-permute-start.4 = (s32[2,5,17]{2,0,1:T(2,128)S(1)}, s32[2,5,17]{2,0,1:T(2,128)S(1)}, u32[]{:S(2)}, u32[]{:S(2)}) collective-permute-start(s32[2,5,17]{2,0,1:T(2,128)S(1)} %add_add_fusion), channel_id=1, source_target_pairs={{0,2},{6,4},{1,3},{7,5},{8,10},{14,12},{9,11},{15,13},{16,18},{22,... | collective-permute-start | bytes 2048 | tf_op jit(solution)/shard_map/ppermute | solution.py:318
  58.8 25.8 %collective-permute-start.2 = (bf16[2,96,2048]{2,1,0:T(8,128)(2,1)}, bf16[2,96,2048]{2,1,0:T(8,128)(2,1)S(1)}, u32[]{:S(2)}, u32[]{:S(2)}) collective-permute-start(bf16[2,96,2048]{2,1,0:T(8,128)(2,1)} %bitcast.91), channel_id=1, source_target_pairs={{0,2},{6,4},{1,3},{7,5},{8,10},{14,12},{9,11},{15,13},{16,18},{22,... | collective-permute-start | bytes 2359304 | tf_op jit(solution)/shard_map/ppermute | solution.py:318
  60.1 48.0 %collective-permute-start.5 = (bf16[512,2048]{1,0:T(8,128)(2,1)}, bf16[512,2048]{1,0:T(8,128)(2,1)}, u32[]{:S(2)}, u32[]{:S(2)}) collective-permute-start(bf16[512,2048]{1,0:T(8,128)(2,1)} %collective-permute-done.rest_1_.rest_5_), channel_id=1, source_target_pairs={{4,2},{2,4},{5,3},{3,5},{12,10},{10,12},{13,11},{11,13},{20,18},{1... | collective-permute-start | bytes 6291464 | tf_op jit(solution)/shard_map/ppermute | solution.py:324
  64.7 43.5 %copy-start = (bf16[1,512,2048]{2,1,0:T(8,128)(2,1)S(1)}, bf16[1,512,2048]{2,1,0:T(8,128)(2,1)}, u32[]{:S(2)}) copy-start(bf16[1,512,2048]{2,1,0:T(8,128)(2,1)} %param.17) | copy-start | bytes 6291460
  64.7 19.1 %collective-permute-start.3 = (bf16[96,2048]{1,0:T(8,128)(2,1)S(1)}, bf16[96,2048]{1,0:T(8,128)(2,1)S(1)}, u32[]{:S(2)}, u32[]{:S(2)}) collective-permute-start(bf16[96,2048]{1,0:T(8,128)(2,1)S(1)} %bitcast.96), channel_id=1, source_target_pairs={{0,2},{6,4},{1,3},{7,5},{8,10},{14,12},{9,11},{15,13},{16,18},{22,... | collective-permute-start | bytes 1179656 | tf_op jit(solution)/shard_map/ppermute | solution.py:318
  85.4 15.3 %collective-permute-start.8 = (bf16[512,512]{1,0:T(8,128)(2,1)S(1)}, bf16[512,512]{1,0:T(8,128)(2,1)S(1)}, u32[]{:S(2)}, u32[]{:S(2)}) collective-permute-start(bf16[512,512]{1,0:T(8,128)(2,1)S(1)} %bitcast.79), channel_id=1, source_target_pairs={{0,2},{6,4},{1,3},{7,5},{8,10},{14,12},{9,11},{15,13},{16,18},{22,... | collective-permute-start | bytes 1572872 | tf_op jit(solution)/shard_map/ppermute | solution.py:318
  100.1 35.5 %collective-permute-start.9 = (bf16[512,512]{1,0:T(8,128)(2,1)S(1)}, bf16[512,512]{1,0:T(8,128)(2,1)S(1)}, u32[]{:S(2)}, u32[]{:S(2)}) collective-permute-start(bf16[512,512]{1,0:T(8,128)(2,1)S(1)} %bitcast.80), channel_id=1, source_target_pairs={{4,2},{2,4},{5,3},{3,5},{12,10},{10,12},{13,11},{11,13},{20,18},{1... | collective-permute-start | bytes 1572872 | tf_op jit(solution)/shard_map/ppermute | solution.py:324
  100.8 34.7 %collective-permute-start.10 = (bf16[512,512]{1,0:T(8,128)(2,1)S(1)}, bf16[512,512]{1,0:T(8,128)(2,1)S(1)}, u32[]{:S(2)}, u32[]{:S(2)}) collective-permute-start(bf16[512,512]{1,0:T(8,128)(2,1)S(1)} %collective-permute-done.8.rest_1_.rest_5_), channel_id=1, source_target_pairs={{4,2},{2,4},{5,3},{3,5},{12,10},{10,12},{13,11},{11,13},{20,18},{1... | collective-permute-start | bytes 1572872 | tf_op jit(solution)/shard_map/ppermute | solution.py:324
  101.6 24.0 %copy-start.35 = (f32[4,192,192]{2,1,0:T(8,128)}, f32[4,192,192]{2,1,0:T(8,128)S(1)}, u32[]{:S(2)}) copy-start(f32[4,192,192]{2,1,0:T(8,128)S(1)} %select_maximum_fusion.keep) | copy-start | bytes 1769476
  101.7 28.3 %collective-permute-start.6 = (bf16[96,2048]{1,0:T(8,128)(2,1)S(1)}, bf16[96,2048]{1,0:T(8,128)(2,1)S(1)}, u32[]{:S(2)}, u32[]{:S(2)}) collective-permute-start(bf16[96,2048]{1,0:T(8,128)(2,1)S(1)} %bitcast.85), channel_id=1, source_target_pairs={{0,2},{6,4},{1,3},{7,5},{8,10},{14,12},{9,11},{15,13},{16,18},{22,... | collective-permute-start | bytes 1179656 | tf_op jit(solution)/shard_map/ppermute | solution.py:318
  106.9 23.9 %collective-permute-start.7 = (bf16[96,2048]{1,0:T(8,128)(2,1)S(1)}, bf16[96,2048]{1,0:T(8,128)(2,1)S(1)}, u32[]{:S(2)}, u32[]{:S(2)}) collective-permute-start(bf16[96,2048]{1,0:T(8,128)(2,1)S(1)} %bitcast.88), channel_id=1, source_target_pairs={{0,2},{6,4},{1,3},{7,5},{8,10},{14,12},{9,11},{15,13},{16,18},{22,... | collective-permute-start | bytes 1179656 | tf_op jit(solution)/shard_map/ppermute | solution.py:318
  139.0 5.7 %collective-permute-start.11 = (bf16[2,48,2048]{2,1,0:T(8,128)(2,1)}, bf16[2,48,2048]{2,1,0:T(8,128)(2,1)}, u32[]{:S(2)}, u32[]{:S(2)}) collective-permute-start(bf16[2,48,2048]{2,1,0:T(8,128)(2,1)} %get-tuple-element.92), channel_id=1, source_target_pairs={{0,1},{1,0},{2,3},{3,2},{4,5},{5,4},{6,7},{7,6},{8,9},{9,8},{10,11... | collective-permute-start | bytes 1179656 | tf_op jit(solution)/shard_map/ppermute | solution.py:332
  142.6 25.8 %collective-permute-start.13 = (bf16[192,1536]{1,0:T(8,128)(2,1)}, bf16[192,1536]{1,0:T(8,128)(2,1)S(1)}, u32[]{:S(2)}, u32[]{:S(2)}) collective-permute-start(bf16[192,1536]{1,0:T(8,128)(2,1)} %copy-done.67), channel_id=1, source_target_pairs={{2,0},{4,6},{3,1},{5,7},{10,8},{12,14},{11,9},{13,15},{18,16},{20,... | collective-permute-start | bytes 1769480 | tf_op jit(solution)/shard_map/ppermute | solution.py:321
  144.0 24.4 %collective-permute-start.14 = (bf16[192,1536]{1,0:T(8,128)(2,1)}, bf16[192,1536]{1,0:T(8,128)(2,1)S(1)}, u32[]{:S(2)}, u32[]{:S(2)}) collective-permute-start(bf16[192,1536]{1,0:T(8,128)(2,1)} %copy-done.66), channel_id=1, source_target_pairs={{4,2},{2,4},{5,3},{3,5},{12,10},{10,12},{13,11},{11,13},{20,18},{1... | collective-permute-start | bytes 1769480 | tf_op jit(solution)/shard_map/ppermute | solution.py:324
  146.1 22.3 %copy-start.69 = (bf16[2,48,2048]{2,1,0:T(8,128)(2,1)}, bf16[2,48,2048]{2,1,0:T(8,128)(2,1)S(1)}, u32[]{:S(2)}) copy-start(bf16[2,48,2048]{2,1,0:T(8,128)(2,1)S(1)} %add_convert_fusion.3) | copy-start | bytes 1179652
  146.1 22.3 %collective-permute-start.12 = (bf16[2,48,2048]{2,1,0:T(8,128)(2,1)S(1)}, bf16[2,48,2048]{2,1,0:T(8,128)(2,1)}, u32[]{:S(2)}, u32[]{:S(2)}) collective-permute-start(bf16[2,48,2048]{2,1,0:T(8,128)(2,1)S(1)} %add_convert_fusion.3), channel_id=1, source_target_pairs={{0,8},{8,16},{16,24},{1,9},{9,17},{17,25},{2,10},{10,18},{18,26},{... | collective-permute-start | bytes 1179656 | tf_op jit(solution)/shard_map/ppermute | solution.py:336
  168.5 1.9 collective-permute-start.15
  168.9 21.2 %collective-permute-start.19 = (bf16[192,1536]{1,0:T(8,128)(2,1)}, bf16[192,1536]{1,0:T(8,128)(2,1)}, u32[]{:S(2)}, u32[]{:S(2)}) collective-permute-start(bf16[192,1536]{1,0:T(8,128)(2,1)} %get-tuple-element.111), channel_id=1, source_target_pairs={{4,0},{2,6},{5,1},{3,7},{12,8},{10,14},{13,9},{11,15},{20,16},{18,... | collective-permute-start | bytes 1769480 | tf_op jit(solution)/shard_map/ppermute | solution.py:327
  170.2 4.4 %collective-permute-start.17 = (bf16[2,48,2048]{2,1,0:T(8,128)(2,1)}, bf16[2,48,2048]{2,1,0:T(8,128)(2,1)}, u32[]{:S(2)}, u32[]{:S(2)}) collective-permute-start(bf16[2,48,2048]{2,1,0:T(8,128)(2,1)} %collective-permute-done.12.mine), channel_id=1, source_target_pairs={{0,1},{1,0},{2,3},{3,2},{4,5},{5,4},{6,7},{7,6},{8,9},{9,8},{10,11... | collective-permute-start | bytes 1179656 | tf_op jit(solution)/shard_map/ppermute | solution.py:332
  171.3 18.7 %collective-permute-start.18 = (bf16[2,48,2048]{2,1,0:T(8,128)(2,1)}, bf16[2,48,2048]{2,1,0:T(8,128)(2,1)}, u32[]{:S(2)}, u32[]{:S(2)}) collective-permute-start(bf16[2,48,2048]{2,1,0:T(8,128)(2,1)} %add_convert_fusion.2), channel_id=1, source_target_pairs={{8,0},{16,8},{24,16},{9,1},{17,9},{25,17},{10,2},{18,10},{26,18},{... | collective-permute-start | bytes 1179656 | tf_op jit(solution)/shard_map/ppermute | solution.py:336
  190.0 4.4 %collective-permute-start.22 = (bf16[2,48,2048]{2,1,0:T(8,128)(2,1)}, bf16[2,48,2048]{2,1,0:T(8,128)(2,1)}, u32[]{:S(2)}, u32[]{:S(2)}) collective-permute-start(bf16[2,48,2048]{2,1,0:T(8,128)(2,1)} %collective-permute-done.18.mine), channel_id=1, source_target_pairs={{0,1},{1,0},{2,3},{3,2},{4,5},{5,4},{6,7},{7,6},{8,9},{9,8},{10,11... | collective-permute-start | bytes 1179656 | tf_op jit(solution)/shard_map/ppermute | solution.py:332
  192.4 28.1 %collective-permute-start.16 = (bf16[2,48,2048]{2,1,0:T(8,128)(2,1)}, bf16[2,48,2048]{2,1,0:T(8,128)(2,1)}, u32[]{:S(2)}, u32[]{:S(2)}) collective-permute-start(bf16[2,48,2048]{2,1,0:T(8,128)(2,1)} %pad_maximum_fusion), channel_id=1, source_target_pairs={{2,0},{4,6},{3,1},{5,7},{10,8},{12,14},{11,9},{13,15},{18,16},{20,... | collective-permute-start | bytes 1179656 | tf_op jit(solution)/shard_map/ppermute | solution.py:321
  194.4 30.3 %collective-permute-start.20 = (bf16[2,48,2048]{2,1,0:T(8,128)(2,1)}, bf16[2,48,2048]{2,1,0:T(8,128)(2,1)S(1)}, u32[]{:S(2)}, u32[]{:S(2)}) collective-permute-start(bf16[2,48,2048]{2,1,0:T(8,128)(2,1)} %copy-done.68), channel_id=1, source_target_pairs={{0,1},{1,0},{2,3},{3,2},{4,5},{5,4},{6,7},{7,6},{8,9},{9,8},{10,11... | collective-permute-start | bytes 1179656 | tf_op jit(solution)/shard_map/ppermute | solution.py:332
  196.8 23.2 %collective-permute-start.23 = (bf16[192,512]{1,0:T(8,128)(2,1)S(1)}, bf16[192,512]{1,0:T(8,128)(2,1)S(1)}, u32[]{:S(2)}, u32[]{:S(2)}) collective-permute-start(bf16[192,512]{1,0:T(8,128)(2,1)S(1)} %get-tuple-element.118), channel_id=1, source_target_pairs={{2,0},{4,6},{3,1},{5,7},{10,8},{12,14},{11,9},{13,15},{18,16},{20,... | collective-permute-start | bytes 589832 | tf_op jit(solution)/shard_map/ppermute | solution.py:321
  198.1 21.9 %collective-permute-start.24 = (bf16[192,512]{1,0:T(8,128)(2,1)S(1)}, bf16[192,512]{1,0:T(8,128)(2,1)S(1)}, u32[]{:S(2)}, u32[]{:S(2)}) collective-permute-start(bf16[192,512]{1,0:T(8,128)(2,1)S(1)} %get-tuple-element.119), channel_id=1, source_target_pairs={{4,2},{2,4},{5,3},{3,5},{12,10},{10,12},{13,11},{11,13},{20,18},{1... | collective-permute-start | bytes 589832 | tf_op jit(solution)/shard_map/ppermute | solution.py:324
  198.8 21.2 %collective-permute-start.25 = (bf16[192,512]{1,0:T(8,128)(2,1)S(1)}, bf16[192,512]{1,0:T(8,128)(2,1)S(1)}, u32[]{:S(2)}, u32[]{:S(2)}) collective-permute-start(bf16[192,512]{1,0:T(8,128)(2,1)S(1)} %get-tuple-element.120), channel_id=1, source_target_pairs={{4,0},{2,6},{5,1},{3,7},{12,8},{10,14},{13,9},{11,15},{20,16},{18,... | collective-permute-start | bytes 589832 | tf_op jit(solution)/shard_map/ppermute | solution.py:327
  220.1 4.6 %collective-permute-start.26 = (bf16[2,48,2048]{2,1,0:T(8,128)(2,1)S(1)}, bf16[2,48,2048]{2,1,0:T(8,128)(2,1)S(1)}, u32[]{:S(2)}, u32[]{:S(2)}) collective-permute-start(bf16[2,48,2048]{2,1,0:T(8,128)(2,1)S(1)} %get-tuple-element.122), channel_id=1, source_target_pairs={{0,1},{1,0},{2,3},{3,2},{4,5},{5,4},{6,7},{7,6},{8,9},{9,8},{10,11... | collective-permute-start | bytes 1179656 | tf_op jit(solution)/shard_map/ppermute | solution.py:332
  226.3 14.9 %collective-permute-start.21 = (bf16[48,2048]{1,0:T(8,128)(2,1)S(1)}, bf16[48,2048]{1,0:T(8,128)(2,1)S(1)}, u32[]{:S(2)}, u32[]{:S(2)}) collective-permute-start(bf16[48,2048]{1,0:T(8,128)(2,1)S(1)} %slice_bitcast_fusion.2), channel_id=1, source_target_pairs={{2,0},{4,6},{3,1},{5,7},{10,8},{12,14},{11,9},{13,15},{18,16},{20,... | collective-permute-start | bytes 589832 | tf_op jit(solution)/shard_map/ppermute | solution.py:321
  227.6 17.8 %collective-permute-start.27 = (bf16[48,2048]{1,0:T(8,128)(2,1)S(1)}, bf16[48,2048]{1,0:T(8,128)(2,1)S(1)}, u32[]{:S(2)}, u32[]{:S(2)}) collective-permute-start(bf16[48,2048]{1,0:T(8,128)(2,1)S(1)} %slice_bitcast_fusion), channel_id=1, source_target_pairs={{2,0},{4,6},{3,1},{5,7},{10,8},{12,14},{11,9},{13,15},{18,16},{20,... | collective-permute-start | bytes 589832 | tf_op jit(solution)/shard_map/ppermute | solution.py:321
  (68 other events, 208.3 us)

commit v4 on v3

--- a/solution.py
+++ b/solution.py
@@ -12,7 +12,7 @@
 BLOCKS = 4
 EPSILON = 1e-06
 SCALING = HEAD_DIM ** (-0.5)
-VMEM_BYTES = 24 * 1024 * 1024
+VMEM_BYTES = 50 * 1024 * 1024
 
 F32 = jnp.float32
 BF16 = jnp.bfloat16
@@ -54,16 +54,23 @@
     return sig, gate, vqk, scores, sig_s, probs, mixed, gated
 
 
-def project_kernel(n, heads, offs, x_own, x_theirs, stash_own, stash_theirs, keep, *rest):
-    weights = rest[:n]
-    gated_out, gate_out, vqk_out, slope_out, mixed_out, probs_out, factor_out, normed = rest[n:]
-    depth = weights[0].shape[0]
+def project(normed, offs, weights):
+    total = None
+    for j, weight in enumerate(weights):
+        depth = weight.shape[0]
+        columns = pl.ds(pl.multiple_of(offs[j], depth), depth)
+        term = dot(normed[:, columns], weight[...])
+        total = term if total is None else total + term
+    return total
+
+
+def project_kernel(parts, offs, x_own, x_theirs, stash_own, stash_theirs, keep, *rest):
+    weights = rest[:parts]
+    gated_out, gate_out, vqk_out, slope_out, mixed_out, probs_out, factor_out, normed = rest[parts:]
     length = x_own.shape[0]
     rows = 2 * length
-    wide = 4 * HEAD_DIM
-    head = pl.program_id(0)
-
-    @pl.when(head == 0)
+
+    @pl.when(pl.program_id(0) == 0)
     def _():
         sources = [x_own, x_theirs]
         for t in range(stash_own.shape[0]):
@@ -72,12 +79,7 @@
             floats = source[...].astype(F32)
             normed[pl.ds(i * length, length), :] = (floats * row_root(floats)).astype(BF16)
 
-    here = pl.ds(pl.multiple_of(head * wide, wide), wide)
-    pre_all = None
-    for j in range(n):
-        columns = pl.ds(pl.multiple_of(offs[j], depth), depth)
-        term = dot(normed[:, columns], weights[j][:, here])
-        pre_all = term if pre_all is None else pre_all + term
+    pre_all = project(normed, offs, weights)
     for i in range(1 + stash_own.shape[0]):
         pre = pre_all[i * rows : (i + 1) * rows]
         kept = keep[i]
@@ -126,11 +128,11 @@
             whole[pl.ds(at, share), :] = jnp.where(use_fresh, rows, landed[r])
 
 
-def forward_kernel(n, heads, core, offs, fresh, mine, theirs, new_own, new_theirs, keep, *rest):
-    in_parts = rest[:n]
-    out_parts = rest[n : 2 * n]
-    send, kept, whole, normed, gated, part = rest[2 * n :]
-    depth = in_parts[0].shape[0]
+def forward_kernel(parts, heads, core, in_offs, offs, fresh, mine, theirs, new_own, new_theirs, keep, *rest):
+    in_parts = rest[:parts]
+    out_parts = rest[parts:-6]
+    send, kept, whole, normed, gated, part = rest[-6:]
+    depth = out_parts[0].shape[1]
     head = pl.program_id(0)
 
     @pl.when(head == 0)
@@ -139,18 +141,11 @@
         floats = whole[...].astype(F32)
         normed[...] = (floats * row_root(floats)).astype(BF16)
 
-    wide = 4 * HEAD_DIM
-    here = pl.ds(pl.multiple_of(head * wide, wide), wide)
-    pre = None
-    for j in range(n):
-        columns = pl.ds(pl.multiple_of(offs[j], depth), depth)
-        term = dot(normed[:, columns], in_parts[j][:, here])
-        pre = term if pre is None else pre + term
-    gated[head] = attend(pre, keep[keep.shape[0] - 1])[-1]
+    gated[head] = attend(project(normed, in_offs, in_parts), keep[0])[-1]
 
     @pl.when(head == heads - 1)
     def _():
-        for j in range(n):
+        for j in range(len(out_parts)):
             columns = pl.ds(pl.multiple_of(offs[j], depth), depth)
             total = None
             for h in range(heads):
@@ -160,49 +155,69 @@
         split_rows(core[0], part, send, kept)
 
 
-def backward_kernel(
-    n, heads, tick, core, offs, ups, x_own, x_theirs, gate, vqk, slope, mixed, probs, factor, *rest
-):
-    out_parts = rest[:n]
-    in_parts = rest[n : 2 * n]
-    send, keep, grad_normed, part = rest[2 * n :]
+def backward_kernel(parts, n, tick, core, in_offs, offs, *rest):
+    count = 9 + n + parts
+    sources, rest = rest[:count], rest[count:]
+    send, keep = rest[:2]
+    held, (grad_normed, part, sems) = rest[2 : 2 + count], rest[2 + count :]
+    ups, gate, vqk, slope, mixed, probs, factor, x_own, x_theirs = held[:9]
+    out_parts, in_parts = held[9 : 9 + n], held[9 + n :]
+    copies = []
+    for i, (source, target) in enumerate(zip(sources, held)):
+        if 1 <= i < 9:
+            source = source.at[tick]
+        copies.append(pltpu.make_async_copy(source, target, sems.at[i]))
+    first = [0] + list(range(9, 9 + n))
+    second = [1, 4, 2, 5, 6, 3]
+    last = list(range(9 + n, count))
+    for i in first + second + last + [7, 8]:
+        copies[i].start()
+    for i in first:
+        copies[i].wait()
     depth = out_parts[0].shape[1]
-    length = x_own.shape[1]
+    length = x_own.shape[0]
     wide = 4 * HEAD_DIM
+    heads = out_parts[0].shape[0] // HEAD_DIM
     grad_gated = None
     for j in range(n):
         columns = pl.ds(pl.multiple_of(offs[j], depth), depth)
         term = dot_nt(ups[:, columns], out_parts[j][...])
         grad_gated = term if grad_gated is None else grad_gated + term
     grad_gated = grad_gated.astype(BF16).astype(F32)
+    for i in second:
+        copies[i].wait()
     grads_pre = []
     for h in range(heads):
         cut = slice(h * HEAD_DIM, (h + 1) * HEAD_DIM)
         up = grad_gated[:, cut]
-        mixed_h = mixed[tick, :, cut]
+        mixed_h = mixed[:, cut]
         root = row_root(mixed_h)
         normed = mixed_h * root
-        grad_n = up * gate[tick, :, cut]
+        grad_n = up * gate[:, cut]
         grad_gate = up * normed
         grad_mixed = root * (grad_n - normed * jnp.mean(grad_n * normed, axis=-1, keepdims=True))
         low = grad_mixed.astype(BF16)
         base = 3 * h * HEAD_DIM
-        value = vqk[tick, :, base : base + HEAD_DIM]
-        query = vqk[tick, :, base + HEAD_DIM : base + 2 * HEAD_DIM]
-        key = vqk[tick, :, base + 2 * HEAD_DIM : base + 3 * HEAD_DIM]
-        grad_scores = (dot_nt(low, value) * factor[tick, h]).astype(BF16)
-        grad_value = dot_tn(probs[tick, h], low)
+        value = vqk[:, base : base + HEAD_DIM]
+        query = vqk[:, base + HEAD_DIM : base + 2 * HEAD_DIM]
+        key = vqk[:, base + 2 * HEAD_DIM : base + 3 * HEAD_DIM]
+        grad_scores = (dot_nt(low, value) * factor[h]).astype(BF16)
+        grad_value = dot_tn(probs[h], low)
         grad_query = dot(grad_scores, key)
         grad_key = dot_tn(grad_scores, query)
         grad_active = jnp.concatenate([grad_gate, grad_value, grad_query, grad_key], axis=1)
-        grads_pre.append((grad_active * slope[tick, :, h * wide : (h + 1) * wide]).astype(BF16))
+        grads_pre.append((grad_active * slope[:, h * wide : (h + 1) * wide]).astype(BF16))
     grad_pre = jnp.concatenate(grads_pre, axis=1)
-    for j in range(n):
-        columns = pl.ds(pl.multiple_of(offs[j], depth), depth)
+    for j in range(parts):
+        rows_of = in_parts[j].shape[0]
+        columns = pl.ds(pl.multiple_of(in_offs[j], rows_of), rows_of)
+        copies[last[j]].wait()
         grad_normed[:, columns] = dot_nt(grad_pre, in_parts[j][...])
+    for i in (7, 8):
+        copies[i].wait()
     for r, source in enumerate((x_own, x_theirs)):
         rows = pl.ds(r * length, length)
-        floats = source[tick].astype(F32)
+        floats = source[...].astype(F32)
         root = row_root(floats)
         scaled = floats * root
         grad_n = grad_normed[rows, :]
@@ -339,17 +354,23 @@
     last_section = section_no == sections - 1
     between = range(1, n // 2)
 
-    in_near = from_partner(in_shard)
+    pieces = max(1, min(2, depth // 256))
+    piece = depth // pieces
     in_far = [from_host(in_shard, m) for m in between]
-    in_near, in_far, rows_in, tables_in = lax.optimization_barrier(
+    in_near = [
+        from_partner(in_shard[i * piece : (i + 1) * piece]) for i in range(pieces)
+    ]
+    in_pass = [from_host(in_near[0], m) for m in between]
+    in_far, in_near, rows_in, tables_in = lax.optimization_barrier(
         (
+            in_far,
             in_near,
-            in_far,
             (arrivals, in_flight, cotangent, grad_flight, stashed),
             (forward_blocks, forward_marks, backward_blocks, backward_marks),
         )
     )
-    in_parts = [in_shard, in_near] + in_far + [from_host(in_near, m) for m in between]
+    in_pass += [from_host(in_near[i], m) for i in range(1, pieces) for m in between]
+    in_parts = [in_shard] + in_far + in_near + in_pass
     arrivals, in_flight, cotangent, grad_flight, stashed = rows_in
     tables = jnp.concatenate(
         [
@@ -373,10 +394,14 @@
     up_theirs = from_partner(up_late)
     new_theirs = from_partner(new_late)
     out_parts = [out_shard, out_near] + out_far + [from_host(out_near, m) for m in between]
-    owners = [dp_no, dp_no ^ 1]
-    owners += [host_table[(dp_no // 2) ^ m] for m in range(1, n // 2)]
-    owners += [host_table[(dp_no // 2) ^ m] ^ 1 for m in range(1, n // 2)]
+    far_hosts = [host_table[(dp_no // 2) ^ m] for m in between]
+    owners = [dp_no, dp_no ^ 1] + far_hosts + [h ^ 1 for h in far_hosts]
     offs = jnp.stack(owners).astype(jnp.int32) * depth
+    in_offs = [dp_no * depth] + [h * depth for h in far_hosts]
+    in_offs += [(dp_no ^ 1) * depth + i * piece for i in range(pieces)]
+    in_offs += [(h ^ 1) * depth + i * piece for i in range(pieces) for h in far_hosts]
+    in_offs = jnp.stack(in_offs).astype(jnp.int32)
+    parts = len(in_parts)
     core = jnp.reshape(core_no, (1,)).astype(jnp.int32)
     first_flag = jnp.reshape(first_section, (1,)).astype(jnp.int32)
     host_flag = jnp.reshape(is_host, (1,)).astype(jnp.int32)
@@ -406,7 +431,14 @@
     )
 
     smem = pl.BlockSpec(memory_space=pltpu.SMEM)
-    vmem = pl.BlockSpec(memory_space=pltpu.VMEM)
+    hbm = pl.BlockSpec(memory_space=pl.ANY)
+
+    def all_of(*arrays):
+        return [pl.BlockSpec(x.shape, lambda *_, d=x.ndim: (0,) * d) for x in arrays]
+
+    def row_of(x, i):
+        return pl.BlockSpec((1,) + x.shape[1:], lambda *_: (i,) + (0,) * (x.ndim - 1))
+
     params = pltpu.CompilerParams(vmem_limit_bytes=VMEM_BYTES)
 
     def cost(multiply_adds, bytes_accessed):
@@ -424,9 +456,11 @@
     by_head = lambda lead, last: pl.BlockSpec(lead + (last,), lambda h: (0,) * len(lead) + (h,))
     square = pl.BlockSpec((2, 1, rows, rows), lambda h: (0, h, 0, 0))
     gated, gate, vqk, slope, mixed, probs, factor = pl.pallas_call(
-        functools.partial(project_kernel, n, heads),
+        functools.partial(project_kernel, parts),
         grid=(heads,),
-        in_specs=[smem] + [vmem] * (5 + n),
+        in_specs=[smem]
+        + all_of(x_own, x_theirs, stash_own, stash_theirs, keep)
+        + [by_head((x.shape[0],), wide) for x in in_parts],
         out_specs=[
             by_head((3, rows), HEAD_DIM),
             by_head((2, rows), HEAD_DIM),
@@ -449,23 +483,29 @@
         compiler_params=params,
         cost_estimate=cost(3 * matmul, 2 * weight_bytes),
         name="project",
-    )(offs, x_own, x_theirs, stash_own, stash_theirs, keep, *in_parts)
+    )(in_offs, x_own, x_theirs, stash_own, stash_theirs, keep, *in_parts)
 
     def backward(ups, tick_no):
-        saved = [gate, vqk, slope, mixed, probs, factor]
+        layered = [gate, vqk, slope, mixed, probs, factor, stash_own, stash_theirs]
+        plain = list(out_parts) + list(in_parts)
         return pl.pallas_call(
-            functools.partial(backward_kernel, n, heads, tick_no),
-            in_specs=[smem] * 2 + [vmem] * (3 + len(saved) + 2 * n),
-            out_specs=[vmem] * 2,
+            functools.partial(backward_kernel, parts, n, tick_no),
+            grid=(1,),
+            in_specs=[smem] * 3 + [hbm] * (1 + len(layered) + len(plain)),
+            out_specs=all_of(*halves),
             out_shape=halves,
-            scratch_shapes=[
+            scratch_shapes=[pltpu.VMEM(ups.shape, BF16)]
+            + [pltpu.VMEM(x.shape[1:], x.dtype) for x in layered]
+            + [pltpu.VMEM(x.shape, x.dtype) for x in plain]
+            + [
                 pltpu.VMEM((rows, width), F32),
                 pltpu.VMEM((rows, width), BF16),
+                pltpu.SemaphoreType.DMA((1 + len(layered) + len(plain),)),
             ],
             compiler_params=params,
             cost_estimate=cost(2 * matmul, 2 * weight_bytes),
             name="backward",
-        )(core, offs, ups, stash_own, stash_theirs, *saved, *out_parts, *in_parts)
+        )(core, in_offs, offs, ups, *layered, *plain)
 
     gated, new_theirs = lax.optimization_barrier((gated, new_theirs))
 
@@ -475,12 +515,14 @@
     def own_rows(mine, others):
         return lax.dynamic_slice_in_dim(jnp.stack([mine, others]), core_no * share, share, axis=1)
 
+    pack_shapes = [struct((rows, width), BF16)]
+    pack_shapes += [struct((rows, 2 * slab + depth), BF16)] * (n - 1)
     up_0, *packs = pl.pallas_call(
         functools.partial(pack_kernel, n),
-        in_specs=[smem] + [vmem] * 3,
-        out_specs=[vmem] * n,
-        out_shape=[struct((rows, width), BF16)]
-        + [struct((rows, 2 * slab + depth), BF16)] * (n - 1),
+        grid=(1,),
+        in_specs=[smem] + all_of(gated, up_own, up_theirs),
+        out_specs=all_of(*pack_shapes),
+        out_shape=pack_shapes,
         compiler_params=params,
         name="pack",
     )(offs, gated, up_own, up_theirs)
@@ -488,8 +530,9 @@
 
     ahead_send, ahead_keep = pl.pallas_call(
         functools.partial(out_kernel, n),
-        in_specs=[smem] * 2 + [vmem] * (1 + n),
-        out_specs=[vmem] * 2,
+        grid=(1,),
+        in_specs=[smem] * 2 + [row_of(gated, 0)] + all_of(*out_parts),
+        out_specs=all_of(*halves),
         out_shape=halves,
         scratch_shapes=[pltpu.VMEM((rows, width), BF16)],
         compiler_params=params,
@@ -509,10 +552,14 @@
     packs_beyond = [to_beyond(packs[n // 2 + m - 1], m) for m in between]
     ahead_their = swap_cores(ahead_in)
     ahead_send, ahead_keep = pl.pallas_call(
-        functools.partial(forward_kernel, n, heads),
+        functools.partial(forward_kernel, parts, heads),
         grid=(heads,),
-        in_specs=[smem] * 3 + [vmem] * (5 + 2 * n),
-        out_specs=[vmem] * 2,
+        in_specs=[smem] * 4
+        + all_of(ahead_in, ahead_their, new_own, new_theirs)
+        + [row_of(keep, keep.shape[0] - 1)]
+        + [by_head((x.shape[0],), wide) for x in in_parts]
+        + all_of(*out_parts),
+        out_specs=all_of(*halves),
         out_shape=halves,
         scratch_shapes=[
             pltpu.VMEM((rows, width), BF16),
@@ -524,7 +571,17 @@
         cost_estimate=cost(2 * matmul, 2 * weight_bytes),
         name="forward",
     )(
-        core, offs, first_flag, ahead_in, ahead_their, new_own, new_theirs, keep, *in_parts, *out_parts
+        core,
+        in_offs,
+        offs,
+        first_flag,
+        ahead_in,
+        ahead_their,
+        new_own,
+        new_theirs,
+        keep,
+        *in_parts,
+        *out_parts,
     )
     ahead_send, ahead_keep, back_in, packs_beyond = lax.optimization_barrier(
         (ahead_send, ahead_keep, back_in, packs_beyond)
@@ -535,16 +592,18 @@
     )
 
     back_their = swap_cores(back_in)
-    up_1, *pieces = pl.pallas_call(
+    cut_shapes = [struct((rows, width), BF16)] + [struct((rows, depth), BF16)] * (n - 1)
+    up_1, *cuts = pl.pallas_call(
         functools.partial(gather_kernel, n),
-        in_specs=[smem] * 3 + [vmem] * 4,
-        out_specs=[vmem] * n,
-        out_shape=[struct((rows, width), BF16)] + [struct((rows, depth), BF16)] * (n - 1),
+        grid=(1,),
+        in_specs=[smem] * 3 + all_of(back_in, back_their, new_own, new_theirs),
+        out_specs=all_of(*cut_shapes),
+        out_shape=cut_shapes,
         compiler_params=params,
         name="gather",
     )(core, offs, last_flag, back_in, back_their, new_own, new_theirs)
-    landed = [to_partner(pieces[0])] + [from_host(pieces[m], m) for m in between]
-    landed += [to_beyond(pieces[n // 2 + m - 1], m) for m in between]
+    landed = [to_partner(cuts[0])] + [from_host(cuts[m], m) for m in between]
+    landed += [to_beyond(cuts[n // 2 + m - 1], m) for m in between]
     back_send, back_keep = backward(up_1, 1)
     back_send, back_keep, landed = lax.optimization_barrier((back_send, back_keep, landed))
     back_1 = summed(
@@ -553,8 +612,9 @@
 
     grads = pl.pallas_call(
         functools.partial(grads_kernel, n, (ticks * length * n) ** (-0.5)),
-        in_specs=[smem] * 2 + [vmem] * (3 + 2 * (n - 1)),
-        out_specs=vmem,
+        grid=(1,),
+        in_specs=[smem] * 2 + all_of(gated, up_0, up_1, *packs_near, *packs_beyond, *landed),
+        out_specs=pl.BlockSpec((slab, depth), lambda *_: (0, 0)),
         out_shape=struct((slab, depth), F32),
         compiler_params=params,
         cost_estimate=cost(matmul // 4, weight_bytes // 4),

time: 248 us -> 217 us (0.88)
  local copies, waits for them, and re-layouts: 65.2 us -> 15 us
  waiting for transfers between devices: 69.4 us -> 80.2 us
  Pallas kernels: 42.9 us -> 48.8 us
  starting transfers between devices: 51.2 us -> 56.1 us
  other arithmetic: 14.9 us -> 11.7 us
    unnamed x144 -> x80, local copies, waits for them, and re-layouts: 51.2 us -> 9.04 us
    ppermute x7 -> x8, waiting for transfers between devices: 53.6 us -> 60.6 us  [from_partner(): return lax.ppermute(x, 'dp', [(h ^ 1, h) for h in hosts])]
    pallas_call x7, Pallas kernels: 40 us -> 45.7 us  [the longest x2 18.9 us: backward(): pl.pallas_call(functools.partial(backward_kernel, parts, n, tick_no), gri...]
    eq x4, local copies, waits for them, and re-layouts: 5.83 us -> 0.54 us  [block_keep(): jnp.repeat(jnp.repeat(block_marks, BLOCK, axis=-2), BLOCK, axis=-1) == 1]
    ppermute x2, waiting for transfers between devices: 0.01 us -> 4.1 us  [to_beyond(): lax.ppermute(x, 'dp', [(hosts[k ^ m], hosts[k] ^ 1) for k in range(n // 2)])]
    slice x0 -> x1, local copies, waits for them, and re-layouts: none -> 3.13 us  [per_device(): in_shard[i * piece:(i + 1) * piece]]
    ppermute x7 -> x8, starting transfers between devices: 24.6 us -> 27.2 us  [from_partner(): return lax.ppermute(x, 'dp', [(h ^ 1, h) for h in hosts])]
    ppermute x6 -> x7, starting transfers between devices: 5.76 us -> 6.99 us  [from_host(): lax.ppermute(x, 'dp', [(hosts[k ^ m], hosts[k]) for k in range(n // 2)])]
  transfers between devices with their start and end apart: 28 -> 30, of which waited for: 4 -> 9; matrix products, arithmetic and copies ran while one was open for 9% -> 7% of each run, Pallas kernels for 17% -> 22%
where the time goes in v4:
time: 217 us; the launch traced here: 215 us
  waiting for transfers between devices  80.2 us (37%)
  starting transfers between devices  56.1 us (26%)
  Pallas kernels  48.8 us (22%)
  local copies, waits for them, and re-layouts  15 us (7%)
  other arithmetic  11.7 us (5%)
  between operations  3.34 us (2%)
    ppermute x8, waiting for transfers between devices, from_partner(): return lax.ppermute(x, 'dp', [(h ^ 1, h) for h in hosts])  60.6 us
    ppermute x8, starting transfers between devices, from_partner(): return lax.ppermute(x, 'dp', [(h ^ 1, h) for h in hosts])  27.2 us
    pallas_call x2, Pallas kernels, backward(): pl.pallas_call(functools.partial(backward_kernel, parts, n, tick_no), gri...  18.9 us
    ppermute x5, waiting for transfers between devices, to_partner(): return lax.ppermute(x, 'dp', [(h, h ^ 1) for h in hosts])  15.4 us
    pallas_call x1, Pallas kernels, per_device(): pl.pallas_call(functools.partial(project_kernel, parts), grid=(heads,), i...  13.6 us
    unnamed x80, local copies, waits for them, and re-layouts  9.04 us
    pallas_call x1, Pallas kernels, per_device(): pl.pallas_call(functools.partial(forward_kernel, parts, heads), grid=(hea...  8.54 us
    ppermute x7, starting transfers between devices, from_host(): lax.ppermute(x, 'dp', [(hosts[k ^ m], hosts[k]) for k in range(n // 2)])  6.99 us
  transfers between devices with their start and end apart: 30, of which 9 were waited for; matrix products, arithmetic and copies ran while one was open for 7% of the time, Pallas kernels for 22%

profile of v4, /device:TPU:5, one launch (start us, length us, event | category | flops | bytes accessed | tf_op | source)
XLA Modules:
  0.0 215.0 jit_solution(18315174761336039609)
XLA Ops:
  1.6 3.1 %slice_bitcast_fusion = (bf16[256,2048]{1,0:T(8,128)(2,1)}, bf16[256,2048]{1,0:T(8,128)(2,1)}) fusion(bf16[1,512,2048]{2,1,0:T(8,128)(2,1)} %param.17), kind=kLoop, calls=%fused_computation | loop fusion | bytes 4194304 | tf_op jit(solution)/shard_map/slice | solution.py:361
  4.8 6.7 %collective-permute-start.1 = (bf16[256,2048]{1,0:T(8,128)(2,1)}, bf16[256,2048]{1,0:T(8,128)(2,1)}, u32[]{:S(2)}, u32[]{:S(2)}) collective-permute-start(bf16[256,2048]{1,0:T(8,128)(2,1)} %get-tuple-element.132), channel_id=1, source_target_pairs={{0,2},{6,4},{1,3},{7,5},{8,10},{14,12},{9,11},{15,13},{16,18},{22,... | collective-permute-start | bytes 3145736 | tf_op jit(solution)/shard_map/ppermute | solution.py:333
  11.5 2.3 %collective-permute-start.2 = (bf16[256,2048]{1,0:T(8,128)(2,1)}, bf16[256,2048]{1,0:T(8,128)(2,1)}, u32[]{:S(2)}, u32[]{:S(2)}) collective-permute-start(bf16[256,2048]{1,0:T(8,128)(2,1)} %get-tuple-element.131), channel_id=1, source_target_pairs={{0,2},{6,4},{1,3},{7,5},{8,10},{14,12},{9,11},{15,13},{16,18},{22,... | collective-permute-start | bytes 3145736 | tf_op jit(solution)/shard_map/ppermute | solution.py:333
  16.6 15.7 %collective-permute-done.1.rest_2_.rest_15_ = bf16[256,2048]{1,0:T(8,128)(2,1)} collective-permute-done((bf16[256,2048]{1,0:T(8,128)(2,1)}, bf16[256,2048]{1,0:T(8,128)(2,1)}, u32[]{:S(2)}, u32[]{:S(2)}) %collective-permute-start.1) | collective-permute-done | bytes 1048608 | tf_op jit(solution)/shard_map/ppermute | solution.py:333
  32.3 1.7 collective-permute-start.6
  34.0 20.8 %collective-permute-done.2.rest_3_.rest_16_ = bf16[256,2048]{1,0:T(8,128)(2,1)} collective-permute-done((bf16[256,2048]{1,0:T(8,128)(2,1)}, bf16[256,2048]{1,0:T(8,128)(2,1)}, u32[]{:S(2)}, u32[]{:S(2)}) %collective-permute-start.2) | collective-permute-done | bytes 1048608 | tf_op jit(solution)/shard_map/ppermute | solution.py:333
  55.3 4.1 %collective-permute-start.5 = (s32[2,5,17]{2,0,1:T(2,128)S(1)}, s32[2,5,17]{2,0,1:T(2,128)S(1)}, u32[]{:S(2)}, u32[]{:S(2)}) collective-permute-start(s32[2,5,17]{2,0,1:T(2,128)S(1)} %add_add_fusion), channel_id=1, source_target_pairs={{0,2},{6,4},{1,3},{7,5},{8,10},{14,12},{9,11},{15,13},{16,18},{22,... | collective-permute-start | bytes 2048 | tf_op jit(solution)/shard_map/ppermute | solution.py:333
  59.4 1.3 collective-permute-start.3
  60.8 1.6 collective-permute-start.7
  62.4 1.7 slice_select_fusion
  64.2 1.7 collective-permute-start.4
  66.9 17.3 %collective-permute-done.4.x_theirs = bf16[96,2048]{1,0:T(8,128)(2,1)S(1)} collective-permute-done((bf16[96,2048]{1,0:T(8,128)(2,1)S(1)}, bf16[96,2048]{1,0:T(8,128)(2,1)S(1)}, u32[]{:S(2)}, u32[]{:S(2)}) %collective-permute-start.4) | collective-permute-done | bytes 393248 | tf_op jit(solution)/shard_map/ppermute | solution.py:333
  85.9 4.2 %collective-permute-start.10 = (bf16[512,512]{1,0:T(8,128)(2,1)S(1)}, bf16[512,512]{1,0:T(8,128)(2,1)S(1)}, u32[]{:S(2)}, u32[]{:S(2)}) collective-permute-start(bf16[512,512]{1,0:T(8,128)(2,1)S(1)} %bitcast.80), channel_id=1, source_target_pairs={{0,2},{6,4},{1,3},{7,5},{8,10},{14,12},{9,11},{15,13},{16,18},{22,... | collective-permute-start | bytes 1572872 | tf_op jit(solution)/shard_map/ppermute | solution.py:333
  91.8 6.8 %collective-permute-done.10.rest_1_.rest_10_.rest_7_ = bf16[512,512]{1,0:T(8,128)(2,1)S(1)} collective-permute-done((bf16[512,512]{1,0:T(8,128)(2,1)S(1)}, bf16[512,512]{1,0:T(8,128)(2,1)S(1)}, u32[]{:S(2)}, u32[]{:S(2)}) %collective-permute-start.10) | collective-permute-done | bytes 524320 | tf_op jit(solution)/shard_map/ppermute | solution.py:333
  100.4 5.5 %collective-permute-start.8 = (bf16[96,2048]{1,0:T(8,128)(2,1)S(1)}, bf16[96,2048]{1,0:T(8,128)(2,1)S(1)}, u32[]{:S(2)}, u32[]{:S(2)}) collective-permute-start(bf16[96,2048]{1,0:T(8,128)(2,1)S(1)} %bitcast.86), channel_id=1, source_target_pairs={{0,2},{6,4},{1,3},{7,5},{8,10},{14,12},{9,11},{15,13},{16,18},{22,... | collective-permute-start | bytes 1179656 | tf_op jit(solution)/shard_map/ppermute | solution.py:333
  107.3 13.6 %project.1 = (bf16[3,192,512]{2,1,0:T(8,128)(2,1)S(1)}, f32[2,192,512]{2,1,0:T(8,128)S(1)}, bf16[2,192,1536]{2,1,0:T(8,128)(2,1)}, f32[2,192,2048]{2,1,0:T(8,128...) custom-call(s32[6]{0:T(128)S(1)} %stack.95.offs.in_offs, ...), custom_call_target="tpu_custom_call" | custom-call | flops 4831838208 | bytes 20971520 | tf_op jit(solution)/shard_map/project/pallas_call | solution.py:458
  124.3 1.5 pack.1
  126.8 1.9 out.1
  129.4 4.1 %collective-permute-start.13 = (bf16[2,48,2048]{2,1,0:T(8,128)(2,1)}, bf16[2,48,2048]{2,1,0:T(8,128)(2,1)}, u32[]{:S(2)}, u32[]{:S(2)}) collective-permute-start(bf16[2,48,2048]{2,1,0:T(8,128)(2,1)} %get-tuple-element.94), channel_id=1, source_target_pairs={{0,1},{1,0},{2,3},{3,2},{4,5},{5,4},{6,7},{7,6},{8,9},{9,8},{10,11... | collective-permute-start | bytes 1179656 | tf_op jit(solution)/shard_map/ppermute | solution.py:347
  133.5 1.4 collective-permute-start.15
  135.7 1.4 add_convert_fusion.3
  137.1 3.1 %collective-permute-start.14 = (bf16[2,48,2048]{2,1,0:T(8,128)(2,1)S(1)}, bf16[2,48,2048]{2,1,0:T(8,128)(2,1)}, u32[]{:S(2)}, u32[]{:S(2)}) collective-permute-start(bf16[2,48,2048]{2,1,0:T(8,128)(2,1)S(1)} %add_convert_fusion.3), channel_id=1, source_target_pairs={{0,8},{8,16},{16,24},{1,9},{9,17},{17,25},{2,10},{10,18},{18,26},{... | collective-permute-start | bytes 1179656 | tf_op jit(solution)/shard_map/ppermute | solution.py:351
  140.2 9.4 %backward.2 = (bf16[2,48,2048]{2,1,0:T(8,128)(2,1)S(1)}, bf16[2,48,2048]{2,1,0:T(8,128)(2,1)S(1)}) custom-call(s32[1]{0:T(128)} %bitcast.10.core, s32[6]{0:T(128)S(1)} %stack.95.offs.in_offs, s32[4]{0:T(128)S(1)} %add_multiply_fusion.offs, bf16[192,2048]{1,0:T(8,128)(2,1)S(1)} %copy-done.10, f32[2,192,512]{2,1,0:T(8,128)} %copy-done.6, ...), custom_call_target="tpu_custom_call" | custom-call | flops 3221225472 | bytes 20971520 | tf_op jit(solution)/shard_map/backward/pallas_call | solution.py:491
  153.9 3.2 %collective-permute-start.20 = (bf16[2,48,2048]{2,1,0:T(8,128)(2,1)}, bf16[2,48,2048]{2,1,0:T(8,128)(2,1)}, u32[]{:S(2)}, u32[]{:S(2)}) collective-permute-start(bf16[2,48,2048]{2,1,0:T(8,128)(2,1)} %add_convert_fusion.2), channel_id=1, source_target_pairs={{8,0},{16,8},{24,16},{9,1},{17,9},{25,17},{10,2},{18,10},{26,18},{... | collective-permute-start | bytes 1179656 | tf_op jit(solution)/shard_map/ppermute | solution.py:351
  157.2 8.5 %forward.1 = (bf16[2,48,2048]{2,1,0:T(8,128)(2,1)S(1)}, bf16[2,48,2048]{2,1,0:T(8,128)(2,1)S(1)}) custom-call(s32[1]{0:T(128)} %bitcast.10.core, s32[6]{0:T(128)S(1)} %stack.95.offs.in_offs, s32[4]{0:T(128)S(1)} %add_multiply_fusion.offs, s32[1]{0:T(128)} %bitcast.35.fresh, bf16[2,48,2048]{2,1,0:T(8,128)(2,1)} %collective-permute-done.14.mine, ...), custom_call_target="tpu_custom_call" | custom-call | flops 3221225472 | bytes 20971520 | tf_op jit(solution)/shard_map/forward/pallas_call | solution.py:554
  167.2 4.1 %collective-permute-done.21.rest_2_ = bf16[192,1536]{1,0:T(8,128)(2,1)} collective-permute-done((bf16[192,1536]{1,0:T(8,128)(2,1)}, bf16[192,1536]{1,0:T(8,128)(2,1)}, u32[]{:S(2)}, u32[]{:S(2)}) %collective-permute-start.21) | collective-permute-done | bytes 589856 | tf_op jit(solution)/shard_map/ppermute | solution.py:342
  180.3 9.4 %backward.3 = (bf16[2,48,2048]{2,1,0:T(8,128)(2,1)S(1)}, bf16[2,48,2048]{2,1,0:T(8,128)(2,1)S(1)}) custom-call(s32[1]{0:T(128)} %bitcast.10.core, s32[6]{0:T(128)S(1)} %stack.95.offs.in_offs, s32[4]{0:T(128)S(1)} %add_multiply_fusion.offs, bf16[192,2048]{1,0:T(8,128)(2,1)S(1)} %get-tuple-element.117.rest_0_.up_1, f32[2,192,512]{2,1,0:T(8,128)} %copy-done.6, ...), custom_call_target="tpu_custom_call" | custom-call | flops 3221225472 | bytes 20971520 | tf_op jit(solution)/shard_map/backward/pallas_call | solution.py:491
  189.8 5.1 %collective-permute-done.25.rest_3_ = bf16[192,512]{1,0:T(8,128)(2,1)S(1)} collective-permute-done((bf16[192,512]{1,0:T(8,128)(2,1)S(1)}, bf16[192,512]{1,0:T(8,128)(2,1)S(1)}, u32[]{:S(2)}, u32[]{:S(2)}) %collective-permute-start.25) | collective-permute-done | bytes 196640 | tf_op jit(solution)/shard_map/ppermute | solution.py:336
  196.9 3.1 %grads.1 = f32[512,512]{1,0:T(8,128)} custom-call(s32[1]{0:T(128)} %bitcast.45.host, s32[4]{0:T(128)S(1)} %add_multiply_fusion.offs, bf16[3,192,512]{2,1,0:T(8,128)(2,1)S(1)} %get-tuple-element.83.gated, bf16[192,2048]{1,0:T(8,128)(2,1)S(1)} %copy-done.11, bf16[192,2048]{1,0:T(8,128)(2,1)} %copy-done.12, bf16[192,1536]{1,0:T(8,128)(2,1)S(1)} %copy-done.18, ...), custom_call_target="tpu_custom_call" | custom-call | flops 402653184 | bytes 2621440 | tf_op jit(solution)/shard_map/grads/pallas_call | solution.py:613
  200.0 1.6 add_convert_fusion
  204.2 5.8 %collective-permute-done.23 = bf16[48,2048]{1,0:T(8,128)(2,1)S(1)} collective-permute-done((bf16[48,2048]{1,0:T(8,128)(2,1)S(1)}, bf16[48,2048]{1,0:T(8,128)(2,1)S(1)}, u32[]{:S(2)}, u32[]{:S(2)}) %collective-permute-start.23) | collective-permute-done | bytes 196640 | tf_op jit(solution)/shard_map/ppermute | solution.py:336
  210.8 3.4 %collective-permute-done.29 = bf16[48,2048]{1,0:T(8,128)(2,1)S(1)} collective-permute-done((bf16[48,2048]{1,0:T(8,128)(2,1)S(1)}, bf16[48,2048]{1,0:T(8,128)(2,1)S(1)}, u32[]{:S(2)}, u32[]{:S(2)}) %collective-permute-start.29) | collective-permute-done | bytes 196640 | tf_op jit(solution)/shard_map/ppermute | solution.py:336
  (158 shorter events, 36.3 us)
Async XLA Ops:
  0.7 58.7 %copy-start.30 = (bf16[1,2,96,2048]{3,2,1,0:T(8,128)(2,1)S(1)}, bf16[1,2,96,2048]{3,2,1,0:T(8,128)(2,1)}, u32[]{:S(2)}) copy-start(bf16[1,2,96,2048]{3,2,1,0:T(8,128)(2,1)} %param.16) | copy-start | bytes 2359300
  0.7 54.1 %collective-permute-start = (bf16[512,2048]{1,0:T(8,128)(2,1)}, bf16[512,2048]{1,0:T(8,128)(2,1)S(1)}, u32[]{:S(2)}, u32[]{:S(2)}) collective-permute-start(bf16[512,2048]{1,0:T(8,128)(2,1)} %bitcast.96), channel_id=1, source_target_pairs={{4,2},{2,4},{5,3},{3,5},{12,10},{10,12},{13,11},{11,13},{20,18},{1... | collective-permute-start | bytes 6291464 | tf_op jit(solution)/shard_map/ppermute | solution.py:339
  4.8 81.1 %copy-start = (bf16[1,512,512]{2,1,0:T(8,128)(2,1)S(1)}, bf16[1,512,512]{2,1,0:T(8,128)(2,1)}, u32[]{:S(2)}) copy-start(bf16[1,512,512]{2,1,0:T(8,128)(2,1)} %param.18) | copy-start | bytes 1572868
  4.8 27.5 %collective-permute-start.1 = (bf16[256,2048]{1,0:T(8,128)(2,1)}, bf16[256,2048]{1,0:T(8,128)(2,1)}, u32[]{:S(2)}, u32[]{:S(2)}) collective-permute-start(bf16[256,2048]{1,0:T(8,128)(2,1)} %get-tuple-element.132), channel_id=1, source_target_pairs={{0,2},{6,4},{1,3},{7,5},{8,10},{14,12},{9,11},{15,13},{16,18},{22,... | collective-permute-start | bytes 3145736 | tf_op jit(solution)/shard_map/ppermute | solution.py:333
  11.5 43.3 %collective-permute-start.2 = (bf16[256,2048]{1,0:T(8,128)(2,1)}, bf16[256,2048]{1,0:T(8,128)(2,1)}, u32[]{:S(2)}, u32[]{:S(2)}) collective-permute-start(bf16[256,2048]{1,0:T(8,128)(2,1)} %get-tuple-element.131), channel_id=1, source_target_pairs={{0,2},{6,4},{1,3},{7,5},{8,10},{14,12},{9,11},{15,13},{16,18},{22,... | collective-permute-start | bytes 3145736 | tf_op jit(solution)/shard_map/ppermute | solution.py:333
  32.3 73.6 %collective-permute-start.6 = (bf16[256,2048]{1,0:T(8,128)(2,1)}, bf16[256,2048]{1,0:T(8,128)(2,1)}, u32[]{:S(2)}, u32[]{:S(2)}) collective-permute-start(bf16[256,2048]{1,0:T(8,128)(2,1)} %collective-permute-done.1.rest_2_.rest_15_), channel_id=1, source_target_pairs={{4,2},{2,4},{5,3},{3,5},{12,10},{10,12},{13,11},{11,13},{20,18},{1... | collective-permute-start | bytes 3145736 | tf_op jit(solution)/shard_map/ppermute | solution.py:339
  55.3 11.3 %collective-permute-start.5 = (s32[2,5,17]{2,0,1:T(2,128)S(1)}, s32[2,5,17]{2,0,1:T(2,128)S(1)}, u32[]{:S(2)}, u32[]{:S(2)}) collective-permute-start(s32[2,5,17]{2,0,1:T(2,128)S(1)} %add_add_fusion), channel_id=1, source_target_pairs={{0,2},{6,4},{1,3},{7,5},{8,10},{14,12},{9,11},{15,13},{16,18},{22,... | collective-permute-start | bytes 2048 | tf_op jit(solution)/shard_map/ppermute | solution.py:333
  59.4 25.5 %collective-permute-start.3 = (bf16[2,96,2048]{2,1,0:T(8,128)(2,1)S(1)}, bf16[2,96,2048]{2,1,0:T(8,128)(2,1)S(1)}, u32[]{:S(2)}, u32[]{:S(2)}) collective-permute-start(bf16[2,96,2048]{2,1,0:T(8,128)(2,1)S(1)} %bitcast.104), channel_id=1, source_target_pairs={{0,2},{6,4},{1,3},{7,5},{8,10},{14,12},{9,11},{15,13},{16,18},{22,... | collective-permute-start | bytes 2359304 | tf_op jit(solution)/shard_map/ppermute | solution.py:333
  60.8 46.4 %collective-permute-start.7 = (bf16[256,2048]{1,0:T(8,128)(2,1)}, bf16[256,2048]{1,0:T(8,128)(2,1)}, u32[]{:S(2)}, u32[]{:S(2)}) collective-permute-start(bf16[256,2048]{1,0:T(8,128)(2,1)} %collective-permute-done.2.rest_3_.rest_16_), channel_id=1, source_target_pairs={{4,2},{2,4},{5,3},{3,5},{12,10},{10,12},{13,11},{11,13},{20,18},{1... | collective-permute-start | bytes 3145736 | tf_op jit(solution)/shard_map/ppermute | solution.py:339
  64.2 20.1 %collective-permute-start.4 = (bf16[96,2048]{1,0:T(8,128)(2,1)S(1)}, bf16[96,2048]{1,0:T(8,128)(2,1)S(1)}, u32[]{:S(2)}, u32[]{:S(2)}) collective-permute-start(bf16[96,2048]{1,0:T(8,128)(2,1)S(1)} %bitcast.93), channel_id=1, source_target_pairs={{0,2},{6,4},{1,3},{7,5},{8,10},{14,12},{9,11},{15,13},{16,18},{22,... | collective-permute-start | bytes 1179656 | tf_op jit(solution)/shard_map/ppermute | solution.py:333
  85.9 12.8 %collective-permute-start.10 = (bf16[512,512]{1,0:T(8,128)(2,1)S(1)}, bf16[512,512]{1,0:T(8,128)(2,1)S(1)}, u32[]{:S(2)}, u32[]{:S(2)}) collective-permute-start(bf16[512,512]{1,0:T(8,128)(2,1)S(1)} %bitcast.80), channel_id=1, source_target_pairs={{0,2},{6,4},{1,3},{7,5},{8,10},{14,12},{9,11},{15,13},{16,18},{22,... | collective-permute-start | bytes 1572872 | tf_op jit(solution)/shard_map/ppermute | solution.py:333
  91.1 35.6 %collective-permute-start.11 = (bf16[512,512]{1,0:T(8,128)(2,1)S(1)}, bf16[512,512]{1,0:T(8,128)(2,1)S(1)}, u32[]{:S(2)}, u32[]{:S(2)}) collective-permute-start(bf16[512,512]{1,0:T(8,128)(2,1)S(1)} %bitcast.81), channel_id=1, source_target_pairs={{4,2},{2,4},{5,3},{3,5},{12,10},{10,12},{13,11},{11,13},{20,18},{1... | collective-permute-start | bytes 1572872 | tf_op jit(solution)/shard_map/ppermute | solution.py:339
  98.6 28.1 %collective-permute-start.12 = (bf16[512,512]{1,0:T(8,128)(2,1)S(1)}, bf16[512,512]{1,0:T(8,128)(2,1)S(1)}, u32[]{:S(2)}, u32[]{:S(2)}) collective-permute-start(bf16[512,512]{1,0:T(8,128)(2,1)S(1)} %collective-permute-done.10.rest_1_.rest_10_.rest_7_), channel_id=1, source_target_pairs={{4,2},{2,4},{5,3},{3,5},{12,10},{10,12},{13,11},{11,13},{20,18},{1... | collective-permute-start | bytes 1572872 | tf_op jit(solution)/shard_map/ppermute | solution.py:339
  100.4 23.2 %collective-permute-start.8 = (bf16[96,2048]{1,0:T(8,128)(2,1)S(1)}, bf16[96,2048]{1,0:T(8,128)(2,1)S(1)}, u32[]{:S(2)}, u32[]{:S(2)}) collective-permute-start(bf16[96,2048]{1,0:T(8,128)(2,1)S(1)} %bitcast.86), channel_id=1, source_target_pairs={{0,2},{6,4},{1,3},{7,5},{8,10},{14,12},{9,11},{15,13},{16,18},{22,... | collective-permute-start | bytes 1179656 | tf_op jit(solution)/shard_map/ppermute | solution.py:333
  105.9 18.4 %collective-permute-start.9 = (bf16[96,2048]{1,0:T(8,128)(2,1)S(1)}, bf16[96,2048]{1,0:T(8,128)(2,1)S(1)}, u32[]{:S(2)}, u32[]{:S(2)}) collective-permute-start(bf16[96,2048]{1,0:T(8,128)(2,1)S(1)} %bitcast.89), channel_id=1, source_target_pairs={{0,2},{6,4},{1,3},{7,5},{8,10},{14,12},{9,11},{15,13},{16,18},{22,... | collective-permute-start | bytes 1179656 | tf_op jit(solution)/shard_map/ppermute | solution.py:333
  129.4 6.2 %collective-permute-start.13 = (bf16[2,48,2048]{2,1,0:T(8,128)(2,1)}, bf16[2,48,2048]{2,1,0:T(8,128)(2,1)}, u32[]{:S(2)}, u32[]{:S(2)}) collective-permute-start(bf16[2,48,2048]{2,1,0:T(8,128)(2,1)} %get-tuple-element.94), channel_id=1, source_target_pairs={{0,1},{1,0},{2,3},{3,2},{4,5},{5,4},{6,7},{7,6},{8,9},{9,8},{10,11... | collective-permute-start | bytes 1179656 | tf_op jit(solution)/shard_map/ppermute | solution.py:347
  133.5 17.3 %collective-permute-start.15 = (bf16[192,1536]{1,0:T(8,128)(2,1)}, bf16[192,1536]{1,0:T(8,128)(2,1)S(1)}, u32[]{:S(2)}, u32[]{:S(2)}) collective-permute-start(bf16[192,1536]{1,0:T(8,128)(2,1)} %copy-done.27), channel_id=1, source_target_pairs={{2,0},{4,6},{3,1},{5,7},{10,8},{12,14},{11,9},{13,15},{18,16},{20,... | collective-permute-start | bytes 1769480 | tf_op jit(solution)/shard_map/ppermute | solution.py:336
  135.0 15.9 %collective-permute-start.16 = (bf16[192,1536]{1,0:T(8,128)(2,1)}, bf16[192,1536]{1,0:T(8,128)(2,1)S(1)}, u32[]{:S(2)}, u32[]{:S(2)}) collective-permute-start(bf16[192,1536]{1,0:T(8,128)(2,1)} %copy-done.26), channel_id=1, source_target_pairs={{4,2},{2,4},{5,3},{3,5},{12,10},{10,12},{13,11},{11,13},{20,18},{1... | collective-permute-start | bytes 1769480 | tf_op jit(solution)/shard_map/ppermute | solution.py:339
  137.1 13.7 %collective-permute-start.14 = (bf16[2,48,2048]{2,1,0:T(8,128)(2,1)S(1)}, bf16[2,48,2048]{2,1,0:T(8,128)(2,1)}, u32[]{:S(2)}, u32[]{:S(2)}) collective-permute-start(bf16[2,48,2048]{2,1,0:T(8,128)(2,1)S(1)} %add_convert_fusion.3), channel_id=1, source_target_pairs={{0,8},{8,16},{16,24},{1,9},{9,17},{17,25},{2,10},{10,18},{18,26},{... | collective-permute-start | bytes 1179656 | tf_op jit(solution)/shard_map/ppermute | solution.py:351
  150.8 2.1 collective-permute-start.17
  151.6 19.7 %collective-permute-start.21 = (bf16[192,1536]{1,0:T(8,128)(2,1)}, bf16[192,1536]{1,0:T(8,128)(2,1)}, u32[]{:S(2)}, u32[]{:S(2)}) collective-permute-start(bf16[192,1536]{1,0:T(8,128)(2,1)} %get-tuple-element.113), channel_id=1, source_target_pairs={{4,0},{2,6},{5,1},{3,7},{12,8},{10,14},{13,9},{11,15},{20,16},{18,... | collective-permute-start | bytes 1769480 | tf_op jit(solution)/shard_map/ppermute | solution.py:342
  152.9 4.2 %collective-permute-start.19 = (bf16[2,48,2048]{2,1,0:T(8,128)(2,1)}, bf16[2,48,2048]{2,1,0:T(8,128)(2,1)}, u32[]{:S(2)}, u32[]{:S(2)}) collective-permute-start(bf16[2,48,2048]{2,1,0:T(8,128)(2,1)} %collective-permute-done.14.mine), channel_id=1, source_target_pairs={{0,1},{1,0},{2,3},{3,2},{4,5},{5,4},{6,7},{7,6},{8,9},{9,8},{10,11... | collective-permute-start | bytes 1179656 | tf_op jit(solution)/shard_map/ppermute | solution.py:347
  153.9 17.4 %collective-permute-start.20 = (bf16[2,48,2048]{2,1,0:T(8,128)(2,1)}, bf16[2,48,2048]{2,1,0:T(8,128)(2,1)}, u32[]{:S(2)}, u32[]{:S(2)}) collective-permute-start(bf16[2,48,2048]{2,1,0:T(8,128)(2,1)} %add_convert_fusion.2), channel_id=1, source_target_pairs={{8,0},{16,8},{24,16},{9,1},{17,9},{25,17},{10,2},{18,10},{26,18},{... | collective-permute-start | bytes 1179656 | tf_op jit(solution)/shard_map/ppermute | solution.py:351
  171.3 4.4 %collective-permute-start.24 = (bf16[2,48,2048]{2,1,0:T(8,128)(2,1)}, bf16[2,48,2048]{2,1,0:T(8,128)(2,1)}, u32[]{:S(2)}, u32[]{:S(2)}) collective-permute-start(bf16[2,48,2048]{2,1,0:T(8,128)(2,1)} %collective-permute-done.20.mine), channel_id=1, source_target_pairs={{0,1},{1,0},{2,3},{3,2},{4,5},{5,4},{6,7},{7,6},{8,9},{9,8},{10,11... | collective-permute-start | bytes 1179656 | tf_op jit(solution)/shard_map/ppermute | solution.py:347
  173.6 22.1 %collective-permute-start.18 = (bf16[2,48,2048]{2,1,0:T(8,128)(2,1)}, bf16[2,48,2048]{2,1,0:T(8,128)(2,1)}, u32[]{:S(2)}, u32[]{:S(2)}) collective-permute-start(bf16[2,48,2048]{2,1,0:T(8,128)(2,1)} %pad_maximum_fusion), channel_id=1, source_target_pairs={{2,0},{4,6},{3,1},{5,7},{10,8},{12,14},{11,9},{13,15},{18,16},{20,... | collective-permute-start | bytes 1179656 | tf_op jit(solution)/shard_map/ppermute | solution.py:336
  175.6 24.4 %collective-permute-start.22 = (bf16[2,48,2048]{2,1,0:T(8,128)(2,1)}, bf16[2,48,2048]{2,1,0:T(8,128)(2,1)S(1)}, u32[]{:S(2)}, u32[]{:S(2)}) collective-permute-start(bf16[2,48,2048]{2,1,0:T(8,128)(2,1)} %copy-done.28), channel_id=1, source_target_pairs={{0,1},{1,0},{2,3},{3,2},{4,5},{5,4},{6,7},{7,6},{8,9},{9,8},{10,11... | collective-permute-start | bytes 1179656 | tf_op jit(solution)/shard_map/ppermute | solution.py:347
  177.0 17.9 %collective-permute-start.25 = (bf16[192,512]{1,0:T(8,128)(2,1)S(1)}, bf16[192,512]{1,0:T(8,128)(2,1)S(1)}, u32[]{:S(2)}, u32[]{:S(2)}) collective-permute-start(bf16[192,512]{1,0:T(8,128)(2,1)S(1)} %get-tuple-element.120), channel_id=1, source_target_pairs={{2,0},{4,6},{3,1},{5,7},{10,8},{12,14},{11,9},{13,15},{18,16},{20,... | collective-permute-start | bytes 589832 | tf_op jit(solution)/shard_map/ppermute | solution.py:336
  178.3 16.6 %collective-permute-start.26 = (bf16[192,512]{1,0:T(8,128)(2,1)S(1)}, bf16[192,512]{1,0:T(8,128)(2,1)S(1)}, u32[]{:S(2)}, u32[]{:S(2)}) collective-permute-start(bf16[192,512]{1,0:T(8,128)(2,1)S(1)} %get-tuple-element.121), channel_id=1, source_target_pairs={{4,2},{2,4},{5,3},{3,5},{12,10},{10,12},{13,11},{11,13},{20,18},{1... | collective-permute-start | bytes 589832 | tf_op jit(solution)/shard_map/ppermute | solution.py:339
  179.0 15.9 %collective-permute-start.27 = (bf16[192,512]{1,0:T(8,128)(2,1)S(1)}, bf16[192,512]{1,0:T(8,128)(2,1)S(1)}, u32[]{:S(2)}, u32[]{:S(2)}) collective-permute-start(bf16[192,512]{1,0:T(8,128)(2,1)S(1)} %get-tuple-element.122), channel_id=1, source_target_pairs={{4,0},{2,6},{5,1},{3,7},{12,8},{10,14},{13,9},{11,15},{20,16},{18,... | collective-permute-start | bytes 589832 | tf_op jit(solution)/shard_map/ppermute | solution.py:342
  194.9 5.1 %collective-permute-start.28 = (bf16[2,48,2048]{2,1,0:T(8,128)(2,1)S(1)}, bf16[2,48,2048]{2,1,0:T(8,128)(2,1)S(1)}, u32[]{:S(2)}, u32[]{:S(2)}) collective-permute-start(bf16[2,48,2048]{2,1,0:T(8,128)(2,1)S(1)} %get-tuple-element.124), channel_id=1, source_target_pairs={{0,1},{1,0},{2,3},{3,2},{4,5},{5,4},{6,7},{7,6},{8,9},{9,8},{10,11... | collective-permute-start | bytes 1179656 | tf_op jit(solution)/shard_map/ppermute | solution.py:347
  201.6 8.4 %collective-permute-start.23 = (bf16[48,2048]{1,0:T(8,128)(2,1)S(1)}, bf16[48,2048]{1,0:T(8,128)(2,1)S(1)}, u32[]{:S(2)}, u32[]{:S(2)}) collective-permute-start(bf16[48,2048]{1,0:T(8,128)(2,1)S(1)} %slice_bitcast_fusion.4), channel_id=1, source_target_pairs={{2,0},{4,6},{3,1},{5,7},{10,8},{12,14},{11,9},{13,15},{18,16},{20,... | collective-permute-start | bytes 589832 | tf_op jit(solution)/shard_map/ppermute | solution.py:336
  202.9 11.3 %collective-permute-start.29 = (bf16[48,2048]{1,0:T(8,128)(2,1)S(1)}, bf16[48,2048]{1,0:T(8,128)(2,1)S(1)}, u32[]{:S(2)}, u32[]{:S(2)}) collective-permute-start(bf16[48,2048]{1,0:T(8,128)(2,1)S(1)} %slice_bitcast_fusion.2), channel_id=1, source_target_pairs={{2,0},{4,6},{3,1},{5,7},{10,8},{12,14},{11,9},{13,15},{18,16},{20,... | collective-permute-start | bytes 589832 | tf_op jit(solution)/shard_map/ppermute | solution.py:336
  (38 other events, 471.5 us)

commit v5 on v4

--- a/solution.py
+++ b/solution.py
@@ -12,7 +12,7 @@
 BLOCKS = 4
 EPSILON = 1e-06
 SCALING = HEAD_DIM ** (-0.5)
-VMEM_BYTES = 50 * 1024 * 1024
+VMEM_BYTES = 30 * 1024 * 1024
 
 F32 = jnp.float32
 BF16 = jnp.bfloat16
@@ -242,6 +242,18 @@
         pack[length:, 2 * slab :] = up_theirs[:, columns]
 
 
+def settle_kernel(core, fresh, own, theirs, passed, keep, landed, earlier, total, pair):
+    share = keep.shape[1]
+    here = pl.ds(pl.multiple_of(core[0] * share, share), share)
+    for r, source in enumerate((own, theirs)):
+        residual = jnp.where(fresh[0] != 0, source[here, :], passed[r])
+        total[r] = (
+            residual.astype(F32) + keep[r].astype(F32) + landed[r].astype(F32)
+        ).astype(BF16)
+    pair[0] = earlier[1]
+    pair[1] = total[1]
+
+
 def gather_kernel(n, core, offs, fresh, mine, theirs, new_own, new_theirs, whole, *pieces):
     assemble(core[0], fresh[0], mine, theirs, new_own, new_theirs, whole)
     depth = pieces[0].shape[1]
@@ -360,6 +372,7 @@
     in_near = [
         from_partner(in_shard[i * piece : (i + 1) * piece]) for i in range(pieces)
     ]
+    out_near = from_partner(out_shard)
     in_pass = [from_host(in_near[0], m) for m in between]
     in_far, in_near, rows_in, tables_in = lax.optimization_barrier(
         (
@@ -386,14 +399,14 @@
     x_theirs = from_partner(x_own)
     up_own = jnp.where(last_section, cotangent[0], grad_flight[0])
     new_own = jnp.where(first_section, arrivals[1], cotangent[1])
-    out_late, up_late, new_late, stash_theirs, x_theirs = lax.optimization_barrier(
-        (out_shard, up_own, new_own, stash_theirs, x_theirs)
-    )
-    out_near = from_partner(out_late)
-    out_far = [from_host(out_late, m) for m in between]
+    out_own, out_near, near_tables = lax.optimization_barrier((out_shard, out_near, near_tables))
+    out_far = [from_host(out_own, m) for m in between]
+    out_parts = [out_shard, out_near] + out_far + [from_host(out_near, m) for m in between]
+    up_late, new_late, stash_theirs, x_theirs = lax.optimization_barrier(
+        (up_own, new_own, stash_theirs, x_theirs)
+    )
     up_theirs = from_partner(up_late)
     new_theirs = from_partner(new_late)
-    out_parts = [out_shard, out_near] + out_far + [from_host(out_near, m) for m in between]
     far_hosts = [host_table[(dp_no // 2) ^ m] for m in between]
     owners = [dp_no, dp_no ^ 1] + far_hosts + [h ^ 1 for h in far_hosts]
     offs = jnp.stack(owners).astype(jnp.int32) * depth
@@ -404,6 +417,7 @@
     parts = len(in_parts)
     core = jnp.reshape(core_no, (1,)).astype(jnp.int32)
     first_flag = jnp.reshape(first_section, (1,)).astype(jnp.int32)
+    always = jnp.ones((1,), jnp.int32)
     host_flag = jnp.reshape(is_host, (1,)).astype(jnp.int32)
     last_flag = jnp.reshape(last_section, (1,)).astype(jnp.int32)
 
@@ -546,8 +560,19 @@
     back_send, back_keep, ahead_in, packs_near = lax.optimization_barrier(
         (back_send, back_keep, ahead_in, packs_near)
     )
-    back_0 = summed(own_rows(up_own, up_theirs), back_keep, swap_cores(back_send))
+    back_landed = swap_cores(back_send)
+    back_0, first_pair = pl.pallas_call(
+        settle_kernel,
+        grid=(1,),
+        in_specs=[smem] * 2
+        + all_of(up_own, up_theirs, back_keep, back_keep, back_landed, ahead_0),
+        out_specs=all_of(*halves),
+        out_shape=halves,
+        compiler_params=params,
+        name="settle",
+    )(core, always, up_own, up_theirs, back_keep, back_keep, back_landed, ahead_0)
     back_in = along_sections(back_0, -1)
+    first_pair = to_partner(first_pair)
 
     packs_beyond = [to_beyond(packs[n // 2 + m - 1], m) for m in between]
     ahead_their = swap_cores(ahead_in)
@@ -583,8 +608,8 @@
         *in_parts,
         *out_parts,
     )
-    ahead_send, ahead_keep, back_in, packs_beyond = lax.optimization_barrier(
-        (ahead_send, ahead_keep, back_in, packs_beyond)
+    ahead_send, ahead_keep, back_in, packs_beyond, first_pair = lax.optimization_barrier(
+        (ahead_send, ahead_keep, back_in, packs_beyond, first_pair)
     )
     new_rows = own_rows(new_own, new_theirs)
     ahead_1 = summed(
@@ -605,7 +630,10 @@
     landed = [to_partner(cuts[0])] + [from_host(cuts[m], m) for m in between]
     landed += [to_beyond(cuts[n // 2 + m - 1], m) for m in between]
     back_send, back_keep = backward(up_1, 1)
-    back_send, back_keep, landed = lax.optimization_barrier((back_send, back_keep, landed))
+    ahead_given = to_partner(ahead_1[1])
+    back_send, back_keep, landed, ahead_given = lax.optimization_barrier(
+        (back_send, back_keep, landed, ahead_given)
+    )
     back_1 = summed(
         jnp.where(last_section, new_rows, back_in), back_keep, swap_cores(back_send)
     )
@@ -620,14 +648,13 @@
         cost_estimate=cost(matmul // 4, weight_bytes // 4),
         name="grads",
     )(
-        host_flag, offs, gated, up_0, up_1, *packs_near, *packs_beyond, *landed
-    )
-
-    first_pair = to_partner(jnp.stack([ahead_0[1], back_0[1]]))
+        host_flag, offs, after(gated, back_1), up_0, up_1, *packs_near, *packs_beyond, *landed
+    )
+
     ahead = jnp.stack(
         [
             jnp.where(is_host, ahead_0[0], first_pair[0]),
-            jnp.where(is_host, ahead_1[0], to_partner(ahead_1[1])),
+            jnp.where(is_host, ahead_1[0], ahead_given),
         ]
     )
     back = jnp.stack(

time: 217 us -> 224 us (1.032)
  local copies, waits for them, and re-layouts: 15 us -> 40.4 us
  waiting for transfers between devices: 80.2 us -> 60.4 us
  other arithmetic: 11.7 us -> 14.6 us
  starting transfers between devices: 56.1 us -> 53.2 us
    unnamed x80 -> x122, local copies, waits for them, and re-layouts: 9.04 us -> 30.1 us
    ppermute x8, waiting for transfers between devices: 60.6 us -> 46.4 us  [from_partner(): return lax.ppermute(x, 'dp', [(h ^ 1, h) for h in hosts])]
    ppermute x5, waiting for transfers between devices: 15.4 us -> 10.6 us  [to_partner(): return lax.ppermute(x, 'dp', [(h, h ^ 1) for h in hosts])]
  transfers between devices with their start and end apart: 30 -> 30, of which waited for: 9 -> 7; matrix products, arithmetic and copies ran while one was open for 7% -> 10% of each run, Pallas kernels for 22% -> 21%
where the time goes in v5:
time: 224 us; the launch traced here: 221 us
  waiting for transfers between devices  60.4 us (27%)
  starting transfers between devices  53.2 us (24%)
  Pallas kernels  48.8 us (22%)
  local copies, waits for them, and re-layouts  40.4 us (18%)
  other arithmetic  14.6 us (7%)
  between operations  3.39 us (2%)
    ppermute x8, waiting for transfers between devices, from_partner(): return lax.ppermute(x, 'dp', [(h ^ 1, h) for h in hosts])  46.4 us
    unnamed x122, local copies, waits for them, and re-layouts  30.1 us
    ppermute x8, starting transfers between devices, from_partner(): return lax.ppermute(x, 'dp', [(h ^ 1, h) for h in hosts])  25.4 us
    pallas_call x2, Pallas kernels, backward(): pl.pallas_call(functools.partial(backward_kernel, parts, n, tick_no), gri...  19 us
    pallas_call x1, Pallas kernels, per_device(): pl.pallas_call(functools.partial(project_kernel, parts), grid=(heads,), i...  12.2 us
    ppermute x5, waiting for transfers between devices, to_partner(): return lax.ppermute(x, 'dp', [(h, h ^ 1) for h in hosts])  10.6 us
    pallas_call x1, Pallas kernels, per_device(): pl.pallas_call(functools.partial(forward_kernel, parts, heads), grid=(hea...  7.87 us
    ppermute x7, starting transfers between devices, from_host(): lax.ppermute(x, 'dp', [(hosts[k ^ m], hosts[k]) for k in range(n // 2)])  7.09 us
  transfers between devices with their start and end apart: 30, of which 7 were waited for; matrix products, arithmetic and copies ran while one was open for 10% of the time, Pallas kernels for 21%

profile of v5, /device:TPU:5, one launch (start us, length us, event | category | flops | bytes accessed | tf_op | source)
XLA Modules:
  0.0 220.7 jit_solution(3848558721974319441)
XLA Ops:
  1.6 3.1 %slice_bitcast_fusion = (bf16[256,2048]{1,0:T(8,128)(2,1)}, bf16[256,2048]{1,0:T(8,128)(2,1)}) fusion(bf16[1,512,2048]{2,1,0:T(8,128)(2,1)} %param.17), kind=kLoop, calls=%fused_computation | loop fusion | bytes 4194304 | tf_op jit(solution)/shard_map/slice | solution.py:373
  4.7 5.7 %collective-permute-start.1 = (bf16[256,2048]{1,0:T(8,128)(2,1)}, bf16[256,2048]{1,0:T(8,128)(2,1)S(1)}, u32[]{:S(2)}, u32[]{:S(2)}) collective-permute-start(bf16[256,2048]{1,0:T(8,128)(2,1)} %get-tuple-element.146), channel_id=1, source_target_pairs={{0,2},{6,4},{1,3},{7,5},{8,10},{14,12},{9,11},{15,13},{16,18},{22,... | collective-permute-start | bytes 3145736 | tf_op jit(solution)/shard_map/ppermute | solution.py:345
  10.4 2.3 %collective-permute-start.2 = (bf16[256,2048]{1,0:T(8,128)(2,1)}, bf16[256,2048]{1,0:T(8,128)(2,1)}, u32[]{:S(2)}, u32[]{:S(2)}) collective-permute-start(bf16[256,2048]{1,0:T(8,128)(2,1)} %get-tuple-element.145), channel_id=1, source_target_pairs={{0,2},{6,4},{1,3},{7,5},{8,10},{14,12},{9,11},{15,13},{16,18},{22,... | collective-permute-start | bytes 3145736 | tf_op jit(solution)/shard_map/ppermute | solution.py:345
  12.7 2.1 collective-permute-start.5
  18.2 14.0 %collective-permute-done.1.rest_2_.rest_15_ = bf16[256,2048]{1,0:T(8,128)(2,1)S(1)} collective-permute-done((bf16[256,2048]{1,0:T(8,128)(2,1)}, bf16[256,2048]{1,0:T(8,128)(2,1)S(1)}, u32[]{:S(2)}, u32[]{:S(2)}) %collective-permute-start.1) | collective-permute-done | bytes 1048608 | tf_op jit(solution)/shard_map/ppermute | solution.py:345
  32.1 1.6 collective-permute-start.7
  33.8 20.8 %collective-permute-done.2.rest_3_.rest_16_ = bf16[256,2048]{1,0:T(8,128)(2,1)} collective-permute-done((bf16[256,2048]{1,0:T(8,128)(2,1)}, bf16[256,2048]{1,0:T(8,128)(2,1)}, u32[]{:S(2)}, u32[]{:S(2)}) %collective-permute-start.2) | collective-permute-done | bytes 1048608 | tf_op jit(solution)/shard_map/ppermute | solution.py:345
  58.5 4.1 %collective-permute-start.6 = (s32[2,5,17]{2,0,1:T(2,128)S(1)}, s32[2,5,17]{2,0,1:T(2,128)S(1)}, u32[]{:S(2)}, u32[]{:S(2)}) collective-permute-start(s32[2,5,17]{2,0,1:T(2,128)S(1)} %add_add_fusion), channel_id=1, source_target_pairs={{0,2},{6,4},{1,3},{7,5},{8,10},{14,12},{9,11},{15,13},{16,18},{22,... | collective-permute-start | bytes 2048 | tf_op jit(solution)/shard_map/ppermute | solution.py:345
  62.6 2.3 %collective-permute-start.3 = (bf16[2,96,2048]{2,1,0:T(8,128)(2,1)}, bf16[2,96,2048]{2,1,0:T(8,128)(2,1)}, u32[]{:S(2)}, u32[]{:S(2)}) collective-permute-start(bf16[2,96,2048]{2,1,0:T(8,128)(2,1)} %bitcast.90), channel_id=1, source_target_pairs={{0,2},{6,4},{1,3},{7,5},{8,10},{14,12},{9,11},{15,13},{16,18},{22,... | collective-permute-start | bytes 2359304 | tf_op jit(solution)/shard_map/ppermute | solution.py:345
  64.9 1.7 collective-permute-start.8
  66.5 2.5 %slice_select_fusion = (bf16[1,96,2048]{2,1,0:T(8,128)(2,1)S(1)}, bf16[1,96,2048]{2,1,0:T(8,128)(2,1)}, bf16[96,2048]{1,0:T(8,128)(2,1)}) fusion(bf16[2,96,2048]{2,1,0:T(8,128)(2,1)} %param.14, bf16[2,96,2048]{2,1,0:T(8,128)(2,1)} %param.12, pred[]{:T(512)S(6)} %eq.44, bf16[1,96,2048]{2,1,0:T(8,128)(2,1)S(1)} %copy-done.58, bf16[1,96,2048]{2,1,0:T(8,128)(2,1)} %param.15, ...), kind=kLoop, calls=%fused_computation.16 | loop fusion | flops 589824 | bytes 3538946 | tf_op jit(solution)/shard_map/jit(_where)/select_n | solution.py:401
  69.0 2.2 collective-permute-start.4
  74.5 1.7 copy.49
  79.6 11.6 %collective-permute-done.4.x_theirs = bf16[96,2048]{1,0:T(8,128)(2,1)} collective-permute-done((bf16[96,2048]{1,0:T(8,128)(2,1)}, bf16[96,2048]{1,0:T(8,128)(2,1)}, u32[]{:S(2)}, u32[]{:S(2)}) %collective-permute-start.4) | collective-permute-done | bytes 393248 | tf_op jit(solution)/shard_map/ppermute | solution.py:345
  92.1 5.5 %collective-permute-start.9 = (bf16[96,2048]{1,0:T(8,128)(2,1)S(1)}, bf16[96,2048]{1,0:T(8,128)(2,1)S(1)}, u32[]{:S(2)}, u32[]{:S(2)}) collective-permute-start(bf16[96,2048]{1,0:T(8,128)(2,1)S(1)} %bitcast.85), channel_id=1, source_target_pairs={{0,2},{6,4},{1,3},{7,5},{8,10},{14,12},{9,11},{15,13},{16,18},{22,... | collective-permute-start | bytes 1179656 | tf_op jit(solution)/shard_map/ppermute | solution.py:345
  99.0 1.6 copy-done.2
  101.7 12.2 %project.1 = (bf16[3,192,512]{2,1,0:T(8,128)(2,1)S(1)}, f32[2,192,512]{2,1,0:T(8,128)S(1)}, bf16[2,192,1536]{2,1,0:T(8,128)(2,1)S(1)}, f32[2,192,2048]{2,1,0:T(8...) custom-call(s32[6]{0:T(128)S(1)} %stack.85.offs.in_offs, ...), custom_call_target="tpu_custom_call" | custom-call | flops 4831838208 | bytes 20971520 | tf_op jit(solution)/shard_map/project/pallas_call | solution.py:472
  114.0 1.6 copy-done.6
  118.5 1.8 pack.1
  123.7 2.8 %out.1 = (bf16[2,48,2048]{2,1,0:T(8,128)(2,1)}, bf16[2,48,2048]{2,1,0:T(8,128)(2,1)S(1)}) custom-call(s32[1]{0:T(128)} %bitcast.9.core, s32[4]{0:T(128)S(1)} %add_multiply_fusion.offs, bf16[3,192,512]{2,1,0:T(8,128)(2,1)S(1)} %get-tuple-element.138.gated, bf16[512,512]{1,0:T(8,128)(2,1)} %bitcast.20.rest_0_.rest_9_.rest_6_, ...), custom_call_target="tpu_custom_call" | custom-call | flops 402653184 | bytes 2621440 | tf_op jit(solution)/shard_map/out/pallas_call | solution.py:545
  128.0 2.5 %collective-permute-start.13 = (bf16[2,48,2048]{2,1,0:T(8,128)(2,1)}, bf16[2,48,2048]{2,1,0:T(8,128)(2,1)}, u32[]{:S(2)}, u32[]{:S(2)}) collective-permute-start(bf16[2,48,2048]{2,1,0:T(8,128)(2,1)} %get-tuple-element.103), channel_id=1, source_target_pairs={{0,1},{1,0},{2,3},{3,2},{4,5},{5,4},{6,7},{7,6},{8,9},{9,8},{10,11... | collective-permute-start | bytes 1179656 | tf_op jit(solution)/shard_map/ppermute | solution.py:359
  134.1 3.1 %collective-permute-start.14 = (bf16[2,48,2048]{2,1,0:T(8,128)(2,1)S(1)}, bf16[2,48,2048]{2,1,0:T(8,128)(2,1)}, u32[]{:S(2)}, u32[]{:S(2)}) collective-permute-start(bf16[2,48,2048]{2,1,0:T(8,128)(2,1)S(1)} %add_convert_fusion.2.earlier), channel_id=1, source_target_pairs={{0,8},{8,16},{16,24},{1,9},{9,17},{17,25},{2,10},{10,18},{18,26},{... | collective-permute-start | bytes 1179656 | tf_op jit(solution)/shard_map/ppermute | solution.py:363
  138.8 1.9 copy-done.7
  147.9 9.5 %backward.2 = (bf16[2,48,2048]{2,1,0:T(8,128)(2,1)S(1)}, bf16[2,48,2048]{2,1,0:T(8,128)(2,1)S(1)}) custom-call(s32[1]{0:T(128)} %bitcast.9.core, s32[6]{0:T(128)S(1)} %stack.85.offs.in_offs, s32[4]{0:T(128)S(1)} %add_multiply_fusion.offs, bf16[192,2048]{1,0:T(8,128)(2,1)S(1)} %copy-done.43, f32[2,192,512]{2,1,0:T(8,128)S(1)} %copy-done.34, ...), custom_call_target="tpu_custom_call" | custom-call | flops 3221225472 | bytes 20971520 | tf_op jit(solution)/shard_map/backward/pallas_call | solution.py:505
  162.0 3.1 %collective-permute-start.19 = (bf16[2,48,2048]{2,1,0:T(8,128)(2,1)}, bf16[2,48,2048]{2,1,0:T(8,128)(2,1)}, u32[]{:S(2)}, u32[]{:S(2)}) collective-permute-start(bf16[2,48,2048]{2,1,0:T(8,128)(2,1)} %get-tuple-element.122), channel_id=1, source_target_pairs={{8,0},{16,8},{24,16},{9,1},{17,9},{25,17},{10,2},{18,10},{26,18},{... | collective-permute-start | bytes 1179656 | tf_op jit(solution)/shard_map/ppermute | solution.py:363
  171.6 7.9 %forward.1 = (bf16[2,48,2048]{2,1,0:T(8,128)(2,1)S(1)}, bf16[2,48,2048]{2,1,0:T(8,128)(2,1)S(1)}) custom-call(s32[1]{0:T(128)} %bitcast.9.core, s32[6]{0:T(128)S(1)} %stack.85.offs.in_offs, s32[4]{0:T(128)S(1)} %add_multiply_fusion.offs, s32[1]{0:T(128)} %bitcast.33.fresh, bf16[2,48,2048]{2,1,0:T(8,128)(2,1)} %collective-permute-done.14.mine, ...), custom_call_target="tpu_custom_call" | custom-call | flops 3221225472 | bytes 20971520 | tf_op jit(solution)/shard_map/forward/pallas_call | solution.py:579
  179.5 7.4 %collective-permute-done.21 = bf16[2,48,2048]{2,1,0:T(8,128)(2,1)} collective-permute-done((bf16[2,48,2048]{2,1,0:T(8,128)(2,1)}, bf16[2,48,2048]{2,1,0:T(8,128)(2,1)}, u32[]{:S(2)}, u32[]{:S(2)}) %collective-permute-start.21) | collective-permute-done | bytes 393248 | tf_op jit(solution)/shard_map/ppermute | solution.py:348
  195.9 9.5 %backward.3 = (bf16[2,48,2048]{2,1,0:T(8,128)(2,1)S(1)}, bf16[2,48,2048]{2,1,0:T(8,128)(2,1)S(1)}) custom-call(s32[1]{0:T(128)} %bitcast.9.core, s32[6]{0:T(128)S(1)} %stack.85.offs.in_offs, s32[4]{0:T(128)S(1)} %add_multiply_fusion.offs, bf16[192,2048]{1,0:T(8,128)(2,1)S(1)} %get-tuple-element.129.rest_0_.up_1, f32[2,192,512]{2,1,0:T(8,128)S(1)} %copy-done.35, ...), custom_call_target="tpu_custom_call" | custom-call | flops 3221225472 | bytes 20971520 | tf_op jit(solution)/shard_map/backward/pallas_call | solution.py:505
  205.5 2.0 collective-permute-done.26.rest_5_
  207.5 1.6 collective-permute-start.28
  213.8 2.8 %grads.1 = f32[512,512]{1,0:T(8,128)} custom-call(s32[1]{0:T(128)} %bitcast.44.host, s32[4]{0:T(128)S(1)} %add_multiply_fusion.offs, bf16[3,192,512]{2,1,0:T(8,128)(2,1)S(1)} %copy-done.24, bf16[192,2048]{1,0:T(8,128)(2,1)S(1)} %copy-done.44, bf16[192,2048]{1,0:T(8,128)(2,1)S(1)} %get-tuple-element.129.rest_0_.up_1, bf16[192,1536]{1,0:T(8,128)(2,1)S(1)} %copy-done.52, ...), custom_call_target="tpu_custom_call" | custom-call | flops 402653184 | bytes 2621440 | tf_op jit(solution)/shard_map/grads/pallas_call | solution.py:641
  216.6 3.2 %collective-permute-done.29 = bf16[48,2048]{1,0:T(8,128)(2,1)S(1)} collective-permute-done((bf16[48,2048]{1,0:T(8,128)(2,1)S(1)}, bf16[48,2048]{1,0:T(8,128)(2,1)S(1)}, u32[]{:S(2)}, u32[]{:S(2)}) %collective-permute-start.29) | collective-permute-done | bytes 196640 | tf_op jit(solution)/shard_map/ppermute | solution.py:348
  (198 shorter events, 61.8 us)
Async XLA Ops:
  0.6 56.1 %copy-start.59 = (s32[1,5,4,4]{1,3,2,0:T(4,128)S(1)}, s32[1,5,4,4]{1,3,2,0:T(4,128)}, u32[]{:S(2)}) copy-start(s32[1,5,4,4]{1,3,2,0:T(4,128)} %param.21) | copy-start | bytes 964
  0.7 65.9 %copy-start.58 = (bf16[1,96,2048]{2,1,0:T(8,128)(2,1)S(1)}, bf16[1,96,2048]{2,1,0:T(8,128)(2,1)}, u32[]{:S(2)}) copy-start(bf16[1,96,2048]{2,1,0:T(8,128)(2,1)} %param.13) | copy-start | bytes 1179652
  0.7 53.9 %collective-permute-start = (bf16[512,2048]{1,0:T(8,128)(2,1)}, bf16[512,2048]{1,0:T(8,128)(2,1)S(1)}, u32[]{:S(2)}, u32[]{:S(2)}) collective-permute-start(bf16[512,2048]{1,0:T(8,128)(2,1)} %bitcast.80), channel_id=1, source_target_pairs={{4,2},{2,4},{5,3},{3,5},{12,10},{10,12},{13,11},{11,13},{20,18},{1... | collective-permute-start | bytes 6291464 | tf_op jit(solution)/shard_map/ppermute | solution.py:351
  4.7 27.4 %collective-permute-start.1 = (bf16[256,2048]{1,0:T(8,128)(2,1)}, bf16[256,2048]{1,0:T(8,128)(2,1)S(1)}, u32[]{:S(2)}, u32[]{:S(2)}) collective-permute-start(bf16[256,2048]{1,0:T(8,128)(2,1)} %get-tuple-element.146), channel_id=1, source_target_pairs={{0,2},{6,4},{1,3},{7,5},{8,10},{14,12},{9,11},{15,13},{16,18},{22,... | collective-permute-start | bytes 3145736 | tf_op jit(solution)/shard_map/ppermute | solution.py:345
  10.4 44.2 %collective-permute-start.2 = (bf16[256,2048]{1,0:T(8,128)(2,1)}, bf16[256,2048]{1,0:T(8,128)(2,1)}, u32[]{:S(2)}, u32[]{:S(2)}) collective-permute-start(bf16[256,2048]{1,0:T(8,128)(2,1)} %get-tuple-element.145), channel_id=1, source_target_pairs={{0,2},{6,4},{1,3},{7,5},{8,10},{14,12},{9,11},{15,13},{16,18},{22,... | collective-permute-start | bytes 3145736 | tf_op jit(solution)/shard_map/ppermute | solution.py:345
  12.7 56.4 %collective-permute-start.5 = (bf16[512,512]{1,0:T(8,128)(2,1)}, bf16[512,512]{1,0:T(8,128)(2,1)}, u32[]{:S(2)}, u32[]{:S(2)}) collective-permute-start(bf16[512,512]{1,0:T(8,128)(2,1)} %bitcast.20.rest_0_.rest_9_.rest_6_), channel_id=1, source_target_pairs={{0,2},{6,4},{1,3},{7,5},{8,10},{14,12},{9,11},{15,13},{16,18},{22,... | collective-permute-start | bytes 1572872 | tf_op jit(solution)/shard_map/ppermute | solution.py:345
  32.1 65.5 %collective-permute-start.7 = (bf16[256,2048]{1,0:T(8,128)(2,1)S(1)}, bf16[256,2048]{1,0:T(8,128)(2,1)}, u32[]{:S(2)}, u32[]{:S(2)}) collective-permute-start(bf16[256,2048]{1,0:T(8,128)(2,1)S(1)} %collective-permute-done.1.rest_2_.rest_15_), channel_id=1, source_target_pairs={{4,2},{2,4},{5,3},{3,5},{12,10},{10,12},{13,11},{11,13},{20,18},{1... | collective-permute-start | bytes 3145736 | tf_op jit(solution)/shard_map/ppermute | solution.py:351
  58.5 12.7 %collective-permute-start.6 = (s32[2,5,17]{2,0,1:T(2,128)S(1)}, s32[2,5,17]{2,0,1:T(2,128)S(1)}, u32[]{:S(2)}, u32[]{:S(2)}) collective-permute-start(s32[2,5,17]{2,0,1:T(2,128)S(1)} %add_add_fusion), channel_id=1, source_target_pairs={{0,2},{6,4},{1,3},{7,5},{8,10},{14,12},{9,11},{15,13},{16,18},{22,... | collective-permute-start | bytes 2048 | tf_op jit(solution)/shard_map/ppermute | solution.py:345
  62.6 29.5 %collective-permute-start.3 = (bf16[2,96,2048]{2,1,0:T(8,128)(2,1)}, bf16[2,96,2048]{2,1,0:T(8,128)(2,1)}, u32[]{:S(2)}, u32[]{:S(2)}) collective-permute-start(bf16[2,96,2048]{2,1,0:T(8,128)(2,1)} %bitcast.90), channel_id=1, source_target_pairs={{0,2},{6,4},{1,3},{7,5},{8,10},{14,12},{9,11},{15,13},{16,18},{22,... | collective-permute-start | bytes 2359304 | tf_op jit(solution)/shard_map/ppermute | solution.py:345
  64.9 34.1 %collective-permute-start.8 = (bf16[256,2048]{1,0:T(8,128)(2,1)}, bf16[256,2048]{1,0:T(8,128)(2,1)}, u32[]{:S(2)}, u32[]{:S(2)}) collective-permute-start(bf16[256,2048]{1,0:T(8,128)(2,1)} %collective-permute-done.2.rest_3_.rest_16_), channel_id=1, source_target_pairs={{4,2},{2,4},{5,3},{3,5},{12,10},{10,12},{13,11},{11,13},{20,18},{1... | collective-permute-start | bytes 3145736 | tf_op jit(solution)/shard_map/ppermute | solution.py:351
  69.0 22.2 %collective-permute-start.4 = (bf16[96,2048]{1,0:T(8,128)(2,1)}, bf16[96,2048]{1,0:T(8,128)(2,1)}, u32[]{:S(2)}, u32[]{:S(2)}) collective-permute-start(bf16[96,2048]{1,0:T(8,128)(2,1)} %bitcast.7.x_own), channel_id=1, source_target_pairs={{0,2},{6,4},{1,3},{7,5},{8,10},{14,12},{9,11},{15,13},{16,18},{22,... | collective-permute-start | bytes 1179656 | tf_op jit(solution)/shard_map/ppermute | solution.py:345
  76.2 47.5 %collective-permute-start.11 = (bf16[512,512]{1,0:T(8,128)(2,1)}, bf16[512,512]{1,0:T(8,128)(2,1)S(1)}, u32[]{:S(2)}, u32[]{:S(2)}) collective-permute-start(bf16[512,512]{1,0:T(8,128)(2,1)} %bitcast.20.rest_0_.rest_9_.rest_6_), channel_id=1, source_target_pairs={{4,2},{2,4},{5,3},{3,5},{12,10},{10,12},{13,11},{11,13},{20,18},{1... | collective-permute-start | bytes 1572872 | tf_op jit(solution)/shard_map/ppermute | solution.py:351
  91.2 32.5 %collective-permute-start.12 = (bf16[512,512]{1,0:T(8,128)(2,1)}, bf16[512,512]{1,0:T(8,128)(2,1)S(1)}, u32[]{:S(2)}, u32[]{:S(2)}) collective-permute-start(bf16[512,512]{1,0:T(8,128)(2,1)} %collective-permute-done.5.rest_1_.rest_10_.rest_7_), channel_id=1, source_target_pairs={{4,2},{2,4},{5,3},{3,5},{12,10},{10,12},{13,11},{11,13},{20,18},{1... | collective-permute-start | bytes 1572872 | tf_op jit(solution)/shard_map/ppermute | solution.py:351
  92.1 26.4 %collective-permute-start.9 = (bf16[96,2048]{1,0:T(8,128)(2,1)S(1)}, bf16[96,2048]{1,0:T(8,128)(2,1)S(1)}, u32[]{:S(2)}, u32[]{:S(2)}) collective-permute-start(bf16[96,2048]{1,0:T(8,128)(2,1)S(1)} %bitcast.85), channel_id=1, source_target_pairs={{0,2},{6,4},{1,3},{7,5},{8,10},{14,12},{9,11},{15,13},{16,18},{22,... | collective-permute-start | bytes 1179656 | tf_op jit(solution)/shard_map/ppermute | solution.py:345
  97.6 20.9 %collective-permute-start.10 = (bf16[96,2048]{1,0:T(8,128)(2,1)S(1)}, bf16[96,2048]{1,0:T(8,128)(2,1)S(1)}, u32[]{:S(2)}, u32[]{:S(2)}) collective-permute-start(bf16[96,2048]{1,0:T(8,128)(2,1)S(1)} %copy-done.28), channel_id=1, source_target_pairs={{0,2},{6,4},{1,3},{7,5},{8,10},{14,12},{9,11},{15,13},{16,18},{22,... | collective-permute-start | bytes 1179656 | tf_op jit(solution)/shard_map/ppermute | solution.py:345
  128.0 4.6 %collective-permute-start.13 = (bf16[2,48,2048]{2,1,0:T(8,128)(2,1)}, bf16[2,48,2048]{2,1,0:T(8,128)(2,1)}, u32[]{:S(2)}, u32[]{:S(2)}) collective-permute-start(bf16[2,48,2048]{2,1,0:T(8,128)(2,1)} %get-tuple-element.103), channel_id=1, source_target_pairs={{0,1},{1,0},{2,3},{3,2},{4,5},{5,4},{6,7},{7,6},{8,9},{9,8},{10,11... | collective-permute-start | bytes 1179656 | tf_op jit(solution)/shard_map/ppermute | solution.py:359
  130.5 26.9 %collective-permute-start.15 = (bf16[192,1536]{1,0:T(8,128)(2,1)}, bf16[192,1536]{1,0:T(8,128)(2,1)S(1)}, u32[]{:S(2)}, u32[]{:S(2)}) collective-permute-start(bf16[192,1536]{1,0:T(8,128)(2,1)} %copy-done.57), channel_id=1, source_target_pairs={{2,0},{4,6},{3,1},{5,7},{10,8},{12,14},{11,9},{13,15},{18,16},{20,... | collective-permute-start | bytes 1769480 | tf_op jit(solution)/shard_map/ppermute | solution.py:348
  132.0 25.5 %collective-permute-start.16 = (bf16[192,1536]{1,0:T(8,128)(2,1)}, bf16[192,1536]{1,0:T(8,128)(2,1)S(1)}, u32[]{:S(2)}, u32[]{:S(2)}) collective-permute-start(bf16[192,1536]{1,0:T(8,128)(2,1)} %copy-done.56), channel_id=1, source_target_pairs={{4,2},{2,4},{5,3},{3,5},{12,10},{10,12},{13,11},{11,13},{20,18},{1... | collective-permute-start | bytes 1769480 | tf_op jit(solution)/shard_map/ppermute | solution.py:351
  134.1 23.4 %collective-permute-start.14 = (bf16[2,48,2048]{2,1,0:T(8,128)(2,1)S(1)}, bf16[2,48,2048]{2,1,0:T(8,128)(2,1)}, u32[]{:S(2)}, u32[]{:S(2)}) collective-permute-start(bf16[2,48,2048]{2,1,0:T(8,128)(2,1)S(1)} %add_convert_fusion.2.earlier), channel_id=1, source_target_pairs={{0,8},{8,16},{16,24},{1,9},{9,17},{17,25},{2,10},{10,18},{18,26},{... | collective-permute-start | bytes 1179656 | tf_op jit(solution)/shard_map/ppermute | solution.py:363
  157.4 2.0 collective-permute-start.18
  157.8 7.8 %collective-permute-start.17 = (bf16[2,48,2048]{2,1,0:T(8,128)(2,1)}, bf16[2,48,2048]{2,1,0:T(8,128)(2,1)}, u32[]{:S(2)}, u32[]{:S(2)}) collective-permute-start(bf16[2,48,2048]{2,1,0:T(8,128)(2,1)} %collective-permute-done.14.mine), channel_id=1, source_target_pairs={{0,1},{1,0},{2,3},{3,2},{4,5},{5,4},{6,7},{7,6},{8,9},{9,8},{10,11... | collective-permute-start | bytes 1179656 | tf_op jit(solution)/shard_map/ppermute | solution.py:359
  158.0 21.4 %collective-permute-start.20 = (bf16[192,1536]{1,0:T(8,128)(2,1)}, bf16[192,1536]{1,0:T(8,128)(2,1)}, u32[]{:S(2)}, u32[]{:S(2)}) collective-permute-start(bf16[192,1536]{1,0:T(8,128)(2,1)} %get-tuple-element.123), channel_id=1, source_target_pairs={{4,0},{2,6},{5,1},{3,7},{12,8},{10,14},{13,9},{11,15},{20,16},{18,... | collective-permute-start | bytes 1769480 | tf_op jit(solution)/shard_map/ppermute | solution.py:354
  160.7 26.1 %collective-permute-start.21 = (bf16[2,48,2048]{2,1,0:T(8,128)(2,1)}, bf16[2,48,2048]{2,1,0:T(8,128)(2,1)}, u32[]{:S(2)}, u32[]{:S(2)}) collective-permute-start(bf16[2,48,2048]{2,1,0:T(8,128)(2,1)} %get-tuple-element.124), channel_id=1, source_target_pairs={{2,0},{4,6},{3,1},{5,7},{10,8},{12,14},{11,9},{13,15},{18,16},{20,... | collective-permute-start | bytes 1179656 | tf_op jit(solution)/shard_map/ppermute | solution.py:348
  162.0 24.9 %collective-permute-start.19 = (bf16[2,48,2048]{2,1,0:T(8,128)(2,1)}, bf16[2,48,2048]{2,1,0:T(8,128)(2,1)}, u32[]{:S(2)}, u32[]{:S(2)}) collective-permute-start(bf16[2,48,2048]{2,1,0:T(8,128)(2,1)} %get-tuple-element.122), channel_id=1, source_target_pairs={{8,0},{16,8},{24,16},{9,1},{17,9},{25,17},{10,2},{18,10},{26,18},{... | collective-permute-start | bytes 1179656 | tf_op jit(solution)/shard_map/ppermute | solution.py:363
  186.8 1.8 collective-permute-start.22
  187.3 4.1 %collective-permute-start.23 = (bf16[2,48,2048]{2,1,0:T(8,128)(2,1)}, bf16[2,48,2048]{2,1,0:T(8,128)(2,1)S(1)}, u32[]{:S(2)}, u32[]{:S(2)}) collective-permute-start(bf16[2,48,2048]{2,1,0:T(8,128)(2,1)} %collective-permute-done.19.mine), channel_id=1, source_target_pairs={{0,1},{1,0},{2,3},{3,2},{4,5},{5,4},{6,7},{7,6},{8,9},{9,8},{10,11... | collective-permute-start | bytes 1179656 | tf_op jit(solution)/shard_map/ppermute | solution.py:359
  190.1 15.4 %collective-permute-start.27 = (bf16[48,2048]{1,0:T(8,128)(2,1)S(1)}, bf16[48,2048]{1,0:T(8,128)(2,1)S(1)}, u32[]{:S(2)}, u32[]{:S(2)}) collective-permute-start(bf16[48,2048]{1,0:T(8,128)(2,1)S(1)} %slice_bitcast_fusion.4), channel_id=1, source_target_pairs={{2,0},{4,6},{3,1},{5,7},{10,8},{12,14},{11,9},{13,15},{18,16},{20,... | collective-permute-start | bytes 589832 | tf_op jit(solution)/shard_map/ppermute | solution.py:348
  192.6 12.9 %collective-permute-start.24 = (bf16[192,512]{1,0:T(8,128)(2,1)S(1)}, bf16[192,512]{1,0:T(8,128)(2,1)S(1)}, u32[]{:S(2)}, u32[]{:S(2)}) collective-permute-start(bf16[192,512]{1,0:T(8,128)(2,1)S(1)} %get-tuple-element.132), channel_id=1, source_target_pairs={{2,0},{4,6},{3,1},{5,7},{10,8},{12,14},{11,9},{13,15},{18,16},{20,... | collective-permute-start | bytes 589832 | tf_op jit(solution)/shard_map/ppermute | solution.py:348
  193.9 11.7 %collective-permute-start.25 = (bf16[192,512]{1,0:T(8,128)(2,1)S(1)}, bf16[192,512]{1,0:T(8,128)(2,1)S(1)}, u32[]{:S(2)}, u32[]{:S(2)}) collective-permute-start(bf16[192,512]{1,0:T(8,128)(2,1)S(1)} %get-tuple-element.133), channel_id=1, source_target_pairs={{4,2},{2,4},{5,3},{3,5},{12,10},{10,12},{13,11},{11,13},{20,18},{1... | collective-permute-start | bytes 589832 | tf_op jit(solution)/shard_map/ppermute | solution.py:351
  194.5 12.9 %collective-permute-start.26 = (bf16[192,512]{1,0:T(8,128)(2,1)S(1)}, bf16[192,512]{1,0:T(8,128)(2,1)S(1)}, u32[]{:S(2)}, u32[]{:S(2)}) collective-permute-start(bf16[192,512]{1,0:T(8,128)(2,1)S(1)} %get-tuple-element.134), channel_id=1, source_target_pairs={{4,0},{2,6},{5,1},{3,7},{12,8},{10,14},{13,9},{11,15},{20,16},{18,... | collective-permute-start | bytes 589832 | tf_op jit(solution)/shard_map/ppermute | solution.py:354
  207.5 3.0 %collective-permute-start.28 = (bf16[2,48,2048]{2,1,0:T(8,128)(2,1)S(1)}, bf16[2,48,2048]{2,1,0:T(8,128)(2,1)S(1)}, u32[]{:S(2)}, u32[]{:S(2)}) collective-permute-start(bf16[2,48,2048]{2,1,0:T(8,128)(2,1)S(1)} %get-tuple-element.137), channel_id=1, source_target_pairs={{0,1},{1,0},{2,3},{3,2},{4,5},{5,4},{6,7},{7,6},{8,9},{9,8},{10,11... | collective-permute-start | bytes 1179656 | tf_op jit(solution)/shard_map/ppermute | solution.py:359
  211.7 8.1 %collective-permute-start.29 = (bf16[48,2048]{1,0:T(8,128)(2,1)S(1)}, bf16[48,2048]{1,0:T(8,128)(2,1)S(1)}, u32[]{:S(2)}, u32[]{:S(2)}) collective-permute-start(bf16[48,2048]{1,0:T(8,128)(2,1)S(1)} %slice_bitcast_fusion.2), channel_id=1, source_target_pairs={{2,0},{4,6},{3,1},{5,7},{10,8},{12,14},{11,9},{13,15},{18,16},{20,... | collective-permute-start | bytes 589832 | tf_op jit(solution)/shard_map/ppermute | solution.py:348
  (59 other events, 510.4 us)

commit v6 on v5

--- a/solution.py
+++ b/solution.py
@@ -12,10 +12,17 @@
 BLOCKS = 4
 EPSILON = 1e-06
 SCALING = HEAD_DIM ** (-0.5)
-VMEM_BYTES = 30 * 1024 * 1024
+VMEM_BYTES = 58 * 1024 * 1024
 
 F32 = jnp.float32
 BF16 = jnp.bfloat16
+
+
+def on_host(kernel):
+    def guarded(host, *refs):
+        pl.when(host[0] != 0)(functools.partial(kernel, *refs))
+
+    return guarded
 
 
 def dot(a, b):
@@ -356,11 +363,17 @@
         )
 
     def swap_cores(x):
-        return lax.ppermute(x, "cores", [(c, cores - 1 - c) for c in range(cores)])
+        pairs = [(h * cores + c, (h + 1) * cores - 1 - c) for h in hosts for c in range(cores)]
+        return lax.ppermute(x, ("dp", "cores"), pairs)
 
     def along_sections(x, by):
-        pairs = [(i, i + by) for i in range(sections) if 0 <= i + by < sections]
-        return lax.ppermute(x, "section", pairs)
+        pairs = [
+            (i * n + h, (i + by) * n + h)
+            for i in range(sections)
+            if 0 <= i + by < sections
+            for h in hosts
+        ]
+        return lax.ppermute(x, ("section", "dp"), pairs)
 
     first_section = section_no == 0
     last_section = section_no == sections - 1
@@ -470,9 +483,9 @@
     by_head = lambda lead, last: pl.BlockSpec(lead + (last,), lambda h: (0,) * len(lead) + (h,))
     square = pl.BlockSpec((2, 1, rows, rows), lambda h: (0, h, 0, 0))
     gated, gate, vqk, slope, mixed, probs, factor = pl.pallas_call(
-        functools.partial(project_kernel, parts),
+        on_host(functools.partial(project_kernel, parts)),
         grid=(heads,),
-        in_specs=[smem]
+        in_specs=[smem] * 2
         + all_of(x_own, x_theirs, stash_own, stash_theirs, keep)
         + [by_head((x.shape[0],), wide) for x in in_parts],
         out_specs=[
@@ -497,15 +510,15 @@
         compiler_params=params,
         cost_estimate=cost(3 * matmul, 2 * weight_bytes),
         name="project",
-    )(in_offs, x_own, x_theirs, stash_own, stash_theirs, keep, *in_parts)
+    )(host_flag, in_offs, x_own, x_theirs, stash_own, stash_theirs, keep, *in_parts)
 
     def backward(ups, tick_no):
         layered = [gate, vqk, slope, mixed, probs, factor, stash_own, stash_theirs]
         plain = list(out_parts) + list(in_parts)
         return pl.pallas_call(
-            functools.partial(backward_kernel, parts, n, tick_no),
+            on_host(functools.partial(backward_kernel, parts, n, tick_no)),
             grid=(1,),
-            in_specs=[smem] * 3 + [hbm] * (1 + len(layered) + len(plain)),
+            in_specs=[smem] * 4 + [hbm] * (1 + len(layered) + len(plain)),
             out_specs=all_of(*halves),
             out_shape=halves,
             scratch_shapes=[pltpu.VMEM(ups.shape, BF16)]
@@ -519,7 +532,7 @@
             compiler_params=params,
             cost_estimate=cost(2 * matmul, 2 * weight_bytes),
             name="backward",
-        )(core, in_offs, offs, ups, *layered, *plain)
+        )(host_flag, core, in_offs, offs, ups, *layered, *plain)
 
     gated, new_theirs = lax.optimization_barrier((gated, new_theirs))
 
@@ -532,27 +545,27 @@
     pack_shapes = [struct((rows, width), BF16)]
     pack_shapes += [struct((rows, 2 * slab + depth), BF16)] * (n - 1)
     up_0, *packs = pl.pallas_call(
-        functools.partial(pack_kernel, n),
+        on_host(functools.partial(pack_kernel, n)),
         grid=(1,),
-        in_specs=[smem] + all_of(gated, up_own, up_theirs),
+        in_specs=[smem] * 2 + all_of(gated, up_own, up_theirs),
         out_specs=all_of(*pack_shapes),
         out_shape=pack_shapes,
         compiler_params=params,
         name="pack",
-    )(offs, gated, up_own, up_theirs)
+    )(host_flag, offs, gated, up_own, up_theirs)
     packs, out_parts = lax.optimization_barrier((packs, out_parts))
 
     ahead_send, ahead_keep = pl.pallas_call(
-        functools.partial(out_kernel, n),
+        on_host(functools.partial(out_kernel, n)),
         grid=(1,),
-        in_specs=[smem] * 2 + [row_of(gated, 0)] + all_of(*out_parts),
+        in_specs=[smem] * 3 + [row_of(gated, 0)] + all_of(*out_parts),
         out_specs=all_of(*halves),
         out_shape=halves,
         scratch_shapes=[pltpu.VMEM((rows, width), BF16)],
         compiler_params=params,
         cost_estimate=cost(matmul // 4, weight_bytes // 4),
         name="out",
-    )(core, offs, gated, *out_parts)
+    )(host_flag, core, offs, gated, *out_parts)
     ahead_0 = summed(own_rows(x_own, x_theirs), ahead_keep, swap_cores(ahead_send))
     ahead_in = along_sections(ahead_0, 1)
     packs_near = [to_partner(packs[0])] + [from_host(packs[m], m) for m in between]
@@ -562,24 +575,24 @@
     )
     back_landed = swap_cores(back_send)
     back_0, first_pair = pl.pallas_call(
-        settle_kernel,
+        on_host(settle_kernel),
         grid=(1,),
-        in_specs=[smem] * 2
+        in_specs=[smem] * 3
         + all_of(up_own, up_theirs, back_keep, back_keep, back_landed, ahead_0),
         out_specs=all_of(*halves),
         out_shape=halves,
         compiler_params=params,
         name="settle",
-    )(core, always, up_own, up_theirs, back_keep, back_keep, back_landed, ahead_0)
+    )(host_flag, core, always, up_own, up_theirs, back_keep, back_keep, back_landed, ahead_0)
     back_in = along_sections(back_0, -1)
     first_pair = to_partner(first_pair)
 
     packs_beyond = [to_beyond(packs[n // 2 + m - 1], m) for m in between]
     ahead_their = swap_cores(ahead_in)
     ahead_send, ahead_keep = pl.pallas_call(
-        functools.partial(forward_kernel, parts, heads),
+        on_host(functools.partial(forward_kernel, parts, heads)),
         grid=(heads,),
-        in_specs=[smem] * 4
+        in_specs=[smem] * 5
         + all_of(ahead_in, ahead_their, new_own, new_theirs)
         + [row_of(keep, keep.shape[0] - 1)]
         + [by_head((x.shape[0],), wide) for x in in_parts]
@@ -595,8 +608,7 @@
         compiler_params=params,
         cost_estimate=cost(2 * matmul, 2 * weight_bytes),
         name="forward",
-    )(
-        core,
+    )(host_flag, core,
         in_offs,
         offs,
         first_flag,
@@ -619,14 +631,14 @@
     back_their = swap_cores(back_in)
     cut_shapes = [struct((rows, width), BF16)] + [struct((rows, depth), BF16)] * (n - 1)
     up_1, *cuts = pl.pallas_call(
-        functools.partial(gather_kernel, n),
+        on_host(functools.partial(gather_kernel, n)),
         grid=(1,),
-        in_specs=[smem] * 3 + all_of(back_in, back_their, new_own, new_theirs),
+        in_specs=[smem] * 4 + all_of(back_in, back_their, new_own, new_theirs),
         out_specs=all_of(*cut_shapes),
         out_shape=cut_shapes,
         compiler_params=params,
         name="gather",
-    )(core, offs, last_flag, back_in, back_their, new_own, new_theirs)
+    )(host_flag, core, offs, last_flag, back_in, back_their, new_own, new_theirs)
     landed = [to_partner(cuts[0])] + [from_host(cuts[m], m) for m in between]
     landed += [to_beyond(cuts[n // 2 + m - 1], m) for m in between]
     back_send, back_keep = backward(up_1, 1)

time: 224 us -> 219 us (0.978)
  waiting for transfers between devices: 60.4 us -> 102 us
  local copies, waits for them, and re-layouts: 40.4 us -> 14.1 us
  Pallas kernels: 48.8 us -> 32.4 us
  starting transfers between devices: 53.2 us -> 49.8 us
    unnamed x122 -> x68, local copies, waits for them, and re-layouts: 30.1 us -> 4 us
    ppermute x5, waiting for transfers between devices: 10.6 us -> 36.5 us  [to_partner(): return lax.ppermute(x, 'dp', [(h, h ^ 1) for h in hosts])]
    pallas_call x8, Pallas kernels: 46 us -> 28.5 us  [the longest x1 8.26 us: per_device(): pl.pallas_call(on_host(functools.partial(project_kernel, parts)), grid=(h...]
    ppermute x2, waiting for transfers between devices: 1.96 us -> 16.1 us  [to_beyond(): lax.ppermute(x, 'dp', [(hosts[k ^ m], hosts[k] ^ 1) for k in range(n // 2)])]
    ppermute x8, starting transfers between devices: 11.4 us -> 5.63 us  [the longest x6 4.08 us: swap_cores(): return lax.ppermute(x, ('dp', 'cores'), pairs)]
    ppermute x8, starting transfers between devices: 25.4 us -> 28 us  [from_partner(): return lax.ppermute(x, 'dp', [(h ^ 1, h) for h in hosts])]
    ppermute x8, waiting for transfers between devices: 46.4 us -> 49.1 us  [from_partner(): return lax.ppermute(x, 'dp', [(h ^ 1, h) for h in hosts])]
  transfers between devices with their start and end apart: 30 -> 30, of which waited for: 7 -> 11; matrix products, arithmetic and copies ran while one was open for 10% -> 10% of each run, Pallas kernels for 21% -> 14%
where the time goes in v6:
time: 219 us; the launch traced here: 216 us
  waiting for transfers between devices  102 us (47%)
  starting transfers between devices  49.8 us (23%)
  Pallas kernels  32.4 us (15%)
  other arithmetic  14.6 us (7%)
  local copies, waits for them, and re-layouts  14.1 us (6%)
  between operations  3.35 us (2%)
    ppermute x8, waiting for transfers between devices, from_partner(): return lax.ppermute(x, 'dp', [(h ^ 1, h) for h in hosts])  49.1 us
    ppermute x5, waiting for transfers between devices, to_partner(): return lax.ppermute(x, 'dp', [(h, h ^ 1) for h in hosts])  36.5 us
    ppermute x8, starting transfers between devices, from_partner(): return lax.ppermute(x, 'dp', [(h ^ 1, h) for h in hosts])  28 us
    ppermute x2, waiting for transfers between devices, to_beyond(): lax.ppermute(x, 'dp', [(hosts[k ^ m], hosts[k] ^ 1) for k in range(n // 2)])  16.1 us
    pallas_call x1, Pallas kernels, per_device(): pl.pallas_call(on_host(functools.partial(project_kernel, parts)), grid=(h...  8.26 us
    ppermute x7, starting transfers between devices, from_host(): lax.ppermute(x, 'dp', [(hosts[k ^ m], hosts[k]) for k in range(n // 2)])  7.15 us
    ppermute x5, starting transfers between devices, to_partner(): return lax.ppermute(x, 'dp', [(h, h ^ 1) for h in hosts])  6.44 us
    pallas_call x1, Pallas kernels, per_device(): pl.pallas_call(on_host(functools.partial(forward_kernel, parts, heads)),...  6.27 us
  transfers between devices with their start and end apart: 30, of which 11 were waited for; matrix products, arithmetic and copies ran while one was open for 10% of the time, Pallas kernels for 14%

profile of v6, /device:TPU:5, one launch (start us, length us, event | category | flops | bytes accessed | tf_op | source)
XLA Modules:
  0.0 216.0 jit_solution(9779014753833409306)
XLA Ops:
  1.6 3.1 %slice_bitcast_fusion = (bf16[256,2048]{1,0:T(8,128)(2,1)}, bf16[256,2048]{1,0:T(8,128)(2,1)}) fusion(bf16[1,512,2048]{2,1,0:T(8,128)(2,1)} %param.17), kind=kLoop, calls=%fused_computation | loop fusion | bytes 4194304 | tf_op jit(solution)/shard_map/slice | solution.py:386
  4.7 5.7 %collective-permute-start.1 = (bf16[256,2048]{1,0:T(8,128)(2,1)}, bf16[256,2048]{1,0:T(8,128)(2,1)S(1)}, u32[]{:S(2)}, u32[]{:S(2)}) collective-permute-start(bf16[256,2048]{1,0:T(8,128)(2,1)} %get-tuple-element.146), channel_id=1, source_target_pairs={{0,2},{6,4},{1,3},{7,5},{8,10},{14,12},{9,11},{15,13},{16,18},{22,... | collective-permute-start | bytes 3145736 | tf_op jit(solution)/shard_map/ppermute | solution.py:352
  10.4 2.3 %collective-permute-start.2 = (bf16[256,2048]{1,0:T(8,128)(2,1)}, bf16[256,2048]{1,0:T(8,128)(2,1)}, u32[]{:S(2)}, u32[]{:S(2)}) collective-permute-start(bf16[256,2048]{1,0:T(8,128)(2,1)} %get-tuple-element.145), channel_id=1, source_target_pairs={{0,2},{6,4},{1,3},{7,5},{8,10},{14,12},{9,11},{15,13},{16,18},{22,... | collective-permute-start | bytes 3145736 | tf_op jit(solution)/shard_map/ppermute | solution.py:352
  12.7 2.1 collective-permute-start.5
  20.0 12.2 %collective-permute-done.1.refs_8_.refs_18_.refs_11_ = bf16[256,2048]{1,0:T(8,128)(2,1)S(1)} collective-permute-done((bf16[256,2048]{1,0:T(8,128)(2,1)}, bf16[256,2048]{1,0:T(8,128)(2,1)S(1)}, u32[]{:S(2)}, u32[]{:S(2)}) %collective-permute-start.1) | collective-permute-done | bytes 1048608 | tf_op jit(solution)/shard_map/ppermute | solution.py:352
  32.2 1.6 collective-permute-start.7
  33.8 20.8 %collective-permute-done.2.refs_9_.refs_19_.refs_12_ = bf16[256,2048]{1,0:T(8,128)(2,1)} collective-permute-done((bf16[256,2048]{1,0:T(8,128)(2,1)}, bf16[256,2048]{1,0:T(8,128)(2,1)}, u32[]{:S(2)}, u32[]{:S(2)}) %collective-permute-start.2) | collective-permute-done | bytes 1048608 | tf_op jit(solution)/shard_map/ppermute | solution.py:352
  55.2 4.1 %collective-permute-start.6 = (s32[2,5,17]{2,0,1:T(2,128)S(1)}, s32[2,5,17]{2,0,1:T(2,128)S(1)}, u32[]{:S(2)}, u32[]{:S(2)}) collective-permute-start(s32[2,5,17]{2,0,1:T(2,128)S(1)} %add_add_fusion), channel_id=1, source_target_pairs={{0,2},{6,4},{1,3},{7,5},{8,10},{14,12},{9,11},{15,13},{16,18},{22,... | collective-permute-start | bytes 2048 | tf_op jit(solution)/shard_map/ppermute | solution.py:352
  59.3 2.2 %collective-permute-start.3 = (bf16[2,96,2048]{2,1,0:T(8,128)(2,1)}, bf16[2,96,2048]{2,1,0:T(8,128)(2,1)}, u32[]{:S(2)}, u32[]{:S(2)}) collective-permute-start(bf16[2,96,2048]{2,1,0:T(8,128)(2,1)} %bitcast.90), channel_id=1, source_target_pairs={{0,2},{6,4},{1,3},{7,5},{8,10},{14,12},{9,11},{15,13},{16,18},{22,... | collective-permute-start | bytes 2359304 | tf_op jit(solution)/shard_map/ppermute | solution.py:352
  61.5 1.7 collective-permute-start.8
  63.2 2.6 %slice_select_fusion = (bf16[1,96,2048]{2,1,0:T(8,128)(2,1)S(1)}, bf16[1,96,2048]{2,1,0:T(8,128)(2,1)}, bf16[96,2048]{1,0:T(8,128)(2,1)}) fusion(bf16[2,96,2048]{2,1,0:T(8,128)(2,1)} %param.14, bf16[2,96,2048]{2,1,0:T(8,128)(2,1)} %param.12, pred[]{:T(512)S(6)} %eq.44, bf16[1,96,2048]{2,1,0:T(8,128)(2,1)} %param.13, bf16[1,96,2048]{2,1,0:T(8,128)(2,1)} %param.15, ...), kind=kLoop, calls=%fused_computation.16 | loop fusion | flops 589824 | bytes 3538946 | tf_op jit(solution)/shard_map/jit(_where)/select_n | solution.py:414
  65.9 4.8 %collective-permute-start.4 = (bf16[96,2048]{1,0:T(8,128)(2,1)}, bf16[96,2048]{1,0:T(8,128)(2,1)}, u32[]{:S(2)}, u32[]{:S(2)}) collective-permute-start(bf16[96,2048]{1,0:T(8,128)(2,1)} %bitcast.7.refs_1_), channel_id=1, source_target_pairs={{0,2},{6,4},{1,3},{7,5},{8,10},{14,12},{9,11},{15,13},{16,18},{22,... | collective-permute-start | bytes 1179656 | tf_op jit(solution)/shard_map/ppermute | solution.py:352
  75.2 1.7 copy.49
  80.2 11.0 %collective-permute-done.4.refs_2_ = bf16[96,2048]{1,0:T(8,128)(2,1)} collective-permute-done((bf16[96,2048]{1,0:T(8,128)(2,1)}, bf16[96,2048]{1,0:T(8,128)(2,1)}, u32[]{:S(2)}, u32[]{:S(2)}) %collective-permute-start.4) | collective-permute-done | bytes 393248 | tf_op jit(solution)/shard_map/ppermute | solution.py:352
  93.0 5.5 %collective-permute-start.9 = (bf16[96,2048]{1,0:T(8,128)(2,1)S(1)}, bf16[96,2048]{1,0:T(8,128)(2,1)S(1)}, u32[]{:S(2)}, u32[]{:S(2)}) collective-permute-start(bf16[96,2048]{1,0:T(8,128)(2,1)S(1)} %bitcast.85), channel_id=1, source_target_pairs={{0,2},{6,4},{1,3},{7,5},{8,10},{14,12},{9,11},{15,13},{16,18},{22,... | collective-permute-start | bytes 1179656 | tf_op jit(solution)/shard_map/ppermute | solution.py:352
  99.9 8.3 %project.1 = (bf16[3,192,512]{2,1,0:T(8,128)(2,1)}, f32[2,192,512]{2,1,0:T(8,128)}, bf16[2,192,1536]{2,1,0:T(8,128)(2,1)}, f32[2,192,2048]{2,1,0:T(8,128)}, f32[...) custom-call(s32[1]{0:T(128)} %bitcast.9.host, s32[6]{0:T(128)} %stack.85.refs_0_.refs_1_, ...), custom_call_target="tpu_custom_call" | custom-call | flops 4831838208 | bytes 20971520 | tf_op jit(solution)/shard_map/project/pallas_call | solution.py:485
  108.2 5.0 %collective-permute-done.10.refs_3_ = bf16[96,2048]{1,0:T(8,128)(2,1)S(1)} collective-permute-done((bf16[96,2048]{1,0:T(8,128)(2,1)S(1)}, bf16[96,2048]{1,0:T(8,128)(2,1)S(1)}, u32[]{:S(2)}, u32[]{:S(2)}) %collective-permute-start.10) | collective-permute-done | bytes 393248 | tf_op jit(solution)/shard_map/ppermute | solution.py:352
  113.9 2.8 %pack.1 = (bf16[192,2048]{1,0:T(8,128)(2,1)}, bf16[192,1536]{1,0:T(8,128)(2,1)}, bf16[192,1536]{1,0:T(8,128)(2,1)}, bf16[192,1536]{1,0:T(8,128)(2,1)}) custom-call(s32[1]{0:T(128)} %bitcast.9.host, s32[4]{0:T(128)} %add_multiply_fusion.refs_0_.refs_1_.refs_2_.offs, bf16[3,192,512]{2,1,0:T(8,128)(2,1)} %get-tuple-element.138.refs_1_.refs_2_.gated, ...), custom_call_target="tpu_custom_call" | custom-call | tf_op jit(solution)/shard_map/pack/pallas_call | solution.py:547
  117.7 2.5 %out.1 = (bf16[2,48,2048]{2,1,0:T(8,128)(2,1)}, bf16[2,48,2048]{2,1,0:T(8,128)(2,1)}) custom-call(s32[1]{0:T(128)} %bitcast.9.host, s32[1]{0:T(128)} %bitcast.10.refs_0_, s32[4]{0:T(128)} %add_multiply_fusion.refs_0_.refs_1_.refs_2_.offs, bf16[3,192,512]{2,1,0:T(8,128)(2,1)} %get-tuple-element.138.refs_1_.refs_2_.gated, ...), custom_call_target="tpu_custom_call" | custom-call | flops 402653184 | bytes 2621440 | tf_op jit(solution)/shard_map/out/pallas_call | solution.py:558
  124.9 1.8 backward.2
  126.7 16.4 %collective-permute-done.15.rest_0_ = bf16[192,1536]{1,0:T(8,128)(2,1)S(1)} collective-permute-done((bf16[192,1536]{1,0:T(8,128)(2,1)S(1)}, bf16[192,1536]{1,0:T(8,128)(2,1)S(1)}, u32[]{:S(2)}, u32[]{:S(2)}) %collective-permute-start.15) | collective-permute-done | bytes 589856 | tf_op jit(solution)/shard_map/ppermute | solution.py:355
  146.6 2.5 %settle.1 = (bf16[2,48,2048]{2,1,0:T(8,128)(2,1)}, bf16[2,48,2048]{2,1,0:T(8,128)(2,1)}) custom-call(s32[1]{0:T(128)} %bitcast.9.host, s32[1]{0:T(128)} %bitcast.10.refs_0_, s32[1]{0:T(128)} %constant.77.clone.1.refs_1_, bf16[96,2048]{1,0:T(8,128)(2,1)} %get-tuple-element.92.refs_2_, bf16[96,2048]{1,0:T(8,128)(2,1)} %copy-done.14, ...), custom_call_target="tpu_custom_call" | custom-call | tf_op jit(solution)/shard_map/settle/pallas_call | solution.py:577
  152.0 6.3 %forward.1 = (bf16[2,48,2048]{2,1,0:T(8,128)(2,1)}, bf16[2,48,2048]{2,1,0:T(8,128)(2,1)}) custom-call(s32[1]{0:T(128)} %bitcast.9.host, s32[1]{0:T(128)} %bitcast.10.refs_0_, s32[6]{0:T(128)} %stack.85.refs_0_.refs_1_, s32[4]{0:T(128)} %add_multiply_fusion.refs_0_.refs_1_.refs_2_.offs, s32[1]{0:T(128)} %bitcast.34.refs_3_, bf16[2,48,2048]{2,1,0:T(8,128)(2,1)} %copy-done.13, ...), custom_call_target="tpu_custom_call" | custom-call | flops 3221225472 | bytes 20971520 | tf_op jit(solution)/shard_map/forward/pallas_call | solution.py:592
  158.3 9.1 %collective-permute-done.20.rest_2_ = bf16[192,1536]{1,0:T(8,128)(2,1)S(1)} collective-permute-done((bf16[192,1536]{1,0:T(8,128)(2,1)}, bf16[192,1536]{1,0:T(8,128)(2,1)S(1)}, u32[]{:S(2)}, u32[]{:S(2)}) %collective-permute-start.20) | collective-permute-done | bytes 589856 | tf_op jit(solution)/shard_map/ppermute | solution.py:361
  167.5 8.9 %collective-permute-done.21 = bf16[2,48,2048]{2,1,0:T(8,128)(2,1)S(1)} collective-permute-done((bf16[2,48,2048]{2,1,0:T(8,128)(2,1)}, bf16[2,48,2048]{2,1,0:T(8,128)(2,1)S(1)}, u32[]{:S(2)}, u32[]{:S(2)}) %collective-permute-start.21) | collective-permute-done | bytes 393248 | tf_op jit(solution)/shard_map/ppermute | solution.py:355
  177.9 1.4 add_convert_fusion.1
  181.3 2.5 %gather.1 = (bf16[192,2048]{1,0:T(8,128)(2,1)}, bf16[192,512]{1,0:T(8,128)(2,1)}, bf16[192,512]{1,0:T(8,128)(2,1)}, bf16[192,512]{1,0:T(8,128)(2,1)}) custom-call(s32[1]{0:T(128)} %bitcast.9.host, s32[1]{0:T(128)} %bitcast.10.refs_0_, s32[4]{0:T(128)} %add_multiply_fusion.refs_0_.refs_1_.refs_2_.offs, s32[1]{0:T(128)} %bitcast.37.refs_2_, ...), custom_call_target="tpu_custom_call" | custom-call | tf_op jit(solution)/shard_map/gather/pallas_call | solution.py:633
  187.1 1.9 backward.3
  189.0 3.6 %collective-permute-done.24.rest_3_ = bf16[192,512]{1,0:T(8,128)(2,1)S(1)} collective-permute-done((bf16[192,512]{1,0:T(8,128)(2,1)}, bf16[192,512]{1,0:T(8,128)(2,1)S(1)}, u32[]{:S(2)}, u32[]{:S(2)}) %collective-permute-start.24) | collective-permute-done | bytes 196640 | tf_op jit(solution)/shard_map/ppermute | solution.py:355
  192.6 7.0 %collective-permute-done.26.rest_5_ = bf16[192,512]{1,0:T(8,128)(2,1)S(1)} collective-permute-done((bf16[192,512]{1,0:T(8,128)(2,1)}, bf16[192,512]{1,0:T(8,128)(2,1)S(1)}, u32[]{:S(2)}, u32[]{:S(2)}) %collective-permute-start.26) | collective-permute-done | bytes 196640 | tf_op jit(solution)/shard_map/ppermute | solution.py:361
  203.7 4.0 %grads.1 = f32[512,512]{1,0:T(8,128)} custom-call(s32[1]{0:T(128)} %bitcast.9.host, s32[4]{0:T(128)} %add_multiply_fusion.refs_0_.refs_1_.refs_2_.offs, bf16[3,192,512]{2,1,0:T(8,128)(2,1)} %get-tuple-element.138.refs_1_.refs_2_.gated, bf16[192,2048]{1,0:T(8,128)(2,1)} %get-tuple-element.105.refs_3_.up_0, bf16[192,2048]{1,0:T(8,128)(2,1)} %get-tuple-element.129.refs_3_.up_1, ...), custom_call_target="tpu_custom_call" | custom-call | flops 402653184 | bytes 2621440 | tf_op jit(solution)/shard_map/grads/pallas_call | solution.py:653
  207.7 7.5 %collective-permute-done.29 = bf16[48,2048]{1,0:T(8,128)(2,1)S(1)} collective-permute-done((bf16[48,2048]{1,0:T(8,128)(2,1)S(1)}, bf16[48,2048]{1,0:T(8,128)(2,1)S(1)}, u32[]{:S(2)}, u32[]{:S(2)}) %collective-permute-start.29) | collective-permute-done | bytes 196640 | tf_op jit(solution)/shard_map/ppermute | solution.py:355
  (144 shorter events, 39.8 us)
Async XLA Ops:
  0.7 54.1 %copy-start.31 = (s32[1,5]{1,0:T(1,128)S(1)}, s32[1,5]{1,0:T(1,128)}, u32[]{:S(2)}) copy-start(s32[1,5]{1,0:T(1,128)} %param.20) | copy-start | bytes 64
  0.7 54.2 %copy-start.28 = (s32[1,5,4,4]{1,3,2,0:T(4,128)S(1)}, s32[1,5,4,4]{1,3,2,0:T(4,128)}, u32[]{:S(2)}) copy-start(s32[1,5,4,4]{1,3,2,0:T(4,128)} %param.22) | copy-start | bytes 964
  0.7 53.9 %collective-permute-start = (bf16[512,2048]{1,0:T(8,128)(2,1)}, bf16[512,2048]{1,0:T(8,128)(2,1)S(1)}, u32[]{:S(2)}, u32[]{:S(2)}) collective-permute-start(bf16[512,2048]{1,0:T(8,128)(2,1)} %bitcast.80), channel_id=1, source_target_pairs={{4,2},{2,4},{5,3},{3,5},{12,10},{10,12},{13,11},{11,13},{20,18},{1... | collective-permute-start | bytes 6291464 | tf_op jit(solution)/shard_map/ppermute | solution.py:358
  4.7 27.4 %collective-permute-start.1 = (bf16[256,2048]{1,0:T(8,128)(2,1)}, bf16[256,2048]{1,0:T(8,128)(2,1)S(1)}, u32[]{:S(2)}, u32[]{:S(2)}) collective-permute-start(bf16[256,2048]{1,0:T(8,128)(2,1)} %get-tuple-element.146), channel_id=1, source_target_pairs={{0,2},{6,4},{1,3},{7,5},{8,10},{14,12},{9,11},{15,13},{16,18},{22,... | collective-permute-start | bytes 3145736 | tf_op jit(solution)/shard_map/ppermute | solution.py:352
  10.4 44.2 %collective-permute-start.2 = (bf16[256,2048]{1,0:T(8,128)(2,1)}, bf16[256,2048]{1,0:T(8,128)(2,1)}, u32[]{:S(2)}, u32[]{:S(2)}) collective-permute-start(bf16[256,2048]{1,0:T(8,128)(2,1)} %get-tuple-element.145), channel_id=1, source_target_pairs={{0,2},{6,4},{1,3},{7,5},{8,10},{14,12},{9,11},{15,13},{16,18},{22,... | collective-permute-start | bytes 3145736 | tf_op jit(solution)/shard_map/ppermute | solution.py:352
  12.7 53.1 %collective-permute-start.5 = (bf16[512,512]{1,0:T(8,128)(2,1)}, bf16[512,512]{1,0:T(8,128)(2,1)}, u32[]{:S(2)}, u32[]{:S(2)}) collective-permute-start(bf16[512,512]{1,0:T(8,128)(2,1)} %bitcast.21.refs_3_.refs_12_.refs_15_), channel_id=1, source_target_pairs={{0,2},{6,4},{1,3},{7,5},{8,10},{14,12},{9,11},{15,13},{16,18},{22,... | collective-permute-start | bytes 1572872 | tf_op jit(solution)/shard_map/ppermute | solution.py:352
  32.2 66.4 %collective-permute-start.7 = (bf16[256,2048]{1,0:T(8,128)(2,1)S(1)}, bf16[256,2048]{1,0:T(8,128)(2,1)}, u32[]{:S(2)}, u32[]{:S(2)}) collective-permute-start(bf16[256,2048]{1,0:T(8,128)(2,1)S(1)} %collective-permute-done.1.refs_8_.refs_18_.refs_11_), channel_id=1, source_target_pairs={{4,2},{2,4},{5,3},{3,5},{12,10},{10,12},{13,11},{11,13},{20,18},{1... | collective-permute-start | bytes 3145736 | tf_op jit(solution)/shard_map/ppermute | solution.py:358
  55.2 15.6 %collective-permute-start.6 = (s32[2,5,17]{2,0,1:T(2,128)S(1)}, s32[2,5,17]{2,0,1:T(2,128)S(1)}, u32[]{:S(2)}, u32[]{:S(2)}) collective-permute-start(s32[2,5,17]{2,0,1:T(2,128)S(1)} %add_add_fusion), channel_id=1, source_target_pairs={{0,2},{6,4},{1,3},{7,5},{8,10},{14,12},{9,11},{15,13},{16,18},{22,... | collective-permute-start | bytes 2048 | tf_op jit(solution)/shard_map/ppermute | solution.py:352
  59.3 33.7 %collective-permute-start.3 = (bf16[2,96,2048]{2,1,0:T(8,128)(2,1)}, bf16[2,96,2048]{2,1,0:T(8,128)(2,1)}, u32[]{:S(2)}, u32[]{:S(2)}) collective-permute-start(bf16[2,96,2048]{2,1,0:T(8,128)(2,1)} %bitcast.90), channel_id=1, source_target_pairs={{0,2},{6,4},{1,3},{7,5},{8,10},{14,12},{9,11},{15,13},{16,18},{22,... | collective-permute-start | bytes 2359304 | tf_op jit(solution)/shard_map/ppermute | solution.py:352
  61.5 38.4 %collective-permute-start.8 = (bf16[256,2048]{1,0:T(8,128)(2,1)}, bf16[256,2048]{1,0:T(8,128)(2,1)}, u32[]{:S(2)}, u32[]{:S(2)}) collective-permute-start(bf16[256,2048]{1,0:T(8,128)(2,1)} %collective-permute-done.2.refs_9_.refs_19_.refs_12_), channel_id=1, source_target_pairs={{4,2},{2,4},{5,3},{3,5},{12,10},{10,12},{13,11},{11,13},{20,18},{1... | collective-permute-start | bytes 3145736 | tf_op jit(solution)/shard_map/ppermute | solution.py:358
  65.9 25.4 %collective-permute-start.4 = (bf16[96,2048]{1,0:T(8,128)(2,1)}, bf16[96,2048]{1,0:T(8,128)(2,1)}, u32[]{:S(2)}, u32[]{:S(2)}) collective-permute-start(bf16[96,2048]{1,0:T(8,128)(2,1)} %bitcast.7.refs_1_), channel_id=1, source_target_pairs={{0,2},{6,4},{1,3},{7,5},{8,10},{14,12},{9,11},{15,13},{16,18},{22,... | collective-permute-start | bytes 1179656 | tf_op jit(solution)/shard_map/ppermute | solution.py:352
  76.9 39.9 %collective-permute-start.11 = (bf16[512,512]{1,0:T(8,128)(2,1)}, bf16[512,512]{1,0:T(8,128)(2,1)S(1)}, u32[]{:S(2)}, u32[]{:S(2)}) collective-permute-start(bf16[512,512]{1,0:T(8,128)(2,1)} %bitcast.21.refs_3_.refs_12_.refs_15_), channel_id=1, source_target_pairs={{4,2},{2,4},{5,3},{3,5},{12,10},{10,12},{13,11},{11,13},{20,18},{1... | collective-permute-start | bytes 1572872 | tf_op jit(solution)/shard_map/ppermute | solution.py:358
  91.2 25.5 %collective-permute-start.12 = (bf16[512,512]{1,0:T(8,128)(2,1)}, bf16[512,512]{1,0:T(8,128)(2,1)S(1)}, u32[]{:S(2)}, u32[]{:S(2)}) collective-permute-start(bf16[512,512]{1,0:T(8,128)(2,1)} %collective-permute-done.5.refs_4_.refs_13_.refs_16_), channel_id=1, source_target_pairs={{4,2},{2,4},{5,3},{3,5},{12,10},{10,12},{13,11},{11,13},{20,18},{1... | collective-permute-start | bytes 1572872 | tf_op jit(solution)/shard_map/ppermute | solution.py:358
  93.0 15.1 %collective-permute-start.9 = (bf16[96,2048]{1,0:T(8,128)(2,1)S(1)}, bf16[96,2048]{1,0:T(8,128)(2,1)S(1)}, u32[]{:S(2)}, u32[]{:S(2)}) collective-permute-start(bf16[96,2048]{1,0:T(8,128)(2,1)S(1)} %bitcast.85), channel_id=1, source_target_pairs={{0,2},{6,4},{1,3},{7,5},{8,10},{14,12},{9,11},{15,13},{16,18},{22,... | collective-permute-start | bytes 1179656 | tf_op jit(solution)/shard_map/ppermute | solution.py:352
  98.5 14.6 %collective-permute-start.10 = (bf16[96,2048]{1,0:T(8,128)(2,1)S(1)}, bf16[96,2048]{1,0:T(8,128)(2,1)S(1)}, u32[]{:S(2)}, u32[]{:S(2)}) collective-permute-start(bf16[96,2048]{1,0:T(8,128)(2,1)S(1)} %copy-done.10), channel_id=1, source_target_pairs={{0,2},{6,4},{1,3},{7,5},{8,10},{14,12},{9,11},{15,13},{16,18},{22,... | collective-permute-start | bytes 1179656 | tf_op jit(solution)/shard_map/ppermute | solution.py:352
  120.2 2.7 %collective-permute-start.13 = (bf16[2,48,2048]{2,1,0:T(8,128)(2,1)}, bf16[2,48,2048]{2,1,0:T(8,128)(2,1)S(1)}, u32[]{:S(2)}, u32[]{:S(2)}) collective-permute-start(bf16[2,48,2048]{2,1,0:T(8,128)(2,1)} %get-tuple-element.103), channel_id=1, source_target_pairs={{2,3},{3,2},{4,5},{5,4},{10,11},{11,10},{12,13},{13,12},{18,19},{1... | collective-permute-start | bytes 1179656 | tf_op jit(solution)/shard_map/ppermute | solution.py:367
  120.9 22.2 %collective-permute-start.15 = (bf16[192,1536]{1,0:T(8,128)(2,1)S(1)}, bf16[192,1536]{1,0:T(8,128)(2,1)S(1)}, u32[]{:S(2)}, u32[]{:S(2)}) collective-permute-start(bf16[192,1536]{1,0:T(8,128)(2,1)S(1)} %copy-done.33), channel_id=1, source_target_pairs={{2,0},{4,6},{3,1},{5,7},{10,8},{12,14},{11,9},{13,15},{18,16},{20,... | collective-permute-start | bytes 1769480 | tf_op jit(solution)/shard_map/ppermute | solution.py:355
  122.2 20.9 %collective-permute-start.16 = (bf16[192,1536]{1,0:T(8,128)(2,1)S(1)}, bf16[192,1536]{1,0:T(8,128)(2,1)S(1)}, u32[]{:S(2)}, u32[]{:S(2)}) collective-permute-start(bf16[192,1536]{1,0:T(8,128)(2,1)S(1)} %copy-done.32), channel_id=1, source_target_pairs={{4,2},{2,4},{5,3},{3,5},{12,10},{10,12},{13,11},{11,13},{20,18},{1... | collective-permute-start | bytes 1769480 | tf_op jit(solution)/shard_map/ppermute | solution.py:358
  124.2 18.9 %collective-permute-start.14 = (bf16[2,48,2048]{2,1,0:T(8,128)(2,1)S(1)}, bf16[2,48,2048]{2,1,0:T(8,128)(2,1)S(1)}, u32[]{:S(2)}, u32[]{:S(2)}) collective-permute-start(bf16[2,48,2048]{2,1,0:T(8,128)(2,1)S(1)} %add_convert_fusion.2.refs_7_), channel_id=1, source_target_pairs={{2,10},{4,12},{10,18},{12,20},{18,26},{20,28},{3,11},{5,13},{11,19... | collective-permute-start | bytes 1179656 | tf_op jit(solution)/shard_map/ppermute | solution.py:376
  143.1 2.7 %collective-permute-start.18 = (bf16[2,48,2048]{2,1,0:T(8,128)(2,1)}, bf16[2,48,2048]{2,1,0:T(8,128)(2,1)S(1)}, u32[]{:S(2)}, u32[]{:S(2)}) collective-permute-start(bf16[2,48,2048]{2,1,0:T(8,128)(2,1)} %get-tuple-element.121), channel_id=1, source_target_pairs={{2,3},{3,2},{4,5},{5,4},{10,11},{11,10},{12,13},{13,12},{18,19},{1... | collective-permute-start | bytes 1179656 | tf_op jit(solution)/shard_map/ppermute | solution.py:367
  143.8 7.4 %collective-permute-start.17 = (bf16[2,48,2048]{2,1,0:T(8,128)(2,1)S(1)}, bf16[2,48,2048]{2,1,0:T(8,128)(2,1)S(1)}, u32[]{:S(2)}, u32[]{:S(2)}) collective-permute-start(bf16[2,48,2048]{2,1,0:T(8,128)(2,1)S(1)} %collective-permute-done.14.refs_4_), channel_id=1, source_target_pairs={{2,3},{3,2},{4,5},{5,4},{10,11},{11,10},{12,13},{13,12},{18,19},{1... | collective-permute-start | bytes 1179656 | tf_op jit(solution)/shard_map/ppermute | solution.py:367
  144.5 22.9 %collective-permute-start.20 = (bf16[192,1536]{1,0:T(8,128)(2,1)}, bf16[192,1536]{1,0:T(8,128)(2,1)S(1)}, u32[]{:S(2)}, u32[]{:S(2)}) collective-permute-start(bf16[192,1536]{1,0:T(8,128)(2,1)} %get-tuple-element.123), channel_id=1, source_target_pairs={{4,0},{2,6},{5,1},{3,7},{12,8},{10,14},{13,9},{11,15},{20,16},{18,... | collective-permute-start | bytes 1769480 | tf_op jit(solution)/shard_map/ppermute | solution.py:361
  149.1 27.3 %collective-permute-start.21 = (bf16[2,48,2048]{2,1,0:T(8,128)(2,1)}, bf16[2,48,2048]{2,1,0:T(8,128)(2,1)S(1)}, u32[]{:S(2)}, u32[]{:S(2)}) collective-permute-start(bf16[2,48,2048]{2,1,0:T(8,128)(2,1)} %get-tuple-element.124), channel_id=1, source_target_pairs={{2,0},{4,6},{3,1},{5,7},{10,8},{12,14},{11,9},{13,15},{18,16},{20,... | collective-permute-start | bytes 1179656 | tf_op jit(solution)/shard_map/ppermute | solution.py:355
  150.4 26.0 %collective-permute-start.19 = (bf16[2,48,2048]{2,1,0:T(8,128)(2,1)}, bf16[2,48,2048]{2,1,0:T(8,128)(2,1)S(1)}, u32[]{:S(2)}, u32[]{:S(2)}) collective-permute-start(bf16[2,48,2048]{2,1,0:T(8,128)(2,1)} %get-tuple-element.122), channel_id=1, source_target_pairs={{10,2},{12,4},{18,10},{20,12},{26,18},{28,20},{11,3},{13,5},{19,11... | collective-permute-start | bytes 1179656 | tf_op jit(solution)/shard_map/ppermute | solution.py:376
  176.4 1.5 collective-permute-start.22
  177.1 3.5 %collective-permute-start.23 = (bf16[2,48,2048]{2,1,0:T(8,128)(2,1)S(1)}, bf16[2,48,2048]{2,1,0:T(8,128)(2,1)S(1)}, u32[]{:S(2)}, u32[]{:S(2)}) collective-permute-start(bf16[2,48,2048]{2,1,0:T(8,128)(2,1)S(1)} %collective-permute-done.19.refs_3_), channel_id=1, source_target_pairs={{2,3},{3,2},{4,5},{5,4},{10,11},{11,10},{12,13},{13,12},{18,19},{1... | collective-permute-start | bytes 1179656 | tf_op jit(solution)/shard_map/ppermute | solution.py:367
  179.3 9.8 %collective-permute-start.27 = (bf16[48,2048]{1,0:T(8,128)(2,1)S(1)}, bf16[48,2048]{1,0:T(8,128)(2,1)S(1)}, u32[]{:S(2)}, u32[]{:S(2)}) collective-permute-start(bf16[48,2048]{1,0:T(8,128)(2,1)S(1)} %slice_bitcast_fusion.4), channel_id=1, source_target_pairs={{2,0},{4,6},{3,1},{5,7},{10,8},{12,14},{11,9},{13,15},{18,16},{20,... | collective-permute-start | bytes 589832 | tf_op jit(solution)/shard_map/ppermute | solution.py:355
  183.8 8.8 %collective-permute-start.24 = (bf16[192,512]{1,0:T(8,128)(2,1)}, bf16[192,512]{1,0:T(8,128)(2,1)S(1)}, u32[]{:S(2)}, u32[]{:S(2)}) collective-permute-start(bf16[192,512]{1,0:T(8,128)(2,1)} %get-tuple-element.132), channel_id=1, source_target_pairs={{2,0},{4,6},{3,1},{5,7},{10,8},{12,14},{11,9},{13,15},{18,16},{20,... | collective-permute-start | bytes 589832 | tf_op jit(solution)/shard_map/ppermute | solution.py:355
  185.1 7.5 %collective-permute-start.25 = (bf16[192,512]{1,0:T(8,128)(2,1)}, bf16[192,512]{1,0:T(8,128)(2,1)S(1)}, u32[]{:S(2)}, u32[]{:S(2)}) collective-permute-start(bf16[192,512]{1,0:T(8,128)(2,1)} %get-tuple-element.133), channel_id=1, source_target_pairs={{4,2},{2,4},{5,3},{3,5},{12,10},{10,12},{13,11},{11,13},{20,18},{1... | collective-permute-start | bytes 589832 | tf_op jit(solution)/shard_map/ppermute | solution.py:358
  185.8 13.8 %collective-permute-start.26 = (bf16[192,512]{1,0:T(8,128)(2,1)}, bf16[192,512]{1,0:T(8,128)(2,1)S(1)}, u32[]{:S(2)}, u32[]{:S(2)}) collective-permute-start(bf16[192,512]{1,0:T(8,128)(2,1)} %get-tuple-element.134), channel_id=1, source_target_pairs={{4,0},{2,6},{5,1},{3,7},{12,8},{10,14},{13,9},{11,15},{20,16},{18,... | collective-permute-start | bytes 589832 | tf_op jit(solution)/shard_map/ppermute | solution.py:361
  199.6 0.7 collective-permute-start.28
  201.6 13.6 %collective-permute-start.29 = (bf16[48,2048]{1,0:T(8,128)(2,1)S(1)}, bf16[48,2048]{1,0:T(8,128)(2,1)S(1)}, u32[]{:S(2)}, u32[]{:S(2)}) collective-permute-start(bf16[48,2048]{1,0:T(8,128)(2,1)S(1)} %slice_bitcast_fusion.2), channel_id=1, source_target_pairs={{2,0},{4,6},{3,1},{5,7},{10,8},{12,14},{11,9},{13,15},{18,16},{20,... | collective-permute-start | bytes 589832 | tf_op jit(solution)/shard_map/ppermute | solution.py:355
  (32 other events, 521.1 us)

commit v7 on v6

--- a/solution.py
+++ b/solution.py
@@ -12,7 +12,8 @@
 BLOCKS = 4
 EPSILON = 1e-06
 SCALING = HEAD_DIM ** (-0.5)
-VMEM_BYTES = 58 * 1024 * 1024
+VMEM_BYTES = 50 * 1024 * 1024
+SMALL_VMEM_BYTES = 16 * 1024 * 1024
 
 F32 = jnp.float32
 BF16 = jnp.bfloat16
@@ -363,8 +364,7 @@
         )
 
     def swap_cores(x):
-        pairs = [(h * cores + c, (h + 1) * cores - 1 - c) for h in hosts for c in range(cores)]
-        return lax.ppermute(x, ("dp", "cores"), pairs)
+        return lax.ppermute(x, "cores", [(c, cores - 1 - c) for c in range(cores)])
 
     def along_sections(x, by):
         pairs = [
@@ -415,9 +415,7 @@
     out_own, out_near, near_tables = lax.optimization_barrier((out_shard, out_near, near_tables))
     out_far = [from_host(out_own, m) for m in between]
     out_parts = [out_shard, out_near] + out_far + [from_host(out_near, m) for m in between]
-    up_late, new_late, stash_theirs, x_theirs = lax.optimization_barrier(
-        (up_own, new_own, stash_theirs, x_theirs)
-    )
+    up_late, new_late, stash_theirs = lax.optimization_barrier((up_own, new_own, stash_theirs))
     up_theirs = from_partner(up_late)
     new_theirs = from_partner(new_late)
     far_hosts = [host_table[(dp_no // 2) ^ m] for m in between]
@@ -467,6 +465,7 @@
         return pl.BlockSpec((1,) + x.shape[1:], lambda *_: (i,) + (0,) * (x.ndim - 1))
 
     params = pltpu.CompilerParams(vmem_limit_bytes=VMEM_BYTES)
+    small = pltpu.CompilerParams(vmem_limit_bytes=SMALL_VMEM_BYTES)
 
     def cost(multiply_adds, bytes_accessed):
         return pl.CostEstimate(
@@ -545,27 +544,27 @@
     pack_shapes = [struct((rows, width), BF16)]
     pack_shapes += [struct((rows, 2 * slab + depth), BF16)] * (n - 1)
     up_0, *packs = pl.pallas_call(
-        on_host(functools.partial(pack_kernel, n)),
+        functools.partial(pack_kernel, n),
         grid=(1,),
-        in_specs=[smem] * 2 + all_of(gated, up_own, up_theirs),
+        in_specs=[smem] * 1 + all_of(gated, up_own, up_theirs),
         out_specs=all_of(*pack_shapes),
         out_shape=pack_shapes,
-        compiler_params=params,
+        compiler_params=small,
         name="pack",
-    )(host_flag, offs, gated, up_own, up_theirs)
+    )(offs, gated, up_own, up_theirs)
     packs, out_parts = lax.optimization_barrier((packs, out_parts))
 
     ahead_send, ahead_keep = pl.pallas_call(
-        on_host(functools.partial(out_kernel, n)),
+        functools.partial(out_kernel, n),
         grid=(1,),
-        in_specs=[smem] * 3 + [row_of(gated, 0)] + all_of(*out_parts),
+        in_specs=[smem] * 2 + [row_of(gated, 0)] + all_of(*out_parts),
         out_specs=all_of(*halves),
         out_shape=halves,
         scratch_shapes=[pltpu.VMEM((rows, width), BF16)],
-        compiler_params=params,
+        compiler_params=small,
         cost_estimate=cost(matmul // 4, weight_bytes // 4),
         name="out",
-    )(host_flag, core, offs, gated, *out_parts)
+    )(core, offs, gated, *out_parts)
     ahead_0 = summed(own_rows(x_own, x_theirs), ahead_keep, swap_cores(ahead_send))
     ahead_in = along_sections(ahead_0, 1)
     packs_near = [to_partner(packs[0])] + [from_host(packs[m], m) for m in between]
@@ -575,15 +574,15 @@
     )
     back_landed = swap_cores(back_send)
     back_0, first_pair = pl.pallas_call(
-        on_host(settle_kernel),
+        settle_kernel,
         grid=(1,),
-        in_specs=[smem] * 3
+        in_specs=[smem] * 2
         + all_of(up_own, up_theirs, back_keep, back_keep, back_landed, ahead_0),
         out_specs=all_of(*halves),
         out_shape=halves,
-        compiler_params=params,
+        compiler_params=small,
         name="settle",
-    )(host_flag, core, always, up_own, up_theirs, back_keep, back_keep, back_landed, ahead_0)
+    )(core, always, up_own, up_theirs, back_keep, back_keep, back_landed, ahead_0)
     back_in = along_sections(back_0, -1)
     first_pair = to_partner(first_pair)
 
@@ -631,14 +630,14 @@
     back_their = swap_cores(back_in)
     cut_shapes = [struct((rows, width), BF16)] + [struct((rows, depth), BF16)] * (n - 1)
     up_1, *cuts = pl.pallas_call(
-        on_host(functools.partial(gather_kernel, n)),
+        functools.partial(gather_kernel, n),
         grid=(1,),
-        in_specs=[smem] * 4 + all_of(back_in, back_their, new_own, new_theirs),
+        in_specs=[smem] * 3 + all_of(back_in, back_their, new_own, new_theirs),
         out_specs=all_of(*cut_shapes),
         out_shape=cut_shapes,
-        compiler_params=params,
+        compiler_params=small,
         name="gather",
-    )(host_flag, core, offs, last_flag, back_in, back_their, new_own, new_theirs)
+    )(core, offs, last_flag, back_in, back_their, new_own, new_theirs)
     landed = [to_partner(cuts[0])] + [from_host(cuts[m], m) for m in between]
     landed += [to_beyond(cuts[n // 2 + m - 1], m) for m in between]
     back_send, back_keep = backward(up_1, 1)
@@ -656,7 +655,7 @@
         in_specs=[smem] * 2 + all_of(gated, up_0, up_1, *packs_near, *packs_beyond, *landed),
         out_specs=pl.BlockSpec((slab, depth), lambda *_: (0, 0)),
         out_shape=struct((slab, depth), F32),
-        compiler_params=params,
+        compiler_params=small,
         cost_estimate=cost(matmul // 4, weight_bytes // 4),
         name="grads",
     )(

time: 219 us -> 201 us (0.918)
  Pallas kernels: 32.4 us -> 22.9 us
  waiting for transfers between devices: 102 us -> 93.5 us
  starting transfers between devices: 49.8 us -> 53 us
    ppermute x8, waiting for transfers between devices: 49.1 us -> 44.8 us  [from_partner(): return lax.ppermute(x, 'dp', [(h ^ 1, h) for h in hosts])]
    pallas_call x4, Pallas kernels: 10.3 us -> 6.75 us  [the longest x1 2.15 us: per_device(): pl.pallas_call(settle_kernel, grid=(1,), in_specs=[smem] * 2 + all_of(up_...]
    ppermute x2, waiting for transfers between devices: 16.1 us -> 12.9 us  [to_beyond(): lax.ppermute(x, 'dp', [(hosts[k ^ m], hosts[k] ^ 1) for k in range(n // 2)])]
    eq x4, local copies, waits for them, and re-layouts: 3.2 us -> 0.54 us  [block_keep(): jnp.repeat(jnp.repeat(block_marks, BLOCK, axis=-2), BLOCK, axis=-1) == 1]
    reshape x2, local copies, waits for them, and re-layouts: 0.16 us -> 2.73 us  [per_device(): m.reshape(m.shape[:2] + (-1,))]
    ppermute x6, starting transfers between devices: 4.08 us -> 6.36 us  [swap_cores(): return lax.ppermute(x, 'cores', [(c, cores - 1 - c) for c in range(cores)])]
    unnamed x68 -> x56, local copies, waits for them, and re-layouts: 4 us -> 5.39 us
  transfers between devices with their start and end apart: 30 -> 30, of which waited for: 11 -> 14; matrix products, arithmetic and copies ran while one was open for 10% -> 10% of each run, Pallas kernels for 14% -> 11%
where the time goes in v7:
time: 201 us; the launch traced here: 199 us
  waiting for transfers between devices  93.5 us (47%)
  starting transfers between devices  53 us (26%)
  Pallas kernels  22.9 us (11%)
  local copies, waits for them, and re-layouts  13.6 us (7%)
  other arithmetic  12.6 us (6%)
  between operations  3.12 us (2%)
    ppermute x8, waiting for transfers between devices, from_partner(): return lax.ppermute(x, 'dp', [(h ^ 1, h) for h in hosts])  44.8 us
    ppermute x5, waiting for transfers between devices, to_partner(): return lax.ppermute(x, 'dp', [(h, h ^ 1) for h in hosts])  34.3 us
    ppermute x8, starting transfers between devices, from_partner(): return lax.ppermute(x, 'dp', [(h ^ 1, h) for h in hosts])  28.2 us
    ppermute x2, waiting for transfers between devices, to_beyond(): lax.ppermute(x, 'dp', [(hosts[k ^ m], hosts[k] ^ 1) for k in range(n // 2)])  12.9 us
    pallas_call x1, Pallas kernels, per_device(): pl.pallas_call(on_host(functools.partial(project_kernel, parts)), grid=(h...  7.25 us
    ppermute x7, starting transfers between devices, from_host(): lax.ppermute(x, 'dp', [(hosts[k ^ m], hosts[k]) for k in range(n // 2)])  6.99 us
    ppermute x5, starting transfers between devices, to_partner(): return lax.ppermute(x, 'dp', [(h, h ^ 1) for h in hosts])  6.57 us
    ppermute x6, starting transfers between devices, swap_cores(): return lax.ppermute(x, 'cores', [(c, cores - 1 - c) for c in range(cores)])  6.36 us
  transfers between devices with their start and end apart: 30, of which 14 were waited for; matrix products, arithmetic and copies ran while one was open for 10% of the time, Pallas kernels for 11%

profile of v7, /device:TPU:5, one launch (start us, length us, event | category | flops | bytes accessed | tf_op | source)
XLA Modules:
  0.0 198.7 jit_solution(8973834775619245755)
XLA Ops:
  1.6 3.2 %slice_bitcast_fusion = (bf16[256,2048]{1,0:T(8,128)(2,1)}, bf16[256,2048]{1,0:T(8,128)(2,1)}) fusion(bf16[1,512,2048]{2,1,0:T(8,128)(2,1)} %param.17), kind=kLoop, calls=%fused_computation | loop fusion | bytes 4194304 | tf_op jit(solution)/shard_map/slice | solution.py:386
  4.8 6.6 %collective-permute-start.1 = (bf16[256,2048]{1,0:T(8,128)(2,1)}, bf16[256,2048]{1,0:T(8,128)(2,1)}, u32[]{:S(2)}, u32[]{:S(2)}) collective-permute-start(bf16[256,2048]{1,0:T(8,128)(2,1)} %get-tuple-element.144), channel_id=1, source_target_pairs={{0,2},{6,4},{1,3},{7,5},{8,10},{14,12},{9,11},{15,13},{16,18},{22,... | collective-permute-start | bytes 3145736 | tf_op jit(solution)/shard_map/ppermute | solution.py:353
  11.4 2.3 %collective-permute-start.2 = (bf16[256,2048]{1,0:T(8,128)(2,1)}, bf16[256,2048]{1,0:T(8,128)(2,1)}, u32[]{:S(2)}, u32[]{:S(2)}) collective-permute-start(bf16[256,2048]{1,0:T(8,128)(2,1)} %get-tuple-element.143), channel_id=1, source_target_pairs={{0,2},{6,4},{1,3},{7,5},{8,10},{14,12},{9,11},{15,13},{16,18},{22,... | collective-permute-start | bytes 3145736 | tf_op jit(solution)/shard_map/ppermute | solution.py:353
  19.1 13.1 %collective-permute-done.1.refs_8_.refs_18_.refs_11_ = bf16[256,2048]{1,0:T(8,128)(2,1)} collective-permute-done((bf16[256,2048]{1,0:T(8,128)(2,1)}, bf16[256,2048]{1,0:T(8,128)(2,1)}, u32[]{:S(2)}, u32[]{:S(2)}) %collective-permute-start.1) | collective-permute-done | bytes 1048608 | tf_op jit(solution)/shard_map/ppermute | solution.py:353
  32.2 1.6 collective-permute-start.7
  33.8 20.8 %collective-permute-done.2.refs_9_.refs_19_.refs_12_ = bf16[256,2048]{1,0:T(8,128)(2,1)} collective-permute-done((bf16[256,2048]{1,0:T(8,128)(2,1)}, bf16[256,2048]{1,0:T(8,128)(2,1)}, u32[]{:S(2)}, u32[]{:S(2)}) %collective-permute-start.2) | collective-permute-done | bytes 1048608 | tf_op jit(solution)/shard_map/ppermute | solution.py:353
  59.8 4.1 %collective-permute-start.6 = (s32[2,5,17]{2,0,1:T(2,128)S(1)}, s32[2,5,17]{2,0,1:T(2,128)S(1)}, u32[]{:S(2)}, u32[]{:S(2)}) collective-permute-start(s32[2,5,17]{2,0,1:T(2,128)S(1)} %add_add_fusion), channel_id=1, source_target_pairs={{0,2},{6,4},{1,3},{7,5},{8,10},{14,12},{9,11},{15,13},{16,18},{22,... | collective-permute-start | bytes 2048 | tf_op jit(solution)/shard_map/ppermute | solution.py:353
  63.9 2.2 %collective-permute-start.4 = (bf16[2,96,2048]{2,1,0:T(8,128)(2,1)}, bf16[2,96,2048]{2,1,0:T(8,128)(2,1)}, u32[]{:S(2)}, u32[]{:S(2)}) collective-permute-start(bf16[2,96,2048]{2,1,0:T(8,128)(2,1)} %bitcast.98), channel_id=1, source_target_pairs={{0,2},{6,4},{1,3},{7,5},{8,10},{14,12},{9,11},{15,13},{16,18},{22,... | collective-permute-start | bytes 2359304 | tf_op jit(solution)/shard_map/ppermute | solution.py:353
  66.1 1.7 collective-permute-start.8
  67.8 2.4 %slice_select_fusion = (bf16[1,96,2048]{2,1,0:T(8,128)(2,1)S(1)}, bf16[1,96,2048]{2,1,0:T(8,128)(2,1)S(1)}, bf16[96,2048]{1,0:T(8,128)(2,1)}) fusion(bf16[2,96,2048]{2,1,0:T(8,128)(2,1)} %param.14, bf16[2,96,2048]{2,1,0:T(8,128)(2,1)} %param.12, pred[]{:T(512)S(6)} %eq.44, bf16[1,96,2048]{2,1,0:T(8,128)(2,1)S(1)} %copy-done.23, ...), kind=kLoop, calls=%fused_computation.16 | loop fusion | flops 589824 | bytes 3538946 | tf_op jit(solution)/shard_map/jit(_where)/select_n | solution.py:414
  70.2 2.1 %collective-permute-start.3 = (bf16[96,2048]{1,0:T(8,128)(2,1)S(1)}, bf16[96,2048]{1,0:T(8,128)(2,1)}, u32[]{:S(2)}, u32[]{:S(2)}) collective-permute-start(bf16[96,2048]{1,0:T(8,128)(2,1)S(1)} %bitcast.91), channel_id=1, source_target_pairs={{0,2},{6,4},{1,3},{7,5},{8,10},{14,12},{9,11},{15,13},{16,18},{22,... | collective-permute-start | bytes 1179656 | tf_op jit(solution)/shard_map/ppermute | solution.py:353
  74.3 7.7 %collective-permute-done.4.refs_4_.refs_11_ = bf16[2,96,2048]{2,1,0:T(8,128)(2,1)} collective-permute-done((bf16[2,96,2048]{2,1,0:T(8,128)(2,1)}, bf16[2,96,2048]{2,1,0:T(8,128)(2,1)}, u32[]{:S(2)}, u32[]{:S(2)}) %collective-permute-start.4) | collective-permute-done | bytes 786464 | tf_op jit(solution)/shard_map/ppermute | solution.py:353
  83.7 5.5 %collective-permute-start.9 = (bf16[96,2048]{1,0:T(8,128)(2,1)S(1)}, bf16[96,2048]{1,0:T(8,128)(2,1)S(1)}, u32[]{:S(2)}, u32[]{:S(2)}) collective-permute-start(bf16[96,2048]{1,0:T(8,128)(2,1)S(1)} %bitcast.80), channel_id=1, source_target_pairs={{0,2},{6,4},{1,3},{7,5},{8,10},{14,12},{9,11},{15,13},{16,18},{22,... | collective-permute-start | bytes 1179656 | tf_op jit(solution)/shard_map/ppermute | solution.py:353
  90.3 4.2 %collective-permute-start.10 = (bf16[96,2048]{1,0:T(8,128)(2,1)}, bf16[96,2048]{1,0:T(8,128)(2,1)S(1)}, u32[]{:S(2)}, u32[]{:S(2)}) collective-permute-start(bf16[96,2048]{1,0:T(8,128)(2,1)} %get-tuple-element.90.up_own.own), channel_id=1, source_target_pairs={{0,2},{6,4},{1,3},{7,5},{8,10},{14,12},{9,11},{15,13},{16,18},{22,... | collective-permute-start | bytes 1179656 | tf_op jit(solution)/shard_map/ppermute | solution.py:353
  95.5 7.2 %project.1 = (bf16[3,192,512]{2,1,0:T(8,128)(2,1)S(1)}, f32[2,192,512]{2,1,0:T(8,128)S(1)}, bf16[2,192,1536]{2,1,0:T(8,128)(2,1)}, f32[2,192,2048]{2,1,0:T(8,128...) custom-call(s32[1]{0:T(128)} %bitcast.9.host, ...), custom_call_target="tpu_custom_call" | custom-call | flops 4831838208 | bytes 20971520 | tf_op jit(solution)/shard_map/project/pallas_call | solution.py:484
  104.6 2.0 %collective-permute-done.10.up_theirs.theirs = bf16[96,2048]{1,0:T(8,128)(2,1)S(1)} collective-permute-done((bf16[96,2048]{1,0:T(8,128)(2,1)}, bf16[96,2048]{1,0:T(8,128)(2,1)S(1)}, u32[]{:S(2)}, u32[]{:S(2)}) %collective-permute-start.10) | collective-permute-done | bytes 393248 | tf_op jit(solution)/shard_map/ppermute | solution.py:353
  106.6 2.0 %pack.1 = (bf16[192,2048]{1,0:T(8,128)(2,1)S(1)}, bf16[192,1536]{1,0:T(8,128)(2,1)S(1)}, bf16[192,1536]{1,0:T(8,128)(2,1)S(1)}, bf16[192,1536]{1,0:T(8,128)(2,1)}) custom-call(s32[4]{0:T(128)S(1)} %add_multiply_fusion.offs.refs_2_, bf16[3,192,512]{2,1,0:T(8,128)(2,1)S(1)} %get-tuple-element.136.gated, bf16[96,2048]{1,0:T(8,128)(2,1)} %get-tuple-element.90.up_own.own, ...), custom_call_target="tpu_custom_call" | custom-call | tf_op jit(solution)/shard_map/pack/pallas_call | solution.py:546
  109.6 1.9 out.1
  112.3 3.6 %collective-permute-start.13 = (bf16[2,48,2048]{2,1,0:T(8,128)(2,1)}, bf16[2,48,2048]{2,1,0:T(8,128)(2,1)}, u32[]{:S(2)}, u32[]{:S(2)}) collective-permute-start(bf16[2,48,2048]{2,1,0:T(8,128)(2,1)} %get-tuple-element.101), channel_id=1, source_target_pairs={{0,1},{1,0},{2,3},{3,2},{4,5},{5,4},{6,7},{7,6},{8,9},{9,8},{10,11... | collective-permute-start | bytes 1179656 | tf_op jit(solution)/shard_map/ppermute | solution.py:367
  115.9 1.4 collective-permute-start.15
  119.4 1.4 collective-permute-start.14
  121.6 16.1 %collective-permute-done.15.rest_0_ = bf16[192,1536]{1,0:T(8,128)(2,1)S(1)} collective-permute-done((bf16[192,1536]{1,0:T(8,128)(2,1)}, bf16[192,1536]{1,0:T(8,128)(2,1)S(1)}, u32[]{:S(2)}, u32[]{:S(2)}) %collective-permute-start.15) | collective-permute-done | bytes 589856 | tf_op jit(solution)/shard_map/ppermute | solution.py:356
  140.6 2.1 %settle.1 = (bf16[2,48,2048]{2,1,0:T(8,128)(2,1)}, bf16[2,48,2048]{2,1,0:T(8,128)(2,1)}) custom-call(s32[1]{0:T(128)} %bitcast.6.core.refs_0_, s32[1]{0:T(128)} %constant.76.clone.1.fresh, bf16[96,2048]{1,0:T(8,128)(2,1)} %get-tuple-element.90.up_own.own, bf16[96,2048]{1,0:T(8,128)(2,1)S(1)} %copy-done.14, ...), custom_call_target="tpu_custom_call" | custom-call | tf_op jit(solution)/shard_map/settle/pallas_call | solution.py:576
  144.9 4.6 %forward.1 = (bf16[2,48,2048]{2,1,0:T(8,128)(2,1)S(1)}, bf16[2,48,2048]{2,1,0:T(8,128)(2,1)S(1)}) custom-call(s32[1]{0:T(128)} %bitcast.9.host, s32[1]{0:T(128)} %bitcast.6.core.refs_0_, s32[6]{0:T(128)S(1)} %stack.85.refs_0_.refs_1_, s32[4]{0:T(128)S(1)} %add_multiply_fusion.offs.refs_2_, s32[1]{0:T(128)} %bitcast.34.refs_3_, ...), custom_call_target="tpu_custom_call" | custom-call | flops 3221225472 | bytes 20971520 | tf_op jit(solution)/shard_map/forward/pallas_call | solution.py:591
  149.5 8.1 %collective-permute-done.20.rest_2_ = bf16[192,1536]{1,0:T(8,128)(2,1)} collective-permute-done((bf16[192,1536]{1,0:T(8,128)(2,1)}, bf16[192,1536]{1,0:T(8,128)(2,1)}, u32[]{:S(2)}, u32[]{:S(2)}) %collective-permute-start.20) | collective-permute-done | bytes 589856 | tf_op jit(solution)/shard_map/ppermute | solution.py:362
  157.6 9.0 %collective-permute-done.21 = bf16[2,48,2048]{2,1,0:T(8,128)(2,1)} collective-permute-done((bf16[2,48,2048]{2,1,0:T(8,128)(2,1)}, bf16[2,48,2048]{2,1,0:T(8,128)(2,1)}, u32[]{:S(2)}, u32[]{:S(2)}) %collective-permute-start.21) | collective-permute-done | bytes 393248 | tf_op jit(solution)/shard_map/ppermute | solution.py:356
  175.8 2.0 collective-permute-done.27
  177.7 4.2 %collective-permute-done.24.rest_3_ = bf16[192,512]{1,0:T(8,128)(2,1)S(1)} collective-permute-done((bf16[192,512]{1,0:T(8,128)(2,1)S(1)}, bf16[192,512]{1,0:T(8,128)(2,1)S(1)}, u32[]{:S(2)}, u32[]{:S(2)}) %collective-permute-start.24) | collective-permute-done | bytes 196640 | tf_op jit(solution)/shard_map/ppermute | solution.py:356
  182.0 4.8 %collective-permute-done.26.rest_5_ = bf16[192,512]{1,0:T(8,128)(2,1)S(1)} collective-permute-done((bf16[192,512]{1,0:T(8,128)(2,1)S(1)}, bf16[192,512]{1,0:T(8,128)(2,1)S(1)}, u32[]{:S(2)}, u32[]{:S(2)}) %collective-permute-start.26) | collective-permute-done | bytes 196640 | tf_op jit(solution)/shard_map/ppermute | solution.py:362
  186.7 1.5 collective-permute-start.28
  192.0 2.8 %grads.1 = f32[512,512]{1,0:T(8,128)} custom-call(s32[1]{0:T(128)} %bitcast.9.host, s32[4]{0:T(128)S(1)} %add_multiply_fusion.offs.refs_2_, bf16[3,192,512]{2,1,0:T(8,128)(2,1)S(1)} %get-tuple-element.136.gated, bf16[192,2048]{1,0:T(8,128)(2,1)S(1)} %copy-done.8, bf16[192,2048]{1,0:T(8,128)(2,1)S(1)} %get-tuple-element.127.refs_3_.up_1, ...), custom_call_target="tpu_custom_call" | custom-call | flops 402653184 | bytes 2621440 | tf_op jit(solution)/shard_map/grads/pallas_call | solution.py:652
  194.8 3.1 %collective-permute-done.29 = bf16[48,2048]{1,0:T(8,128)(2,1)S(1)} collective-permute-done((bf16[48,2048]{1,0:T(8,128)(2,1)S(1)}, bf16[48,2048]{1,0:T(8,128)(2,1)S(1)}, u32[]{:S(2)}, u32[]{:S(2)}) %collective-permute-start.29) | collective-permute-done | bytes 196640 | tf_op jit(solution)/shard_map/ppermute | solution.py:356
  (132 shorter events, 40.2 us)
Async XLA Ops:
  0.7 54.0 %copy-start.27 = (s32[1,5]{1,0:T(1,128)S(1)}, s32[1,5]{1,0:T(1,128)}, u32[]{:S(2)}) copy-start(s32[1,5]{1,0:T(1,128)} %param.19) | copy-start | bytes 64
  0.7 67.1 %copy-start.23 = (bf16[1,96,2048]{2,1,0:T(8,128)(2,1)S(1)}, bf16[1,96,2048]{2,1,0:T(8,128)(2,1)}, u32[]{:S(2)}) copy-start(bf16[1,96,2048]{2,1,0:T(8,128)(2,1)} %param.13) | copy-start | bytes 1179652
  0.7 54.0 %collective-permute-start = (bf16[512,2048]{1,0:T(8,128)(2,1)}, bf16[512,2048]{1,0:T(8,128)(2,1)S(1)}, u32[]{:S(2)}, u32[]{:S(2)}) collective-permute-start(bf16[512,2048]{1,0:T(8,128)(2,1)} %bitcast.93), channel_id=1, source_target_pairs={{4,2},{2,4},{5,3},{3,5},{12,10},{10,12},{13,11},{11,13},{20,18},{1... | collective-permute-start | bytes 6291464 | tf_op jit(solution)/shard_map/ppermute | solution.py:359
  4.8 27.4 %collective-permute-start.1 = (bf16[256,2048]{1,0:T(8,128)(2,1)}, bf16[256,2048]{1,0:T(8,128)(2,1)}, u32[]{:S(2)}, u32[]{:S(2)}) collective-permute-start(bf16[256,2048]{1,0:T(8,128)(2,1)} %get-tuple-element.144), channel_id=1, source_target_pairs={{0,2},{6,4},{1,3},{7,5},{8,10},{14,12},{9,11},{15,13},{16,18},{22,... | collective-permute-start | bytes 3145736 | tf_op jit(solution)/shard_map/ppermute | solution.py:353
  11.4 43.3 %collective-permute-start.2 = (bf16[256,2048]{1,0:T(8,128)(2,1)}, bf16[256,2048]{1,0:T(8,128)(2,1)}, u32[]{:S(2)}, u32[]{:S(2)}) collective-permute-start(bf16[256,2048]{1,0:T(8,128)(2,1)} %get-tuple-element.143), channel_id=1, source_target_pairs={{0,2},{6,4},{1,3},{7,5},{8,10},{14,12},{9,11},{15,13},{16,18},{22,... | collective-permute-start | bytes 3145736 | tf_op jit(solution)/shard_map/ppermute | solution.py:353
  13.6 56.6 %collective-permute-start.5 = (bf16[512,512]{1,0:T(8,128)(2,1)S(1)}, bf16[512,512]{1,0:T(8,128)(2,1)S(1)}, u32[]{:S(2)}, u32[]{:S(2)}) collective-permute-start(bf16[512,512]{1,0:T(8,128)(2,1)S(1)} %bitcast.83), channel_id=1, source_target_pairs={{0,2},{6,4},{1,3},{7,5},{8,10},{14,12},{9,11},{15,13},{16,18},{22,... | collective-permute-start | bytes 1572872 | tf_op jit(solution)/shard_map/ppermute | solution.py:353
  32.2 51.5 %collective-permute-start.7 = (bf16[256,2048]{1,0:T(8,128)(2,1)}, bf16[256,2048]{1,0:T(8,128)(2,1)}, u32[]{:S(2)}, u32[]{:S(2)}) collective-permute-start(bf16[256,2048]{1,0:T(8,128)(2,1)} %collective-permute-done.1.refs_8_.refs_18_.refs_11_), channel_id=1, source_target_pairs={{4,2},{2,4},{5,3},{3,5},{12,10},{10,12},{13,11},{11,13},{20,18},{1... | collective-permute-start | bytes 3145736 | tf_op jit(solution)/shard_map/ppermute | solution.py:359
  59.8 12.4 %collective-permute-start.6 = (s32[2,5,17]{2,0,1:T(2,128)S(1)}, s32[2,5,17]{2,0,1:T(2,128)S(1)}, u32[]{:S(2)}, u32[]{:S(2)}) collective-permute-start(s32[2,5,17]{2,0,1:T(2,128)S(1)} %add_add_fusion), channel_id=1, source_target_pairs={{0,2},{6,4},{1,3},{7,5},{8,10},{14,12},{9,11},{15,13},{16,18},{22,... | collective-permute-start | bytes 2048 | tf_op jit(solution)/shard_map/ppermute | solution.py:353
  63.9 18.0 %collective-permute-start.4 = (bf16[2,96,2048]{2,1,0:T(8,128)(2,1)}, bf16[2,96,2048]{2,1,0:T(8,128)(2,1)}, u32[]{:S(2)}, u32[]{:S(2)}) collective-permute-start(bf16[2,96,2048]{2,1,0:T(8,128)(2,1)} %bitcast.98), channel_id=1, source_target_pairs={{0,2},{6,4},{1,3},{7,5},{8,10},{14,12},{9,11},{15,13},{16,18},{22,... | collective-permute-start | bytes 2359304 | tf_op jit(solution)/shard_map/ppermute | solution.py:353
  66.1 28.4 %collective-permute-start.8 = (bf16[256,2048]{1,0:T(8,128)(2,1)}, bf16[256,2048]{1,0:T(8,128)(2,1)}, u32[]{:S(2)}, u32[]{:S(2)}) collective-permute-start(bf16[256,2048]{1,0:T(8,128)(2,1)} %collective-permute-done.2.refs_9_.refs_19_.refs_12_), channel_id=1, source_target_pairs={{4,2},{2,4},{5,3},{3,5},{12,10},{10,12},{13,11},{11,13},{20,18},{1... | collective-permute-start | bytes 3145736 | tf_op jit(solution)/shard_map/ppermute | solution.py:359
  70.2 20.1 %collective-permute-start.3 = (bf16[96,2048]{1,0:T(8,128)(2,1)S(1)}, bf16[96,2048]{1,0:T(8,128)(2,1)}, u32[]{:S(2)}, u32[]{:S(2)}) collective-permute-start(bf16[96,2048]{1,0:T(8,128)(2,1)S(1)} %bitcast.91), channel_id=1, source_target_pairs={{0,2},{6,4},{1,3},{7,5},{8,10},{14,12},{9,11},{15,13},{16,18},{22,... | collective-permute-start | bytes 1179656 | tf_op jit(solution)/shard_map/ppermute | solution.py:353
  73.2 36.3 %collective-permute-start.11 = (bf16[512,512]{1,0:T(8,128)(2,1)S(1)}, bf16[512,512]{1,0:T(8,128)(2,1)S(1)}, u32[]{:S(2)}, u32[]{:S(2)}) collective-permute-start(bf16[512,512]{1,0:T(8,128)(2,1)S(1)} %bitcast.84), channel_id=1, source_target_pairs={{4,2},{2,4},{5,3},{3,5},{12,10},{10,12},{13,11},{11,13},{20,18},{1... | collective-permute-start | bytes 1572872 | tf_op jit(solution)/shard_map/ppermute | solution.py:359
  81.9 27.6 %collective-permute-start.12 = (bf16[512,512]{1,0:T(8,128)(2,1)S(1)}, bf16[512,512]{1,0:T(8,128)(2,1)S(1)}, u32[]{:S(2)}, u32[]{:S(2)}) collective-permute-start(bf16[512,512]{1,0:T(8,128)(2,1)S(1)} %collective-permute-done.5.rest_1_.refs_13_.refs_16_), channel_id=1, source_target_pairs={{4,2},{2,4},{5,3},{3,5},{12,10},{10,12},{13,11},{11,13},{20,18},{1... | collective-permute-start | bytes 1572872 | tf_op jit(solution)/shard_map/ppermute | solution.py:359
  83.7 20.9 %collective-permute-start.9 = (bf16[96,2048]{1,0:T(8,128)(2,1)S(1)}, bf16[96,2048]{1,0:T(8,128)(2,1)S(1)}, u32[]{:S(2)}, u32[]{:S(2)}) collective-permute-start(bf16[96,2048]{1,0:T(8,128)(2,1)S(1)} %bitcast.80), channel_id=1, source_target_pairs={{0,2},{6,4},{1,3},{7,5},{8,10},{14,12},{9,11},{15,13},{16,18},{22,... | collective-permute-start | bytes 1179656 | tf_op jit(solution)/shard_map/ppermute | solution.py:353
  90.3 16.4 %collective-permute-start.10 = (bf16[96,2048]{1,0:T(8,128)(2,1)}, bf16[96,2048]{1,0:T(8,128)(2,1)S(1)}, u32[]{:S(2)}, u32[]{:S(2)}) collective-permute-start(bf16[96,2048]{1,0:T(8,128)(2,1)} %get-tuple-element.90.up_own.own), channel_id=1, source_target_pairs={{0,2},{6,4},{1,3},{7,5},{8,10},{14,12},{9,11},{15,13},{16,18},{22,... | collective-permute-start | bytes 1179656 | tf_op jit(solution)/shard_map/ppermute | solution.py:353
  112.3 5.7 %collective-permute-start.13 = (bf16[2,48,2048]{2,1,0:T(8,128)(2,1)}, bf16[2,48,2048]{2,1,0:T(8,128)(2,1)}, u32[]{:S(2)}, u32[]{:S(2)}) collective-permute-start(bf16[2,48,2048]{2,1,0:T(8,128)(2,1)} %get-tuple-element.101), channel_id=1, source_target_pairs={{0,1},{1,0},{2,3},{3,2},{4,5},{5,4},{6,7},{7,6},{8,9},{9,8},{10,11... | collective-permute-start | bytes 1179656 | tf_op jit(solution)/shard_map/ppermute | solution.py:367
  115.9 21.8 %collective-permute-start.15 = (bf16[192,1536]{1,0:T(8,128)(2,1)}, bf16[192,1536]{1,0:T(8,128)(2,1)S(1)}, u32[]{:S(2)}, u32[]{:S(2)}) collective-permute-start(bf16[192,1536]{1,0:T(8,128)(2,1)} %copy-done.21), channel_id=1, source_target_pairs={{2,0},{4,6},{3,1},{5,7},{10,8},{12,14},{11,9},{13,15},{18,16},{20,... | collective-permute-start | bytes 1769480 | tf_op jit(solution)/shard_map/ppermute | solution.py:356
  117.3 21.2 %collective-permute-start.16 = (bf16[192,1536]{1,0:T(8,128)(2,1)}, bf16[192,1536]{1,0:T(8,128)(2,1)S(1)}, u32[]{:S(2)}, u32[]{:S(2)}) collective-permute-start(bf16[192,1536]{1,0:T(8,128)(2,1)} %copy-done.20), channel_id=1, source_target_pairs={{4,2},{2,4},{5,3},{3,5},{12,10},{10,12},{13,11},{11,13},{20,18},{1... | collective-permute-start | bytes 1769480 | tf_op jit(solution)/shard_map/ppermute | solution.py:359
  119.4 19.1 %collective-permute-start.14 = (bf16[2,48,2048]{2,1,0:T(8,128)(2,1)S(1)}, bf16[2,48,2048]{2,1,0:T(8,128)(2,1)}, u32[]{:S(2)}, u32[]{:S(2)}) collective-permute-start(bf16[2,48,2048]{2,1,0:T(8,128)(2,1)S(1)} %add_convert_fusion.2.earlier), channel_id=1, source_target_pairs={{2,10},{4,12},{10,18},{12,20},{18,26},{20,28},{3,11},{5,13},{11,19... | collective-permute-start | bytes 1179656 | tf_op jit(solution)/shard_map/ppermute | solution.py:376
  138.5 2.0 %collective-permute-start.18 = (bf16[2,48,2048]{2,1,0:T(8,128)(2,1)S(1)}, bf16[2,48,2048]{2,1,0:T(8,128)(2,1)S(1)}, u32[]{:S(2)}, u32[]{:S(2)}) collective-permute-start(bf16[2,48,2048]{2,1,0:T(8,128)(2,1)S(1)} %get-tuple-element.119), channel_id=1, source_target_pairs={{0,1},{1,0},{2,3},{3,2},{4,5},{5,4},{6,7},{7,6},{8,9},{9,8},{10,11... | collective-permute-start | bytes 1179656 | tf_op jit(solution)/shard_map/ppermute | solution.py:367
  139.2 5.7 %collective-permute-start.17 = (bf16[2,48,2048]{2,1,0:T(8,128)(2,1)}, bf16[2,48,2048]{2,1,0:T(8,128)(2,1)}, u32[]{:S(2)}, u32[]{:S(2)}) collective-permute-start(bf16[2,48,2048]{2,1,0:T(8,128)(2,1)} %collective-permute-done.14.refs_4_), channel_id=1, source_target_pairs={{0,1},{1,0},{2,3},{3,2},{4,5},{5,4},{6,7},{7,6},{8,9},{9,8},{10,11... | collective-permute-start | bytes 1179656 | tf_op jit(solution)/shard_map/ppermute | solution.py:367
  139.2 18.4 %collective-permute-start.20 = (bf16[192,1536]{1,0:T(8,128)(2,1)}, bf16[192,1536]{1,0:T(8,128)(2,1)}, u32[]{:S(2)}, u32[]{:S(2)}) collective-permute-start(bf16[192,1536]{1,0:T(8,128)(2,1)} %get-tuple-element.121), channel_id=1, source_target_pairs={{4,0},{2,6},{5,1},{3,7},{12,8},{10,14},{13,9},{11,15},{20,16},{18,... | collective-permute-start | bytes 1769480 | tf_op jit(solution)/shard_map/ppermute | solution.py:362
  142.7 23.9 %collective-permute-start.21 = (bf16[2,48,2048]{2,1,0:T(8,128)(2,1)}, bf16[2,48,2048]{2,1,0:T(8,128)(2,1)}, u32[]{:S(2)}, u32[]{:S(2)}) collective-permute-start(bf16[2,48,2048]{2,1,0:T(8,128)(2,1)} %get-tuple-element.122), channel_id=1, source_target_pairs={{2,0},{4,6},{3,1},{5,7},{10,8},{12,14},{11,9},{13,15},{18,16},{20,... | collective-permute-start | bytes 1179656 | tf_op jit(solution)/shard_map/ppermute | solution.py:356
  144.0 22.6 %collective-permute-start.19 = (bf16[2,48,2048]{2,1,0:T(8,128)(2,1)}, bf16[2,48,2048]{2,1,0:T(8,128)(2,1)S(1)}, u32[]{:S(2)}, u32[]{:S(2)}) collective-permute-start(bf16[2,48,2048]{2,1,0:T(8,128)(2,1)} %get-tuple-element.120), channel_id=1, source_target_pairs={{10,2},{12,4},{18,10},{20,12},{26,18},{28,20},{11,3},{13,5},{19,11... | collective-permute-start | bytes 1179656 | tf_op jit(solution)/shard_map/ppermute | solution.py:376
  166.6 1.8 collective-permute-start.22
  167.1 4.0 %collective-permute-start.23 = (bf16[2,48,2048]{2,1,0:T(8,128)(2,1)S(1)}, bf16[2,48,2048]{2,1,0:T(8,128)(2,1)S(1)}, u32[]{:S(2)}, u32[]{:S(2)}) collective-permute-start(bf16[2,48,2048]{2,1,0:T(8,128)(2,1)S(1)} %collective-permute-done.19.mine), channel_id=1, source_target_pairs={{0,1},{1,0},{2,3},{3,2},{4,5},{5,4},{6,7},{7,6},{8,9},{9,8},{10,11... | collective-permute-start | bytes 1179656 | tf_op jit(solution)/shard_map/ppermute | solution.py:367
  169.7 8.0 %collective-permute-start.27 = (bf16[48,2048]{1,0:T(8,128)(2,1)S(1)}, bf16[48,2048]{1,0:T(8,128)(2,1)S(1)}, u32[]{:S(2)}, u32[]{:S(2)}) collective-permute-start(bf16[48,2048]{1,0:T(8,128)(2,1)S(1)} %slice_bitcast_fusion.4), channel_id=1, source_target_pairs={{2,0},{4,6},{3,1},{5,7},{10,8},{12,14},{11,9},{13,15},{18,16},{20,... | collective-permute-start | bytes 589832 | tf_op jit(solution)/shard_map/ppermute | solution.py:356
  171.7 10.2 %collective-permute-start.24 = (bf16[192,512]{1,0:T(8,128)(2,1)S(1)}, bf16[192,512]{1,0:T(8,128)(2,1)S(1)}, u32[]{:S(2)}, u32[]{:S(2)}) collective-permute-start(bf16[192,512]{1,0:T(8,128)(2,1)S(1)} %get-tuple-element.130), channel_id=1, source_target_pairs={{2,0},{4,6},{3,1},{5,7},{10,8},{12,14},{11,9},{13,15},{18,16},{20,... | collective-permute-start | bytes 589832 | tf_op jit(solution)/shard_map/ppermute | solution.py:356
  173.0 8.9 %collective-permute-start.25 = (bf16[192,512]{1,0:T(8,128)(2,1)S(1)}, bf16[192,512]{1,0:T(8,128)(2,1)S(1)}, u32[]{:S(2)}, u32[]{:S(2)}) collective-permute-start(bf16[192,512]{1,0:T(8,128)(2,1)S(1)} %get-tuple-element.131), channel_id=1, source_target_pairs={{4,2},{2,4},{5,3},{3,5},{12,10},{10,12},{13,11},{11,13},{20,18},{1... | collective-permute-start | bytes 589832 | tf_op jit(solution)/shard_map/ppermute | solution.py:359
  173.7 13.0 %collective-permute-start.26 = (bf16[192,512]{1,0:T(8,128)(2,1)S(1)}, bf16[192,512]{1,0:T(8,128)(2,1)S(1)}, u32[]{:S(2)}, u32[]{:S(2)}) collective-permute-start(bf16[192,512]{1,0:T(8,128)(2,1)S(1)} %get-tuple-element.132), channel_id=1, source_target_pairs={{4,0},{2,6},{5,1},{3,7},{12,8},{10,14},{13,9},{11,15},{20,16},{18,... | collective-permute-start | bytes 589832 | tf_op jit(solution)/shard_map/ppermute | solution.py:362
  186.7 2.9 %collective-permute-start.28 = (bf16[2,48,2048]{2,1,0:T(8,128)(2,1)S(1)}, bf16[2,48,2048]{2,1,0:T(8,128)(2,1)S(1)}, u32[]{:S(2)}, u32[]{:S(2)}) collective-permute-start(bf16[2,48,2048]{2,1,0:T(8,128)(2,1)S(1)} %get-tuple-element.135), channel_id=1, source_target_pairs={{0,1},{1,0},{2,3},{3,2},{4,5},{5,4},{6,7},{7,6},{8,9},{9,8},{10,11... | collective-permute-start | bytes 1179656 | tf_op jit(solution)/shard_map/ppermute | solution.py:367
  189.9 8.0 %collective-permute-start.29 = (bf16[48,2048]{1,0:T(8,128)(2,1)S(1)}, bf16[48,2048]{1,0:T(8,128)(2,1)S(1)}, u32[]{:S(2)}, u32[]{:S(2)}) collective-permute-start(bf16[48,2048]{1,0:T(8,128)(2,1)S(1)} %slice_bitcast_fusion.2), channel_id=1, source_target_pairs={{2,0},{4,6},{3,1},{5,7},{10,8},{12,14},{11,9},{13,15},{18,16},{20,... | collective-permute-start | bytes 589832 | tf_op jit(solution)/shard_map/ppermute | solution.py:356
  (26 other events, 233.5 us)

commit v8 on v7

--- a/solution.py
+++ b/solution.py
@@ -170,22 +170,39 @@
     held, (grad_normed, part, sems) = rest[2 : 2 + count], rest[2 + count :]
     ups, gate, vqk, slope, mixed, probs, factor, x_own, x_theirs = held[:9]
     out_parts, in_parts = held[9 : 9 + n], held[9 + n :]
+    wide = 4 * HEAD_DIM
+    heads = out_parts[0].shape[0] // HEAD_DIM
     copies = []
-    for i, (source, target) in enumerate(zip(sources, held)):
+    for i, (source, target) in enumerate(zip(sources[: 9 + n], held[: 9 + n])):
         if 1 <= i < 9:
             source = source.at[tick]
         copies.append(pltpu.make_async_copy(source, target, sems.at[i]))
+    by_head = []
+    for h in range(heads):
+        of_head = slice(h * wide, (h + 1) * wide)
+        by_head.append(
+            [
+                pltpu.make_async_copy(
+                    sources[9 + n + j].at[:, of_head],
+                    in_parts[j].at[:, of_head],
+                    sems.at[9 + n + h * parts + j],
+                )
+                for j in range(parts)
+            ]
+        )
     first = [0] + list(range(9, 9 + n))
     second = [1, 4, 2, 5, 6, 3]
-    last = list(range(9 + n, count))
-    for i in first + second + last + [7, 8]:
+    for i in first + second:
+        copies[i].start()
+    for of_head in by_head:
+        for copy in of_head:
+            copy.start()
+    for i in (7, 8):
         copies[i].start()
     for i in first:
         copies[i].wait()
     depth = out_parts[0].shape[1]
     length = x_own.shape[0]
-    wide = 4 * HEAD_DIM
-    heads = out_parts[0].shape[0] // HEAD_DIM
     grad_gated = None
     for j in range(n):
         columns = pl.ds(pl.multiple_of(offs[j], depth), depth)
@@ -194,8 +211,8 @@
     grad_gated = grad_gated.astype(BF16).astype(F32)
     for i in second:
         copies[i].wait()
-    grads_pre = []
-    for h in range(heads):
+
+    def through_head(h):
         cut = slice(h * HEAD_DIM, (h + 1) * HEAD_DIM)
         up = grad_gated[:, cut]
         mixed_h = mixed[:, cut]
@@ -214,13 +231,22 @@
         grad_query = dot(grad_scores, key)
         grad_key = dot_tn(grad_scores, query)
         grad_active = jnp.concatenate([grad_gate, grad_value, grad_query, grad_key], axis=1)
-        grads_pre.append((grad_active * slope[:, h * wide : (h + 1) * wide]).astype(BF16))
-    grad_pre = jnp.concatenate(grads_pre, axis=1)
-    for j in range(parts):
-        rows_of = in_parts[j].shape[0]
-        columns = pl.ds(pl.multiple_of(in_offs[j], rows_of), rows_of)
-        copies[last[j]].wait()
-        grad_normed[:, columns] = dot_nt(grad_pre, in_parts[j][...])
+        return (grad_active * slope[:, h * wide : (h + 1) * wide]).astype(BF16)
+
+    grad_pre = through_head(0)
+    for h in range(heads):
+        for copy in by_head[h]:
+            copy.wait()
+        following = through_head(h + 1) if h + 1 < heads else None
+        for j in range(parts):
+            rows_of = in_parts[j].shape[0]
+            columns = pl.ds(pl.multiple_of(in_offs[j], rows_of), rows_of)
+            term = dot_nt(grad_pre, in_parts[j][:, h * wide : (h + 1) * wide])
+            if h == 0:
+                grad_normed[:, columns] = term
+            else:
+                grad_normed[:, columns] += term
+        grad_pre = following
     for i in (7, 8):
         copies[i].wait()
     for r, source in enumerate((x_own, x_theirs)):
@@ -428,7 +454,6 @@
     parts = len(in_parts)
     core = jnp.reshape(core_no, (1,)).astype(jnp.int32)
     first_flag = jnp.reshape(first_section, (1,)).astype(jnp.int32)
-    always = jnp.ones((1,), jnp.int32)
     host_flag = jnp.reshape(is_host, (1,)).astype(jnp.int32)
     last_flag = jnp.reshape(last_section, (1,)).astype(jnp.int32)
 
@@ -526,7 +551,7 @@
             + [
                 pltpu.VMEM((rows, width), F32),
                 pltpu.VMEM((rows, width), BF16),
-                pltpu.SemaphoreType.DMA((1 + len(layered) + len(plain),)),
+                pltpu.SemaphoreType.DMA((1 + len(layered) + n + heads * parts,)),
             ],
             compiler_params=params,
             cost_estimate=cost(2 * matmul, 2 * weight_bytes),
@@ -569,22 +594,13 @@
     ahead_in = along_sections(ahead_0, 1)
     packs_near = [to_partner(packs[0])] + [from_host(packs[m], m) for m in between]
     back_send, back_keep = backward(after(up_0, ahead_0), 0)
-    back_send, back_keep, ahead_in, packs_near = lax.optimization_barrier(
-        (back_send, back_keep, ahead_in, packs_near)
+    ahead_given = to_partner(ahead_0[1])
+    back_send, back_keep, ahead_in, packs_near, ahead_given = lax.optimization_barrier(
+        (back_send, back_keep, ahead_in, packs_near, ahead_given)
     )
     back_landed = swap_cores(back_send)
-    back_0, first_pair = pl.pallas_call(
-        settle_kernel,
-        grid=(1,),
-        in_specs=[smem] * 2
-        + all_of(up_own, up_theirs, back_keep, back_keep, back_landed, ahead_0),
-        out_specs=all_of(*halves),
-        out_shape=halves,
-        compiler_params=small,
-        name="settle",
-    )(core, always, up_own, up_theirs, back_keep, back_keep, back_landed, ahead_0)
+    back_0 = summed(own_rows(up_own, up_theirs), back_keep, back_landed)
     back_in = along_sections(back_0, -1)
-    first_pair = to_partner(first_pair)
 
     packs_beyond = [to_beyond(packs[n // 2 + m - 1], m) for m in between]
     ahead_their = swap_cores(ahead_in)
@@ -619,13 +635,21 @@
         *in_parts,
         *out_parts,
     )
-    ahead_send, ahead_keep, back_in, packs_beyond, first_pair = lax.optimization_barrier(
-        (ahead_send, ahead_keep, back_in, packs_beyond, first_pair)
+    ahead_send, ahead_keep, back_in, packs_beyond = lax.optimization_barrier(
+        (ahead_send, ahead_keep, back_in, packs_beyond)
     )
     new_rows = own_rows(new_own, new_theirs)
-    ahead_1 = summed(
-        jnp.where(first_section, new_rows, ahead_in), ahead_keep, swap_cores(ahead_send)
-    )
+    ahead_landed = swap_cores(ahead_send)
+    ahead_1, pair = pl.pallas_call(
+        settle_kernel,
+        grid=(1,),
+        in_specs=[smem] * 2
+        + all_of(new_own, new_theirs, ahead_in, ahead_keep, ahead_landed, back_0),
+        out_specs=all_of(*halves),
+        out_shape=halves,
+        compiler_params=small,
+        name="settle",
+    )(core, first_flag, new_own, new_theirs, ahead_in, ahead_keep, ahead_landed, back_0)
 
     back_their = swap_cores(back_in)
     cut_shapes = [struct((rows, width), BF16)] + [struct((rows, depth), BF16)] * (n - 1)
@@ -641,9 +665,9 @@
     landed = [to_partner(cuts[0])] + [from_host(cuts[m], m) for m in between]
     landed += [to_beyond(cuts[n // 2 + m - 1], m) for m in between]
     back_send, back_keep = backward(up_1, 1)
-    ahead_given = to_partner(ahead_1[1])
-    back_send, back_keep, landed, ahead_given = lax.optimization_barrier(
-        (back_send, back_keep, landed, ahead_given)
+    pair = to_partner(pair)
+    back_send, back_keep, landed, pair = lax.optimization_barrier(
+        (back_send, back_keep, landed, pair)
     )
     back_1 = summed(
         jnp.where(last_section, new_rows, back_in), back_keep, swap_cores(back_send)
@@ -662,15 +686,16 @@
         host_flag, offs, after(gated, back_1), up_0, up_1, *packs_near, *packs_beyond, *landed
     )
 
+    ahead_given, pair = lax.optimization_barrier((ahead_given, pair, back_1))[:2]
     ahead = jnp.stack(
         [
-            jnp.where(is_host, ahead_0[0], first_pair[0]),
-            jnp.where(is_host, ahead_1[0], ahead_given),
+            jnp.where(is_host, ahead_0[0], ahead_given),
+            jnp.where(is_host, ahead_1[0], pair[1]),
         ]
     )
     back = jnp.stack(
         [
-            jnp.where(is_host, back_0[0], first_pair[1]),
+            jnp.where(is_host, back_0[0], pair[0]),
             jnp.where(is_host, back_1[0], to_partner(back_1[1])),
         ]
     )

time: 201 us -> 203 us (level)
    ppermute x2, waiting for transfers between devices: 12.9 us -> 8.72 us  [to_beyond(): lax.ppermute(x, 'dp', [(hosts[k ^ m], hosts[k] ^ 1) for k in range(n // 2)])]
    unnamed x56 -> x64, local copies, waits for them, and re-layouts: 5.39 us -> 5.26 us
  transfers between devices with their start and end apart: 30 -> 30, of which waited for: 14 -> 12; matrix products, arithmetic and copies ran while one was open for 10% -> 10% of each run, Pallas kernels for 11% -> 11%
where the time goes in v8:
time: 203 us; the launch traced here: 200 us
  waiting for transfers between devices  92.2 us (45%)
  starting transfers between devices  53.4 us (26%)
  Pallas kernels  23.7 us (12%)
  other arithmetic  14.4 us (7%)
  local copies, waits for them, and re-layouts  13.4 us (7%)
  between operations  3.17 us (2%)
    ppermute x8, waiting for transfers between devices, from_partner(): return lax.ppermute(x, 'dp', [(h ^ 1, h) for h in hosts])  44.8 us
    ppermute x5, waiting for transfers between devices, to_partner(): return lax.ppermute(x, 'dp', [(h, h ^ 1) for h in hosts])  35.4 us
    ppermute x8, starting transfers between devices, from_partner(): return lax.ppermute(x, 'dp', [(h ^ 1, h) for h in hosts])  28.2 us
    ppermute x2, waiting for transfers between devices, to_beyond(): lax.ppermute(x, 'dp', [(hosts[k ^ m], hosts[k] ^ 1) for k in range(n // 2)])  8.72 us
    pallas_call x1, Pallas kernels, per_device(): pl.pallas_call(on_host(functools.partial(project_kernel, parts)), grid=(h...  7.25 us
    ppermute x7, starting transfers between devices, from_host(): lax.ppermute(x, 'dp', [(hosts[k ^ m], hosts[k]) for k in range(n // 2)])  7 us
    ppermute x5, starting transfers between devices, to_partner(): return lax.ppermute(x, 'dp', [(h, h ^ 1) for h in hosts])  6.57 us
    ppermute x6, starting transfers between devices, swap_cores(): return lax.ppermute(x, 'cores', [(c, cores - 1 - c) for c in range(cores)])  6 us
  transfers between devices with their start and end apart: 30, of which 12 were waited for; matrix products, arithmetic and copies ran while one was open for 10% of the time, Pallas kernels for 11%

profile of v8, /device:TPU:5, one launch (start us, length us, event | category | flops | bytes accessed | tf_op | source)
XLA Modules:
  0.0 200.2 jit_solution(2767965703432527512)
XLA Ops:
  1.6 3.2 %slice_bitcast_fusion = (bf16[256,2048]{1,0:T(8,128)(2,1)}, bf16[256,2048]{1,0:T(8,128)(2,1)}) fusion(bf16[1,512,2048]{2,1,0:T(8,128)(2,1)} %param.17), kind=kLoop, calls=%fused_computation | loop fusion | bytes 4194304 | tf_op jit(solution)/shard_map/slice | solution.py:412
  4.8 6.6 %collective-permute-start.1 = (bf16[256,2048]{1,0:T(8,128)(2,1)}, bf16[256,2048]{1,0:T(8,128)(2,1)}, u32[]{:S(2)}, u32[]{:S(2)}) collective-permute-start(bf16[256,2048]{1,0:T(8,128)(2,1)} %get-tuple-element.148), channel_id=1, source_target_pairs={{0,2},{6,4},{1,3},{7,5},{8,10},{14,12},{9,11},{15,13},{16,18},{22,... | collective-permute-start | bytes 3145736 | tf_op jit(solution)/shard_map/ppermute | solution.py:379
  11.3 2.3 %collective-permute-start.2 = (bf16[256,2048]{1,0:T(8,128)(2,1)}, bf16[256,2048]{1,0:T(8,128)(2,1)}, u32[]{:S(2)}, u32[]{:S(2)}) collective-permute-start(bf16[256,2048]{1,0:T(8,128)(2,1)} %get-tuple-element.147), channel_id=1, source_target_pairs={{0,2},{6,4},{1,3},{7,5},{8,10},{14,12},{9,11},{15,13},{16,18},{22,... | collective-permute-start | bytes 3145736 | tf_op jit(solution)/shard_map/ppermute | solution.py:379
  19.0 13.2 %collective-permute-done.1.refs_8_.refs_18_.refs_11_ = bf16[256,2048]{1,0:T(8,128)(2,1)} collective-permute-done((bf16[256,2048]{1,0:T(8,128)(2,1)}, bf16[256,2048]{1,0:T(8,128)(2,1)}, u32[]{:S(2)}, u32[]{:S(2)}) %collective-permute-start.1) | collective-permute-done | bytes 1048608 | tf_op jit(solution)/shard_map/ppermute | solution.py:379
  32.2 1.6 collective-permute-start.7
  33.8 20.8 %collective-permute-done.2.refs_9_.refs_19_.refs_12_ = bf16[256,2048]{1,0:T(8,128)(2,1)} collective-permute-done((bf16[256,2048]{1,0:T(8,128)(2,1)}, bf16[256,2048]{1,0:T(8,128)(2,1)}, u32[]{:S(2)}, u32[]{:S(2)}) %collective-permute-start.2) | collective-permute-done | bytes 1048608 | tf_op jit(solution)/shard_map/ppermute | solution.py:379
  59.8 4.1 %collective-permute-start.6 = (s32[2,5,17]{2,0,1:T(2,128)S(1)}, s32[2,5,17]{2,0,1:T(2,128)S(1)}, u32[]{:S(2)}, u32[]{:S(2)}) collective-permute-start(s32[2,5,17]{2,0,1:T(2,128)S(1)} %add_add_fusion), channel_id=1, source_target_pairs={{0,2},{6,4},{1,3},{7,5},{8,10},{14,12},{9,11},{15,13},{16,18},{22,... | collective-permute-start | bytes 2048 | tf_op jit(solution)/shard_map/ppermute | solution.py:379
  63.9 2.2 %collective-permute-start.4 = (bf16[2,96,2048]{2,1,0:T(8,128)(2,1)}, bf16[2,96,2048]{2,1,0:T(8,128)(2,1)}, u32[]{:S(2)}, u32[]{:S(2)}) collective-permute-start(bf16[2,96,2048]{2,1,0:T(8,128)(2,1)} %bitcast.99), channel_id=1, source_target_pairs={{0,2},{6,4},{1,3},{7,5},{8,10},{14,12},{9,11},{15,13},{16,18},{22,... | collective-permute-start | bytes 2359304 | tf_op jit(solution)/shard_map/ppermute | solution.py:379
  66.1 1.7 collective-permute-start.8
  67.8 2.4 %slice_select_fusion = (bf16[1,96,2048]{2,1,0:T(8,128)(2,1)S(1)}, bf16[1,96,2048]{2,1,0:T(8,128)(2,1)S(1)}, bf16[1,96,2048]{2,1,0:T(8,128)(2,1)}) fusion(bf16[2,96,2048]{2,1,0:T(8,128)(2,1)} %param.14, bf16[2,96,2048]{2,1,0:T(8,128)(2,1)} %param.12, pred[]{:T(512)S(6)} %eq.44, bf16[1,96,2048]{2,1,0:T(8,128)(2,1)S(1)} %copy-done.25, ...), kind=kLoop, calls=%fused_computation.20 | loop fusion | flops 589824 | bytes 3538946 | tf_op jit(solution)/shard_map/jit(_where)/select_n | solution.py:440
  70.2 2.1 %collective-permute-start.3 = (bf16[96,2048]{1,0:T(8,128)(2,1)S(1)}, bf16[96,2048]{1,0:T(8,128)(2,1)}, u32[]{:S(2)}, u32[]{:S(2)}) collective-permute-start(bf16[96,2048]{1,0:T(8,128)(2,1)S(1)} %bitcast.92), channel_id=1, source_target_pairs={{0,2},{6,4},{1,3},{7,5},{8,10},{14,12},{9,11},{15,13},{16,18},{22,... | collective-permute-start | bytes 1179656 | tf_op jit(solution)/shard_map/ppermute | solution.py:379
  74.3 7.7 %collective-permute-done.4.refs_4_.refs_11_ = bf16[2,96,2048]{2,1,0:T(8,128)(2,1)} collective-permute-done((bf16[2,96,2048]{2,1,0:T(8,128)(2,1)}, bf16[2,96,2048]{2,1,0:T(8,128)(2,1)}, u32[]{:S(2)}, u32[]{:S(2)}) %collective-permute-start.4) | collective-permute-done | bytes 786464 | tf_op jit(solution)/shard_map/ppermute | solution.py:379
  83.7 5.5 %collective-permute-start.9 = (bf16[96,2048]{1,0:T(8,128)(2,1)S(1)}, bf16[96,2048]{1,0:T(8,128)(2,1)S(1)}, u32[]{:S(2)}, u32[]{:S(2)}) collective-permute-start(bf16[96,2048]{1,0:T(8,128)(2,1)S(1)} %bitcast.80), channel_id=1, source_target_pairs={{0,2},{6,4},{1,3},{7,5},{8,10},{14,12},{9,11},{15,13},{16,18},{22,... | collective-permute-start | bytes 1179656 | tf_op jit(solution)/shard_map/ppermute | solution.py:379
  90.3 4.2 %collective-permute-start.10 = (bf16[96,2048]{1,0:T(8,128)(2,1)}, bf16[96,2048]{1,0:T(8,128)(2,1)S(1)}, u32[]{:S(2)}, u32[]{:S(2)}) collective-permute-start(bf16[96,2048]{1,0:T(8,128)(2,1)} %bitcast.14.up_own), channel_id=1, source_target_pairs={{0,2},{6,4},{1,3},{7,5},{8,10},{14,12},{9,11},{15,13},{16,18},{22,... | collective-permute-start | bytes 1179656 | tf_op jit(solution)/shard_map/ppermute | solution.py:379
  95.5 7.3 %project.1 = (bf16[3,192,512]{2,1,0:T(8,128)(2,1)S(1)}, f32[2,192,512]{2,1,0:T(8,128)S(1)}, bf16[2,192,1536]{2,1,0:T(8,128)(2,1)}, f32[2,192,2048]{2,1,0:T(8,128...) custom-call(s32[1]{0:T(128)} %bitcast.9.host, ...), custom_call_target="tpu_custom_call" | custom-call | flops 4831838208 | bytes 20971520 | tf_op jit(solution)/shard_map/project/pallas_call | solution.py:509
  104.6 2.0 %collective-permute-done.10.up_theirs = bf16[96,2048]{1,0:T(8,128)(2,1)S(1)} collective-permute-done((bf16[96,2048]{1,0:T(8,128)(2,1)}, bf16[96,2048]{1,0:T(8,128)(2,1)S(1)}, u32[]{:S(2)}, u32[]{:S(2)}) %collective-permute-start.10) | collective-permute-done | bytes 393248 | tf_op jit(solution)/shard_map/ppermute | solution.py:379
  106.6 2.0 %pack.1 = (bf16[192,2048]{1,0:T(8,128)(2,1)S(1)}, bf16[192,1536]{1,0:T(8,128)(2,1)S(1)}, bf16[192,1536]{1,0:T(8,128)(2,1)S(1)}, bf16[192,1536]{1,0:T(8,128)(2,1)}) custom-call(s32[4]{0:T(128)S(1)} %add_multiply_fusion.offs.refs_2_, bf16[3,192,512]{2,1,0:T(8,128)(2,1)S(1)} %get-tuple-element.140.gated, bf16[96,2048]{1,0:T(8,128)(2,1)} %bitcast.14.up_own, ...), custom_call_target="tpu_custom_call" | custom-call | tf_op jit(solution)/shard_map/pack/pallas_call | solution.py:571
  109.6 1.9 out.1
  112.2 3.6 %collective-permute-start.13 = (bf16[2,48,2048]{2,1,0:T(8,128)(2,1)}, bf16[2,48,2048]{2,1,0:T(8,128)(2,1)}, u32[]{:S(2)}, u32[]{:S(2)}) collective-permute-start(bf16[2,48,2048]{2,1,0:T(8,128)(2,1)} %get-tuple-element.103), channel_id=1, source_target_pairs={{0,1},{1,0},{2,3},{3,2},{4,5},{5,4},{6,7},{7,6},{8,9},{9,8},{10,11... | collective-permute-start | bytes 1179656 | tf_op jit(solution)/shard_map/ppermute | solution.py:393
  115.8 1.4 collective-permute-start.15
  119.3 1.4 collective-permute-start.14
  123.0 14.6 %collective-permute-done.15.rest_0_ = bf16[192,1536]{1,0:T(8,128)(2,1)S(1)} collective-permute-done((bf16[192,1536]{1,0:T(8,128)(2,1)}, bf16[192,1536]{1,0:T(8,128)(2,1)S(1)}, u32[]{:S(2)}, u32[]{:S(2)}) %collective-permute-start.15) | collective-permute-done | bytes 589856 | tf_op jit(solution)/shard_map/ppermute | solution.py:382
  137.7 4.2 %collective-permute-done.17 = bf16[48,2048]{1,0:T(8,128)(2,1)S(1)} collective-permute-done((bf16[48,2048]{1,0:T(8,128)(2,1)S(1)}, bf16[48,2048]{1,0:T(8,128)(2,1)S(1)}, u32[]{:S(2)}, u32[]{:S(2)}) %collective-permute-start.17) | collective-permute-done | bytes 196640 | tf_op jit(solution)/shard_map/ppermute | solution.py:382
  143.8 1.8 add_convert_fusion.1.earlier
  145.7 1.6 collective-permute-start.20
  147.3 4.5 %forward.1 = (bf16[2,48,2048]{2,1,0:T(8,128)(2,1)S(1)}, bf16[2,48,2048]{2,1,0:T(8,128)(2,1)S(1)}) custom-call(s32[1]{0:T(128)} %bitcast.9.host, s32[1]{0:T(128)} %bitcast.6.core.refs_0_, s32[6]{0:T(128)S(1)} %stack.92.refs_0_.refs_1_, s32[4]{0:T(128)S(1)} %add_multiply_fusion.offs.refs_2_, s32[1]{0:T(128)} %bitcast.37.refs_3_.fresh, ...), custom_call_target="tpu_custom_call" | custom-call | flops 3221225472 | bytes 20971520 | tf_op jit(solution)/shard_map/forward/pallas_call | solution.py:607
  151.8 8.7 %collective-permute-done.21.rest_2_ = bf16[192,1536]{1,0:T(8,128)(2,1)} collective-permute-done((bf16[192,1536]{1,0:T(8,128)(2,1)}, bf16[192,1536]{1,0:T(8,128)(2,1)}, u32[]{:S(2)}, u32[]{:S(2)}) %collective-permute-start.21) | collective-permute-done | bytes 589856 | tf_op jit(solution)/shard_map/ppermute | solution.py:388
  161.3 1.9 collective-permute-done.26.landed
  163.2 2.1 %settle.1 = (bf16[2,48,2048]{2,1,0:T(8,128)(2,1)S(1)}, bf16[2,48,2048]{2,1,0:T(8,128)(2,1)}) custom-call(s32[1]{0:T(128)} %bitcast.6.core.refs_0_, s32[1]{0:T(128)} %bitcast.37.refs_3_.fresh, bf16[96,2048]{1,0:T(8,128)(2,1)S(1)} %bitcast.82, bf16[96,2048]{1,0:T(8,128)(2,1)S(1)} %collective-permute-done.9.refs_7_.new_theirs.theirs, ...), custom_call_target="tpu_custom_call" | custom-call | tf_op jit(solution)/shard_map/settle/pallas_call | solution.py:643
  172.9 14.7 %collective-permute-done.23.rest_3_ = bf16[192,512]{1,0:T(8,128)(2,1)S(1)} collective-permute-done((bf16[192,512]{1,0:T(8,128)(2,1)S(1)}, bf16[192,512]{1,0:T(8,128)(2,1)S(1)}, u32[]{:S(2)}, u32[]{:S(2)}) %collective-permute-start.23) | collective-permute-done | bytes 196640 | tf_op jit(solution)/shard_map/ppermute | solution.py:382
  193.9 2.8 %grads.1 = f32[512,512]{1,0:T(8,128)} custom-call(s32[1]{0:T(128)} %bitcast.9.host, s32[4]{0:T(128)S(1)} %add_multiply_fusion.offs.refs_2_, bf16[3,192,512]{2,1,0:T(8,128)(2,1)S(1)} %get-tuple-element.140.gated, bf16[192,2048]{1,0:T(8,128)(2,1)S(1)} %copy-done.8, bf16[192,2048]{1,0:T(8,128)(2,1)S(1)} %get-tuple-element.125.refs_3_.up_1, ...), custom_call_target="tpu_custom_call" | custom-call | flops 402653184 | bytes 2621440 | tf_op jit(solution)/shard_map/grads/pallas_call | solution.py:676
  197.5 1.9 collective-permute-done.29
  (140 shorter events, 41.0 us)
Async XLA Ops:
  0.7 54.0 %copy-start.31 = (s32[1,5]{1,0:T(1,128)S(1)}, s32[1,5]{1,0:T(1,128)}, u32[]{:S(2)}) copy-start(s32[1,5]{1,0:T(1,128)} %param.19) | copy-start | bytes 64
  0.7 67.1 %copy-start.25 = (bf16[1,96,2048]{2,1,0:T(8,128)(2,1)S(1)}, bf16[1,96,2048]{2,1,0:T(8,128)(2,1)}, u32[]{:S(2)}) copy-start(bf16[1,96,2048]{2,1,0:T(8,128)(2,1)} %param.13) | copy-start | bytes 1179652
  0.7 54.0 %collective-permute-start = (bf16[512,2048]{1,0:T(8,128)(2,1)}, bf16[512,2048]{1,0:T(8,128)(2,1)S(1)}, u32[]{:S(2)}, u32[]{:S(2)}) collective-permute-start(bf16[512,2048]{1,0:T(8,128)(2,1)} %bitcast.94), channel_id=1, source_target_pairs={{4,2},{2,4},{5,3},{3,5},{12,10},{10,12},{13,11},{11,13},{20,18},{1... | collective-permute-start | bytes 6291464 | tf_op jit(solution)/shard_map/ppermute | solution.py:385
  4.8 27.4 %collective-permute-start.1 = (bf16[256,2048]{1,0:T(8,128)(2,1)}, bf16[256,2048]{1,0:T(8,128)(2,1)}, u32[]{:S(2)}, u32[]{:S(2)}) collective-permute-start(bf16[256,2048]{1,0:T(8,128)(2,1)} %get-tuple-element.148), channel_id=1, source_target_pairs={{0,2},{6,4},{1,3},{7,5},{8,10},{14,12},{9,11},{15,13},{16,18},{22,... | collective-permute-start | bytes 3145736 | tf_op jit(solution)/shard_map/ppermute | solution.py:379
  11.3 43.3 %collective-permute-start.2 = (bf16[256,2048]{1,0:T(8,128)(2,1)}, bf16[256,2048]{1,0:T(8,128)(2,1)}, u32[]{:S(2)}, u32[]{:S(2)}) collective-permute-start(bf16[256,2048]{1,0:T(8,128)(2,1)} %get-tuple-element.147), channel_id=1, source_target_pairs={{0,2},{6,4},{1,3},{7,5},{8,10},{14,12},{9,11},{15,13},{16,18},{22,... | collective-permute-start | bytes 3145736 | tf_op jit(solution)/shard_map/ppermute | solution.py:379
  13.6 56.6 %collective-permute-start.5 = (bf16[512,512]{1,0:T(8,128)(2,1)S(1)}, bf16[512,512]{1,0:T(8,128)(2,1)S(1)}, u32[]{:S(2)}, u32[]{:S(2)}) collective-permute-start(bf16[512,512]{1,0:T(8,128)(2,1)S(1)} %bitcast.84), channel_id=1, source_target_pairs={{0,2},{6,4},{1,3},{7,5},{8,10},{14,12},{9,11},{15,13},{16,18},{22,... | collective-permute-start | bytes 1572872 | tf_op jit(solution)/shard_map/ppermute | solution.py:379
  32.2 51.5 %collective-permute-start.7 = (bf16[256,2048]{1,0:T(8,128)(2,1)}, bf16[256,2048]{1,0:T(8,128)(2,1)}, u32[]{:S(2)}, u32[]{:S(2)}) collective-permute-start(bf16[256,2048]{1,0:T(8,128)(2,1)} %collective-permute-done.1.refs_8_.refs_18_.refs_11_), channel_id=1, source_target_pairs={{4,2},{2,4},{5,3},{3,5},{12,10},{10,12},{13,11},{11,13},{20,18},{1... | collective-permute-start | bytes 3145736 | tf_op jit(solution)/shard_map/ppermute | solution.py:385
  59.8 12.5 %collective-permute-start.6 = (s32[2,5,17]{2,0,1:T(2,128)S(1)}, s32[2,5,17]{2,0,1:T(2,128)S(1)}, u32[]{:S(2)}, u32[]{:S(2)}) collective-permute-start(s32[2,5,17]{2,0,1:T(2,128)S(1)} %add_add_fusion), channel_id=1, source_target_pairs={{0,2},{6,4},{1,3},{7,5},{8,10},{14,12},{9,11},{15,13},{16,18},{22,... | collective-permute-start | bytes 2048 | tf_op jit(solution)/shard_map/ppermute | solution.py:379
  63.9 18.0 %collective-permute-start.4 = (bf16[2,96,2048]{2,1,0:T(8,128)(2,1)}, bf16[2,96,2048]{2,1,0:T(8,128)(2,1)}, u32[]{:S(2)}, u32[]{:S(2)}) collective-permute-start(bf16[2,96,2048]{2,1,0:T(8,128)(2,1)} %bitcast.99), channel_id=1, source_target_pairs={{0,2},{6,4},{1,3},{7,5},{8,10},{14,12},{9,11},{15,13},{16,18},{22,... | collective-permute-start | bytes 2359304 | tf_op jit(solution)/shard_map/ppermute | solution.py:379
  66.1 28.4 %collective-permute-start.8 = (bf16[256,2048]{1,0:T(8,128)(2,1)}, bf16[256,2048]{1,0:T(8,128)(2,1)}, u32[]{:S(2)}, u32[]{:S(2)}) collective-permute-start(bf16[256,2048]{1,0:T(8,128)(2,1)} %collective-permute-done.2.refs_9_.refs_19_.refs_12_), channel_id=1, source_target_pairs={{4,2},{2,4},{5,3},{3,5},{12,10},{10,12},{13,11},{11,13},{20,18},{1... | collective-permute-start | bytes 3145736 | tf_op jit(solution)/shard_map/ppermute | solution.py:385
  70.2 20.0 %collective-permute-start.3 = (bf16[96,2048]{1,0:T(8,128)(2,1)S(1)}, bf16[96,2048]{1,0:T(8,128)(2,1)}, u32[]{:S(2)}, u32[]{:S(2)}) collective-permute-start(bf16[96,2048]{1,0:T(8,128)(2,1)S(1)} %bitcast.92), channel_id=1, source_target_pairs={{0,2},{6,4},{1,3},{7,5},{8,10},{14,12},{9,11},{15,13},{16,18},{22,... | collective-permute-start | bytes 1179656 | tf_op jit(solution)/shard_map/ppermute | solution.py:379
  73.3 36.3 %collective-permute-start.11 = (bf16[512,512]{1,0:T(8,128)(2,1)S(1)}, bf16[512,512]{1,0:T(8,128)(2,1)S(1)}, u32[]{:S(2)}, u32[]{:S(2)}) collective-permute-start(bf16[512,512]{1,0:T(8,128)(2,1)S(1)} %bitcast.85), channel_id=1, source_target_pairs={{4,2},{2,4},{5,3},{3,5},{12,10},{10,12},{13,11},{11,13},{20,18},{1... | collective-permute-start | bytes 1572872 | tf_op jit(solution)/shard_map/ppermute | solution.py:385
  81.9 27.6 %collective-permute-start.12 = (bf16[512,512]{1,0:T(8,128)(2,1)S(1)}, bf16[512,512]{1,0:T(8,128)(2,1)S(1)}, u32[]{:S(2)}, u32[]{:S(2)}) collective-permute-start(bf16[512,512]{1,0:T(8,128)(2,1)S(1)} %collective-permute-done.5.rest_1_.refs_13_.refs_16_), channel_id=1, source_target_pairs={{4,2},{2,4},{5,3},{3,5},{12,10},{10,12},{13,11},{11,13},{20,18},{1... | collective-permute-start | bytes 1572872 | tf_op jit(solution)/shard_map/ppermute | solution.py:385
  83.7 20.9 %collective-permute-start.9 = (bf16[96,2048]{1,0:T(8,128)(2,1)S(1)}, bf16[96,2048]{1,0:T(8,128)(2,1)S(1)}, u32[]{:S(2)}, u32[]{:S(2)}) collective-permute-start(bf16[96,2048]{1,0:T(8,128)(2,1)S(1)} %bitcast.80), channel_id=1, source_target_pairs={{0,2},{6,4},{1,3},{7,5},{8,10},{14,12},{9,11},{15,13},{16,18},{22,... | collective-permute-start | bytes 1179656 | tf_op jit(solution)/shard_map/ppermute | solution.py:379
  90.3 16.4 %collective-permute-start.10 = (bf16[96,2048]{1,0:T(8,128)(2,1)}, bf16[96,2048]{1,0:T(8,128)(2,1)S(1)}, u32[]{:S(2)}, u32[]{:S(2)}) collective-permute-start(bf16[96,2048]{1,0:T(8,128)(2,1)} %bitcast.14.up_own), channel_id=1, source_target_pairs={{0,2},{6,4},{1,3},{7,5},{8,10},{14,12},{9,11},{15,13},{16,18},{22,... | collective-permute-start | bytes 1179656 | tf_op jit(solution)/shard_map/ppermute | solution.py:379
  112.2 5.7 %collective-permute-start.13 = (bf16[2,48,2048]{2,1,0:T(8,128)(2,1)}, bf16[2,48,2048]{2,1,0:T(8,128)(2,1)}, u32[]{:S(2)}, u32[]{:S(2)}) collective-permute-start(bf16[2,48,2048]{2,1,0:T(8,128)(2,1)} %get-tuple-element.103), channel_id=1, source_target_pairs={{0,1},{1,0},{2,3},{3,2},{4,5},{5,4},{6,7},{7,6},{8,9},{9,8},{10,11... | collective-permute-start | bytes 1179656 | tf_op jit(solution)/shard_map/ppermute | solution.py:393
  115.8 21.8 %collective-permute-start.15 = (bf16[192,1536]{1,0:T(8,128)(2,1)}, bf16[192,1536]{1,0:T(8,128)(2,1)S(1)}, u32[]{:S(2)}, u32[]{:S(2)}) collective-permute-start(bf16[192,1536]{1,0:T(8,128)(2,1)} %copy-done.21), channel_id=1, source_target_pairs={{2,0},{4,6},{3,1},{5,7},{10,8},{12,14},{11,9},{13,15},{18,16},{20,... | collective-permute-start | bytes 1769480 | tf_op jit(solution)/shard_map/ppermute | solution.py:382
  117.2 20.4 %collective-permute-start.16 = (bf16[192,1536]{1,0:T(8,128)(2,1)}, bf16[192,1536]{1,0:T(8,128)(2,1)S(1)}, u32[]{:S(2)}, u32[]{:S(2)}) collective-permute-start(bf16[192,1536]{1,0:T(8,128)(2,1)} %copy-done.20), channel_id=1, source_target_pairs={{4,2},{2,4},{5,3},{3,5},{12,10},{10,12},{13,11},{11,13},{20,18},{1... | collective-permute-start | bytes 1769480 | tf_op jit(solution)/shard_map/ppermute | solution.py:385
  119.3 22.5 %collective-permute-start.14 = (bf16[2,48,2048]{2,1,0:T(8,128)(2,1)S(1)}, bf16[2,48,2048]{2,1,0:T(8,128)(2,1)}, u32[]{:S(2)}, u32[]{:S(2)}) collective-permute-start(bf16[2,48,2048]{2,1,0:T(8,128)(2,1)S(1)} %add_convert_fusion.2), channel_id=1, source_target_pairs={{2,10},{4,12},{10,18},{12,20},{18,26},{20,28},{3,11},{5,13},{11,19... | collective-permute-start | bytes 1179656 | tf_op jit(solution)/shard_map/ppermute | solution.py:402
  120.8 21.1 %collective-permute-start.17 = (bf16[48,2048]{1,0:T(8,128)(2,1)S(1)}, bf16[48,2048]{1,0:T(8,128)(2,1)S(1)}, u32[]{:S(2)}, u32[]{:S(2)}) collective-permute-start(bf16[48,2048]{1,0:T(8,128)(2,1)S(1)} %slice_bitcast_fusion.4), channel_id=1, source_target_pairs={{2,0},{4,6},{3,1},{5,7},{10,8},{12,14},{11,9},{13,15},{18,16},{20,... | collective-permute-start | bytes 589832 | tf_op jit(solution)/shard_map/ppermute | solution.py:382
  141.9 2.0 collective-permute-start.19
  142.5 18.0 %collective-permute-start.21 = (bf16[192,1536]{1,0:T(8,128)(2,1)}, bf16[192,1536]{1,0:T(8,128)(2,1)}, u32[]{:S(2)}, u32[]{:S(2)}) collective-permute-start(bf16[192,1536]{1,0:T(8,128)(2,1)} %get-tuple-element.123), channel_id=1, source_target_pairs={{4,0},{2,6},{5,1},{3,7},{12,8},{10,14},{13,9},{11,15},{20,16},{18,... | collective-permute-start | bytes 1769480 | tf_op jit(solution)/shard_map/ppermute | solution.py:388
  143.7 3.6 %collective-permute-start.18 = (bf16[2,48,2048]{2,1,0:T(8,128)(2,1)}, bf16[2,48,2048]{2,1,0:T(8,128)(2,1)S(1)}, u32[]{:S(2)}, u32[]{:S(2)}) collective-permute-start(bf16[2,48,2048]{2,1,0:T(8,128)(2,1)} %collective-permute-done.14.refs_4_.passed), channel_id=1, source_target_pairs={{0,1},{1,0},{2,3},{3,2},{4,5},{5,4},{6,7},{7,6},{8,9},{9,8},{10,11... | collective-permute-start | bytes 1179656 | tf_op jit(solution)/shard_map/ppermute | solution.py:393
  145.7 14.8 %collective-permute-start.20 = (bf16[2,48,2048]{2,1,0:T(8,128)(2,1)}, bf16[2,48,2048]{2,1,0:T(8,128)(2,1)}, u32[]{:S(2)}, u32[]{:S(2)}) collective-permute-start(bf16[2,48,2048]{2,1,0:T(8,128)(2,1)} %add_convert_fusion.1.earlier), channel_id=1, source_target_pairs={{10,2},{12,4},{18,10},{20,12},{26,18},{28,20},{11,3},{13,5},{19,11... | collective-permute-start | bytes 1179656 | tf_op jit(solution)/shard_map/ppermute | solution.py:402
  160.5 2.7 %collective-permute-start.26 = (bf16[2,48,2048]{2,1,0:T(8,128)(2,1)S(1)}, bf16[2,48,2048]{2,1,0:T(8,128)(2,1)S(1)}, u32[]{:S(2)}, u32[]{:S(2)}) collective-permute-start(bf16[2,48,2048]{2,1,0:T(8,128)(2,1)S(1)} %get-tuple-element.132), channel_id=1, source_target_pairs={{0,1},{1,0},{2,3},{3,2},{4,5},{5,4},{6,7},{7,6},{8,9},{9,8},{10,11... | collective-permute-start | bytes 1179656 | tf_op jit(solution)/shard_map/ppermute | solution.py:393
  161.3 6.1 %collective-permute-start.22 = (bf16[2,48,2048]{2,1,0:T(8,128)(2,1)}, bf16[2,48,2048]{2,1,0:T(8,128)(2,1)}, u32[]{:S(2)}, u32[]{:S(2)}) collective-permute-start(bf16[2,48,2048]{2,1,0:T(8,128)(2,1)} %collective-permute-done.20.mine), channel_id=1, source_target_pairs={{0,1},{1,0},{2,3},{3,2},{4,5},{5,4},{6,7},{7,6},{8,9},{9,8},{10,11... | collective-permute-start | bytes 1179656 | tf_op jit(solution)/shard_map/ppermute | solution.py:393
  166.1 21.5 %collective-permute-start.27 = (bf16[2,48,2048]{2,1,0:T(8,128)(2,1)}, bf16[2,48,2048]{2,1,0:T(8,128)(2,1)}, u32[]{:S(2)}, u32[]{:S(2)}) collective-permute-start(bf16[2,48,2048]{2,1,0:T(8,128)(2,1)} %get-tuple-element.133), channel_id=1, source_target_pairs={{2,0},{4,6},{3,1},{5,7},{10,8},{12,14},{11,9},{13,15},{18,16},{20,... | collective-permute-start | bytes 1179656 | tf_op jit(solution)/shard_map/ppermute | solution.py:382
  168.6 18.9 %collective-permute-start.23 = (bf16[192,512]{1,0:T(8,128)(2,1)S(1)}, bf16[192,512]{1,0:T(8,128)(2,1)S(1)}, u32[]{:S(2)}, u32[]{:S(2)}) collective-permute-start(bf16[192,512]{1,0:T(8,128)(2,1)S(1)} %get-tuple-element.128), channel_id=1, source_target_pairs={{2,0},{4,6},{3,1},{5,7},{10,8},{12,14},{11,9},{13,15},{18,16},{20,... | collective-permute-start | bytes 589832 | tf_op jit(solution)/shard_map/ppermute | solution.py:382
  169.9 17.6 %collective-permute-start.24 = (bf16[192,512]{1,0:T(8,128)(2,1)S(1)}, bf16[192,512]{1,0:T(8,128)(2,1)S(1)}, u32[]{:S(2)}, u32[]{:S(2)}) collective-permute-start(bf16[192,512]{1,0:T(8,128)(2,1)S(1)} %get-tuple-element.129), channel_id=1, source_target_pairs={{4,2},{2,4},{5,3},{3,5},{12,10},{10,12},{13,11},{11,13},{20,18},{1... | collective-permute-start | bytes 589832 | tf_op jit(solution)/shard_map/ppermute | solution.py:385
  170.6 17.0 %collective-permute-start.25 = (bf16[192,512]{1,0:T(8,128)(2,1)S(1)}, bf16[192,512]{1,0:T(8,128)(2,1)S(1)}, u32[]{:S(2)}, u32[]{:S(2)}) collective-permute-start(bf16[192,512]{1,0:T(8,128)(2,1)S(1)} %get-tuple-element.130), channel_id=1, source_target_pairs={{4,0},{2,6},{5,1},{3,7},{12,8},{10,14},{13,9},{11,15},{20,16},{18,... | collective-permute-start | bytes 589832 | tf_op jit(solution)/shard_map/ppermute | solution.py:388
  187.6 2.3 %collective-permute-start.28 = (bf16[2,48,2048]{2,1,0:T(8,128)(2,1)S(1)}, bf16[2,48,2048]{2,1,0:T(8,128)(2,1)S(1)}, u32[]{:S(2)}, u32[]{:S(2)}) collective-permute-start(bf16[2,48,2048]{2,1,0:T(8,128)(2,1)S(1)} %get-tuple-element.136), channel_id=1, source_target_pairs={{0,1},{1,0},{2,3},{3,2},{4,5},{5,4},{6,7},{7,6},{8,9},{9,8},{10,11... | collective-permute-start | bytes 1179656 | tf_op jit(solution)/shard_map/ppermute | solution.py:393
  191.3 8.0 %collective-permute-start.29 = (bf16[48,2048]{1,0:T(8,128)(2,1)S(1)}, bf16[48,2048]{1,0:T(8,128)(2,1)S(1)}, u32[]{:S(2)}, u32[]{:S(2)}) collective-permute-start(bf16[48,2048]{1,0:T(8,128)(2,1)S(1)} %slice_bitcast_fusion.2), channel_id=1, source_target_pairs={{2,0},{4,6},{3,1},{5,7},{10,8},{12,14},{11,9},{13,15},{18,16},{20,... | collective-permute-start | bytes 589832 | tf_op jit(solution)/shard_map/ppermute | solution.py:382
  (30 other events, 246.2 us)

commit v9 on v8

--- a/solution.py
+++ b/solution.py
@@ -262,7 +262,7 @@
 
 
 def pack_kernel(n, offs, gated, up_own, up_theirs, whole, *packs):
-    depth = packs[0].shape[1] - 2 * gated.shape[2]
+    depth = packs[-1].shape[1] - 2 * gated.shape[2]
     slab = gated.shape[2]
     length = up_own.shape[0]
     whole[:length, :] = up_own[...]
@@ -272,11 +272,12 @@
         columns = pl.ds(pl.multiple_of(offs[j], depth), depth)
         pack[:, :slab] = gated[1]
         pack[:, slab : 2 * slab] = gated[2]
-        pack[:length, 2 * slab :] = up_own[:, columns]
-        pack[length:, 2 * slab :] = up_theirs[:, columns]
-
-
-def settle_kernel(core, fresh, own, theirs, passed, keep, landed, earlier, total, pair):
+        if j > 1:
+            pack[:length, 2 * slab :] = up_own[:, columns]
+            pack[length:, 2 * slab :] = up_theirs[:, columns]
+
+
+def settle_kernel(core, fresh, own, theirs, passed, keep, landed, total, other):
     share = keep.shape[1]
     here = pl.ds(pl.multiple_of(core[0] * share, share), share)
     for r, source in enumerate((own, theirs)):
@@ -284,8 +285,7 @@
         total[r] = (
             residual.astype(F32) + keep[r].astype(F32) + landed[r].astype(F32)
         ).astype(BF16)
-    pair[0] = earlier[1]
-    pair[1] = total[1]
+    other[...] = total[1]
 
 
 def gather_kernel(n, core, offs, fresh, mine, theirs, new_own, new_theirs, whole, *pieces):
@@ -296,7 +296,7 @@
         pieces[j - 1][...] = whole[:, columns]
 
 
-def grads_kernel(n, scaling, host, offs, gated, up_0, up_1, *rest):
+def grads_kernel(n, scaling, host, offs, gated, up_0, up_1, up_own, up_near, *rest):
     packs = rest[: n - 1]
     pieces = rest[n - 1 : 2 * n - 2]
     out = rest[2 * n - 2]
@@ -308,10 +308,11 @@
     def product(first, second, third, fourth):
         return dot_tn(first, third) + dot_tn(second, fourth)
 
+    up_pair = jnp.concatenate([up_near[...], up_own[:, columns]], axis=0)
     total = product(
         jnp.where(at_host, gated[1], packs[0][:, :slab]),
         jnp.where(at_host, gated[2], packs[0][:, slab : 2 * slab]),
-        jnp.where(at_host, up_0[:, columns], packs[0][:, 2 * slab :]),
+        jnp.where(at_host, up_0[:, columns], up_pair),
         jnp.where(at_host, up_1[:, columns], pieces[0][...]),
     )
     for m in range(1, n // 2):
@@ -443,6 +444,9 @@
     out_parts = [out_shard, out_near] + out_far + [from_host(out_near, m) for m in between]
     up_late, new_late, stash_theirs = lax.optimization_barrier((up_own, new_own, stash_theirs))
     up_theirs = from_partner(up_late)
+    up_near = to_partner(
+        lax.dynamic_slice_in_dim(up_late, (dp_no ^ 1) * depth, depth, axis=1)
+    )
     new_theirs = from_partner(new_late)
     far_hosts = [host_table[(dp_no // 2) ^ m] for m in between]
     owners = [dp_no, dp_no ^ 1] + far_hosts + [h ^ 1 for h in far_hosts]
@@ -558,7 +562,7 @@
             name="backward",
         )(host_flag, core, in_offs, offs, ups, *layered, *plain)
 
-    gated, new_theirs = lax.optimization_barrier((gated, new_theirs))
+    gated, new_theirs, up_near = lax.optimization_barrier((gated, new_theirs, up_near))
 
     def summed(residual, mine, landed):
         return (residual.astype(F32) + mine.astype(F32) + landed.astype(F32)).astype(BF16)
@@ -567,7 +571,8 @@
         return lax.dynamic_slice_in_dim(jnp.stack([mine, others]), core_no * share, share, axis=1)
 
     pack_shapes = [struct((rows, width), BF16)]
-    pack_shapes += [struct((rows, 2 * slab + depth), BF16)] * (n - 1)
+    pack_shapes += [struct((rows, 2 * slab), BF16)]
+    pack_shapes += [struct((rows, 2 * slab + depth), BF16)] * (n - 2)
     up_0, *packs = pl.pallas_call(
         functools.partial(pack_kernel, n),
         grid=(1,),
@@ -635,21 +640,23 @@
         *in_parts,
         *out_parts,
     )
-    ahead_send, ahead_keep, back_in, packs_beyond = lax.optimization_barrier(
-        (ahead_send, ahead_keep, back_in, packs_beyond)
-    )
     new_rows = own_rows(new_own, new_theirs)
     ahead_landed = swap_cores(ahead_send)
-    ahead_1, pair = pl.pallas_call(
+    settled = [halves[0], struct((share, width), BF16)]
+    ahead_1, ahead_other = pl.pallas_call(
         settle_kernel,
         grid=(1,),
         in_specs=[smem] * 2
-        + all_of(new_own, new_theirs, ahead_in, ahead_keep, ahead_landed, back_0),
-        out_specs=all_of(*halves),
-        out_shape=halves,
+        + all_of(new_own, new_theirs, ahead_in, ahead_keep, ahead_landed),
+        out_specs=all_of(*settled),
+        out_shape=settled,
         compiler_params=small,
         name="settle",
-    )(core, first_flag, new_own, new_theirs, ahead_in, ahead_keep, ahead_landed, back_0)
+    )(core, first_flag, new_own, new_theirs, ahead_in, ahead_keep, ahead_landed)
+    back_given = to_partner(back_0[1])
+    ahead_1, ahead_other, back_in, packs_beyond, back_given = lax.optimization_barrier(
+        (ahead_1, ahead_other, back_in, packs_beyond, back_given)
+    )
 
     back_their = swap_cores(back_in)
     cut_shapes = [struct((rows, width), BF16)] + [struct((rows, depth), BF16)] * (n - 1)
@@ -665,9 +672,9 @@
     landed = [to_partner(cuts[0])] + [from_host(cuts[m], m) for m in between]
     landed += [to_beyond(cuts[n // 2 + m - 1], m) for m in between]
     back_send, back_keep = backward(up_1, 1)
-    pair = to_partner(pair)
-    back_send, back_keep, landed, pair = lax.optimization_barrier(
-        (back_send, back_keep, landed, pair)
+    ahead_last = to_partner(ahead_other)
+    back_send, back_keep, landed, ahead_last = lax.optimization_barrier(
+        (back_send, back_keep, landed, ahead_last)
     )
     back_1 = summed(
         jnp.where(last_section, new_rows, back_in), back_keep, swap_cores(back_send)
@@ -676,26 +683,30 @@
     grads = pl.pallas_call(
         functools.partial(grads_kernel, n, (ticks * length * n) ** (-0.5)),
         grid=(1,),
-        in_specs=[smem] * 2 + all_of(gated, up_0, up_1, *packs_near, *packs_beyond, *landed),
+        in_specs=[smem] * 2 + all_of(
+            gated, up_0, up_1, up_own, up_near, *packs_near, *packs_beyond, *landed
+        ),
         out_specs=pl.BlockSpec((slab, depth), lambda *_: (0, 0)),
         out_shape=struct((slab, depth), F32),
         compiler_params=small,
         cost_estimate=cost(matmul // 4, weight_bytes // 4),
         name="grads",
     )(
-        host_flag, offs, after(gated, back_1), up_0, up_1, *packs_near, *packs_beyond, *landed
-    )
-
-    ahead_given, pair = lax.optimization_barrier((ahead_given, pair, back_1))[:2]
+        host_flag, offs, after(gated, back_1), up_0, up_1, up_own, up_near, *packs_near, *packs_beyond, *landed
+    )
+
+    ahead_given, back_given, ahead_last = lax.optimization_barrier(
+        (ahead_given, back_given, ahead_last, back_1)
+    )[:3]
     ahead = jnp.stack(
         [
             jnp.where(is_host, ahead_0[0], ahead_given),
-            jnp.where(is_host, ahead_1[0], pair[1]),
+            jnp.where(is_host, ahead_1[0], ahead_last),
         ]
     )
     back = jnp.stack(
         [
-            jnp.where(is_host, back_0[0], pair[0]),
+            jnp.where(is_host, back_0[0], back_given),
             jnp.where(is_host, back_1[0], to_partner(back_1[1])),
         ]
     )

time: 203 us -> 202 us (level)
  starting transfers between devices: 53.4 us -> 59.8 us
  waiting for transfers between devices: 92.2 us -> 88.4 us
  other arithmetic: 14.4 us -> 11.2 us
  local copies, waits for them, and re-layouts: 13.4 us -> 15.8 us
    ppermute x5 -> x7, waiting for transfers between devices: 35.4 us -> 25.7 us  [to_partner(): return lax.ppermute(x, 'dp', [(h, h ^ 1) for h in hosts])]
    unnamed x64 -> x88, local copies, waits for them, and re-layouts: 5.26 us -> 10.9 us
    ppermute x2, waiting for transfers between devices: 8.72 us -> 13.6 us  [to_beyond(): lax.ppermute(x, 'dp', [(hosts[k ^ m], hosts[k] ^ 1) for k in range(n // 2)])]
    ppermute x8, starting transfers between devices: 28.2 us -> 32.1 us  [from_partner(): return lax.ppermute(x, 'dp', [(h ^ 1, h) for h in hosts])]
    reshape x2, local copies, waits for them, and re-layouts: 2.73 us -> 0.16 us  [per_device(): m.reshape(m.shape[:2] + (-1,))]
    ppermute x5 -> x7, starting transfers between devices: 6.57 us -> 9.14 us  [to_partner(): return lax.ppermute(x, 'dp', [(h, h ^ 1) for h in hosts])]
    ppermute x8, waiting for transfers between devices: 44.8 us -> 47.3 us  [from_partner(): return lax.ppermute(x, 'dp', [(h ^ 1, h) for h in hosts])]
  transfers between devices with their start and end apart: 30 -> 32, of which waited for: 12 -> 16; matrix products, arithmetic and copies ran while one was open for 10% -> 7% of each run, Pallas kernels for 11% -> 10%
where the time goes in v9:
time: 202 us; the launch traced here: 200 us
  waiting for transfers between devices  88.4 us (44%)
  starting transfers between devices  59.8 us (30%)
  Pallas kernels  21.7 us (11%)
  local copies, waits for them, and re-layouts  15.8 us (8%)
  other arithmetic  11.2 us (6%)
  between operations  3.34 us (2%)
    ppermute x8, waiting for transfers between devices, from_partner(): return lax.ppermute(x, 'dp', [(h ^ 1, h) for h in hosts])  47.3 us
    ppermute x8, starting transfers between devices, from_partner(): return lax.ppermute(x, 'dp', [(h ^ 1, h) for h in hosts])  32.1 us
    ppermute x7, waiting for transfers between devices, to_partner(): return lax.ppermute(x, 'dp', [(h, h ^ 1) for h in hosts])  25.7 us
    ppermute x2, waiting for transfers between devices, to_beyond(): lax.ppermute(x, 'dp', [(hosts[k ^ m], hosts[k] ^ 1) for k in range(n // 2)])  13.6 us
    unnamed x88, local copies, waits for them, and re-layouts  10.9 us
    ppermute x7, starting transfers between devices, to_partner(): return lax.ppermute(x, 'dp', [(h, h ^ 1) for h in hosts])  9.14 us
    pallas_call x1, Pallas kernels, per_device(): pl.pallas_call(on_host(functools.partial(project_kernel, parts)), grid=(h...  7.32 us
    ppermute x7, starting transfers between devices, from_host(): lax.ppermute(x, 'dp', [(hosts[k ^ m], hosts[k]) for k in range(n // 2)])  7 us
  transfers between devices with their start and end apart: 32, of which 16 were waited for; matrix products, arithmetic and copies ran while one was open for 7% of the time, Pallas kernels for 10%

profile of v9, /device:TPU:5, one launch (start us, length us, event | category | flops | bytes accessed | tf_op | source)
XLA Modules:
  0.0 200.2 jit_solution(11251430886447940)
XLA Ops:
  1.6 3.1 %slice_bitcast_fusion = (bf16[256,2048]{1,0:T(8,128)(2,1)}, bf16[256,2048]{1,0:T(8,128)(2,1)}) fusion(bf16[1,512,2048]{2,1,0:T(8,128)(2,1)} %param.17), kind=kLoop, calls=%fused_computation | loop fusion | bytes 4194304 | tf_op jit(solution)/shard_map/slice | solution.py:413
  4.7 6.6 %collective-permute-start.1 = (bf16[256,2048]{1,0:T(8,128)(2,1)}, bf16[256,2048]{1,0:T(8,128)(2,1)}, u32[]{:S(2)}, u32[]{:S(2)}) collective-permute-start(bf16[256,2048]{1,0:T(8,128)(2,1)} %get-tuple-element.154), channel_id=1, source_target_pairs={{0,2},{6,4},{1,3},{7,5},{8,10},{14,12},{9,11},{15,13},{16,18},{22,... | collective-permute-start | bytes 3145736 | tf_op jit(solution)/shard_map/ppermute | solution.py:380
  11.3 2.3 %collective-permute-start.2 = (bf16[256,2048]{1,0:T(8,128)(2,1)}, bf16[256,2048]{1,0:T(8,128)(2,1)}, u32[]{:S(2)}, u32[]{:S(2)}) collective-permute-start(bf16[256,2048]{1,0:T(8,128)(2,1)} %get-tuple-element.153), channel_id=1, source_target_pairs={{0,2},{6,4},{1,3},{7,5},{8,10},{14,12},{9,11},{15,13},{16,18},{22,... | collective-permute-start | bytes 3145736 | tf_op jit(solution)/shard_map/ppermute | solution.py:380
  19.6 12.6 %collective-permute-done.1.refs_8_.refs_18_.refs_11_ = bf16[256,2048]{1,0:T(8,128)(2,1)} collective-permute-done((bf16[256,2048]{1,0:T(8,128)(2,1)}, bf16[256,2048]{1,0:T(8,128)(2,1)}, u32[]{:S(2)}, u32[]{:S(2)}) %collective-permute-start.1) | collective-permute-done | bytes 1048608 | tf_op jit(solution)/shard_map/ppermute | solution.py:380
  32.2 1.6 collective-permute-start.7
  33.8 20.8 %collective-permute-done.2.refs_9_.refs_19_.refs_12_ = bf16[256,2048]{1,0:T(8,128)(2,1)} collective-permute-done((bf16[256,2048]{1,0:T(8,128)(2,1)}, bf16[256,2048]{1,0:T(8,128)(2,1)}, u32[]{:S(2)}, u32[]{:S(2)}) %collective-permute-start.2) | collective-permute-done | bytes 1048608 | tf_op jit(solution)/shard_map/ppermute | solution.py:380
  55.2 4.1 %collective-permute-start.6 = (s32[2,5,17]{2,0,1:T(2,128)S(1)}, s32[2,5,17]{2,0,1:T(2,128)S(1)}, u32[]{:S(2)}, u32[]{:S(2)}) collective-permute-start(s32[2,5,17]{2,0,1:T(2,128)S(1)} %add_add_fusion), channel_id=1, source_target_pairs={{0,2},{6,4},{1,3},{7,5},{8,10},{14,12},{9,11},{15,13},{16,18},{22,... | collective-permute-start | bytes 2048 | tf_op jit(solution)/shard_map/ppermute | solution.py:380
  59.3 2.2 %collective-permute-start.4 = (bf16[2,96,2048]{2,1,0:T(8,128)(2,1)}, bf16[2,96,2048]{2,1,0:T(8,128)(2,1)}, u32[]{:S(2)}, u32[]{:S(2)}) collective-permute-start(bf16[2,96,2048]{2,1,0:T(8,128)(2,1)} %bitcast.119), channel_id=1, source_target_pairs={{0,2},{6,4},{1,3},{7,5},{8,10},{14,12},{9,11},{15,13},{16,18},{22,... | collective-permute-start | bytes 2359304 | tf_op jit(solution)/shard_map/ppermute | solution.py:380
  61.5 1.7 collective-permute-start.8
  63.1 1.7 slice_select_fusion
  65.8 5.0 %collective-permute-start.3 = (bf16[96,2048]{1,0:T(8,128)(2,1)S(1)}, bf16[96,2048]{1,0:T(8,128)(2,1)}, u32[]{:S(2)}, u32[]{:S(2)}) collective-permute-start(bf16[96,2048]{1,0:T(8,128)(2,1)S(1)} %bitcast.112), channel_id=1, source_target_pairs={{0,2},{6,4},{1,3},{7,5},{8,10},{14,12},{9,11},{15,13},{16,18},{22,... | collective-permute-start | bytes 1179656 | tf_op jit(solution)/shard_map/ppermute | solution.py:380
  73.8 9.0 %collective-permute-done.4.refs_4_.refs_11_ = bf16[2,96,2048]{2,1,0:T(8,128)(2,1)} collective-permute-done((bf16[2,96,2048]{2,1,0:T(8,128)(2,1)}, bf16[2,96,2048]{2,1,0:T(8,128)(2,1)}, u32[]{:S(2)}, u32[]{:S(2)}) %collective-permute-start.4) | collective-permute-done | bytes 786464 | tf_op jit(solution)/shard_map/ppermute | solution.py:380
  83.5 5.5 %collective-permute-start.11 = (bf16[96,2048]{1,0:T(8,128)(2,1)S(1)}, bf16[96,2048]{1,0:T(8,128)(2,1)S(1)}, u32[]{:S(2)}, u32[]{:S(2)}) collective-permute-start(bf16[96,2048]{1,0:T(8,128)(2,1)S(1)} %bitcast.107), channel_id=1, source_target_pairs={{0,2},{6,4},{1,3},{7,5},{8,10},{14,12},{9,11},{15,13},{16,18},{22,... | collective-permute-start | bytes 1179656 | tf_op jit(solution)/shard_map/ppermute | solution.py:380
  89.1 2.1 %collective-permute-done.3.refs_2_ = bf16[96,2048]{1,0:T(8,128)(2,1)} collective-permute-done((bf16[96,2048]{1,0:T(8,128)(2,1)S(1)}, bf16[96,2048]{1,0:T(8,128)(2,1)}, u32[]{:S(2)}, u32[]{:S(2)}) %collective-permute-start.3) | collective-permute-done | bytes 393248 | tf_op jit(solution)/shard_map/ppermute | solution.py:380
  92.5 5.2 %collective-permute-start.9 = (bf16[96,2048]{1,0:T(8,128)(2,1)S(1)}, bf16[96,2048]{1,0:T(8,128)(2,1)S(1)}, u32[]{:S(2)}, u32[]{:S(2)}) collective-permute-start(bf16[96,2048]{1,0:T(8,128)(2,1)S(1)} %bitcast.96), channel_id=1, source_target_pairs={{0,2},{6,4},{1,3},{7,5},{8,10},{14,12},{9,11},{15,13},{16,18},{22,... | collective-permute-start | bytes 1179656 | tf_op jit(solution)/shard_map/ppermute | solution.py:380
  98.7 7.3 %project.1 = (bf16[3,192,512]{2,1,0:T(8,128)(2,1)S(1)}, f32[2,192,512]{2,1,0:T(8,128)S(1)}, bf16[2,192,1536]{2,1,0:T(8,128)(2,1)}, f32[2,192,2048]{2,1,0:T(8,128...) custom-call(s32[1]{0:T(128)} %bitcast.9.host, ...), custom_call_target="tpu_custom_call" | custom-call | flops 4831838208 | bytes 20971520 | tf_op jit(solution)/shard_map/project/pallas_call | solution.py:513
  106.1 1.9 collective-permute-done.9.refs_7_.theirs.new_theirs
  111.9 1.9 out.1
  114.5 1.9 collective-permute-start.14
  120.0 1.4 collective-permute-start.15
  122.8 1.6 backward.2
  125.2 8.3 %collective-permute-done.16.rest_0_ = bf16[192,1024]{1,0:T(8,128)(2,1)S(1)} collective-permute-done((bf16[192,1024]{1,0:T(8,128)(2,1)}, bf16[192,1024]{1,0:T(8,128)(2,1)S(1)}, u32[]{:S(2)}, u32[]{:S(2)}) %collective-permute-start.16) | collective-permute-done | bytes 393248 | tf_op jit(solution)/shard_map/ppermute | solution.py:383
  135.1 2.6 %collective-permute-done.18 = bf16[48,2048]{1,0:T(8,128)(2,1)S(1)} collective-permute-done((bf16[48,2048]{1,0:T(8,128)(2,1)S(1)}, bf16[48,2048]{1,0:T(8,128)(2,1)S(1)}, u32[]{:S(2)}, u32[]{:S(2)}) %collective-permute-start.18) | collective-permute-done | bytes 196640 | tf_op jit(solution)/shard_map/ppermute | solution.py:383
  139.5 1.5 collective-permute-start.23
  143.7 4.5 %forward.1 = (bf16[2,48,2048]{2,1,0:T(8,128)(2,1)S(1)}, bf16[2,48,2048]{2,1,0:T(8,128)(2,1)S(1)}) custom-call(s32[1]{0:T(128)} %bitcast.9.host, s32[1]{0:T(128)} %bitcast.6.core.refs_0_, s32[6]{0:T(128)S(1)} %stack.96.refs_0_.refs_1_, s32[4]{0:T(128)S(1)} %add_multiply_fusion.offs.refs_2_, s32[1]{0:T(128)} %bitcast.36.refs_3_.fresh, ...), custom_call_target="tpu_custom_call" | custom-call | flops 3221225472 | bytes 20971520 | tf_op jit(solution)/shard_map/forward/pallas_call | solution.py:612
  152.8 8.5 %collective-permute-done.23.rest_2_ = bf16[192,1536]{1,0:T(8,128)(2,1)S(1)} collective-permute-done((bf16[192,1536]{1,0:T(8,128)(2,1)}, bf16[192,1536]{1,0:T(8,128)(2,1)S(1)}, u32[]{:S(2)}, u32[]{:S(2)}) %collective-permute-start.23) | collective-permute-done | bytes 589856 | tf_op jit(solution)/shard_map/ppermute | solution.py:389
  162.1 5.7 %collective-permute-done.24 = bf16[48,2048]{1,0:T(8,128)(2,1)S(1)} collective-permute-done((bf16[48,2048]{1,0:T(8,128)(2,1)S(1)}, bf16[48,2048]{1,0:T(8,128)(2,1)S(1)}, u32[]{:S(2)}, u32[]{:S(2)}) %collective-permute-start.24) | collective-permute-done | bytes 196640 | tf_op jit(solution)/shard_map/ppermute | solution.py:383
  177.8 4.2 %collective-permute-done.26.rest_3_ = bf16[192,512]{1,0:T(8,128)(2,1)S(1)} collective-permute-done((bf16[192,512]{1,0:T(8,128)(2,1)S(1)}, bf16[192,512]{1,0:T(8,128)(2,1)S(1)}, u32[]{:S(2)}, u32[]{:S(2)}) %collective-permute-start.26) | collective-permute-done | bytes 196640 | tf_op jit(solution)/shard_map/ppermute | solution.py:383
  182.0 5.1 %collective-permute-done.28.rest_5_ = bf16[192,512]{1,0:T(8,128)(2,1)S(1)} collective-permute-done((bf16[192,512]{1,0:T(8,128)(2,1)S(1)}, bf16[192,512]{1,0:T(8,128)(2,1)S(1)}, u32[]{:S(2)}, u32[]{:S(2)}) %collective-permute-start.28) | collective-permute-done | bytes 196640 | tf_op jit(solution)/shard_map/ppermute | solution.py:389
  187.1 1.5 collective-permute-start.30
  192.9 2.3 %grads.1 = f32[512,512]{1,0:T(8,128)} custom-call(s32[1]{0:T(128)} %bitcast.9.host, s32[4]{0:T(128)S(1)} %add_multiply_fusion.offs.refs_2_, bf16[3,192,512]{2,1,0:T(8,128)(2,1)S(1)} %copy-done.4, bf16[192,2048]{1,0:T(8,128)(2,1)S(1)} %copy-done.10, bf16[192,2048]{1,0:T(8,128)(2,1)S(1)} %get-tuple-element.131.refs_3_.up_1, bf16[96,2048]{1,0:T(8,128)(2,1)S(1)} %bitcast.109, ...), custom_call_target="tpu_custom_call" | custom-call | flops 402653184 | bytes 2621440 | tf_op jit(solution)/shard_map/grads/pallas_call | solution.py:683
  196.0 3.5 %collective-permute-done.31 = bf16[48,2048]{1,0:T(8,128)(2,1)S(1)} collective-permute-done((bf16[48,2048]{1,0:T(8,128)(2,1)S(1)}, bf16[48,2048]{1,0:T(8,128)(2,1)S(1)}, u32[]{:S(2)}, u32[]{:S(2)}) %collective-permute-start.31) | collective-permute-done | bytes 196640 | tf_op jit(solution)/shard_map/ppermute | solution.py:383
  (172 shorter events, 49.7 us)
Async XLA Ops:
  0.7 53.9 %collective-permute-start = (bf16[512,2048]{1,0:T(8,128)(2,1)}, bf16[512,2048]{1,0:T(8,128)(2,1)S(1)}, u32[]{:S(2)}, u32[]{:S(2)}) collective-permute-start(bf16[512,2048]{1,0:T(8,128)(2,1)} %bitcast.114), channel_id=1, source_target_pairs={{4,2},{2,4},{5,3},{3,5},{12,10},{10,12},{13,11},{11,13},{20,18},{1... | collective-permute-start | bytes 6291464 | tf_op jit(solution)/shard_map/ppermute | solution.py:386
  4.7 27.4 %collective-permute-start.1 = (bf16[256,2048]{1,0:T(8,128)(2,1)}, bf16[256,2048]{1,0:T(8,128)(2,1)}, u32[]{:S(2)}, u32[]{:S(2)}) collective-permute-start(bf16[256,2048]{1,0:T(8,128)(2,1)} %get-tuple-element.154), channel_id=1, source_target_pairs={{0,2},{6,4},{1,3},{7,5},{8,10},{14,12},{9,11},{15,13},{16,18},{22,... | collective-permute-start | bytes 3145736 | tf_op jit(solution)/shard_map/ppermute | solution.py:380
  11.3 43.3 %collective-permute-start.2 = (bf16[256,2048]{1,0:T(8,128)(2,1)}, bf16[256,2048]{1,0:T(8,128)(2,1)}, u32[]{:S(2)}, u32[]{:S(2)}) collective-permute-start(bf16[256,2048]{1,0:T(8,128)(2,1)} %get-tuple-element.153), channel_id=1, source_target_pairs={{0,2},{6,4},{1,3},{7,5},{8,10},{14,12},{9,11},{15,13},{16,18},{22,... | collective-permute-start | bytes 3145736 | tf_op jit(solution)/shard_map/ppermute | solution.py:380
  13.6 52.2 %collective-permute-start.5 = (bf16[512,512]{1,0:T(8,128)(2,1)S(1)}, bf16[512,512]{1,0:T(8,128)(2,1)S(1)}, u32[]{:S(2)}, u32[]{:S(2)}) collective-permute-start(bf16[512,512]{1,0:T(8,128)(2,1)S(1)} %bitcast.100), channel_id=1, source_target_pairs={{0,2},{6,4},{1,3},{7,5},{8,10},{14,12},{9,11},{15,13},{16,18},{22,... | collective-permute-start | bytes 1572872 | tf_op jit(solution)/shard_map/ppermute | solution.py:380
  32.2 51.4 %collective-permute-start.7 = (bf16[256,2048]{1,0:T(8,128)(2,1)}, bf16[256,2048]{1,0:T(8,128)(2,1)}, u32[]{:S(2)}, u32[]{:S(2)}) collective-permute-start(bf16[256,2048]{1,0:T(8,128)(2,1)} %collective-permute-done.1.refs_8_.refs_18_.refs_11_), channel_id=1, source_target_pairs={{4,2},{2,4},{5,3},{3,5},{12,10},{10,12},{13,11},{11,13},{20,18},{1... | collective-permute-start | bytes 3145736 | tf_op jit(solution)/shard_map/ppermute | solution.py:386
  55.2 15.6 %collective-permute-start.6 = (s32[2,5,17]{2,0,1:T(2,128)S(1)}, s32[2,5,17]{2,0,1:T(2,128)S(1)}, u32[]{:S(2)}, u32[]{:S(2)}) collective-permute-start(s32[2,5,17]{2,0,1:T(2,128)S(1)} %add_add_fusion), channel_id=1, source_target_pairs={{0,2},{6,4},{1,3},{7,5},{8,10},{14,12},{9,11},{15,13},{16,18},{22,... | collective-permute-start | bytes 2048 | tf_op jit(solution)/shard_map/ppermute | solution.py:380
  59.3 23.6 %collective-permute-start.4 = (bf16[2,96,2048]{2,1,0:T(8,128)(2,1)}, bf16[2,96,2048]{2,1,0:T(8,128)(2,1)}, u32[]{:S(2)}, u32[]{:S(2)}) collective-permute-start(bf16[2,96,2048]{2,1,0:T(8,128)(2,1)} %bitcast.119), channel_id=1, source_target_pairs={{0,2},{6,4},{1,3},{7,5},{8,10},{14,12},{9,11},{15,13},{16,18},{22,... | collective-permute-start | bytes 2359304 | tf_op jit(solution)/shard_map/ppermute | solution.py:380
  61.5 31.0 %collective-permute-start.8 = (bf16[256,2048]{1,0:T(8,128)(2,1)}, bf16[256,2048]{1,0:T(8,128)(2,1)}, u32[]{:S(2)}, u32[]{:S(2)}) collective-permute-start(bf16[256,2048]{1,0:T(8,128)(2,1)} %collective-permute-done.2.refs_9_.refs_19_.refs_12_), channel_id=1, source_target_pairs={{4,2},{2,4},{5,3},{3,5},{12,10},{10,12},{13,11},{11,13},{20,18},{1... | collective-permute-start | bytes 3145736 | tf_op jit(solution)/shard_map/ppermute | solution.py:386
  65.8 25.4 %collective-permute-start.3 = (bf16[96,2048]{1,0:T(8,128)(2,1)S(1)}, bf16[96,2048]{1,0:T(8,128)(2,1)}, u32[]{:S(2)}, u32[]{:S(2)}) collective-permute-start(bf16[96,2048]{1,0:T(8,128)(2,1)S(1)} %bitcast.112), channel_id=1, source_target_pairs={{0,2},{6,4},{1,3},{7,5},{8,10},{14,12},{9,11},{15,13},{16,18},{22,... | collective-permute-start | bytes 1179656 | tf_op jit(solution)/shard_map/ppermute | solution.py:380
  71.7 40.1 %collective-permute-start.12 = (bf16[512,512]{1,0:T(8,128)(2,1)S(1)}, bf16[512,512]{1,0:T(8,128)(2,1)S(1)}, u32[]{:S(2)}, u32[]{:S(2)}) collective-permute-start(bf16[512,512]{1,0:T(8,128)(2,1)S(1)} %bitcast.101), channel_id=1, source_target_pairs={{4,2},{2,4},{5,3},{3,5},{12,10},{10,12},{13,11},{11,13},{20,18},{1... | collective-permute-start | bytes 1572872 | tf_op jit(solution)/shard_map/ppermute | solution.py:386
  82.8 29.0 %collective-permute-start.13 = (bf16[512,512]{1,0:T(8,128)(2,1)S(1)}, bf16[512,512]{1,0:T(8,128)(2,1)S(1)}, u32[]{:S(2)}, u32[]{:S(2)}) collective-permute-start(bf16[512,512]{1,0:T(8,128)(2,1)S(1)} %collective-permute-done.5.rest_1_.refs_13_.refs_16_), channel_id=1, source_target_pairs={{4,2},{2,4},{5,3},{3,5},{12,10},{10,12},{13,11},{11,13},{20,18},{1... | collective-permute-start | bytes 1572872 | tf_op jit(solution)/shard_map/ppermute | solution.py:386
  83.5 24.5 %collective-permute-start.11 = (bf16[96,2048]{1,0:T(8,128)(2,1)S(1)}, bf16[96,2048]{1,0:T(8,128)(2,1)S(1)}, u32[]{:S(2)}, u32[]{:S(2)}) collective-permute-start(bf16[96,2048]{1,0:T(8,128)(2,1)S(1)} %bitcast.107), channel_id=1, source_target_pairs={{0,2},{6,4},{1,3},{7,5},{8,10},{14,12},{9,11},{15,13},{16,18},{22,... | collective-permute-start | bytes 1179656 | tf_op jit(solution)/shard_map/ppermute | solution.py:380
  91.1 14.9 %collective-permute-start.10 = (bf16[96,512]{1,0:T(8,128)(2,1)S(1)}, bf16[96,512]{1,0:T(8,128)(2,1)S(1)}, u32[]{:S(2)}, u32[]{:S(2)}) collective-permute-start(bf16[96,512]{1,0:T(8,128)(2,1)S(1)} %constant_dynamic-slice_fusion.1), channel_id=1, source_target_pairs={{2,0},{4,6},{3,1},{5,7},{10,8},{12,14},{11,9},{13,15},{18,16},{20,... | collective-permute-start | bytes 294920 | tf_op jit(solution)/shard_map/ppermute | solution.py:383
  92.5 15.5 %collective-permute-start.9 = (bf16[96,2048]{1,0:T(8,128)(2,1)S(1)}, bf16[96,2048]{1,0:T(8,128)(2,1)S(1)}, u32[]{:S(2)}, u32[]{:S(2)}) collective-permute-start(bf16[96,2048]{1,0:T(8,128)(2,1)S(1)} %bitcast.96), channel_id=1, source_target_pairs={{0,2},{6,4},{1,3},{7,5},{8,10},{14,12},{9,11},{15,13},{16,18},{22,... | collective-permute-start | bytes 1179656 | tf_op jit(solution)/shard_map/ppermute | solution.py:380
  114.5 4.1 %collective-permute-start.14 = (bf16[2,48,2048]{2,1,0:T(8,128)(2,1)}, bf16[2,48,2048]{2,1,0:T(8,128)(2,1)}, u32[]{:S(2)}, u32[]{:S(2)}) collective-permute-start(bf16[2,48,2048]{2,1,0:T(8,128)(2,1)} %get-tuple-element.106), channel_id=1, source_target_pairs={{0,1},{1,0},{2,3},{3,2},{4,5},{5,4},{6,7},{7,6},{8,9},{9,8},{10,11... | collective-permute-start | bytes 1179656 | tf_op jit(solution)/shard_map/ppermute | solution.py:394
  116.5 17.0 %collective-permute-start.16 = (bf16[192,1024]{1,0:T(8,128)(2,1)}, bf16[192,1024]{1,0:T(8,128)(2,1)S(1)}, u32[]{:S(2)}, u32[]{:S(2)}) collective-permute-start(bf16[192,1024]{1,0:T(8,128)(2,1)} %copy-done.26), channel_id=1, source_target_pairs={{2,0},{4,6},{3,1},{5,7},{10,8},{12,14},{11,9},{13,15},{18,16},{20,... | collective-permute-start | bytes 1179656 | tf_op jit(solution)/shard_map/ppermute | solution.py:383
  117.9 16.4 %collective-permute-start.17 = (bf16[192,1536]{1,0:T(8,128)(2,1)}, bf16[192,1536]{1,0:T(8,128)(2,1)S(1)}, u32[]{:S(2)}, u32[]{:S(2)}) collective-permute-start(bf16[192,1536]{1,0:T(8,128)(2,1)} %copy-done.25), channel_id=1, source_target_pairs={{4,2},{2,4},{5,3},{3,5},{12,10},{10,12},{13,11},{11,13},{20,18},{1... | collective-permute-start | bytes 1769480 | tf_op jit(solution)/shard_map/ppermute | solution.py:386
  120.0 17.6 %collective-permute-start.15 = (bf16[2,48,2048]{2,1,0:T(8,128)(2,1)S(1)}, bf16[2,48,2048]{2,1,0:T(8,128)(2,1)}, u32[]{:S(2)}, u32[]{:S(2)}) collective-permute-start(bf16[2,48,2048]{2,1,0:T(8,128)(2,1)S(1)} %add_convert_fusion.2), channel_id=1, source_target_pairs={{2,10},{4,12},{10,18},{12,20},{18,26},{20,28},{3,11},{5,13},{11,19... | collective-permute-start | bytes 1179656 | tf_op jit(solution)/shard_map/ppermute | solution.py:403
  121.5 16.2 %collective-permute-start.18 = (bf16[48,2048]{1,0:T(8,128)(2,1)S(1)}, bf16[48,2048]{1,0:T(8,128)(2,1)S(1)}, u32[]{:S(2)}, u32[]{:S(2)}) collective-permute-start(bf16[48,2048]{1,0:T(8,128)(2,1)S(1)} %slice_bitcast_fusion.6), channel_id=1, source_target_pairs={{2,0},{4,6},{3,1},{5,7},{10,8},{12,14},{11,9},{13,15},{18,16},{20,... | collective-permute-start | bytes 589832 | tf_op jit(solution)/shard_map/ppermute | solution.py:383
  138.3 2.7 %collective-permute-start.21 = (bf16[2,48,2048]{2,1,0:T(8,128)(2,1)}, bf16[2,48,2048]{2,1,0:T(8,128)(2,1)S(1)}, u32[]{:S(2)}, u32[]{:S(2)}) collective-permute-start(bf16[2,48,2048]{2,1,0:T(8,128)(2,1)} %get-tuple-element.127), channel_id=1, source_target_pairs={{0,1},{1,0},{2,3},{3,2},{4,5},{5,4},{6,7},{7,6},{8,9},{9,8},{10,11... | collective-permute-start | bytes 1179656 | tf_op jit(solution)/shard_map/ppermute | solution.py:394
  139.5 21.8 %collective-permute-start.23 = (bf16[192,1536]{1,0:T(8,128)(2,1)}, bf16[192,1536]{1,0:T(8,128)(2,1)S(1)}, u32[]{:S(2)}, u32[]{:S(2)}) collective-permute-start(bf16[192,1536]{1,0:T(8,128)(2,1)} %copy-done.24), channel_id=1, source_target_pairs={{4,0},{2,6},{5,1},{3,7},{12,8},{10,14},{13,9},{11,15},{20,16},{18,... | collective-permute-start | bytes 1769480 | tf_op jit(solution)/shard_map/ppermute | solution.py:389
  140.9 2.8 %collective-permute-start.19 = (bf16[2,48,2048]{2,1,0:T(8,128)(2,1)}, bf16[2,48,2048]{2,1,0:T(8,128)(2,1)S(1)}, u32[]{:S(2)}, u32[]{:S(2)}) collective-permute-start(bf16[2,48,2048]{2,1,0:T(8,128)(2,1)} %collective-permute-done.15.refs_4_.passed), channel_id=1, source_target_pairs={{0,1},{1,0},{2,3},{3,2},{4,5},{5,4},{6,7},{7,6},{8,9},{9,8},{10,11... | collective-permute-start | bytes 1179656 | tf_op jit(solution)/shard_map/ppermute | solution.py:394
  142.3 25.5 %collective-permute-start.22 = (bf16[2,48,2048]{2,1,0:T(8,128)(2,1)S(1)}, bf16[2,48,2048]{2,1,0:T(8,128)(2,1)}, u32[]{:S(2)}, u32[]{:S(2)}) collective-permute-start(bf16[2,48,2048]{2,1,0:T(8,128)(2,1)S(1)} %add_convert_fusion.1), channel_id=1, source_target_pairs={{10,2},{12,4},{18,10},{20,12},{26,18},{28,20},{11,3},{13,5},{19,11... | collective-permute-start | bytes 1179656 | tf_op jit(solution)/shard_map/ppermute | solution.py:403
  148.2 1.9 collective-permute-start.20
  148.7 19.0 %collective-permute-start.24 = (bf16[48,2048]{1,0:T(8,128)(2,1)S(1)}, bf16[48,2048]{1,0:T(8,128)(2,1)S(1)}, u32[]{:S(2)}, u32[]{:S(2)}) collective-permute-start(bf16[48,2048]{1,0:T(8,128)(2,1)S(1)} %slice_bitcast_fusion.5), channel_id=1, source_target_pairs={{2,0},{4,6},{3,1},{5,7},{10,8},{12,14},{11,9},{13,15},{18,16},{20,... | collective-permute-start | bytes 589832 | tf_op jit(solution)/shard_map/ppermute | solution.py:383
  168.4 2.4 %collective-permute-start.25 = (bf16[2,48,2048]{2,1,0:T(8,128)(2,1)}, bf16[2,48,2048]{2,1,0:T(8,128)(2,1)}, u32[]{:S(2)}, u32[]{:S(2)}) collective-permute-start(bf16[2,48,2048]{2,1,0:T(8,128)(2,1)} %collective-permute-done.22.mine), channel_id=1, source_target_pairs={{0,1},{1,0},{2,3},{3,2},{4,5},{5,4},{6,7},{7,6},{8,9},{9,8},{10,11... | collective-permute-start | bytes 1179656 | tf_op jit(solution)/shard_map/ppermute | solution.py:394
  169.2 8.6 %collective-permute-start.29 = (bf16[48,2048]{1,0:T(8,128)(2,1)}, bf16[48,2048]{1,0:T(8,128)(2,1)S(1)}, u32[]{:S(2)}, u32[]{:S(2)}) collective-permute-start(bf16[48,2048]{1,0:T(8,128)(2,1)} %copy-done.27), channel_id=1, source_target_pairs={{2,0},{4,6},{3,1},{5,7},{10,8},{12,14},{11,9},{13,15},{18,16},{20,... | collective-permute-start | bytes 589832 | tf_op jit(solution)/shard_map/ppermute | solution.py:383
  172.1 9.9 %collective-permute-start.26 = (bf16[192,512]{1,0:T(8,128)(2,1)S(1)}, bf16[192,512]{1,0:T(8,128)(2,1)S(1)}, u32[]{:S(2)}, u32[]{:S(2)}) collective-permute-start(bf16[192,512]{1,0:T(8,128)(2,1)S(1)} %get-tuple-element.134), channel_id=1, source_target_pairs={{2,0},{4,6},{3,1},{5,7},{10,8},{12,14},{11,9},{13,15},{18,16},{20,... | collective-permute-start | bytes 589832 | tf_op jit(solution)/shard_map/ppermute | solution.py:383
  173.4 8.6 %collective-permute-start.27 = (bf16[192,512]{1,0:T(8,128)(2,1)S(1)}, bf16[192,512]{1,0:T(8,128)(2,1)S(1)}, u32[]{:S(2)}, u32[]{:S(2)}) collective-permute-start(bf16[192,512]{1,0:T(8,128)(2,1)S(1)} %get-tuple-element.135), channel_id=1, source_target_pairs={{4,2},{2,4},{5,3},{3,5},{12,10},{10,12},{13,11},{11,13},{20,18},{1... | collective-permute-start | bytes 589832 | tf_op jit(solution)/shard_map/ppermute | solution.py:386
  174.1 13.0 %collective-permute-start.28 = (bf16[192,512]{1,0:T(8,128)(2,1)S(1)}, bf16[192,512]{1,0:T(8,128)(2,1)S(1)}, u32[]{:S(2)}, u32[]{:S(2)}) collective-permute-start(bf16[192,512]{1,0:T(8,128)(2,1)S(1)} %get-tuple-element.136), channel_id=1, source_target_pairs={{4,0},{2,6},{5,1},{3,7},{12,8},{10,14},{13,9},{11,15},{20,16},{18,... | collective-permute-start | bytes 589832 | tf_op jit(solution)/shard_map/ppermute | solution.py:389
  187.1 2.9 %collective-permute-start.30 = (bf16[2,48,2048]{2,1,0:T(8,128)(2,1)S(1)}, bf16[2,48,2048]{2,1,0:T(8,128)(2,1)S(1)}, u32[]{:S(2)}, u32[]{:S(2)}) collective-permute-start(bf16[2,48,2048]{2,1,0:T(8,128)(2,1)S(1)} %get-tuple-element.140), channel_id=1, source_target_pairs={{0,1},{1,0},{2,3},{3,2},{4,5},{5,4},{6,7},{7,6},{8,9},{9,8},{10,11... | collective-permute-start | bytes 1179656 | tf_op jit(solution)/shard_map/ppermute | solution.py:394
  191.4 8.0 %collective-permute-start.31 = (bf16[48,2048]{1,0:T(8,128)(2,1)S(1)}, bf16[48,2048]{1,0:T(8,128)(2,1)S(1)}, u32[]{:S(2)}, u32[]{:S(2)}) collective-permute-start(bf16[48,2048]{1,0:T(8,128)(2,1)S(1)} %slice_bitcast_fusion.2), channel_id=1, source_target_pairs={{2,0},{4,6},{3,1},{5,7},{10,8},{12,14},{11,9},{13,15},{18,16},{20,... | collective-permute-start | bytes 589832 | tf_op jit(solution)/shard_map/ppermute | solution.py:383
  (44 other events, 493.0 us)

commit v10 on v9

--- a/solution.py
+++ b/solution.py
@@ -12,7 +12,7 @@
 BLOCKS = 4
 EPSILON = 1e-06
 SCALING = HEAD_DIM ** (-0.5)
-VMEM_BYTES = 50 * 1024 * 1024
+VMEM_BYTES = 34 * 1024 * 1024
 SMALL_VMEM_BYTES = 16 * 1024 * 1024
 
 F32 = jnp.float32
@@ -62,44 +62,90 @@
     return sig, gate, vqk, scores, sig_s, probs, mixed, gated
 
 
-def project(normed, offs, weights):
+def project(normed, offs, weights, of_head):
     total = None
     for j, weight in enumerate(weights):
         depth = weight.shape[0]
         columns = pl.ds(pl.multiple_of(offs[j], depth), depth)
-        term = dot(normed[:, columns], weight[...])
+        term = dot(normed[:, columns], weight[:, of_head])
         total = term if total is None else total + term
     return total
 
 
-def project_kernel(parts, offs, x_own, x_theirs, stash_own, stash_theirs, keep, *rest):
-    weights = rest[:parts]
-    gated_out, gate_out, vqk_out, slope_out, mixed_out, probs_out, factor_out, normed = rest[parts:]
+def columns_of_head(h, size):
+    return pl.ds(pl.multiple_of(h * size, size), size)
+
+
+def weight_copies(sources, targets, sems, h):
+    of_head = columns_of_head(h, 4 * HEAD_DIM)
+    return [
+        pltpu.make_async_copy(
+            source.at[:, of_head], target.at[:, of_head], sems.at[h * len(sources) + j]
+        )
+        for j, (source, target) in enumerate(zip(sources, targets))
+    ]
+
+
+def project_kernel(parts, heads, offs, x_own, x_theirs, stash_own, stash_theirs, keep, *rest):
+    sources, rest = rest[:parts], rest[parts:]
+    gated_out, saved, rest = rest[0], rest[1:7], rest[7:]
+    weights, rest = rest[:parts], rest[parts:]
+    held, (normed, sems, out_sems) = rest[:6], rest[6:]
+    gate_out, vqk_out, slope_out, mixed_out, probs_out, factor_out = held
     length = x_own.shape[0]
     rows = 2 * length
-
-    @pl.when(pl.program_id(0) == 0)
+    head = pl.program_id(0)
+
+    def saved_copies(h):
+        copies = []
+        for i, (source, target) in enumerate(zip(held, saved)):
+            if i < 4:
+                at = (slice(None), slice(None), columns_of_head(h, source.shape[2] // heads))
+            else:
+                at = (slice(None), h)
+            copies.append(
+                pltpu.make_async_copy(source.at[at], target.at[at], out_sems.at[h * 6 + i])
+            )
+        return copies
+
+    @pl.when(head == 0)
     def _():
-        sources = [x_own, x_theirs]
+        for h in range(heads):
+            for copy in weight_copies(sources, weights, sems, h):
+                copy.start()
+        blocks = [x_own, x_theirs]
         for t in range(stash_own.shape[0]):
-            sources += [stash_own.at[t], stash_theirs.at[t]]
-        for i, source in enumerate(sources):
-            floats = source[...].astype(F32)
+            blocks += [stash_own.at[t], stash_theirs.at[t]]
+        for i, block in enumerate(blocks):
+            floats = block[...].astype(F32)
             normed[pl.ds(i * length, length), :] = (floats * row_root(floats)).astype(BF16)
 
-    pre_all = project(normed, offs, weights)
+    for copy in weight_copies(sources, weights, sems, head):
+        copy.wait()
+    pre_all = project(normed, offs, weights, columns_of_head(head, 4 * HEAD_DIM))
     for i in range(1 + stash_own.shape[0]):
         pre = pre_all[i * rows : (i + 1) * rows]
         kept = keep[i]
         sig, gate, vqk, scores, sig_s, probs, mixed, gated = attend(pre, kept)
         gated_out[i] = gated
         if i > 0:
-            gate_out[i - 1] = gate
-            vqk_out[i - 1] = vqk
-            slope_out[i - 1] = sig * (1.0 + pre * (1.0 - sig))
-            mixed_out[i - 1] = mixed
-            probs_out[i - 1, 0] = probs
-            factor_out[i - 1, 0] = kept * sig_s * (1.0 + scores * (1.0 - sig_s)) * SCALING
+            narrow = columns_of_head(head, HEAD_DIM)
+            gate_out[i - 1, :, narrow] = gate
+            vqk_out[i - 1, :, columns_of_head(head, 3 * HEAD_DIM)] = vqk
+            slope_out[i - 1, :, columns_of_head(head, 4 * HEAD_DIM)] = sig * (
+                1.0 + pre * (1.0 - sig)
+            )
+            mixed_out[i - 1, :, narrow] = mixed
+            probs_out[i - 1, head] = probs
+            factor_out[i - 1, head] = kept * sig_s * (1.0 + scores * (1.0 - sig_s)) * SCALING
+    for copy in saved_copies(head):
+        copy.start()
+
+    @pl.when(head == heads - 1)
+    def _():
+        for h in range(heads):
+            for copy in saved_copies(h):
+                copy.wait()
 
 
 def split_rows(core, part, send, keep):
@@ -137,19 +183,26 @@
 
 
 def forward_kernel(parts, heads, core, in_offs, offs, fresh, mine, theirs, new_own, new_theirs, keep, *rest):
-    in_parts = rest[:parts]
-    out_parts = rest[parts:-6]
-    send, kept, whole, normed, gated, part = rest[-6:]
+    sources, rest = rest[:parts], rest[parts:]
+    in_parts, rest = rest[-parts:], rest[:-parts]
+    out_parts = rest[:-7]
+    send, kept, whole, normed, gated, part, sems = rest[-7:]
     depth = out_parts[0].shape[1]
     head = pl.program_id(0)
 
     @pl.when(head == 0)
     def _():
+        for h in range(heads):
+            for copy in weight_copies(sources, in_parts, sems, h):
+                copy.start()
         assemble(core[0], fresh[0], mine, theirs, new_own, new_theirs, whole)
         floats = whole[...].astype(F32)
         normed[...] = (floats * row_root(floats)).astype(BF16)
 
-    gated[head] = attend(project(normed, in_offs, in_parts), keep[0])[-1]
+    for copy in weight_copies(sources, in_parts, sems, head):
+        copy.wait()
+    pre = project(normed, in_offs, in_parts, columns_of_head(head, 4 * HEAD_DIM))
+    gated[head] = attend(pre, keep[0])[-1]
 
     @pl.when(head == heads - 1)
     def _():
@@ -325,6 +378,10 @@
     out[...] = total * scaling
 
 
+def in_hbm(arrays):
+    return [pltpu.with_memory_space_constraint(x, pltpu.HBM) for x in arrays]
+
+
 def after(value, *earlier):
     return lax.optimization_barrier((value,) + earlier)[0]
 
@@ -485,7 +542,7 @@
     )
 
     smem = pl.BlockSpec(memory_space=pltpu.SMEM)
-    hbm = pl.BlockSpec(memory_space=pl.ANY)
+    hbm = pl.BlockSpec(memory_space=pltpu.HBM)
 
     def all_of(*arrays):
         return [pl.BlockSpec(x.shape, lambda *_, d=x.ndim: (0,) * d) for x in arrays]
@@ -509,36 +566,35 @@
     weight_bytes = 2 * width * 5 * slab
 
     by_head = lambda lead, last: pl.BlockSpec(lead + (last,), lambda h: (0,) * len(lead) + (h,))
-    square = pl.BlockSpec((2, 1, rows, rows), lambda h: (0, h, 0, 0))
+    saved_shapes = [
+        struct((2, rows, slab), F32),
+        struct((2, rows, 3 * slab), BF16),
+        struct((2, rows, 4 * slab), F32),
+        struct((2, rows, slab), F32),
+        struct((2, heads, rows, rows), BF16),
+        struct((2, heads, rows, rows), F32),
+    ]
+    weight_scratch = [pltpu.VMEM(x.shape, BF16) for x in in_parts]
     gated, gate, vqk, slope, mixed, probs, factor = pl.pallas_call(
-        on_host(functools.partial(project_kernel, parts)),
+        on_host(functools.partial(project_kernel, parts, heads)),
         grid=(heads,),
         in_specs=[smem] * 2
         + all_of(x_own, x_theirs, stash_own, stash_theirs, keep)
-        + [by_head((x.shape[0],), wide) for x in in_parts],
-        out_specs=[
-            by_head((3, rows), HEAD_DIM),
-            by_head((2, rows), HEAD_DIM),
-            by_head((2, rows), 3 * HEAD_DIM),
-            by_head((2, rows), wide),
-            by_head((2, rows), HEAD_DIM),
-            square,
-            square,
+        + [hbm] * parts,
+        out_specs=[by_head((3, rows), HEAD_DIM)] + [hbm] * 6,
+        out_shape=[struct((3, rows, slab), BF16)]
+        + [pltpu.HBM(x.shape, x.dtype) for x in saved_shapes],
+        scratch_shapes=weight_scratch
+        + [pltpu.VMEM(x.shape, x.dtype) for x in saved_shapes]
+        + [
+            pltpu.VMEM((3 * rows, width), BF16),
+            pltpu.SemaphoreType.DMA((heads * parts,)),
+            pltpu.SemaphoreType.DMA((heads * 6,)),
         ],
-        out_shape=[
-            struct((3, rows, slab), BF16),
-            struct((2, rows, slab), F32),
-            struct((2, rows, 3 * slab), BF16),
-            struct((2, rows, 4 * slab), F32),
-            struct((2, rows, slab), F32),
-            struct((2, heads, rows, rows), BF16),
-            struct((2, heads, rows, rows), F32),
-        ],
-        scratch_shapes=[pltpu.VMEM((3 * rows, width), BF16)],
         compiler_params=params,
         cost_estimate=cost(3 * matmul, 2 * weight_bytes),
         name="project",
-    )(host_flag, in_offs, x_own, x_theirs, stash_own, stash_theirs, keep, *in_parts)
+    )(host_flag, in_offs, x_own, x_theirs, stash_own, stash_theirs, keep, *in_hbm(in_parts))
 
     def backward(ups, tick_no):
         layered = [gate, vqk, slope, mixed, probs, factor, stash_own, stash_theirs]
@@ -560,7 +616,7 @@
             compiler_params=params,
             cost_estimate=cost(2 * matmul, 2 * weight_bytes),
             name="backward",
-        )(host_flag, core, in_offs, offs, ups, *layered, *plain)
+        )(host_flag, core, in_offs, offs, ups, *in_hbm(layered), *out_parts, *in_hbm(in_parts))
 
     gated, new_theirs, up_near = lax.optimization_barrier((gated, new_theirs, up_near))
 
@@ -615,7 +671,7 @@
         in_specs=[smem] * 5
         + all_of(ahead_in, ahead_their, new_own, new_theirs)
         + [row_of(keep, keep.shape[0] - 1)]
-        + [by_head((x.shape[0],), wide) for x in in_parts]
+        + [hbm] * parts
         + all_of(*out_parts),
         out_specs=all_of(*halves),
         out_shape=halves,
@@ -624,7 +680,9 @@
             pltpu.VMEM((rows, width), BF16),
             pltpu.VMEM((heads, rows, HEAD_DIM), BF16),
             pltpu.VMEM((rows, width), BF16),
-        ],
+            pltpu.SemaphoreType.DMA((heads * parts,)),
+        ]
+        + weight_scratch,
         compiler_params=params,
         cost_estimate=cost(2 * matmul, 2 * weight_bytes),
         name="forward",
@@ -637,7 +695,7 @@
         new_own,
         new_theirs,
         keep,
-        *in_parts,
+        *in_hbm(in_parts),
         *out_parts,
     )
     new_rows = own_rows(new_own, new_theirs)

time: 202 us -> 202 us (level)
  waiting for transfers between devices: 88.4 us -> 100 us
  Pallas kernels: 21.7 us -> 13.5 us
  other arithmetic: 11.2 us -> 9.02 us
    ppermute x8, waiting for transfers between devices: 47.3 us -> 54 us  [from_partner(): return lax.ppermute(x, 'dp', [(h ^ 1, h) for h in hosts])]
    pallas_call x1, Pallas kernels: 7.32 us -> 2.18 us  [per_device(): pl.pallas_call(on_host(functools.partial(project_kernel, parts, heads)),...]
    pallas_call x1, Pallas kernels: 4.46 us -> 1.36 us  [per_device(): pl.pallas_call(on_host(functools.partial(forward_kernel, parts, heads)),...]
    ppermute x2, waiting for transfers between devices: 13.6 us -> 16.6 us  [to_beyond(): lax.ppermute(x, 'dp', [(hosts[k ^ m], hosts[k] ^ 1) for k in range(n // 2)])]
    unnamed x88 -> x78, local copies, waits for them, and re-layouts: 10.9 us -> 9.42 us
  transfers between devices with their start and end apart: 32 -> 32, of which waited for: 16 -> 16; matrix products, arithmetic and copies ran while one was open for 7% -> 6% of each run, Pallas kernels for 10% -> 6%
where the time goes in v10:
time: 202 us; the launch traced here: 200 us
  waiting for transfers between devices  100 us (50%)
  starting transfers between devices  60.3 us (30%)
  local copies, waits for them, and re-layouts  14 us (7%)
  Pallas kernels  13.5 us (7%)
  other arithmetic  9.02 us (4%)
  between operations  3.39 us (2%)
    ppermute x8, waiting for transfers between devices, from_partner(): return lax.ppermute(x, 'dp', [(h ^ 1, h) for h in hosts])  54 us
    ppermute x8, starting transfers between devices, from_partner(): return lax.ppermute(x, 'dp', [(h ^ 1, h) for h in hosts])  31.4 us
    ppermute x7, waiting for transfers between devices, to_partner(): return lax.ppermute(x, 'dp', [(h, h ^ 1) for h in hosts])  27.5 us
    ppermute x2, waiting for transfers between devices, to_beyond(): lax.ppermute(x, 'dp', [(hosts[k ^ m], hosts[k] ^ 1) for k in range(n // 2)])  16.6 us
    unnamed x78, local copies, waits for them, and re-layouts  9.42 us
    ppermute x7, starting transfers between devices, to_partner(): return lax.ppermute(x, 'dp', [(h, h ^ 1) for h in hosts])  9.14 us
    ppermute x7, starting transfers between devices, from_host(): lax.ppermute(x, 'dp', [(hosts[k ^ m], hosts[k]) for k in range(n // 2)])  8.23 us
    ppermute x6, starting transfers between devices, swap_cores(): return lax.ppermute(x, 'cores', [(c, cores - 1 - c) for c in range(cores)])  5.75 us
  transfers between devices with their start and end apart: 32, of which 16 were waited for; matrix products, arithmetic and copies ran while one was open for 6% of the time, Pallas kernels for 6%

profile of v10, /device:TPU:5, one launch (start us, length us, event | category | flops | bytes accessed | tf_op | source)
XLA Modules:
  0.0 200.1 jit_solution(7322299309379190126)
XLA Ops:
  0.7 2.2 %collective-permute-start = (bf16[512,2048]{1,0:T(8,128)(2,1)}, bf16[512,2048]{1,0:T(8,128)(2,1)}, u32[]{:S(2)}, u32[]{:S(2)}) collective-permute-start(bf16[512,2048]{1,0:T(8,128)(2,1)} %bitcast.114), channel_id=1, source_target_pairs={{4,2},{2,4},{5,3},{3,5},{12,10},{10,12},{13,11},{11,13},{20,18},{1... | collective-permute-start | bytes 6291464 | tf_op jit(solution)/shard_map/ppermute | solution.py:443
  2.9 2.7 %slice_bitcast_fusion = (bf16[256,2048]{1,0:T(8,128)(2,1)S(1)}, bf16[256,2048]{1,0:T(8,128)(2,1)}) fusion(bf16[1,512,2048]{2,1,0:T(8,128)(2,1)} %param.17), kind=kLoop, calls=%fused_computation | loop fusion | bytes 4194304 | tf_op jit(solution)/shard_map/slice | solution.py:470
  5.6 5.4 %collective-permute-start.1 = (bf16[256,2048]{1,0:T(8,128)(2,1)}, bf16[256,2048]{1,0:T(8,128)(2,1)}, u32[]{:S(2)}, u32[]{:S(2)}) collective-permute-start(bf16[256,2048]{1,0:T(8,128)(2,1)} %get-tuple-element.154), channel_id=1, source_target_pairs={{0,2},{6,4},{1,3},{7,5},{8,10},{14,12},{9,11},{15,13},{16,18},{22,... | collective-permute-start | bytes 3145736 | tf_op jit(solution)/shard_map/ppermute | solution.py:437
  10.9 2.3 %collective-permute-start.2 = (bf16[256,2048]{1,0:T(8,128)(2,1)S(1)}, bf16[256,2048]{1,0:T(8,128)(2,1)}, u32[]{:S(2)}, u32[]{:S(2)}) collective-permute-start(bf16[256,2048]{1,0:T(8,128)(2,1)S(1)} %get-tuple-element.153), channel_id=1, source_target_pairs={{0,2},{6,4},{1,3},{7,5},{8,10},{14,12},{9,11},{15,13},{16,18},{22,... | collective-permute-start | bytes 3145736 | tf_op jit(solution)/shard_map/ppermute | solution.py:437
  18.1 13.6 %collective-permute-done.1.refs_8_.refs_18_.refs_11_ = bf16[256,2048]{1,0:T(8,128)(2,1)} collective-permute-done((bf16[256,2048]{1,0:T(8,128)(2,1)}, bf16[256,2048]{1,0:T(8,128)(2,1)}, u32[]{:S(2)}, u32[]{:S(2)}) %collective-permute-start.1) | collective-permute-done | bytes 1048608 | tf_op jit(solution)/shard_map/ppermute | solution.py:437
  31.8 1.6 collective-permute-start.7
  33.4 20.7 %collective-permute-done.2.refs_9_.refs_19_.refs_12_ = bf16[256,2048]{1,0:T(8,128)(2,1)} collective-permute-done((bf16[256,2048]{1,0:T(8,128)(2,1)S(1)}, bf16[256,2048]{1,0:T(8,128)(2,1)}, u32[]{:S(2)}, u32[]{:S(2)}) %collective-permute-start.2) | collective-permute-done | bytes 1048608 | tf_op jit(solution)/shard_map/ppermute | solution.py:437
  54.7 4.2 %collective-permute-start.6 = (s32[2,5,17]{2,0,1:T(2,128)S(1)}, s32[2,5,17]{2,0,1:T(2,128)S(1)}, u32[]{:S(2)}, u32[]{:S(2)}) collective-permute-start(s32[2,5,17]{2,0,1:T(2,128)S(1)} %add_add_fusion), channel_id=1, source_target_pairs={{0,2},{6,4},{1,3},{7,5},{8,10},{14,12},{9,11},{15,13},{16,18},{22,... | collective-permute-start | bytes 2048 | tf_op jit(solution)/shard_map/ppermute | solution.py:437
  58.9 2.2 %collective-permute-start.4 = (bf16[2,96,2048]{2,1,0:T(8,128)(2,1)}, bf16[2,96,2048]{2,1,0:T(8,128)(2,1)}, u32[]{:S(2)}, u32[]{:S(2)}) collective-permute-start(bf16[2,96,2048]{2,1,0:T(8,128)(2,1)} %bitcast.13.refs_3_.refs_10_), channel_id=1, source_target_pairs={{0,2},{6,4},{1,3},{7,5},{8,10},{14,12},{9,11},{15,13},{16,18},{22,... | collective-permute-start | bytes 2359304 | tf_op jit(solution)/shard_map/ppermute | solution.py:437
  61.1 1.7 collective-permute-start.8
  62.8 1.6 slice_select_fusion
  65.4 5.0 %collective-permute-start.3 = (bf16[96,2048]{1,0:T(8,128)(2,1)S(1)}, bf16[96,2048]{1,0:T(8,128)(2,1)}, u32[]{:S(2)}, u32[]{:S(2)}) collective-permute-start(bf16[96,2048]{1,0:T(8,128)(2,1)S(1)} %bitcast.112), channel_id=1, source_target_pairs={{0,2},{6,4},{1,3},{7,5},{8,10},{14,12},{9,11},{15,13},{16,18},{22,... | collective-permute-start | bytes 1179656 | tf_op jit(solution)/shard_map/ppermute | solution.py:437
  72.5 9.9 %collective-permute-done.4.refs_4_.refs_11_ = bf16[2,96,2048]{2,1,0:T(8,128)(2,1)} collective-permute-done((bf16[2,96,2048]{2,1,0:T(8,128)(2,1)}, bf16[2,96,2048]{2,1,0:T(8,128)(2,1)}, u32[]{:S(2)}, u32[]{:S(2)}) %collective-permute-start.4) | collective-permute-done | bytes 786464 | tf_op jit(solution)/shard_map/ppermute | solution.py:437
  83.2 5.5 %collective-permute-start.11 = (bf16[96,2048]{1,0:T(8,128)(2,1)S(1)}, bf16[96,2048]{1,0:T(8,128)(2,1)S(1)}, u32[]{:S(2)}, u32[]{:S(2)}) collective-permute-start(bf16[96,2048]{1,0:T(8,128)(2,1)S(1)} %bitcast.107), channel_id=1, source_target_pairs={{0,2},{6,4},{1,3},{7,5},{8,10},{14,12},{9,11},{15,13},{16,18},{22,... | collective-permute-start | bytes 1179656 | tf_op jit(solution)/shard_map/ppermute | solution.py:437
  88.7 2.1 %collective-permute-done.3.refs_2_ = bf16[96,2048]{1,0:T(8,128)(2,1)} collective-permute-done((bf16[96,2048]{1,0:T(8,128)(2,1)S(1)}, bf16[96,2048]{1,0:T(8,128)(2,1)}, u32[]{:S(2)}, u32[]{:S(2)}) %collective-permute-start.3) | collective-permute-done | bytes 393248 | tf_op jit(solution)/shard_map/ppermute | solution.py:437
  92.1 5.6 %collective-permute-start.9 = (bf16[96,2048]{1,0:T(8,128)(2,1)S(1)}, bf16[96,2048]{1,0:T(8,128)(2,1)S(1)}, u32[]{:S(2)}, u32[]{:S(2)}) collective-permute-start(bf16[96,2048]{1,0:T(8,128)(2,1)S(1)} %bitcast.96), channel_id=1, source_target_pairs={{0,2},{6,4},{1,3},{7,5},{8,10},{14,12},{9,11},{15,13},{16,18},{22,... | collective-permute-start | bytes 1179656 | tf_op jit(solution)/shard_map/ppermute | solution.py:437
  98.7 2.2 %project.1 = (bf16[3,192,512]{2,1,0:T(8,128)(2,1)S(1)}, f32[2,192,512]{2,1,0:T(8,128)}, bf16[2,192,1536]{2,1,0:T(8,128)(2,1)}, f32[2,192,2048]{2,1,0:T(8,128)}, ...) custom-call(s32[1]{0:T(128)} %bitcast.9.host, s32[6]{0:T(128)S(1)} %stack.96.refs_0_.refs_1_, ...), custom_call_target="tpu_custom_call" | custom-call | flops 4831838208 | bytes 20971520 | tf_op jit(solution)/shard_map/project/pallas_call | solution.py:578
  100.9 6.7 %collective-permute-done.9.refs_7_.theirs.new_theirs = bf16[96,2048]{1,0:T(8,128)(2,1)S(1)} collective-permute-done((bf16[96,2048]{1,0:T(8,128)(2,1)S(1)}, bf16[96,2048]{1,0:T(8,128)(2,1)S(1)}, u32[]{:S(2)}, u32[]{:S(2)}) %collective-permute-start.9) | collective-permute-done | bytes 393248 | tf_op jit(solution)/shard_map/ppermute | solution.py:437
  110.0 1.9 out.1
  112.7 1.9 collective-permute-start.14
  120.8 1.6 backward.2
  123.2 10.2 %collective-permute-done.16.rest_0_ = bf16[192,1024]{1,0:T(8,128)(2,1)S(1)} collective-permute-done((bf16[192,1024]{1,0:T(8,128)(2,1)}, bf16[192,1024]{1,0:T(8,128)(2,1)S(1)}, u32[]{:S(2)}, u32[]{:S(2)}) %collective-permute-start.16) | collective-permute-done | bytes 393248 | tf_op jit(solution)/shard_map/ppermute | solution.py:440
  135.0 2.5 %collective-permute-done.18 = bf16[48,2048]{1,0:T(8,128)(2,1)S(1)} collective-permute-done((bf16[48,2048]{1,0:T(8,128)(2,1)S(1)}, bf16[48,2048]{1,0:T(8,128)(2,1)S(1)}, u32[]{:S(2)}, u32[]{:S(2)}) %collective-permute-start.18) | collective-permute-done | bytes 196640 | tf_op jit(solution)/shard_map/ppermute | solution.py:440
  139.4 1.6 collective-permute-start.23
  149.8 11.5 %collective-permute-done.23.rest_2_ = bf16[192,1536]{1,0:T(8,128)(2,1)S(1)} collective-permute-done((bf16[192,1536]{1,0:T(8,128)(2,1)}, bf16[192,1536]{1,0:T(8,128)(2,1)S(1)}, u32[]{:S(2)}, u32[]{:S(2)}) %collective-permute-start.23) | collective-permute-done | bytes 589856 | tf_op jit(solution)/shard_map/ppermute | solution.py:446
  162.1 5.7 %collective-permute-done.24 = bf16[48,2048]{1,0:T(8,128)(2,1)S(1)} collective-permute-done((bf16[48,2048]{1,0:T(8,128)(2,1)S(1)}, bf16[48,2048]{1,0:T(8,128)(2,1)S(1)}, u32[]{:S(2)}, u32[]{:S(2)}) %collective-permute-start.24) | collective-permute-done | bytes 196640 | tf_op jit(solution)/shard_map/ppermute | solution.py:440
  176.2 1.4 collective-permute-done.29
  177.7 4.2 %collective-permute-done.26.rest_3_ = bf16[192,512]{1,0:T(8,128)(2,1)S(1)} collective-permute-done((bf16[192,512]{1,0:T(8,128)(2,1)S(1)}, bf16[192,512]{1,0:T(8,128)(2,1)S(1)}, u32[]{:S(2)}, u32[]{:S(2)}) %collective-permute-start.26) | collective-permute-done | bytes 196640 | tf_op jit(solution)/shard_map/ppermute | solution.py:440
  181.9 5.1 %collective-permute-done.28.rest_5_ = bf16[192,512]{1,0:T(8,128)(2,1)S(1)} collective-permute-done((bf16[192,512]{1,0:T(8,128)(2,1)S(1)}, bf16[192,512]{1,0:T(8,128)(2,1)S(1)}, u32[]{:S(2)}, u32[]{:S(2)}) %collective-permute-start.28) | collective-permute-done | bytes 196640 | tf_op jit(solution)/shard_map/ppermute | solution.py:446
  187.0 1.5 collective-permute-start.30
  192.8 2.3 %grads.1 = f32[512,512]{1,0:T(8,128)} custom-call(s32[1]{0:T(128)} %bitcast.9.host, s32[4]{0:T(128)S(1)} %add_multiply_fusion.offs.refs_2_, bf16[3,192,512]{2,1,0:T(8,128)(2,1)S(1)} %copy-done.2, bf16[192,2048]{1,0:T(8,128)(2,1)S(1)} %copy-done.5, bf16[192,2048]{1,0:T(8,128)(2,1)S(1)} %get-tuple-element.131.refs_3_.up_1, bf16[96,2048]{1,0:T(8,128)(2,1)S(1)} %bitcast.109, ...), custom_call_target="tpu_custom_call" | custom-call | flops 402653184 | bytes 2621440 | tf_op jit(solution)/shard_map/grads/pallas_call | solution.py:741
  195.8 3.5 %collective-permute-done.31 = bf16[48,2048]{1,0:T(8,128)(2,1)S(1)} collective-permute-done((bf16[48,2048]{1,0:T(8,128)(2,1)S(1)}, bf16[48,2048]{1,0:T(8,128)(2,1)S(1)}, u32[]{:S(2)}, u32[]{:S(2)}) %collective-permute-start.31) | collective-permute-done | bytes 196640 | tf_op jit(solution)/shard_map/ppermute | solution.py:440
  (162 shorter events, 46.7 us)
Async XLA Ops:
  0.7 53.4 %collective-permute-start = (bf16[512,2048]{1,0:T(8,128)(2,1)}, bf16[512,2048]{1,0:T(8,128)(2,1)}, u32[]{:S(2)}, u32[]{:S(2)}) collective-permute-start(bf16[512,2048]{1,0:T(8,128)(2,1)} %bitcast.114), channel_id=1, source_target_pairs={{4,2},{2,4},{5,3},{3,5},{12,10},{10,12},{13,11},{11,13},{20,18},{1... | collective-permute-start | bytes 6291464 | tf_op jit(solution)/shard_map/ppermute | solution.py:443
  5.6 26.2 %collective-permute-start.1 = (bf16[256,2048]{1,0:T(8,128)(2,1)}, bf16[256,2048]{1,0:T(8,128)(2,1)}, u32[]{:S(2)}, u32[]{:S(2)}) collective-permute-start(bf16[256,2048]{1,0:T(8,128)(2,1)} %get-tuple-element.154), channel_id=1, source_target_pairs={{0,2},{6,4},{1,3},{7,5},{8,10},{14,12},{9,11},{15,13},{16,18},{22,... | collective-permute-start | bytes 3145736 | tf_op jit(solution)/shard_map/ppermute | solution.py:437
  10.9 43.2 %collective-permute-start.2 = (bf16[256,2048]{1,0:T(8,128)(2,1)S(1)}, bf16[256,2048]{1,0:T(8,128)(2,1)}, u32[]{:S(2)}, u32[]{:S(2)}) collective-permute-start(bf16[256,2048]{1,0:T(8,128)(2,1)S(1)} %get-tuple-element.153), channel_id=1, source_target_pairs={{0,2},{6,4},{1,3},{7,5},{8,10},{14,12},{9,11},{15,13},{16,18},{22,... | collective-permute-start | bytes 3145736 | tf_op jit(solution)/shard_map/ppermute | solution.py:437
  13.2 52.2 %collective-permute-start.5 = (bf16[512,512]{1,0:T(8,128)(2,1)S(1)}, bf16[512,512]{1,0:T(8,128)(2,1)S(1)}, u32[]{:S(2)}, u32[]{:S(2)}) collective-permute-start(bf16[512,512]{1,0:T(8,128)(2,1)S(1)} %bitcast.100), channel_id=1, source_target_pairs={{0,2},{6,4},{1,3},{7,5},{8,10},{14,12},{9,11},{15,13},{16,18},{22,... | collective-permute-start | bytes 1572872 | tf_op jit(solution)/shard_map/ppermute | solution.py:437
  31.8 51.4 %collective-permute-start.7 = (bf16[256,2048]{1,0:T(8,128)(2,1)}, bf16[256,2048]{1,0:T(8,128)(2,1)}, u32[]{:S(2)}, u32[]{:S(2)}) collective-permute-start(bf16[256,2048]{1,0:T(8,128)(2,1)} %collective-permute-done.1.refs_8_.refs_18_.refs_11_), channel_id=1, source_target_pairs={{4,2},{2,4},{5,3},{3,5},{12,10},{10,12},{13,11},{11,13},{20,18},{1... | collective-permute-start | bytes 3145736 | tf_op jit(solution)/shard_map/ppermute | solution.py:443
  54.7 15.7 %collective-permute-start.6 = (s32[2,5,17]{2,0,1:T(2,128)S(1)}, s32[2,5,17]{2,0,1:T(2,128)S(1)}, u32[]{:S(2)}, u32[]{:S(2)}) collective-permute-start(s32[2,5,17]{2,0,1:T(2,128)S(1)} %add_add_fusion), channel_id=1, source_target_pairs={{0,2},{6,4},{1,3},{7,5},{8,10},{14,12},{9,11},{15,13},{16,18},{22,... | collective-permute-start | bytes 2048 | tf_op jit(solution)/shard_map/ppermute | solution.py:437
  58.9 23.6 %collective-permute-start.4 = (bf16[2,96,2048]{2,1,0:T(8,128)(2,1)}, bf16[2,96,2048]{2,1,0:T(8,128)(2,1)}, u32[]{:S(2)}, u32[]{:S(2)}) collective-permute-start(bf16[2,96,2048]{2,1,0:T(8,128)(2,1)} %bitcast.13.refs_3_.refs_10_), channel_id=1, source_target_pairs={{0,2},{6,4},{1,3},{7,5},{8,10},{14,12},{9,11},{15,13},{16,18},{22,... | collective-permute-start | bytes 2359304 | tf_op jit(solution)/shard_map/ppermute | solution.py:437
  61.1 31.0 %collective-permute-start.8 = (bf16[256,2048]{1,0:T(8,128)(2,1)}, bf16[256,2048]{1,0:T(8,128)(2,1)}, u32[]{:S(2)}, u32[]{:S(2)}) collective-permute-start(bf16[256,2048]{1,0:T(8,128)(2,1)} %collective-permute-done.2.refs_9_.refs_19_.refs_12_), channel_id=1, source_target_pairs={{4,2},{2,4},{5,3},{3,5},{12,10},{10,12},{13,11},{11,13},{20,18},{1... | collective-permute-start | bytes 3145736 | tf_op jit(solution)/shard_map/ppermute | solution.py:443
  65.4 25.4 %collective-permute-start.3 = (bf16[96,2048]{1,0:T(8,128)(2,1)S(1)}, bf16[96,2048]{1,0:T(8,128)(2,1)}, u32[]{:S(2)}, u32[]{:S(2)}) collective-permute-start(bf16[96,2048]{1,0:T(8,128)(2,1)S(1)} %bitcast.112), channel_id=1, source_target_pairs={{0,2},{6,4},{1,3},{7,5},{8,10},{14,12},{9,11},{15,13},{16,18},{22,... | collective-permute-start | bytes 1179656 | tf_op jit(solution)/shard_map/ppermute | solution.py:437
  71.3 38.6 %collective-permute-start.12 = (bf16[512,512]{1,0:T(8,128)(2,1)S(1)}, bf16[512,512]{1,0:T(8,128)(2,1)S(1)}, u32[]{:S(2)}, u32[]{:S(2)}) collective-permute-start(bf16[512,512]{1,0:T(8,128)(2,1)S(1)} %bitcast.101), channel_id=1, source_target_pairs={{4,2},{2,4},{5,3},{3,5},{12,10},{10,12},{13,11},{11,13},{20,18},{1... | collective-permute-start | bytes 1572872 | tf_op jit(solution)/shard_map/ppermute | solution.py:443
  82.4 27.6 %collective-permute-start.13 = (bf16[512,512]{1,0:T(8,128)(2,1)S(1)}, bf16[512,512]{1,0:T(8,128)(2,1)S(1)}, u32[]{:S(2)}, u32[]{:S(2)}) collective-permute-start(bf16[512,512]{1,0:T(8,128)(2,1)S(1)} %collective-permute-done.5.rest_1_.refs_13_.refs_16_), channel_id=1, source_target_pairs={{4,2},{2,4},{5,3},{3,5},{12,10},{10,12},{13,11},{11,13},{20,18},{1... | collective-permute-start | bytes 1572872 | tf_op jit(solution)/shard_map/ppermute | solution.py:443
  83.2 24.5 %collective-permute-start.11 = (bf16[96,2048]{1,0:T(8,128)(2,1)S(1)}, bf16[96,2048]{1,0:T(8,128)(2,1)S(1)}, u32[]{:S(2)}, u32[]{:S(2)}) collective-permute-start(bf16[96,2048]{1,0:T(8,128)(2,1)S(1)} %bitcast.107), channel_id=1, source_target_pairs={{0,2},{6,4},{1,3},{7,5},{8,10},{14,12},{9,11},{15,13},{16,18},{22,... | collective-permute-start | bytes 1179656 | tf_op jit(solution)/shard_map/ppermute | solution.py:437
  90.8 10.2 %collective-permute-start.10 = (bf16[96,512]{1,0:T(8,128)(2,1)S(1)}, bf16[96,512]{1,0:T(8,128)(2,1)S(1)}, u32[]{:S(2)}, u32[]{:S(2)}) collective-permute-start(bf16[96,512]{1,0:T(8,128)(2,1)S(1)} %constant_dynamic-slice_fusion.1), channel_id=1, source_target_pairs={{2,0},{4,6},{3,1},{5,7},{10,8},{12,14},{11,9},{13,15},{18,16},{20,... | collective-permute-start | bytes 294920 | tf_op jit(solution)/shard_map/ppermute | solution.py:440
  92.1 15.5 %collective-permute-start.9 = (bf16[96,2048]{1,0:T(8,128)(2,1)S(1)}, bf16[96,2048]{1,0:T(8,128)(2,1)S(1)}, u32[]{:S(2)}, u32[]{:S(2)}) collective-permute-start(bf16[96,2048]{1,0:T(8,128)(2,1)S(1)} %bitcast.96), channel_id=1, source_target_pairs={{0,2},{6,4},{1,3},{7,5},{8,10},{14,12},{9,11},{15,13},{16,18},{22,... | collective-permute-start | bytes 1179656 | tf_op jit(solution)/shard_map/ppermute | solution.py:437
  112.7 4.0 %collective-permute-start.14 = (bf16[2,48,2048]{2,1,0:T(8,128)(2,1)}, bf16[2,48,2048]{2,1,0:T(8,128)(2,1)}, u32[]{:S(2)}, u32[]{:S(2)}) collective-permute-start(bf16[2,48,2048]{2,1,0:T(8,128)(2,1)} %get-tuple-element.106), channel_id=1, source_target_pairs={{0,1},{1,0},{2,3},{3,2},{4,5},{5,4},{6,7},{7,6},{8,9},{9,8},{10,11... | collective-permute-start | bytes 1179656 | tf_op jit(solution)/shard_map/ppermute | solution.py:451
  114.5 18.9 %collective-permute-start.16 = (bf16[192,1024]{1,0:T(8,128)(2,1)}, bf16[192,1024]{1,0:T(8,128)(2,1)S(1)}, u32[]{:S(2)}, u32[]{:S(2)}) collective-permute-start(bf16[192,1024]{1,0:T(8,128)(2,1)} %copy-done.23), channel_id=1, source_target_pairs={{2,0},{4,6},{3,1},{5,7},{10,8},{12,14},{11,9},{13,15},{18,16},{20,... | collective-permute-start | bytes 1179656 | tf_op jit(solution)/shard_map/ppermute | solution.py:440
  116.0 18.2 %collective-permute-start.17 = (bf16[192,1536]{1,0:T(8,128)(2,1)}, bf16[192,1536]{1,0:T(8,128)(2,1)S(1)}, u32[]{:S(2)}, u32[]{:S(2)}) collective-permute-start(bf16[192,1536]{1,0:T(8,128)(2,1)} %copy-done.22), channel_id=1, source_target_pairs={{4,2},{2,4},{5,3},{3,5},{12,10},{10,12},{13,11},{11,13},{20,18},{1... | collective-permute-start | bytes 1769480 | tf_op jit(solution)/shard_map/ppermute | solution.py:443
  118.1 19.5 %collective-permute-start.15 = (bf16[2,48,2048]{2,1,0:T(8,128)(2,1)S(1)}, bf16[2,48,2048]{2,1,0:T(8,128)(2,1)}, u32[]{:S(2)}, u32[]{:S(2)}) collective-permute-start(bf16[2,48,2048]{2,1,0:T(8,128)(2,1)S(1)} %add_convert_fusion.2), channel_id=1, source_target_pairs={{2,10},{4,12},{10,18},{12,20},{18,26},{20,28},{3,11},{5,13},{11,19... | collective-permute-start | bytes 1179656 | tf_op jit(solution)/shard_map/ppermute | solution.py:460
  119.5 18.1 %collective-permute-start.18 = (bf16[48,2048]{1,0:T(8,128)(2,1)S(1)}, bf16[48,2048]{1,0:T(8,128)(2,1)S(1)}, u32[]{:S(2)}, u32[]{:S(2)}) collective-permute-start(bf16[48,2048]{1,0:T(8,128)(2,1)S(1)} %slice_bitcast_fusion.6), channel_id=1, source_target_pairs={{2,0},{4,6},{3,1},{5,7},{10,8},{12,14},{11,9},{13,15},{18,16},{20,... | collective-permute-start | bytes 589832 | tf_op jit(solution)/shard_map/ppermute | solution.py:440
  138.2 2.8 %collective-permute-start.21 = (bf16[2,48,2048]{2,1,0:T(8,128)(2,1)}, bf16[2,48,2048]{2,1,0:T(8,128)(2,1)}, u32[]{:S(2)}, u32[]{:S(2)}) collective-permute-start(bf16[2,48,2048]{2,1,0:T(8,128)(2,1)} %get-tuple-element.127), channel_id=1, source_target_pairs={{0,1},{1,0},{2,3},{3,2},{4,5},{5,4},{6,7},{7,6},{8,9},{9,8},{10,11... | collective-permute-start | bytes 1179656 | tf_op jit(solution)/shard_map/ppermute | solution.py:451
  139.4 21.9 %collective-permute-start.23 = (bf16[192,1536]{1,0:T(8,128)(2,1)}, bf16[192,1536]{1,0:T(8,128)(2,1)S(1)}, u32[]{:S(2)}, u32[]{:S(2)}) collective-permute-start(bf16[192,1536]{1,0:T(8,128)(2,1)} %copy-done.21), channel_id=1, source_target_pairs={{4,0},{2,6},{5,1},{3,7},{12,8},{10,14},{13,9},{11,15},{20,16},{18,... | collective-permute-start | bytes 1769480 | tf_op jit(solution)/shard_map/ppermute | solution.py:446
  141.0 2.8 %collective-permute-start.19 = (bf16[2,48,2048]{2,1,0:T(8,128)(2,1)}, bf16[2,48,2048]{2,1,0:T(8,128)(2,1)S(1)}, u32[]{:S(2)}, u32[]{:S(2)}) collective-permute-start(bf16[2,48,2048]{2,1,0:T(8,128)(2,1)} %collective-permute-done.15.refs_4_.passed), channel_id=1, source_target_pairs={{0,1},{1,0},{2,3},{3,2},{4,5},{5,4},{6,7},{7,6},{8,9},{9,8},{10,11... | collective-permute-start | bytes 1179656 | tf_op jit(solution)/shard_map/ppermute | solution.py:451
  142.4 25.4 %collective-permute-start.22 = (bf16[2,48,2048]{2,1,0:T(8,128)(2,1)S(1)}, bf16[2,48,2048]{2,1,0:T(8,128)(2,1)}, u32[]{:S(2)}, u32[]{:S(2)}) collective-permute-start(bf16[2,48,2048]{2,1,0:T(8,128)(2,1)S(1)} %add_convert_fusion.1), channel_id=1, source_target_pairs={{10,2},{12,4},{18,10},{20,12},{26,18},{28,20},{11,3},{13,5},{19,11... | collective-permute-start | bytes 1179656 | tf_op jit(solution)/shard_map/ppermute | solution.py:460
  145.2 1.9 collective-permute-start.20
  145.8 22.0 %collective-permute-start.24 = (bf16[48,2048]{1,0:T(8,128)(2,1)S(1)}, bf16[48,2048]{1,0:T(8,128)(2,1)S(1)}, u32[]{:S(2)}, u32[]{:S(2)}) collective-permute-start(bf16[48,2048]{1,0:T(8,128)(2,1)S(1)} %slice_bitcast_fusion.5), channel_id=1, source_target_pairs={{2,0},{4,6},{3,1},{5,7},{10,8},{12,14},{11,9},{13,15},{18,16},{20,... | collective-permute-start | bytes 589832 | tf_op jit(solution)/shard_map/ppermute | solution.py:440
  168.4 2.3 %collective-permute-start.25 = (bf16[2,48,2048]{2,1,0:T(8,128)(2,1)}, bf16[2,48,2048]{2,1,0:T(8,128)(2,1)}, u32[]{:S(2)}, u32[]{:S(2)}) collective-permute-start(bf16[2,48,2048]{2,1,0:T(8,128)(2,1)} %collective-permute-done.22.mine), channel_id=1, source_target_pairs={{0,1},{1,0},{2,3},{3,2},{4,5},{5,4},{6,7},{7,6},{8,9},{9,8},{10,11... | collective-permute-start | bytes 1179656 | tf_op jit(solution)/shard_map/ppermute | solution.py:451
  169.0 8.6 %collective-permute-start.29 = (bf16[48,2048]{1,0:T(8,128)(2,1)}, bf16[48,2048]{1,0:T(8,128)(2,1)S(1)}, u32[]{:S(2)}, u32[]{:S(2)}) collective-permute-start(bf16[48,2048]{1,0:T(8,128)(2,1)} %copy-done.24), channel_id=1, source_target_pairs={{2,0},{4,6},{3,1},{5,7},{10,8},{12,14},{11,9},{13,15},{18,16},{20,... | collective-permute-start | bytes 589832 | tf_op jit(solution)/shard_map/ppermute | solution.py:440
  172.0 9.9 %collective-permute-start.26 = (bf16[192,512]{1,0:T(8,128)(2,1)S(1)}, bf16[192,512]{1,0:T(8,128)(2,1)S(1)}, u32[]{:S(2)}, u32[]{:S(2)}) collective-permute-start(bf16[192,512]{1,0:T(8,128)(2,1)S(1)} %get-tuple-element.134), channel_id=1, source_target_pairs={{2,0},{4,6},{3,1},{5,7},{10,8},{12,14},{11,9},{13,15},{18,16},{20,... | collective-permute-start | bytes 589832 | tf_op jit(solution)/shard_map/ppermute | solution.py:440
  173.3 8.6 %collective-permute-start.27 = (bf16[192,512]{1,0:T(8,128)(2,1)S(1)}, bf16[192,512]{1,0:T(8,128)(2,1)S(1)}, u32[]{:S(2)}, u32[]{:S(2)}) collective-permute-start(bf16[192,512]{1,0:T(8,128)(2,1)S(1)} %get-tuple-element.135), channel_id=1, source_target_pairs={{4,2},{2,4},{5,3},{3,5},{12,10},{10,12},{13,11},{11,13},{20,18},{1... | collective-permute-start | bytes 589832 | tf_op jit(solution)/shard_map/ppermute | solution.py:443
  174.0 13.0 %collective-permute-start.28 = (bf16[192,512]{1,0:T(8,128)(2,1)S(1)}, bf16[192,512]{1,0:T(8,128)(2,1)S(1)}, u32[]{:S(2)}, u32[]{:S(2)}) collective-permute-start(bf16[192,512]{1,0:T(8,128)(2,1)S(1)} %get-tuple-element.136), channel_id=1, source_target_pairs={{4,0},{2,6},{5,1},{3,7},{12,8},{10,14},{13,9},{11,15},{20,16},{18,... | collective-permute-start | bytes 589832 | tf_op jit(solution)/shard_map/ppermute | solution.py:446
  187.0 2.9 %collective-permute-start.30 = (bf16[2,48,2048]{2,1,0:T(8,128)(2,1)S(1)}, bf16[2,48,2048]{2,1,0:T(8,128)(2,1)S(1)}, u32[]{:S(2)}, u32[]{:S(2)}) collective-permute-start(bf16[2,48,2048]{2,1,0:T(8,128)(2,1)S(1)} %get-tuple-element.140), channel_id=1, source_target_pairs={{0,1},{1,0},{2,3},{3,2},{4,5},{5,4},{6,7},{7,6},{8,9},{9,8},{10,11... | collective-permute-start | bytes 1179656 | tf_op jit(solution)/shard_map/ppermute | solution.py:451
  191.3 8.0 %collective-permute-start.31 = (bf16[48,2048]{1,0:T(8,128)(2,1)S(1)}, bf16[48,2048]{1,0:T(8,128)(2,1)S(1)}, u32[]{:S(2)}, u32[]{:S(2)}) collective-permute-start(bf16[48,2048]{1,0:T(8,128)(2,1)S(1)} %slice_bitcast_fusion.2), channel_id=1, source_target_pairs={{2,0},{4,6},{3,1},{5,7},{10,8},{12,14},{11,9},{13,15},{18,16},{20,... | collective-permute-start | bytes 589832 | tf_op jit(solution)/shard_map/ppermute | solution.py:440
  (39 other events, 502.3 us)

commit v11 on v10

--- a/solution.py
+++ b/solution.py
@@ -315,19 +315,45 @@
 
 
 def pack_kernel(n, offs, gated, up_own, up_theirs, whole, *packs):
-    depth = packs[-1].shape[1] - 2 * gated.shape[2]
+    depth = packs[0].shape[1] - 2 * gated.shape[2]
     slab = gated.shape[2]
     length = up_own.shape[0]
     whole[:length, :] = up_own[...]
     whole[length:, :] = up_theirs[...]
-    for j in range(1, n):
-        pack = packs[j - 1]
+    for j in range(2, n):
+        pack = packs[j - 2]
         columns = pl.ds(pl.multiple_of(offs[j], depth), depth)
         pack[:, :slab] = gated[1]
         pack[:, slab : 2 * slab] = gated[2]
-        if j > 1:
-            pack[:length, 2 * slab :] = up_own[:, columns]
-            pack[length:, 2 * slab :] = up_theirs[:, columns]
+        pack[:length, 2 * slab :] = up_own[:, columns]
+        pack[length:, 2 * slab :] = up_theirs[:, columns]
+
+
+def fold(rows, target, start):
+    share, width = rows.shape
+    blocks = target.shape[0] // share
+    size = width // blocks
+    for k in range(blocks):
+        target[k * share : (k + 1) * share, start:] = rows[:, k * size : (k + 1) * size]
+
+
+def unfold(folded, share):
+    return jnp.concatenate(
+        [folded[i : i + share] for i in range(0, folded.shape[0], share)], axis=1
+    )
+
+
+def first_kernel(core, own, theirs, keep, landed, gated, total, pack):
+    share = keep.shape[1]
+    slab = gated.shape[2]
+    here = pl.ds(pl.multiple_of(core[0] * share, share), share)
+    for r, source in enumerate((own, theirs)):
+        total[r] = (
+            source[here, :].astype(F32) + keep[r].astype(F32) + landed[r].astype(F32)
+        ).astype(BF16)
+    pack[:, :slab] = gated[1]
+    pack[:, slab : 2 * slab] = gated[2]
+    fold(total[1], pack, 2 * slab)
 
 
 def settle_kernel(core, fresh, own, theirs, passed, keep, landed, total, other):
@@ -341,12 +367,15 @@
     other[...] = total[1]
 
 
-def gather_kernel(n, core, offs, fresh, mine, theirs, new_own, new_theirs, whole, *pieces):
+def gather_kernel(
+    n, core, offs, fresh, mine, theirs, new_own, new_theirs, other, whole, *pieces
+):
     assemble(core[0], fresh[0], mine, theirs, new_own, new_theirs, whole)
-    depth = pieces[0].shape[1]
+    depth = pieces[-1].shape[1]
     for j in range(1, n):
         columns = pl.ds(pl.multiple_of(offs[j], depth), depth)
-        pieces[j - 1][...] = whole[:, columns]
+        pieces[j - 1][:, :depth] = whole[:, columns]
+    fold(other[...], pieces[0], depth)
 
 
 def grads_kernel(n, scaling, host, offs, gated, up_0, up_1, up_own, up_near, *rest):
@@ -366,7 +395,7 @@
         jnp.where(at_host, gated[1], packs[0][:, :slab]),
         jnp.where(at_host, gated[2], packs[0][:, slab : 2 * slab]),
         jnp.where(at_host, up_0[:, columns], up_pair),
-        jnp.where(at_host, up_1[:, columns], pieces[0][...]),
+        jnp.where(at_host, up_1[:, columns], pieces[0][:, :depth]),
     )
     for m in range(1, n // 2):
         near, beyond = m, n // 2 + m - 1
@@ -627,8 +656,8 @@
         return lax.dynamic_slice_in_dim(jnp.stack([mine, others]), core_no * share, share, axis=1)
 
     pack_shapes = [struct((rows, width), BF16)]
-    pack_shapes += [struct((rows, 2 * slab), BF16)]
     pack_shapes += [struct((rows, 2 * slab + depth), BF16)] * (n - 2)
+    folded = share * width // rows
     up_0, *packs = pl.pallas_call(
         functools.partial(pack_kernel, n),
         grid=(1,),
@@ -651,19 +680,28 @@
         cost_estimate=cost(matmul // 4, weight_bytes // 4),
         name="out",
     )(core, offs, gated, *out_parts)
-    ahead_0 = summed(own_rows(x_own, x_theirs), ahead_keep, swap_cores(ahead_send))
+    ahead_landed = swap_cores(ahead_send)
+    first_shapes = [halves[0], struct((rows, 2 * slab + folded), BF16)]
+    ahead_0, partner_pack = pl.pallas_call(
+        first_kernel,
+        grid=(1,),
+        in_specs=[smem] + all_of(x_own, x_theirs, ahead_keep, ahead_landed, gated),
+        out_specs=all_of(*first_shapes),
+        out_shape=first_shapes,
+        compiler_params=small,
+        name="first",
+    )(core, x_own, x_theirs, ahead_keep, ahead_landed, gated)
     ahead_in = along_sections(ahead_0, 1)
-    packs_near = [to_partner(packs[0])] + [from_host(packs[m], m) for m in between]
+    packs_near = [to_partner(partner_pack)] + [from_host(packs[m - 1], m) for m in between]
     back_send, back_keep = backward(after(up_0, ahead_0), 0)
-    ahead_given = to_partner(ahead_0[1])
-    back_send, back_keep, ahead_in, packs_near, ahead_given = lax.optimization_barrier(
-        (back_send, back_keep, ahead_in, packs_near, ahead_given)
+    back_send, back_keep, ahead_in, packs_near = lax.optimization_barrier(
+        (back_send, back_keep, ahead_in, packs_near)
     )
     back_landed = swap_cores(back_send)
     back_0 = summed(own_rows(up_own, up_theirs), back_keep, back_landed)
     back_in = along_sections(back_0, -1)
 
-    packs_beyond = [to_beyond(packs[n // 2 + m - 1], m) for m in between]
+    packs_beyond = [to_beyond(packs[n // 2 + m - 2], m) for m in between]
     ahead_their = swap_cores(ahead_in)
     ahead_send, ahead_keep = pl.pallas_call(
         on_host(functools.partial(forward_kernel, parts, heads)),
@@ -717,23 +755,21 @@
     )
 
     back_their = swap_cores(back_in)
-    cut_shapes = [struct((rows, width), BF16)] + [struct((rows, depth), BF16)] * (n - 1)
+    cut_shapes = [struct((rows, width), BF16), struct((rows, depth + folded), BF16)]
+    cut_shapes += [struct((rows, depth), BF16)] * (n - 2)
     up_1, *cuts = pl.pallas_call(
         functools.partial(gather_kernel, n),
         grid=(1,),
-        in_specs=[smem] * 3 + all_of(back_in, back_their, new_own, new_theirs),
+        in_specs=[smem] * 3 + all_of(back_in, back_their, new_own, new_theirs, ahead_other),
         out_specs=all_of(*cut_shapes),
         out_shape=cut_shapes,
         compiler_params=small,
         name="gather",
-    )(core, offs, last_flag, back_in, back_their, new_own, new_theirs)
+    )(core, offs, last_flag, back_in, back_their, new_own, new_theirs, ahead_other)
     landed = [to_partner(cuts[0])] + [from_host(cuts[m], m) for m in between]
     landed += [to_beyond(cuts[n // 2 + m - 1], m) for m in between]
     back_send, back_keep = backward(up_1, 1)
-    ahead_last = to_partner(ahead_other)
-    back_send, back_keep, landed, ahead_last = lax.optimization_barrier(
-        (back_send, back_keep, landed, ahead_last)
-    )
+    back_send, back_keep, landed = lax.optimization_barrier((back_send, back_keep, landed))
     back_1 = summed(
         jnp.where(last_section, new_rows, back_in), back_keep, swap_cores(back_send)
     )
@@ -753,13 +789,13 @@
         host_flag, offs, after(gated, back_1), up_0, up_1, up_own, up_near, *packs_near, *packs_beyond, *landed
     )
 
-    ahead_given, back_given, ahead_last = lax.optimization_barrier(
-        (ahead_given, back_given, ahead_last, back_1)
+    first_pack, last_cut, back_given = lax.optimization_barrier(
+        (packs_near[0], landed[0], back_given, grads)
     )[:3]
     ahead = jnp.stack(
         [
-            jnp.where(is_host, ahead_0[0], ahead_given),
-            jnp.where(is_host, ahead_1[0], ahead_last),
+            jnp.where(is_host, ahead_0[0], unfold(first_pack[:, 2 * slab :], share)),
+            jnp.where(is_host, ahead_1[0], unfold(last_cut[:, depth:], share)),
         ]
     )
     back = jnp.stack(

time: 202 us -> 205 us (1.015)
  waiting for transfers between devices: 100 us -> 108 us
  starting transfers between devices: 60.3 us -> 56.4 us
    ppermute x7 -> x5, waiting for transfers between devices: 27.5 us -> 30.9 us  [to_partner(): return lax.ppermute(x, 'dp', [(h, h ^ 1) for h in hosts])]
    ppermute x7 -> x5, starting transfers between devices: 9.14 us -> 6.45 us  [to_partner(): return lax.ppermute(x, 'dp', [(h, h ^ 1) for h in hosts])]
  transfers between devices with their start and end apart: 32 -> 30, of which waited for: 16 -> 15; matrix products, arithmetic and copies ran while one was open for 6% -> 5% of each run, Pallas kernels for 6% -> 5%
where the time goes in v11:
time: 205 us; the launch traced here: 203 us
  waiting for transfers between devices  108 us (53%)
  starting transfers between devices  56.4 us (28%)
  local copies, waits for them, and re-layouts  14.2 us (7%)
  Pallas kernels  14 us (7%)
  other arithmetic  7.66 us (4%)
  between operations  3.41 us (2%)
    ppermute x8, waiting for transfers between devices, from_partner(): return lax.ppermute(x, 'dp', [(h ^ 1, h) for h in hosts])  54.4 us
    ppermute x8, starting transfers between devices, from_partner(): return lax.ppermute(x, 'dp', [(h ^ 1, h) for h in hosts])  32.1 us
    ppermute x5, waiting for transfers between devices, to_partner(): return lax.ppermute(x, 'dp', [(h, h ^ 1) for h in hosts])  30.9 us
    ppermute x2, waiting for transfers between devices, to_beyond(): lax.ppermute(x, 'dp', [(hosts[k ^ m], hosts[k] ^ 1) for k in range(n // 2)])  18.5 us
    unnamed x78, local copies, waits for them, and re-layouts  9.15 us
    ppermute x7, starting transfers between devices, from_host(): lax.ppermute(x, 'dp', [(hosts[k ^ m], hosts[k]) for k in range(n // 2)])  6.99 us
    ppermute x5, starting transfers between devices, to_partner(): return lax.ppermute(x, 'dp', [(h, h ^ 1) for h in hosts])  6.45 us
    ppermute x6, starting transfers between devices, swap_cores(): return lax.ppermute(x, 'cores', [(c, cores - 1 - c) for c in range(cores)])  5.16 us
  transfers between devices with their start and end apart: 30, of which 15 were waited for; matrix products, arithmetic and copies ran while one was open for 5% of the time, Pallas kernels for 5%

profile of v11, /device:TPU:5, one launch (start us, length us, event | category | flops | bytes accessed | tf_op | source)
XLA Modules:
  0.0 203.2 jit_solution(8492796668490022873)
XLA Ops:
  1.6 3.1 %slice_bitcast_fusion = (bf16[256,2048]{1,0:T(8,128)(2,1)}, bf16[256,2048]{1,0:T(8,128)(2,1)}) fusion(bf16[1,512,2048]{2,1,0:T(8,128)(2,1)} %param.17), kind=kLoop, calls=%fused_computation | loop fusion | bytes 4194304 | tf_op jit(solution)/shard_map/slice | solution.py:499
  4.7 6.6 %collective-permute-start.1 = (bf16[256,2048]{1,0:T(8,128)(2,1)}, bf16[256,2048]{1,0:T(8,128)(2,1)}, u32[]{:S(2)}, u32[]{:S(2)}) collective-permute-start(bf16[256,2048]{1,0:T(8,128)(2,1)} %get-tuple-element.150), channel_id=1, source_target_pairs={{0,2},{6,4},{1,3},{7,5},{8,10},{14,12},{9,11},{15,13},{16,18},{22,... | collective-permute-start | bytes 3145736 | tf_op jit(solution)/shard_map/ppermute | solution.py:466
  11.3 2.3 %collective-permute-start.2 = (bf16[256,2048]{1,0:T(8,128)(2,1)}, bf16[256,2048]{1,0:T(8,128)(2,1)}, u32[]{:S(2)}, u32[]{:S(2)}) collective-permute-start(bf16[256,2048]{1,0:T(8,128)(2,1)} %get-tuple-element.149), channel_id=1, source_target_pairs={{0,2},{6,4},{1,3},{7,5},{8,10},{14,12},{9,11},{15,13},{16,18},{22,... | collective-permute-start | bytes 3145736 | tf_op jit(solution)/shard_map/ppermute | solution.py:466
  18.5 13.6 %collective-permute-done.1.refs_8_.refs_18_.refs_11_ = bf16[256,2048]{1,0:T(8,128)(2,1)} collective-permute-done((bf16[256,2048]{1,0:T(8,128)(2,1)}, bf16[256,2048]{1,0:T(8,128)(2,1)}, u32[]{:S(2)}, u32[]{:S(2)}) %collective-permute-start.1) | collective-permute-done | bytes 1048608 | tf_op jit(solution)/shard_map/ppermute | solution.py:466
  32.2 1.6 collective-permute-start.7
  33.8 20.8 %collective-permute-done.2.refs_9_.refs_19_.refs_12_ = bf16[256,2048]{1,0:T(8,128)(2,1)} collective-permute-done((bf16[256,2048]{1,0:T(8,128)(2,1)}, bf16[256,2048]{1,0:T(8,128)(2,1)}, u32[]{:S(2)}, u32[]{:S(2)}) %collective-permute-start.2) | collective-permute-done | bytes 1048608 | tf_op jit(solution)/shard_map/ppermute | solution.py:466
  55.2 4.1 %collective-permute-start.6 = (s32[2,5,17]{2,0,1:T(2,128)S(1)}, s32[2,5,17]{2,0,1:T(2,128)S(1)}, u32[]{:S(2)}, u32[]{:S(2)}) collective-permute-start(s32[2,5,17]{2,0,1:T(2,128)S(1)} %add_add_fusion), channel_id=1, source_target_pairs={{0,2},{6,4},{1,3},{7,5},{8,10},{14,12},{9,11},{15,13},{16,18},{22,... | collective-permute-start | bytes 2048 | tf_op jit(solution)/shard_map/ppermute | solution.py:466
  59.3 2.2 %collective-permute-start.4 = (bf16[2,96,2048]{2,1,0:T(8,128)(2,1)}, bf16[2,96,2048]{2,1,0:T(8,128)(2,1)}, u32[]{:S(2)}, u32[]{:S(2)}) collective-permute-start(bf16[2,96,2048]{2,1,0:T(8,128)(2,1)} %bitcast.12.refs_3_.refs_10_), channel_id=1, source_target_pairs={{0,2},{6,4},{1,3},{7,5},{8,10},{14,12},{9,11},{15,13},{16,18},{22,... | collective-permute-start | bytes 2359304 | tf_op jit(solution)/shard_map/ppermute | solution.py:466
  61.5 1.7 collective-permute-start.8
  63.2 1.7 slice_select_fusion
  65.8 4.9 %collective-permute-start.3 = (bf16[96,2048]{1,0:T(8,128)(2,1)S(1)}, bf16[96,2048]{1,0:T(8,128)(2,1)}, u32[]{:S(2)}, u32[]{:S(2)}) collective-permute-start(bf16[96,2048]{1,0:T(8,128)(2,1)S(1)} %get-tuple-element.152.refs_1_.own), channel_id=1, source_target_pairs={{0,2},{6,4},{1,3},{7,5},{8,10},{14,12},{9,11},{15,13},{16,18},{22,... | collective-permute-start | bytes 1179656 | tf_op jit(solution)/shard_map/ppermute | solution.py:466
  72.9 9.9 %collective-permute-done.4.refs_4_.refs_11_ = bf16[2,96,2048]{2,1,0:T(8,128)(2,1)} collective-permute-done((bf16[2,96,2048]{2,1,0:T(8,128)(2,1)}, bf16[2,96,2048]{2,1,0:T(8,128)(2,1)}, u32[]{:S(2)}, u32[]{:S(2)}) %collective-permute-start.4) | collective-permute-done | bytes 786464 | tf_op jit(solution)/shard_map/ppermute | solution.py:466
  83.6 5.5 %collective-permute-start.11 = (bf16[96,2048]{1,0:T(8,128)(2,1)S(1)}, bf16[96,2048]{1,0:T(8,128)(2,1)S(1)}, u32[]{:S(2)}, u32[]{:S(2)}) collective-permute-start(bf16[96,2048]{1,0:T(8,128)(2,1)S(1)} %bitcast.107), channel_id=1, source_target_pairs={{0,2},{6,4},{1,3},{7,5},{8,10},{14,12},{9,11},{15,13},{16,18},{22,... | collective-permute-start | bytes 1179656 | tf_op jit(solution)/shard_map/ppermute | solution.py:466
  89.1 2.1 %collective-permute-done.3.refs_2_.theirs = bf16[96,2048]{1,0:T(8,128)(2,1)} collective-permute-done((bf16[96,2048]{1,0:T(8,128)(2,1)S(1)}, bf16[96,2048]{1,0:T(8,128)(2,1)}, u32[]{:S(2)}, u32[]{:S(2)}) %collective-permute-start.3) | collective-permute-done | bytes 393248 | tf_op jit(solution)/shard_map/ppermute | solution.py:466
  92.5 5.2 %collective-permute-start.9 = (bf16[96,2048]{1,0:T(8,128)(2,1)S(1)}, bf16[96,2048]{1,0:T(8,128)(2,1)S(1)}, u32[]{:S(2)}, u32[]{:S(2)}) collective-permute-start(bf16[96,2048]{1,0:T(8,128)(2,1)S(1)} %bitcast.96), channel_id=1, source_target_pairs={{0,2},{6,4},{1,3},{7,5},{8,10},{14,12},{9,11},{15,13},{16,18},{22,... | collective-permute-start | bytes 1179656 | tf_op jit(solution)/shard_map/ppermute | solution.py:466
  98.7 2.2 %project.1 = (bf16[3,192,512]{2,1,0:T(8,128)(2,1)S(1)}, f32[2,192,512]{2,1,0:T(8,128)}, bf16[2,192,1536]{2,1,0:T(8,128)(2,1)}, f32[2,192,2048]{2,1,0:T(8,128)}, ...) custom-call(s32[1]{0:T(128)} %bitcast.8.host, s32[6]{0:T(128)S(1)} %stack.83.refs_0_.refs_1_, ...), custom_call_target="tpu_custom_call" | custom-call | flops 4831838208 | bytes 20971520 | tf_op jit(solution)/shard_map/project/pallas_call | solution.py:607
  100.9 7.1 %collective-permute-done.9.refs_7_.theirs.new_theirs = bf16[96,2048]{1,0:T(8,128)(2,1)S(1)} collective-permute-done((bf16[96,2048]{1,0:T(8,128)(2,1)S(1)}, bf16[96,2048]{1,0:T(8,128)(2,1)S(1)}, u32[]{:S(2)}, u32[]{:S(2)}) %collective-permute-start.9) | collective-permute-done | bytes 393248 | tf_op jit(solution)/shard_map/ppermute | solution.py:466
  110.7 1.9 collective-permute-start.14
  116.6 1.4 collective-permute-start.15
  118.0 1.6 backward.2
  121.2 19.0 %collective-permute-done.16.rest_0_ = bf16[192,1536]{1,0:T(8,128)(2,1)S(1)} collective-permute-done((bf16[192,1536]{1,0:T(8,128)(2,1)S(1)}, bf16[192,1536]{1,0:T(8,128)(2,1)S(1)}, u32[]{:S(2)}, u32[]{:S(2)}) %collective-permute-start.16) | collective-permute-done | bytes 589856 | tf_op jit(solution)/shard_map/ppermute | solution.py:469
  141.9 1.6 collective-permute-start.22
  144.9 1.4 collective-permute-start.21
  146.3 1.4 forward.1
  152.3 7.7 %collective-permute-done.22.rest_2_ = bf16[192,1536]{1,0:T(8,128)(2,1)S(1)} collective-permute-done((bf16[192,1536]{1,0:T(8,128)(2,1)}, bf16[192,1536]{1,0:T(8,128)(2,1)S(1)}, u32[]{:S(2)}, u32[]{:S(2)}) %collective-permute-start.22) | collective-permute-done | bytes 589856 | tf_op jit(solution)/shard_map/ppermute | solution.py:475
  160.8 4.8 %collective-permute-done.23 = bf16[48,2048]{1,0:T(8,128)(2,1)S(1)} collective-permute-done((bf16[48,2048]{1,0:T(8,128)(2,1)S(1)}, bf16[48,2048]{1,0:T(8,128)(2,1)S(1)}, u32[]{:S(2)}, u32[]{:S(2)}) %collective-permute-start.23) | collective-permute-done | bytes 196640 | tf_op jit(solution)/shard_map/ppermute | solution.py:469
  166.8 1.7 collective-permute-done.24.theirs
  176.0 10.8 %collective-permute-done.27.rest_5_ = bf16[192,512]{1,0:T(8,128)(2,1)S(1)} collective-permute-done((bf16[192,512]{1,0:T(8,128)(2,1)S(1)}, bf16[192,512]{1,0:T(8,128)(2,1)S(1)}, u32[]{:S(2)}, u32[]{:S(2)}) %collective-permute-start.27) | collective-permute-done | bytes 196640 | tf_op jit(solution)/shard_map/ppermute | solution.py:475
  186.8 1.4 collective-permute-done.25.rest_3_
  189.4 1.3 collective-permute-done.28
  192.1 2.3 %grads.1 = f32[512,512]{1,0:T(8,128)} custom-call(s32[1]{0:T(128)} %bitcast.8.host, s32[4]{0:T(128)S(1)} %add_multiply_fusion.offs.refs_2_, bf16[3,192,512]{2,1,0:T(8,128)(2,1)S(1)} %get-tuple-element.139.gated, bf16[192,2048]{1,0:T(8,128)(2,1)S(1)} %copy-done.6, bf16[192,2048]{1,0:T(8,128)(2,1)S(1)} %get-tuple-element.129.refs_3_.up_1, ...), custom_call_target="tpu_custom_call" | custom-call | flops 402653184 | bytes 2621440 | tf_op jit(solution)/shard_map/grads/pallas_call | solution.py:777
  196.6 5.8 %collective-permute-done.29 = bf16[48,2048]{1,0:T(8,128)(2,1)S(1)} collective-permute-done((bf16[48,2048]{1,0:T(8,128)(2,1)S(1)}, bf16[48,2048]{1,0:T(8,128)(2,1)S(1)}, u32[]{:S(2)}, u32[]{:S(2)}) %collective-permute-start.29) | collective-permute-done | bytes 196640 | tf_op jit(solution)/shard_map/ppermute | solution.py:469
  (159 shorter events, 41.1 us)
Async XLA Ops:
  0.7 54.1 %copy-start.38 = (s32[1,5]{1,0:T(1,128)S(1)}, s32[1,5]{1,0:T(1,128)}, u32[]{:S(2)}) copy-start(s32[1,5]{1,0:T(1,128)} %param.20) | copy-start | bytes 64
  0.7 54.2 %copy-start.35 = (s32[1,5,4,4]{1,3,2,0:T(4,128)S(1)}, s32[1,5,4,4]{1,3,2,0:T(4,128)}, u32[]{:S(2)}) copy-start(s32[1,5,4,4]{1,3,2,0:T(4,128)} %param.22) | copy-start | bytes 964
  0.7 53.9 %collective-permute-start = (bf16[512,2048]{1,0:T(8,128)(2,1)}, bf16[512,2048]{1,0:T(8,128)(2,1)S(1)}, u32[]{:S(2)}, u32[]{:S(2)}) collective-permute-start(bf16[512,2048]{1,0:T(8,128)(2,1)} %bitcast.112), channel_id=1, source_target_pairs={{4,2},{2,4},{5,3},{3,5},{12,10},{10,12},{13,11},{11,13},{20,18},{1... | collective-permute-start | bytes 6291464 | tf_op jit(solution)/shard_map/ppermute | solution.py:472
  4.7 27.4 %collective-permute-start.1 = (bf16[256,2048]{1,0:T(8,128)(2,1)}, bf16[256,2048]{1,0:T(8,128)(2,1)}, u32[]{:S(2)}, u32[]{:S(2)}) collective-permute-start(bf16[256,2048]{1,0:T(8,128)(2,1)} %get-tuple-element.150), channel_id=1, source_target_pairs={{0,2},{6,4},{1,3},{7,5},{8,10},{14,12},{9,11},{15,13},{16,18},{22,... | collective-permute-start | bytes 3145736 | tf_op jit(solution)/shard_map/ppermute | solution.py:466
  11.3 43.3 %collective-permute-start.2 = (bf16[256,2048]{1,0:T(8,128)(2,1)}, bf16[256,2048]{1,0:T(8,128)(2,1)}, u32[]{:S(2)}, u32[]{:S(2)}) collective-permute-start(bf16[256,2048]{1,0:T(8,128)(2,1)} %get-tuple-element.149), channel_id=1, source_target_pairs={{0,2},{6,4},{1,3},{7,5},{8,10},{14,12},{9,11},{15,13},{16,18},{22,... | collective-permute-start | bytes 3145736 | tf_op jit(solution)/shard_map/ppermute | solution.py:466
  13.6 52.2 %collective-permute-start.5 = (bf16[512,512]{1,0:T(8,128)(2,1)S(1)}, bf16[512,512]{1,0:T(8,128)(2,1)S(1)}, u32[]{:S(2)}, u32[]{:S(2)}) collective-permute-start(bf16[512,512]{1,0:T(8,128)(2,1)S(1)} %bitcast.100), channel_id=1, source_target_pairs={{0,2},{6,4},{1,3},{7,5},{8,10},{14,12},{9,11},{15,13},{16,18},{22,... | collective-permute-start | bytes 1572872 | tf_op jit(solution)/shard_map/ppermute | solution.py:466
  32.2 51.4 %collective-permute-start.7 = (bf16[256,2048]{1,0:T(8,128)(2,1)}, bf16[256,2048]{1,0:T(8,128)(2,1)}, u32[]{:S(2)}, u32[]{:S(2)}) collective-permute-start(bf16[256,2048]{1,0:T(8,128)(2,1)} %collective-permute-done.1.refs_8_.refs_18_.refs_11_), channel_id=1, source_target_pairs={{4,2},{2,4},{5,3},{3,5},{12,10},{10,12},{13,11},{11,13},{20,18},{1... | collective-permute-start | bytes 3145736 | tf_op jit(solution)/shard_map/ppermute | solution.py:472
  55.2 15.6 %collective-permute-start.6 = (s32[2,5,17]{2,0,1:T(2,128)S(1)}, s32[2,5,17]{2,0,1:T(2,128)S(1)}, u32[]{:S(2)}, u32[]{:S(2)}) collective-permute-start(s32[2,5,17]{2,0,1:T(2,128)S(1)} %add_add_fusion), channel_id=1, source_target_pairs={{0,2},{6,4},{1,3},{7,5},{8,10},{14,12},{9,11},{15,13},{16,18},{22,... | collective-permute-start | bytes 2048 | tf_op jit(solution)/shard_map/ppermute | solution.py:466
  59.3 23.6 %collective-permute-start.4 = (bf16[2,96,2048]{2,1,0:T(8,128)(2,1)}, bf16[2,96,2048]{2,1,0:T(8,128)(2,1)}, u32[]{:S(2)}, u32[]{:S(2)}) collective-permute-start(bf16[2,96,2048]{2,1,0:T(8,128)(2,1)} %bitcast.12.refs_3_.refs_10_), channel_id=1, source_target_pairs={{0,2},{6,4},{1,3},{7,5},{8,10},{14,12},{9,11},{15,13},{16,18},{22,... | collective-permute-start | bytes 2359304 | tf_op jit(solution)/shard_map/ppermute | solution.py:466
  61.5 31.0 %collective-permute-start.8 = (bf16[256,2048]{1,0:T(8,128)(2,1)}, bf16[256,2048]{1,0:T(8,128)(2,1)}, u32[]{:S(2)}, u32[]{:S(2)}) collective-permute-start(bf16[256,2048]{1,0:T(8,128)(2,1)} %collective-permute-done.2.refs_9_.refs_19_.refs_12_), channel_id=1, source_target_pairs={{4,2},{2,4},{5,3},{3,5},{12,10},{10,12},{13,11},{11,13},{20,18},{1... | collective-permute-start | bytes 3145736 | tf_op jit(solution)/shard_map/ppermute | solution.py:472
  65.8 25.4 %collective-permute-start.3 = (bf16[96,2048]{1,0:T(8,128)(2,1)S(1)}, bf16[96,2048]{1,0:T(8,128)(2,1)}, u32[]{:S(2)}, u32[]{:S(2)}) collective-permute-start(bf16[96,2048]{1,0:T(8,128)(2,1)S(1)} %get-tuple-element.152.refs_1_.own), channel_id=1, source_target_pairs={{0,2},{6,4},{1,3},{7,5},{8,10},{14,12},{9,11},{15,13},{16,18},{22,... | collective-permute-start | bytes 1179656 | tf_op jit(solution)/shard_map/ppermute | solution.py:466
  71.7 37.8 %collective-permute-start.12 = (bf16[512,512]{1,0:T(8,128)(2,1)S(1)}, bf16[512,512]{1,0:T(8,128)(2,1)S(1)}, u32[]{:S(2)}, u32[]{:S(2)}) collective-permute-start(bf16[512,512]{1,0:T(8,128)(2,1)S(1)} %bitcast.101), channel_id=1, source_target_pairs={{4,2},{2,4},{5,3},{3,5},{12,10},{10,12},{13,11},{11,13},{20,18},{1... | collective-permute-start | bytes 1572872 | tf_op jit(solution)/shard_map/ppermute | solution.py:472
  82.8 26.7 %collective-permute-start.13 = (bf16[512,512]{1,0:T(8,128)(2,1)S(1)}, bf16[512,512]{1,0:T(8,128)(2,1)S(1)}, u32[]{:S(2)}, u32[]{:S(2)}) collective-permute-start(bf16[512,512]{1,0:T(8,128)(2,1)S(1)} %collective-permute-done.5.rest_1_.refs_13_.refs_16_), channel_id=1, source_target_pairs={{4,2},{2,4},{5,3},{3,5},{12,10},{10,12},{13,11},{11,13},{20,18},{1... | collective-permute-start | bytes 1572872 | tf_op jit(solution)/shard_map/ppermute | solution.py:472
  83.6 24.5 %collective-permute-start.11 = (bf16[96,2048]{1,0:T(8,128)(2,1)S(1)}, bf16[96,2048]{1,0:T(8,128)(2,1)S(1)}, u32[]{:S(2)}, u32[]{:S(2)}) collective-permute-start(bf16[96,2048]{1,0:T(8,128)(2,1)S(1)} %bitcast.107), channel_id=1, source_target_pairs={{0,2},{6,4},{1,3},{7,5},{8,10},{14,12},{9,11},{15,13},{16,18},{22,... | collective-permute-start | bytes 1179656 | tf_op jit(solution)/shard_map/ppermute | solution.py:466
  91.2 9.8 %collective-permute-start.10 = (bf16[96,512]{1,0:T(8,128)(2,1)S(1)}, bf16[96,512]{1,0:T(8,128)(2,1)S(1)}, u32[]{:S(2)}, u32[]{:S(2)}) collective-permute-start(bf16[96,512]{1,0:T(8,128)(2,1)S(1)} %constant_dynamic-slice_fusion.2), channel_id=1, source_target_pairs={{2,0},{4,6},{3,1},{5,7},{10,8},{12,14},{11,9},{13,15},{18,16},{20,... | collective-permute-start | bytes 294920 | tf_op jit(solution)/shard_map/ppermute | solution.py:469
  92.5 15.6 %collective-permute-start.9 = (bf16[96,2048]{1,0:T(8,128)(2,1)S(1)}, bf16[96,2048]{1,0:T(8,128)(2,1)S(1)}, u32[]{:S(2)}, u32[]{:S(2)}) collective-permute-start(bf16[96,2048]{1,0:T(8,128)(2,1)S(1)} %bitcast.96), channel_id=1, source_target_pairs={{0,2},{6,4},{1,3},{7,5},{8,10},{14,12},{9,11},{15,13},{16,18},{22,... | collective-permute-start | bytes 1179656 | tf_op jit(solution)/shard_map/ppermute | solution.py:466
  110.7 3.3 %collective-permute-start.14 = (bf16[2,48,2048]{2,1,0:T(8,128)(2,1)S(1)}, bf16[2,48,2048]{2,1,0:T(8,128)(2,1)S(1)}, u32[]{:S(2)}, u32[]{:S(2)}) collective-permute-start(bf16[2,48,2048]{2,1,0:T(8,128)(2,1)S(1)} %get-tuple-element.103), channel_id=1, source_target_pairs={{0,1},{1,0},{2,3},{3,2},{4,5},{5,4},{6,7},{7,6},{8,9},{9,8},{10,11... | collective-permute-start | bytes 1179656 | tf_op jit(solution)/shard_map/ppermute | solution.py:480
  112.6 7.8 %collective-permute-start.17 = (bf16[192,1536]{1,0:T(8,128)(2,1)S(1)}, bf16[192,1536]{1,0:T(8,128)(2,1)S(1)}, u32[]{:S(2)}, u32[]{:S(2)}) collective-permute-start(bf16[192,1536]{1,0:T(8,128)(2,1)S(1)} %get-tuple-element.116), channel_id=1, source_target_pairs={{4,2},{2,4},{5,3},{3,5},{12,10},{10,12},{13,11},{11,13},{20,18},{1... | collective-permute-start | bytes 1769480 | tf_op jit(solution)/shard_map/ppermute | solution.py:472
  115.3 24.9 %collective-permute-start.16 = (bf16[192,1536]{1,0:T(8,128)(2,1)S(1)}, bf16[192,1536]{1,0:T(8,128)(2,1)S(1)}, u32[]{:S(2)}, u32[]{:S(2)}) collective-permute-start(bf16[192,1536]{1,0:T(8,128)(2,1)S(1)} %get-tuple-element.115), channel_id=1, source_target_pairs={{2,0},{4,6},{3,1},{5,7},{10,8},{12,14},{11,9},{13,15},{18,16},{20,... | collective-permute-start | bytes 1769480 | tf_op jit(solution)/shard_map/ppermute | solution.py:469
  116.6 4.6 %collective-permute-start.15 = (bf16[2,48,2048]{2,1,0:T(8,128)(2,1)S(1)}, bf16[2,48,2048]{2,1,0:T(8,128)(2,1)}, u32[]{:S(2)}, u32[]{:S(2)}) collective-permute-start(bf16[2,48,2048]{2,1,0:T(8,128)(2,1)S(1)} %get-tuple-element.104), channel_id=1, source_target_pairs={{2,10},{4,12},{10,18},{12,20},{18,26},{20,28},{3,11},{5,13},{11,19... | collective-permute-start | bytes 1179656 | tf_op jit(solution)/shard_map/ppermute | solution.py:489
  141.1 2.5 %collective-permute-start.20 = (bf16[2,48,2048]{2,1,0:T(8,128)(2,1)}, bf16[2,48,2048]{2,1,0:T(8,128)(2,1)}, u32[]{:S(2)}, u32[]{:S(2)}) collective-permute-start(bf16[2,48,2048]{2,1,0:T(8,128)(2,1)} %get-tuple-element.125), channel_id=1, source_target_pairs={{0,1},{1,0},{2,3},{3,2},{4,5},{5,4},{6,7},{7,6},{8,9},{9,8},{10,11... | collective-permute-start | bytes 1179656 | tf_op jit(solution)/shard_map/ppermute | solution.py:480
  141.9 18.1 %collective-permute-start.22 = (bf16[192,1536]{1,0:T(8,128)(2,1)}, bf16[192,1536]{1,0:T(8,128)(2,1)S(1)}, u32[]{:S(2)}, u32[]{:S(2)}) collective-permute-start(bf16[192,1536]{1,0:T(8,128)(2,1)} %copy-done.28), channel_id=1, source_target_pairs={{4,0},{2,6},{5,1},{3,7},{12,8},{10,14},{13,9},{11,15},{20,16},{18,... | collective-permute-start | bytes 1769480 | tf_op jit(solution)/shard_map/ppermute | solution.py:475
  143.5 2.8 %collective-permute-start.18 = (bf16[2,48,2048]{2,1,0:T(8,128)(2,1)}, bf16[2,48,2048]{2,1,0:T(8,128)(2,1)S(1)}, u32[]{:S(2)}, u32[]{:S(2)}) collective-permute-start(bf16[2,48,2048]{2,1,0:T(8,128)(2,1)} %collective-permute-done.15.refs_4_.passed), channel_id=1, source_target_pairs={{0,1},{1,0},{2,3},{3,2},{4,5},{5,4},{6,7},{7,6},{8,9},{9,8},{10,11... | collective-permute-start | bytes 1179656 | tf_op jit(solution)/shard_map/ppermute | solution.py:480
  144.9 20.7 %collective-permute-start.21 = (bf16[2,48,2048]{2,1,0:T(8,128)(2,1)S(1)}, bf16[2,48,2048]{2,1,0:T(8,128)(2,1)}, u32[]{:S(2)}, u32[]{:S(2)}) collective-permute-start(bf16[2,48,2048]{2,1,0:T(8,128)(2,1)S(1)} %add_convert_fusion.1), channel_id=1, source_target_pairs={{10,2},{12,4},{18,10},{20,12},{26,18},{28,20},{11,3},{13,5},{19,11... | collective-permute-start | bytes 1179656 | tf_op jit(solution)/shard_map/ppermute | solution.py:489
  147.7 1.9 collective-permute-start.19
  148.3 17.3 %collective-permute-start.23 = (bf16[48,2048]{1,0:T(8,128)(2,1)S(1)}, bf16[48,2048]{1,0:T(8,128)(2,1)S(1)}, u32[]{:S(2)}, u32[]{:S(2)}) collective-permute-start(bf16[48,2048]{1,0:T(8,128)(2,1)S(1)} %slice_bitcast_fusion.5), channel_id=1, source_target_pairs={{2,0},{4,6},{3,1},{5,7},{10,8},{12,14},{11,9},{13,15},{18,16},{20,... | collective-permute-start | bytes 589832 | tf_op jit(solution)/shard_map/ppermute | solution.py:469
  166.2 2.3 %collective-permute-start.24 = (bf16[2,48,2048]{2,1,0:T(8,128)(2,1)}, bf16[2,48,2048]{2,1,0:T(8,128)(2,1)}, u32[]{:S(2)}, u32[]{:S(2)}) collective-permute-start(bf16[2,48,2048]{2,1,0:T(8,128)(2,1)} %collective-permute-done.21.mine), channel_id=1, source_target_pairs={{0,1},{1,0},{2,3},{3,2},{4,5},{5,4},{6,7},{7,6},{8,9},{9,8},{10,11... | collective-permute-start | bytes 1179656 | tf_op jit(solution)/shard_map/ppermute | solution.py:480
  171.7 16.4 %collective-permute-start.25 = (bf16[192,1024]{1,0:T(8,128)(2,1)S(1)}, bf16[192,1024]{1,0:T(8,128)(2,1)S(1)}, u32[]{:S(2)}, u32[]{:S(2)}) collective-permute-start(bf16[192,1024]{1,0:T(8,128)(2,1)S(1)} %get-tuple-element.132), channel_id=1, source_target_pairs={{2,0},{4,6},{3,1},{5,7},{10,8},{12,14},{11,9},{13,15},{18,16},{20,... | collective-permute-start | bytes 1179656 | tf_op jit(solution)/shard_map/ppermute | solution.py:469
  173.0 3.0 %collective-permute-start.26 = (bf16[192,512]{1,0:T(8,128)(2,1)S(1)}, bf16[192,512]{1,0:T(8,128)(2,1)S(1)}, u32[]{:S(2)}, u32[]{:S(2)}) collective-permute-start(bf16[192,512]{1,0:T(8,128)(2,1)S(1)} %get-tuple-element.133), channel_id=1, source_target_pairs={{4,2},{2,4},{5,3},{3,5},{12,10},{10,12},{13,11},{11,13},{20,18},{1... | collective-permute-start | bytes 589832 | tf_op jit(solution)/shard_map/ppermute | solution.py:472
  173.7 13.1 %collective-permute-start.27 = (bf16[192,512]{1,0:T(8,128)(2,1)S(1)}, bf16[192,512]{1,0:T(8,128)(2,1)S(1)}, u32[]{:S(2)}, u32[]{:S(2)}) collective-permute-start(bf16[192,512]{1,0:T(8,128)(2,1)S(1)} %get-tuple-element.134), channel_id=1, source_target_pairs={{4,0},{2,6},{5,1},{3,7},{12,8},{10,14},{13,9},{11,15},{20,16},{18,... | collective-permute-start | bytes 589832 | tf_op jit(solution)/shard_map/ppermute | solution.py:475
  188.2 2.6 %collective-permute-start.28 = (bf16[2,48,2048]{2,1,0:T(8,128)(2,1)S(1)}, bf16[2,48,2048]{2,1,0:T(8,128)(2,1)S(1)}, u32[]{:S(2)}, u32[]{:S(2)}) collective-permute-start(bf16[2,48,2048]{2,1,0:T(8,128)(2,1)S(1)} %get-tuple-element.138), channel_id=1, source_target_pairs={{0,1},{1,0},{2,3},{3,2},{4,5},{5,4},{6,7},{7,6},{8,9},{9,8},{10,11... | collective-permute-start | bytes 1179656 | tf_op jit(solution)/shard_map/ppermute | solution.py:480
  194.4 8.0 %collective-permute-start.29 = (bf16[48,2048]{1,0:T(8,128)(2,1)S(1)}, bf16[48,2048]{1,0:T(8,128)(2,1)S(1)}, u32[]{:S(2)}, u32[]{:S(2)}) collective-permute-start(bf16[48,2048]{1,0:T(8,128)(2,1)S(1)} %slice_bitcast_fusion.2), channel_id=1, source_target_pairs={{2,0},{4,6},{3,1},{5,7},{10,8},{12,14},{11,9},{13,15},{18,16},{20,... | collective-permute-start | bytes 589832 | tf_op jit(solution)/shard_map/ppermute | solution.py:469
  (37 other events, 387.0 us)

commit v12 on v11

--- a/solution.py
+++ b/solution.py
@@ -216,20 +216,40 @@
         split_rows(core[0], part, send, kept)
 
 
-def backward_kernel(parts, n, tick, core, in_offs, offs, *rest):
-    count = 9 + n + parts
-    sources, rest = rest[:count], rest[count:]
+def backward_kernel(parts, n, tick, split, core, in_offs, offs, *rest):
+    count = 8 + n + parts
+    up_sources, rest = rest[: 1 + split], rest[1 + split :]
+    sources, rest = (None,) + rest[:count], rest[count:]
     send, keep = rest[:2]
-    held, (grad_normed, part, sems) = rest[2 : 2 + count], rest[2 + count :]
+    held, (grad_normed, part, up_sems, sems) = rest[2 : 3 + count], rest[3 + count :]
     ups, gate, vqk, slope, mixed, probs, factor, x_own, x_theirs = held[:9]
     out_parts, in_parts = held[9 : 9 + n], held[9 + n :]
     wide = 4 * HEAD_DIM
     heads = out_parts[0].shape[0] // HEAD_DIM
     copies = []
     for i, (source, target) in enumerate(zip(sources[: 9 + n], held[: 9 + n])):
-        if 1 <= i < 9:
+        if i == 0:
+            continue
+        if i < 9:
             source = source.at[tick]
         copies.append(pltpu.make_async_copy(source, target, sems.at[i]))
+    up_copies = []
+    if split:
+        share = up_sources[0].shape[1]
+        cores = ups.shape[0] // (2 * share)
+        for half, owner in enumerate((core[0], cores - 1 - core[0])):
+            for r in range(2):
+                at = pl.multiple_of((r * cores + owner) * share, share)
+                up_copies.append(
+                    pltpu.make_async_copy(
+                        up_sources[half].at[r],
+                        ups.at[pl.ds(at, share), :],
+                        up_sems.at[2 * half + r],
+                    )
+                )
+    else:
+        up_copies.append(pltpu.make_async_copy(up_sources[0], ups, up_sems.at[0]))
+    copies = [None] + copies
     by_head = []
     for h in range(heads):
         of_head = slice(h * wide, (h + 1) * wide)
@@ -243,8 +263,10 @@
                 for j in range(parts)
             ]
         )
-    first = [0] + list(range(9, 9 + n))
+    first = list(range(9, 9 + n))
     second = [1, 4, 2, 5, 6, 3]
+    for copy in up_copies:
+        copy.start()
     for i in first + second:
         copies[i].start()
     for of_head in by_head:
@@ -252,6 +274,8 @@
             copy.start()
     for i in (7, 8):
         copies[i].start()
+    for copy in up_copies:
+        copy.wait()
     for i in first:
         copies[i].wait()
     depth = out_parts[0].shape[1]
@@ -334,7 +358,9 @@
     blocks = target.shape[0] // share
     size = width // blocks
     for k in range(blocks):
-        target[k * share : (k + 1) * share, start:] = rows[:, k * size : (k + 1) * size]
+        target[k * share : (k + 1) * share, start : start + size] = rows[
+            :, k * size : (k + 1) * size
+        ]
 
 
 def unfold(folded, share):
@@ -356,53 +382,73 @@
     fold(total[1], pack, 2 * slab)
 
 
-def settle_kernel(core, fresh, own, theirs, passed, keep, landed, total, other):
+def last_kernel(
+    core, fresh, new_own, new_theirs, passed, keep, landed, up, up_keep, up_landed, ahead, back, pair
+):
     share = keep.shape[1]
     here = pl.ds(pl.multiple_of(core[0] * share, share), share)
-    for r, source in enumerate((own, theirs)):
+    for r, source in enumerate((new_own, new_theirs)):
         residual = jnp.where(fresh[0] != 0, source[here, :], passed[r])
-        total[r] = (
+        ahead[r] = (
             residual.astype(F32) + keep[r].astype(F32) + landed[r].astype(F32)
         ).astype(BF16)
-    other[...] = total[1]
-
-
-def gather_kernel(
-    n, core, offs, fresh, mine, theirs, new_own, new_theirs, other, whole, *pieces
+        back[r] = (
+            up[r].astype(F32) + up_keep[r].astype(F32) + up_landed[r].astype(F32)
+        ).astype(BF16)
+    pair[0] = ahead[1]
+    pair[1] = back[1]
+
+
+def cut_kernel(n, core, offs, fresh, landed, new_own, new_theirs, back, mine, *pieces):
+    share = landed.shape[1]
+    depth = pieces[-1].shape[1]
+    here = pl.ds(pl.multiple_of(core[0] * share, share), share)
+    for r, source in enumerate((new_own, new_theirs)):
+        mine[r] = jnp.where(fresh[0] != 0, source[here, :], landed[r])
+        for j in range(1, n):
+            columns = pl.ds(pl.multiple_of(offs[j], depth), depth)
+            pieces[j - 1][r * share : (r + 1) * share, :depth] = mine[r, :, columns]
+    fold(back[1], pieces[0], depth)
+
+
+def grads_kernel(
+    n, scaling, host, core, offs, gated, up_0, up_own, up_near, mine, theirs, halves, other, *rest
 ):
-    assemble(core[0], fresh[0], mine, theirs, new_own, new_theirs, whole)
-    depth = pieces[-1].shape[1]
-    for j in range(1, n):
-        columns = pl.ds(pl.multiple_of(offs[j], depth), depth)
-        pieces[j - 1][:, :depth] = whole[:, columns]
-    fold(other[...], pieces[0], depth)
-
-
-def grads_kernel(n, scaling, host, offs, gated, up_0, up_1, up_own, up_near, *rest):
     packs = rest[: n - 1]
-    pieces = rest[n - 1 : 2 * n - 2]
-    out = rest[2 * n - 2]
+    out, whole = rest[n - 1 :]
     slab = gated.shape[2]
     depth = out.shape[1]
+    share = mine.shape[1]
+    cores = whole.shape[0] // (2 * share)
     at_host = host[0] != 0
     columns = pl.ds(pl.multiple_of(offs[0], depth), depth)
 
-    def product(first, second, third, fourth):
-        return dot_tn(first, third) + dot_tn(second, fourth)
+    def product(first, second, third, upstream):
+        for half, owner in enumerate((core[0], cores - 1 - core[0])):
+            for r in range(2):
+                at = pl.multiple_of((r * cores + owner) * share, share)
+                whole[pl.ds(at, share), :] = upstream(half, r)
+        return dot_tn(first, third) + dot_tn(second, whole[...])
 
     up_pair = jnp.concatenate([up_near[...], up_own[:, columns]], axis=0)
     total = product(
         jnp.where(at_host, gated[1], packs[0][:, :slab]),
         jnp.where(at_host, gated[2], packs[0][:, slab : 2 * slab]),
         jnp.where(at_host, up_0[:, columns], up_pair),
-        jnp.where(at_host, up_1[:, columns], pieces[0][:, :depth]),
+        lambda half, r: jnp.where(
+            at_host,
+            (mine, theirs)[half][r, :, columns],
+            (halves, other)[half][0, r * share : (r + 1) * share, :],
+        ),
     )
     for m in range(1, n // 2):
         near, beyond = m, n // 2 + m - 1
         pack = jnp.where(at_host, packs[near][...], packs[beyond][...])
-        piece = jnp.where(at_host, pieces[near][...], pieces[beyond][...])
         total = total + product(
-            pack[:, :slab], pack[:, slab : 2 * slab], pack[:, 2 * slab :], piece
+            pack[:, :slab],
+            pack[:, slab : 2 * slab],
+            pack[:, 2 * slab :],
+            lambda half, r: (halves, other)[half][m, r * share : (r + 1) * share, :],
         )
     out[...] = total * scaling
 
@@ -626,26 +672,28 @@
     )(host_flag, in_offs, x_own, x_theirs, stash_own, stash_theirs, keep, *in_hbm(in_parts))
 
     def backward(ups, tick_no):
+        split = len(ups) - 1
         layered = [gate, vqk, slope, mixed, probs, factor, stash_own, stash_theirs]
         plain = list(out_parts) + list(in_parts)
         return pl.pallas_call(
-            on_host(functools.partial(backward_kernel, parts, n, tick_no)),
+            on_host(functools.partial(backward_kernel, parts, n, tick_no, split)),
             grid=(1,),
-            in_specs=[smem] * 4 + [hbm] * (1 + len(layered) + len(plain)),
+            in_specs=[smem] * 4 + [hbm] * (len(ups) + len(layered) + len(plain)),
             out_specs=all_of(*halves),
             out_shape=halves,
-            scratch_shapes=[pltpu.VMEM(ups.shape, BF16)]
+            scratch_shapes=[pltpu.VMEM((rows, width), BF16)]
             + [pltpu.VMEM(x.shape[1:], x.dtype) for x in layered]
             + [pltpu.VMEM(x.shape, x.dtype) for x in plain]
             + [
                 pltpu.VMEM((rows, width), F32),
                 pltpu.VMEM((rows, width), BF16),
+                pltpu.SemaphoreType.DMA((4,)),
                 pltpu.SemaphoreType.DMA((1 + len(layered) + n + heads * parts,)),
             ],
             compiler_params=params,
             cost_estimate=cost(2 * matmul, 2 * weight_bytes),
             name="backward",
-        )(host_flag, core, in_offs, offs, ups, *in_hbm(layered), *out_parts, *in_hbm(in_parts))
+        )(host_flag, core, in_offs, offs, *ups, *in_hbm(layered), *out_parts, *in_hbm(in_parts))
 
     gated, new_theirs, up_near = lax.optimization_barrier((gated, new_theirs, up_near))
 
@@ -693,7 +741,7 @@
     )(core, x_own, x_theirs, ahead_keep, ahead_landed, gated)
     ahead_in = along_sections(ahead_0, 1)
     packs_near = [to_partner(partner_pack)] + [from_host(packs[m - 1], m) for m in between]
-    back_send, back_keep = backward(after(up_0, ahead_0), 0)
+    back_send, back_keep = backward([after(up_0, ahead_0)], 0)
     back_send, back_keep, ahead_in, packs_near = lax.optimization_barrier(
         (back_send, back_keep, ahead_in, packs_near)
     )
@@ -736,72 +784,72 @@
         *in_hbm(in_parts),
         *out_parts,
     )
-    new_rows = own_rows(new_own, new_theirs)
+    ahead_send, ahead_keep, back_in, packs_beyond = lax.optimization_barrier(
+        (ahead_send, ahead_keep, back_in, packs_beyond)
+    )
     ahead_landed = swap_cores(ahead_send)
-    settled = [halves[0], struct((share, width), BF16)]
-    ahead_1, ahead_other = pl.pallas_call(
-        settle_kernel,
+
+    cut_shapes = [halves[0], struct((2 * share, depth + width // 2), BF16)]
+    cut_shapes += [struct((2 * share, depth), BF16)] * (n - 2)
+    up_mine, *cuts = pl.pallas_call(
+        functools.partial(cut_kernel, n),
         grid=(1,),
-        in_specs=[smem] * 2
-        + all_of(new_own, new_theirs, ahead_in, ahead_keep, ahead_landed),
-        out_specs=all_of(*settled),
-        out_shape=settled,
-        compiler_params=small,
-        name="settle",
-    )(core, first_flag, new_own, new_theirs, ahead_in, ahead_keep, ahead_landed)
-    back_given = to_partner(back_0[1])
-    ahead_1, ahead_other, back_in, packs_beyond, back_given = lax.optimization_barrier(
-        (ahead_1, ahead_other, back_in, packs_beyond, back_given)
-    )
-
-    back_their = swap_cores(back_in)
-    cut_shapes = [struct((rows, width), BF16), struct((rows, depth + folded), BF16)]
-    cut_shapes += [struct((rows, depth), BF16)] * (n - 2)
-    up_1, *cuts = pl.pallas_call(
-        functools.partial(gather_kernel, n),
-        grid=(1,),
-        in_specs=[smem] * 3 + all_of(back_in, back_their, new_own, new_theirs, ahead_other),
+        in_specs=[smem] * 3 + all_of(back_in, new_own, new_theirs, back_0),
         out_specs=all_of(*cut_shapes),
         out_shape=cut_shapes,
         compiler_params=small,
-        name="gather",
-    )(core, offs, last_flag, back_in, back_their, new_own, new_theirs, ahead_other)
+        name="cut",
+    )(core, offs, last_flag, back_in, new_own, new_theirs, back_0)
+    up_their = swap_cores(up_mine)
     landed = [to_partner(cuts[0])] + [from_host(cuts[m], m) for m in between]
     landed += [to_beyond(cuts[n // 2 + m - 1], m) for m in between]
-    back_send, back_keep = backward(up_1, 1)
+    back_send, back_keep = backward([up_mine, up_their], 1)
     back_send, back_keep, landed = lax.optimization_barrier((back_send, back_keep, landed))
-    back_1 = summed(
-        jnp.where(last_section, new_rows, back_in), back_keep, swap_cores(back_send)
-    )
-
+    last_inputs = [new_own, new_theirs, ahead_in, ahead_keep, ahead_landed]
+    last_inputs += [up_mine, back_keep, swap_cores(back_send)]
+    last_shapes = [halves[0]] * 3
+    ahead_1, back_1, pair = pl.pallas_call(
+        last_kernel,
+        grid=(1,),
+        in_specs=[smem] * 2 + all_of(*last_inputs),
+        out_specs=all_of(*last_shapes),
+        out_shape=last_shapes,
+        compiler_params=small,
+        name="last",
+    )(core, first_flag, *last_inputs)
+    pair = to_partner(pair)
+
+    landed_halves = jnp.stack(
+        [landed[0][:, :depth]]
+        + [jnp.where(is_host, landed[m], landed[n // 2 + m - 1]) for m in between]
+    )
+    landed_other = swap_cores(landed_halves)
+    grad_inputs = [gated, up_0, up_own, up_near, up_mine, up_their, landed_halves, landed_other]
+    grad_inputs += packs_near + packs_beyond
+    grad_inputs[0] = after(gated, back_1)
     grads = pl.pallas_call(
         functools.partial(grads_kernel, n, (ticks * length * n) ** (-0.5)),
         grid=(1,),
-        in_specs=[smem] * 2 + all_of(
-            gated, up_0, up_1, up_own, up_near, *packs_near, *packs_beyond, *landed
-        ),
+        in_specs=[smem] * 3 + all_of(*grad_inputs),
         out_specs=pl.BlockSpec((slab, depth), lambda *_: (0, 0)),
         out_shape=struct((slab, depth), F32),
+        scratch_shapes=[pltpu.VMEM((rows, depth), BF16)],
         compiler_params=small,
         cost_estimate=cost(matmul // 4, weight_bytes // 4),
         name="grads",
-    )(
-        host_flag, offs, after(gated, back_1), up_0, up_1, up_own, up_near, *packs_near, *packs_beyond, *landed
-    )
-
-    first_pack, last_cut, back_given = lax.optimization_barrier(
-        (packs_near[0], landed[0], back_given, grads)
-    )[:3]
+    )(host_flag, core, offs, *grad_inputs)
+
+    first_pack, last_cut = lax.optimization_barrier((packs_near[0], landed[0], back_1))[:2]
     ahead = jnp.stack(
         [
             jnp.where(is_host, ahead_0[0], unfold(first_pack[:, 2 * slab :], share)),
-            jnp.where(is_host, ahead_1[0], unfold(last_cut[:, depth:], share)),
+            jnp.where(is_host, ahead_1[0], pair[0]),
         ]
     )
     back = jnp.stack(
         [
-            jnp.where(is_host, back_0[0], back_given),
-            jnp.where(is_host, back_1[0], to_partner(back_1[1])),
+            jnp.where(is_host, back_0[0], unfold(last_cut[:, depth:], share)),
+            jnp.where(is_host, back_1[0], pair[1]),
         ]
     )
     return (ahead[None], back[None], grads[None])

time: 205 us -> 198 us (0.966)
  waiting for transfers between devices: 108 us -> 98 us
  starting transfers between devices: 56.4 us -> 53.1 us
  other arithmetic: 7.66 us -> 10.7 us
    ppermute x8, waiting for transfers between devices: 54.4 us -> 49.9 us  [from_partner(): return lax.ppermute(x, 'dp', [(h ^ 1, h) for h in hosts])]
    ppermute x2, waiting for transfers between devices: 18.5 us -> 14.3 us  [to_beyond(): lax.ppermute(x, 'dp', [(hosts[k ^ m], hosts[k] ^ 1) for k in range(n // 2)])]
    unnamed x78 -> x50, local copies, waits for them, and re-layouts: 9.15 us -> 5.62 us
    reshape x2, local copies, waits for them, and re-layouts: 0.16 us -> 2.73 us  [per_device(): m.reshape(m.shape[:2] + (-1,))]
    ppermute x5 -> x4, starting transfers between devices: 6.45 us -> 5.16 us  [to_partner(): return lax.ppermute(x, 'dp', [(h, h ^ 1) for h in hosts])]
    ppermute x5 -> x4, waiting for transfers between devices: 30.9 us -> 31.7 us  [to_partner(): return lax.ppermute(x, 'dp', [(h, h ^ 1) for h in hosts])]
    ppermute x6 -> x7, starting transfers between devices: 5.16 us -> 5.31 us  [swap_cores(): return lax.ppermute(x, 'cores', [(c, cores - 1 - c) for c in range(cores)])]
  transfers between devices with their start and end apart: 30 -> 30, of which waited for: 15 -> 13; matrix products, arithmetic and copies ran while one was open for 5% -> 9% of each run, Pallas kernels for 5% -> 7%
where the time goes in v12:
time: 198 us; the launch traced here: 195 us
  waiting for transfers between devices  98 us (49%)
  starting transfers between devices  53.1 us (27%)
  Pallas kernels  15.1 us (8%)
  local copies, waits for them, and re-layouts  14.7 us (7%)
  other arithmetic  10.7 us (5%)
  between operations  3.14 us (2%)
    ppermute x8, waiting for transfers between devices, from_partner(): return lax.ppermute(x, 'dp', [(h ^ 1, h) for h in hosts])  49.9 us
    ppermute x4, waiting for transfers between devices, to_partner(): return lax.ppermute(x, 'dp', [(h, h ^ 1) for h in hosts])  31.7 us
    ppermute x8, starting transfers between devices, from_partner(): return lax.ppermute(x, 'dp', [(h ^ 1, h) for h in hosts])  30.1 us
    ppermute x2, waiting for transfers between devices, to_beyond(): lax.ppermute(x, 'dp', [(hosts[k ^ m], hosts[k] ^ 1) for k in range(n // 2)])  14.3 us
    ppermute x7, starting transfers between devices, from_host(): lax.ppermute(x, 'dp', [(hosts[k ^ m], hosts[k]) for k in range(n // 2)])  6.97 us
    unnamed x50, local copies, waits for them, and re-layouts  5.62 us
    ppermute x7, starting transfers between devices, swap_cores(): return lax.ppermute(x, 'cores', [(c, cores - 1 - c) for c in range(cores)])  5.31 us
    ppermute x4, starting transfers between devices, to_partner(): return lax.ppermute(x, 'dp', [(h, h ^ 1) for h in hosts])  5.16 us
  transfers between devices with their start and end apart: 30, of which 13 were waited for; matrix products, arithmetic and copies ran while one was open for 9% of the time, Pallas kernels for 7%

profile of v12, /device:TPU:5, one launch (start us, length us, event | category | flops | bytes accessed | tf_op | source)
XLA Modules:
  0.0 194.7 jit_solution(12641762974906477970)
XLA Ops:
  1.6 3.2 %slice_bitcast_fusion = (bf16[256,2048]{1,0:T(8,128)(2,1)}, bf16[256,2048]{1,0:T(8,128)(2,1)}) fusion(bf16[1,512,2048]{2,1,0:T(8,128)(2,1)} %param.17), kind=kLoop, calls=%fused_computation | loop fusion | bytes 4194304 | tf_op jit(solution)/shard_map/slice | solution.py:545
  4.8 6.6 %collective-permute-start.1 = (bf16[256,2048]{1,0:T(8,128)(2,1)}, bf16[256,2048]{1,0:T(8,128)(2,1)}, u32[]{:S(2)}, u32[]{:S(2)}) collective-permute-start(bf16[256,2048]{1,0:T(8,128)(2,1)} %get-tuple-element.148), channel_id=1, source_target_pairs={{0,2},{6,4},{1,3},{7,5},{8,10},{14,12},{9,11},{15,13},{16,18},{22,... | collective-permute-start | bytes 3145736 | tf_op jit(solution)/shard_map/ppermute | solution.py:512
  11.4 2.3 %collective-permute-start.2 = (bf16[256,2048]{1,0:T(8,128)(2,1)}, bf16[256,2048]{1,0:T(8,128)(2,1)}, u32[]{:S(2)}, u32[]{:S(2)}) collective-permute-start(bf16[256,2048]{1,0:T(8,128)(2,1)} %get-tuple-element.147), channel_id=1, source_target_pairs={{0,2},{6,4},{1,3},{7,5},{8,10},{14,12},{9,11},{15,13},{16,18},{22,... | collective-permute-start | bytes 3145736 | tf_op jit(solution)/shard_map/ppermute | solution.py:512
  19.6 12.6 %collective-permute-done.1.refs_8_.refs_18_.refs_11_.refs_19_ = bf16[256,2048]{1,0:T(8,128)(2,1)} collective-permute-done((bf16[256,2048]{1,0:T(8,128)(2,1)}, bf16[256,2048]{1,0:T(8,128)(2,1)}, u32[]{:S(2)}, u32[]{:S(2)}) %collective-permute-start.1) | collective-permute-done | bytes 1048608 | tf_op jit(solution)/shard_map/ppermute | solution.py:512
  32.2 1.6 collective-permute-start.7
  33.8 20.8 %collective-permute-done.2.refs_9_.refs_19_.refs_12_.refs_20_ = bf16[256,2048]{1,0:T(8,128)(2,1)} collective-permute-done((bf16[256,2048]{1,0:T(8,128)(2,1)}, bf16[256,2048]{1,0:T(8,128)(2,1)}, u32[]{:S(2)}, u32[]{:S(2)}) %collective-permute-start.2) | collective-permute-done | bytes 1048608 | tf_op jit(solution)/shard_map/ppermute | solution.py:512
  54.8 1.4 copy.51
  59.8 4.1 %collective-permute-start.6 = (s32[2,5,17]{2,0,1:T(2,128)S(1)}, s32[2,5,17]{2,0,1:T(2,128)S(1)}, u32[]{:S(2)}, u32[]{:S(2)}) collective-permute-start(s32[2,5,17]{2,0,1:T(2,128)S(1)} %add_add_fusion), channel_id=1, source_target_pairs={{0,2},{6,4},{1,3},{7,5},{8,10},{14,12},{9,11},{15,13},{16,18},{22,... | collective-permute-start | bytes 2048 | tf_op jit(solution)/shard_map/ppermute | solution.py:512
  63.9 2.2 %collective-permute-start.4 = (bf16[2,96,2048]{2,1,0:T(8,128)(2,1)}, bf16[2,96,2048]{2,1,0:T(8,128)(2,1)}, u32[]{:S(2)}, u32[]{:S(2)}) collective-permute-start(bf16[2,96,2048]{2,1,0:T(8,128)(2,1)} %bitcast.12.refs_3_.refs_10_.refs_11_), channel_id=1, source_target_pairs={{0,2},{6,4},{1,3},{7,5},{8,10},{14,12},{9,11},{15,13},{16,18},{22,... | collective-permute-start | bytes 2359304 | tf_op jit(solution)/shard_map/ppermute | solution.py:512
  66.1 1.7 collective-permute-start.8
  67.8 1.7 slice_select_fusion
  69.5 2.1 %collective-permute-start.3 = (bf16[96,2048]{1,0:T(8,128)(2,1)S(1)}, bf16[96,2048]{1,0:T(8,128)(2,1)}, u32[]{:S(2)}, u32[]{:S(2)}) collective-permute-start(bf16[96,2048]{1,0:T(8,128)(2,1)S(1)} %get-tuple-element.151.refs_1_.own), channel_id=1, source_target_pairs={{0,2},{6,4},{1,3},{7,5},{8,10},{14,12},{9,11},{15,13},{16,18},{22,... | collective-permute-start | bytes 1179656 | tf_op jit(solution)/shard_map/ppermute | solution.py:512
  73.7 8.2 %collective-permute-done.4.refs_4_.refs_11_.refs_12_ = bf16[2,96,2048]{2,1,0:T(8,128)(2,1)} collective-permute-done((bf16[2,96,2048]{2,1,0:T(8,128)(2,1)}, bf16[2,96,2048]{2,1,0:T(8,128)(2,1)}, u32[]{:S(2)}, u32[]{:S(2)}) %collective-permute-start.4) | collective-permute-done | bytes 786464 | tf_op jit(solution)/shard_map/ppermute | solution.py:512
  82.7 5.5 %collective-permute-start.11 = (bf16[96,2048]{1,0:T(8,128)(2,1)S(1)}, bf16[96,2048]{1,0:T(8,128)(2,1)S(1)}, u32[]{:S(2)}, u32[]{:S(2)}) collective-permute-start(bf16[96,2048]{1,0:T(8,128)(2,1)S(1)} %bitcast.83), channel_id=1, source_target_pairs={{0,2},{6,4},{1,3},{7,5},{8,10},{14,12},{9,11},{15,13},{16,18},{22,... | collective-permute-start | bytes 1179656 | tf_op jit(solution)/shard_map/ppermute | solution.py:512
  88.2 2.1 %collective-permute-done.3.refs_2_.theirs = bf16[96,2048]{1,0:T(8,128)(2,1)} collective-permute-done((bf16[96,2048]{1,0:T(8,128)(2,1)S(1)}, bf16[96,2048]{1,0:T(8,128)(2,1)}, u32[]{:S(2)}, u32[]{:S(2)}) %collective-permute-start.3) | collective-permute-done | bytes 393248 | tf_op jit(solution)/shard_map/ppermute | solution.py:512
  91.6 6.1 %collective-permute-start.9 = (bf16[96,2048]{1,0:T(8,128)(2,1)S(1)}, bf16[96,2048]{1,0:T(8,128)(2,1)S(1)}, u32[]{:S(2)}, u32[]{:S(2)}) collective-permute-start(bf16[96,2048]{1,0:T(8,128)(2,1)S(1)} %get-tuple-element.90.refs_6_.new_own), channel_id=1, source_target_pairs={{0,2},{6,4},{1,3},{7,5},{8,10},{14,12},{9,11},{15,13},{16,18},{22,... | collective-permute-start | bytes 1179656 | tf_op jit(solution)/shard_map/ppermute | solution.py:512
  98.7 2.2 %project.1 = (bf16[3,192,512]{2,1,0:T(8,128)(2,1)S(1)}, f32[2,192,512]{2,1,0:T(8,128)}, bf16[2,192,1536]{2,1,0:T(8,128)(2,1)}, f32[2,192,2048]{2,1,0:T(8,128)}, ...) custom-call(s32[1]{0:T(128)} %bitcast.8.host, s32[6]{0:T(128)S(1)} %stack.81.refs_0_.refs_1_, ...), custom_call_target="tpu_custom_call" | custom-call | flops 4831838208 | bytes 20971520 | tf_op jit(solution)/shard_map/project/pallas_call | solution.py:653
  100.9 6.2 %collective-permute-done.9.refs_7_.new_theirs = bf16[96,2048]{1,0:T(8,128)(2,1)S(1)} collective-permute-done((bf16[96,2048]{1,0:T(8,128)(2,1)S(1)}, bf16[96,2048]{1,0:T(8,128)(2,1)S(1)}, u32[]{:S(2)}, u32[]{:S(2)}) %collective-permute-start.9) | collective-permute-done | bytes 393248 | tf_op jit(solution)/shard_map/ppermute | solution.py:512
  109.8 2.9 %collective-permute-start.14 = (bf16[2,48,2048]{2,1,0:T(8,128)(2,1)S(1)}, bf16[2,48,2048]{2,1,0:T(8,128)(2,1)S(1)}, u32[]{:S(2)}, u32[]{:S(2)}) collective-permute-start(bf16[2,48,2048]{2,1,0:T(8,128)(2,1)S(1)} %get-tuple-element.102), channel_id=1, source_target_pairs={{0,1},{1,0},{2,3},{3,2},{4,5},{5,4},{6,7},{7,6},{8,9},{9,8},{10,11... | collective-permute-start | bytes 1179656 | tf_op jit(solution)/shard_map/ppermute | solution.py:526
  116.6 1.4 collective-permute-start.15
  118.1 1.7 backward.2
  121.3 19.0 %collective-permute-done.16.rest_0_ = bf16[192,1536]{1,0:T(8,128)(2,1)} collective-permute-done((bf16[192,1536]{1,0:T(8,128)(2,1)S(1)}, bf16[192,1536]{1,0:T(8,128)(2,1)}, u32[]{:S(2)}, u32[]{:S(2)}) %collective-permute-start.16) | collective-permute-done | bytes 589856 | tf_op jit(solution)/shard_map/ppermute | solution.py:515
  141.1 1.5 collective-permute-start.21
  142.8 2.1 %add_convert_fusion.back = bf16[2,48,2048]{2,1,0:T(8,128)(2,1)} fusion(bf16[2,48,2048]{2,1,0:T(8,128)(2,1)} %collective-permute-done.19, bf16[2,48,2048]{2,1,0:T(8,128)(2,1)} %copy-done.13, s32[]{:T(128)S(6)} %select_n.123, bf16[1,96,2048]{2,1,0:T(8,128)(2,1)S(1)} %get-tuple-element.149, bf16[1,96,2048]{2,1,0:T(8,128)(2,1)} %bitcast.86), kind=kLoop, calls=%fused_computation.7 | loop fusion | flops 1769472 | bytes 1966084 | tf_op jit(solution)/shard_map/convert_element_type | solution.py:701
  144.9 1.4 collective-permute-start.20
  148.4 1.5 forward.1
  149.9 9.3 %collective-permute-done.21.rest_2_ = bf16[192,1536]{1,0:T(8,128)(2,1)} collective-permute-done((bf16[192,1536]{1,0:T(8,128)(2,1)}, bf16[192,1536]{1,0:T(8,128)(2,1)}, u32[]{:S(2)}, u32[]{:S(2)}) %collective-permute-start.21) | collective-permute-done | bytes 589856 | tf_op jit(solution)/shard_map/ppermute | solution.py:521
  165.5 5.1 %collective-permute-done.25 = bf16[96,512]{1,0:T(8,128)(2,1)S(1)} collective-permute-done((bf16[96,512]{1,0:T(8,128)(2,1)S(1)}, bf16[96,512]{1,0:T(8,128)(2,1)S(1)}, u32[]{:S(2)}, u32[]{:S(2)}) %collective-permute-start.25) | collective-permute-done | bytes 98336 | tf_op jit(solution)/shard_map/ppermute | solution.py:521
  170.6 6.8 %collective-permute-done.23 = bf16[96,1536]{1,0:T(8,128)(2,1)S(1)} collective-permute-done((bf16[96,1536]{1,0:T(8,128)(2,1)S(1)}, bf16[96,1536]{1,0:T(8,128)(2,1)S(1)}, u32[]{:S(2)}, u32[]{:S(2)}) %collective-permute-start.23) | collective-permute-done | bytes 294944 | tf_op jit(solution)/shard_map/ppermute | solution.py:515
  179.4 1.5 last.1
  183.1 3.1 %grads.1 = f32[512,512]{1,0:T(8,128)} custom-call(s32[1]{0:T(128)} %bitcast.8.host, s32[1]{0:T(128)} %bitcast.1.core.refs_0_, s32[4]{0:T(128)S(1)} %add_multiply_fusion.offs.refs_2_, bf16[3,192,512]{2,1,0:T(8,128)(2,1)S(1)} %get-tuple-element.141.gated, bf16[192,2048]{1,0:T(8,128)(2,1)S(1)} %copy-done.4, bf16[96,2048]{1,0:T(8,128)(2,1)S(1)} %bitcast.85, ...), custom_call_target="tpu_custom_call" | custom-call | flops 402653184 | bytes 2621440 | tf_op jit(solution)/shard_map/grads/pallas_call | solution.py:830
  187.2 5.9 %collective-permute-done.28 = bf16[2,48,2048]{2,1,0:T(8,128)(2,1)S(1)} collective-permute-done((bf16[2,48,2048]{2,1,0:T(8,128)(2,1)S(1)}, bf16[2,48,2048]{2,1,0:T(8,128)(2,1)S(1)}, u32[]{:S(2)}, u32[]{:S(2)}) %collective-permute-start.28) | collective-permute-done | bytes 393248 | tf_op jit(solution)/shard_map/ppermute | solution.py:515
  (129 shorter events, 38.2 us)
Async XLA Ops:
  0.7 54.0 %copy-start.24 = (s32[1,5]{1,0:T(1,128)S(1)}, s32[1,5]{1,0:T(1,128)}, u32[]{:S(2)}) copy-start(s32[1,5]{1,0:T(1,128)} %param.19) | copy-start | bytes 64
  0.7 67.1 %copy-start.20 = (bf16[1,96,2048]{2,1,0:T(8,128)(2,1)S(1)}, bf16[1,96,2048]{2,1,0:T(8,128)(2,1)}, u32[]{:S(2)}) copy-start(bf16[1,96,2048]{2,1,0:T(8,128)(2,1)} %param.15) | copy-start | bytes 1179652
  0.7 54.0 %collective-permute-start = (bf16[512,2048]{1,0:T(8,128)(2,1)}, bf16[512,2048]{1,0:T(8,128)(2,1)S(1)}, u32[]{:S(2)}, u32[]{:S(2)}) collective-permute-start(bf16[512,2048]{1,0:T(8,128)(2,1)} %bitcast.87), channel_id=1, source_target_pairs={{4,2},{2,4},{5,3},{3,5},{12,10},{10,12},{13,11},{11,13},{20,18},{1... | collective-permute-start | bytes 6291464 | tf_op jit(solution)/shard_map/ppermute | solution.py:518
  4.8 27.4 %collective-permute-start.1 = (bf16[256,2048]{1,0:T(8,128)(2,1)}, bf16[256,2048]{1,0:T(8,128)(2,1)}, u32[]{:S(2)}, u32[]{:S(2)}) collective-permute-start(bf16[256,2048]{1,0:T(8,128)(2,1)} %get-tuple-element.148), channel_id=1, source_target_pairs={{0,2},{6,4},{1,3},{7,5},{8,10},{14,12},{9,11},{15,13},{16,18},{22,... | collective-permute-start | bytes 3145736 | tf_op jit(solution)/shard_map/ppermute | solution.py:512
  11.4 43.3 %collective-permute-start.2 = (bf16[256,2048]{1,0:T(8,128)(2,1)}, bf16[256,2048]{1,0:T(8,128)(2,1)}, u32[]{:S(2)}, u32[]{:S(2)}) collective-permute-start(bf16[256,2048]{1,0:T(8,128)(2,1)} %get-tuple-element.147), channel_id=1, source_target_pairs={{0,2},{6,4},{1,3},{7,5},{8,10},{14,12},{9,11},{15,13},{16,18},{22,... | collective-permute-start | bytes 3145736 | tf_op jit(solution)/shard_map/ppermute | solution.py:512
  13.6 55.8 %collective-permute-start.5 = (bf16[512,512]{1,0:T(8,128)(2,1)S(1)}, bf16[512,512]{1,0:T(8,128)(2,1)S(1)}, u32[]{:S(2)}, u32[]{:S(2)}) collective-permute-start(bf16[512,512]{1,0:T(8,128)(2,1)S(1)} %bitcast.76), channel_id=1, source_target_pairs={{0,2},{6,4},{1,3},{7,5},{8,10},{14,12},{9,11},{15,13},{16,18},{22,... | collective-permute-start | bytes 1572872 | tf_op jit(solution)/shard_map/ppermute | solution.py:512
  32.2 50.5 %collective-permute-start.7 = (bf16[256,2048]{1,0:T(8,128)(2,1)}, bf16[256,2048]{1,0:T(8,128)(2,1)}, u32[]{:S(2)}, u32[]{:S(2)}) collective-permute-start(bf16[256,2048]{1,0:T(8,128)(2,1)} %collective-permute-done.1.refs_8_.refs_18_.refs_11_.refs_19_), channel_id=1, source_target_pairs={{4,2},{2,4},{5,3},{3,5},{12,10},{10,12},{13,11},{11,13},{20,18},{1... | collective-permute-start | bytes 3145736 | tf_op jit(solution)/shard_map/ppermute | solution.py:518
  59.8 11.7 %collective-permute-start.6 = (s32[2,5,17]{2,0,1:T(2,128)S(1)}, s32[2,5,17]{2,0,1:T(2,128)S(1)}, u32[]{:S(2)}, u32[]{:S(2)}) collective-permute-start(s32[2,5,17]{2,0,1:T(2,128)S(1)} %add_add_fusion), channel_id=1, source_target_pairs={{0,2},{6,4},{1,3},{7,5},{8,10},{14,12},{9,11},{15,13},{16,18},{22,... | collective-permute-start | bytes 2048 | tf_op jit(solution)/shard_map/ppermute | solution.py:512
  63.9 18.0 %collective-permute-start.4 = (bf16[2,96,2048]{2,1,0:T(8,128)(2,1)}, bf16[2,96,2048]{2,1,0:T(8,128)(2,1)}, u32[]{:S(2)}, u32[]{:S(2)}) collective-permute-start(bf16[2,96,2048]{2,1,0:T(8,128)(2,1)} %bitcast.12.refs_3_.refs_10_.refs_11_), channel_id=1, source_target_pairs={{0,2},{6,4},{1,3},{7,5},{8,10},{14,12},{9,11},{15,13},{16,18},{22,... | collective-permute-start | bytes 2359304 | tf_op jit(solution)/shard_map/ppermute | solution.py:512
  66.1 25.5 %collective-permute-start.8 = (bf16[256,2048]{1,0:T(8,128)(2,1)}, bf16[256,2048]{1,0:T(8,128)(2,1)}, u32[]{:S(2)}, u32[]{:S(2)}) collective-permute-start(bf16[256,2048]{1,0:T(8,128)(2,1)} %collective-permute-done.2.refs_9_.refs_19_.refs_12_.refs_20_), channel_id=1, source_target_pairs={{4,2},{2,4},{5,3},{3,5},{12,10},{10,12},{13,11},{11,13},{20,18},{1... | collective-permute-start | bytes 3145736 | tf_op jit(solution)/shard_map/ppermute | solution.py:518
  69.5 20.8 %collective-permute-start.3 = (bf16[96,2048]{1,0:T(8,128)(2,1)S(1)}, bf16[96,2048]{1,0:T(8,128)(2,1)}, u32[]{:S(2)}, u32[]{:S(2)}) collective-permute-start(bf16[96,2048]{1,0:T(8,128)(2,1)S(1)} %get-tuple-element.151.refs_1_.own), channel_id=1, source_target_pairs={{0,2},{6,4},{1,3},{7,5},{8,10},{14,12},{9,11},{15,13},{16,18},{22,... | collective-permute-start | bytes 1179656 | tf_op jit(solution)/shard_map/ppermute | solution.py:512
  72.5 36.1 %collective-permute-start.12 = (bf16[512,512]{1,0:T(8,128)(2,1)S(1)}, bf16[512,512]{1,0:T(8,128)(2,1)S(1)}, u32[]{:S(2)}, u32[]{:S(2)}) collective-permute-start(bf16[512,512]{1,0:T(8,128)(2,1)S(1)} %bitcast.77), channel_id=1, source_target_pairs={{4,2},{2,4},{5,3},{3,5},{12,10},{10,12},{13,11},{11,13},{20,18},{1... | collective-permute-start | bytes 1572872 | tf_op jit(solution)/shard_map/ppermute | solution.py:518
  81.9 26.7 %collective-permute-start.13 = (bf16[512,512]{1,0:T(8,128)(2,1)S(1)}, bf16[512,512]{1,0:T(8,128)(2,1)S(1)}, u32[]{:S(2)}, u32[]{:S(2)}) collective-permute-start(bf16[512,512]{1,0:T(8,128)(2,1)S(1)} %collective-permute-done.5.rest_1_.refs_13_.refs_16_.refs_14_), channel_id=1, source_target_pairs={{4,2},{2,4},{5,3},{3,5},{12,10},{10,12},{13,11},{11,13},{20,18},{1... | collective-permute-start | bytes 1572872 | tf_op jit(solution)/shard_map/ppermute | solution.py:518
  82.7 24.5 %collective-permute-start.11 = (bf16[96,2048]{1,0:T(8,128)(2,1)S(1)}, bf16[96,2048]{1,0:T(8,128)(2,1)S(1)}, u32[]{:S(2)}, u32[]{:S(2)}) collective-permute-start(bf16[96,2048]{1,0:T(8,128)(2,1)S(1)} %bitcast.83), channel_id=1, source_target_pairs={{0,2},{6,4},{1,3},{7,5},{8,10},{14,12},{9,11},{15,13},{16,18},{22,... | collective-permute-start | bytes 1179656 | tf_op jit(solution)/shard_map/ppermute | solution.py:512
  90.3 10.6 %collective-permute-start.10 = (bf16[96,512]{1,0:T(8,128)(2,1)S(1)}, bf16[96,512]{1,0:T(8,128)(2,1)S(1)}, u32[]{:S(2)}, u32[]{:S(2)}) collective-permute-start(bf16[96,512]{1,0:T(8,128)(2,1)S(1)} %constant_dynamic-slice_fusion), channel_id=1, source_target_pairs={{2,0},{4,6},{3,1},{5,7},{10,8},{12,14},{11,9},{13,15},{18,16},{20,... | collective-permute-start | bytes 294920 | tf_op jit(solution)/shard_map/ppermute | solution.py:515
  91.6 15.6 %collective-permute-start.9 = (bf16[96,2048]{1,0:T(8,128)(2,1)S(1)}, bf16[96,2048]{1,0:T(8,128)(2,1)S(1)}, u32[]{:S(2)}, u32[]{:S(2)}) collective-permute-start(bf16[96,2048]{1,0:T(8,128)(2,1)S(1)} %get-tuple-element.90.refs_6_.new_own), channel_id=1, source_target_pairs={{0,2},{6,4},{1,3},{7,5},{8,10},{14,12},{9,11},{15,13},{16,18},{22,... | collective-permute-start | bytes 1179656 | tf_op jit(solution)/shard_map/ppermute | solution.py:512
  109.8 4.2 %collective-permute-start.14 = (bf16[2,48,2048]{2,1,0:T(8,128)(2,1)S(1)}, bf16[2,48,2048]{2,1,0:T(8,128)(2,1)S(1)}, u32[]{:S(2)}, u32[]{:S(2)}) collective-permute-start(bf16[2,48,2048]{2,1,0:T(8,128)(2,1)S(1)} %get-tuple-element.102), channel_id=1, source_target_pairs={{0,1},{1,0},{2,3},{3,2},{4,5},{5,4},{6,7},{7,6},{8,9},{9,8},{10,11... | collective-permute-start | bytes 1179656 | tf_op jit(solution)/shard_map/ppermute | solution.py:526
  112.7 7.8 %collective-permute-start.17 = (bf16[192,1536]{1,0:T(8,128)(2,1)S(1)}, bf16[192,1536]{1,0:T(8,128)(2,1)S(1)}, u32[]{:S(2)}, u32[]{:S(2)}) collective-permute-start(bf16[192,1536]{1,0:T(8,128)(2,1)S(1)} %get-tuple-element.115), channel_id=1, source_target_pairs={{4,2},{2,4},{5,3},{3,5},{12,10},{10,12},{13,11},{11,13},{20,18},{1... | collective-permute-start | bytes 1769480 | tf_op jit(solution)/shard_map/ppermute | solution.py:518
  115.3 25.0 %collective-permute-start.16 = (bf16[192,1536]{1,0:T(8,128)(2,1)S(1)}, bf16[192,1536]{1,0:T(8,128)(2,1)}, u32[]{:S(2)}, u32[]{:S(2)}) collective-permute-start(bf16[192,1536]{1,0:T(8,128)(2,1)S(1)} %get-tuple-element.114), channel_id=1, source_target_pairs={{2,0},{4,6},{3,1},{5,7},{10,8},{12,14},{11,9},{13,15},{18,16},{20,... | collective-permute-start | bytes 1769480 | tf_op jit(solution)/shard_map/ppermute | solution.py:515
  116.6 4.7 %collective-permute-start.15 = (bf16[2,48,2048]{2,1,0:T(8,128)(2,1)S(1)}, bf16[2,48,2048]{2,1,0:T(8,128)(2,1)}, u32[]{:S(2)}, u32[]{:S(2)}) collective-permute-start(bf16[2,48,2048]{2,1,0:T(8,128)(2,1)S(1)} %get-tuple-element.103), channel_id=1, source_target_pairs={{2,10},{4,12},{10,18},{12,20},{18,26},{20,28},{3,11},{5,13},{11,19... | collective-permute-start | bytes 1179656 | tf_op jit(solution)/shard_map/ppermute | solution.py:535
  140.3 2.5 %collective-permute-start.19 = (bf16[2,48,2048]{2,1,0:T(8,128)(2,1)}, bf16[2,48,2048]{2,1,0:T(8,128)(2,1)}, u32[]{:S(2)}, u32[]{:S(2)}) collective-permute-start(bf16[2,48,2048]{2,1,0:T(8,128)(2,1)} %get-tuple-element.122), channel_id=1, source_target_pairs={{0,1},{1,0},{2,3},{3,2},{4,5},{5,4},{6,7},{7,6},{8,9},{9,8},{10,11... | collective-permute-start | bytes 1179656 | tf_op jit(solution)/shard_map/ppermute | solution.py:526
  141.1 18.1 %collective-permute-start.21 = (bf16[192,1536]{1,0:T(8,128)(2,1)}, bf16[192,1536]{1,0:T(8,128)(2,1)}, u32[]{:S(2)}, u32[]{:S(2)}) collective-permute-start(bf16[192,1536]{1,0:T(8,128)(2,1)} %copy-done.18), channel_id=1, source_target_pairs={{4,0},{2,6},{5,1},{3,7},{12,8},{10,14},{13,9},{11,15},{20,16},{18,... | collective-permute-start | bytes 1769480 | tf_op jit(solution)/shard_map/ppermute | solution.py:521
  142.6 3.7 %collective-permute-start.18 = (bf16[2,48,2048]{2,1,0:T(8,128)(2,1)}, bf16[2,48,2048]{2,1,0:T(8,128)(2,1)}, u32[]{:S(2)}, u32[]{:S(2)}) collective-permute-start(bf16[2,48,2048]{2,1,0:T(8,128)(2,1)} %collective-permute-done.15.refs_4_.passed), channel_id=1, source_target_pairs={{0,1},{1,0},{2,3},{3,2},{4,5},{5,4},{6,7},{7,6},{8,9},{9,8},{10,11... | collective-permute-start | bytes 1179656 | tf_op jit(solution)/shard_map/ppermute | solution.py:526
  144.9 14.3 %collective-permute-start.20 = (bf16[2,48,2048]{2,1,0:T(8,128)(2,1)}, bf16[2,48,2048]{2,1,0:T(8,128)(2,1)}, u32[]{:S(2)}, u32[]{:S(2)}) collective-permute-start(bf16[2,48,2048]{2,1,0:T(8,128)(2,1)} %add_convert_fusion.back), channel_id=1, source_target_pairs={{10,2},{12,4},{18,10},{20,12},{26,18},{28,20},{11,3},{13,5},{19,11... | collective-permute-start | bytes 1179656 | tf_op jit(solution)/shard_map/ppermute | solution.py:535
  160.4 4.2 %collective-permute-start.22 = (bf16[2,48,2048]{2,1,0:T(8,128)(2,1)S(1)}, bf16[2,48,2048]{2,1,0:T(8,128)(2,1)S(1)}, u32[]{:S(2)}, u32[]{:S(2)}) collective-permute-start(bf16[2,48,2048]{2,1,0:T(8,128)(2,1)S(1)} %get-tuple-element.125.refs_3_.up.mine), channel_id=1, source_target_pairs={{0,1},{1,0},{2,3},{3,2},{4,5},{5,4},{6,7},{7,6},{8,9},{9,8},{10,11... | collective-permute-start | bytes 1179656 | tf_op jit(solution)/shard_map/ppermute | solution.py:526
  161.2 17.0 %collective-permute-start.26 = (bf16[2,48,2048]{2,1,0:T(8,128)(2,1)S(1)}, bf16[2,48,2048]{2,1,0:T(8,128)(2,1)S(1)}, u32[]{:S(2)}, u32[]{:S(2)}) collective-permute-start(bf16[2,48,2048]{2,1,0:T(8,128)(2,1)S(1)} %get-tuple-element.133), channel_id=1, source_target_pairs={{0,1},{1,0},{2,3},{3,2},{4,5},{5,4},{6,7},{7,6},{8,9},{9,8},{10,11... | collective-permute-start | bytes 1179656 | tf_op jit(solution)/shard_map/ppermute | solution.py:526
  161.3 4.2 %collective-permute-start.24 = (bf16[96,512]{1,0:T(8,128)(2,1)S(1)}, bf16[96,512]{1,0:T(8,128)(2,1)S(1)}, u32[]{:S(2)}, u32[]{:S(2)}) collective-permute-start(bf16[96,512]{1,0:T(8,128)(2,1)S(1)} %get-tuple-element.129), channel_id=1, source_target_pairs={{4,2},{2,4},{5,3},{3,5},{12,10},{10,12},{13,11},{11,13},{20,18},{1... | collective-permute-start | bytes 294920 | tf_op jit(solution)/shard_map/ppermute | solution.py:518
  162.0 8.6 %collective-permute-start.25 = (bf16[96,512]{1,0:T(8,128)(2,1)S(1)}, bf16[96,512]{1,0:T(8,128)(2,1)S(1)}, u32[]{:S(2)}, u32[]{:S(2)}) collective-permute-start(bf16[96,512]{1,0:T(8,128)(2,1)S(1)} %get-tuple-element.130), channel_id=1, source_target_pairs={{4,0},{2,6},{5,1},{3,7},{12,8},{10,14},{13,9},{11,15},{20,16},{18,... | collective-permute-start | bytes 294920 | tf_op jit(solution)/shard_map/ppermute | solution.py:521
  163.3 14.2 %collective-permute-start.23 = (bf16[96,1536]{1,0:T(8,128)(2,1)S(1)}, bf16[96,1536]{1,0:T(8,128)(2,1)S(1)}, u32[]{:S(2)}, u32[]{:S(2)}) collective-permute-start(bf16[96,1536]{1,0:T(8,128)(2,1)S(1)} %get-tuple-element.128), channel_id=1, source_target_pairs={{2,0},{4,6},{3,1},{5,7},{10,8},{12,14},{11,9},{13,15},{18,16},{20,... | collective-permute-start | bytes 884744 | tf_op jit(solution)/shard_map/ppermute | solution.py:515
  177.4 1.9 collective-permute-start.27
  178.1 5.0 %collective-permute-start.29 = (bf16[2,96,512]{2,1,0:T(8,128)(2,1)S(1)}, bf16[2,96,512]{2,1,0:T(8,128)(2,1)S(1)}, u32[]{:S(2)}, u32[]{:S(2)}) collective-permute-start(bf16[2,96,512]{2,1,0:T(8,128)(2,1)S(1)} %pad_maximum_fusion.halves), channel_id=1, source_target_pairs={{0,1},{1,0},{2,3},{3,2},{4,5},{5,4},{6,7},{7,6},{8,9},{9,8},{10,11... | collective-permute-start | bytes 589832 | tf_op jit(solution)/shard_map/ppermute | solution.py:526
  180.9 12.2 %collective-permute-start.28 = (bf16[2,48,2048]{2,1,0:T(8,128)(2,1)S(1)}, bf16[2,48,2048]{2,1,0:T(8,128)(2,1)S(1)}, u32[]{:S(2)}, u32[]{:S(2)}) collective-permute-start(bf16[2,48,2048]{2,1,0:T(8,128)(2,1)S(1)} %get-tuple-element.139), channel_id=1, source_target_pairs={{2,0},{4,6},{3,1},{5,7},{10,8},{12,14},{11,9},{13,15},{18,16},{20,... | collective-permute-start | bytes 1179656 | tf_op jit(solution)/shard_map/ppermute | solution.py:515
  (23 other events, 186.9 us)

commit v13 on v12

--- a/solution.py
+++ b/solution.py
@@ -276,13 +276,12 @@
         copies[i].start()
     for copy in up_copies:
         copy.wait()
-    for i in first:
-        copies[i].wait()
     depth = out_parts[0].shape[1]
     length = x_own.shape[0]
     grad_gated = None
     for j in range(n):
         columns = pl.ds(pl.multiple_of(offs[j], depth), depth)
+        copies[first[j]].wait()
         term = dot_nt(ups[:, columns], out_parts[j][...])
         grad_gated = term if grad_gated is None else grad_gated + term
     grad_gated = grad_gated.astype(BF16).astype(F32)
@@ -363,10 +362,31 @@
         ]
 
 
-def unfold(folded, share):
-    return jnp.concatenate(
-        [folded[i : i + share] for i in range(0, folded.shape[0], share)], axis=1
-    )
+def unfold(folded, start, target):
+    share, width = target.shape
+    blocks = folded.shape[0] // share
+    size = width // blocks
+    for k in range(blocks):
+        target[:, k * size : (k + 1) * size] = folded[
+            k * share : (k + 1) * share, start : start + size
+        ]
+
+
+def finish_kernel(slab, host, ahead_0, ahead_1, back_0, pack, message, ahead, back):
+    width = back.shape[1]
+    depth = message.shape[1] - width
+
+    @pl.when(host[0] != 0)
+    def _():
+        ahead[0] = ahead_0[0]
+        ahead[1] = ahead_1[0]
+        back[...] = back_0[0]
+
+    @pl.when(host[0] == 0)
+    def _():
+        unfold(pack, 2 * slab, ahead.at[0])
+        unfold(message, depth + width // 2, ahead.at[1])
+        unfold(message, depth, back)
 
 
 def first_kernel(core, own, theirs, keep, landed, gated, total, pack):
@@ -382,33 +402,40 @@
     fold(total[1], pack, 2 * slab)
 
 
-def last_kernel(
-    core, fresh, new_own, new_theirs, passed, keep, landed, up, up_keep, up_landed, ahead, back, pair
+def message_kernel(
+    core, offs, fresh, new_own, new_theirs, passed, keep, landed, up, back, ahead, message
 ):
     share = keep.shape[1]
+    depth = message.shape[1] - up.shape[2]
     here = pl.ds(pl.multiple_of(core[0] * share, share), share)
+    columns = pl.ds(pl.multiple_of(offs[1], depth), depth)
     for r, source in enumerate((new_own, new_theirs)):
         residual = jnp.where(fresh[0] != 0, source[here, :], passed[r])
         ahead[r] = (
             residual.astype(F32) + keep[r].astype(F32) + landed[r].astype(F32)
         ).astype(BF16)
+        message[r * share : (r + 1) * share, :depth] = up[r, :, columns]
+    fold(back[1], message, depth)
+    fold(ahead[1], message, depth + up.shape[2] // 2)
+
+
+def last_kernel(up, keep, landed, back, other):
+    for r in range(2):
         back[r] = (
-            up[r].astype(F32) + up_keep[r].astype(F32) + up_landed[r].astype(F32)
+            up[r].astype(F32) + keep[r].astype(F32) + landed[r].astype(F32)
         ).astype(BF16)
-    pair[0] = ahead[1]
-    pair[1] = back[1]
-
-
-def cut_kernel(n, core, offs, fresh, landed, new_own, new_theirs, back, mine, *pieces):
+    other[...] = back[1]
+
+
+def cut_kernel(n, core, offs, fresh, landed, new_own, new_theirs, mine, *pieces):
     share = landed.shape[1]
     depth = pieces[-1].shape[1]
     here = pl.ds(pl.multiple_of(core[0] * share, share), share)
     for r, source in enumerate((new_own, new_theirs)):
         mine[r] = jnp.where(fresh[0] != 0, source[here, :], landed[r])
-        for j in range(1, n):
+        for j in range(2, n):
             columns = pl.ds(pl.multiple_of(offs[j], depth), depth)
-            pieces[j - 1][r * share : (r + 1) * share, :depth] = mine[r, :, columns]
-    fold(back[1], pieces[0], depth)
+            pieces[j - 2][r * share : (r + 1) * share, :] = mine[r, :, columns]
 
 
 def grads_kernel(
@@ -789,35 +816,45 @@
     )
     ahead_landed = swap_cores(ahead_send)
 
-    cut_shapes = [halves[0], struct((2 * share, depth + width // 2), BF16)]
-    cut_shapes += [struct((2 * share, depth), BF16)] * (n - 2)
+    cut_shapes = [halves[0]] + [struct((2 * share, depth), BF16)] * (n - 2)
     up_mine, *cuts = pl.pallas_call(
         functools.partial(cut_kernel, n),
         grid=(1,),
-        in_specs=[smem] * 3 + all_of(back_in, new_own, new_theirs, back_0),
+        in_specs=[smem] * 3 + all_of(back_in, new_own, new_theirs),
         out_specs=all_of(*cut_shapes),
         out_shape=cut_shapes,
         compiler_params=small,
         name="cut",
-    )(core, offs, last_flag, back_in, new_own, new_theirs, back_0)
+    )(core, offs, last_flag, back_in, new_own, new_theirs)
     up_their = swap_cores(up_mine)
-    landed = [to_partner(cuts[0])] + [from_host(cuts[m], m) for m in between]
-    landed += [to_beyond(cuts[n // 2 + m - 1], m) for m in between]
+    landed = [from_host(cuts[m - 1], m) for m in between]
+    landed += [to_beyond(cuts[n // 2 + m - 2], m) for m in between]
+    message_inputs = [new_own, new_theirs, ahead_in, ahead_keep, ahead_landed, up_mine, back_0]
+    message_shapes = [halves[0], struct((2 * share, depth + width), BF16)]
+    ahead_1, message = pl.pallas_call(
+        message_kernel,
+        grid=(1,),
+        in_specs=[smem] * 3 + all_of(*message_inputs),
+        out_specs=all_of(*message_shapes),
+        out_shape=message_shapes,
+        compiler_params=small,
+        name="message",
+    )(core, offs, first_flag, *message_inputs)
+    landed = [to_partner(message)] + landed
     back_send, back_keep = backward([up_mine, up_their], 1)
     back_send, back_keep, landed = lax.optimization_barrier((back_send, back_keep, landed))
-    last_inputs = [new_own, new_theirs, ahead_in, ahead_keep, ahead_landed]
-    last_inputs += [up_mine, back_keep, swap_cores(back_send)]
-    last_shapes = [halves[0]] * 3
-    ahead_1, back_1, pair = pl.pallas_call(
+    last_inputs = [up_mine, back_keep, swap_cores(back_send)]
+    last_shapes = [halves[0], struct((share, width), BF16)]
+    back_1, back_other = pl.pallas_call(
         last_kernel,
         grid=(1,),
-        in_specs=[smem] * 2 + all_of(*last_inputs),
+        in_specs=all_of(*last_inputs),
         out_specs=all_of(*last_shapes),
         out_shape=last_shapes,
         compiler_params=small,
         name="last",
-    )(core, first_flag, *last_inputs)
-    pair = to_partner(pair)
+    )(*last_inputs)
+    back_last = to_partner(back_other)
 
     landed_halves = jnp.stack(
         [landed[0][:, :depth]]
@@ -840,18 +877,18 @@
     )(host_flag, core, offs, *grad_inputs)
 
     first_pack, last_cut = lax.optimization_barrier((packs_near[0], landed[0], back_1))[:2]
-    ahead = jnp.stack(
-        [
-            jnp.where(is_host, ahead_0[0], unfold(first_pack[:, 2 * slab :], share)),
-            jnp.where(is_host, ahead_1[0], pair[0]),
-        ]
-    )
-    back = jnp.stack(
-        [
-            jnp.where(is_host, back_0[0], unfold(last_cut[:, depth:], share)),
-            jnp.where(is_host, back_1[0], pair[1]),
-        ]
-    )
+    finish_inputs = [ahead_0, ahead_1, back_0, first_pack, last_cut]
+    finish_shapes = [struct((ticks, share, width), BF16), struct((share, width), BF16)]
+    ahead, back_first = pl.pallas_call(
+        functools.partial(finish_kernel, slab),
+        grid=(1,),
+        in_specs=[smem] + all_of(*finish_inputs),
+        out_specs=all_of(*finish_shapes),
+        out_shape=finish_shapes,
+        compiler_params=small,
+        name="finish",
+    )(host_flag, *finish_inputs)
+    back = jnp.stack([back_first, jnp.where(is_host, back_1[0], back_last)])
     return (ahead[None], back[None], grads[None])
 
 

time: 198 us -> 199 us (level)
  local copies, waits for them, and re-layouts: 14.7 us -> 20.2 us
  waiting for transfers between devices: 98 us -> 95 us
  Pallas kernels: 15.1 us -> 17.4 us
    unnamed x50 -> x66, local copies, waits for them, and re-layouts: 5.62 us -> 12.1 us
    ppermute x4, waiting for transfers between devices: 31.7 us -> 27.1 us  [to_partner(): return lax.ppermute(x, 'dp', [(h, h ^ 1) for h in hosts])]
  transfers between devices with their start and end apart: 30 -> 30, of which waited for: 13 -> 13; matrix products, arithmetic and copies ran while one was open for 9% -> 8% of each run, Pallas kernels for 7% -> 8%
where the time goes in v13:
time: 199 us; the launch traced here: 197 us
  waiting for transfers between devices  95 us (48%)
  starting transfers between devices  52.8 us (27%)
  local copies, waits for them, and re-layouts  20.2 us (10%)
  Pallas kernels  17.4 us (9%)
  other arithmetic  8.88 us (4%)
  between operations  3.16 us (2%)
    ppermute x8, waiting for transfers between devices, from_partner(): return lax.ppermute(x, 'dp', [(h ^ 1, h) for h in hosts])  49.9 us
    ppermute x8, starting transfers between devices, from_partner(): return lax.ppermute(x, 'dp', [(h ^ 1, h) for h in hosts])  30.1 us
    ppermute x4, waiting for transfers between devices, to_partner(): return lax.ppermute(x, 'dp', [(h, h ^ 1) for h in hosts])  27.1 us
    ppermute x2, waiting for transfers between devices, to_beyond(): lax.ppermute(x, 'dp', [(hosts[k ^ m], hosts[k] ^ 1) for k in range(n // 2)])  15.8 us
    unnamed x66, local copies, waits for them, and re-layouts  12.1 us
    ppermute x7, starting transfers between devices, from_host(): lax.ppermute(x, 'dp', [(hosts[k ^ m], hosts[k]) for k in range(n // 2)])  6.98 us
    ppermute x7, starting transfers between devices, swap_cores(): return lax.ppermute(x, 'cores', [(c, cores - 1 - c) for c in range(cores)])  5.68 us
    ppermute x4, starting transfers between devices, to_partner(): return lax.ppermute(x, 'dp', [(h, h ^ 1) for h in hosts])  5.16 us
  transfers between devices with their start and end apart: 30, of which 13 were waited for; matrix products, arithmetic and copies ran while one was open for 8% of the time, Pallas kernels for 8%

profile of v13, /device:TPU:5, one launch (start us, length us, event | category | flops | bytes accessed | tf_op | source)
XLA Modules:
  0.0 197.4 jit_solution(15687623513560069820)
XLA Ops:
  1.6 3.1 %slice_bitcast_fusion = (bf16[256,2048]{1,0:T(8,128)(2,1)}, bf16[256,2048]{1,0:T(8,128)(2,1)}) fusion(bf16[1,512,2048]{2,1,0:T(8,128)(2,1)} %param.17), kind=kLoop, calls=%fused_computation | loop fusion | bytes 4194304 | tf_op jit(solution)/shard_map/slice | solution.py:572
  4.7 6.6 %collective-permute-start.1 = (bf16[256,2048]{1,0:T(8,128)(2,1)}, bf16[256,2048]{1,0:T(8,128)(2,1)}, u32[]{:S(2)}, u32[]{:S(2)}) collective-permute-start(bf16[256,2048]{1,0:T(8,128)(2,1)} %get-tuple-element.152), channel_id=1, source_target_pairs={{0,2},{6,4},{1,3},{7,5},{8,10},{14,12},{9,11},{15,13},{16,18},{22,... | collective-permute-start | bytes 3145736 | tf_op jit(solution)/shard_map/ppermute | solution.py:539
  11.3 2.3 %collective-permute-start.2 = (bf16[256,2048]{1,0:T(8,128)(2,1)}, bf16[256,2048]{1,0:T(8,128)(2,1)}, u32[]{:S(2)}, u32[]{:S(2)}) collective-permute-start(bf16[256,2048]{1,0:T(8,128)(2,1)} %get-tuple-element.151), channel_id=1, source_target_pairs={{0,2},{6,4},{1,3},{7,5},{8,10},{14,12},{9,11},{15,13},{16,18},{22,... | collective-permute-start | bytes 3145736 | tf_op jit(solution)/shard_map/ppermute | solution.py:539
  19.5 12.6 %collective-permute-done.1.refs_8_.refs_18_.refs_11_.refs_19_ = bf16[256,2048]{1,0:T(8,128)(2,1)} collective-permute-done((bf16[256,2048]{1,0:T(8,128)(2,1)}, bf16[256,2048]{1,0:T(8,128)(2,1)}, u32[]{:S(2)}, u32[]{:S(2)}) %collective-permute-start.1) | collective-permute-done | bytes 1048608 | tf_op jit(solution)/shard_map/ppermute | solution.py:539
  32.2 1.6 collective-permute-start.7
  33.8 20.9 %collective-permute-done.2.refs_9_.refs_19_.refs_12_.refs_20_ = bf16[256,2048]{1,0:T(8,128)(2,1)} collective-permute-done((bf16[256,2048]{1,0:T(8,128)(2,1)}, bf16[256,2048]{1,0:T(8,128)(2,1)}, u32[]{:S(2)}, u32[]{:S(2)}) %collective-permute-start.2) | collective-permute-done | bytes 1048608 | tf_op jit(solution)/shard_map/ppermute | solution.py:539
  54.7 1.4 copy.51
  59.8 4.1 %collective-permute-start.6 = (s32[2,5,17]{2,0,1:T(2,128)S(1)}, s32[2,5,17]{2,0,1:T(2,128)S(1)}, u32[]{:S(2)}, u32[]{:S(2)}) collective-permute-start(s32[2,5,17]{2,0,1:T(2,128)S(1)} %add_add_fusion), channel_id=1, source_target_pairs={{0,2},{6,4},{1,3},{7,5},{8,10},{14,12},{9,11},{15,13},{16,18},{22,... | collective-permute-start | bytes 2048 | tf_op jit(solution)/shard_map/ppermute | solution.py:539
  63.9 2.2 %collective-permute-start.4 = (bf16[2,96,2048]{2,1,0:T(8,128)(2,1)}, bf16[2,96,2048]{2,1,0:T(8,128)(2,1)}, u32[]{:S(2)}, u32[]{:S(2)}) collective-permute-start(bf16[2,96,2048]{2,1,0:T(8,128)(2,1)} %bitcast.12.refs_3_.refs_10_.refs_11_), channel_id=1, source_target_pairs={{0,2},{6,4},{1,3},{7,5},{8,10},{14,12},{9,11},{15,13},{16,18},{22,... | collective-permute-start | bytes 2359304 | tf_op jit(solution)/shard_map/ppermute | solution.py:539
  66.1 1.7 collective-permute-start.8
  67.8 1.7 select_bitcast_fusion
  69.5 2.1 %collective-permute-start.3 = (bf16[96,2048]{1,0:T(8,128)(2,1)S(1)}, bf16[96,2048]{1,0:T(8,128)(2,1)}, u32[]{:S(2)}, u32[]{:S(2)}) collective-permute-start(bf16[96,2048]{1,0:T(8,128)(2,1)S(1)} %get-tuple-element.154.refs_1_.own), channel_id=1, source_target_pairs={{0,2},{6,4},{1,3},{7,5},{8,10},{14,12},{9,11},{15,13},{16,18},{22,... | collective-permute-start | bytes 1179656 | tf_op jit(solution)/shard_map/ppermute | solution.py:539
  73.7 8.2 %collective-permute-done.4.refs_4_.refs_11_.refs_12_ = bf16[2,96,2048]{2,1,0:T(8,128)(2,1)} collective-permute-done((bf16[2,96,2048]{2,1,0:T(8,128)(2,1)}, bf16[2,96,2048]{2,1,0:T(8,128)(2,1)}, u32[]{:S(2)}, u32[]{:S(2)}) %collective-permute-start.4) | collective-permute-done | bytes 786464 | tf_op jit(solution)/shard_map/ppermute | solution.py:539
  82.6 5.5 %collective-permute-start.11 = (bf16[96,2048]{1,0:T(8,128)(2,1)S(1)}, bf16[96,2048]{1,0:T(8,128)(2,1)S(1)}, u32[]{:S(2)}, u32[]{:S(2)}) collective-permute-start(bf16[96,2048]{1,0:T(8,128)(2,1)S(1)} %bitcast.77), channel_id=1, source_target_pairs={{0,2},{6,4},{1,3},{7,5},{8,10},{14,12},{9,11},{15,13},{16,18},{22,... | collective-permute-start | bytes 1179656 | tf_op jit(solution)/shard_map/ppermute | solution.py:539
  88.2 2.1 %collective-permute-done.3.refs_2_.theirs = bf16[96,2048]{1,0:T(8,128)(2,1)} collective-permute-done((bf16[96,2048]{1,0:T(8,128)(2,1)S(1)}, bf16[96,2048]{1,0:T(8,128)(2,1)}, u32[]{:S(2)}, u32[]{:S(2)}) %collective-permute-start.3) | collective-permute-done | bytes 393248 | tf_op jit(solution)/shard_map/ppermute | solution.py:539
  91.5 6.1 %collective-permute-start.9 = (bf16[96,2048]{1,0:T(8,128)(2,1)S(1)}, bf16[96,2048]{1,0:T(8,128)(2,1)S(1)}, u32[]{:S(2)}, u32[]{:S(2)}) collective-permute-start(bf16[96,2048]{1,0:T(8,128)(2,1)S(1)} %get-tuple-element.92.refs_6_.new_own), channel_id=1, source_target_pairs={{0,2},{6,4},{1,3},{7,5},{8,10},{14,12},{9,11},{15,13},{16,18},{22,... | collective-permute-start | bytes 1179656 | tf_op jit(solution)/shard_map/ppermute | solution.py:539
  98.7 2.2 %project.1 = (bf16[3,192,512]{2,1,0:T(8,128)(2,1)S(1)}, f32[2,192,512]{2,1,0:T(8,128)}, bf16[2,192,1536]{2,1,0:T(8,128)(2,1)}, f32[2,192,2048]{2,1,0:T(8,128)}, ...) custom-call(s32[1]{0:T(128)} %bitcast.1.host, s32[6]{0:T(128)S(1)} %stack.80.refs_0_.refs_1_, ...), custom_call_target="tpu_custom_call" | custom-call | flops 4831838208 | bytes 20971520 | tf_op jit(solution)/shard_map/project/pallas_call | solution.py:680
  100.9 6.2 %collective-permute-done.9.refs_7_.new_theirs = bf16[96,2048]{1,0:T(8,128)(2,1)S(1)} collective-permute-done((bf16[96,2048]{1,0:T(8,128)(2,1)S(1)}, bf16[96,2048]{1,0:T(8,128)(2,1)S(1)}, u32[]{:S(2)}, u32[]{:S(2)}) %collective-permute-start.9) | collective-permute-done | bytes 393248 | tf_op jit(solution)/shard_map/ppermute | solution.py:539
  109.8 2.9 %collective-permute-start.14 = (bf16[2,48,2048]{2,1,0:T(8,128)(2,1)S(1)}, bf16[2,48,2048]{2,1,0:T(8,128)(2,1)S(1)}, u32[]{:S(2)}, u32[]{:S(2)}) collective-permute-start(bf16[2,48,2048]{2,1,0:T(8,128)(2,1)S(1)} %get-tuple-element.104), channel_id=1, source_target_pairs={{0,1},{1,0},{2,3},{3,2},{4,5},{5,4},{6,7},{7,6},{8,9},{9,8},{10,11... | collective-permute-start | bytes 1179656 | tf_op jit(solution)/shard_map/ppermute | solution.py:553
  117.3 1.7 backward.2
  120.6 19.6 %collective-permute-done.16.pack.rest_0_ = bf16[192,1536]{1,0:T(8,128)(2,1)S(1)} collective-permute-done((bf16[192,1536]{1,0:T(8,128)(2,1)S(1)}, bf16[192,1536]{1,0:T(8,128)(2,1)S(1)}, u32[]{:S(2)}, u32[]{:S(2)}) %collective-permute-start.16) | collective-permute-done | bytes 589856 | tf_op jit(solution)/shard_map/ppermute | solution.py:542
  141.8 1.5 collective-permute-start.21
  143.5 2.1 %add_convert_fusion.back.back_0 = bf16[2,48,2048]{2,1,0:T(8,128)(2,1)} fusion(bf16[2,48,2048]{2,1,0:T(8,128)(2,1)} %collective-permute-done.19, bf16[2,48,2048]{2,1,0:T(8,128)(2,1)} %copy-done.21, s32[]{:T(128)S(6)} %select_n.106, bf16[1,96,2048]{2,1,0:T(8,128)(2,1)S(1)} %get-tuple-element.155, bf16[1,96,2048]{2,1,0:T(8,128)(2,1)} %bitcast.80), kind=kLoop, calls=%fused_computation.7 | loop fusion | flops 1769472 | bytes 1966084 | tf_op jit(solution)/shard_map/convert_element_type | solution.py:728
  145.6 1.4 collective-permute-start.20
  150.2 2.1 %forward.1 = (bf16[2,48,2048]{2,1,0:T(8,128)(2,1)}, bf16[2,48,2048]{2,1,0:T(8,128)(2,1)S(1)}) custom-call(s32[1]{0:T(128)} %bitcast.1.host, s32[1]{0:T(128)} %bitcast.2.core.refs_0_, s32[6]{0:T(128)S(1)} %stack.80.refs_0_.refs_1_, s32[4]{0:T(128)S(1)} %add_multiply_fusion.offs.refs_2_, s32[1]{0:T(128)} %bitcast.33.refs_3_.fresh, ...), custom_call_target="tpu_custom_call" | custom-call | flops 3221225472 | bytes 20971520 | tf_op jit(solution)/shard_map/forward/pallas_call | solution.py:781
  153.0 6.9 %collective-permute-done.21.rest_2_ = bf16[192,1536]{1,0:T(8,128)(2,1)} collective-permute-done((bf16[192,1536]{1,0:T(8,128)(2,1)}, bf16[192,1536]{1,0:T(8,128)(2,1)}, u32[]{:S(2)}, u32[]{:S(2)}) %collective-permute-start.21) | collective-permute-done | bytes 589856 | tf_op jit(solution)/shard_map/ppermute | solution.py:548
  165.8 1.4 message.1
  171.5 9.0 %collective-permute-done.26 = bf16[96,512]{1,0:T(8,128)(2,1)S(1)} collective-permute-done((bf16[96,512]{1,0:T(8,128)(2,1)S(1)}, bf16[96,512]{1,0:T(8,128)(2,1)S(1)}, u32[]{:S(2)}, u32[]{:S(2)}) %collective-permute-start.26) | collective-permute-done | bytes 98336 | tf_op jit(solution)/shard_map/ppermute | solution.py:548
  180.4 5.5 %collective-permute-done.24.message = bf16[96,2560]{1,0:T(8,128)(2,1)S(1)} collective-permute-done((bf16[96,2560]{1,0:T(8,128)(2,1)S(1)}, bf16[96,2560]{1,0:T(8,128)(2,1)S(1)}, u32[]{:S(2)}, u32[]{:S(2)}) %collective-permute-start.24) | collective-permute-done | bytes 491552 | tf_op jit(solution)/shard_map/ppermute | solution.py:542
  189.9 1.8 finish.1
  191.7 2.8 %grads.1 = f32[512,512]{1,0:T(8,128)} custom-call(s32[1]{0:T(128)} %bitcast.1.host, s32[1]{0:T(128)} %bitcast.2.core.refs_0_, s32[4]{0:T(128)S(1)} %add_multiply_fusion.offs.refs_2_, bf16[3,192,512]{2,1,0:T(8,128)(2,1)S(1)} %get-tuple-element.145.gated, bf16[192,2048]{1,0:T(8,128)(2,1)S(1)} %copy-done.6, bf16[96,2048]{1,0:T(8,128)(2,1)S(1)} %bitcast.79, ...), custom_call_target="tpu_custom_call" | custom-call | flops 402653184 | bytes 2621440 | tf_op jit(solution)/shard_map/grads/pallas_call | solution.py:867
  194.5 2.1 %collective-permute-done.28 = bf16[48,2048]{1,0:T(8,128)(2,1)S(1)} collective-permute-done((bf16[48,2048]{1,0:T(8,128)(2,1)S(1)}, bf16[48,2048]{1,0:T(8,128)(2,1)S(1)}, u32[]{:S(2)}, u32[]{:S(2)}) %collective-permute-start.28) | collective-permute-done | bytes 196640 | tf_op jit(solution)/shard_map/ppermute | solution.py:542
  (143 shorter events, 43.2 us)
Async XLA Ops:
  0.7 54.0 %copy-start.32 = (s32[1,5]{1,0:T(1,128)S(1)}, s32[1,5]{1,0:T(1,128)}, u32[]{:S(2)}) copy-start(s32[1,5]{1,0:T(1,128)} %param.19) | copy-start | bytes 64
  0.7 67.1 %copy-start.28 = (bf16[1,96,2048]{2,1,0:T(8,128)(2,1)S(1)}, bf16[1,96,2048]{2,1,0:T(8,128)(2,1)}, u32[]{:S(2)}) copy-start(bf16[1,96,2048]{2,1,0:T(8,128)(2,1)} %param.13) | copy-start | bytes 1179652
  0.7 54.0 %collective-permute-start = (bf16[512,2048]{1,0:T(8,128)(2,1)}, bf16[512,2048]{1,0:T(8,128)(2,1)S(1)}, u32[]{:S(2)}, u32[]{:S(2)}) collective-permute-start(bf16[512,2048]{1,0:T(8,128)(2,1)} %bitcast.82), channel_id=1, source_target_pairs={{4,2},{2,4},{5,3},{3,5},{12,10},{10,12},{13,11},{11,13},{20,18},{1... | collective-permute-start | bytes 6291464 | tf_op jit(solution)/shard_map/ppermute | solution.py:545
  4.7 27.4 %collective-permute-start.1 = (bf16[256,2048]{1,0:T(8,128)(2,1)}, bf16[256,2048]{1,0:T(8,128)(2,1)}, u32[]{:S(2)}, u32[]{:S(2)}) collective-permute-start(bf16[256,2048]{1,0:T(8,128)(2,1)} %get-tuple-element.152), channel_id=1, source_target_pairs={{0,2},{6,4},{1,3},{7,5},{8,10},{14,12},{9,11},{15,13},{16,18},{22,... | collective-permute-start | bytes 3145736 | tf_op jit(solution)/shard_map/ppermute | solution.py:539
  11.3 43.3 %collective-permute-start.2 = (bf16[256,2048]{1,0:T(8,128)(2,1)}, bf16[256,2048]{1,0:T(8,128)(2,1)}, u32[]{:S(2)}, u32[]{:S(2)}) collective-permute-start(bf16[256,2048]{1,0:T(8,128)(2,1)} %get-tuple-element.151), channel_id=1, source_target_pairs={{0,2},{6,4},{1,3},{7,5},{8,10},{14,12},{9,11},{15,13},{16,18},{22,... | collective-permute-start | bytes 3145736 | tf_op jit(solution)/shard_map/ppermute | solution.py:539
  13.6 55.9 %collective-permute-start.5 = (bf16[512,512]{1,0:T(8,128)(2,1)S(1)}, bf16[512,512]{1,0:T(8,128)(2,1)S(1)}, u32[]{:S(2)}, u32[]{:S(2)}) collective-permute-start(bf16[512,512]{1,0:T(8,128)(2,1)S(1)} %bitcast.70), channel_id=1, source_target_pairs={{0,2},{6,4},{1,3},{7,5},{8,10},{14,12},{9,11},{15,13},{16,18},{22,... | collective-permute-start | bytes 1572872 | tf_op jit(solution)/shard_map/ppermute | solution.py:539
  32.2 50.5 %collective-permute-start.7 = (bf16[256,2048]{1,0:T(8,128)(2,1)}, bf16[256,2048]{1,0:T(8,128)(2,1)}, u32[]{:S(2)}, u32[]{:S(2)}) collective-permute-start(bf16[256,2048]{1,0:T(8,128)(2,1)} %collective-permute-done.1.refs_8_.refs_18_.refs_11_.refs_19_), channel_id=1, source_target_pairs={{4,2},{2,4},{5,3},{3,5},{12,10},{10,12},{13,11},{11,13},{20,18},{1... | collective-permute-start | bytes 3145736 | tf_op jit(solution)/shard_map/ppermute | solution.py:545
  59.8 11.8 %collective-permute-start.6 = (s32[2,5,17]{2,0,1:T(2,128)S(1)}, s32[2,5,17]{2,0,1:T(2,128)S(1)}, u32[]{:S(2)}, u32[]{:S(2)}) collective-permute-start(s32[2,5,17]{2,0,1:T(2,128)S(1)} %add_add_fusion), channel_id=1, source_target_pairs={{0,2},{6,4},{1,3},{7,5},{8,10},{14,12},{9,11},{15,13},{16,18},{22,... | collective-permute-start | bytes 2048 | tf_op jit(solution)/shard_map/ppermute | solution.py:539
  63.9 18.0 %collective-permute-start.4 = (bf16[2,96,2048]{2,1,0:T(8,128)(2,1)}, bf16[2,96,2048]{2,1,0:T(8,128)(2,1)}, u32[]{:S(2)}, u32[]{:S(2)}) collective-permute-start(bf16[2,96,2048]{2,1,0:T(8,128)(2,1)} %bitcast.12.refs_3_.refs_10_.refs_11_), channel_id=1, source_target_pairs={{0,2},{6,4},{1,3},{7,5},{8,10},{14,12},{9,11},{15,13},{16,18},{22,... | collective-permute-start | bytes 2359304 | tf_op jit(solution)/shard_map/ppermute | solution.py:539
  66.1 25.5 %collective-permute-start.8 = (bf16[256,2048]{1,0:T(8,128)(2,1)}, bf16[256,2048]{1,0:T(8,128)(2,1)}, u32[]{:S(2)}, u32[]{:S(2)}) collective-permute-start(bf16[256,2048]{1,0:T(8,128)(2,1)} %collective-permute-done.2.refs_9_.refs_19_.refs_12_.refs_20_), channel_id=1, source_target_pairs={{4,2},{2,4},{5,3},{3,5},{12,10},{10,12},{13,11},{11,13},{20,18},{1... | collective-permute-start | bytes 3145736 | tf_op jit(solution)/shard_map/ppermute | solution.py:545
  69.5 20.8 %collective-permute-start.3 = (bf16[96,2048]{1,0:T(8,128)(2,1)S(1)}, bf16[96,2048]{1,0:T(8,128)(2,1)}, u32[]{:S(2)}, u32[]{:S(2)}) collective-permute-start(bf16[96,2048]{1,0:T(8,128)(2,1)S(1)} %get-tuple-element.154.refs_1_.own), channel_id=1, source_target_pairs={{0,2},{6,4},{1,3},{7,5},{8,10},{14,12},{9,11},{15,13},{16,18},{22,... | collective-permute-start | bytes 1179656 | tf_op jit(solution)/shard_map/ppermute | solution.py:539
  72.5 36.0 %collective-permute-start.12 = (bf16[512,512]{1,0:T(8,128)(2,1)S(1)}, bf16[512,512]{1,0:T(8,128)(2,1)S(1)}, u32[]{:S(2)}, u32[]{:S(2)}) collective-permute-start(bf16[512,512]{1,0:T(8,128)(2,1)S(1)} %bitcast.71), channel_id=1, source_target_pairs={{4,2},{2,4},{5,3},{3,5},{12,10},{10,12},{13,11},{11,13},{20,18},{1... | collective-permute-start | bytes 1572872 | tf_op jit(solution)/shard_map/ppermute | solution.py:545
  81.9 26.7 %collective-permute-start.13 = (bf16[512,512]{1,0:T(8,128)(2,1)S(1)}, bf16[512,512]{1,0:T(8,128)(2,1)S(1)}, u32[]{:S(2)}, u32[]{:S(2)}) collective-permute-start(bf16[512,512]{1,0:T(8,128)(2,1)S(1)} %collective-permute-done.5.rest_1_.refs_13_.refs_16_.refs_14_), channel_id=1, source_target_pairs={{4,2},{2,4},{5,3},{3,5},{12,10},{10,12},{13,11},{11,13},{20,18},{1... | collective-permute-start | bytes 1572872 | tf_op jit(solution)/shard_map/ppermute | solution.py:545
  82.6 24.5 %collective-permute-start.11 = (bf16[96,2048]{1,0:T(8,128)(2,1)S(1)}, bf16[96,2048]{1,0:T(8,128)(2,1)S(1)}, u32[]{:S(2)}, u32[]{:S(2)}) collective-permute-start(bf16[96,2048]{1,0:T(8,128)(2,1)S(1)} %bitcast.77), channel_id=1, source_target_pairs={{0,2},{6,4},{1,3},{7,5},{8,10},{14,12},{9,11},{15,13},{16,18},{22,... | collective-permute-start | bytes 1179656 | tf_op jit(solution)/shard_map/ppermute | solution.py:539
  90.2 10.7 %collective-permute-start.10 = (bf16[96,512]{1,0:T(8,128)(2,1)S(1)}, bf16[96,512]{1,0:T(8,128)(2,1)S(1)}, u32[]{:S(2)}, u32[]{:S(2)}) collective-permute-start(bf16[96,512]{1,0:T(8,128)(2,1)S(1)} %constant_dynamic-slice_fusion), channel_id=1, source_target_pairs={{2,0},{4,6},{3,1},{5,7},{10,8},{12,14},{11,9},{13,15},{18,16},{20,... | collective-permute-start | bytes 294920 | tf_op jit(solution)/shard_map/ppermute | solution.py:542
  91.5 15.6 %collective-permute-start.9 = (bf16[96,2048]{1,0:T(8,128)(2,1)S(1)}, bf16[96,2048]{1,0:T(8,128)(2,1)S(1)}, u32[]{:S(2)}, u32[]{:S(2)}) collective-permute-start(bf16[96,2048]{1,0:T(8,128)(2,1)S(1)} %get-tuple-element.92.refs_6_.new_own), channel_id=1, source_target_pairs={{0,2},{6,4},{1,3},{7,5},{8,10},{14,12},{9,11},{15,13},{16,18},{22,... | collective-permute-start | bytes 1179656 | tf_op jit(solution)/shard_map/ppermute | solution.py:539
  109.8 4.2 %collective-permute-start.14 = (bf16[2,48,2048]{2,1,0:T(8,128)(2,1)S(1)}, bf16[2,48,2048]{2,1,0:T(8,128)(2,1)S(1)}, u32[]{:S(2)}, u32[]{:S(2)}) collective-permute-start(bf16[2,48,2048]{2,1,0:T(8,128)(2,1)S(1)} %get-tuple-element.104), channel_id=1, source_target_pairs={{0,1},{1,0},{2,3},{3,2},{4,5},{5,4},{6,7},{7,6},{8,9},{9,8},{10,11... | collective-permute-start | bytes 1179656 | tf_op jit(solution)/shard_map/ppermute | solution.py:553
  112.6 7.1 %collective-permute-start.17 = (bf16[192,1536]{1,0:T(8,128)(2,1)S(1)}, bf16[192,1536]{1,0:T(8,128)(2,1)S(1)}, u32[]{:S(2)}, u32[]{:S(2)}) collective-permute-start(bf16[192,1536]{1,0:T(8,128)(2,1)S(1)} %get-tuple-element.118), channel_id=1, source_target_pairs={{4,2},{2,4},{5,3},{3,5},{12,10},{10,12},{13,11},{11,13},{20,18},{1... | collective-permute-start | bytes 1769480 | tf_op jit(solution)/shard_map/ppermute | solution.py:545
  115.3 24.9 %collective-permute-start.16 = (bf16[192,1536]{1,0:T(8,128)(2,1)S(1)}, bf16[192,1536]{1,0:T(8,128)(2,1)S(1)}, u32[]{:S(2)}, u32[]{:S(2)}) collective-permute-start(bf16[192,1536]{1,0:T(8,128)(2,1)S(1)} %get-tuple-element.117), channel_id=1, source_target_pairs={{2,0},{4,6},{3,1},{5,7},{10,8},{12,14},{11,9},{13,15},{18,16},{20,... | collective-permute-start | bytes 1769480 | tf_op jit(solution)/shard_map/ppermute | solution.py:542
  116.6 4.0 %collective-permute-start.15 = (bf16[2,48,2048]{2,1,0:T(8,128)(2,1)S(1)}, bf16[2,48,2048]{2,1,0:T(8,128)(2,1)S(1)}, u32[]{:S(2)}, u32[]{:S(2)}) collective-permute-start(bf16[2,48,2048]{2,1,0:T(8,128)(2,1)S(1)} %get-tuple-element.105.ahead_0), channel_id=1, source_target_pairs={{2,10},{4,12},{10,18},{12,20},{18,26},{20,28},{3,11},{5,13},{11,19... | collective-permute-start | bytes 1179656 | tf_op jit(solution)/shard_map/ppermute | solution.py:562
  141.0 2.5 %collective-permute-start.19 = (bf16[2,48,2048]{2,1,0:T(8,128)(2,1)}, bf16[2,48,2048]{2,1,0:T(8,128)(2,1)}, u32[]{:S(2)}, u32[]{:S(2)}) collective-permute-start(bf16[2,48,2048]{2,1,0:T(8,128)(2,1)} %get-tuple-element.123), channel_id=1, source_target_pairs={{0,1},{1,0},{2,3},{3,2},{4,5},{5,4},{6,7},{7,6},{8,9},{9,8},{10,11... | collective-permute-start | bytes 1179656 | tf_op jit(solution)/shard_map/ppermute | solution.py:553
  141.8 18.1 %collective-permute-start.21 = (bf16[192,1536]{1,0:T(8,128)(2,1)}, bf16[192,1536]{1,0:T(8,128)(2,1)}, u32[]{:S(2)}, u32[]{:S(2)}) collective-permute-start(bf16[192,1536]{1,0:T(8,128)(2,1)} %copy-done.26), channel_id=1, source_target_pairs={{4,0},{2,6},{5,1},{3,7},{12,8},{10,14},{13,9},{11,15},{20,16},{18,... | collective-permute-start | bytes 1769480 | tf_op jit(solution)/shard_map/ppermute | solution.py:548
  143.3 3.7 %collective-permute-start.18 = (bf16[2,48,2048]{2,1,0:T(8,128)(2,1)}, bf16[2,48,2048]{2,1,0:T(8,128)(2,1)}, u32[]{:S(2)}, u32[]{:S(2)}) collective-permute-start(bf16[2,48,2048]{2,1,0:T(8,128)(2,1)} %copy-done.11), channel_id=1, source_target_pairs={{0,1},{1,0},{2,3},{3,2},{4,5},{5,4},{6,7},{7,6},{8,9},{9,8},{10,11... | collective-permute-start | bytes 1179656 | tf_op jit(solution)/shard_map/ppermute | solution.py:553
  145.6 14.3 %collective-permute-start.20 = (bf16[2,48,2048]{2,1,0:T(8,128)(2,1)}, bf16[2,48,2048]{2,1,0:T(8,128)(2,1)}, u32[]{:S(2)}, u32[]{:S(2)}) collective-permute-start(bf16[2,48,2048]{2,1,0:T(8,128)(2,1)} %add_convert_fusion.back.back_0), channel_id=1, source_target_pairs={{10,2},{12,4},{18,10},{20,12},{26,18},{28,20},{11,3},{13,5},{19,11... | collective-permute-start | bytes 1179656 | tf_op jit(solution)/shard_map/ppermute | solution.py:562
  159.9 2.9 %collective-permute-start.22 = (bf16[2,48,2048]{2,1,0:T(8,128)(2,1)}, bf16[2,48,2048]{2,1,0:T(8,128)(2,1)}, u32[]{:S(2)}, u32[]{:S(2)}) collective-permute-start(bf16[2,48,2048]{2,1,0:T(8,128)(2,1)} %get-tuple-element.126), channel_id=1, source_target_pairs={{0,1},{1,0},{2,3},{3,2},{4,5},{5,4},{6,7},{7,6},{8,9},{9,8},{10,11... | collective-permute-start | bytes 1179656 | tf_op jit(solution)/shard_map/ppermute | solution.py:553
  162.7 7.8 %collective-permute-start.23 = (bf16[2,48,2048]{2,1,0:T(8,128)(2,1)S(1)}, bf16[2,48,2048]{2,1,0:T(8,128)(2,1)S(1)}, u32[]{:S(2)}, u32[]{:S(2)}) collective-permute-start(bf16[2,48,2048]{2,1,0:T(8,128)(2,1)S(1)} %get-tuple-element.128.up.refs_3_.mine), channel_id=1, source_target_pairs={{0,1},{1,0},{2,3},{3,2},{4,5},{5,4},{6,7},{7,6},{8,9},{9,8},{10,11... | collective-permute-start | bytes 1179656 | tf_op jit(solution)/shard_map/ppermute | solution.py:553
  167.2 18.7 %collective-permute-start.24 = (bf16[96,2560]{1,0:T(8,128)(2,1)S(1)}, bf16[96,2560]{1,0:T(8,128)(2,1)S(1)}, u32[]{:S(2)}, u32[]{:S(2)}) collective-permute-start(bf16[96,2560]{1,0:T(8,128)(2,1)S(1)} %get-tuple-element.133), channel_id=1, source_target_pairs={{2,0},{4,6},{3,1},{5,7},{10,8},{12,14},{11,9},{13,15},{18,16},{20,... | collective-permute-start | bytes 1474568 | tf_op jit(solution)/shard_map/ppermute | solution.py:542
  168.5 3.0 %collective-permute-start.25 = (bf16[96,512]{1,0:T(8,128)(2,1)S(1)}, bf16[96,512]{1,0:T(8,128)(2,1)S(1)}, u32[]{:S(2)}, u32[]{:S(2)}) collective-permute-start(bf16[96,512]{1,0:T(8,128)(2,1)S(1)} %get-tuple-element.134), channel_id=1, source_target_pairs={{4,2},{2,4},{5,3},{3,5},{12,10},{10,12},{13,11},{11,13},{20,18},{1... | collective-permute-start | bytes 294920 | tf_op jit(solution)/shard_map/ppermute | solution.py:545
  169.2 11.3 %collective-permute-start.26 = (bf16[96,512]{1,0:T(8,128)(2,1)S(1)}, bf16[96,512]{1,0:T(8,128)(2,1)S(1)}, u32[]{:S(2)}, u32[]{:S(2)}) collective-permute-start(bf16[96,512]{1,0:T(8,128)(2,1)S(1)} %get-tuple-element.135), channel_id=1, source_target_pairs={{4,0},{2,6},{5,1},{3,7},{12,8},{10,14},{13,9},{11,15},{20,16},{18,... | collective-permute-start | bytes 294920 | tf_op jit(solution)/shard_map/ppermute | solution.py:548
  185.9 2.4 %collective-permute-start.27 = (bf16[2,48,2048]{2,1,0:T(8,128)(2,1)S(1)}, bf16[2,48,2048]{2,1,0:T(8,128)(2,1)S(1)}, u32[]{:S(2)}, u32[]{:S(2)}) collective-permute-start(bf16[2,48,2048]{2,1,0:T(8,128)(2,1)S(1)} %get-tuple-element.138), channel_id=1, source_target_pairs={{0,1},{1,0},{2,3},{3,2},{4,5},{5,4},{6,7},{7,6},{8,9},{9,8},{10,11... | collective-permute-start | bytes 1179656 | tf_op jit(solution)/shard_map/ppermute | solution.py:553
  187.0 4.7 %collective-permute-start.29 = (bf16[2,96,512]{2,1,0:T(8,128)(2,1)S(1)}, bf16[2,96,512]{2,1,0:T(8,128)(2,1)S(1)}, u32[]{:S(2)}, u32[]{:S(2)}) collective-permute-start(bf16[2,96,512]{2,1,0:T(8,128)(2,1)S(1)} %pad_maximum_fusion.halves), channel_id=1, source_target_pairs={{0,1},{1,0},{2,3},{3,2},{4,5},{5,4},{6,7},{7,6},{8,9},{9,8},{10,11... | collective-permute-start | bytes 589832 | tf_op jit(solution)/shard_map/ppermute | solution.py:553
  188.5 8.0 %collective-permute-start.28 = (bf16[48,2048]{1,0:T(8,128)(2,1)S(1)}, bf16[48,2048]{1,0:T(8,128)(2,1)S(1)}, u32[]{:S(2)}, u32[]{:S(2)}) collective-permute-start(bf16[48,2048]{1,0:T(8,128)(2,1)S(1)} %get-tuple-element.144), channel_id=1, source_target_pairs={{2,0},{4,6},{3,1},{5,7},{10,8},{12,14},{11,9},{13,15},{18,16},{20,... | collective-permute-start | bytes 589832 | tf_op jit(solution)/shard_map/ppermute | solution.py:542
  (31 other events, 233.9 us)

commit v14 on v13

--- a/solution.py
+++ b/solution.py
@@ -389,14 +389,18 @@
         unfold(message, depth, back)
 
 
-def first_kernel(core, own, theirs, keep, landed, gated, total, pack):
+def settle_kernel(core, own, theirs, keep, landed, total):
     share = keep.shape[1]
-    slab = gated.shape[2]
     here = pl.ds(pl.multiple_of(core[0] * share, share), share)
     for r, source in enumerate((own, theirs)):
         total[r] = (
             source[here, :].astype(F32) + keep[r].astype(F32) + landed[r].astype(F32)
         ).astype(BF16)
+
+
+def first_kernel(core, own, theirs, keep, landed, gated, total, pack):
+    slab = gated.shape[2]
+    settle_kernel(core, own, theirs, keep, landed, total)
     pack[:, :slab] = gated[1]
     pack[:, slab : 2 * slab] = gated[2]
     fold(total[1], pack, 2 * slab)
@@ -664,6 +668,7 @@
         return jax.ShapeDtypeStruct(shape, dtype)
 
     halves = [struct((2, share, width), BF16)] * 2
+    kept_halves = [halves[0], pltpu.HBM(halves[0].shape, BF16)]
     matmul = rows * width * 4 * slab
     weight_bytes = 2 * width * 5 * slab
 
@@ -707,7 +712,7 @@
             grid=(1,),
             in_specs=[smem] * 4 + [hbm] * (len(ups) + len(layered) + len(plain)),
             out_specs=all_of(*halves),
-            out_shape=halves,
+            out_shape=kept_halves,
             scratch_shapes=[pltpu.VMEM((rows, width), BF16)]
             + [pltpu.VMEM(x.shape[1:], x.dtype) for x in layered]
             + [pltpu.VMEM(x.shape, x.dtype) for x in plain]
@@ -724,12 +729,6 @@
 
     gated, new_theirs, up_near = lax.optimization_barrier((gated, new_theirs, up_near))
 
-    def summed(residual, mine, landed):
-        return (residual.astype(F32) + mine.astype(F32) + landed.astype(F32)).astype(BF16)
-
-    def own_rows(mine, others):
-        return lax.dynamic_slice_in_dim(jnp.stack([mine, others]), core_no * share, share, axis=1)
-
     pack_shapes = [struct((rows, width), BF16)]
     pack_shapes += [struct((rows, 2 * slab + depth), BF16)] * (n - 2)
     folded = share * width // rows
@@ -738,7 +737,7 @@
         grid=(1,),
         in_specs=[smem] * 1 + all_of(gated, up_own, up_theirs),
         out_specs=all_of(*pack_shapes),
-        out_shape=pack_shapes,
+        out_shape=[pltpu.HBM(pack_shapes[0].shape, BF16)] + pack_shapes[1:],
         compiler_params=small,
         name="pack",
     )(offs, gated, up_own, up_theirs)
@@ -765,15 +764,23 @@
         out_shape=first_shapes,
         compiler_params=small,
         name="first",
-    )(core, x_own, x_theirs, ahead_keep, ahead_landed, gated)
+    )(core, *in_hbm([x_own, x_theirs]), ahead_keep, ahead_landed, gated)
     ahead_in = along_sections(ahead_0, 1)
     packs_near = [to_partner(partner_pack)] + [from_host(packs[m - 1], m) for m in between]
-    back_send, back_keep = backward([after(up_0, ahead_0)], 0)
+    back_send, back_keep = backward(in_hbm([after(up_0, ahead_0)]), 0)
     back_send, back_keep, ahead_in, packs_near = lax.optimization_barrier(
         (back_send, back_keep, ahead_in, packs_near)
     )
     back_landed = swap_cores(back_send)
-    back_0 = summed(own_rows(up_own, up_theirs), back_keep, back_landed)
+    back_0 = pl.pallas_call(
+        settle_kernel,
+        grid=(1,),
+        in_specs=[smem] + all_of(up_own, up_theirs, back_keep, back_landed),
+        out_specs=all_of(halves[0])[0],
+        out_shape=halves[0],
+        compiler_params=small,
+        name="settle",
+    )(core, *in_hbm([up_own, up_theirs, back_keep]), back_landed)
     back_in = along_sections(back_0, -1)
 
     packs_beyond = [to_beyond(packs[n // 2 + m - 2], m) for m in between]
@@ -787,7 +794,7 @@
         + [hbm] * parts
         + all_of(*out_parts),
         out_specs=all_of(*halves),
-        out_shape=halves,
+        out_shape=kept_halves,
         scratch_shapes=[
             pltpu.VMEM((rows, width), BF16),
             pltpu.VMEM((rows, width), BF16),
@@ -803,11 +810,9 @@
         in_offs,
         offs,
         first_flag,
-        ahead_in,
+        *in_hbm([ahead_in]),
         ahead_their,
-        new_own,
-        new_theirs,
-        keep,
+        *in_hbm([new_own, new_theirs, keep]),
         *in_hbm(in_parts),
         *out_parts,
     )
@@ -825,7 +830,7 @@
         out_shape=cut_shapes,
         compiler_params=small,
         name="cut",
-    )(core, offs, last_flag, back_in, new_own, new_theirs)
+    )(core, offs, last_flag, back_in, *in_hbm([new_own, new_theirs]))
     up_their = swap_cores(up_mine)
     landed = [from_host(cuts[m - 1], m) for m in between]
     landed += [to_beyond(cuts[n // 2 + m - 2], m) for m in between]
@@ -839,11 +844,11 @@
         out_shape=message_shapes,
         compiler_params=small,
         name="message",
-    )(core, offs, first_flag, *message_inputs)
+    )(core, offs, first_flag, *in_hbm(message_inputs[:4]), *message_inputs[4:6], *in_hbm([back_0]))
     landed = [to_partner(message)] + landed
     back_send, back_keep = backward([up_mine, up_their], 1)
     back_send, back_keep, landed = lax.optimization_barrier((back_send, back_keep, landed))
-    last_inputs = [up_mine, back_keep, swap_cores(back_send)]
+    last_inputs = [up_mine, *in_hbm([back_keep]), swap_cores(back_send)]
     last_shapes = [halves[0], struct((share, width), BF16)]
     back_1, back_other = pl.pallas_call(
         last_kernel,
@@ -864,6 +869,7 @@
     grad_inputs = [gated, up_0, up_own, up_near, up_mine, up_their, landed_halves, landed_other]
     grad_inputs += packs_near + packs_beyond
     grad_inputs[0] = after(gated, back_1)
+    grad_inputs[8:] = in_hbm(grad_inputs[8:])
     grads = pl.pallas_call(
         functools.partial(grads_kernel, n, (ticks * length * n) ** (-0.5)),
         grid=(1,),

time: 199 us -> 196 us (0.985)
  local copies, waits for them, and re-layouts: 20.2 us -> 7.16 us
  waiting for transfers between devices: 95 us -> 102 us
  Pallas kernels: 17.4 us -> 21.9 us
  other arithmetic: 8.88 us -> 4.88 us
    unnamed x66 -> x52, local copies, waits for them, and re-layouts: 12.1 us -> 2.64 us
    ppermute x8, waiting for transfers between devices: 49.9 us -> 54 us  [from_partner(): return lax.ppermute(x, 'dp', [(h ^ 1, h) for h in hosts])]
    reshape x2, local copies, waits for them, and re-layouts: 2.73 us -> 0.16 us  [per_device(): m.reshape(m.shape[:2] + (-1,))]
    convert_element_type x1 -> x0, other arithmetic: 2.09 us -> none  [summed(): (residual.astype(F32) + mine.astype(F32) + landed.astype(F32)).astype(BF16)]
  transfers between devices with their start and end apart: 30 -> 30, of which waited for: 13 -> 15; matrix products, arithmetic and copies ran while one was open for 8% -> 4% of each run, Pallas kernels for 8% -> 11%
where the time goes in v14:
time: 196 us; the launch traced here: 193 us
  waiting for transfers between devices  102 us (52%)
  starting transfers between devices  54.4 us (28%)
  Pallas kernels  21.9 us (11%)
  local copies, waits for them, and re-layouts  7.16 us (4%)
  other arithmetic  4.88 us (2%)
  between operations  3.27 us (2%)
    ppermute x8, waiting for transfers between devices, from_partner(): return lax.ppermute(x, 'dp', [(h ^ 1, h) for h in hosts])  54 us
    ppermute x8, starting transfers between devices, from_partner(): return lax.ppermute(x, 'dp', [(h ^ 1, h) for h in hosts])  30 us
    ppermute x4, waiting for transfers between devices, to_partner(): return lax.ppermute(x, 'dp', [(h, h ^ 1) for h in hosts])  28.6 us
    ppermute x2, waiting for transfers between devices, to_beyond(): lax.ppermute(x, 'dp', [(hosts[k ^ m], hosts[k] ^ 1) for k in range(n // 2)])  16.3 us
    ppermute x7, starting transfers between devices, from_host(): lax.ppermute(x, 'dp', [(hosts[k ^ m], hosts[k]) for k in range(n // 2)])  8.29 us
    ppermute x7, starting transfers between devices, swap_cores(): return lax.ppermute(x, 'cores', [(c, cores - 1 - c) for c in range(cores)])  5.45 us
    ppermute x4, starting transfers between devices, to_partner(): return lax.ppermute(x, 'dp', [(h, h ^ 1) for h in hosts])  5.16 us
  transfers between devices with their start and end apart: 30, of which 15 were waited for; matrix products, arithmetic and copies ran while one was open for 4% of the time, Pallas kernels for 11%

profile of v14, /device:TPU:5, one launch (start us, length us, event | category | flops | bytes accessed | tf_op | source)
XLA Modules:
  0.0 193.2 jit_solution(11467358757504361069)
XLA Ops:
  0.7 2.1 %collective-permute-start = (bf16[512,2048]{1,0:T(8,128)(2,1)}, bf16[512,2048]{1,0:T(8,128)(2,1)}, u32[]{:S(2)}, u32[]{:S(2)}) collective-permute-start(bf16[512,2048]{1,0:T(8,128)(2,1)} %bitcast.77), channel_id=1, source_target_pairs={{4,2},{2,4},{5,3},{3,5},{12,10},{10,12},{13,11},{11,13},{20,18},{1... | collective-permute-start | bytes 6291464 | tf_op jit(solution)/shard_map/ppermute | solution.py:549
  2.8 2.7 %slice_bitcast_fusion = (bf16[256,2048]{1,0:T(8,128)(2,1)S(1)}, bf16[256,2048]{1,0:T(8,128)(2,1)}) fusion(bf16[1,512,2048]{2,1,0:T(8,128)(2,1)} %param.17), kind=kLoop, calls=%fused_computation | loop fusion | bytes 4194304 | tf_op jit(solution)/shard_map/slice | solution.py:576
  5.5 5.4 %collective-permute-start.1 = (bf16[256,2048]{1,0:T(8,128)(2,1)}, bf16[256,2048]{1,0:T(8,128)(2,1)}, u32[]{:S(2)}, u32[]{:S(2)}) collective-permute-start(bf16[256,2048]{1,0:T(8,128)(2,1)} %get-tuple-element.152), channel_id=1, source_target_pairs={{0,2},{6,4},{1,3},{7,5},{8,10},{14,12},{9,11},{15,13},{16,18},{22,... | collective-permute-start | bytes 3145736 | tf_op jit(solution)/shard_map/ppermute | solution.py:543
  10.9 2.2 %collective-permute-start.2 = (bf16[256,2048]{1,0:T(8,128)(2,1)S(1)}, bf16[256,2048]{1,0:T(8,128)(2,1)}, u32[]{:S(2)}, u32[]{:S(2)}) collective-permute-start(bf16[256,2048]{1,0:T(8,128)(2,1)S(1)} %get-tuple-element.151), channel_id=1, source_target_pairs={{0,2},{6,4},{1,3},{7,5},{8,10},{14,12},{9,11},{15,13},{16,18},{22,... | collective-permute-start | bytes 3145736 | tf_op jit(solution)/shard_map/ppermute | solution.py:543
  18.1 13.7 %collective-permute-done.1.refs_8_.refs_18_.refs_11_.refs_19_ = bf16[256,2048]{1,0:T(8,128)(2,1)} collective-permute-done((bf16[256,2048]{1,0:T(8,128)(2,1)}, bf16[256,2048]{1,0:T(8,128)(2,1)}, u32[]{:S(2)}, u32[]{:S(2)}) %collective-permute-start.1) | collective-permute-done | bytes 1048608 | tf_op jit(solution)/shard_map/ppermute | solution.py:543
  31.8 1.6 collective-permute-start.7
  33.4 20.7 %collective-permute-done.2.refs_9_.refs_19_.refs_12_.refs_20_ = bf16[256,2048]{1,0:T(8,128)(2,1)} collective-permute-done((bf16[256,2048]{1,0:T(8,128)(2,1)S(1)}, bf16[256,2048]{1,0:T(8,128)(2,1)}, u32[]{:S(2)}, u32[]{:S(2)}) %collective-permute-start.2) | collective-permute-done | bytes 1048608 | tf_op jit(solution)/shard_map/ppermute | solution.py:543
  54.6 4.2 %collective-permute-start.6 = (s32[2,5,17]{2,0,1:T(2,128)S(1)}, s32[2,5,17]{2,0,1:T(2,128)S(1)}, u32[]{:S(2)}, u32[]{:S(2)}) collective-permute-start(s32[2,5,17]{2,0,1:T(2,128)S(1)} %add_add_fusion), channel_id=1, source_target_pairs={{0,2},{6,4},{1,3},{7,5},{8,10},{14,12},{9,11},{15,13},{16,18},{22,... | collective-permute-start | bytes 2048 | tf_op jit(solution)/shard_map/ppermute | solution.py:543
  58.9 2.2 %collective-permute-start.4 = (bf16[2,96,2048]{2,1,0:T(8,128)(2,1)}, bf16[2,96,2048]{2,1,0:T(8,128)(2,1)}, u32[]{:S(2)}, u32[]{:S(2)}) collective-permute-start(bf16[2,96,2048]{2,1,0:T(8,128)(2,1)} %bitcast.12.refs_3_.refs_10_.refs_11_), channel_id=1, source_target_pairs={{0,2},{6,4},{1,3},{7,5},{8,10},{14,12},{9,11},{15,13},{16,18},{22,... | collective-permute-start | bytes 2359304 | tf_op jit(solution)/shard_map/ppermute | solution.py:543
  61.0 1.7 collective-permute-start.8
  62.7 2.4 %select_bitcast_fusion = (bf16[96,2048]{1,0:T(8,128)(2,1)}, bf16[96,2048]{1,0:T(8,128)(2,1)S(1)}, bf16[96,2048]{1,0:T(8,128)(2,1)S(1)}) fusion(bf16[2,96,2048]{2,1,0:T(8,128)(2,1)} %param.14, bf16[2,96,2048]{2,1,0:T(8,128)(2,1)} %param.12, pred[]{:T(512)S(6)} %eq.44, bf16[1,96,2048]{2,1,0:T(8,128)(2,1)S(1)} %copy-done.20, bf16[1,96,2048]{2,1,0:T(8,128)(2,1)} %param.15, ...), kind=kLoop, calls=%fused_computation.6 | loop fusion | flops 589824 | bytes 3538946 | tf_op jit(solution)/shard_map/jit(_where)/select_n | solution.py:604
  65.4 4.2 %collective-permute-start.3 = (bf16[96,2048]{1,0:T(8,128)(2,1)S(1)}, bf16[96,2048]{1,0:T(8,128)(2,1)S(1)}, u32[]{:S(2)}, u32[]{:S(2)}) collective-permute-start(bf16[96,2048]{1,0:T(8,128)(2,1)S(1)} %get-tuple-element.154.refs_1_.own), channel_id=1, source_target_pairs={{0,2},{6,4},{1,3},{7,5},{8,10},{14,12},{9,11},{15,13},{16,18},{22,... | collective-permute-start | bytes 1179656 | tf_op jit(solution)/shard_map/ppermute | solution.py:543
  71.9 10.5 %collective-permute-done.4.refs_4_.refs_11_.refs_12_ = bf16[2,96,2048]{2,1,0:T(8,128)(2,1)} collective-permute-done((bf16[2,96,2048]{2,1,0:T(8,128)(2,1)}, bf16[2,96,2048]{2,1,0:T(8,128)(2,1)}, u32[]{:S(2)}, u32[]{:S(2)}) %collective-permute-start.4) | collective-permute-done | bytes 786464 | tf_op jit(solution)/shard_map/ppermute | solution.py:543
  83.1 5.5 %collective-permute-start.11 = (bf16[96,2048]{1,0:T(8,128)(2,1)S(1)}, bf16[96,2048]{1,0:T(8,128)(2,1)S(1)}, u32[]{:S(2)}, u32[]{:S(2)}) collective-permute-start(bf16[96,2048]{1,0:T(8,128)(2,1)S(1)} %get-tuple-element.93.up_own.own), channel_id=1, source_target_pairs={{0,2},{6,4},{1,3},{7,5},{8,10},{14,12},{9,11},{15,13},{16,18},{22,... | collective-permute-start | bytes 1179656 | tf_op jit(solution)/shard_map/ppermute | solution.py:543
  88.7 2.1 %collective-permute-done.3.refs_2_.theirs = bf16[96,2048]{1,0:T(8,128)(2,1)S(1)} collective-permute-done((bf16[96,2048]{1,0:T(8,128)(2,1)S(1)}, bf16[96,2048]{1,0:T(8,128)(2,1)S(1)}, u32[]{:S(2)}, u32[]{:S(2)}) %collective-permute-start.3) | collective-permute-done | bytes 393248 | tf_op jit(solution)/shard_map/ppermute | solution.py:543
  92.8 4.9 %collective-permute-start.9 = (bf16[96,2048]{1,0:T(8,128)(2,1)S(1)}, bf16[96,2048]{1,0:T(8,128)(2,1)S(1)}, u32[]{:S(2)}, u32[]{:S(2)}) collective-permute-start(bf16[96,2048]{1,0:T(8,128)(2,1)S(1)} %copy-done.17), channel_id=1, source_target_pairs={{0,2},{6,4},{1,3},{7,5},{8,10},{14,12},{9,11},{15,13},{16,18},{22,... | collective-permute-start | bytes 1179656 | tf_op jit(solution)/shard_map/ppermute | solution.py:543
  98.7 2.1 %project.1 = (bf16[3,192,512]{2,1,0:T(8,128)(2,1)S(1)}, f32[2,192,512]{2,1,0:T(8,128)}, bf16[2,192,1536]{2,1,0:T(8,128)(2,1)}, f32[2,192,2048]{2,1,0:T(8,128)}, ...) custom-call(s32[1]{0:T(128)} %bitcast.1.host, s32[6]{0:T(128)S(1)} %stack.73.refs_0_.refs_1_, ...), custom_call_target="tpu_custom_call" | custom-call | flops 4831838208 | bytes 20971520 | tf_op jit(solution)/shard_map/project/pallas_call | solution.py:685
  100.8 6.8 %collective-permute-done.9.refs_7_.new_theirs = bf16[96,2048]{1,0:T(8,128)(2,1)S(1)} collective-permute-done((bf16[96,2048]{1,0:T(8,128)(2,1)S(1)}, bf16[96,2048]{1,0:T(8,128)(2,1)S(1)}, u32[]{:S(2)}, u32[]{:S(2)}) %collective-permute-start.9) | collective-permute-done | bytes 393248 | tf_op jit(solution)/shard_map/ppermute | solution.py:543
  107.6 1.7 pack.1
  110.5 1.9 collective-permute-start.14
  116.5 1.4 collective-permute-start.15
  118.0 1.7 backward.2
  119.7 20.7 %collective-permute-done.16.pack.rest_0_ = bf16[192,1536]{1,0:T(8,128)(2,1)S(1)} collective-permute-done((bf16[192,1536]{1,0:T(8,128)(2,1)S(1)}, bf16[192,1536]{1,0:T(8,128)(2,1)S(1)}, u32[]{:S(2)}, u32[]{:S(2)}) %collective-permute-start.16) | collective-permute-done | bytes 589856 | tf_op jit(solution)/shard_map/ppermute | solution.py:546
  142.0 1.5 collective-permute-start.21
  146.6 2.5 %forward.1 = (bf16[2,48,2048]{2,1,0:T(8,128)(2,1)}, bf16[2,48,2048]{2,1,0:T(8,128)(2,1)}) custom-call(s32[1]{0:T(128)} %bitcast.1.host, s32[1]{0:T(128)} %bitcast.2.core.refs_0_, s32[6]{0:T(128)S(1)} %stack.73.refs_0_.refs_1_, s32[4]{0:T(128)S(1)} %add_multiply_fusion.offs.refs_2_, s32[1]{0:T(128)} %bitcast.33.refs_3_.fresh, ...), custom_call_target="tpu_custom_call" | custom-call | flops 3221225472 | bytes 20971520 | tf_op jit(solution)/shard_map/forward/pallas_call | solution.py:788
  149.2 10.2 %collective-permute-done.21.rest_2_ = bf16[192,1536]{1,0:T(8,128)(2,1)} collective-permute-done((bf16[192,1536]{1,0:T(8,128)(2,1)}, bf16[192,1536]{1,0:T(8,128)(2,1)}, u32[]{:S(2)}, u32[]{:S(2)}) %collective-permute-start.21) | collective-permute-done | bytes 589856 | tf_op jit(solution)/shard_map/ppermute | solution.py:552
  162.4 1.8 message.1
  167.4 1.7 backward.3
  169.1 6.1 %collective-permute-done.26 = bf16[96,512]{1,0:T(8,128)(2,1)S(1)} collective-permute-done((bf16[96,512]{1,0:T(8,128)(2,1)S(1)}, bf16[96,512]{1,0:T(8,128)(2,1)S(1)}, u32[]{:S(2)}, u32[]{:S(2)}) %collective-permute-start.26) | collective-permute-done | bytes 98336 | tf_op jit(solution)/shard_map/ppermute | solution.py:552
  175.3 5.3 %collective-permute-done.24.message = bf16[96,2560]{1,0:T(8,128)(2,1)S(1)} collective-permute-done((bf16[96,2560]{1,0:T(8,128)(2,1)S(1)}, bf16[96,2560]{1,0:T(8,128)(2,1)S(1)}, u32[]{:S(2)}, u32[]{:S(2)}) %collective-permute-start.24) | collective-permute-done | bytes 491552 | tf_op jit(solution)/shard_map/ppermute | solution.py:546
  186.5 3.2 %grads.1 = f32[512,512]{1,0:T(8,128)} custom-call(s32[1]{0:T(128)} %bitcast.1.host, s32[1]{0:T(128)} %bitcast.2.core.refs_0_, s32[4]{0:T(128)S(1)} %add_multiply_fusion.offs.refs_2_, bf16[3,192,512]{2,1,0:T(8,128)(2,1)S(1)} %get-tuple-element.145.gated, bf16[192,2048]{1,0:T(8,128)(2,1)S(1)} %copy-done.5, bf16[96,2048]{1,0:T(8,128)(2,1)S(1)} %copy-done.2, ...), custom_call_target="tpu_custom_call" | custom-call | flops 402653184 | bytes 2621440 | tf_op jit(solution)/shard_map/grads/pallas_call | solution.py:873
  189.7 2.7 %collective-permute-done.28 = bf16[48,2048]{1,0:T(8,128)(2,1)S(1)} collective-permute-done((bf16[48,2048]{1,0:T(8,128)(2,1)S(1)}, bf16[48,2048]{1,0:T(8,128)(2,1)S(1)}, u32[]{:S(2)}, u32[]{:S(2)}) %collective-permute-start.28) | collective-permute-done | bytes 196640 | tf_op jit(solution)/shard_map/ppermute | solution.py:546
  (129 shorter events, 32.6 us)
Async XLA Ops:
  0.7 53.7 %copy-start.22 = (s32[1,5,4,4]{1,3,2,0:T(4,128)S(1)}, s32[1,5,4,4]{1,3,2,0:T(4,128)}, u32[]{:S(2)}) copy-start(s32[1,5,4,4]{1,3,2,0:T(4,128)} %param.22) | copy-start | bytes 964
  0.7 62.0 %copy-start.20 = (bf16[1,96,2048]{2,1,0:T(8,128)(2,1)S(1)}, bf16[1,96,2048]{2,1,0:T(8,128)(2,1)}, u32[]{:S(2)}) copy-start(bf16[1,96,2048]{2,1,0:T(8,128)(2,1)} %param.13) | copy-start | bytes 1179652
  0.7 53.4 %collective-permute-start = (bf16[512,2048]{1,0:T(8,128)(2,1)}, bf16[512,2048]{1,0:T(8,128)(2,1)}, u32[]{:S(2)}, u32[]{:S(2)}) collective-permute-start(bf16[512,2048]{1,0:T(8,128)(2,1)} %bitcast.77), channel_id=1, source_target_pairs={{4,2},{2,4},{5,3},{3,5},{12,10},{10,12},{13,11},{11,13},{20,18},{1... | collective-permute-start | bytes 6291464 | tf_op jit(solution)/shard_map/ppermute | solution.py:549
  5.5 26.2 %collective-permute-start.1 = (bf16[256,2048]{1,0:T(8,128)(2,1)}, bf16[256,2048]{1,0:T(8,128)(2,1)}, u32[]{:S(2)}, u32[]{:S(2)}) collective-permute-start(bf16[256,2048]{1,0:T(8,128)(2,1)} %get-tuple-element.152), channel_id=1, source_target_pairs={{0,2},{6,4},{1,3},{7,5},{8,10},{14,12},{9,11},{15,13},{16,18},{22,... | collective-permute-start | bytes 3145736 | tf_op jit(solution)/shard_map/ppermute | solution.py:543
  10.9 43.2 %collective-permute-start.2 = (bf16[256,2048]{1,0:T(8,128)(2,1)S(1)}, bf16[256,2048]{1,0:T(8,128)(2,1)}, u32[]{:S(2)}, u32[]{:S(2)}) collective-permute-start(bf16[256,2048]{1,0:T(8,128)(2,1)S(1)} %get-tuple-element.151), channel_id=1, source_target_pairs={{0,2},{6,4},{1,3},{7,5},{8,10},{14,12},{9,11},{15,13},{16,18},{22,... | collective-permute-start | bytes 3145736 | tf_op jit(solution)/shard_map/ppermute | solution.py:543
  13.2 52.2 %collective-permute-start.5 = (bf16[512,512]{1,0:T(8,128)(2,1)S(1)}, bf16[512,512]{1,0:T(8,128)(2,1)S(1)}, u32[]{:S(2)}, u32[]{:S(2)}) collective-permute-start(bf16[512,512]{1,0:T(8,128)(2,1)S(1)} %bitcast.70), channel_id=1, source_target_pairs={{0,2},{6,4},{1,3},{7,5},{8,10},{14,12},{9,11},{15,13},{16,18},{22,... | collective-permute-start | bytes 1572872 | tf_op jit(solution)/shard_map/ppermute | solution.py:543
  31.8 51.4 %collective-permute-start.7 = (bf16[256,2048]{1,0:T(8,128)(2,1)}, bf16[256,2048]{1,0:T(8,128)(2,1)}, u32[]{:S(2)}, u32[]{:S(2)}) collective-permute-start(bf16[256,2048]{1,0:T(8,128)(2,1)} %collective-permute-done.1.refs_8_.refs_18_.refs_11_.refs_19_), channel_id=1, source_target_pairs={{4,2},{2,4},{5,3},{3,5},{12,10},{10,12},{13,11},{11,13},{20,18},{1... | collective-permute-start | bytes 3145736 | tf_op jit(solution)/shard_map/ppermute | solution.py:549
  54.6 14.9 %collective-permute-start.6 = (s32[2,5,17]{2,0,1:T(2,128)S(1)}, s32[2,5,17]{2,0,1:T(2,128)S(1)}, u32[]{:S(2)}, u32[]{:S(2)}) collective-permute-start(s32[2,5,17]{2,0,1:T(2,128)S(1)} %add_add_fusion), channel_id=1, source_target_pairs={{0,2},{6,4},{1,3},{7,5},{8,10},{14,12},{9,11},{15,13},{16,18},{22,... | collective-permute-start | bytes 2048 | tf_op jit(solution)/shard_map/ppermute | solution.py:543
  58.9 23.6 %collective-permute-start.4 = (bf16[2,96,2048]{2,1,0:T(8,128)(2,1)}, bf16[2,96,2048]{2,1,0:T(8,128)(2,1)}, u32[]{:S(2)}, u32[]{:S(2)}) collective-permute-start(bf16[2,96,2048]{2,1,0:T(8,128)(2,1)} %bitcast.12.refs_3_.refs_10_.refs_11_), channel_id=1, source_target_pairs={{0,2},{6,4},{1,3},{7,5},{8,10},{14,12},{9,11},{15,13},{16,18},{22,... | collective-permute-start | bytes 2359304 | tf_op jit(solution)/shard_map/ppermute | solution.py:543
  61.0 31.7 %collective-permute-start.8 = (bf16[256,2048]{1,0:T(8,128)(2,1)}, bf16[256,2048]{1,0:T(8,128)(2,1)}, u32[]{:S(2)}, u32[]{:S(2)}) collective-permute-start(bf16[256,2048]{1,0:T(8,128)(2,1)} %collective-permute-done.2.refs_9_.refs_19_.refs_12_.refs_20_), channel_id=1, source_target_pairs={{4,2},{2,4},{5,3},{3,5},{12,10},{10,12},{13,11},{11,13},{20,18},{1... | collective-permute-start | bytes 3145736 | tf_op jit(solution)/shard_map/ppermute | solution.py:549
  65.4 25.4 %collective-permute-start.3 = (bf16[96,2048]{1,0:T(8,128)(2,1)S(1)}, bf16[96,2048]{1,0:T(8,128)(2,1)S(1)}, u32[]{:S(2)}, u32[]{:S(2)}) collective-permute-start(bf16[96,2048]{1,0:T(8,128)(2,1)S(1)} %get-tuple-element.154.refs_1_.own), channel_id=1, source_target_pairs={{0,2},{6,4},{1,3},{7,5},{8,10},{14,12},{9,11},{15,13},{16,18},{22,... | collective-permute-start | bytes 1179656 | tf_op jit(solution)/shard_map/ppermute | solution.py:543
  70.6 38.7 %collective-permute-start.12 = (bf16[512,512]{1,0:T(8,128)(2,1)S(1)}, bf16[512,512]{1,0:T(8,128)(2,1)S(1)}, u32[]{:S(2)}, u32[]{:S(2)}) collective-permute-start(bf16[512,512]{1,0:T(8,128)(2,1)S(1)} %bitcast.71), channel_id=1, source_target_pairs={{4,2},{2,4},{5,3},{3,5},{12,10},{10,12},{13,11},{11,13},{20,18},{1... | collective-permute-start | bytes 1572872 | tf_op jit(solution)/shard_map/ppermute | solution.py:549
  82.4 26.9 %collective-permute-start.13 = (bf16[512,512]{1,0:T(8,128)(2,1)S(1)}, bf16[512,512]{1,0:T(8,128)(2,1)S(1)}, u32[]{:S(2)}, u32[]{:S(2)}) collective-permute-start(bf16[512,512]{1,0:T(8,128)(2,1)S(1)} %collective-permute-done.5.rest_1_.refs_13_.refs_16_.refs_14_), channel_id=1, source_target_pairs={{4,2},{2,4},{5,3},{3,5},{12,10},{10,12},{13,11},{11,13},{20,18},{1... | collective-permute-start | bytes 1572872 | tf_op jit(solution)/shard_map/ppermute | solution.py:549
  83.1 24.5 %collective-permute-start.11 = (bf16[96,2048]{1,0:T(8,128)(2,1)S(1)}, bf16[96,2048]{1,0:T(8,128)(2,1)S(1)}, u32[]{:S(2)}, u32[]{:S(2)}) collective-permute-start(bf16[96,2048]{1,0:T(8,128)(2,1)S(1)} %get-tuple-element.93.up_own.own), channel_id=1, source_target_pairs={{0,2},{6,4},{1,3},{7,5},{8,10},{14,12},{9,11},{15,13},{16,18},{22,... | collective-permute-start | bytes 1179656 | tf_op jit(solution)/shard_map/ppermute | solution.py:543
  91.5 9.3 %collective-permute-start.10 = (bf16[96,512]{1,0:T(8,128)(2,1)S(1)}, bf16[96,512]{1,0:T(8,128)(2,1)S(1)}, u32[]{:S(2)}, u32[]{:S(2)}) collective-permute-start(bf16[96,512]{1,0:T(8,128)(2,1)S(1)} %constant_dynamic-slice_fusion), channel_id=1, source_target_pairs={{2,0},{4,6},{3,1},{5,7},{10,8},{12,14},{11,9},{13,15},{18,16},{20,... | collective-permute-start | bytes 294920 | tf_op jit(solution)/shard_map/ppermute | solution.py:546
  92.8 14.8 %collective-permute-start.9 = (bf16[96,2048]{1,0:T(8,128)(2,1)S(1)}, bf16[96,2048]{1,0:T(8,128)(2,1)S(1)}, u32[]{:S(2)}, u32[]{:S(2)}) collective-permute-start(bf16[96,2048]{1,0:T(8,128)(2,1)S(1)} %copy-done.17), channel_id=1, source_target_pairs={{0,2},{6,4},{1,3},{7,5},{8,10},{14,12},{9,11},{15,13},{16,18},{22,... | collective-permute-start | bytes 1179656 | tf_op jit(solution)/shard_map/ppermute | solution.py:543
  110.5 3.3 %collective-permute-start.14 = (bf16[2,48,2048]{2,1,0:T(8,128)(2,1)S(1)}, bf16[2,48,2048]{2,1,0:T(8,128)(2,1)S(1)}, u32[]{:S(2)}, u32[]{:S(2)}) collective-permute-start(bf16[2,48,2048]{2,1,0:T(8,128)(2,1)S(1)} %get-tuple-element.104), channel_id=1, source_target_pairs={{0,1},{1,0},{2,3},{3,2},{4,5},{5,4},{6,7},{7,6},{8,9},{9,8},{10,11... | collective-permute-start | bytes 1179656 | tf_op jit(solution)/shard_map/ppermute | solution.py:557
  112.5 7.2 %collective-permute-start.17 = (bf16[192,1536]{1,0:T(8,128)(2,1)S(1)}, bf16[192,1536]{1,0:T(8,128)(2,1)S(1)}, u32[]{:S(2)}, u32[]{:S(2)}) collective-permute-start(bf16[192,1536]{1,0:T(8,128)(2,1)S(1)} %get-tuple-element.118), channel_id=1, source_target_pairs={{4,2},{2,4},{5,3},{3,5},{12,10},{10,12},{13,11},{11,13},{20,18},{1... | collective-permute-start | bytes 1769480 | tf_op jit(solution)/shard_map/ppermute | solution.py:549
  115.2 25.1 %collective-permute-start.16 = (bf16[192,1536]{1,0:T(8,128)(2,1)S(1)}, bf16[192,1536]{1,0:T(8,128)(2,1)S(1)}, u32[]{:S(2)}, u32[]{:S(2)}) collective-permute-start(bf16[192,1536]{1,0:T(8,128)(2,1)S(1)} %get-tuple-element.117), channel_id=1, source_target_pairs={{2,0},{4,6},{3,1},{5,7},{10,8},{12,14},{11,9},{13,15},{18,16},{20,... | collective-permute-start | bytes 1769480 | tf_op jit(solution)/shard_map/ppermute | solution.py:546
  116.5 3.1 %collective-permute-start.15 = (bf16[2,48,2048]{2,1,0:T(8,128)(2,1)S(1)}, bf16[2,48,2048]{2,1,0:T(8,128)(2,1)}, u32[]{:S(2)}, u32[]{:S(2)}) collective-permute-start(bf16[2,48,2048]{2,1,0:T(8,128)(2,1)S(1)} %get-tuple-element.105.ahead_0), channel_id=1, source_target_pairs={{2,10},{4,12},{10,18},{12,20},{18,26},{20,28},{3,11},{5,13},{11,19... | collective-permute-start | bytes 1179656 | tf_op jit(solution)/shard_map/ppermute | solution.py:566
  141.1 2.7 %collective-permute-start.19 = (bf16[2,48,2048]{2,1,0:T(8,128)(2,1)S(1)}, bf16[2,48,2048]{2,1,0:T(8,128)(2,1)S(1)}, u32[]{:S(2)}, u32[]{:S(2)}) collective-permute-start(bf16[2,48,2048]{2,1,0:T(8,128)(2,1)S(1)} %get-tuple-element.123), channel_id=1, source_target_pairs={{0,1},{1,0},{2,3},{3,2},{4,5},{5,4},{6,7},{7,6},{8,9},{9,8},{10,11... | collective-permute-start | bytes 1179656 | tf_op jit(solution)/shard_map/ppermute | solution.py:557
  142.0 4.7 %collective-permute-start.18 = (bf16[2,48,2048]{2,1,0:T(8,128)(2,1)}, bf16[2,48,2048]{2,1,0:T(8,128)(2,1)S(1)}, u32[]{:S(2)}, u32[]{:S(2)}) collective-permute-start(bf16[2,48,2048]{2,1,0:T(8,128)(2,1)} %collective-permute-done.15.refs_4_.passed), channel_id=1, source_target_pairs={{0,1},{1,0},{2,3},{3,2},{4,5},{5,4},{6,7},{7,6},{8,9},{9,8},{10,11... | collective-permute-start | bytes 1179656 | tf_op jit(solution)/shard_map/ppermute | solution.py:557
  142.0 17.5 %collective-permute-start.21 = (bf16[192,1536]{1,0:T(8,128)(2,1)}, bf16[192,1536]{1,0:T(8,128)(2,1)}, u32[]{:S(2)}, u32[]{:S(2)}) collective-permute-start(bf16[192,1536]{1,0:T(8,128)(2,1)} %get-tuple-element.124), channel_id=1, source_target_pairs={{4,0},{2,6},{5,1},{3,7},{12,8},{10,14},{13,9},{11,15},{20,16},{18,... | collective-permute-start | bytes 1769480 | tf_op jit(solution)/shard_map/ppermute | solution.py:552
  145.2 14.2 %collective-permute-start.20 = (bf16[2,48,2048]{2,1,0:T(8,128)(2,1)S(1)}, bf16[2,48,2048]{2,1,0:T(8,128)(2,1)}, u32[]{:S(2)}, u32[]{:S(2)}) collective-permute-start(bf16[2,48,2048]{2,1,0:T(8,128)(2,1)S(1)} %settle.1.back.back_0), channel_id=1, source_target_pairs={{10,2},{12,4},{18,10},{20,12},{26,18},{28,20},{11,3},{13,5},{19,11... | collective-permute-start | bytes 1179656 | tf_op jit(solution)/shard_map/ppermute | solution.py:566
  159.4 2.9 %collective-permute-start.22 = (bf16[2,48,2048]{2,1,0:T(8,128)(2,1)}, bf16[2,48,2048]{2,1,0:T(8,128)(2,1)S(1)}, u32[]{:S(2)}, u32[]{:S(2)}) collective-permute-start(bf16[2,48,2048]{2,1,0:T(8,128)(2,1)} %get-tuple-element.126), channel_id=1, source_target_pairs={{0,1},{1,0},{2,3},{3,2},{4,5},{5,4},{6,7},{7,6},{8,9},{9,8},{10,11... | collective-permute-start | bytes 1179656 | tf_op jit(solution)/shard_map/ppermute | solution.py:557
  162.1 5.3 %collective-permute-start.23 = (bf16[2,48,2048]{2,1,0:T(8,128)(2,1)S(1)}, bf16[2,48,2048]{2,1,0:T(8,128)(2,1)S(1)}, u32[]{:S(2)}, u32[]{:S(2)}) collective-permute-start(bf16[2,48,2048]{2,1,0:T(8,128)(2,1)S(1)} %get-tuple-element.128.up.refs_3_.mine), channel_id=1, source_target_pairs={{0,1},{1,0},{2,3},{3,2},{4,5},{5,4},{6,7},{7,6},{8,9},{9,8},{10,11... | collective-permute-start | bytes 1179656 | tf_op jit(solution)/shard_map/ppermute | solution.py:557
  164.1 16.4 %collective-permute-start.24 = (bf16[96,2560]{1,0:T(8,128)(2,1)S(1)}, bf16[96,2560]{1,0:T(8,128)(2,1)S(1)}, u32[]{:S(2)}, u32[]{:S(2)}) collective-permute-start(bf16[96,2560]{1,0:T(8,128)(2,1)S(1)} %get-tuple-element.133), channel_id=1, source_target_pairs={{2,0},{4,6},{3,1},{5,7},{10,8},{12,14},{11,9},{13,15},{18,16},{20,... | collective-permute-start | bytes 1474568 | tf_op jit(solution)/shard_map/ppermute | solution.py:546
  165.4 3.7 %collective-permute-start.25 = (bf16[96,512]{1,0:T(8,128)(2,1)S(1)}, bf16[96,512]{1,0:T(8,128)(2,1)S(1)}, u32[]{:S(2)}, u32[]{:S(2)}) collective-permute-start(bf16[96,512]{1,0:T(8,128)(2,1)S(1)} %get-tuple-element.134), channel_id=1, source_target_pairs={{4,2},{2,4},{5,3},{3,5},{12,10},{10,12},{13,11},{11,13},{20,18},{1... | collective-permute-start | bytes 294920 | tf_op jit(solution)/shard_map/ppermute | solution.py:549
  166.1 9.2 %collective-permute-start.26 = (bf16[96,512]{1,0:T(8,128)(2,1)S(1)}, bf16[96,512]{1,0:T(8,128)(2,1)S(1)}, u32[]{:S(2)}, u32[]{:S(2)}) collective-permute-start(bf16[96,512]{1,0:T(8,128)(2,1)S(1)} %get-tuple-element.135), channel_id=1, source_target_pairs={{4,0},{2,6},{5,1},{3,7},{12,8},{10,14},{13,9},{11,15},{20,16},{18,... | collective-permute-start | bytes 294920 | tf_op jit(solution)/shard_map/ppermute | solution.py:552
  180.6 2.6 %collective-permute-start.27 = (bf16[2,48,2048]{2,1,0:T(8,128)(2,1)S(1)}, bf16[2,48,2048]{2,1,0:T(8,128)(2,1)S(1)}, u32[]{:S(2)}, u32[]{:S(2)}) collective-permute-start(bf16[2,48,2048]{2,1,0:T(8,128)(2,1)S(1)} %get-tuple-element.138), channel_id=1, source_target_pairs={{0,1},{1,0},{2,3},{3,2},{4,5},{5,4},{6,7},{7,6},{8,9},{9,8},{10,11... | collective-permute-start | bytes 1179656 | tf_op jit(solution)/shard_map/ppermute | solution.py:557
  181.8 4.7 %collective-permute-start.29 = (bf16[2,96,512]{2,1,0:T(8,128)(2,1)S(1)}, bf16[2,96,512]{2,1,0:T(8,128)(2,1)S(1)}, u32[]{:S(2)}, u32[]{:S(2)}) collective-permute-start(bf16[2,96,512]{2,1,0:T(8,128)(2,1)S(1)} %pad_maximum_fusion.halves), channel_id=1, source_target_pairs={{0,1},{1,0},{2,3},{3,2},{4,5},{5,4},{6,7},{7,6},{8,9},{9,8},{10,11... | collective-permute-start | bytes 589832 | tf_op jit(solution)/shard_map/ppermute | solution.py:557
  184.4 8.0 %collective-permute-start.28 = (bf16[48,2048]{1,0:T(8,128)(2,1)S(1)}, bf16[48,2048]{1,0:T(8,128)(2,1)S(1)}, u32[]{:S(2)}, u32[]{:S(2)}) collective-permute-start(bf16[48,2048]{1,0:T(8,128)(2,1)S(1)} %get-tuple-element.144), channel_id=1, source_target_pairs={{2,0},{4,6},{3,1},{5,7},{10,8},{12,14},{11,9},{13,15},{18,16},{20,... | collective-permute-start | bytes 589832 | tf_op jit(solution)/shard_map/ppermute | solution.py:546
  (24 other events, 449.9 us)

commit v15 on v14

--- a/solution.py
+++ b/solution.py
@@ -269,19 +269,20 @@
         copy.start()
     for i in first + second:
         copies[i].start()
+    for copy in up_copies:
+        copy.wait()
+    for i in first:
+        copies[i].wait()
     for of_head in by_head:
         for copy in of_head:
             copy.start()
     for i in (7, 8):
         copies[i].start()
-    for copy in up_copies:
-        copy.wait()
     depth = out_parts[0].shape[1]
     length = x_own.shape[0]
     grad_gated = None
     for j in range(n):
         columns = pl.ds(pl.multiple_of(offs[j], depth), depth)
-        copies[first[j]].wait()
         term = dot_nt(ups[:, columns], out_parts[j][...])
         grad_gated = term if grad_gated is None else grad_gated + term
     grad_gated = grad_gated.astype(BF16).astype(F32)
@@ -783,7 +784,7 @@
     )(core, *in_hbm([up_own, up_theirs, back_keep]), back_landed)
     back_in = along_sections(back_0, -1)
 
-    packs_beyond = [to_beyond(packs[n // 2 + m - 2], m) for m in between]
+    packs_beyond = [to_beyond(after(packs[n // 2 + m - 2], back_0), m) for m in between]
     ahead_their = swap_cores(ahead_in)
     ahead_send, ahead_keep = pl.pallas_call(
         on_host(functools.partial(forward_kernel, parts, heads)),
@@ -845,9 +846,10 @@
         compiler_params=small,
         name="message",
     )(core, offs, first_flag, *in_hbm(message_inputs[:4]), *message_inputs[4:6], *in_hbm([back_0]))
-    landed = [to_partner(message)] + landed
+    landed = landed + [to_partner(message)]
     back_send, back_keep = backward([up_mine, up_their], 1)
     back_send, back_keep, landed = lax.optimization_barrier((back_send, back_keep, landed))
+    landed = landed[-1:] + landed[:-1]
     last_inputs = [up_mine, *in_hbm([back_keep]), swap_cores(back_send)]
     last_shapes = [halves[0], struct((share, width), BF16)]
     back_1, back_other = pl.pallas_call(

time: 196 us -> 199 us (1.015)
  waiting for transfers between devices: 102 us -> 105 us
where the time goes in v15:
time: 199 us; the launch traced here: 196 us
  waiting for transfers between devices  105 us (53%)
  starting transfers between devices  54.3 us (27%)
  Pallas kernels  21.9 us (11%)
  local copies, waits for them, and re-layouts  6.35 us (3%)
  other arithmetic  4.88 us (2%)
  between operations  3.28 us (2%)
    ppermute x8, waiting for transfers between devices, from_partner(): return lax.ppermute(x, 'dp', [(h ^ 1, h) for h in hosts])  54 us
    ppermute x8, starting transfers between devices, from_partner(): return lax.ppermute(x, 'dp', [(h ^ 1, h) for h in hosts])  30 us
    ppermute x4, waiting for transfers between devices, to_partner(): return lax.ppermute(x, 'dp', [(h, h ^ 1) for h in hosts])  28.6 us
    ppermute x2, waiting for transfers between devices, to_beyond(): lax.ppermute(x, 'dp', [(hosts[k ^ m], hosts[k] ^ 1) for k in range(n // 2)])  18.3 us
    ppermute x7, starting transfers between devices, from_host(): lax.ppermute(x, 'dp', [(hosts[k ^ m], hosts[k]) for k in range(n // 2)])  8.29 us
    ppermute x7, starting transfers between devices, swap_cores(): return lax.ppermute(x, 'cores', [(c, cores - 1 - c) for c in range(cores)])  5.29 us
    ppermute x4, starting transfers between devices, to_partner(): return lax.ppermute(x, 'dp', [(h, h ^ 1) for h in hosts])  5.16 us
  transfers between devices with their start and end apart: 30, of which 15 were waited for; matrix products, arithmetic and copies ran while one was open for 4% of the time, Pallas kernels for 11%

profile of v15, /device:TPU:5, one launch (start us, length us, event | category | flops | bytes accessed | tf_op | source)
XLA Modules:
  0.0 195.6 jit_solution(4557321422693700086)
XLA Ops:
  0.7 2.1 %collective-permute-start = (bf16[512,2048]{1,0:T(8,128)(2,1)}, bf16[512,2048]{1,0:T(8,128)(2,1)}, u32[]{:S(2)}, u32[]{:S(2)}) collective-permute-start(bf16[512,2048]{1,0:T(8,128)(2,1)} %bitcast.77), channel_id=1, source_target_pairs={{4,2},{2,4},{5,3},{3,5},{12,10},{10,12},{13,11},{11,13},{20,18},{1... | collective-permute-start | bytes 6291464 | tf_op jit(solution)/shard_map/ppermute | solution.py:550
  2.8 2.7 %slice_bitcast_fusion = (bf16[256,2048]{1,0:T(8,128)(2,1)S(1)}, bf16[256,2048]{1,0:T(8,128)(2,1)}) fusion(bf16[1,512,2048]{2,1,0:T(8,128)(2,1)} %param.17), kind=kLoop, calls=%fused_computation | loop fusion | bytes 4194304 | tf_op jit(solution)/shard_map/slice | solution.py:577
  5.5 5.4 %collective-permute-start.1 = (bf16[256,2048]{1,0:T(8,128)(2,1)}, bf16[256,2048]{1,0:T(8,128)(2,1)}, u32[]{:S(2)}, u32[]{:S(2)}) collective-permute-start(bf16[256,2048]{1,0:T(8,128)(2,1)} %get-tuple-element.154), channel_id=1, source_target_pairs={{0,2},{6,4},{1,3},{7,5},{8,10},{14,12},{9,11},{15,13},{16,18},{22,... | collective-permute-start | bytes 3145736 | tf_op jit(solution)/shard_map/ppermute | solution.py:544
  10.9 2.2 %collective-permute-start.2 = (bf16[256,2048]{1,0:T(8,128)(2,1)S(1)}, bf16[256,2048]{1,0:T(8,128)(2,1)}, u32[]{:S(2)}, u32[]{:S(2)}) collective-permute-start(bf16[256,2048]{1,0:T(8,128)(2,1)S(1)} %get-tuple-element.153), channel_id=1, source_target_pairs={{0,2},{6,4},{1,3},{7,5},{8,10},{14,12},{9,11},{15,13},{16,18},{22,... | collective-permute-start | bytes 3145736 | tf_op jit(solution)/shard_map/ppermute | solution.py:544
  18.1 13.7 %collective-permute-done.1.refs_8_.refs_18_.refs_11_.refs_19_ = bf16[256,2048]{1,0:T(8,128)(2,1)} collective-permute-done((bf16[256,2048]{1,0:T(8,128)(2,1)}, bf16[256,2048]{1,0:T(8,128)(2,1)}, u32[]{:S(2)}, u32[]{:S(2)}) %collective-permute-start.1) | collective-permute-done | bytes 1048608 | tf_op jit(solution)/shard_map/ppermute | solution.py:544
  31.8 1.6 collective-permute-start.7
  33.4 20.7 %collective-permute-done.2.refs_9_.refs_19_.refs_12_.refs_20_ = bf16[256,2048]{1,0:T(8,128)(2,1)} collective-permute-done((bf16[256,2048]{1,0:T(8,128)(2,1)S(1)}, bf16[256,2048]{1,0:T(8,128)(2,1)}, u32[]{:S(2)}, u32[]{:S(2)}) %collective-permute-start.2) | collective-permute-done | bytes 1048608 | tf_op jit(solution)/shard_map/ppermute | solution.py:544
  54.6 4.2 %collective-permute-start.6 = (s32[2,5,17]{2,0,1:T(2,128)S(1)}, s32[2,5,17]{2,0,1:T(2,128)S(1)}, u32[]{:S(2)}, u32[]{:S(2)}) collective-permute-start(s32[2,5,17]{2,0,1:T(2,128)S(1)} %add_add_fusion), channel_id=1, source_target_pairs={{0,2},{6,4},{1,3},{7,5},{8,10},{14,12},{9,11},{15,13},{16,18},{22,... | collective-permute-start | bytes 2048 | tf_op jit(solution)/shard_map/ppermute | solution.py:544
  58.9 2.2 %collective-permute-start.4 = (bf16[2,96,2048]{2,1,0:T(8,128)(2,1)}, bf16[2,96,2048]{2,1,0:T(8,128)(2,1)}, u32[]{:S(2)}, u32[]{:S(2)}) collective-permute-start(bf16[2,96,2048]{2,1,0:T(8,128)(2,1)} %bitcast.12.refs_3_.refs_10_.refs_11_), channel_id=1, source_target_pairs={{0,2},{6,4},{1,3},{7,5},{8,10},{14,12},{9,11},{15,13},{16,18},{22,... | collective-permute-start | bytes 2359304 | tf_op jit(solution)/shard_map/ppermute | solution.py:544
  61.0 1.7 collective-permute-start.8
  62.7 2.4 %select_bitcast_fusion = (bf16[96,2048]{1,0:T(8,128)(2,1)}, bf16[96,2048]{1,0:T(8,128)(2,1)S(1)}, bf16[96,2048]{1,0:T(8,128)(2,1)S(1)}) fusion(bf16[2,96,2048]{2,1,0:T(8,128)(2,1)} %param.14, bf16[2,96,2048]{2,1,0:T(8,128)(2,1)} %param.12, pred[]{:T(512)S(6)} %eq.44, bf16[1,96,2048]{2,1,0:T(8,128)(2,1)S(1)} %copy-done.20, bf16[1,96,2048]{2,1,0:T(8,128)(2,1)} %param.15, ...), kind=kLoop, calls=%fused_computation.6 | loop fusion | flops 589824 | bytes 3538946 | tf_op jit(solution)/shard_map/jit(_where)/select_n | solution.py:605
  65.4 4.2 %collective-permute-start.3 = (bf16[96,2048]{1,0:T(8,128)(2,1)S(1)}, bf16[96,2048]{1,0:T(8,128)(2,1)S(1)}, u32[]{:S(2)}, u32[]{:S(2)}) collective-permute-start(bf16[96,2048]{1,0:T(8,128)(2,1)S(1)} %get-tuple-element.156.refs_1_.own), channel_id=1, source_target_pairs={{0,2},{6,4},{1,3},{7,5},{8,10},{14,12},{9,11},{15,13},{16,18},{22,... | collective-permute-start | bytes 1179656 | tf_op jit(solution)/shard_map/ppermute | solution.py:544
  71.9 10.5 %collective-permute-done.4.refs_4_.refs_11_.refs_12_ = bf16[2,96,2048]{2,1,0:T(8,128)(2,1)} collective-permute-done((bf16[2,96,2048]{2,1,0:T(8,128)(2,1)}, bf16[2,96,2048]{2,1,0:T(8,128)(2,1)}, u32[]{:S(2)}, u32[]{:S(2)}) %collective-permute-start.4) | collective-permute-done | bytes 786464 | tf_op jit(solution)/shard_map/ppermute | solution.py:544
  83.1 5.5 %collective-permute-start.11 = (bf16[96,2048]{1,0:T(8,128)(2,1)S(1)}, bf16[96,2048]{1,0:T(8,128)(2,1)S(1)}, u32[]{:S(2)}, u32[]{:S(2)}) collective-permute-start(bf16[96,2048]{1,0:T(8,128)(2,1)S(1)} %get-tuple-element.94.up_own.own), channel_id=1, source_target_pairs={{0,2},{6,4},{1,3},{7,5},{8,10},{14,12},{9,11},{15,13},{16,18},{22,... | collective-permute-start | bytes 1179656 | tf_op jit(solution)/shard_map/ppermute | solution.py:544
  88.7 2.1 %collective-permute-done.3.refs_2_.theirs = bf16[96,2048]{1,0:T(8,128)(2,1)S(1)} collective-permute-done((bf16[96,2048]{1,0:T(8,128)(2,1)S(1)}, bf16[96,2048]{1,0:T(8,128)(2,1)S(1)}, u32[]{:S(2)}, u32[]{:S(2)}) %collective-permute-start.3) | collective-permute-done | bytes 393248 | tf_op jit(solution)/shard_map/ppermute | solution.py:544
  92.8 4.9 %collective-permute-start.9 = (bf16[96,2048]{1,0:T(8,128)(2,1)S(1)}, bf16[96,2048]{1,0:T(8,128)(2,1)S(1)}, u32[]{:S(2)}, u32[]{:S(2)}) collective-permute-start(bf16[96,2048]{1,0:T(8,128)(2,1)S(1)} %copy-done.17), channel_id=1, source_target_pairs={{0,2},{6,4},{1,3},{7,5},{8,10},{14,12},{9,11},{15,13},{16,18},{22,... | collective-permute-start | bytes 1179656 | tf_op jit(solution)/shard_map/ppermute | solution.py:544
  98.7 2.1 %project.1 = (bf16[3,192,512]{2,1,0:T(8,128)(2,1)S(1)}, f32[2,192,512]{2,1,0:T(8,128)}, bf16[2,192,1536]{2,1,0:T(8,128)(2,1)}, f32[2,192,2048]{2,1,0:T(8,128)}, ...) custom-call(s32[1]{0:T(128)} %bitcast.1.host, s32[6]{0:T(128)S(1)} %stack.73.refs_0_.refs_1_, ...), custom_call_target="tpu_custom_call" | custom-call | flops 4831838208 | bytes 20971520 | tf_op jit(solution)/shard_map/project/pallas_call | solution.py:686
  100.8 6.8 %collective-permute-done.9.refs_7_.new_theirs = bf16[96,2048]{1,0:T(8,128)(2,1)S(1)} collective-permute-done((bf16[96,2048]{1,0:T(8,128)(2,1)S(1)}, bf16[96,2048]{1,0:T(8,128)(2,1)S(1)}, u32[]{:S(2)}, u32[]{:S(2)}) %collective-permute-start.9) | collective-permute-done | bytes 393248 | tf_op jit(solution)/shard_map/ppermute | solution.py:544
  107.6 1.7 pack.1
  110.5 1.9 collective-permute-start.14
  118.0 1.7 backward.2
  119.7 20.7 %collective-permute-done.16.pack.rest_0_ = bf16[192,1536]{1,0:T(8,128)(2,1)S(1)} collective-permute-done((bf16[192,1536]{1,0:T(8,128)(2,1)S(1)}, bf16[192,1536]{1,0:T(8,128)(2,1)S(1)}, u32[]{:S(2)}, u32[]{:S(2)}) %collective-permute-start.16) | collective-permute-done | bytes 589856 | tf_op jit(solution)/shard_map/ppermute | solution.py:547
  141.2 1.9 collective-permute-done.19.landed
  144.4 1.5 collective-permute-start.21
  147.3 2.5 %forward.1 = (bf16[2,48,2048]{2,1,0:T(8,128)(2,1)}, bf16[2,48,2048]{2,1,0:T(8,128)(2,1)}) custom-call(s32[1]{0:T(128)} %bitcast.1.host, s32[1]{0:T(128)} %bitcast.2.core.refs_0_, s32[6]{0:T(128)S(1)} %stack.73.refs_0_.refs_1_, s32[4]{0:T(128)S(1)} %add_multiply_fusion.offs.refs_2_, s32[1]{0:T(128)} %bitcast.33.refs_3_.fresh, ...), custom_call_target="tpu_custom_call" | custom-call | flops 3221225472 | bytes 20971520 | tf_op jit(solution)/shard_map/forward/pallas_call | solution.py:789
  149.9 12.2 %collective-permute-done.21.rest_2_ = bf16[192,1536]{1,0:T(8,128)(2,1)} collective-permute-done((bf16[192,1536]{1,0:T(8,128)(2,1)}, bf16[192,1536]{1,0:T(8,128)(2,1)}, u32[]{:S(2)}, u32[]{:S(2)}) %collective-permute-start.21) | collective-permute-done | bytes 589856 | tf_op jit(solution)/shard_map/ppermute | solution.py:553
  164.8 1.8 message.1
  169.9 1.7 backward.3
  171.6 6.1 %collective-permute-done.25 = bf16[96,512]{1,0:T(8,128)(2,1)S(1)} collective-permute-done((bf16[96,512]{1,0:T(8,128)(2,1)S(1)}, bf16[96,512]{1,0:T(8,128)(2,1)S(1)}, u32[]{:S(2)}, u32[]{:S(2)}) %collective-permute-start.25) | collective-permute-done | bytes 98336 | tf_op jit(solution)/shard_map/ppermute | solution.py:553
  177.7 5.3 %collective-permute-done.26.message = bf16[96,2560]{1,0:T(8,128)(2,1)S(1)} collective-permute-done((bf16[96,2560]{1,0:T(8,128)(2,1)S(1)}, bf16[96,2560]{1,0:T(8,128)(2,1)S(1)}, u32[]{:S(2)}, u32[]{:S(2)}) %collective-permute-start.26) | collective-permute-done | bytes 491552 | tf_op jit(solution)/shard_map/ppermute | solution.py:547
  189.0 3.2 %grads.1 = f32[512,512]{1,0:T(8,128)} custom-call(s32[1]{0:T(128)} %bitcast.1.host, s32[1]{0:T(128)} %bitcast.2.core.refs_0_, s32[4]{0:T(128)S(1)} %add_multiply_fusion.offs.refs_2_, bf16[3,192,512]{2,1,0:T(8,128)(2,1)S(1)} %get-tuple-element.147.gated, bf16[192,2048]{1,0:T(8,128)(2,1)S(1)} %copy-done.5, bf16[96,2048]{1,0:T(8,128)(2,1)S(1)} %copy-done.2, ...), custom_call_target="tpu_custom_call" | custom-call | flops 402653184 | bytes 2621440 | tf_op jit(solution)/shard_map/grads/pallas_call | solution.py:875
  192.2 2.7 %collective-permute-done.28 = bf16[48,2048]{1,0:T(8,128)(2,1)S(1)} collective-permute-done((bf16[48,2048]{1,0:T(8,128)(2,1)S(1)}, bf16[48,2048]{1,0:T(8,128)(2,1)S(1)}, u32[]{:S(2)}, u32[]{:S(2)}) %collective-permute-start.28) | collective-permute-done | bytes 196640 | tf_op jit(solution)/shard_map/ppermute | solution.py:547
  (129 shorter events, 32.6 us)
Async XLA Ops:
  0.7 53.7 %copy-start.22 = (s32[1,5,4,4]{1,3,2,0:T(4,128)S(1)}, s32[1,5,4,4]{1,3,2,0:T(4,128)}, u32[]{:S(2)}) copy-start(s32[1,5,4,4]{1,3,2,0:T(4,128)} %param.22) | copy-start | bytes 964
  0.7 62.0 %copy-start.20 = (bf16[1,96,2048]{2,1,0:T(8,128)(2,1)S(1)}, bf16[1,96,2048]{2,1,0:T(8,128)(2,1)}, u32[]{:S(2)}) copy-start(bf16[1,96,2048]{2,1,0:T(8,128)(2,1)} %param.13) | copy-start | bytes 1179652
  0.7 53.4 %collective-permute-start = (bf16[512,2048]{1,0:T(8,128)(2,1)}, bf16[512,2048]{1,0:T(8,128)(2,1)}, u32[]{:S(2)}, u32[]{:S(2)}) collective-permute-start(bf16[512,2048]{1,0:T(8,128)(2,1)} %bitcast.77), channel_id=1, source_target_pairs={{4,2},{2,4},{5,3},{3,5},{12,10},{10,12},{13,11},{11,13},{20,18},{1... | collective-permute-start | bytes 6291464 | tf_op jit(solution)/shard_map/ppermute | solution.py:550
  5.5 26.2 %collective-permute-start.1 = (bf16[256,2048]{1,0:T(8,128)(2,1)}, bf16[256,2048]{1,0:T(8,128)(2,1)}, u32[]{:S(2)}, u32[]{:S(2)}) collective-permute-start(bf16[256,2048]{1,0:T(8,128)(2,1)} %get-tuple-element.154), channel_id=1, source_target_pairs={{0,2},{6,4},{1,3},{7,5},{8,10},{14,12},{9,11},{15,13},{16,18},{22,... | collective-permute-start | bytes 3145736 | tf_op jit(solution)/shard_map/ppermute | solution.py:544
  10.9 43.2 %collective-permute-start.2 = (bf16[256,2048]{1,0:T(8,128)(2,1)S(1)}, bf16[256,2048]{1,0:T(8,128)(2,1)}, u32[]{:S(2)}, u32[]{:S(2)}) collective-permute-start(bf16[256,2048]{1,0:T(8,128)(2,1)S(1)} %get-tuple-element.153), channel_id=1, source_target_pairs={{0,2},{6,4},{1,3},{7,5},{8,10},{14,12},{9,11},{15,13},{16,18},{22,... | collective-permute-start | bytes 3145736 | tf_op jit(solution)/shard_map/ppermute | solution.py:544
  13.2 52.2 %collective-permute-start.5 = (bf16[512,512]{1,0:T(8,128)(2,1)S(1)}, bf16[512,512]{1,0:T(8,128)(2,1)S(1)}, u32[]{:S(2)}, u32[]{:S(2)}) collective-permute-start(bf16[512,512]{1,0:T(8,128)(2,1)S(1)} %bitcast.70), channel_id=1, source_target_pairs={{0,2},{6,4},{1,3},{7,5},{8,10},{14,12},{9,11},{15,13},{16,18},{22,... | collective-permute-start | bytes 1572872 | tf_op jit(solution)/shard_map/ppermute | solution.py:544
  31.8 51.4 %collective-permute-start.7 = (bf16[256,2048]{1,0:T(8,128)(2,1)}, bf16[256,2048]{1,0:T(8,128)(2,1)}, u32[]{:S(2)}, u32[]{:S(2)}) collective-permute-start(bf16[256,2048]{1,0:T(8,128)(2,1)} %collective-permute-done.1.refs_8_.refs_18_.refs_11_.refs_19_), channel_id=1, source_target_pairs={{4,2},{2,4},{5,3},{3,5},{12,10},{10,12},{13,11},{11,13},{20,18},{1... | collective-permute-start | bytes 3145736 | tf_op jit(solution)/shard_map/ppermute | solution.py:550
  54.6 14.9 %collective-permute-start.6 = (s32[2,5,17]{2,0,1:T(2,128)S(1)}, s32[2,5,17]{2,0,1:T(2,128)S(1)}, u32[]{:S(2)}, u32[]{:S(2)}) collective-permute-start(s32[2,5,17]{2,0,1:T(2,128)S(1)} %add_add_fusion), channel_id=1, source_target_pairs={{0,2},{6,4},{1,3},{7,5},{8,10},{14,12},{9,11},{15,13},{16,18},{22,... | collective-permute-start | bytes 2048 | tf_op jit(solution)/shard_map/ppermute | solution.py:544
  58.9 23.6 %collective-permute-start.4 = (bf16[2,96,2048]{2,1,0:T(8,128)(2,1)}, bf16[2,96,2048]{2,1,0:T(8,128)(2,1)}, u32[]{:S(2)}, u32[]{:S(2)}) collective-permute-start(bf16[2,96,2048]{2,1,0:T(8,128)(2,1)} %bitcast.12.refs_3_.refs_10_.refs_11_), channel_id=1, source_target_pairs={{0,2},{6,4},{1,3},{7,5},{8,10},{14,12},{9,11},{15,13},{16,18},{22,... | collective-permute-start | bytes 2359304 | tf_op jit(solution)/shard_map/ppermute | solution.py:544
  61.0 31.7 %collective-permute-start.8 = (bf16[256,2048]{1,0:T(8,128)(2,1)}, bf16[256,2048]{1,0:T(8,128)(2,1)}, u32[]{:S(2)}, u32[]{:S(2)}) collective-permute-start(bf16[256,2048]{1,0:T(8,128)(2,1)} %collective-permute-done.2.refs_9_.refs_19_.refs_12_.refs_20_), channel_id=1, source_target_pairs={{4,2},{2,4},{5,3},{3,5},{12,10},{10,12},{13,11},{11,13},{20,18},{1... | collective-permute-start | bytes 3145736 | tf_op jit(solution)/shard_map/ppermute | solution.py:550
  65.4 25.4 %collective-permute-start.3 = (bf16[96,2048]{1,0:T(8,128)(2,1)S(1)}, bf16[96,2048]{1,0:T(8,128)(2,1)S(1)}, u32[]{:S(2)}, u32[]{:S(2)}) collective-permute-start(bf16[96,2048]{1,0:T(8,128)(2,1)S(1)} %get-tuple-element.156.refs_1_.own), channel_id=1, source_target_pairs={{0,2},{6,4},{1,3},{7,5},{8,10},{14,12},{9,11},{15,13},{16,18},{22,... | collective-permute-start | bytes 1179656 | tf_op jit(solution)/shard_map/ppermute | solution.py:544
  70.6 38.7 %collective-permute-start.12 = (bf16[512,512]{1,0:T(8,128)(2,1)S(1)}, bf16[512,512]{1,0:T(8,128)(2,1)S(1)}, u32[]{:S(2)}, u32[]{:S(2)}) collective-permute-start(bf16[512,512]{1,0:T(8,128)(2,1)S(1)} %bitcast.71), channel_id=1, source_target_pairs={{4,2},{2,4},{5,3},{3,5},{12,10},{10,12},{13,11},{11,13},{20,18},{1... | collective-permute-start | bytes 1572872 | tf_op jit(solution)/shard_map/ppermute | solution.py:550
  82.4 26.9 %collective-permute-start.13 = (bf16[512,512]{1,0:T(8,128)(2,1)S(1)}, bf16[512,512]{1,0:T(8,128)(2,1)S(1)}, u32[]{:S(2)}, u32[]{:S(2)}) collective-permute-start(bf16[512,512]{1,0:T(8,128)(2,1)S(1)} %collective-permute-done.5.rest_1_.refs_13_.refs_16_.refs_14_), channel_id=1, source_target_pairs={{4,2},{2,4},{5,3},{3,5},{12,10},{10,12},{13,11},{11,13},{20,18},{1... | collective-permute-start | bytes 1572872 | tf_op jit(solution)/shard_map/ppermute | solution.py:550
  83.1 24.5 %collective-permute-start.11 = (bf16[96,2048]{1,0:T(8,128)(2,1)S(1)}, bf16[96,2048]{1,0:T(8,128)(2,1)S(1)}, u32[]{:S(2)}, u32[]{:S(2)}) collective-permute-start(bf16[96,2048]{1,0:T(8,128)(2,1)S(1)} %get-tuple-element.94.up_own.own), channel_id=1, source_target_pairs={{0,2},{6,4},{1,3},{7,5},{8,10},{14,12},{9,11},{15,13},{16,18},{22,... | collective-permute-start | bytes 1179656 | tf_op jit(solution)/shard_map/ppermute | solution.py:544
  91.5 9.3 %collective-permute-start.10 = (bf16[96,512]{1,0:T(8,128)(2,1)S(1)}, bf16[96,512]{1,0:T(8,128)(2,1)S(1)}, u32[]{:S(2)}, u32[]{:S(2)}) collective-permute-start(bf16[96,512]{1,0:T(8,128)(2,1)S(1)} %constant_dynamic-slice_fusion), channel_id=1, source_target_pairs={{2,0},{4,6},{3,1},{5,7},{10,8},{12,14},{11,9},{13,15},{18,16},{20,... | collective-permute-start | bytes 294920 | tf_op jit(solution)/shard_map/ppermute | solution.py:547
  92.8 14.8 %collective-permute-start.9 = (bf16[96,2048]{1,0:T(8,128)(2,1)S(1)}, bf16[96,2048]{1,0:T(8,128)(2,1)S(1)}, u32[]{:S(2)}, u32[]{:S(2)}) collective-permute-start(bf16[96,2048]{1,0:T(8,128)(2,1)S(1)} %copy-done.17), channel_id=1, source_target_pairs={{0,2},{6,4},{1,3},{7,5},{8,10},{14,12},{9,11},{15,13},{16,18},{22,... | collective-permute-start | bytes 1179656 | tf_op jit(solution)/shard_map/ppermute | solution.py:544
  110.5 3.3 %collective-permute-start.14 = (bf16[2,48,2048]{2,1,0:T(8,128)(2,1)S(1)}, bf16[2,48,2048]{2,1,0:T(8,128)(2,1)S(1)}, u32[]{:S(2)}, u32[]{:S(2)}) collective-permute-start(bf16[2,48,2048]{2,1,0:T(8,128)(2,1)S(1)} %get-tuple-element.105), channel_id=1, source_target_pairs={{0,1},{1,0},{2,3},{3,2},{4,5},{5,4},{6,7},{7,6},{8,9},{9,8},{10,11... | collective-permute-start | bytes 1179656 | tf_op jit(solution)/shard_map/ppermute | solution.py:558
  112.5 7.2 %collective-permute-start.17 = (bf16[192,1536]{1,0:T(8,128)(2,1)S(1)}, bf16[192,1536]{1,0:T(8,128)(2,1)S(1)}, u32[]{:S(2)}, u32[]{:S(2)}) collective-permute-start(bf16[192,1536]{1,0:T(8,128)(2,1)S(1)} %get-tuple-element.119), channel_id=1, source_target_pairs={{4,2},{2,4},{5,3},{3,5},{12,10},{10,12},{13,11},{11,13},{20,18},{1... | collective-permute-start | bytes 1769480 | tf_op jit(solution)/shard_map/ppermute | solution.py:550
  115.2 25.1 %collective-permute-start.16 = (bf16[192,1536]{1,0:T(8,128)(2,1)S(1)}, bf16[192,1536]{1,0:T(8,128)(2,1)S(1)}, u32[]{:S(2)}, u32[]{:S(2)}) collective-permute-start(bf16[192,1536]{1,0:T(8,128)(2,1)S(1)} %get-tuple-element.118), channel_id=1, source_target_pairs={{2,0},{4,6},{3,1},{5,7},{10,8},{12,14},{11,9},{13,15},{18,16},{20,... | collective-permute-start | bytes 1769480 | tf_op jit(solution)/shard_map/ppermute | solution.py:547
  116.5 3.1 %collective-permute-start.15 = (bf16[2,48,2048]{2,1,0:T(8,128)(2,1)S(1)}, bf16[2,48,2048]{2,1,0:T(8,128)(2,1)}, u32[]{:S(2)}, u32[]{:S(2)}) collective-permute-start(bf16[2,48,2048]{2,1,0:T(8,128)(2,1)S(1)} %get-tuple-element.106.ahead_0), channel_id=1, source_target_pairs={{2,10},{4,12},{10,18},{12,20},{18,26},{20,28},{3,11},{5,13},{11,19... | collective-permute-start | bytes 1179656 | tf_op jit(solution)/shard_map/ppermute | solution.py:567
  140.3 2.7 %collective-permute-start.19 = (bf16[2,48,2048]{2,1,0:T(8,128)(2,1)S(1)}, bf16[2,48,2048]{2,1,0:T(8,128)(2,1)S(1)}, u32[]{:S(2)}, u32[]{:S(2)}) collective-permute-start(bf16[2,48,2048]{2,1,0:T(8,128)(2,1)S(1)} %get-tuple-element.124), channel_id=1, source_target_pairs={{0,1},{1,0},{2,3},{3,2},{4,5},{5,4},{6,7},{7,6},{8,9},{9,8},{10,11... | collective-permute-start | bytes 1179656 | tf_op jit(solution)/shard_map/ppermute | solution.py:558
  141.1 6.2 %collective-permute-start.18 = (bf16[2,48,2048]{2,1,0:T(8,128)(2,1)}, bf16[2,48,2048]{2,1,0:T(8,128)(2,1)S(1)}, u32[]{:S(2)}, u32[]{:S(2)}) collective-permute-start(bf16[2,48,2048]{2,1,0:T(8,128)(2,1)} %collective-permute-done.15.refs_4_.passed), channel_id=1, source_target_pairs={{0,1},{1,0},{2,3},{3,2},{4,5},{5,4},{6,7},{7,6},{8,9},{9,8},{10,11... | collective-permute-start | bytes 1179656 | tf_op jit(solution)/shard_map/ppermute | solution.py:558
  144.4 17.7 %collective-permute-start.21 = (bf16[192,1536]{1,0:T(8,128)(2,1)}, bf16[192,1536]{1,0:T(8,128)(2,1)}, u32[]{:S(2)}, u32[]{:S(2)}) collective-permute-start(bf16[192,1536]{1,0:T(8,128)(2,1)} %get-tuple-element.126), channel_id=1, source_target_pairs={{4,0},{2,6},{5,1},{3,7},{12,8},{10,14},{13,9},{11,15},{20,16},{18,... | collective-permute-start | bytes 1769480 | tf_op jit(solution)/shard_map/ppermute | solution.py:553
  145.9 4.0 %collective-permute-start.20 = (bf16[2,48,2048]{2,1,0:T(8,128)(2,1)S(1)}, bf16[2,48,2048]{2,1,0:T(8,128)(2,1)}, u32[]{:S(2)}, u32[]{:S(2)}) collective-permute-start(bf16[2,48,2048]{2,1,0:T(8,128)(2,1)S(1)} %settle.1.back.back_0), channel_id=1, source_target_pairs={{10,2},{12,4},{18,10},{20,12},{26,18},{28,20},{11,3},{13,5},{19,11... | collective-permute-start | bytes 1179656 | tf_op jit(solution)/shard_map/ppermute | solution.py:567
  162.1 2.8 %collective-permute-start.22 = (bf16[2,48,2048]{2,1,0:T(8,128)(2,1)}, bf16[2,48,2048]{2,1,0:T(8,128)(2,1)S(1)}, u32[]{:S(2)}, u32[]{:S(2)}) collective-permute-start(bf16[2,48,2048]{2,1,0:T(8,128)(2,1)} %get-tuple-element.128), channel_id=1, source_target_pairs={{0,1},{1,0},{2,3},{3,2},{4,5},{5,4},{6,7},{7,6},{8,9},{9,8},{10,11... | collective-permute-start | bytes 1179656 | tf_op jit(solution)/shard_map/ppermute | solution.py:558
  164.6 5.3 %collective-permute-start.23 = (bf16[2,48,2048]{2,1,0:T(8,128)(2,1)S(1)}, bf16[2,48,2048]{2,1,0:T(8,128)(2,1)S(1)}, u32[]{:S(2)}, u32[]{:S(2)}) collective-permute-start(bf16[2,48,2048]{2,1,0:T(8,128)(2,1)S(1)} %get-tuple-element.130.up.refs_3_.mine), channel_id=1, source_target_pairs={{0,1},{1,0},{2,3},{3,2},{4,5},{5,4},{6,7},{7,6},{8,9},{9,8},{10,11... | collective-permute-start | bytes 1179656 | tf_op jit(solution)/shard_map/ppermute | solution.py:558
  166.6 16.4 %collective-permute-start.26 = (bf16[96,2560]{1,0:T(8,128)(2,1)S(1)}, bf16[96,2560]{1,0:T(8,128)(2,1)S(1)}, u32[]{:S(2)}, u32[]{:S(2)}) collective-permute-start(bf16[96,2560]{1,0:T(8,128)(2,1)S(1)} %get-tuple-element.137), channel_id=1, source_target_pairs={{2,0},{4,6},{3,1},{5,7},{10,8},{12,14},{11,9},{13,15},{18,16},{20,... | collective-permute-start | bytes 1474568 | tf_op jit(solution)/shard_map/ppermute | solution.py:547
  167.9 3.7 %collective-permute-start.24 = (bf16[96,512]{1,0:T(8,128)(2,1)S(1)}, bf16[96,512]{1,0:T(8,128)(2,1)S(1)}, u32[]{:S(2)}, u32[]{:S(2)}) collective-permute-start(bf16[96,512]{1,0:T(8,128)(2,1)S(1)} %get-tuple-element.135), channel_id=1, source_target_pairs={{4,2},{2,4},{5,3},{3,5},{12,10},{10,12},{13,11},{11,13},{20,18},{1... | collective-permute-start | bytes 294920 | tf_op jit(solution)/shard_map/ppermute | solution.py:550
  168.6 9.2 %collective-permute-start.25 = (bf16[96,512]{1,0:T(8,128)(2,1)S(1)}, bf16[96,512]{1,0:T(8,128)(2,1)S(1)}, u32[]{:S(2)}, u32[]{:S(2)}) collective-permute-start(bf16[96,512]{1,0:T(8,128)(2,1)S(1)} %get-tuple-element.136), channel_id=1, source_target_pairs={{4,0},{2,6},{5,1},{3,7},{12,8},{10,14},{13,9},{11,15},{20,16},{18,... | collective-permute-start | bytes 294920 | tf_op jit(solution)/shard_map/ppermute | solution.py:553
  183.0 2.6 %collective-permute-start.27 = (bf16[2,48,2048]{2,1,0:T(8,128)(2,1)S(1)}, bf16[2,48,2048]{2,1,0:T(8,128)(2,1)S(1)}, u32[]{:S(2)}, u32[]{:S(2)}) collective-permute-start(bf16[2,48,2048]{2,1,0:T(8,128)(2,1)S(1)} %get-tuple-element.140), channel_id=1, source_target_pairs={{0,1},{1,0},{2,3},{3,2},{4,5},{5,4},{6,7},{7,6},{8,9},{9,8},{10,11... | collective-permute-start | bytes 1179656 | tf_op jit(solution)/shard_map/ppermute | solution.py:558
  184.3 4.7 %collective-permute-start.29 = (bf16[2,96,512]{2,1,0:T(8,128)(2,1)S(1)}, bf16[2,96,512]{2,1,0:T(8,128)(2,1)S(1)}, u32[]{:S(2)}, u32[]{:S(2)}) collective-permute-start(bf16[2,96,512]{2,1,0:T(8,128)(2,1)S(1)} %pad_maximum_fusion.halves), channel_id=1, source_target_pairs={{0,1},{1,0},{2,3},{3,2},{4,5},{5,4},{6,7},{7,6},{8,9},{9,8},{10,11... | collective-permute-start | bytes 589832 | tf_op jit(solution)/shard_map/ppermute | solution.py:558
  186.8 8.0 %collective-permute-start.28 = (bf16[48,2048]{1,0:T(8,128)(2,1)S(1)}, bf16[48,2048]{1,0:T(8,128)(2,1)S(1)}, u32[]{:S(2)}, u32[]{:S(2)}) collective-permute-start(bf16[48,2048]{1,0:T(8,128)(2,1)S(1)} %get-tuple-element.146), channel_id=1, source_target_pairs={{2,0},{4,6},{3,1},{5,7},{10,8},{12,14},{11,9},{13,15},{18,16},{20,... | collective-permute-start | bytes 589832 | tf_op jit(solution)/shard_map/ppermute | solution.py:547
  (24 other events, 455.3 us)

commit v16 on v14

--- a/solution.py
+++ b/solution.py
@@ -221,7 +221,7 @@
     up_sources, rest = rest[: 1 + split], rest[1 + split :]
     sources, rest = (None,) + rest[:count], rest[count:]
     send, keep = rest[:2]
-    held, (grad_normed, part, up_sems, sems) = rest[2 : 3 + count], rest[3 + count :]
+    held, (grad_normed, part, up_sem, sems) = rest[2 : 3 + count], rest[3 + count :]
     ups, gate, vqk, slope, mixed, probs, factor, x_own, x_theirs = held[:9]
     out_parts, in_parts = held[9 : 9 + n], held[9 + n :]
     wide = 4 * HEAD_DIM
@@ -234,21 +234,8 @@
             source = source.at[tick]
         copies.append(pltpu.make_async_copy(source, target, sems.at[i]))
     up_copies = []
-    if split:
-        share = up_sources[0].shape[1]
-        cores = ups.shape[0] // (2 * share)
-        for half, owner in enumerate((core[0], cores - 1 - core[0])):
-            for r in range(2):
-                at = pl.multiple_of((r * cores + owner) * share, share)
-                up_copies.append(
-                    pltpu.make_async_copy(
-                        up_sources[half].at[r],
-                        ups.at[pl.ds(at, share), :],
-                        up_sems.at[2 * half + r],
-                    )
-                )
-    else:
-        up_copies.append(pltpu.make_async_copy(up_sources[0], ups, up_sems.at[0]))
+    if not split:
+        up_copies.append(pltpu.make_async_copy(up_sources[0], ups, up_sem))
     copies = [None] + copies
     by_head = []
     for h in range(heads):
@@ -274,6 +261,13 @@
             copy.start()
     for i in (7, 8):
         copies[i].start()
+    if split:
+        share = up_sources[0].shape[1]
+        cores = ups.shape[0] // (2 * share)
+        for half, owner in enumerate((core[0], cores - 1 - core[0])):
+            for r in range(2):
+                at = pl.multiple_of((r * cores + owner) * share, share)
+                ups[pl.ds(at, share), :] = up_sources[half][r]
     for copy in up_copies:
         copy.wait()
     depth = out_parts[0].shape[1]
@@ -649,6 +643,7 @@
 
     smem = pl.BlockSpec(memory_space=pltpu.SMEM)
     hbm = pl.BlockSpec(memory_space=pltpu.HBM)
+    vmem = pl.BlockSpec(memory_space=pltpu.VMEM)
 
     def all_of(*arrays):
         return [pl.BlockSpec(x.shape, lambda *_, d=x.ndim: (0,) * d) for x in arrays]
@@ -710,7 +705,9 @@
         return pl.pallas_call(
             on_host(functools.partial(backward_kernel, parts, n, tick_no, split)),
             grid=(1,),
-            in_specs=[smem] * 4 + [hbm] * (len(ups) + len(layered) + len(plain)),
+            in_specs=[smem] * 4
+            + [vmem if split else hbm] * len(ups)
+            + [hbm] * (len(layered) + len(plain)),
             out_specs=all_of(*halves),
             out_shape=kept_halves,
             scratch_shapes=[pltpu.VMEM((rows, width), BF16)]
@@ -719,11 +716,11 @@
             + [
                 pltpu.VMEM((rows, width), F32),
                 pltpu.VMEM((rows, width), BF16),
-                pltpu.SemaphoreType.DMA((4,)),
+                pltpu.SemaphoreType.DMA,
                 pltpu.SemaphoreType.DMA((1 + len(layered) + n + heads * parts,)),
             ],
             compiler_params=params,
-            cost_estimate=cost(2 * matmul, 2 * weight_bytes),
+            cost_estimate=cost((16 if split else 2) * matmul, 2 * weight_bytes),
             name="backward",
         )(host_flag, core, in_offs, offs, *ups, *in_hbm(layered), *out_parts, *in_hbm(in_parts))
 
@@ -845,9 +842,10 @@
         compiler_params=small,
         name="message",
     )(core, offs, first_flag, *in_hbm(message_inputs[:4]), *message_inputs[4:6], *in_hbm([back_0]))
-    landed = [to_partner(message)] + landed
+    landed = landed + [to_partner(message)]
     back_send, back_keep = backward([up_mine, up_their], 1)
     back_send, back_keep, landed = lax.optimization_barrier((back_send, back_keep, landed))
+    landed = landed[-1:] + landed[:-1]
     last_inputs = [up_mine, *in_hbm([back_keep]), swap_cores(back_send)]
     last_shapes = [halves[0], struct((share, width), BF16)]
     back_1, back_other = pl.pallas_call(

time: 196 us -> 196 us (level)
    ppermute x4, waiting for transfers between devices: 28.6 us -> 33.8 us  [to_partner(): return lax.ppermute(x, 'dp', [(h, h ^ 1) for h in hosts])]
    ppermute x2, waiting for transfers between devices: 16.3 us -> 11.7 us  [to_beyond(): lax.ppermute(x, 'dp', [(hosts[k ^ m], hosts[k] ^ 1) for k in range(n // 2)])]
  transfers between devices with their start and end apart: 30 -> 30, of which waited for: 15 -> 14; matrix products, arithmetic and copies ran while one was open for 4% -> 4% of each run, Pallas kernels for 11% -> 11%
where the time goes in v16:
time: 196 us; the launch traced here: 193 us
  waiting for transfers between devices  102 us (52%)
  starting transfers between devices  54.6 us (28%)
  Pallas kernels  21.7 us (11%)
  local copies, waits for them, and re-layouts  7.16 us (4%)
  other arithmetic  4.88 us (2%)
  between operations  3.27 us (2%)
    ppermute x8, waiting for transfers between devices, from_partner(): return lax.ppermute(x, 'dp', [(h ^ 1, h) for h in hosts])  54 us
    ppermute x4, waiting for transfers between devices, to_partner(): return lax.ppermute(x, 'dp', [(h, h ^ 1) for h in hosts])  33.8 us
    ppermute x8, starting transfers between devices, from_partner(): return lax.ppermute(x, 'dp', [(h ^ 1, h) for h in hosts])  30 us
    ppermute x2, waiting for transfers between devices, to_beyond(): lax.ppermute(x, 'dp', [(hosts[k ^ m], hosts[k] ^ 1) for k in range(n // 2)])  11.7 us
    ppermute x7, starting transfers between devices, from_host(): lax.ppermute(x, 'dp', [(hosts[k ^ m], hosts[k]) for k in range(n // 2)])  8.29 us
    ppermute x7, starting transfers between devices, swap_cores(): return lax.ppermute(x, 'cores', [(c, cores - 1 - c) for c in range(cores)])  5.58 us
    ppermute x4, starting transfers between devices, to_partner(): return lax.ppermute(x, 'dp', [(h, h ^ 1) for h in hosts])  5.16 us
  transfers between devices with their start and end apart: 30, of which 14 were waited for; matrix products, arithmetic and copies ran while one was open for 4% of the time, Pallas kernels for 11%

profile of v16, /device:TPU:5, one launch (start us, length us, event | category | flops | bytes accessed | tf_op | source)
XLA Modules:
  0.0 193.5 jit_solution(13327662863463011092)
XLA Ops:
  0.7 2.1 %collective-permute-start = (bf16[512,2048]{1,0:T(8,128)(2,1)}, bf16[512,2048]{1,0:T(8,128)(2,1)}, u32[]{:S(2)}, u32[]{:S(2)}) collective-permute-start(bf16[512,2048]{1,0:T(8,128)(2,1)} %bitcast.77), channel_id=1, source_target_pairs={{4,2},{2,4},{5,3},{3,5},{12,10},{10,12},{13,11},{11,13},{20,18},{1... | collective-permute-start | bytes 6291464 | tf_op jit(solution)/shard_map/ppermute | solution.py:543
  2.8 2.7 %slice_bitcast_fusion = (bf16[256,2048]{1,0:T(8,128)(2,1)S(1)}, bf16[256,2048]{1,0:T(8,128)(2,1)}) fusion(bf16[1,512,2048]{2,1,0:T(8,128)(2,1)} %param.17), kind=kLoop, calls=%fused_computation | loop fusion | bytes 4194304 | tf_op jit(solution)/shard_map/slice | solution.py:570
  5.5 5.4 %collective-permute-start.1 = (bf16[256,2048]{1,0:T(8,128)(2,1)}, bf16[256,2048]{1,0:T(8,128)(2,1)}, u32[]{:S(2)}, u32[]{:S(2)}) collective-permute-start(bf16[256,2048]{1,0:T(8,128)(2,1)} %get-tuple-element.152), channel_id=1, source_target_pairs={{0,2},{6,4},{1,3},{7,5},{8,10},{14,12},{9,11},{15,13},{16,18},{22,... | collective-permute-start | bytes 3145736 | tf_op jit(solution)/shard_map/ppermute | solution.py:537
  10.9 2.2 %collective-permute-start.2 = (bf16[256,2048]{1,0:T(8,128)(2,1)S(1)}, bf16[256,2048]{1,0:T(8,128)(2,1)}, u32[]{:S(2)}, u32[]{:S(2)}) collective-permute-start(bf16[256,2048]{1,0:T(8,128)(2,1)S(1)} %get-tuple-element.151), channel_id=1, source_target_pairs={{0,2},{6,4},{1,3},{7,5},{8,10},{14,12},{9,11},{15,13},{16,18},{22,... | collective-permute-start | bytes 3145736 | tf_op jit(solution)/shard_map/ppermute | solution.py:537
  18.1 13.7 %collective-permute-done.1.refs_8_.refs_18_.refs_11_.refs_19_ = bf16[256,2048]{1,0:T(8,128)(2,1)} collective-permute-done((bf16[256,2048]{1,0:T(8,128)(2,1)}, bf16[256,2048]{1,0:T(8,128)(2,1)}, u32[]{:S(2)}, u32[]{:S(2)}) %collective-permute-start.1) | collective-permute-done | bytes 1048608 | tf_op jit(solution)/shard_map/ppermute | solution.py:537
  31.8 1.6 collective-permute-start.7
  33.4 20.7 %collective-permute-done.2.refs_9_.refs_19_.refs_12_.refs_20_ = bf16[256,2048]{1,0:T(8,128)(2,1)} collective-permute-done((bf16[256,2048]{1,0:T(8,128)(2,1)S(1)}, bf16[256,2048]{1,0:T(8,128)(2,1)}, u32[]{:S(2)}, u32[]{:S(2)}) %collective-permute-start.2) | collective-permute-done | bytes 1048608 | tf_op jit(solution)/shard_map/ppermute | solution.py:537
  54.6 4.2 %collective-permute-start.6 = (s32[2,5,17]{2,0,1:T(2,128)S(1)}, s32[2,5,17]{2,0,1:T(2,128)S(1)}, u32[]{:S(2)}, u32[]{:S(2)}) collective-permute-start(s32[2,5,17]{2,0,1:T(2,128)S(1)} %add_add_fusion), channel_id=1, source_target_pairs={{0,2},{6,4},{1,3},{7,5},{8,10},{14,12},{9,11},{15,13},{16,18},{22,... | collective-permute-start | bytes 2048 | tf_op jit(solution)/shard_map/ppermute | solution.py:537
  58.9 2.2 %collective-permute-start.4 = (bf16[2,96,2048]{2,1,0:T(8,128)(2,1)}, bf16[2,96,2048]{2,1,0:T(8,128)(2,1)}, u32[]{:S(2)}, u32[]{:S(2)}) collective-permute-start(bf16[2,96,2048]{2,1,0:T(8,128)(2,1)} %bitcast.12.refs_3_.refs_10_.refs_11_), channel_id=1, source_target_pairs={{0,2},{6,4},{1,3},{7,5},{8,10},{14,12},{9,11},{15,13},{16,18},{22,... | collective-permute-start | bytes 2359304 | tf_op jit(solution)/shard_map/ppermute | solution.py:537
  61.0 1.7 collective-permute-start.8
  62.7 2.4 %select_bitcast_fusion = (bf16[96,2048]{1,0:T(8,128)(2,1)}, bf16[96,2048]{1,0:T(8,128)(2,1)S(1)}, bf16[96,2048]{1,0:T(8,128)(2,1)S(1)}) fusion(bf16[2,96,2048]{2,1,0:T(8,128)(2,1)} %param.14, bf16[2,96,2048]{2,1,0:T(8,128)(2,1)} %param.12, pred[]{:T(512)S(6)} %eq.44, bf16[1,96,2048]{2,1,0:T(8,128)(2,1)S(1)} %copy-done.20, bf16[1,96,2048]{2,1,0:T(8,128)(2,1)} %param.15, ...), kind=kLoop, calls=%fused_computation.6 | loop fusion | flops 589824 | bytes 3538946 | tf_op jit(solution)/shard_map/jit(_where)/select_n | solution.py:598
  65.4 4.2 %collective-permute-start.3 = (bf16[96,2048]{1,0:T(8,128)(2,1)S(1)}, bf16[96,2048]{1,0:T(8,128)(2,1)S(1)}, u32[]{:S(2)}, u32[]{:S(2)}) collective-permute-start(bf16[96,2048]{1,0:T(8,128)(2,1)S(1)} %get-tuple-element.154.refs_1_.own), channel_id=1, source_target_pairs={{0,2},{6,4},{1,3},{7,5},{8,10},{14,12},{9,11},{15,13},{16,18},{22,... | collective-permute-start | bytes 1179656 | tf_op jit(solution)/shard_map/ppermute | solution.py:537
  71.9 10.5 %collective-permute-done.4.refs_4_.refs_11_.refs_12_ = bf16[2,96,2048]{2,1,0:T(8,128)(2,1)} collective-permute-done((bf16[2,96,2048]{2,1,0:T(8,128)(2,1)}, bf16[2,96,2048]{2,1,0:T(8,128)(2,1)}, u32[]{:S(2)}, u32[]{:S(2)}) %collective-permute-start.4) | collective-permute-done | bytes 786464 | tf_op jit(solution)/shard_map/ppermute | solution.py:537
  83.1 5.5 %collective-permute-start.11 = (bf16[96,2048]{1,0:T(8,128)(2,1)S(1)}, bf16[96,2048]{1,0:T(8,128)(2,1)S(1)}, u32[]{:S(2)}, u32[]{:S(2)}) collective-permute-start(bf16[96,2048]{1,0:T(8,128)(2,1)S(1)} %get-tuple-element.93.up_own.own), channel_id=1, source_target_pairs={{0,2},{6,4},{1,3},{7,5},{8,10},{14,12},{9,11},{15,13},{16,18},{22,... | collective-permute-start | bytes 1179656 | tf_op jit(solution)/shard_map/ppermute | solution.py:537
  88.7 2.1 %collective-permute-done.3.refs_2_.theirs = bf16[96,2048]{1,0:T(8,128)(2,1)S(1)} collective-permute-done((bf16[96,2048]{1,0:T(8,128)(2,1)S(1)}, bf16[96,2048]{1,0:T(8,128)(2,1)S(1)}, u32[]{:S(2)}, u32[]{:S(2)}) %collective-permute-start.3) | collective-permute-done | bytes 393248 | tf_op jit(solution)/shard_map/ppermute | solution.py:537
  92.8 4.9 %collective-permute-start.9 = (bf16[96,2048]{1,0:T(8,128)(2,1)S(1)}, bf16[96,2048]{1,0:T(8,128)(2,1)S(1)}, u32[]{:S(2)}, u32[]{:S(2)}) collective-permute-start(bf16[96,2048]{1,0:T(8,128)(2,1)S(1)} %copy-done.17), channel_id=1, source_target_pairs={{0,2},{6,4},{1,3},{7,5},{8,10},{14,12},{9,11},{15,13},{16,18},{22,... | collective-permute-start | bytes 1179656 | tf_op jit(solution)/shard_map/ppermute | solution.py:537
  98.7 2.1 %project.1 = (bf16[3,192,512]{2,1,0:T(8,128)(2,1)S(1)}, f32[2,192,512]{2,1,0:T(8,128)}, bf16[2,192,1536]{2,1,0:T(8,128)(2,1)}, f32[2,192,2048]{2,1,0:T(8,128)}, ...) custom-call(s32[1]{0:T(128)} %bitcast.1.host, s32[6]{0:T(128)S(1)} %stack.73.refs_0_.refs_1_, ...), custom_call_target="tpu_custom_call" | custom-call | flops 4831838208 | bytes 20971520 | tf_op jit(solution)/shard_map/project/pallas_call | solution.py:680
  100.8 6.8 %collective-permute-done.9.refs_7_.new_theirs = bf16[96,2048]{1,0:T(8,128)(2,1)S(1)} collective-permute-done((bf16[96,2048]{1,0:T(8,128)(2,1)S(1)}, bf16[96,2048]{1,0:T(8,128)(2,1)S(1)}, u32[]{:S(2)}, u32[]{:S(2)}) %collective-permute-start.9) | collective-permute-done | bytes 393248 | tf_op jit(solution)/shard_map/ppermute | solution.py:537
  107.6 1.7 pack.1
  110.5 1.9 collective-permute-start.14
  116.5 1.4 collective-permute-start.15
  118.0 1.6 backward.2
  119.6 20.7 %collective-permute-done.16.pack.rest_0_ = bf16[192,1536]{1,0:T(8,128)(2,1)S(1)} collective-permute-done((bf16[192,1536]{1,0:T(8,128)(2,1)S(1)}, bf16[192,1536]{1,0:T(8,128)(2,1)S(1)}, u32[]{:S(2)}, u32[]{:S(2)}) %collective-permute-start.16) | collective-permute-done | bytes 589856 | tf_op jit(solution)/shard_map/ppermute | solution.py:540
  142.0 1.5 collective-permute-start.21
  145.2 1.5 collective-permute-start.20
  146.7 2.4 %forward.1 = (bf16[2,48,2048]{2,1,0:T(8,128)(2,1)S(1)}, bf16[2,48,2048]{2,1,0:T(8,128)(2,1)}) custom-call(s32[1]{0:T(128)} %bitcast.1.host, s32[1]{0:T(128)} %bitcast.2.core.refs_0_, s32[6]{0:T(128)S(1)} %stack.73.refs_0_.refs_1_, s32[4]{0:T(128)S(1)} %add_multiply_fusion.offs.refs_2_, s32[1]{0:T(128)} %bitcast.33.refs_3_.fresh, ...), custom_call_target="tpu_custom_call" | custom-call | flops 3221225472 | bytes 20971520 | tf_op jit(solution)/shard_map/forward/pallas_call | solution.py:785
  149.1 10.3 %collective-permute-done.21.rest_2_ = bf16[192,1536]{1,0:T(8,128)(2,1)} collective-permute-done((bf16[192,1536]{1,0:T(8,128)(2,1)}, bf16[192,1536]{1,0:T(8,128)(2,1)}, u32[]{:S(2)}, u32[]{:S(2)}) %collective-permute-start.21) | collective-permute-done | bytes 589856 | tf_op jit(solution)/shard_map/ppermute | solution.py:546
  164.2 1.8 message.1
  167.2 1.7 backward.3
  170.3 10.4 %collective-permute-done.26.message = bf16[96,2560]{1,0:T(8,128)(2,1)S(1)} collective-permute-done((bf16[96,2560]{1,0:T(8,128)(2,1)S(1)}, bf16[96,2560]{1,0:T(8,128)(2,1)S(1)}, u32[]{:S(2)}, u32[]{:S(2)}) %collective-permute-start.26) | collective-permute-done | bytes 491552 | tf_op jit(solution)/shard_map/ppermute | solution.py:540
  186.8 3.2 %grads.1 = f32[512,512]{1,0:T(8,128)} custom-call(s32[1]{0:T(128)} %bitcast.1.host, s32[1]{0:T(128)} %bitcast.2.core.refs_0_, s32[4]{0:T(128)S(1)} %add_multiply_fusion.offs.refs_2_, bf16[3,192,512]{2,1,0:T(8,128)(2,1)S(1)} %get-tuple-element.145.gated, bf16[192,2048]{1,0:T(8,128)(2,1)S(1)} %copy-done.5, bf16[96,2048]{1,0:T(8,128)(2,1)S(1)} %copy-done.1, ...), custom_call_target="tpu_custom_call" | custom-call | flops 402653184 | bytes 2621440 | tf_op jit(solution)/shard_map/grads/pallas_call | solution.py:871
  190.0 2.7 %collective-permute-done.28 = bf16[48,2048]{1,0:T(8,128)(2,1)S(1)} collective-permute-done((bf16[48,2048]{1,0:T(8,128)(2,1)S(1)}, bf16[48,2048]{1,0:T(8,128)(2,1)S(1)}, u32[]{:S(2)}, u32[]{:S(2)}) %collective-permute-start.28) | collective-permute-done | bytes 196640 | tf_op jit(solution)/shard_map/ppermute | solution.py:540
  (129 shorter events, 32.5 us)
Async XLA Ops:
  0.7 53.7 %copy-start.22 = (s32[1,5,4,4]{1,3,2,0:T(4,128)S(1)}, s32[1,5,4,4]{1,3,2,0:T(4,128)}, u32[]{:S(2)}) copy-start(s32[1,5,4,4]{1,3,2,0:T(4,128)} %param.22) | copy-start | bytes 964
  0.7 62.0 %copy-start.20 = (bf16[1,96,2048]{2,1,0:T(8,128)(2,1)S(1)}, bf16[1,96,2048]{2,1,0:T(8,128)(2,1)}, u32[]{:S(2)}) copy-start(bf16[1,96,2048]{2,1,0:T(8,128)(2,1)} %param.13) | copy-start | bytes 1179652
  0.7 53.4 %collective-permute-start = (bf16[512,2048]{1,0:T(8,128)(2,1)}, bf16[512,2048]{1,0:T(8,128)(2,1)}, u32[]{:S(2)}, u32[]{:S(2)}) collective-permute-start(bf16[512,2048]{1,0:T(8,128)(2,1)} %bitcast.77), channel_id=1, source_target_pairs={{4,2},{2,4},{5,3},{3,5},{12,10},{10,12},{13,11},{11,13},{20,18},{1... | collective-permute-start | bytes 6291464 | tf_op jit(solution)/shard_map/ppermute | solution.py:543
  5.5 26.2 %collective-permute-start.1 = (bf16[256,2048]{1,0:T(8,128)(2,1)}, bf16[256,2048]{1,0:T(8,128)(2,1)}, u32[]{:S(2)}, u32[]{:S(2)}) collective-permute-start(bf16[256,2048]{1,0:T(8,128)(2,1)} %get-tuple-element.152), channel_id=1, source_target_pairs={{0,2},{6,4},{1,3},{7,5},{8,10},{14,12},{9,11},{15,13},{16,18},{22,... | collective-permute-start | bytes 3145736 | tf_op jit(solution)/shard_map/ppermute | solution.py:537
  10.9 43.2 %collective-permute-start.2 = (bf16[256,2048]{1,0:T(8,128)(2,1)S(1)}, bf16[256,2048]{1,0:T(8,128)(2,1)}, u32[]{:S(2)}, u32[]{:S(2)}) collective-permute-start(bf16[256,2048]{1,0:T(8,128)(2,1)S(1)} %get-tuple-element.151), channel_id=1, source_target_pairs={{0,2},{6,4},{1,3},{7,5},{8,10},{14,12},{9,11},{15,13},{16,18},{22,... | collective-permute-start | bytes 3145736 | tf_op jit(solution)/shard_map/ppermute | solution.py:537
  13.2 52.2 %collective-permute-start.5 = (bf16[512,512]{1,0:T(8,128)(2,1)S(1)}, bf16[512,512]{1,0:T(8,128)(2,1)S(1)}, u32[]{:S(2)}, u32[]{:S(2)}) collective-permute-start(bf16[512,512]{1,0:T(8,128)(2,1)S(1)} %bitcast.70), channel_id=1, source_target_pairs={{0,2},{6,4},{1,3},{7,5},{8,10},{14,12},{9,11},{15,13},{16,18},{22,... | collective-permute-start | bytes 1572872 | tf_op jit(solution)/shard_map/ppermute | solution.py:537
  31.8 51.4 %collective-permute-start.7 = (bf16[256,2048]{1,0:T(8,128)(2,1)}, bf16[256,2048]{1,0:T(8,128)(2,1)}, u32[]{:S(2)}, u32[]{:S(2)}) collective-permute-start(bf16[256,2048]{1,0:T(8,128)(2,1)} %collective-permute-done.1.refs_8_.refs_18_.refs_11_.refs_19_), channel_id=1, source_target_pairs={{4,2},{2,4},{5,3},{3,5},{12,10},{10,12},{13,11},{11,13},{20,18},{1... | collective-permute-start | bytes 3145736 | tf_op jit(solution)/shard_map/ppermute | solution.py:543
  54.6 14.9 %collective-permute-start.6 = (s32[2,5,17]{2,0,1:T(2,128)S(1)}, s32[2,5,17]{2,0,1:T(2,128)S(1)}, u32[]{:S(2)}, u32[]{:S(2)}) collective-permute-start(s32[2,5,17]{2,0,1:T(2,128)S(1)} %add_add_fusion), channel_id=1, source_target_pairs={{0,2},{6,4},{1,3},{7,5},{8,10},{14,12},{9,11},{15,13},{16,18},{22,... | collective-permute-start | bytes 2048 | tf_op jit(solution)/shard_map/ppermute | solution.py:537
  58.9 23.6 %collective-permute-start.4 = (bf16[2,96,2048]{2,1,0:T(8,128)(2,1)}, bf16[2,96,2048]{2,1,0:T(8,128)(2,1)}, u32[]{:S(2)}, u32[]{:S(2)}) collective-permute-start(bf16[2,96,2048]{2,1,0:T(8,128)(2,1)} %bitcast.12.refs_3_.refs_10_.refs_11_), channel_id=1, source_target_pairs={{0,2},{6,4},{1,3},{7,5},{8,10},{14,12},{9,11},{15,13},{16,18},{22,... | collective-permute-start | bytes 2359304 | tf_op jit(solution)/shard_map/ppermute | solution.py:537
  61.0 31.7 %collective-permute-start.8 = (bf16[256,2048]{1,0:T(8,128)(2,1)}, bf16[256,2048]{1,0:T(8,128)(2,1)}, u32[]{:S(2)}, u32[]{:S(2)}) collective-permute-start(bf16[256,2048]{1,0:T(8,128)(2,1)} %collective-permute-done.2.refs_9_.refs_19_.refs_12_.refs_20_), channel_id=1, source_target_pairs={{4,2},{2,4},{5,3},{3,5},{12,10},{10,12},{13,11},{11,13},{20,18},{1... | collective-permute-start | bytes 3145736 | tf_op jit(solution)/shard_map/ppermute | solution.py:543
  65.4 25.4 %collective-permute-start.3 = (bf16[96,2048]{1,0:T(8,128)(2,1)S(1)}, bf16[96,2048]{1,0:T(8,128)(2,1)S(1)}, u32[]{:S(2)}, u32[]{:S(2)}) collective-permute-start(bf16[96,2048]{1,0:T(8,128)(2,1)S(1)} %get-tuple-element.154.refs_1_.own), channel_id=1, source_target_pairs={{0,2},{6,4},{1,3},{7,5},{8,10},{14,12},{9,11},{15,13},{16,18},{22,... | collective-permute-start | bytes 1179656 | tf_op jit(solution)/shard_map/ppermute | solution.py:537
  70.6 38.7 %collective-permute-start.12 = (bf16[512,512]{1,0:T(8,128)(2,1)S(1)}, bf16[512,512]{1,0:T(8,128)(2,1)S(1)}, u32[]{:S(2)}, u32[]{:S(2)}) collective-permute-start(bf16[512,512]{1,0:T(8,128)(2,1)S(1)} %bitcast.71), channel_id=1, source_target_pairs={{4,2},{2,4},{5,3},{3,5},{12,10},{10,12},{13,11},{11,13},{20,18},{1... | collective-permute-start | bytes 1572872 | tf_op jit(solution)/shard_map/ppermute | solution.py:543
  82.4 26.9 %collective-permute-start.13 = (bf16[512,512]{1,0:T(8,128)(2,1)S(1)}, bf16[512,512]{1,0:T(8,128)(2,1)S(1)}, u32[]{:S(2)}, u32[]{:S(2)}) collective-permute-start(bf16[512,512]{1,0:T(8,128)(2,1)S(1)} %collective-permute-done.5.rest_1_.refs_13_.refs_16_.refs_14_), channel_id=1, source_target_pairs={{4,2},{2,4},{5,3},{3,5},{12,10},{10,12},{13,11},{11,13},{20,18},{1... | collective-permute-start | bytes 1572872 | tf_op jit(solution)/shard_map/ppermute | solution.py:543
  83.1 24.5 %collective-permute-start.11 = (bf16[96,2048]{1,0:T(8,128)(2,1)S(1)}, bf16[96,2048]{1,0:T(8,128)(2,1)S(1)}, u32[]{:S(2)}, u32[]{:S(2)}) collective-permute-start(bf16[96,2048]{1,0:T(8,128)(2,1)S(1)} %get-tuple-element.93.up_own.own), channel_id=1, source_target_pairs={{0,2},{6,4},{1,3},{7,5},{8,10},{14,12},{9,11},{15,13},{16,18},{22,... | collective-permute-start | bytes 1179656 | tf_op jit(solution)/shard_map/ppermute | solution.py:537
  91.5 9.3 %collective-permute-start.10 = (bf16[96,512]{1,0:T(8,128)(2,1)S(1)}, bf16[96,512]{1,0:T(8,128)(2,1)S(1)}, u32[]{:S(2)}, u32[]{:S(2)}) collective-permute-start(bf16[96,512]{1,0:T(8,128)(2,1)S(1)} %constant_dynamic-slice_fusion), channel_id=1, source_target_pairs={{2,0},{4,6},{3,1},{5,7},{10,8},{12,14},{11,9},{13,15},{18,16},{20,... | collective-permute-start | bytes 294920 | tf_op jit(solution)/shard_map/ppermute | solution.py:540
  92.8 14.8 %collective-permute-start.9 = (bf16[96,2048]{1,0:T(8,128)(2,1)S(1)}, bf16[96,2048]{1,0:T(8,128)(2,1)S(1)}, u32[]{:S(2)}, u32[]{:S(2)}) collective-permute-start(bf16[96,2048]{1,0:T(8,128)(2,1)S(1)} %copy-done.17), channel_id=1, source_target_pairs={{0,2},{6,4},{1,3},{7,5},{8,10},{14,12},{9,11},{15,13},{16,18},{22,... | collective-permute-start | bytes 1179656 | tf_op jit(solution)/shard_map/ppermute | solution.py:537
  110.5 3.3 %collective-permute-start.14 = (bf16[2,48,2048]{2,1,0:T(8,128)(2,1)S(1)}, bf16[2,48,2048]{2,1,0:T(8,128)(2,1)S(1)}, u32[]{:S(2)}, u32[]{:S(2)}) collective-permute-start(bf16[2,48,2048]{2,1,0:T(8,128)(2,1)S(1)} %get-tuple-element.104), channel_id=1, source_target_pairs={{0,1},{1,0},{2,3},{3,2},{4,5},{5,4},{6,7},{7,6},{8,9},{9,8},{10,11... | collective-permute-start | bytes 1179656 | tf_op jit(solution)/shard_map/ppermute | solution.py:551
  112.5 7.2 %collective-permute-start.17 = (bf16[192,1536]{1,0:T(8,128)(2,1)S(1)}, bf16[192,1536]{1,0:T(8,128)(2,1)S(1)}, u32[]{:S(2)}, u32[]{:S(2)}) collective-permute-start(bf16[192,1536]{1,0:T(8,128)(2,1)S(1)} %get-tuple-element.118), channel_id=1, source_target_pairs={{4,2},{2,4},{5,3},{3,5},{12,10},{10,12},{13,11},{11,13},{20,18},{1... | collective-permute-start | bytes 1769480 | tf_op jit(solution)/shard_map/ppermute | solution.py:543
  115.2 25.1 %collective-permute-start.16 = (bf16[192,1536]{1,0:T(8,128)(2,1)S(1)}, bf16[192,1536]{1,0:T(8,128)(2,1)S(1)}, u32[]{:S(2)}, u32[]{:S(2)}) collective-permute-start(bf16[192,1536]{1,0:T(8,128)(2,1)S(1)} %get-tuple-element.117), channel_id=1, source_target_pairs={{2,0},{4,6},{3,1},{5,7},{10,8},{12,14},{11,9},{13,15},{18,16},{20,... | collective-permute-start | bytes 1769480 | tf_op jit(solution)/shard_map/ppermute | solution.py:540
  116.5 3.1 %collective-permute-start.15 = (bf16[2,48,2048]{2,1,0:T(8,128)(2,1)S(1)}, bf16[2,48,2048]{2,1,0:T(8,128)(2,1)}, u32[]{:S(2)}, u32[]{:S(2)}) collective-permute-start(bf16[2,48,2048]{2,1,0:T(8,128)(2,1)S(1)} %get-tuple-element.105.ahead_0), channel_id=1, source_target_pairs={{2,10},{4,12},{10,18},{12,20},{18,26},{20,28},{3,11},{5,13},{11,19... | collective-permute-start | bytes 1179656 | tf_op jit(solution)/shard_map/ppermute | solution.py:560
  141.1 2.7 %collective-permute-start.19 = (bf16[2,48,2048]{2,1,0:T(8,128)(2,1)S(1)}, bf16[2,48,2048]{2,1,0:T(8,128)(2,1)S(1)}, u32[]{:S(2)}, u32[]{:S(2)}) collective-permute-start(bf16[2,48,2048]{2,1,0:T(8,128)(2,1)S(1)} %get-tuple-element.123), channel_id=1, source_target_pairs={{0,1},{1,0},{2,3},{3,2},{4,5},{5,4},{6,7},{7,6},{8,9},{9,8},{10,11... | collective-permute-start | bytes 1179656 | tf_op jit(solution)/shard_map/ppermute | solution.py:551
  142.0 4.7 %collective-permute-start.18 = (bf16[2,48,2048]{2,1,0:T(8,128)(2,1)}, bf16[2,48,2048]{2,1,0:T(8,128)(2,1)S(1)}, u32[]{:S(2)}, u32[]{:S(2)}) collective-permute-start(bf16[2,48,2048]{2,1,0:T(8,128)(2,1)} %collective-permute-done.15.refs_4_.passed), channel_id=1, source_target_pairs={{0,1},{1,0},{2,3},{3,2},{4,5},{5,4},{6,7},{7,6},{8,9},{9,8},{10,11... | collective-permute-start | bytes 1179656 | tf_op jit(solution)/shard_map/ppermute | solution.py:551
  142.0 17.5 %collective-permute-start.21 = (bf16[192,1536]{1,0:T(8,128)(2,1)}, bf16[192,1536]{1,0:T(8,128)(2,1)}, u32[]{:S(2)}, u32[]{:S(2)}) collective-permute-start(bf16[192,1536]{1,0:T(8,128)(2,1)} %get-tuple-element.124), channel_id=1, source_target_pairs={{4,0},{2,6},{5,1},{3,7},{12,8},{10,14},{13,9},{11,15},{20,16},{18,... | collective-permute-start | bytes 1769480 | tf_op jit(solution)/shard_map/ppermute | solution.py:546
  145.2 14.2 %collective-permute-start.20 = (bf16[2,48,2048]{2,1,0:T(8,128)(2,1)S(1)}, bf16[2,48,2048]{2,1,0:T(8,128)(2,1)}, u32[]{:S(2)}, u32[]{:S(2)}) collective-permute-start(bf16[2,48,2048]{2,1,0:T(8,128)(2,1)S(1)} %settle.1.back.back_0), channel_id=1, source_target_pairs={{10,2},{12,4},{18,10},{20,12},{26,18},{28,20},{11,3},{13,5},{19,11... | collective-permute-start | bytes 1179656 | tf_op jit(solution)/shard_map/ppermute | solution.py:560
  159.4 4.7 %collective-permute-start.22 = (bf16[2,48,2048]{2,1,0:T(8,128)(2,1)S(1)}, bf16[2,48,2048]{2,1,0:T(8,128)(2,1)S(1)}, u32[]{:S(2)}, u32[]{:S(2)}) collective-permute-start(bf16[2,48,2048]{2,1,0:T(8,128)(2,1)S(1)} %get-tuple-element.126), channel_id=1, source_target_pairs={{0,1},{1,0},{2,3},{3,2},{4,5},{5,4},{6,7},{7,6},{8,9},{9,8},{10,11... | collective-permute-start | bytes 1179656 | tf_op jit(solution)/shard_map/ppermute | solution.py:551
  162.1 5.1 %collective-permute-start.23 = (bf16[2,48,2048]{2,1,0:T(8,128)(2,1)S(1)}, bf16[2,48,2048]{2,1,0:T(8,128)(2,1)S(1)}, u32[]{:S(2)}, u32[]{:S(2)}) collective-permute-start(bf16[2,48,2048]{2,1,0:T(8,128)(2,1)S(1)} %get-tuple-element.128.up.refs_3_.mine), channel_id=1, source_target_pairs={{0,1},{1,0},{2,3},{3,2},{4,5},{5,4},{6,7},{7,6},{8,9},{9,8},{10,11... | collective-permute-start | bytes 1179656 | tf_op jit(solution)/shard_map/ppermute | solution.py:551
  162.2 6.8 %collective-permute-start.24 = (bf16[96,512]{1,0:T(8,128)(2,1)S(1)}, bf16[96,512]{1,0:T(8,128)(2,1)S(1)}, u32[]{:S(2)}, u32[]{:S(2)}) collective-permute-start(bf16[96,512]{1,0:T(8,128)(2,1)S(1)} %get-tuple-element.133), channel_id=1, source_target_pairs={{4,2},{2,4},{5,3},{3,5},{12,10},{10,12},{13,11},{11,13},{20,18},{1... | collective-permute-start | bytes 294920 | tf_op jit(solution)/shard_map/ppermute | solution.py:543
  162.9 7.5 %collective-permute-start.25 = (bf16[96,512]{1,0:T(8,128)(2,1)S(1)}, bf16[96,512]{1,0:T(8,128)(2,1)S(1)}, u32[]{:S(2)}, u32[]{:S(2)}) collective-permute-start(bf16[96,512]{1,0:T(8,128)(2,1)S(1)} %get-tuple-element.134), channel_id=1, source_target_pairs={{4,0},{2,6},{5,1},{3,7},{12,8},{10,14},{13,9},{11,15},{20,16},{18,... | collective-permute-start | bytes 294920 | tf_op jit(solution)/shard_map/ppermute | solution.py:546
  165.9 14.8 %collective-permute-start.26 = (bf16[96,2560]{1,0:T(8,128)(2,1)S(1)}, bf16[96,2560]{1,0:T(8,128)(2,1)S(1)}, u32[]{:S(2)}, u32[]{:S(2)}) collective-permute-start(bf16[96,2560]{1,0:T(8,128)(2,1)S(1)} %get-tuple-element.135), channel_id=1, source_target_pairs={{2,0},{4,6},{3,1},{5,7},{10,8},{12,14},{11,9},{13,15},{18,16},{20,... | collective-permute-start | bytes 1474568 | tf_op jit(solution)/shard_map/ppermute | solution.py:540
  180.8 2.7 %collective-permute-start.27 = (bf16[2,48,2048]{2,1,0:T(8,128)(2,1)S(1)}, bf16[2,48,2048]{2,1,0:T(8,128)(2,1)S(1)}, u32[]{:S(2)}, u32[]{:S(2)}) collective-permute-start(bf16[2,48,2048]{2,1,0:T(8,128)(2,1)S(1)} %get-tuple-element.138), channel_id=1, source_target_pairs={{0,1},{1,0},{2,3},{3,2},{4,5},{5,4},{6,7},{7,6},{8,9},{9,8},{10,11... | collective-permute-start | bytes 1179656 | tf_op jit(solution)/shard_map/ppermute | solution.py:551
  182.1 4.7 %collective-permute-start.29 = (bf16[2,96,512]{2,1,0:T(8,128)(2,1)S(1)}, bf16[2,96,512]{2,1,0:T(8,128)(2,1)S(1)}, u32[]{:S(2)}, u32[]{:S(2)}) collective-permute-start(bf16[2,96,512]{2,1,0:T(8,128)(2,1)S(1)} %pad_maximum_fusion.halves), channel_id=1, source_target_pairs={{0,1},{1,0},{2,3},{3,2},{4,5},{5,4},{6,7},{7,6},{8,9},{9,8},{10,11... | collective-permute-start | bytes 589832 | tf_op jit(solution)/shard_map/ppermute | solution.py:551
  184.7 8.0 %collective-permute-start.28 = (bf16[48,2048]{1,0:T(8,128)(2,1)S(1)}, bf16[48,2048]{1,0:T(8,128)(2,1)S(1)}, u32[]{:S(2)}, u32[]{:S(2)}) collective-permute-start(bf16[48,2048]{1,0:T(8,128)(2,1)S(1)} %get-tuple-element.144), channel_id=1, source_target_pairs={{2,0},{4,6},{3,1},{5,7},{10,8},{12,14},{11,9},{13,15},{18,16},{20,... | collective-permute-start | bytes 589832 | tf_op jit(solution)/shard_map/ppermute | solution.py:540
  (24 other events, 451.7 us)

commit v17 on v16

--- a/solution.py
+++ b/solution.py
@@ -159,13 +159,25 @@
         keep[r] = part[pl.ds(mine, share), :]
 
 
-def out_kernel(n, core, offs, gated, *rest):
-    weights = rest[:n]
-    send, keep, part = rest[n:]
+def early_kernel(offs, gated, upstream, *rest):
+    weights, (part, grad_gated) = rest[:-2], rest[-2:]
     depth = weights[0].shape[1]
-    for j in range(n):
+    total = None
+    for j, weight in enumerate(weights):
         columns = pl.ds(pl.multiple_of(offs[j], depth), depth)
-        part[:, columns] = dot(gated[0], weights[j][...]).astype(BF16)
+        part[:, columns] = dot(gated[0], weight[...]).astype(BF16)
+        term = dot_nt(upstream[:, columns], weight[...])
+        total = term if total is None else total + term
+    grad_gated[...] = total
+
+
+def out_kernel(skip, core, offs, gated, early, *rest):
+    weights, (send, keep, part) = rest[:-3], rest[-3:]
+    depth = weights[0].shape[1]
+    part[...] = early[...]
+    for j, weight in enumerate(weights):
+        columns = pl.ds(pl.multiple_of(offs[skip + j], depth), depth)
+        part[:, columns] = dot(gated[0], weight[...]).astype(BF16)
     split_rows(core[0], part, send, keep)
 
 
@@ -216,12 +228,17 @@
         split_rows(core[0], part, send, kept)
 
 
-def backward_kernel(parts, n, tick, split, core, in_offs, offs, *rest):
+def backward_kernel(parts, n, skip, tick, split, core, in_offs, offs, *rest):
+    n = n - skip
     count = 8 + n + parts
     up_sources, rest = rest[: 1 + split], rest[1 + split :]
+    early, rest = (rest[0], rest[1:]) if skip else (None, rest)
     sources, rest = (None,) + rest[:count], rest[count:]
     send, keep = rest[:2]
-    held, (grad_normed, part, up_sem, sems) = rest[2 : 3 + count], rest[3 + count :]
+    held, (grad_normed, scaled, part, begun, up_sems, sems) = (
+        rest[2 : 3 + count],
+        rest[3 + count :],
+    )
     ups, gate, vqk, slope, mixed, probs, factor, x_own, x_theirs = held[:9]
     out_parts, in_parts = held[9 : 9 + n], held[9 + n :]
     wide = 4 * HEAD_DIM
@@ -235,7 +252,9 @@
         copies.append(pltpu.make_async_copy(source, target, sems.at[i]))
     up_copies = []
     if not split:
-        up_copies.append(pltpu.make_async_copy(up_sources[0], ups, up_sem))
+        up_copies.append(pltpu.make_async_copy(up_sources[0], ups, up_sems.at[0]))
+    if skip:
+        up_copies.append(pltpu.make_async_copy(early, begun, up_sems.at[1]))
     copies = [None] + copies
     by_head = []
     for h in range(heads):
@@ -252,6 +271,8 @@
         )
     first = list(range(9, 9 + n))
     second = [1, 4, 2, 5, 6, 3]
+    for i in (7, 8):
+        copies[i].start()
     for copy in up_copies:
         copy.start()
     for i in first + second:
@@ -259,8 +280,6 @@
     for of_head in by_head:
         for copy in of_head:
             copy.start()
-    for i in (7, 8):
-        copies[i].start()
     if split:
         share = up_sources[0].shape[1]
         cores = ups.shape[0] // (2 * share)
@@ -268,13 +287,19 @@
             for r in range(2):
                 at = pl.multiple_of((r * cores + owner) * share, share)
                 ups[pl.ds(at, share), :] = up_sources[half][r]
+    roots = []
+    for i, source in ((7, x_own), (8, x_theirs)):
+        copies[i].wait()
+        floats = source[...].astype(F32)
+        roots.append(row_root(floats))
+        scaled[pl.ds((i - 7) * source.shape[0], source.shape[0]), :] = floats * roots[-1]
     for copy in up_copies:
         copy.wait()
     depth = out_parts[0].shape[1]
     length = x_own.shape[0]
-    grad_gated = None
+    grad_gated = begun[...] if skip else None
     for j in range(n):
-        columns = pl.ds(pl.multiple_of(offs[j], depth), depth)
+        columns = pl.ds(pl.multiple_of(offs[skip + j], depth), depth)
         copies[first[j]].wait()
         term = dot_nt(ups[:, columns], out_parts[j][...])
         grad_gated = term if grad_gated is None else grad_gated + term
@@ -317,17 +342,12 @@
             else:
                 grad_normed[:, columns] += term
         grad_pre = following
-    for i in (7, 8):
-        copies[i].wait()
-    for r, source in enumerate((x_own, x_theirs)):
+    for r, root in enumerate(roots):
         rows = pl.ds(r * length, length)
-        floats = source[...].astype(F32)
-        root = row_root(floats)
-        scaled = floats * root
+        scaled_rows = scaled[rows, :]
         grad_n = grad_normed[rows, :]
-        part[rows, :] = (
-            root * (grad_n - scaled * jnp.mean(grad_n * scaled, axis=-1, keepdims=True))
-        ).astype(BF16)
+        mean = jnp.mean(grad_n * scaled_rows, axis=-1, keepdims=True)
+        part[rows, :] = (root * (grad_n - scaled_rows * mean)).astype(BF16)
     split_rows(core[0], part, send, keep)
 
 
@@ -698,16 +718,17 @@
         name="project",
     )(host_flag, in_offs, x_own, x_theirs, stash_own, stash_theirs, keep, *in_hbm(in_parts))
 
-    def backward(ups, tick_no):
+    def backward(ups, tick_no, early=()):
         split = len(ups) - 1
+        skip = soon if early else 0
         layered = [gate, vqk, slope, mixed, probs, factor, stash_own, stash_theirs]
-        plain = list(out_parts) + list(in_parts)
+        plain = list(out_parts[skip:]) + list(in_parts)
         return pl.pallas_call(
-            on_host(functools.partial(backward_kernel, parts, n, tick_no, split)),
+            on_host(functools.partial(backward_kernel, parts, n, skip, tick_no, split)),
             grid=(1,),
             in_specs=[smem] * 4
             + [vmem if split else hbm] * len(ups)
-            + [hbm] * (len(layered) + len(plain)),
+            + [hbm] * (len(early) + len(layered) + len(plain)),
             out_specs=all_of(*halves),
             out_shape=kept_halves,
             scratch_shapes=[pltpu.VMEM((rows, width), BF16)]
@@ -715,14 +736,16 @@
             + [pltpu.VMEM(x.shape, x.dtype) for x in plain]
             + [
                 pltpu.VMEM((rows, width), F32),
+                pltpu.VMEM((rows, width), F32),
                 pltpu.VMEM((rows, width), BF16),
-                pltpu.SemaphoreType.DMA,
+                pltpu.VMEM((rows, slab), F32),
+                pltpu.SemaphoreType.DMA((2,)),
                 pltpu.SemaphoreType.DMA((1 + len(layered) + n + heads * parts,)),
             ],
             compiler_params=params,
             cost_estimate=cost((16 if split else 2) * matmul, 2 * weight_bytes),
             name="backward",
-        )(host_flag, core, in_offs, offs, *ups, *in_hbm(layered), *out_parts, *in_hbm(in_parts))
+        )(host_flag, core, in_offs, offs, *ups, *in_hbm(early + tuple(layered)), *plain[: n - skip], *in_hbm(in_parts))
 
     gated, new_theirs, up_near = lax.optimization_barrier((gated, new_theirs, up_near))
 
@@ -738,19 +761,34 @@
         compiler_params=small,
         name="pack",
     )(offs, gated, up_own, up_theirs)
-    packs, out_parts = lax.optimization_barrier((packs, out_parts))
+    soon = n // 2 + 1
+    packs, soon_parts = lax.optimization_barrier((packs, out_parts[:soon]))
+    early_shapes = [struct((rows, width), BF16), struct((rows, slab), F32)]
+    early_part, early_grad = pl.pallas_call(
+        early_kernel,
+        grid=(1,),
+        in_specs=[smem] + [row_of(gated, 0)] + all_of(up_0, *soon_parts),
+        out_specs=all_of(*early_shapes),
+        out_shape=[early_shapes[0], pltpu.HBM(early_shapes[1].shape, F32)],
+        compiler_params=small,
+        name="early",
+    )(offs, gated, *in_hbm([up_0]), *soon_parts)
+    early_part, early_grad, late_parts = lax.optimization_barrier(
+        (early_part, early_grad, out_parts[soon:])
+    )
+    out_parts = soon_parts + late_parts
 
     ahead_send, ahead_keep = pl.pallas_call(
-        functools.partial(out_kernel, n),
+        functools.partial(out_kernel, soon),
         grid=(1,),
-        in_specs=[smem] * 2 + [row_of(gated, 0)] + all_of(*out_parts),
+        in_specs=[smem] * 2 + [row_of(gated, 0)] + all_of(early_part, *out_parts[soon:]),
         out_specs=all_of(*halves),
         out_shape=halves,
         scratch_shapes=[pltpu.VMEM((rows, width), BF16)],
         compiler_params=small,
         cost_estimate=cost(matmul // 4, weight_bytes // 4),
         name="out",
-    )(core, offs, gated, *out_parts)
+    )(core, offs, gated, early_part, *out_parts[soon:])
     ahead_landed = swap_cores(ahead_send)
     first_shapes = [halves[0], struct((rows, 2 * slab + folded), BF16)]
     ahead_0, partner_pack = pl.pallas_call(
@@ -764,7 +802,7 @@
     )(core, *in_hbm([x_own, x_theirs]), ahead_keep, ahead_landed, gated)
     ahead_in = along_sections(ahead_0, 1)
     packs_near = [to_partner(partner_pack)] + [from_host(packs[m - 1], m) for m in between]
-    back_send, back_keep = backward(in_hbm([after(up_0, ahead_0)]), 0)
+    back_send, back_keep = backward(in_hbm([after(up_0, ahead_0)]), 0, (early_grad,))
     back_send, back_keep, ahead_in, packs_near = lax.optimization_barrier(
         (back_send, back_keep, ahead_in, packs_near)
     )

time: 196 us -> 196 us (level)
  waiting for transfers between devices: 102 us -> 93.1 us
  Pallas kernels: 21.7 us -> 25 us
  local copies, waits for them, and re-layouts: 7.16 us -> 10.3 us
  other arithmetic: 4.88 us -> 7.52 us
    ppermute x8, waiting for transfers between devices: 54 us -> 48.9 us  [from_partner(): return lax.ppermute(x, 'dp', [(h ^ 1, h) for h in hosts])]
    ppermute x4, waiting for transfers between devices: 33.8 us -> 30.1 us  [to_partner(): return lax.ppermute(x, 'dp', [(h, h ^ 1) for h in hosts])]
    pallas_call x3 -> x4, Pallas kernels: 4.46 us -> 7.43 us  [the longest x2 3.51 us: backward(): pl.pallas_call(on_host(functools.partial(backward_kernel, parts, n, skip,...]
    reshape x2, local copies, waits for them, and re-layouts: 0.16 us -> 2.73 us  [per_device(): m.reshape(m.shape[:2] + (-1,))]
  transfers between devices with their start and end apart: 30 -> 30, of which waited for: 14 -> 13; matrix products, arithmetic and copies ran while one was open for 4% -> 8% of each run, Pallas kernels for 11% -> 12%
where the time goes in v17:
time: 196 us; the launch traced here: 193 us
  waiting for transfers between devices  93.1 us (48%)
  starting transfers between devices  54.3 us (28%)
  Pallas kernels  25 us (13%)
  local copies, waits for them, and re-layouts  10.3 us (5%)
  other arithmetic  7.52 us (4%)
  between operations  3.24 us (2%)
    ppermute x8, waiting for transfers between devices, from_partner(): return lax.ppermute(x, 'dp', [(h ^ 1, h) for h in hosts])  48.9 us
    ppermute x4, waiting for transfers between devices, to_partner(): return lax.ppermute(x, 'dp', [(h, h ^ 1) for h in hosts])  30.1 us
    ppermute x8, starting transfers between devices, from_partner(): return lax.ppermute(x, 'dp', [(h ^ 1, h) for h in hosts])  30.1 us
    ppermute x2, waiting for transfers between devices, to_beyond(): lax.ppermute(x, 'dp', [(hosts[k ^ m], hosts[k] ^ 1) for k in range(n // 2)])  11.5 us
    ppermute x7, starting transfers between devices, from_host(): lax.ppermute(x, 'dp', [(hosts[k ^ m], hosts[k]) for k in range(n // 2)])  7.1 us
    ppermute x7, starting transfers between devices, swap_cores(): return lax.ppermute(x, 'cores', [(c, cores - 1 - c) for c in range(cores)])  6.5 us
    ppermute x4, starting transfers between devices, to_partner(): return lax.ppermute(x, 'dp', [(h, h ^ 1) for h in hosts])  5.16 us
  transfers between devices with their start and end apart: 30, of which 13 were waited for; matrix products, arithmetic and copies ran while one was open for 8% of the time, Pallas kernels for 12%

profile of v17, /device:TPU:5, one launch (start us, length us, event | category | flops | bytes accessed | tf_op | source)
XLA Modules:
  0.0 193.5 jit_solution(3494532324821710873)
XLA Ops:
  1.6 3.2 %slice_bitcast_fusion = (bf16[256,2048]{1,0:T(8,128)(2,1)}, bf16[256,2048]{1,0:T(8,128)(2,1)}) fusion(bf16[1,512,2048]{2,1,0:T(8,128)(2,1)} %param.17), kind=kLoop, calls=%fused_computation | loop fusion | bytes 4194304 | tf_op jit(solution)/shard_map/slice | solution.py:590
  4.8 6.6 %collective-permute-start.1 = (bf16[256,2048]{1,0:T(8,128)(2,1)}, bf16[256,2048]{1,0:T(8,128)(2,1)}, u32[]{:S(2)}, u32[]{:S(2)}) collective-permute-start(bf16[256,2048]{1,0:T(8,128)(2,1)} %get-tuple-element.160), channel_id=1, source_target_pairs={{0,2},{6,4},{1,3},{7,5},{8,10},{14,12},{9,11},{15,13},{16,18},{22,... | collective-permute-start | bytes 3145736 | tf_op jit(solution)/shard_map/ppermute | solution.py:557
  11.4 2.3 %collective-permute-start.2 = (bf16[256,2048]{1,0:T(8,128)(2,1)}, bf16[256,2048]{1,0:T(8,128)(2,1)}, u32[]{:S(2)}, u32[]{:S(2)}) collective-permute-start(bf16[256,2048]{1,0:T(8,128)(2,1)} %get-tuple-element.159), channel_id=1, source_target_pairs={{0,2},{6,4},{1,3},{7,5},{8,10},{14,12},{9,11},{15,13},{16,18},{22,... | collective-permute-start | bytes 3145736 | tf_op jit(solution)/shard_map/ppermute | solution.py:557
  19.7 12.5 %collective-permute-done.1.refs_8_.refs_16_.refs_11_.refs_19_ = bf16[256,2048]{1,0:T(8,128)(2,1)} collective-permute-done((bf16[256,2048]{1,0:T(8,128)(2,1)}, bf16[256,2048]{1,0:T(8,128)(2,1)}, u32[]{:S(2)}, u32[]{:S(2)}) %collective-permute-start.1) | collective-permute-done | bytes 1048608 | tf_op jit(solution)/shard_map/ppermute | solution.py:557
  32.2 1.6 collective-permute-start.7
  33.8 20.8 %collective-permute-done.2.refs_9_.refs_17_.refs_12_.refs_20_ = bf16[256,2048]{1,0:T(8,128)(2,1)} collective-permute-done((bf16[256,2048]{1,0:T(8,128)(2,1)}, bf16[256,2048]{1,0:T(8,128)(2,1)}, u32[]{:S(2)}, u32[]{:S(2)}) %collective-permute-start.2) | collective-permute-done | bytes 1048608 | tf_op jit(solution)/shard_map/ppermute | solution.py:557
  59.8 4.1 %collective-permute-start.6 = (s32[2,5,17]{2,0,1:T(2,128)S(1)}, s32[2,5,17]{2,0,1:T(2,128)S(1)}, u32[]{:S(2)}, u32[]{:S(2)}) collective-permute-start(s32[2,5,17]{2,0,1:T(2,128)S(1)} %add_add_fusion), channel_id=1, source_target_pairs={{0,2},{6,4},{1,3},{7,5},{8,10},{14,12},{9,11},{15,13},{16,18},{22,... | collective-permute-start | bytes 2048 | tf_op jit(solution)/shard_map/ppermute | solution.py:557
  63.9 2.2 %collective-permute-start.4 = (bf16[2,96,2048]{2,1,0:T(8,128)(2,1)}, bf16[2,96,2048]{2,1,0:T(8,128)(2,1)}, u32[]{:S(2)}, u32[]{:S(2)}) collective-permute-start(bf16[2,96,2048]{2,1,0:T(8,128)(2,1)} %bitcast.12.refs_3_.refs_11_), channel_id=1, source_target_pairs={{0,2},{6,4},{1,3},{7,5},{8,10},{14,12},{9,11},{15,13},{16,18},{22,... | collective-permute-start | bytes 2359304 | tf_op jit(solution)/shard_map/ppermute | solution.py:557
  66.1 1.7 collective-permute-start.8
  67.8 2.4 %select_bitcast_fusion = (bf16[96,2048]{1,0:T(8,128)(2,1)}, bf16[96,2048]{1,0:T(8,128)(2,1)S(1)}, bf16[96,2048]{1,0:T(8,128)(2,1)S(1)}) fusion(bf16[2,96,2048]{2,1,0:T(8,128)(2,1)} %param.14, bf16[2,96,2048]{2,1,0:T(8,128)(2,1)} %param.12, pred[]{:T(512)S(6)} %eq.44, bf16[1,96,2048]{2,1,0:T(8,128)(2,1)S(1)} %copy-done.19, bf16[1,96,2048]{2,1,0:T(8,128)(2,1)} %param.15, ...), kind=kLoop, calls=%fused_computation.6 | loop fusion | flops 589824 | bytes 3538946 | tf_op jit(solution)/shard_map/jit(_where)/select_n | solution.py:618
  70.2 2.1 %collective-permute-start.3 = (bf16[96,2048]{1,0:T(8,128)(2,1)S(1)}, bf16[96,2048]{1,0:T(8,128)(2,1)}, u32[]{:S(2)}, u32[]{:S(2)}) collective-permute-start(bf16[96,2048]{1,0:T(8,128)(2,1)S(1)} %get-tuple-element.162.refs_1_.own), channel_id=1, source_target_pairs={{0,2},{6,4},{1,3},{7,5},{8,10},{14,12},{9,11},{15,13},{16,18},{22,... | collective-permute-start | bytes 1179656 | tf_op jit(solution)/shard_map/ppermute | solution.py:557
  74.6 7.3 %collective-permute-done.4.refs_4_.refs_12_ = bf16[2,96,2048]{2,1,0:T(8,128)(2,1)} collective-permute-done((bf16[2,96,2048]{2,1,0:T(8,128)(2,1)}, bf16[2,96,2048]{2,1,0:T(8,128)(2,1)}, u32[]{:S(2)}, u32[]{:S(2)}) %collective-permute-start.4) | collective-permute-done | bytes 786464 | tf_op jit(solution)/shard_map/ppermute | solution.py:557
  82.7 5.5 %collective-permute-start.11 = (bf16[96,2048]{1,0:T(8,128)(2,1)S(1)}, bf16[96,2048]{1,0:T(8,128)(2,1)S(1)}, u32[]{:S(2)}, u32[]{:S(2)}) collective-permute-start(bf16[96,2048]{1,0:T(8,128)(2,1)S(1)} %get-tuple-element.97.up_own.own), channel_id=1, source_target_pairs={{0,2},{6,4},{1,3},{7,5},{8,10},{14,12},{9,11},{15,13},{16,18},{22,... | collective-permute-start | bytes 1179656 | tf_op jit(solution)/shard_map/ppermute | solution.py:557
  88.2 2.1 %collective-permute-done.3.refs_2_.theirs = bf16[96,2048]{1,0:T(8,128)(2,1)} collective-permute-done((bf16[96,2048]{1,0:T(8,128)(2,1)S(1)}, bf16[96,2048]{1,0:T(8,128)(2,1)}, u32[]{:S(2)}, u32[]{:S(2)}) %collective-permute-start.3) | collective-permute-done | bytes 393248 | tf_op jit(solution)/shard_map/ppermute | solution.py:557
  91.6 6.1 %collective-permute-start.9 = (bf16[96,2048]{1,0:T(8,128)(2,1)S(1)}, bf16[96,2048]{1,0:T(8,128)(2,1)S(1)}, u32[]{:S(2)}, u32[]{:S(2)}) collective-permute-start(bf16[96,2048]{1,0:T(8,128)(2,1)S(1)} %copy-done.16), channel_id=1, source_target_pairs={{0,2},{6,4},{1,3},{7,5},{8,10},{14,12},{9,11},{15,13},{16,18},{22,... | collective-permute-start | bytes 1179656 | tf_op jit(solution)/shard_map/ppermute | solution.py:557
  98.7 2.2 %project.1 = (bf16[3,192,512]{2,1,0:T(8,128)(2,1)S(1)}, f32[2,192,512]{2,1,0:T(8,128)}, bf16[2,192,1536]{2,1,0:T(8,128)(2,1)}, f32[2,192,2048]{2,1,0:T(8,128)}, ...) custom-call(s32[1]{0:T(128)} %bitcast.1.host, s32[6]{0:T(128)S(1)} %stack.73.refs_0_.refs_1_, ...), custom_call_target="tpu_custom_call" | custom-call | flops 4831838208 | bytes 20971520 | tf_op jit(solution)/shard_map/project/pallas_call | solution.py:700
  100.9 6.2 %collective-permute-done.9.refs_7_.new_theirs = bf16[96,2048]{1,0:T(8,128)(2,1)S(1)} collective-permute-done((bf16[96,2048]{1,0:T(8,128)(2,1)S(1)}, bf16[96,2048]{1,0:T(8,128)(2,1)S(1)}, u32[]{:S(2)}, u32[]{:S(2)}) %collective-permute-start.9) | collective-permute-done | bytes 393248 | tf_op jit(solution)/shard_map/ppermute | solution.py:557
  107.1 1.8 pack.1
  108.9 3.1 %early.1 = (bf16[192,2048]{1,0:T(8,128)(2,1)S(1)}, f32[192,512]{1,0:T(8,128)}) custom-call(s32[4]{0:T(128)S(1)} %add_multiply_fusion.offs.refs_2_, bf16[3,192,512]{2,1,0:T(8,128)(2,1)S(1)} %get-tuple-element.153.gated, bf16[192,2048]{1,0:T(8,128)(2,1)} %get-tuple-element.115.upstream.refs_3_.up_0, bf16[512,512]{1,0:T(8,128)(2,1)S(1)} %bitcast.72, ...), custom_call_target="tpu_custom_call" | custom-call | tf_op jit(solution)/shard_map/early/pallas_call | solution.py:767
  112.8 2.9 %collective-permute-start.14 = (bf16[2,48,2048]{2,1,0:T(8,128)(2,1)S(1)}, bf16[2,48,2048]{2,1,0:T(8,128)(2,1)S(1)}, u32[]{:S(2)}, u32[]{:S(2)}) collective-permute-start(bf16[2,48,2048]{2,1,0:T(8,128)(2,1)S(1)} %get-tuple-element.112), channel_id=1, source_target_pairs={{0,1},{1,0},{2,3},{3,2},{4,5},{5,4},{6,7},{7,6},{8,9},{9,8},{10,11... | collective-permute-start | bytes 1179656 | tf_op jit(solution)/shard_map/ppermute | solution.py:571
  119.8 1.4 collective-permute-start.15
  121.2 1.8 backward.2
  123.1 16.9 %collective-permute-done.16.pack.rest_0_ = bf16[192,1536]{1,0:T(8,128)(2,1)S(1)} collective-permute-done((bf16[192,1536]{1,0:T(8,128)(2,1)S(1)}, bf16[192,1536]{1,0:T(8,128)(2,1)S(1)}, u32[]{:S(2)}, u32[]{:S(2)}) %collective-permute-start.16) | collective-permute-done | bytes 589856 | tf_op jit(solution)/shard_map/ppermute | solution.py:560
  144.1 1.4 collective-permute-start.20
  146.6 2.6 %forward.1 = (bf16[2,48,2048]{2,1,0:T(8,128)(2,1)S(1)}, bf16[2,48,2048]{2,1,0:T(8,128)(2,1)}) custom-call(s32[1]{0:T(128)} %bitcast.1.host, s32[1]{0:T(128)} %bitcast.2.core.refs_0_, s32[6]{0:T(128)S(1)} %stack.73.refs_0_.refs_1_, s32[4]{0:T(128)S(1)} %add_multiply_fusion.offs.refs_2_, s32[1]{0:T(128)} %bitcast.33.refs_3_.fresh, ...), custom_call_target="tpu_custom_call" | custom-call | flops 3221225472 | bytes 20971520 | tf_op jit(solution)/shard_map/forward/pallas_call | solution.py:823
  149.1 9.1 %collective-permute-done.21.rest_2_ = bf16[192,1536]{1,0:T(8,128)(2,1)} collective-permute-done((bf16[192,1536]{1,0:T(8,128)(2,1)}, bf16[192,1536]{1,0:T(8,128)(2,1)}, u32[]{:S(2)}, u32[]{:S(2)}) %collective-permute-start.21) | collective-permute-done | bytes 589856 | tf_op jit(solution)/shard_map/ppermute | solution.py:566
  163.0 1.8 message.1
  166.1 1.7 backward.3
  167.8 2.4 %collective-permute-done.25 = bf16[96,512]{1,0:T(8,128)(2,1)S(1)} collective-permute-done((bf16[96,512]{1,0:T(8,128)(2,1)S(1)}, bf16[96,512]{1,0:T(8,128)(2,1)S(1)}, u32[]{:S(2)}, u32[]{:S(2)}) %collective-permute-start.25) | collective-permute-done | bytes 98336 | tf_op jit(solution)/shard_map/ppermute | solution.py:566
  170.2 10.5 %collective-permute-done.26.message = bf16[96,2560]{1,0:T(8,128)(2,1)S(1)} collective-permute-done((bf16[96,2560]{1,0:T(8,128)(2,1)S(1)}, bf16[96,2560]{1,0:T(8,128)(2,1)S(1)}, u32[]{:S(2)}, u32[]{:S(2)}) %collective-permute-start.26) | collective-permute-done | bytes 491552 | tf_op jit(solution)/shard_map/ppermute | solution.py:560
  186.8 3.2 %grads.1 = f32[512,512]{1,0:T(8,128)} custom-call(s32[1]{0:T(128)} %bitcast.1.host, s32[1]{0:T(128)} %bitcast.2.core.refs_0_, s32[4]{0:T(128)S(1)} %add_multiply_fusion.offs.refs_2_, bf16[3,192,512]{2,1,0:T(8,128)(2,1)S(1)} %get-tuple-element.153.gated, bf16[192,2048]{1,0:T(8,128)(2,1)S(1)} %copy-done.2, bf16[96,2048]{1,0:T(8,128)(2,1)S(1)} %copy-done.1, ...), custom_call_target="tpu_custom_call" | custom-call | flops 402653184 | bytes 2621440 | tf_op jit(solution)/shard_map/grads/pallas_call | solution.py:909
  190.0 2.7 %collective-permute-done.28 = bf16[48,2048]{1,0:T(8,128)(2,1)S(1)} collective-permute-done((bf16[48,2048]{1,0:T(8,128)(2,1)S(1)}, bf16[48,2048]{1,0:T(8,128)(2,1)S(1)}, u32[]{:S(2)}, u32[]{:S(2)}) %collective-permute-start.28) | collective-permute-done | bytes 196640 | tf_op jit(solution)/shard_map/ppermute | solution.py:560
  (126 shorter events, 38.2 us)
Async XLA Ops:
  0.7 54.0 %copy-start.23 = (s32[1,5]{1,0:T(1,128)S(1)}, s32[1,5]{1,0:T(1,128)}, u32[]{:S(2)}) copy-start(s32[1,5]{1,0:T(1,128)} %param.19) | copy-start | bytes 64
  0.7 67.1 %copy-start.19 = (bf16[1,96,2048]{2,1,0:T(8,128)(2,1)S(1)}, bf16[1,96,2048]{2,1,0:T(8,128)(2,1)}, u32[]{:S(2)}) copy-start(bf16[1,96,2048]{2,1,0:T(8,128)(2,1)} %param.13) | copy-start | bytes 1179652
  0.7 54.0 %collective-permute-start = (bf16[512,2048]{1,0:T(8,128)(2,1)}, bf16[512,2048]{1,0:T(8,128)(2,1)S(1)}, u32[]{:S(2)}, u32[]{:S(2)}) collective-permute-start(bf16[512,2048]{1,0:T(8,128)(2,1)} %bitcast.76), channel_id=1, source_target_pairs={{4,2},{2,4},{5,3},{3,5},{12,10},{10,12},{13,11},{11,13},{20,18},{1... | collective-permute-start | bytes 6291464 | tf_op jit(solution)/shard_map/ppermute | solution.py:563
  4.8 27.4 %collective-permute-start.1 = (bf16[256,2048]{1,0:T(8,128)(2,1)}, bf16[256,2048]{1,0:T(8,128)(2,1)}, u32[]{:S(2)}, u32[]{:S(2)}) collective-permute-start(bf16[256,2048]{1,0:T(8,128)(2,1)} %get-tuple-element.160), channel_id=1, source_target_pairs={{0,2},{6,4},{1,3},{7,5},{8,10},{14,12},{9,11},{15,13},{16,18},{22,... | collective-permute-start | bytes 3145736 | tf_op jit(solution)/shard_map/ppermute | solution.py:557
  11.4 43.3 %collective-permute-start.2 = (bf16[256,2048]{1,0:T(8,128)(2,1)}, bf16[256,2048]{1,0:T(8,128)(2,1)}, u32[]{:S(2)}, u32[]{:S(2)}) collective-permute-start(bf16[256,2048]{1,0:T(8,128)(2,1)} %get-tuple-element.159), channel_id=1, source_target_pairs={{0,2},{6,4},{1,3},{7,5},{8,10},{14,12},{9,11},{15,13},{16,18},{22,... | collective-permute-start | bytes 3145736 | tf_op jit(solution)/shard_map/ppermute | solution.py:557
  13.6 56.6 %collective-permute-start.5 = (bf16[512,512]{1,0:T(8,128)(2,1)S(1)}, bf16[512,512]{1,0:T(8,128)(2,1)S(1)}, u32[]{:S(2)}, u32[]{:S(2)}) collective-permute-start(bf16[512,512]{1,0:T(8,128)(2,1)S(1)} %bitcast.70), channel_id=1, source_target_pairs={{0,2},{6,4},{1,3},{7,5},{8,10},{14,12},{9,11},{15,13},{16,18},{22,... | collective-permute-start | bytes 1572872 | tf_op jit(solution)/shard_map/ppermute | solution.py:557
  32.2 50.5 %collective-permute-start.7 = (bf16[256,2048]{1,0:T(8,128)(2,1)}, bf16[256,2048]{1,0:T(8,128)(2,1)}, u32[]{:S(2)}, u32[]{:S(2)}) collective-permute-start(bf16[256,2048]{1,0:T(8,128)(2,1)} %collective-permute-done.1.refs_8_.refs_16_.refs_11_.refs_19_), channel_id=1, source_target_pairs={{4,2},{2,4},{5,3},{3,5},{12,10},{10,12},{13,11},{11,13},{20,18},{1... | collective-permute-start | bytes 3145736 | tf_op jit(solution)/shard_map/ppermute | solution.py:563
  59.8 12.5 %collective-permute-start.6 = (s32[2,5,17]{2,0,1:T(2,128)S(1)}, s32[2,5,17]{2,0,1:T(2,128)S(1)}, u32[]{:S(2)}, u32[]{:S(2)}) collective-permute-start(s32[2,5,17]{2,0,1:T(2,128)S(1)} %add_add_fusion), channel_id=1, source_target_pairs={{0,2},{6,4},{1,3},{7,5},{8,10},{14,12},{9,11},{15,13},{16,18},{22,... | collective-permute-start | bytes 2048 | tf_op jit(solution)/shard_map/ppermute | solution.py:557
  63.9 18.0 %collective-permute-start.4 = (bf16[2,96,2048]{2,1,0:T(8,128)(2,1)}, bf16[2,96,2048]{2,1,0:T(8,128)(2,1)}, u32[]{:S(2)}, u32[]{:S(2)}) collective-permute-start(bf16[2,96,2048]{2,1,0:T(8,128)(2,1)} %bitcast.12.refs_3_.refs_11_), channel_id=1, source_target_pairs={{0,2},{6,4},{1,3},{7,5},{8,10},{14,12},{9,11},{15,13},{16,18},{22,... | collective-permute-start | bytes 2359304 | tf_op jit(solution)/shard_map/ppermute | solution.py:557
  66.1 25.4 %collective-permute-start.8 = (bf16[256,2048]{1,0:T(8,128)(2,1)}, bf16[256,2048]{1,0:T(8,128)(2,1)}, u32[]{:S(2)}, u32[]{:S(2)}) collective-permute-start(bf16[256,2048]{1,0:T(8,128)(2,1)} %collective-permute-done.2.refs_9_.refs_17_.refs_12_.refs_20_), channel_id=1, source_target_pairs={{4,2},{2,4},{5,3},{3,5},{12,10},{10,12},{13,11},{11,13},{20,18},{1... | collective-permute-start | bytes 3145736 | tf_op jit(solution)/shard_map/ppermute | solution.py:563
  70.2 20.0 %collective-permute-start.3 = (bf16[96,2048]{1,0:T(8,128)(2,1)S(1)}, bf16[96,2048]{1,0:T(8,128)(2,1)}, u32[]{:S(2)}, u32[]{:S(2)}) collective-permute-start(bf16[96,2048]{1,0:T(8,128)(2,1)S(1)} %get-tuple-element.162.refs_1_.own), channel_id=1, source_target_pairs={{0,2},{6,4},{1,3},{7,5},{8,10},{14,12},{9,11},{15,13},{16,18},{22,... | collective-permute-start | bytes 1179656 | tf_op jit(solution)/shard_map/ppermute | solution.py:557
  73.3 35.6 %collective-permute-start.12 = (bf16[512,512]{1,0:T(8,128)(2,1)S(1)}, bf16[512,512]{1,0:T(8,128)(2,1)S(1)}, u32[]{:S(2)}, u32[]{:S(2)}) collective-permute-start(bf16[512,512]{1,0:T(8,128)(2,1)S(1)} %bitcast.71), channel_id=1, source_target_pairs={{4,2},{2,4},{5,3},{3,5},{12,10},{10,12},{13,11},{11,13},{20,18},{1... | collective-permute-start | bytes 1572872 | tf_op jit(solution)/shard_map/ppermute | solution.py:563
  81.9 30.0 %collective-permute-start.13 = (bf16[512,512]{1,0:T(8,128)(2,1)S(1)}, bf16[512,512]{1,0:T(8,128)(2,1)S(1)}, u32[]{:S(2)}, u32[]{:S(2)}) collective-permute-start(bf16[512,512]{1,0:T(8,128)(2,1)S(1)} %collective-permute-done.5.rest_1_.refs_16_.refs_14_), channel_id=1, source_target_pairs={{4,2},{2,4},{5,3},{3,5},{12,10},{10,12},{13,11},{11,13},{20,18},{1... | collective-permute-start | bytes 1572872 | tf_op jit(solution)/shard_map/ppermute | solution.py:563
  82.7 24.5 %collective-permute-start.11 = (bf16[96,2048]{1,0:T(8,128)(2,1)S(1)}, bf16[96,2048]{1,0:T(8,128)(2,1)S(1)}, u32[]{:S(2)}, u32[]{:S(2)}) collective-permute-start(bf16[96,2048]{1,0:T(8,128)(2,1)S(1)} %get-tuple-element.97.up_own.own), channel_id=1, source_target_pairs={{0,2},{6,4},{1,3},{7,5},{8,10},{14,12},{9,11},{15,13},{16,18},{22,... | collective-permute-start | bytes 1179656 | tf_op jit(solution)/shard_map/ppermute | solution.py:557
  90.3 10.6 %collective-permute-start.10 = (bf16[96,512]{1,0:T(8,128)(2,1)S(1)}, bf16[96,512]{1,0:T(8,128)(2,1)S(1)}, u32[]{:S(2)}, u32[]{:S(2)}) collective-permute-start(bf16[96,512]{1,0:T(8,128)(2,1)S(1)} %constant_dynamic-slice_fusion), channel_id=1, source_target_pairs={{2,0},{4,6},{3,1},{5,7},{10,8},{12,14},{11,9},{13,15},{18,16},{20,... | collective-permute-start | bytes 294920 | tf_op jit(solution)/shard_map/ppermute | solution.py:560
  91.6 15.5 %collective-permute-start.9 = (bf16[96,2048]{1,0:T(8,128)(2,1)S(1)}, bf16[96,2048]{1,0:T(8,128)(2,1)S(1)}, u32[]{:S(2)}, u32[]{:S(2)}) collective-permute-start(bf16[96,2048]{1,0:T(8,128)(2,1)S(1)} %copy-done.16), channel_id=1, source_target_pairs={{0,2},{6,4},{1,3},{7,5},{8,10},{14,12},{9,11},{15,13},{16,18},{22,... | collective-permute-start | bytes 1179656 | tf_op jit(solution)/shard_map/ppermute | solution.py:557
  112.8 4.2 %collective-permute-start.14 = (bf16[2,48,2048]{2,1,0:T(8,128)(2,1)S(1)}, bf16[2,48,2048]{2,1,0:T(8,128)(2,1)S(1)}, u32[]{:S(2)}, u32[]{:S(2)}) collective-permute-start(bf16[2,48,2048]{2,1,0:T(8,128)(2,1)S(1)} %get-tuple-element.112), channel_id=1, source_target_pairs={{0,1},{1,0},{2,3},{3,2},{4,5},{5,4},{6,7},{7,6},{8,9},{9,8},{10,11... | collective-permute-start | bytes 1179656 | tf_op jit(solution)/shard_map/ppermute | solution.py:571
  115.7 7.3 %collective-permute-start.17 = (bf16[192,1536]{1,0:T(8,128)(2,1)S(1)}, bf16[192,1536]{1,0:T(8,128)(2,1)S(1)}, u32[]{:S(2)}, u32[]{:S(2)}) collective-permute-start(bf16[192,1536]{1,0:T(8,128)(2,1)S(1)} %get-tuple-element.126), channel_id=1, source_target_pairs={{4,2},{2,4},{5,3},{3,5},{12,10},{10,12},{13,11},{11,13},{20,18},{1... | collective-permute-start | bytes 1769480 | tf_op jit(solution)/shard_map/ppermute | solution.py:563
  118.5 21.5 %collective-permute-start.16 = (bf16[192,1536]{1,0:T(8,128)(2,1)S(1)}, bf16[192,1536]{1,0:T(8,128)(2,1)S(1)}, u32[]{:S(2)}, u32[]{:S(2)}) collective-permute-start(bf16[192,1536]{1,0:T(8,128)(2,1)S(1)} %get-tuple-element.125), channel_id=1, source_target_pairs={{2,0},{4,6},{3,1},{5,7},{10,8},{12,14},{11,9},{13,15},{18,16},{20,... | collective-permute-start | bytes 1769480 | tf_op jit(solution)/shard_map/ppermute | solution.py:560
  119.8 3.3 %collective-permute-start.15 = (bf16[2,48,2048]{2,1,0:T(8,128)(2,1)S(1)}, bf16[2,48,2048]{2,1,0:T(8,128)(2,1)}, u32[]{:S(2)}, u32[]{:S(2)}) collective-permute-start(bf16[2,48,2048]{2,1,0:T(8,128)(2,1)S(1)} %get-tuple-element.113.ahead_0), channel_id=1, source_target_pairs={{2,10},{4,12},{10,18},{12,20},{18,26},{20,28},{3,11},{5,13},{11,19... | collective-permute-start | bytes 1179656 | tf_op jit(solution)/shard_map/ppermute | solution.py:580
  140.0 2.7 %collective-permute-start.19 = (bf16[2,48,2048]{2,1,0:T(8,128)(2,1)S(1)}, bf16[2,48,2048]{2,1,0:T(8,128)(2,1)S(1)}, u32[]{:S(2)}, u32[]{:S(2)}) collective-permute-start(bf16[2,48,2048]{2,1,0:T(8,128)(2,1)S(1)} %get-tuple-element.131), channel_id=1, source_target_pairs={{0,1},{1,0},{2,3},{3,2},{4,5},{5,4},{6,7},{7,6},{8,9},{9,8},{10,11... | collective-permute-start | bytes 1179656 | tf_op jit(solution)/shard_map/ppermute | solution.py:571
  140.8 4.7 %collective-permute-start.18 = (bf16[2,48,2048]{2,1,0:T(8,128)(2,1)}, bf16[2,48,2048]{2,1,0:T(8,128)(2,1)}, u32[]{:S(2)}, u32[]{:S(2)}) collective-permute-start(bf16[2,48,2048]{2,1,0:T(8,128)(2,1)} %collective-permute-done.15.refs_4_.passed), channel_id=1, source_target_pairs={{0,1},{1,0},{2,3},{3,2},{4,5},{5,4},{6,7},{7,6},{8,9},{9,8},{10,11... | collective-permute-start | bytes 1179656 | tf_op jit(solution)/shard_map/ppermute | solution.py:571
  140.8 17.5 %collective-permute-start.21 = (bf16[192,1536]{1,0:T(8,128)(2,1)}, bf16[192,1536]{1,0:T(8,128)(2,1)}, u32[]{:S(2)}, u32[]{:S(2)}) collective-permute-start(bf16[192,1536]{1,0:T(8,128)(2,1)} %get-tuple-element.132), channel_id=1, source_target_pairs={{4,0},{2,6},{5,1},{3,7},{12,8},{10,14},{13,9},{11,15},{20,16},{18,... | collective-permute-start | bytes 1769480 | tf_op jit(solution)/shard_map/ppermute | solution.py:566
  144.1 14.2 %collective-permute-start.20 = (bf16[2,48,2048]{2,1,0:T(8,128)(2,1)S(1)}, bf16[2,48,2048]{2,1,0:T(8,128)(2,1)}, u32[]{:S(2)}, u32[]{:S(2)}) collective-permute-start(bf16[2,48,2048]{2,1,0:T(8,128)(2,1)S(1)} %settle.1.back.back_0), channel_id=1, source_target_pairs={{10,2},{12,4},{18,10},{20,12},{26,18},{28,20},{11,3},{13,5},{19,11... | collective-permute-start | bytes 1179656 | tf_op jit(solution)/shard_map/ppermute | solution.py:580
  158.3 4.7 %collective-permute-start.22 = (bf16[2,48,2048]{2,1,0:T(8,128)(2,1)S(1)}, bf16[2,48,2048]{2,1,0:T(8,128)(2,1)S(1)}, u32[]{:S(2)}, u32[]{:S(2)}) collective-permute-start(bf16[2,48,2048]{2,1,0:T(8,128)(2,1)S(1)} %get-tuple-element.134), channel_id=1, source_target_pairs={{0,1},{1,0},{2,3},{3,2},{4,5},{5,4},{6,7},{7,6},{8,9},{9,8},{10,11... | collective-permute-start | bytes 1179656 | tf_op jit(solution)/shard_map/ppermute | solution.py:571
  160.9 5.1 %collective-permute-start.23 = (bf16[2,48,2048]{2,1,0:T(8,128)(2,1)S(1)}, bf16[2,48,2048]{2,1,0:T(8,128)(2,1)S(1)}, u32[]{:S(2)}, u32[]{:S(2)}) collective-permute-start(bf16[2,48,2048]{2,1,0:T(8,128)(2,1)S(1)} %get-tuple-element.136.up.refs_3_.mine), channel_id=1, source_target_pairs={{0,1},{1,0},{2,3},{3,2},{4,5},{5,4},{6,7},{7,6},{8,9},{9,8},{10,11... | collective-permute-start | bytes 1179656 | tf_op jit(solution)/shard_map/ppermute | solution.py:571
  161.0 6.8 %collective-permute-start.24 = (bf16[96,512]{1,0:T(8,128)(2,1)S(1)}, bf16[96,512]{1,0:T(8,128)(2,1)S(1)}, u32[]{:S(2)}, u32[]{:S(2)}) collective-permute-start(bf16[96,512]{1,0:T(8,128)(2,1)S(1)} %get-tuple-element.141), channel_id=1, source_target_pairs={{4,2},{2,4},{5,3},{3,5},{12,10},{10,12},{13,11},{11,13},{20,18},{1... | collective-permute-start | bytes 294920 | tf_op jit(solution)/shard_map/ppermute | solution.py:563
  161.7 8.5 %collective-permute-start.25 = (bf16[96,512]{1,0:T(8,128)(2,1)S(1)}, bf16[96,512]{1,0:T(8,128)(2,1)S(1)}, u32[]{:S(2)}, u32[]{:S(2)}) collective-permute-start(bf16[96,512]{1,0:T(8,128)(2,1)S(1)} %get-tuple-element.142), channel_id=1, source_target_pairs={{4,0},{2,6},{5,1},{3,7},{12,8},{10,14},{13,9},{11,15},{20,16},{18,... | collective-permute-start | bytes 294920 | tf_op jit(solution)/shard_map/ppermute | solution.py:566
  164.8 15.9 %collective-permute-start.26 = (bf16[96,2560]{1,0:T(8,128)(2,1)S(1)}, bf16[96,2560]{1,0:T(8,128)(2,1)S(1)}, u32[]{:S(2)}, u32[]{:S(2)}) collective-permute-start(bf16[96,2560]{1,0:T(8,128)(2,1)S(1)} %get-tuple-element.143), channel_id=1, source_target_pairs={{2,0},{4,6},{3,1},{5,7},{10,8},{12,14},{11,9},{13,15},{18,16},{20,... | collective-permute-start | bytes 1474568 | tf_op jit(solution)/shard_map/ppermute | solution.py:560
  180.7 2.7 %collective-permute-start.27 = (bf16[2,48,2048]{2,1,0:T(8,128)(2,1)S(1)}, bf16[2,48,2048]{2,1,0:T(8,128)(2,1)S(1)}, u32[]{:S(2)}, u32[]{:S(2)}) collective-permute-start(bf16[2,48,2048]{2,1,0:T(8,128)(2,1)S(1)} %get-tuple-element.146), channel_id=1, source_target_pairs={{0,1},{1,0},{2,3},{3,2},{4,5},{5,4},{6,7},{7,6},{8,9},{9,8},{10,11... | collective-permute-start | bytes 1179656 | tf_op jit(solution)/shard_map/ppermute | solution.py:571
  182.1 4.7 %collective-permute-start.29 = (bf16[2,96,512]{2,1,0:T(8,128)(2,1)S(1)}, bf16[2,96,512]{2,1,0:T(8,128)(2,1)S(1)}, u32[]{:S(2)}, u32[]{:S(2)}) collective-permute-start(bf16[2,96,512]{2,1,0:T(8,128)(2,1)S(1)} %pad_maximum_fusion.halves), channel_id=1, source_target_pairs={{0,1},{1,0},{2,3},{3,2},{4,5},{5,4},{6,7},{7,6},{8,9},{9,8},{10,11... | collective-permute-start | bytes 589832 | tf_op jit(solution)/shard_map/ppermute | solution.py:571
  184.7 8.0 %collective-permute-start.28 = (bf16[48,2048]{1,0:T(8,128)(2,1)S(1)}, bf16[48,2048]{1,0:T(8,128)(2,1)S(1)}, u32[]{:S(2)}, u32[]{:S(2)}) collective-permute-start(bf16[48,2048]{1,0:T(8,128)(2,1)S(1)} %get-tuple-element.152), channel_id=1, source_target_pairs={{2,0},{4,6},{3,1},{5,7},{10,8},{12,14},{11,9},{13,15},{18,16},{20,... | collective-permute-start | bytes 589832 | tf_op jit(solution)/shard_map/ppermute | solution.py:560
  (22 other events, 301.4 us)

commit v18 on v17

--- a/solution.py
+++ b/solution.py
@@ -386,9 +386,9 @@
         ]
 
 
-def finish_kernel(slab, host, ahead_0, ahead_1, back_0, pack, message, ahead, back):
+def finish_kernel(slab, host, ahead_0, ahead_1, back_0, pack, message, given, ahead, back):
     width = back.shape[1]
-    depth = message.shape[1] - width
+    depth = message.shape[1] - width // 2
 
     @pl.when(host[0] != 0)
     def _():
@@ -399,8 +399,8 @@
     @pl.when(host[0] == 0)
     def _():
         unfold(pack, 2 * slab, ahead.at[0])
-        unfold(message, depth + width // 2, ahead.at[1])
-        unfold(message, depth, back)
+        unfold(message, depth, ahead.at[1])
+        back[...] = given[...]
 
 
 def settle_kernel(core, own, theirs, keep, landed, total):
@@ -412,6 +412,11 @@
         ).astype(BF16)
 
 
+def settle_two_kernel(core, own, theirs, keep, landed, total, other):
+    settle_kernel(core, own, theirs, keep, landed, total)
+    other[...] = total[1]
+
+
 def first_kernel(core, own, theirs, keep, landed, gated, total, pack):
     slab = gated.shape[2]
     settle_kernel(core, own, theirs, keep, landed, total)
@@ -421,10 +426,10 @@
 
 
 def message_kernel(
-    core, offs, fresh, new_own, new_theirs, passed, keep, landed, up, back, ahead, message
+    core, offs, fresh, new_own, new_theirs, passed, keep, landed, up, ahead, message
 ):
     share = keep.shape[1]
-    depth = message.shape[1] - up.shape[2]
+    depth = message.shape[1] - up.shape[2] // 2
     here = pl.ds(pl.multiple_of(core[0] * share, share), share)
     columns = pl.ds(pl.multiple_of(offs[1], depth), depth)
     for r, source in enumerate((new_own, new_theirs)):
@@ -433,8 +438,7 @@
             residual.astype(F32) + keep[r].astype(F32) + landed[r].astype(F32)
         ).astype(BF16)
         message[r * share : (r + 1) * share, :depth] = up[r, :, columns]
-    fold(back[1], message, depth)
-    fold(ahead[1], message, depth + up.shape[2] // 2)
+    fold(ahead[1], message, depth)
 
 
 def last_kernel(up, keep, landed, back, other):
@@ -807,12 +811,13 @@
         (back_send, back_keep, ahead_in, packs_near)
     )
     back_landed = swap_cores(back_send)
-    back_0 = pl.pallas_call(
-        settle_kernel,
+    settled = [halves[0], struct((share, width), BF16)]
+    back_0, back_given = pl.pallas_call(
+        settle_two_kernel,
         grid=(1,),
         in_specs=[smem] + all_of(up_own, up_theirs, back_keep, back_landed),
-        out_specs=all_of(halves[0])[0],
-        out_shape=halves[0],
+        out_specs=all_of(*settled),
+        out_shape=settled,
         compiler_params=small,
         name="settle",
     )(core, *in_hbm([up_own, up_theirs, back_keep]), back_landed)
@@ -869,8 +874,8 @@
     up_their = swap_cores(up_mine)
     landed = [from_host(cuts[m - 1], m) for m in between]
     landed += [to_beyond(cuts[n // 2 + m - 2], m) for m in between]
-    message_inputs = [new_own, new_theirs, ahead_in, ahead_keep, ahead_landed, up_mine, back_0]
-    message_shapes = [halves[0], struct((2 * share, depth + width), BF16)]
+    message_inputs = [new_own, new_theirs, ahead_in, ahead_keep, ahead_landed, up_mine]
+    message_shapes = [halves[0], struct((2 * share, depth + width // 2), BF16)]
     ahead_1, message = pl.pallas_call(
         message_kernel,
         grid=(1,),
@@ -879,10 +884,13 @@
         out_shape=message_shapes,
         compiler_params=small,
         name="message",
-    )(core, offs, first_flag, *in_hbm(message_inputs[:4]), *message_inputs[4:6], *in_hbm([back_0]))
+    )(core, offs, first_flag, *in_hbm(message_inputs[:4]), *message_inputs[4:])
     landed = landed + [to_partner(message)]
     back_send, back_keep = backward([up_mine, up_their], 1)
-    back_send, back_keep, landed = lax.optimization_barrier((back_send, back_keep, landed))
+    back_given = to_partner(back_given)
+    back_given, back_send, back_keep, landed = lax.optimization_barrier(
+        (back_given, back_send, back_keep, landed)
+    )
     landed = landed[-1:] + landed[:-1]
     last_inputs = [up_mine, *in_hbm([back_keep]), swap_cores(back_send)]
     last_shapes = [halves[0], struct((share, width), BF16)]
@@ -919,7 +927,7 @@
     )(host_flag, core, offs, *grad_inputs)
 
     first_pack, last_cut = lax.optimization_barrier((packs_near[0], landed[0], back_1))[:2]
-    finish_inputs = [ahead_0, ahead_1, back_0, first_pack, last_cut]
+    finish_inputs = [ahead_0, ahead_1, back_0, first_pack, last_cut, back_given]
     finish_shapes = [struct((ticks, share, width), BF16), struct((share, width), BF16)]
     ahead, back_first = pl.pallas_call(
         functools.partial(finish_kernel, slab),

time: 196 us -> 195 us (level)
  waiting for transfers between devices: 93.1 us -> 88.8 us
    ppermute x4 -> x5, waiting for transfers between devices: 30.1 us -> 26.5 us  [to_partner(): return lax.ppermute(x, 'dp', [(h, h ^ 1) for h in hosts])]
    ppermute x4 -> x5, starting transfers between devices: 5.16 us -> 6.45 us  [to_partner(): return lax.ppermute(x, 'dp', [(h, h ^ 1) for h in hosts])]
  transfers between devices with their start and end apart: 30 -> 31, of which waited for: 13 -> 14; matrix products, arithmetic and copies ran while one was open for 8% -> 8% of each run, Pallas kernels for 12% -> 13%
where the time goes in v18:
time: 195 us; the launch traced here: 193 us
  waiting for transfers between devices  88.8 us (46%)
  starting transfers between devices  55.5 us (28%)
  Pallas kernels  26.6 us (14%)
  local copies, waits for them, and re-layouts  10.9 us (6%)
  other arithmetic  7.53 us (4%)
  between operations  3.08 us (2%)
    ppermute x8, waiting for transfers between devices, from_partner(): return lax.ppermute(x, 'dp', [(h ^ 1, h) for h in hosts])  49.1 us
    ppermute x8, starting transfers between devices, from_partner(): return lax.ppermute(x, 'dp', [(h ^ 1, h) for h in hosts])  30.1 us
    ppermute x5, waiting for transfers between devices, to_partner(): return lax.ppermute(x, 'dp', [(h, h ^ 1) for h in hosts])  26.5 us
    ppermute x2, waiting for transfers between devices, to_beyond(): lax.ppermute(x, 'dp', [(hosts[k ^ m], hosts[k] ^ 1) for k in range(n // 2)])  10.7 us
    ppermute x7, starting transfers between devices, from_host(): lax.ppermute(x, 'dp', [(hosts[k ^ m], hosts[k]) for k in range(n // 2)])  7.12 us
    ppermute x7, starting transfers between devices, swap_cores(): return lax.ppermute(x, 'cores', [(c, cores - 1 - c) for c in range(cores)])  6.48 us
    ppermute x5, starting transfers between devices, to_partner(): return lax.ppermute(x, 'dp', [(h, h ^ 1) for h in hosts])  6.45 us
  transfers between devices with their start and end apart: 31, of which 14 were waited for; matrix products, arithmetic and copies ran while one was open for 8% of the time, Pallas kernels for 13%

profile of v18, /device:TPU:5, one launch (start us, length us, event | category | flops | bytes accessed | tf_op | source)
XLA Modules:
  0.0 192.5 jit_solution(18222850727633908972)
XLA Ops:
  1.6 3.2 %slice_bitcast_fusion = (bf16[256,2048]{1,0:T(8,128)(2,1)}, bf16[256,2048]{1,0:T(8,128)(2,1)}) fusion(bf16[1,512,2048]{2,1,0:T(8,128)(2,1)} %param.17), kind=kLoop, calls=%fused_computation | loop fusion | bytes 4194304 | tf_op jit(solution)/shard_map/slice | solution.py:594
  4.8 6.6 %collective-permute-start.1 = (bf16[256,2048]{1,0:T(8,128)(2,1)}, bf16[256,2048]{1,0:T(8,128)(2,1)}, u32[]{:S(2)}, u32[]{:S(2)}) collective-permute-start(bf16[256,2048]{1,0:T(8,128)(2,1)} %get-tuple-element.166), channel_id=1, source_target_pairs={{0,2},{6,4},{1,3},{7,5},{8,10},{14,12},{9,11},{15,13},{16,18},{22,... | collective-permute-start | bytes 3145736 | tf_op jit(solution)/shard_map/ppermute | solution.py:561
  11.4 2.3 %collective-permute-start.2 = (bf16[256,2048]{1,0:T(8,128)(2,1)}, bf16[256,2048]{1,0:T(8,128)(2,1)}, u32[]{:S(2)}, u32[]{:S(2)}) collective-permute-start(bf16[256,2048]{1,0:T(8,128)(2,1)} %get-tuple-element.165), channel_id=1, source_target_pairs={{0,2},{6,4},{1,3},{7,5},{8,10},{14,12},{9,11},{15,13},{16,18},{22,... | collective-permute-start | bytes 3145736 | tf_op jit(solution)/shard_map/ppermute | solution.py:561
  19.5 12.6 %collective-permute-done.1.refs_8_.refs_16_.refs_11_.refs_19_ = bf16[256,2048]{1,0:T(8,128)(2,1)} collective-permute-done((bf16[256,2048]{1,0:T(8,128)(2,1)}, bf16[256,2048]{1,0:T(8,128)(2,1)}, u32[]{:S(2)}, u32[]{:S(2)}) %collective-permute-start.1) | collective-permute-done | bytes 1048608 | tf_op jit(solution)/shard_map/ppermute | solution.py:561
  32.2 1.6 collective-permute-start.7
  33.8 20.8 %collective-permute-done.2.refs_9_.refs_17_.refs_12_.refs_20_ = bf16[256,2048]{1,0:T(8,128)(2,1)} collective-permute-done((bf16[256,2048]{1,0:T(8,128)(2,1)}, bf16[256,2048]{1,0:T(8,128)(2,1)}, u32[]{:S(2)}, u32[]{:S(2)}) %collective-permute-start.2) | collective-permute-done | bytes 1048608 | tf_op jit(solution)/shard_map/ppermute | solution.py:561
  59.8 4.1 %collective-permute-start.6 = (s32[2,5,17]{2,0,1:T(2,128)S(1)}, s32[2,5,17]{2,0,1:T(2,128)S(1)}, u32[]{:S(2)}, u32[]{:S(2)}) collective-permute-start(s32[2,5,17]{2,0,1:T(2,128)S(1)} %add_add_fusion), channel_id=1, source_target_pairs={{0,2},{6,4},{1,3},{7,5},{8,10},{14,12},{9,11},{15,13},{16,18},{22,... | collective-permute-start | bytes 2048 | tf_op jit(solution)/shard_map/ppermute | solution.py:561
  63.9 2.2 %collective-permute-start.4 = (bf16[2,96,2048]{2,1,0:T(8,128)(2,1)}, bf16[2,96,2048]{2,1,0:T(8,128)(2,1)}, u32[]{:S(2)}, u32[]{:S(2)}) collective-permute-start(bf16[2,96,2048]{2,1,0:T(8,128)(2,1)} %bitcast.12.refs_3_.refs_11_), channel_id=1, source_target_pairs={{0,2},{6,4},{1,3},{7,5},{8,10},{14,12},{9,11},{15,13},{16,18},{22,... | collective-permute-start | bytes 2359304 | tf_op jit(solution)/shard_map/ppermute | solution.py:561
  66.1 1.7 collective-permute-start.8
  67.8 2.4 %select_bitcast_fusion = (bf16[96,2048]{1,0:T(8,128)(2,1)}, bf16[96,2048]{1,0:T(8,128)(2,1)S(1)}, bf16[96,2048]{1,0:T(8,128)(2,1)S(1)}) fusion(bf16[2,96,2048]{2,1,0:T(8,128)(2,1)} %param.14, bf16[2,96,2048]{2,1,0:T(8,128)(2,1)} %param.12, pred[]{:T(512)S(6)} %eq.44, bf16[1,96,2048]{2,1,0:T(8,128)(2,1)S(1)} %copy-done.19, bf16[1,96,2048]{2,1,0:T(8,128)(2,1)} %param.15, ...), kind=kLoop, calls=%fused_computation.6 | loop fusion | flops 589824 | bytes 3538946 | tf_op jit(solution)/shard_map/jit(_where)/select_n | solution.py:622
  70.2 2.1 %collective-permute-start.3 = (bf16[96,2048]{1,0:T(8,128)(2,1)S(1)}, bf16[96,2048]{1,0:T(8,128)(2,1)}, u32[]{:S(2)}, u32[]{:S(2)}) collective-permute-start(bf16[96,2048]{1,0:T(8,128)(2,1)S(1)} %get-tuple-element.168.refs_1_.own), channel_id=1, source_target_pairs={{0,2},{6,4},{1,3},{7,5},{8,10},{14,12},{9,11},{15,13},{16,18},{22,... | collective-permute-start | bytes 1179656 | tf_op jit(solution)/shard_map/ppermute | solution.py:561
  74.6 7.3 %collective-permute-done.4.refs_4_.refs_12_ = bf16[2,96,2048]{2,1,0:T(8,128)(2,1)} collective-permute-done((bf16[2,96,2048]{2,1,0:T(8,128)(2,1)}, bf16[2,96,2048]{2,1,0:T(8,128)(2,1)}, u32[]{:S(2)}, u32[]{:S(2)}) %collective-permute-start.4) | collective-permute-done | bytes 786464 | tf_op jit(solution)/shard_map/ppermute | solution.py:561
  82.7 5.5 %collective-permute-start.11 = (bf16[96,2048]{1,0:T(8,128)(2,1)S(1)}, bf16[96,2048]{1,0:T(8,128)(2,1)S(1)}, u32[]{:S(2)}, u32[]{:S(2)}) collective-permute-start(bf16[96,2048]{1,0:T(8,128)(2,1)S(1)} %get-tuple-element.100.up_own.own), channel_id=1, source_target_pairs={{0,2},{6,4},{1,3},{7,5},{8,10},{14,12},{9,11},{15,13},{16,18},{22,... | collective-permute-start | bytes 1179656 | tf_op jit(solution)/shard_map/ppermute | solution.py:561
  88.2 2.1 %collective-permute-done.3.refs_2_.theirs = bf16[96,2048]{1,0:T(8,128)(2,1)} collective-permute-done((bf16[96,2048]{1,0:T(8,128)(2,1)S(1)}, bf16[96,2048]{1,0:T(8,128)(2,1)}, u32[]{:S(2)}, u32[]{:S(2)}) %collective-permute-start.3) | collective-permute-done | bytes 393248 | tf_op jit(solution)/shard_map/ppermute | solution.py:561
  91.6 6.1 %collective-permute-start.9 = (bf16[96,2048]{1,0:T(8,128)(2,1)S(1)}, bf16[96,2048]{1,0:T(8,128)(2,1)S(1)}, u32[]{:S(2)}, u32[]{:S(2)}) collective-permute-start(bf16[96,2048]{1,0:T(8,128)(2,1)S(1)} %copy-done.16), channel_id=1, source_target_pairs={{0,2},{6,4},{1,3},{7,5},{8,10},{14,12},{9,11},{15,13},{16,18},{22,... | collective-permute-start | bytes 1179656 | tf_op jit(solution)/shard_map/ppermute | solution.py:561
  98.7 2.2 %project.1 = (bf16[3,192,512]{2,1,0:T(8,128)(2,1)S(1)}, f32[2,192,512]{2,1,0:T(8,128)}, bf16[2,192,1536]{2,1,0:T(8,128)(2,1)}, f32[2,192,2048]{2,1,0:T(8,128)}, ...) custom-call(s32[1]{0:T(128)} %bitcast.1.host, s32[6]{0:T(128)S(1)} %stack.73.refs_0_.refs_1_, ...), custom_call_target="tpu_custom_call" | custom-call | flops 4831838208 | bytes 20971520 | tf_op jit(solution)/shard_map/project/pallas_call | solution.py:704
  100.9 6.2 %collective-permute-done.9.refs_7_.new_theirs = bf16[96,2048]{1,0:T(8,128)(2,1)S(1)} collective-permute-done((bf16[96,2048]{1,0:T(8,128)(2,1)S(1)}, bf16[96,2048]{1,0:T(8,128)(2,1)S(1)}, u32[]{:S(2)}, u32[]{:S(2)}) %collective-permute-start.9) | collective-permute-done | bytes 393248 | tf_op jit(solution)/shard_map/ppermute | solution.py:561
  107.1 1.7 pack.1
  108.9 3.1 %early.1 = (bf16[192,2048]{1,0:T(8,128)(2,1)S(1)}, f32[192,512]{1,0:T(8,128)}) custom-call(s32[4]{0:T(128)S(1)} %add_multiply_fusion.offs.refs_2_, bf16[3,192,512]{2,1,0:T(8,128)(2,1)S(1)} %get-tuple-element.159.gated, bf16[192,2048]{1,0:T(8,128)(2,1)} %get-tuple-element.118.upstream.refs_3_.up_0, bf16[512,512]{1,0:T(8,128)(2,1)S(1)} %bitcast.72, ...), custom_call_target="tpu_custom_call" | custom-call | tf_op jit(solution)/shard_map/early/pallas_call | solution.py:771
  112.8 2.8 %collective-permute-start.14 = (bf16[2,48,2048]{2,1,0:T(8,128)(2,1)S(1)}, bf16[2,48,2048]{2,1,0:T(8,128)(2,1)S(1)}, u32[]{:S(2)}, u32[]{:S(2)}) collective-permute-start(bf16[2,48,2048]{2,1,0:T(8,128)(2,1)S(1)} %get-tuple-element.115), channel_id=1, source_target_pairs={{0,1},{1,0},{2,3},{3,2},{4,5},{5,4},{6,7},{7,6},{8,9},{9,8},{10,11... | collective-permute-start | bytes 1179656 | tf_op jit(solution)/shard_map/ppermute | solution.py:575
  121.2 1.8 backward.2
  123.1 16.9 %collective-permute-done.16.pack.rest_0_ = bf16[192,1536]{1,0:T(8,128)(2,1)S(1)} collective-permute-done((bf16[192,1536]{1,0:T(8,128)(2,1)S(1)}, bf16[192,1536]{1,0:T(8,128)(2,1)S(1)}, u32[]{:S(2)}, u32[]{:S(2)}) %collective-permute-start.16) | collective-permute-done | bytes 589856 | tf_op jit(solution)/shard_map/ppermute | solution.py:564
  142.7 2.2 %settle.1 = (bf16[2,48,2048]{2,1,0:T(8,128)(2,1)}, bf16[48,2048]{1,0:T(8,128)(2,1)S(1)}) custom-call(s32[1]{0:T(128)} %bitcast.2.core.refs_0_, bf16[96,2048]{1,0:T(8,128)(2,1)} %copy-done, bf16[96,2048]{1,0:T(8,128)(2,1)} %copy-done.10, bf16[2,48,2048]{2,1,0:T(8,128)(2,1)} %get-tuple-element.133.keep, bf16[2,48,2048]{2,1,0:T(8,128)(2,1)S(1)} %collective-permute-done.19.landed), custom_call_target="tpu_custom_call" | custom-call | tf_op jit(solution)/shard_map/settle/pallas_call | solution.py:815
  148.0 2.4 %forward.1 = (bf16[2,48,2048]{2,1,0:T(8,128)(2,1)S(1)}, bf16[2,48,2048]{2,1,0:T(8,128)(2,1)}) custom-call(s32[1]{0:T(128)} %bitcast.1.host, s32[1]{0:T(128)} %bitcast.2.core.refs_0_, s32[6]{0:T(128)S(1)} %stack.73.refs_0_.refs_1_, s32[4]{0:T(128)S(1)} %add_multiply_fusion.offs.refs_2_, s32[1]{0:T(128)} %bitcast.33.refs_3_.fresh, ...), custom_call_target="tpu_custom_call" | custom-call | flops 3221225472 | bytes 20971520 | tf_op jit(solution)/shard_map/forward/pallas_call | solution.py:828
  150.5 7.8 %collective-permute-done.21.rest_2_ = bf16[192,1536]{1,0:T(8,128)(2,1)} collective-permute-done((bf16[192,1536]{1,0:T(8,128)(2,1)}, bf16[192,1536]{1,0:T(8,128)(2,1)}, u32[]{:S(2)}, u32[]{:S(2)}) %collective-permute-start.21) | collective-permute-done | bytes 589856 | tf_op jit(solution)/shard_map/ppermute | solution.py:570
  164.3 1.6 message.1
  167.3 1.7 backward.3
  169.9 2.9 %collective-permute-done.26 = bf16[96,512]{1,0:T(8,128)(2,1)S(1)} collective-permute-done((bf16[96,512]{1,0:T(8,128)(2,1)S(1)}, bf16[96,512]{1,0:T(8,128)(2,1)S(1)}, u32[]{:S(2)}, u32[]{:S(2)}) %collective-permute-start.26) | collective-permute-done | bytes 98336 | tf_op jit(solution)/shard_map/ppermute | solution.py:570
  172.9 6.2 %collective-permute-done.27.message = bf16[96,1536]{1,0:T(8,128)(2,1)S(1)} collective-permute-done((bf16[96,1536]{1,0:T(8,128)(2,1)S(1)}, bf16[96,1536]{1,0:T(8,128)(2,1)S(1)}, u32[]{:S(2)}, u32[]{:S(2)}) %collective-permute-start.27) | collective-permute-done | bytes 294944 | tf_op jit(solution)/shard_map/ppermute | solution.py:564
  184.3 1.8 finish.1
  186.1 3.2 %grads.1 = f32[512,512]{1,0:T(8,128)} custom-call(s32[1]{0:T(128)} %bitcast.1.host, s32[1]{0:T(128)} %bitcast.2.core.refs_0_, s32[4]{0:T(128)S(1)} %add_multiply_fusion.offs.refs_2_, bf16[3,192,512]{2,1,0:T(8,128)(2,1)S(1)} %get-tuple-element.159.gated, bf16[192,2048]{1,0:T(8,128)(2,1)S(1)} %copy-done.2, bf16[96,2048]{1,0:T(8,128)(2,1)S(1)} %copy-done.1, ...), custom_call_target="tpu_custom_call" | custom-call | flops 402653184 | bytes 2621440 | tf_op jit(solution)/shard_map/grads/pallas_call | solution.py:917
  189.3 2.4 %collective-permute-done.29 = bf16[48,2048]{1,0:T(8,128)(2,1)S(1)} collective-permute-done((bf16[48,2048]{1,0:T(8,128)(2,1)S(1)}, bf16[48,2048]{1,0:T(8,128)(2,1)S(1)}, u32[]{:S(2)}, u32[]{:S(2)}) %collective-permute-start.29) | collective-permute-done | bytes 196640 | tf_op jit(solution)/shard_map/ppermute | solution.py:564
  (128 shorter events, 41.7 us)
Async XLA Ops:
  0.7 67.1 %copy-start.19 = (bf16[1,96,2048]{2,1,0:T(8,128)(2,1)S(1)}, bf16[1,96,2048]{2,1,0:T(8,128)(2,1)}, u32[]{:S(2)}) copy-start(bf16[1,96,2048]{2,1,0:T(8,128)(2,1)} %param.13) | copy-start | bytes 1179652
  0.7 54.0 %collective-permute-start = (bf16[512,2048]{1,0:T(8,128)(2,1)}, bf16[512,2048]{1,0:T(8,128)(2,1)S(1)}, u32[]{:S(2)}, u32[]{:S(2)}) collective-permute-start(bf16[512,2048]{1,0:T(8,128)(2,1)} %bitcast.76), channel_id=1, source_target_pairs={{4,2},{2,4},{5,3},{3,5},{12,10},{10,12},{13,11},{11,13},{20,18},{1... | collective-permute-start | bytes 6291464 | tf_op jit(solution)/shard_map/ppermute | solution.py:567
  4.8 27.4 %collective-permute-start.1 = (bf16[256,2048]{1,0:T(8,128)(2,1)}, bf16[256,2048]{1,0:T(8,128)(2,1)}, u32[]{:S(2)}, u32[]{:S(2)}) collective-permute-start(bf16[256,2048]{1,0:T(8,128)(2,1)} %get-tuple-element.166), channel_id=1, source_target_pairs={{0,2},{6,4},{1,3},{7,5},{8,10},{14,12},{9,11},{15,13},{16,18},{22,... | collective-permute-start | bytes 3145736 | tf_op jit(solution)/shard_map/ppermute | solution.py:561
  11.4 43.3 %collective-permute-start.2 = (bf16[256,2048]{1,0:T(8,128)(2,1)}, bf16[256,2048]{1,0:T(8,128)(2,1)}, u32[]{:S(2)}, u32[]{:S(2)}) collective-permute-start(bf16[256,2048]{1,0:T(8,128)(2,1)} %get-tuple-element.165), channel_id=1, source_target_pairs={{0,2},{6,4},{1,3},{7,5},{8,10},{14,12},{9,11},{15,13},{16,18},{22,... | collective-permute-start | bytes 3145736 | tf_op jit(solution)/shard_map/ppermute | solution.py:561
  13.6 56.6 %collective-permute-start.5 = (bf16[512,512]{1,0:T(8,128)(2,1)S(1)}, bf16[512,512]{1,0:T(8,128)(2,1)S(1)}, u32[]{:S(2)}, u32[]{:S(2)}) collective-permute-start(bf16[512,512]{1,0:T(8,128)(2,1)S(1)} %bitcast.70), channel_id=1, source_target_pairs={{0,2},{6,4},{1,3},{7,5},{8,10},{14,12},{9,11},{15,13},{16,18},{22,... | collective-permute-start | bytes 1572872 | tf_op jit(solution)/shard_map/ppermute | solution.py:561
  32.2 50.5 %collective-permute-start.7 = (bf16[256,2048]{1,0:T(8,128)(2,1)}, bf16[256,2048]{1,0:T(8,128)(2,1)}, u32[]{:S(2)}, u32[]{:S(2)}) collective-permute-start(bf16[256,2048]{1,0:T(8,128)(2,1)} %collective-permute-done.1.refs_8_.refs_16_.refs_11_.refs_19_), channel_id=1, source_target_pairs={{4,2},{2,4},{5,3},{3,5},{12,10},{10,12},{13,11},{11,13},{20,18},{1... | collective-permute-start | bytes 3145736 | tf_op jit(solution)/shard_map/ppermute | solution.py:567
  59.8 12.5 %collective-permute-start.6 = (s32[2,5,17]{2,0,1:T(2,128)S(1)}, s32[2,5,17]{2,0,1:T(2,128)S(1)}, u32[]{:S(2)}, u32[]{:S(2)}) collective-permute-start(s32[2,5,17]{2,0,1:T(2,128)S(1)} %add_add_fusion), channel_id=1, source_target_pairs={{0,2},{6,4},{1,3},{7,5},{8,10},{14,12},{9,11},{15,13},{16,18},{22,... | collective-permute-start | bytes 2048 | tf_op jit(solution)/shard_map/ppermute | solution.py:561
  63.9 18.0 %collective-permute-start.4 = (bf16[2,96,2048]{2,1,0:T(8,128)(2,1)}, bf16[2,96,2048]{2,1,0:T(8,128)(2,1)}, u32[]{:S(2)}, u32[]{:S(2)}) collective-permute-start(bf16[2,96,2048]{2,1,0:T(8,128)(2,1)} %bitcast.12.refs_3_.refs_11_), channel_id=1, source_target_pairs={{0,2},{6,4},{1,3},{7,5},{8,10},{14,12},{9,11},{15,13},{16,18},{22,... | collective-permute-start | bytes 2359304 | tf_op jit(solution)/shard_map/ppermute | solution.py:561
  66.1 25.5 %collective-permute-start.8 = (bf16[256,2048]{1,0:T(8,128)(2,1)}, bf16[256,2048]{1,0:T(8,128)(2,1)}, u32[]{:S(2)}, u32[]{:S(2)}) collective-permute-start(bf16[256,2048]{1,0:T(8,128)(2,1)} %collective-permute-done.2.refs_9_.refs_17_.refs_12_.refs_20_), channel_id=1, source_target_pairs={{4,2},{2,4},{5,3},{3,5},{12,10},{10,12},{13,11},{11,13},{20,18},{1... | collective-permute-start | bytes 3145736 | tf_op jit(solution)/shard_map/ppermute | solution.py:567
  70.2 20.1 %collective-permute-start.3 = (bf16[96,2048]{1,0:T(8,128)(2,1)S(1)}, bf16[96,2048]{1,0:T(8,128)(2,1)}, u32[]{:S(2)}, u32[]{:S(2)}) collective-permute-start(bf16[96,2048]{1,0:T(8,128)(2,1)S(1)} %get-tuple-element.168.refs_1_.own), channel_id=1, source_target_pairs={{0,2},{6,4},{1,3},{7,5},{8,10},{14,12},{9,11},{15,13},{16,18},{22,... | collective-permute-start | bytes 1179656 | tf_op jit(solution)/shard_map/ppermute | solution.py:561
  73.3 35.6 %collective-permute-start.12 = (bf16[512,512]{1,0:T(8,128)(2,1)S(1)}, bf16[512,512]{1,0:T(8,128)(2,1)S(1)}, u32[]{:S(2)}, u32[]{:S(2)}) collective-permute-start(bf16[512,512]{1,0:T(8,128)(2,1)S(1)} %bitcast.71), channel_id=1, source_target_pairs={{4,2},{2,4},{5,3},{3,5},{12,10},{10,12},{13,11},{11,13},{20,18},{1... | collective-permute-start | bytes 1572872 | tf_op jit(solution)/shard_map/ppermute | solution.py:567
  81.9 30.0 %collective-permute-start.13 = (bf16[512,512]{1,0:T(8,128)(2,1)S(1)}, bf16[512,512]{1,0:T(8,128)(2,1)S(1)}, u32[]{:S(2)}, u32[]{:S(2)}) collective-permute-start(bf16[512,512]{1,0:T(8,128)(2,1)S(1)} %collective-permute-done.5.rest_1_.refs_16_.refs_14_), channel_id=1, source_target_pairs={{4,2},{2,4},{5,3},{3,5},{12,10},{10,12},{13,11},{11,13},{20,18},{1... | collective-permute-start | bytes 1572872 | tf_op jit(solution)/shard_map/ppermute | solution.py:567
  82.7 24.5 %collective-permute-start.11 = (bf16[96,2048]{1,0:T(8,128)(2,1)S(1)}, bf16[96,2048]{1,0:T(8,128)(2,1)S(1)}, u32[]{:S(2)}, u32[]{:S(2)}) collective-permute-start(bf16[96,2048]{1,0:T(8,128)(2,1)S(1)} %get-tuple-element.100.up_own.own), channel_id=1, source_target_pairs={{0,2},{6,4},{1,3},{7,5},{8,10},{14,12},{9,11},{15,13},{16,18},{22,... | collective-permute-start | bytes 1179656 | tf_op jit(solution)/shard_map/ppermute | solution.py:561
  90.3 10.6 %collective-permute-start.10 = (bf16[96,512]{1,0:T(8,128)(2,1)S(1)}, bf16[96,512]{1,0:T(8,128)(2,1)S(1)}, u32[]{:S(2)}, u32[]{:S(2)}) collective-permute-start(bf16[96,512]{1,0:T(8,128)(2,1)S(1)} %constant_dynamic-slice_fusion), channel_id=1, source_target_pairs={{2,0},{4,6},{3,1},{5,7},{10,8},{12,14},{11,9},{13,15},{18,16},{20,... | collective-permute-start | bytes 294920 | tf_op jit(solution)/shard_map/ppermute | solution.py:564
  91.6 15.5 %collective-permute-start.9 = (bf16[96,2048]{1,0:T(8,128)(2,1)S(1)}, bf16[96,2048]{1,0:T(8,128)(2,1)S(1)}, u32[]{:S(2)}, u32[]{:S(2)}) collective-permute-start(bf16[96,2048]{1,0:T(8,128)(2,1)S(1)} %copy-done.16), channel_id=1, source_target_pairs={{0,2},{6,4},{1,3},{7,5},{8,10},{14,12},{9,11},{15,13},{16,18},{22,... | collective-permute-start | bytes 1179656 | tf_op jit(solution)/shard_map/ppermute | solution.py:561
  112.8 4.2 %collective-permute-start.14 = (bf16[2,48,2048]{2,1,0:T(8,128)(2,1)S(1)}, bf16[2,48,2048]{2,1,0:T(8,128)(2,1)S(1)}, u32[]{:S(2)}, u32[]{:S(2)}) collective-permute-start(bf16[2,48,2048]{2,1,0:T(8,128)(2,1)S(1)} %get-tuple-element.115), channel_id=1, source_target_pairs={{0,1},{1,0},{2,3},{3,2},{4,5},{5,4},{6,7},{7,6},{8,9},{9,8},{10,11... | collective-permute-start | bytes 1179656 | tf_op jit(solution)/shard_map/ppermute | solution.py:575
  115.7 7.3 %collective-permute-start.17 = (bf16[192,1536]{1,0:T(8,128)(2,1)S(1)}, bf16[192,1536]{1,0:T(8,128)(2,1)S(1)}, u32[]{:S(2)}, u32[]{:S(2)}) collective-permute-start(bf16[192,1536]{1,0:T(8,128)(2,1)S(1)} %get-tuple-element.129), channel_id=1, source_target_pairs={{4,2},{2,4},{5,3},{3,5},{12,10},{10,12},{13,11},{11,13},{20,18},{1... | collective-permute-start | bytes 1769480 | tf_op jit(solution)/shard_map/ppermute | solution.py:567
  118.4 21.5 %collective-permute-start.16 = (bf16[192,1536]{1,0:T(8,128)(2,1)S(1)}, bf16[192,1536]{1,0:T(8,128)(2,1)S(1)}, u32[]{:S(2)}, u32[]{:S(2)}) collective-permute-start(bf16[192,1536]{1,0:T(8,128)(2,1)S(1)} %get-tuple-element.128), channel_id=1, source_target_pairs={{2,0},{4,6},{3,1},{5,7},{10,8},{12,14},{11,9},{13,15},{18,16},{20,... | collective-permute-start | bytes 1769480 | tf_op jit(solution)/shard_map/ppermute | solution.py:564
  119.7 3.3 %collective-permute-start.15 = (bf16[2,48,2048]{2,1,0:T(8,128)(2,1)S(1)}, bf16[2,48,2048]{2,1,0:T(8,128)(2,1)}, u32[]{:S(2)}, u32[]{:S(2)}) collective-permute-start(bf16[2,48,2048]{2,1,0:T(8,128)(2,1)S(1)} %get-tuple-element.116.ahead_0), channel_id=1, source_target_pairs={{2,10},{4,12},{10,18},{12,20},{18,26},{20,28},{3,11},{5,13},{11,19... | collective-permute-start | bytes 1179656 | tf_op jit(solution)/shard_map/ppermute | solution.py:584
  140.0 2.7 %collective-permute-start.19 = (bf16[2,48,2048]{2,1,0:T(8,128)(2,1)S(1)}, bf16[2,48,2048]{2,1,0:T(8,128)(2,1)S(1)}, u32[]{:S(2)}, u32[]{:S(2)}) collective-permute-start(bf16[2,48,2048]{2,1,0:T(8,128)(2,1)S(1)} %get-tuple-element.134), channel_id=1, source_target_pairs={{0,1},{1,0},{2,3},{3,2},{4,5},{5,4},{6,7},{7,6},{8,9},{9,8},{10,11... | collective-permute-start | bytes 1179656 | tf_op jit(solution)/shard_map/ppermute | solution.py:575
  140.8 6.2 %collective-permute-start.18 = (bf16[2,48,2048]{2,1,0:T(8,128)(2,1)}, bf16[2,48,2048]{2,1,0:T(8,128)(2,1)S(1)}, u32[]{:S(2)}, u32[]{:S(2)}) collective-permute-start(bf16[2,48,2048]{2,1,0:T(8,128)(2,1)} %collective-permute-done.15.refs_4_.passed), channel_id=1, source_target_pairs={{0,1},{1,0},{2,3},{3,2},{4,5},{5,4},{6,7},{7,6},{8,9},{9,8},{10,11... | collective-permute-start | bytes 1179656 | tf_op jit(solution)/shard_map/ppermute | solution.py:575
  140.8 17.5 %collective-permute-start.21 = (bf16[192,1536]{1,0:T(8,128)(2,1)}, bf16[192,1536]{1,0:T(8,128)(2,1)}, u32[]{:S(2)}, u32[]{:S(2)}) collective-permute-start(bf16[192,1536]{1,0:T(8,128)(2,1)} %get-tuple-element.136), channel_id=1, source_target_pairs={{4,0},{2,6},{5,1},{3,7},{12,8},{10,14},{13,9},{11,15},{20,16},{18,... | collective-permute-start | bytes 1769480 | tf_op jit(solution)/shard_map/ppermute | solution.py:570
  145.6 12.7 %collective-permute-start.20 = (bf16[2,48,2048]{2,1,0:T(8,128)(2,1)}, bf16[2,48,2048]{2,1,0:T(8,128)(2,1)}, u32[]{:S(2)}, u32[]{:S(2)}) collective-permute-start(bf16[2,48,2048]{2,1,0:T(8,128)(2,1)} %get-tuple-element.135.back_0), channel_id=1, source_target_pairs={{10,2},{12,4},{18,10},{20,12},{26,18},{28,20},{11,3},{13,5},{19,11... | collective-permute-start | bytes 1179656 | tf_op jit(solution)/shard_map/ppermute | solution.py:584
  158.3 6.0 %collective-permute-start.22 = (bf16[2,48,2048]{2,1,0:T(8,128)(2,1)S(1)}, bf16[2,48,2048]{2,1,0:T(8,128)(2,1)S(1)}, u32[]{:S(2)}, u32[]{:S(2)}) collective-permute-start(bf16[2,48,2048]{2,1,0:T(8,128)(2,1)S(1)} %get-tuple-element.138), channel_id=1, source_target_pairs={{0,1},{1,0},{2,3},{3,2},{4,5},{5,4},{6,7},{7,6},{8,9},{9,8},{10,11... | collective-permute-start | bytes 1179656 | tf_op jit(solution)/shard_map/ppermute | solution.py:575
  160.9 6.3 %collective-permute-start.24 = (bf16[2,48,2048]{2,1,0:T(8,128)(2,1)S(1)}, bf16[2,48,2048]{2,1,0:T(8,128)(2,1)S(1)}, u32[]{:S(2)}, u32[]{:S(2)}) collective-permute-start(bf16[2,48,2048]{2,1,0:T(8,128)(2,1)S(1)} %get-tuple-element.140.up.refs_3_.mine), channel_id=1, source_target_pairs={{0,1},{1,0},{2,3},{3,2},{4,5},{5,4},{6,7},{7,6},{8,9},{9,8},{10,11... | collective-permute-start | bytes 1179656 | tf_op jit(solution)/shard_map/ppermute | solution.py:575
  161.0 8.9 %collective-permute-start.23 = (bf16[48,2048]{1,0:T(8,128)(2,1)S(1)}, bf16[48,2048]{1,0:T(8,128)(2,1)S(1)}, u32[]{:S(2)}, u32[]{:S(2)}) collective-permute-start(bf16[48,2048]{1,0:T(8,128)(2,1)S(1)} %copy-done.14), channel_id=1, source_target_pairs={{2,0},{4,6},{3,1},{5,7},{10,8},{12,14},{11,9},{13,15},{18,16},{20,... | collective-permute-start | bytes 589832 | tf_op jit(solution)/shard_map/ppermute | solution.py:564
  162.3 7.6 %collective-permute-start.25 = (bf16[96,512]{1,0:T(8,128)(2,1)S(1)}, bf16[96,512]{1,0:T(8,128)(2,1)S(1)}, u32[]{:S(2)}, u32[]{:S(2)}) collective-permute-start(bf16[96,512]{1,0:T(8,128)(2,1)S(1)} %get-tuple-element.146), channel_id=1, source_target_pairs={{4,2},{2,4},{5,3},{3,5},{12,10},{10,12},{13,11},{11,13},{20,18},{1... | collective-permute-start | bytes 294920 | tf_op jit(solution)/shard_map/ppermute | solution.py:567
  163.0 9.9 %collective-permute-start.26 = (bf16[96,512]{1,0:T(8,128)(2,1)S(1)}, bf16[96,512]{1,0:T(8,128)(2,1)S(1)}, u32[]{:S(2)}, u32[]{:S(2)}) collective-permute-start(bf16[96,512]{1,0:T(8,128)(2,1)S(1)} %get-tuple-element.147), channel_id=1, source_target_pairs={{4,0},{2,6},{5,1},{3,7},{12,8},{10,14},{13,9},{11,15},{20,16},{18,... | collective-permute-start | bytes 294920 | tf_op jit(solution)/shard_map/ppermute | solution.py:570
  166.0 13.1 %collective-permute-start.27 = (bf16[96,1536]{1,0:T(8,128)(2,1)S(1)}, bf16[96,1536]{1,0:T(8,128)(2,1)S(1)}, u32[]{:S(2)}, u32[]{:S(2)}) collective-permute-start(bf16[96,1536]{1,0:T(8,128)(2,1)S(1)} %get-tuple-element.148), channel_id=1, source_target_pairs={{2,0},{4,6},{3,1},{5,7},{10,8},{12,14},{11,9},{13,15},{18,16},{20,... | collective-permute-start | bytes 884744 | tf_op jit(solution)/shard_map/ppermute | solution.py:564
  179.1 2.7 %collective-permute-start.28 = (bf16[2,48,2048]{2,1,0:T(8,128)(2,1)S(1)}, bf16[2,48,2048]{2,1,0:T(8,128)(2,1)S(1)}, u32[]{:S(2)}, u32[]{:S(2)}) collective-permute-start(bf16[2,48,2048]{2,1,0:T(8,128)(2,1)S(1)} %get-tuple-element.151), channel_id=1, source_target_pairs={{0,1},{1,0},{2,3},{3,2},{4,5},{5,4},{6,7},{7,6},{8,9},{9,8},{10,11... | collective-permute-start | bytes 1179656 | tf_op jit(solution)/shard_map/ppermute | solution.py:575
  180.4 5.7 %collective-permute-start.30 = (bf16[2,96,512]{2,1,0:T(8,128)(2,1)S(1)}, bf16[2,96,512]{2,1,0:T(8,128)(2,1)S(1)}, u32[]{:S(2)}, u32[]{:S(2)}) collective-permute-start(bf16[2,96,512]{2,1,0:T(8,128)(2,1)S(1)} %pad_maximum_fusion.halves), channel_id=1, source_target_pairs={{0,1},{1,0},{2,3},{3,2},{4,5},{5,4},{6,7},{7,6},{8,9},{9,8},{10,11... | collective-permute-start | bytes 589832 | tf_op jit(solution)/shard_map/ppermute | solution.py:575
  183.0 8.7 %collective-permute-start.29 = (bf16[48,2048]{1,0:T(8,128)(2,1)S(1)}, bf16[48,2048]{1,0:T(8,128)(2,1)S(1)}, u32[]{:S(2)}, u32[]{:S(2)}) collective-permute-start(bf16[48,2048]{1,0:T(8,128)(2,1)S(1)} %get-tuple-element.158), channel_id=1, source_target_pairs={{2,0},{4,6},{3,1},{5,7},{10,8},{12,14},{11,9},{13,15},{18,16},{20,... | collective-permute-start | bytes 589832 | tf_op jit(solution)/shard_map/ppermute | solution.py:564
  (23 other events, 344.2 us)

commit v19 on v18

--- a/solution.py
+++ b/solution.py
@@ -235,7 +235,7 @@
     early, rest = (rest[0], rest[1:]) if skip else (None, rest)
     sources, rest = (None,) + rest[:count], rest[count:]
     send, keep = rest[:2]
-    held, (grad_normed, scaled, part, begun, up_sems, sems) = (
+    held, (grad_normed, part, begun, up_sems, sems) = (
         rest[2 : 3 + count],
         rest[3 + count :],
     )
@@ -271,8 +271,6 @@
         )
     first = list(range(9, 9 + n))
     second = [1, 4, 2, 5, 6, 3]
-    for i in (7, 8):
-        copies[i].start()
     for copy in up_copies:
         copy.start()
     for i in first + second:
@@ -280,6 +278,8 @@
     for of_head in by_head:
         for copy in of_head:
             copy.start()
+    for i in (7, 8):
+        copies[i].start()
     if split:
         share = up_sources[0].shape[1]
         cores = ups.shape[0] // (2 * share)
@@ -287,12 +287,6 @@
             for r in range(2):
                 at = pl.multiple_of((r * cores + owner) * share, share)
                 ups[pl.ds(at, share), :] = up_sources[half][r]
-    roots = []
-    for i, source in ((7, x_own), (8, x_theirs)):
-        copies[i].wait()
-        floats = source[...].astype(F32)
-        roots.append(row_root(floats))
-        scaled[pl.ds((i - 7) * source.shape[0], source.shape[0]), :] = floats * roots[-1]
     for copy in up_copies:
         copy.wait()
     depth = out_parts[0].shape[1]
@@ -342,12 +336,15 @@
             else:
                 grad_normed[:, columns] += term
         grad_pre = following
-    for r, root in enumerate(roots):
+    for r, source in enumerate((x_own, x_theirs)):
+        copies[7 + r].wait()
         rows = pl.ds(r * length, length)
-        scaled_rows = scaled[rows, :]
+        floats = source[...].astype(F32)
+        root = row_root(floats)
+        scaled = floats * root
         grad_n = grad_normed[rows, :]
-        mean = jnp.mean(grad_n * scaled_rows, axis=-1, keepdims=True)
-        part[rows, :] = (root * (grad_n - scaled_rows * mean)).astype(BF16)
+        mean = jnp.mean(grad_n * scaled, axis=-1, keepdims=True)
+        part[rows, :] = (root * (grad_n - scaled * mean)).astype(BF16)
     split_rows(core[0], part, send, keep)
 
 
@@ -410,11 +407,6 @@
         total[r] = (
             source[here, :].astype(F32) + keep[r].astype(F32) + landed[r].astype(F32)
         ).astype(BF16)
-
-
-def settle_two_kernel(core, own, theirs, keep, landed, total, other):
-    settle_kernel(core, own, theirs, keep, landed, total)
-    other[...] = total[1]
 
 
 def first_kernel(core, own, theirs, keep, landed, gated, total, pack):
@@ -740,7 +732,6 @@
             + [pltpu.VMEM(x.shape, x.dtype) for x in plain]
             + [
                 pltpu.VMEM((rows, width), F32),
-                pltpu.VMEM((rows, width), F32),
                 pltpu.VMEM((rows, width), BF16),
                 pltpu.VMEM((rows, slab), F32),
                 pltpu.SemaphoreType.DMA((2,)),
@@ -811,13 +802,12 @@
         (back_send, back_keep, ahead_in, packs_near)
     )
     back_landed = swap_cores(back_send)
-    settled = [halves[0], struct((share, width), BF16)]
-    back_0, back_given = pl.pallas_call(
-        settle_two_kernel,
+    back_0 = pl.pallas_call(
+        settle_kernel,
         grid=(1,),
         in_specs=[smem] + all_of(up_own, up_theirs, back_keep, back_landed),
-        out_specs=all_of(*settled),
-        out_shape=settled,
+        out_specs=all_of(halves[0])[0],
+        out_shape=halves[0],
         compiler_params=small,
         name="settle",
     )(core, *in_hbm([up_own, up_theirs, back_keep]), back_landed)
@@ -887,7 +877,7 @@
     )(core, offs, first_flag, *in_hbm(message_inputs[:4]), *message_inputs[4:])
     landed = landed + [to_partner(message)]
     back_send, back_keep = backward([up_mine, up_their], 1)
-    back_given = to_partner(back_given)
+    back_given = to_partner(back_0[1])
     back_given, back_send, back_keep, landed = lax.optimization_barrier(
         (back_given, back_send, back_keep, landed)
     )

time: 195 us -> 195 us (level)
  waiting for transfers between devices: 88.8 us -> 92 us
  Pallas kernels: 26.6 us -> 24.5 us
  transfers between devices with their start and end apart: 31 -> 31, of which waited for: 14 -> 13; matrix products, arithmetic and copies ran while one was open for 8% -> 8% of each run, Pallas kernels for 13% -> 12%
where the time goes in v19:
time: 195 us; the launch traced here: 192 us
  waiting for transfers between devices  92 us (47%)
  starting transfers between devices  54.7 us (28%)
  Pallas kernels  24.5 us (13%)
  local copies, waits for them, and re-layouts  10.4 us (5%)
  other arithmetic  7.49 us (4%)
  between operations  3.23 us (2%)
    ppermute x8, waiting for transfers between devices, from_partner(): return lax.ppermute(x, 'dp', [(h ^ 1, h) for h in hosts])  50.2 us
    ppermute x8, starting transfers between devices, from_partner(): return lax.ppermute(x, 'dp', [(h ^ 1, h) for h in hosts])  28.8 us
    ppermute x5, waiting for transfers between devices, to_partner(): return lax.ppermute(x, 'dp', [(h, h ^ 1) for h in hosts])  26.9 us
    ppermute x2, waiting for transfers between devices, to_beyond(): lax.ppermute(x, 'dp', [(hosts[k ^ m], hosts[k] ^ 1) for k in range(n // 2)])  12.5 us
    ppermute x7, starting transfers between devices, from_host(): lax.ppermute(x, 'dp', [(hosts[k ^ m], hosts[k]) for k in range(n // 2)])  7.09 us
    ppermute x7, starting transfers between devices, swap_cores(): return lax.ppermute(x, 'cores', [(c, cores - 1 - c) for c in range(cores)])  6.71 us
    ppermute x5, starting transfers between devices, to_partner(): return lax.ppermute(x, 'dp', [(h, h ^ 1) for h in hosts])  6.45 us
  transfers between devices with their start and end apart: 31, of which 13 were waited for; matrix products, arithmetic and copies ran while one was open for 8% of the time, Pallas kernels for 12%

profile of v19, /device:TPU:5, one launch (start us, length us, event | category | flops | bytes accessed | tf_op | source)
XLA Modules:
  0.0 192.2 jit_solution(17010828121445420602)
XLA Ops:
  1.6 3.2 %slice_bitcast_fusion = (bf16[256,2048]{1,0:T(8,128)(2,1)}, bf16[256,2048]{1,0:T(8,128)(2,1)}) fusion(bf16[1,512,2048]{2,1,0:T(8,128)(2,1)} %param.17), kind=kLoop, calls=%fused_computation | loop fusion | bytes 4194304 | tf_op jit(solution)/shard_map/slice | solution.py:586
  4.8 6.6 %collective-permute-start.1 = (bf16[256,2048]{1,0:T(8,128)(2,1)}, bf16[256,2048]{1,0:T(8,128)(2,1)}, u32[]{:S(2)}, u32[]{:S(2)}) collective-permute-start(bf16[256,2048]{1,0:T(8,128)(2,1)} %get-tuple-element.162), channel_id=1, source_target_pairs={{0,2},{6,4},{1,3},{7,5},{8,10},{14,12},{9,11},{15,13},{16,18},{22,... | collective-permute-start | bytes 3145736 | tf_op jit(solution)/shard_map/ppermute | solution.py:553
  11.4 2.2 %collective-permute-start.2 = (bf16[256,2048]{1,0:T(8,128)(2,1)}, bf16[256,2048]{1,0:T(8,128)(2,1)}, u32[]{:S(2)}, u32[]{:S(2)}) collective-permute-start(bf16[256,2048]{1,0:T(8,128)(2,1)} %get-tuple-element.161), channel_id=1, source_target_pairs={{0,2},{6,4},{1,3},{7,5},{8,10},{14,12},{9,11},{15,13},{16,18},{22,... | collective-permute-start | bytes 3145736 | tf_op jit(solution)/shard_map/ppermute | solution.py:553
  19.7 12.5 %collective-permute-done.1.refs_8_.refs_16_.refs_11_.refs_19_ = bf16[256,2048]{1,0:T(8,128)(2,1)} collective-permute-done((bf16[256,2048]{1,0:T(8,128)(2,1)}, bf16[256,2048]{1,0:T(8,128)(2,1)}, u32[]{:S(2)}, u32[]{:S(2)}) %collective-permute-start.1) | collective-permute-done | bytes 1048608 | tf_op jit(solution)/shard_map/ppermute | solution.py:553
  32.2 1.6 collective-permute-start.7
  33.8 20.8 %collective-permute-done.2.refs_9_.refs_17_.refs_12_.refs_20_ = bf16[256,2048]{1,0:T(8,128)(2,1)} collective-permute-done((bf16[256,2048]{1,0:T(8,128)(2,1)}, bf16[256,2048]{1,0:T(8,128)(2,1)}, u32[]{:S(2)}, u32[]{:S(2)}) %collective-permute-start.2) | collective-permute-done | bytes 1048608 | tf_op jit(solution)/shard_map/ppermute | solution.py:553
  59.8 4.1 %collective-permute-start.6 = (s32[2,5,17]{2,0,1:T(2,128)S(1)}, s32[2,5,17]{2,0,1:T(2,128)S(1)}, u32[]{:S(2)}, u32[]{:S(2)}) collective-permute-start(s32[2,5,17]{2,0,1:T(2,128)S(1)} %add_add_fusion), channel_id=1, source_target_pairs={{0,2},{6,4},{1,3},{7,5},{8,10},{14,12},{9,11},{15,13},{16,18},{22,... | collective-permute-start | bytes 2048 | tf_op jit(solution)/shard_map/ppermute | solution.py:553
  63.9 2.2 %collective-permute-start.4 = (bf16[2,96,2048]{2,1,0:T(8,128)(2,1)}, bf16[2,96,2048]{2,1,0:T(8,128)(2,1)}, u32[]{:S(2)}, u32[]{:S(2)}) collective-permute-start(bf16[2,96,2048]{2,1,0:T(8,128)(2,1)} %bitcast.12.refs_3_.refs_11_), channel_id=1, source_target_pairs={{0,2},{6,4},{1,3},{7,5},{8,10},{14,12},{9,11},{15,13},{16,18},{22,... | collective-permute-start | bytes 2359304 | tf_op jit(solution)/shard_map/ppermute | solution.py:553
  66.1 2.4 %select_bitcast_fusion = (bf16[96,2048]{1,0:T(8,128)(2,1)}, bf16[96,2048]{1,0:T(8,128)(2,1)S(1)}, bf16[96,2048]{1,0:T(8,128)(2,1)S(1)}) fusion(bf16[2,96,2048]{2,1,0:T(8,128)(2,1)} %param.14, bf16[2,96,2048]{2,1,0:T(8,128)(2,1)} %param.12, pred[]{:T(512)S(6)} %eq.44, bf16[1,96,2048]{2,1,0:T(8,128)(2,1)S(1)} %copy-done.19, bf16[1,96,2048]{2,1,0:T(8,128)(2,1)} %param.15, ...), kind=kLoop, calls=%fused_computation.6 | loop fusion | flops 589824 | bytes 3538946 | tf_op jit(solution)/shard_map/jit(_where)/select_n | solution.py:614
  68.5 2.1 %collective-permute-start.3 = (bf16[96,2048]{1,0:T(8,128)(2,1)S(1)}, bf16[96,2048]{1,0:T(8,128)(2,1)}, u32[]{:S(2)}, u32[]{:S(2)}) collective-permute-start(bf16[96,2048]{1,0:T(8,128)(2,1)S(1)} %get-tuple-element.164.refs_1_.own), channel_id=1, source_target_pairs={{0,2},{6,4},{1,3},{7,5},{8,10},{14,12},{9,11},{15,13},{16,18},{22,... | collective-permute-start | bytes 1179656 | tf_op jit(solution)/shard_map/ppermute | solution.py:553
  70.5 1.7 collective-permute-start.8
  74.6 7.4 %collective-permute-done.4.refs_4_.refs_12_ = bf16[2,96,2048]{2,1,0:T(8,128)(2,1)} collective-permute-done((bf16[2,96,2048]{2,1,0:T(8,128)(2,1)}, bf16[2,96,2048]{2,1,0:T(8,128)(2,1)}, u32[]{:S(2)}, u32[]{:S(2)}) %collective-permute-start.4) | collective-permute-done | bytes 786464 | tf_op jit(solution)/shard_map/ppermute | solution.py:553
  82.7 5.5 %collective-permute-start.11 = (bf16[96,2048]{1,0:T(8,128)(2,1)S(1)}, bf16[96,2048]{1,0:T(8,128)(2,1)S(1)}, u32[]{:S(2)}, u32[]{:S(2)}) collective-permute-start(bf16[96,2048]{1,0:T(8,128)(2,1)S(1)} %get-tuple-element.98.up_own.own), channel_id=1, source_target_pairs={{0,2},{6,4},{1,3},{7,5},{8,10},{14,12},{9,11},{15,13},{16,18},{22,... | collective-permute-start | bytes 1179656 | tf_op jit(solution)/shard_map/ppermute | solution.py:553
  88.2 2.1 %collective-permute-done.3.refs_2_.theirs = bf16[96,2048]{1,0:T(8,128)(2,1)} collective-permute-done((bf16[96,2048]{1,0:T(8,128)(2,1)S(1)}, bf16[96,2048]{1,0:T(8,128)(2,1)}, u32[]{:S(2)}, u32[]{:S(2)}) %collective-permute-start.3) | collective-permute-done | bytes 393248 | tf_op jit(solution)/shard_map/ppermute | solution.py:553
  91.6 4.8 %collective-permute-start.9 = (bf16[96,2048]{1,0:T(8,128)(2,1)S(1)}, bf16[96,2048]{1,0:T(8,128)(2,1)S(1)}, u32[]{:S(2)}, u32[]{:S(2)}) collective-permute-start(bf16[96,2048]{1,0:T(8,128)(2,1)S(1)} %copy-done.16), channel_id=1, source_target_pairs={{0,2},{6,4},{1,3},{7,5},{8,10},{14,12},{9,11},{15,13},{16,18},{22,... | collective-permute-start | bytes 1179656 | tf_op jit(solution)/shard_map/ppermute | solution.py:553
  97.4 2.2 %project.1 = (bf16[3,192,512]{2,1,0:T(8,128)(2,1)S(1)}, f32[2,192,512]{2,1,0:T(8,128)}, bf16[2,192,1536]{2,1,0:T(8,128)(2,1)}, f32[2,192,2048]{2,1,0:T(8,128)}, ...) custom-call(s32[1]{0:T(128)} %bitcast.1.host, s32[6]{0:T(128)S(1)} %stack.73.refs_0_.refs_1_, ...), custom_call_target="tpu_custom_call" | custom-call | flops 4831838208 | bytes 20971520 | tf_op jit(solution)/shard_map/project/pallas_call | solution.py:696
  99.6 7.5 %collective-permute-done.9.refs_7_.new_theirs = bf16[96,2048]{1,0:T(8,128)(2,1)S(1)} collective-permute-done((bf16[96,2048]{1,0:T(8,128)(2,1)S(1)}, bf16[96,2048]{1,0:T(8,128)(2,1)S(1)}, u32[]{:S(2)}, u32[]{:S(2)}) %collective-permute-start.9) | collective-permute-done | bytes 393248 | tf_op jit(solution)/shard_map/ppermute | solution.py:553
  107.1 1.7 pack.1
  108.9 3.1 %early.1 = (bf16[192,2048]{1,0:T(8,128)(2,1)S(1)}, f32[192,512]{1,0:T(8,128)}) custom-call(s32[4]{0:T(128)S(1)} %add_multiply_fusion.offs.refs_2_, bf16[3,192,512]{2,1,0:T(8,128)(2,1)S(1)} %get-tuple-element.155.gated, bf16[192,2048]{1,0:T(8,128)(2,1)} %get-tuple-element.116.upstream.refs_3_.up_0, bf16[512,512]{1,0:T(8,128)(2,1)S(1)} %bitcast.74, ...), custom_call_target="tpu_custom_call" | custom-call | tf_op jit(solution)/shard_map/early/pallas_call | solution.py:762
  112.8 2.9 %collective-permute-start.14 = (bf16[2,48,2048]{2,1,0:T(8,128)(2,1)S(1)}, bf16[2,48,2048]{2,1,0:T(8,128)(2,1)S(1)}, u32[]{:S(2)}, u32[]{:S(2)}) collective-permute-start(bf16[2,48,2048]{2,1,0:T(8,128)(2,1)S(1)} %get-tuple-element.113), channel_id=1, source_target_pairs={{0,1},{1,0},{2,3},{3,2},{4,5},{5,4},{6,7},{7,6},{8,9},{9,8},{10,11... | collective-permute-start | bytes 1179656 | tf_op jit(solution)/shard_map/ppermute | solution.py:567
  121.2 1.6 backward.2
  122.9 17.1 %collective-permute-done.16.pack.rest_0_ = bf16[192,1536]{1,0:T(8,128)(2,1)S(1)} collective-permute-done((bf16[192,1536]{1,0:T(8,128)(2,1)S(1)}, bf16[192,1536]{1,0:T(8,128)(2,1)S(1)}, u32[]{:S(2)}, u32[]{:S(2)}) %collective-permute-start.16) | collective-permute-done | bytes 589856 | tf_op jit(solution)/shard_map/ppermute | solution.py:556
  140.8 1.5 collective-permute-start.21
  146.5 2.4 %forward.1 = (bf16[2,48,2048]{2,1,0:T(8,128)(2,1)S(1)}, bf16[2,48,2048]{2,1,0:T(8,128)(2,1)}) custom-call(s32[1]{0:T(128)} %bitcast.1.host, s32[1]{0:T(128)} %bitcast.2.core.refs_0_, s32[6]{0:T(128)S(1)} %stack.73.refs_0_.refs_1_, s32[4]{0:T(128)S(1)} %add_multiply_fusion.offs.refs_2_, s32[1]{0:T(128)} %bitcast.33.refs_3_.fresh, ...), custom_call_target="tpu_custom_call" | custom-call | flops 3221225472 | bytes 20971520 | tf_op jit(solution)/shard_map/forward/pallas_call | solution.py:818
  148.9 9.3 %collective-permute-done.21.rest_2_ = bf16[192,1536]{1,0:T(8,128)(2,1)} collective-permute-done((bf16[192,1536]{1,0:T(8,128)(2,1)}, bf16[192,1536]{1,0:T(8,128)(2,1)}, u32[]{:S(2)}, u32[]{:S(2)}) %collective-permute-start.21) | collective-permute-done | bytes 589856 | tf_op jit(solution)/shard_map/ppermute | solution.py:562
  164.4 1.6 message.1
  167.3 1.7 backward.3
  169.0 3.2 %collective-permute-done.26 = bf16[96,512]{1,0:T(8,128)(2,1)S(1)} collective-permute-done((bf16[96,512]{1,0:T(8,128)(2,1)S(1)}, bf16[96,512]{1,0:T(8,128)(2,1)S(1)}, u32[]{:S(2)}, u32[]{:S(2)}) %collective-permute-start.26) | collective-permute-done | bytes 98336 | tf_op jit(solution)/shard_map/ppermute | solution.py:562
  172.2 6.2 %collective-permute-done.27.message = bf16[96,1536]{1,0:T(8,128)(2,1)S(1)} collective-permute-done((bf16[96,1536]{1,0:T(8,128)(2,1)S(1)}, bf16[96,1536]{1,0:T(8,128)(2,1)S(1)}, u32[]{:S(2)}, u32[]{:S(2)}) %collective-permute-start.27) | collective-permute-done | bytes 294944 | tf_op jit(solution)/shard_map/ppermute | solution.py:556
  178.4 1.4 collective-permute-start.28
  184.6 3.2 %grads.1 = f32[512,512]{1,0:T(8,128)} custom-call(s32[1]{0:T(128)} %bitcast.1.host, s32[1]{0:T(128)} %bitcast.2.core.refs_0_, s32[4]{0:T(128)S(1)} %add_multiply_fusion.offs.refs_2_, bf16[3,192,512]{2,1,0:T(8,128)(2,1)S(1)} %get-tuple-element.155.gated, bf16[192,2048]{1,0:T(8,128)(2,1)S(1)} %copy-done.2, bf16[96,2048]{1,0:T(8,128)(2,1)S(1)} %copy-done.1, ...), custom_call_target="tpu_custom_call" | custom-call | flops 402653184 | bytes 2621440 | tf_op jit(solution)/shard_map/grads/pallas_call | solution.py:907
  187.8 3.6 %collective-permute-done.29 = bf16[48,2048]{1,0:T(8,128)(2,1)S(1)} collective-permute-done((bf16[48,2048]{1,0:T(8,128)(2,1)S(1)}, bf16[48,2048]{1,0:T(8,128)(2,1)S(1)}, u32[]{:S(2)}, u32[]{:S(2)}) %collective-permute-start.29) | collective-permute-done | bytes 196640 | tf_op jit(solution)/shard_map/ppermute | solution.py:556
  (129 shorter events, 39.7 us)
Async XLA Ops:
  0.7 65.4 %copy-start.19 = (bf16[1,96,2048]{2,1,0:T(8,128)(2,1)S(1)}, bf16[1,96,2048]{2,1,0:T(8,128)(2,1)}, u32[]{:S(2)}) copy-start(bf16[1,96,2048]{2,1,0:T(8,128)(2,1)} %param.13) | copy-start | bytes 1179652
  0.7 54.0 %collective-permute-start = (bf16[512,2048]{1,0:T(8,128)(2,1)}, bf16[512,2048]{1,0:T(8,128)(2,1)S(1)}, u32[]{:S(2)}, u32[]{:S(2)}) collective-permute-start(bf16[512,2048]{1,0:T(8,128)(2,1)} %bitcast.78), channel_id=1, source_target_pairs={{4,2},{2,4},{5,3},{3,5},{12,10},{10,12},{13,11},{11,13},{20,18},{1... | collective-permute-start | bytes 6291464 | tf_op jit(solution)/shard_map/ppermute | solution.py:559
  4.8 27.4 %collective-permute-start.1 = (bf16[256,2048]{1,0:T(8,128)(2,1)}, bf16[256,2048]{1,0:T(8,128)(2,1)}, u32[]{:S(2)}, u32[]{:S(2)}) collective-permute-start(bf16[256,2048]{1,0:T(8,128)(2,1)} %get-tuple-element.162), channel_id=1, source_target_pairs={{0,2},{6,4},{1,3},{7,5},{8,10},{14,12},{9,11},{15,13},{16,18},{22,... | collective-permute-start | bytes 3145736 | tf_op jit(solution)/shard_map/ppermute | solution.py:553
  11.4 43.3 %collective-permute-start.2 = (bf16[256,2048]{1,0:T(8,128)(2,1)}, bf16[256,2048]{1,0:T(8,128)(2,1)}, u32[]{:S(2)}, u32[]{:S(2)}) collective-permute-start(bf16[256,2048]{1,0:T(8,128)(2,1)} %get-tuple-element.161), channel_id=1, source_target_pairs={{0,2},{6,4},{1,3},{7,5},{8,10},{14,12},{9,11},{15,13},{16,18},{22,... | collective-permute-start | bytes 3145736 | tf_op jit(solution)/shard_map/ppermute | solution.py:553
  13.6 56.9 %collective-permute-start.5 = (bf16[512,512]{1,0:T(8,128)(2,1)S(1)}, bf16[512,512]{1,0:T(8,128)(2,1)S(1)}, u32[]{:S(2)}, u32[]{:S(2)}) collective-permute-start(bf16[512,512]{1,0:T(8,128)(2,1)S(1)} %bitcast.72), channel_id=1, source_target_pairs={{0,2},{6,4},{1,3},{7,5},{8,10},{14,12},{9,11},{15,13},{16,18},{22,... | collective-permute-start | bytes 1572872 | tf_op jit(solution)/shard_map/ppermute | solution.py:553
  32.2 50.5 %collective-permute-start.7 = (bf16[256,2048]{1,0:T(8,128)(2,1)}, bf16[256,2048]{1,0:T(8,128)(2,1)}, u32[]{:S(2)}, u32[]{:S(2)}) collective-permute-start(bf16[256,2048]{1,0:T(8,128)(2,1)} %collective-permute-done.1.refs_8_.refs_16_.refs_11_.refs_19_), channel_id=1, source_target_pairs={{4,2},{2,4},{5,3},{3,5},{12,10},{10,12},{13,11},{11,13},{20,18},{1... | collective-permute-start | bytes 3145736 | tf_op jit(solution)/shard_map/ppermute | solution.py:559
  59.8 12.4 %collective-permute-start.6 = (s32[2,5,17]{2,0,1:T(2,128)S(1)}, s32[2,5,17]{2,0,1:T(2,128)S(1)}, u32[]{:S(2)}, u32[]{:S(2)}) collective-permute-start(s32[2,5,17]{2,0,1:T(2,128)S(1)} %add_add_fusion), channel_id=1, source_target_pairs={{0,2},{6,4},{1,3},{7,5},{8,10},{14,12},{9,11},{15,13},{16,18},{22,... | collective-permute-start | bytes 2048 | tf_op jit(solution)/shard_map/ppermute | solution.py:553
  63.9 18.0 %collective-permute-start.4 = (bf16[2,96,2048]{2,1,0:T(8,128)(2,1)}, bf16[2,96,2048]{2,1,0:T(8,128)(2,1)}, u32[]{:S(2)}, u32[]{:S(2)}) collective-permute-start(bf16[2,96,2048]{2,1,0:T(8,128)(2,1)} %bitcast.12.refs_3_.refs_11_), channel_id=1, source_target_pairs={{0,2},{6,4},{1,3},{7,5},{8,10},{14,12},{9,11},{15,13},{16,18},{22,... | collective-permute-start | bytes 2359304 | tf_op jit(solution)/shard_map/ppermute | solution.py:553
  68.5 21.8 %collective-permute-start.3 = (bf16[96,2048]{1,0:T(8,128)(2,1)S(1)}, bf16[96,2048]{1,0:T(8,128)(2,1)}, u32[]{:S(2)}, u32[]{:S(2)}) collective-permute-start(bf16[96,2048]{1,0:T(8,128)(2,1)S(1)} %get-tuple-element.164.refs_1_.own), channel_id=1, source_target_pairs={{0,2},{6,4},{1,3},{7,5},{8,10},{14,12},{9,11},{15,13},{16,18},{22,... | collective-permute-start | bytes 1179656 | tf_op jit(solution)/shard_map/ppermute | solution.py:553
  70.5 21.0 %collective-permute-start.8 = (bf16[256,2048]{1,0:T(8,128)(2,1)}, bf16[256,2048]{1,0:T(8,128)(2,1)}, u32[]{:S(2)}, u32[]{:S(2)}) collective-permute-start(bf16[256,2048]{1,0:T(8,128)(2,1)} %collective-permute-done.2.refs_9_.refs_17_.refs_12_.refs_20_), channel_id=1, source_target_pairs={{4,2},{2,4},{5,3},{3,5},{12,10},{10,12},{13,11},{11,13},{20,18},{1... | collective-permute-start | bytes 3145736 | tf_op jit(solution)/shard_map/ppermute | solution.py:559
  73.3 35.6 %collective-permute-start.12 = (bf16[512,512]{1,0:T(8,128)(2,1)S(1)}, bf16[512,512]{1,0:T(8,128)(2,1)S(1)}, u32[]{:S(2)}, u32[]{:S(2)}) collective-permute-start(bf16[512,512]{1,0:T(8,128)(2,1)S(1)} %bitcast.73), channel_id=1, source_target_pairs={{4,2},{2,4},{5,3},{3,5},{12,10},{10,12},{13,11},{11,13},{20,18},{1... | collective-permute-start | bytes 1572872 | tf_op jit(solution)/shard_map/ppermute | solution.py:559
  81.9 30.0 %collective-permute-start.13 = (bf16[512,512]{1,0:T(8,128)(2,1)S(1)}, bf16[512,512]{1,0:T(8,128)(2,1)S(1)}, u32[]{:S(2)}, u32[]{:S(2)}) collective-permute-start(bf16[512,512]{1,0:T(8,128)(2,1)S(1)} %collective-permute-done.5.rest_1_.refs_16_.refs_14_), channel_id=1, source_target_pairs={{4,2},{2,4},{5,3},{3,5},{12,10},{10,12},{13,11},{11,13},{20,18},{1... | collective-permute-start | bytes 1572872 | tf_op jit(solution)/shard_map/ppermute | solution.py:559
  82.7 24.5 %collective-permute-start.11 = (bf16[96,2048]{1,0:T(8,128)(2,1)S(1)}, bf16[96,2048]{1,0:T(8,128)(2,1)S(1)}, u32[]{:S(2)}, u32[]{:S(2)}) collective-permute-start(bf16[96,2048]{1,0:T(8,128)(2,1)S(1)} %get-tuple-element.98.up_own.own), channel_id=1, source_target_pairs={{0,2},{6,4},{1,3},{7,5},{8,10},{14,12},{9,11},{15,13},{16,18},{22,... | collective-permute-start | bytes 1179656 | tf_op jit(solution)/shard_map/ppermute | solution.py:553
  90.3 9.4 %collective-permute-start.10 = (bf16[96,512]{1,0:T(8,128)(2,1)S(1)}, bf16[96,512]{1,0:T(8,128)(2,1)S(1)}, u32[]{:S(2)}, u32[]{:S(2)}) collective-permute-start(bf16[96,512]{1,0:T(8,128)(2,1)S(1)} %constant_dynamic-slice_fusion), channel_id=1, source_target_pairs={{2,0},{4,6},{3,1},{5,7},{10,8},{12,14},{11,9},{13,15},{18,16},{20,... | collective-permute-start | bytes 294920 | tf_op jit(solution)/shard_map/ppermute | solution.py:556
  91.6 15.5 %collective-permute-start.9 = (bf16[96,2048]{1,0:T(8,128)(2,1)S(1)}, bf16[96,2048]{1,0:T(8,128)(2,1)S(1)}, u32[]{:S(2)}, u32[]{:S(2)}) collective-permute-start(bf16[96,2048]{1,0:T(8,128)(2,1)S(1)} %copy-done.16), channel_id=1, source_target_pairs={{0,2},{6,4},{1,3},{7,5},{8,10},{14,12},{9,11},{15,13},{16,18},{22,... | collective-permute-start | bytes 1179656 | tf_op jit(solution)/shard_map/ppermute | solution.py:553
  112.8 4.2 %collective-permute-start.14 = (bf16[2,48,2048]{2,1,0:T(8,128)(2,1)S(1)}, bf16[2,48,2048]{2,1,0:T(8,128)(2,1)S(1)}, u32[]{:S(2)}, u32[]{:S(2)}) collective-permute-start(bf16[2,48,2048]{2,1,0:T(8,128)(2,1)S(1)} %get-tuple-element.113), channel_id=1, source_target_pairs={{0,1},{1,0},{2,3},{3,2},{4,5},{5,4},{6,7},{7,6},{8,9},{9,8},{10,11... | collective-permute-start | bytes 1179656 | tf_op jit(solution)/shard_map/ppermute | solution.py:567
  115.7 7.1 %collective-permute-start.17 = (bf16[192,1536]{1,0:T(8,128)(2,1)S(1)}, bf16[192,1536]{1,0:T(8,128)(2,1)S(1)}, u32[]{:S(2)}, u32[]{:S(2)}) collective-permute-start(bf16[192,1536]{1,0:T(8,128)(2,1)S(1)} %get-tuple-element.127), channel_id=1, source_target_pairs={{4,2},{2,4},{5,3},{3,5},{12,10},{10,12},{13,11},{11,13},{20,18},{1... | collective-permute-start | bytes 1769480 | tf_op jit(solution)/shard_map/ppermute | solution.py:559
  118.4 21.5 %collective-permute-start.16 = (bf16[192,1536]{1,0:T(8,128)(2,1)S(1)}, bf16[192,1536]{1,0:T(8,128)(2,1)S(1)}, u32[]{:S(2)}, u32[]{:S(2)}) collective-permute-start(bf16[192,1536]{1,0:T(8,128)(2,1)S(1)} %get-tuple-element.126), channel_id=1, source_target_pairs={{2,0},{4,6},{3,1},{5,7},{10,8},{12,14},{11,9},{13,15},{18,16},{20,... | collective-permute-start | bytes 1769480 | tf_op jit(solution)/shard_map/ppermute | solution.py:556
  119.7 3.1 %collective-permute-start.15 = (bf16[2,48,2048]{2,1,0:T(8,128)(2,1)S(1)}, bf16[2,48,2048]{2,1,0:T(8,128)(2,1)}, u32[]{:S(2)}, u32[]{:S(2)}) collective-permute-start(bf16[2,48,2048]{2,1,0:T(8,128)(2,1)S(1)} %get-tuple-element.114.ahead_0), channel_id=1, source_target_pairs={{2,10},{4,12},{10,18},{12,20},{18,26},{20,28},{3,11},{5,13},{11,19... | collective-permute-start | bytes 1179656 | tf_op jit(solution)/shard_map/ppermute | solution.py:576
  140.0 2.7 %collective-permute-start.19 = (bf16[2,48,2048]{2,1,0:T(8,128)(2,1)S(1)}, bf16[2,48,2048]{2,1,0:T(8,128)(2,1)S(1)}, u32[]{:S(2)}, u32[]{:S(2)}) collective-permute-start(bf16[2,48,2048]{2,1,0:T(8,128)(2,1)S(1)} %get-tuple-element.132), channel_id=1, source_target_pairs={{0,1},{1,0},{2,3},{3,2},{4,5},{5,4},{6,7},{7,6},{8,9},{9,8},{10,11... | collective-permute-start | bytes 1179656 | tf_op jit(solution)/shard_map/ppermute | solution.py:567
  140.8 4.7 %collective-permute-start.18 = (bf16[2,48,2048]{2,1,0:T(8,128)(2,1)}, bf16[2,48,2048]{2,1,0:T(8,128)(2,1)S(1)}, u32[]{:S(2)}, u32[]{:S(2)}) collective-permute-start(bf16[2,48,2048]{2,1,0:T(8,128)(2,1)} %collective-permute-done.15.refs_4_.passed), channel_id=1, source_target_pairs={{0,1},{1,0},{2,3},{3,2},{4,5},{5,4},{6,7},{7,6},{8,9},{9,8},{10,11... | collective-permute-start | bytes 1179656 | tf_op jit(solution)/shard_map/ppermute | solution.py:567
  140.8 17.5 %collective-permute-start.21 = (bf16[192,1536]{1,0:T(8,128)(2,1)}, bf16[192,1536]{1,0:T(8,128)(2,1)}, u32[]{:S(2)}, u32[]{:S(2)}) collective-permute-start(bf16[192,1536]{1,0:T(8,128)(2,1)} %get-tuple-element.133), channel_id=1, source_target_pairs={{4,0},{2,6},{5,1},{3,7},{12,8},{10,14},{13,9},{11,15},{20,16},{18,... | collective-permute-start | bytes 1769480 | tf_op jit(solution)/shard_map/ppermute | solution.py:562
  144.0 14.2 %collective-permute-start.20 = (bf16[2,48,2048]{2,1,0:T(8,128)(2,1)S(1)}, bf16[2,48,2048]{2,1,0:T(8,128)(2,1)}, u32[]{:S(2)}, u32[]{:S(2)}) collective-permute-start(bf16[2,48,2048]{2,1,0:T(8,128)(2,1)S(1)} %settle.1.back_0), channel_id=1, source_target_pairs={{10,2},{12,4},{18,10},{20,12},{26,18},{28,20},{11,3},{13,5},{19,11... | collective-permute-start | bytes 1179656 | tf_op jit(solution)/shard_map/ppermute | solution.py:576
  159.6 7.7 %collective-permute-start.24 = (bf16[2,48,2048]{2,1,0:T(8,128)(2,1)S(1)}, bf16[2,48,2048]{2,1,0:T(8,128)(2,1)S(1)}, u32[]{:S(2)}, u32[]{:S(2)}) collective-permute-start(bf16[2,48,2048]{2,1,0:T(8,128)(2,1)S(1)} %get-tuple-element.137.up.refs_3_.mine), channel_id=1, source_target_pairs={{0,1},{1,0},{2,3},{3,2},{4,5},{5,4},{6,7},{7,6},{8,9},{9,8},{10,11... | collective-permute-start | bytes 1179656 | tf_op jit(solution)/shard_map/ppermute | solution.py:567
  161.0 3.4 %collective-permute-start.22 = (bf16[2,48,2048]{2,1,0:T(8,128)(2,1)S(1)}, bf16[2,48,2048]{2,1,0:T(8,128)(2,1)S(1)}, u32[]{:S(2)}, u32[]{:S(2)}) collective-permute-start(bf16[2,48,2048]{2,1,0:T(8,128)(2,1)S(1)} %get-tuple-element.135), channel_id=1, source_target_pairs={{0,1},{1,0},{2,3},{3,2},{4,5},{5,4},{6,7},{7,6},{8,9},{9,8},{10,11... | collective-permute-start | bytes 1179656 | tf_op jit(solution)/shard_map/ppermute | solution.py:567
  161.1 7.9 %collective-permute-start.23 = (bf16[48,2048]{1,0:T(8,128)(2,1)S(1)}, bf16[48,2048]{1,0:T(8,128)(2,1)S(1)}, u32[]{:S(2)}, u32[]{:S(2)}) collective-permute-start(bf16[48,2048]{1,0:T(8,128)(2,1)S(1)} %slice_bitcast_fusion.2), channel_id=1, source_target_pairs={{2,0},{4,6},{3,1},{5,7},{10,8},{12,14},{11,9},{13,15},{18,16},{20,... | collective-permute-start | bytes 589832 | tf_op jit(solution)/shard_map/ppermute | solution.py:556
  162.4 6.6 %collective-permute-start.25 = (bf16[96,512]{1,0:T(8,128)(2,1)S(1)}, bf16[96,512]{1,0:T(8,128)(2,1)S(1)}, u32[]{:S(2)}, u32[]{:S(2)}) collective-permute-start(bf16[96,512]{1,0:T(8,128)(2,1)S(1)} %get-tuple-element.142), channel_id=1, source_target_pairs={{4,2},{2,4},{5,3},{3,5},{12,10},{10,12},{13,11},{11,13},{20,18},{1... | collective-permute-start | bytes 294920 | tf_op jit(solution)/shard_map/ppermute | solution.py:559
  163.1 9.1 %collective-permute-start.26 = (bf16[96,512]{1,0:T(8,128)(2,1)S(1)}, bf16[96,512]{1,0:T(8,128)(2,1)S(1)}, u32[]{:S(2)}, u32[]{:S(2)}) collective-permute-start(bf16[96,512]{1,0:T(8,128)(2,1)S(1)} %get-tuple-element.143), channel_id=1, source_target_pairs={{4,0},{2,6},{5,1},{3,7},{12,8},{10,14},{13,9},{11,15},{20,16},{18,... | collective-permute-start | bytes 294920 | tf_op jit(solution)/shard_map/ppermute | solution.py:562
  166.0 12.4 %collective-permute-start.27 = (bf16[96,1536]{1,0:T(8,128)(2,1)S(1)}, bf16[96,1536]{1,0:T(8,128)(2,1)S(1)}, u32[]{:S(2)}, u32[]{:S(2)}) collective-permute-start(bf16[96,1536]{1,0:T(8,128)(2,1)S(1)} %get-tuple-element.144), channel_id=1, source_target_pairs={{2,0},{4,6},{3,1},{5,7},{10,8},{12,14},{11,9},{13,15},{18,16},{20,... | collective-permute-start | bytes 884744 | tf_op jit(solution)/shard_map/ppermute | solution.py:556
  178.4 2.8 %collective-permute-start.28 = (bf16[2,48,2048]{2,1,0:T(8,128)(2,1)S(1)}, bf16[2,48,2048]{2,1,0:T(8,128)(2,1)S(1)}, u32[]{:S(2)}, u32[]{:S(2)}) collective-permute-start(bf16[2,48,2048]{2,1,0:T(8,128)(2,1)S(1)} %get-tuple-element.147), channel_id=1, source_target_pairs={{0,1},{1,0},{2,3},{3,2},{4,5},{5,4},{6,7},{7,6},{8,9},{9,8},{10,11... | collective-permute-start | bytes 1179656 | tf_op jit(solution)/shard_map/ppermute | solution.py:567
  179.9 4.7 %collective-permute-start.30 = (bf16[2,96,512]{2,1,0:T(8,128)(2,1)S(1)}, bf16[2,96,512]{2,1,0:T(8,128)(2,1)S(1)}, u32[]{:S(2)}, u32[]{:S(2)}) collective-permute-start(bf16[2,96,512]{2,1,0:T(8,128)(2,1)S(1)} %pad_maximum_fusion.halves), channel_id=1, source_target_pairs={{0,1},{1,0},{2,3},{3,2},{4,5},{5,4},{6,7},{7,6},{8,9},{9,8},{10,11... | collective-permute-start | bytes 589832 | tf_op jit(solution)/shard_map/ppermute | solution.py:567
  182.4 8.9 %collective-permute-start.29 = (bf16[48,2048]{1,0:T(8,128)(2,1)S(1)}, bf16[48,2048]{1,0:T(8,128)(2,1)S(1)}, u32[]{:S(2)}, u32[]{:S(2)}) collective-permute-start(bf16[48,2048]{1,0:T(8,128)(2,1)S(1)} %get-tuple-element.154), channel_id=1, source_target_pairs={{2,0},{4,6},{3,1},{5,7},{10,8},{12,14},{11,9},{13,15},{18,16},{20,... | collective-permute-start | bytes 589832 | tf_op jit(solution)/shard_map/ppermute | solution.py:556
  (23 other events, 347.1 us)

commit v20 on v18

--- a/solution.py
+++ b/solution.py
@@ -386,7 +386,7 @@
         ]
 
 
-def finish_kernel(slab, host, ahead_0, ahead_1, back_0, pack, message, given, ahead, back):
+def finish_kernel(host, ahead_0, ahead_1, back_0, message, given, ahead, back):
     width = back.shape[1]
     depth = message.shape[1] - width // 2
 
@@ -398,9 +398,9 @@
 
     @pl.when(host[0] == 0)
     def _():
-        unfold(pack, 2 * slab, ahead.at[0])
+        ahead[0] = given[0]
         unfold(message, depth, ahead.at[1])
-        back[...] = given[...]
+        back[...] = given[1]
 
 
 def settle_kernel(core, own, theirs, keep, landed, total):
@@ -412,9 +412,10 @@
         ).astype(BF16)
 
 
-def settle_two_kernel(core, own, theirs, keep, landed, total, other):
+def settle_two_kernel(core, own, theirs, keep, landed, earlier, total, pair):
     settle_kernel(core, own, theirs, keep, landed, total)
-    other[...] = total[1]
+    pair[0] = earlier[1]
+    pair[1] = total[1]
 
 
 def first_kernel(core, own, theirs, keep, landed, gated, total, pack):
@@ -422,7 +423,6 @@
     settle_kernel(core, own, theirs, keep, landed, total)
     pack[:, :slab] = gated[1]
     pack[:, slab : 2 * slab] = gated[2]
-    fold(total[1], pack, 2 * slab)
 
 
 def message_kernel(
@@ -794,7 +794,7 @@
         name="out",
     )(core, offs, gated, early_part, *out_parts[soon:])
     ahead_landed = swap_cores(ahead_send)
-    first_shapes = [halves[0], struct((rows, 2 * slab + folded), BF16)]
+    first_shapes = [halves[0], struct((rows, 2 * slab), BF16)]
     ahead_0, partner_pack = pl.pallas_call(
         first_kernel,
         grid=(1,),
@@ -811,16 +811,16 @@
         (back_send, back_keep, ahead_in, packs_near)
     )
     back_landed = swap_cores(back_send)
-    settled = [halves[0], struct((share, width), BF16)]
+    settled = list(halves)
     back_0, back_given = pl.pallas_call(
         settle_two_kernel,
         grid=(1,),
-        in_specs=[smem] + all_of(up_own, up_theirs, back_keep, back_landed),
+        in_specs=[smem] + all_of(up_own, up_theirs, back_keep, back_landed, ahead_0),
         out_specs=all_of(*settled),
         out_shape=settled,
         compiler_params=small,
         name="settle",
-    )(core, *in_hbm([up_own, up_theirs, back_keep]), back_landed)
+    )(core, *in_hbm([up_own, up_theirs, back_keep]), back_landed, *in_hbm([ahead_0]))
     back_in = along_sections(back_0, -1)
 
     packs_beyond = [to_beyond(packs[n // 2 + m - 2], m) for m in between]
@@ -926,11 +926,11 @@
         name="grads",
     )(host_flag, core, offs, *grad_inputs)
 
-    first_pack, last_cut = lax.optimization_barrier((packs_near[0], landed[0], back_1))[:2]
-    finish_inputs = [ahead_0, ahead_1, back_0, first_pack, last_cut, back_given]
+    last_cut = after(landed[0], back_1)
+    finish_inputs = [ahead_0, ahead_1, back_0, last_cut, back_given]
     finish_shapes = [struct((ticks, share, width), BF16), struct((share, width), BF16)]
     ahead, back_first = pl.pallas_call(
-        functools.partial(finish_kernel, slab),
+        finish_kernel,
         grid=(1,),
         in_specs=[smem] + all_of(*finish_inputs),
         out_specs=all_of(*finish_shapes),

time: 195 us -> 196 us (level)
    ppermute x5, waiting for transfers between devices: 26.5 us -> 28.6 us  [to_partner(): return lax.ppermute(x, 'dp', [(h, h ^ 1) for h in hosts])]
  transfers between devices with their start and end apart: 31 -> 31, of which waited for: 14 -> 12; matrix products, arithmetic and copies ran while one was open for 8% -> 8% of each run, Pallas kernels for 13% -> 13%
where the time goes in v20:
time: 196 us; the launch traced here: 192 us
  waiting for transfers between devices  90.3 us (46%)
  starting transfers between devices  55.2 us (28%)
  Pallas kernels  26.3 us (13%)
  local copies, waits for them, and re-layouts  10 us (5%)
  other arithmetic  7.53 us (4%)
  between operations  3.1 us (2%)
    ppermute x8, waiting for transfers between devices, from_partner(): return lax.ppermute(x, 'dp', [(h ^ 1, h) for h in hosts])  49.1 us
    ppermute x8, starting transfers between devices, from_partner(): return lax.ppermute(x, 'dp', [(h ^ 1, h) for h in hosts])  30.1 us
    ppermute x5, waiting for transfers between devices, to_partner(): return lax.ppermute(x, 'dp', [(h, h ^ 1) for h in hosts])  28.6 us
    ppermute x2, waiting for transfers between devices, to_beyond(): lax.ppermute(x, 'dp', [(hosts[k ^ m], hosts[k] ^ 1) for k in range(n // 2)])  10.7 us
    ppermute x7, starting transfers between devices, from_host(): lax.ppermute(x, 'dp', [(hosts[k ^ m], hosts[k]) for k in range(n // 2)])  7.12 us
    ppermute x5, starting transfers between devices, to_partner(): return lax.ppermute(x, 'dp', [(h, h ^ 1) for h in hosts])  6.45 us
    ppermute x7, starting transfers between devices, swap_cores(): return lax.ppermute(x, 'cores', [(c, cores - 1 - c) for c in range(cores)])  5.92 us
  transfers between devices with their start and end apart: 31, of which 12 were waited for; matrix products, arithmetic and copies ran while one was open for 8% of the time, Pallas kernels for 13%

profile of v20, /device:TPU:5, one launch (start us, length us, event | category | flops | bytes accessed | tf_op | source)
XLA Modules:
  0.0 192.4 jit_solution(10658336223754793086)
XLA Ops:
  1.6 3.2 %slice_bitcast_fusion = (bf16[256,2048]{1,0:T(8,128)(2,1)}, bf16[256,2048]{1,0:T(8,128)(2,1)}) fusion(bf16[1,512,2048]{2,1,0:T(8,128)(2,1)} %param.17), kind=kLoop, calls=%fused_computation | loop fusion | bytes 4194304 | tf_op jit(solution)/shard_map/slice | solution.py:594
  4.8 6.6 %collective-permute-start.1 = (bf16[256,2048]{1,0:T(8,128)(2,1)}, bf16[256,2048]{1,0:T(8,128)(2,1)}, u32[]{:S(2)}, u32[]{:S(2)}) collective-permute-start(bf16[256,2048]{1,0:T(8,128)(2,1)} %get-tuple-element.164), channel_id=1, source_target_pairs={{0,2},{6,4},{1,3},{7,5},{8,10},{14,12},{9,11},{15,13},{16,18},{22,... | collective-permute-start | bytes 3145736 | tf_op jit(solution)/shard_map/ppermute | solution.py:561
  11.4 2.3 %collective-permute-start.2 = (bf16[256,2048]{1,0:T(8,128)(2,1)}, bf16[256,2048]{1,0:T(8,128)(2,1)}, u32[]{:S(2)}, u32[]{:S(2)}) collective-permute-start(bf16[256,2048]{1,0:T(8,128)(2,1)} %get-tuple-element.163), channel_id=1, source_target_pairs={{0,2},{6,4},{1,3},{7,5},{8,10},{14,12},{9,11},{15,13},{16,18},{22,... | collective-permute-start | bytes 3145736 | tf_op jit(solution)/shard_map/ppermute | solution.py:561
  19.5 12.6 %collective-permute-done.1.refs_8_.refs_16_.refs_11_.refs_19_ = bf16[256,2048]{1,0:T(8,128)(2,1)} collective-permute-done((bf16[256,2048]{1,0:T(8,128)(2,1)}, bf16[256,2048]{1,0:T(8,128)(2,1)}, u32[]{:S(2)}, u32[]{:S(2)}) %collective-permute-start.1) | collective-permute-done | bytes 1048608 | tf_op jit(solution)/shard_map/ppermute | solution.py:561
  32.2 1.6 collective-permute-start.7
  33.8 20.8 %collective-permute-done.2.refs_9_.refs_17_.refs_12_.refs_20_ = bf16[256,2048]{1,0:T(8,128)(2,1)} collective-permute-done((bf16[256,2048]{1,0:T(8,128)(2,1)}, bf16[256,2048]{1,0:T(8,128)(2,1)}, u32[]{:S(2)}, u32[]{:S(2)}) %collective-permute-start.2) | collective-permute-done | bytes 1048608 | tf_op jit(solution)/shard_map/ppermute | solution.py:561
  59.8 4.1 %collective-permute-start.6 = (s32[2,5,17]{2,0,1:T(2,128)S(1)}, s32[2,5,17]{2,0,1:T(2,128)S(1)}, u32[]{:S(2)}, u32[]{:S(2)}) collective-permute-start(s32[2,5,17]{2,0,1:T(2,128)S(1)} %add_add_fusion), channel_id=1, source_target_pairs={{0,2},{6,4},{1,3},{7,5},{8,10},{14,12},{9,11},{15,13},{16,18},{22,... | collective-permute-start | bytes 2048 | tf_op jit(solution)/shard_map/ppermute | solution.py:561
  63.9 2.2 %collective-permute-start.4 = (bf16[2,96,2048]{2,1,0:T(8,128)(2,1)}, bf16[2,96,2048]{2,1,0:T(8,128)(2,1)}, u32[]{:S(2)}, u32[]{:S(2)}) collective-permute-start(bf16[2,96,2048]{2,1,0:T(8,128)(2,1)} %bitcast.12.refs_3_.refs_11_), channel_id=1, source_target_pairs={{0,2},{6,4},{1,3},{7,5},{8,10},{14,12},{9,11},{15,13},{16,18},{22,... | collective-permute-start | bytes 2359304 | tf_op jit(solution)/shard_map/ppermute | solution.py:561
  66.1 1.7 collective-permute-start.8
  67.8 2.4 %select_bitcast_fusion = (bf16[96,2048]{1,0:T(8,128)(2,1)}, bf16[96,2048]{1,0:T(8,128)(2,1)S(1)}, bf16[96,2048]{1,0:T(8,128)(2,1)S(1)}) fusion(bf16[2,96,2048]{2,1,0:T(8,128)(2,1)} %param.14, bf16[2,96,2048]{2,1,0:T(8,128)(2,1)} %param.12, pred[]{:T(512)S(6)} %eq.44, bf16[1,96,2048]{2,1,0:T(8,128)(2,1)S(1)} %copy-done.19, bf16[1,96,2048]{2,1,0:T(8,128)(2,1)} %param.15, ...), kind=kLoop, calls=%fused_computation.6 | loop fusion | flops 589824 | bytes 3538946 | tf_op jit(solution)/shard_map/jit(_where)/select_n | solution.py:622
  70.2 2.0 %collective-permute-start.3 = (bf16[96,2048]{1,0:T(8,128)(2,1)S(1)}, bf16[96,2048]{1,0:T(8,128)(2,1)}, u32[]{:S(2)}, u32[]{:S(2)}) collective-permute-start(bf16[96,2048]{1,0:T(8,128)(2,1)S(1)} %get-tuple-element.166.refs_1_.own), channel_id=1, source_target_pairs={{0,2},{6,4},{1,3},{7,5},{8,10},{14,12},{9,11},{15,13},{16,18},{22,... | collective-permute-start | bytes 1179656 | tf_op jit(solution)/shard_map/ppermute | solution.py:561
  74.6 7.3 %collective-permute-done.4.refs_4_.refs_12_ = bf16[2,96,2048]{2,1,0:T(8,128)(2,1)} collective-permute-done((bf16[2,96,2048]{2,1,0:T(8,128)(2,1)}, bf16[2,96,2048]{2,1,0:T(8,128)(2,1)}, u32[]{:S(2)}, u32[]{:S(2)}) %collective-permute-start.4) | collective-permute-done | bytes 786464 | tf_op jit(solution)/shard_map/ppermute | solution.py:561
  82.7 5.5 %collective-permute-start.11 = (bf16[96,2048]{1,0:T(8,128)(2,1)S(1)}, bf16[96,2048]{1,0:T(8,128)(2,1)S(1)}, u32[]{:S(2)}, u32[]{:S(2)}) collective-permute-start(bf16[96,2048]{1,0:T(8,128)(2,1)S(1)} %get-tuple-element.99.up_own.own), channel_id=1, source_target_pairs={{0,2},{6,4},{1,3},{7,5},{8,10},{14,12},{9,11},{15,13},{16,18},{22,... | collective-permute-start | bytes 1179656 | tf_op jit(solution)/shard_map/ppermute | solution.py:561
  88.2 2.1 %collective-permute-done.3.refs_2_.theirs = bf16[96,2048]{1,0:T(8,128)(2,1)} collective-permute-done((bf16[96,2048]{1,0:T(8,128)(2,1)S(1)}, bf16[96,2048]{1,0:T(8,128)(2,1)}, u32[]{:S(2)}, u32[]{:S(2)}) %collective-permute-start.3) | collective-permute-done | bytes 393248 | tf_op jit(solution)/shard_map/ppermute | solution.py:561
  91.6 6.1 %collective-permute-start.9 = (bf16[96,2048]{1,0:T(8,128)(2,1)S(1)}, bf16[96,2048]{1,0:T(8,128)(2,1)S(1)}, u32[]{:S(2)}, u32[]{:S(2)}) collective-permute-start(bf16[96,2048]{1,0:T(8,128)(2,1)S(1)} %copy-done.15), channel_id=1, source_target_pairs={{0,2},{6,4},{1,3},{7,5},{8,10},{14,12},{9,11},{15,13},{16,18},{22,... | collective-permute-start | bytes 1179656 | tf_op jit(solution)/shard_map/ppermute | solution.py:561
  98.7 2.2 %project.1 = (bf16[3,192,512]{2,1,0:T(8,128)(2,1)S(1)}, f32[2,192,512]{2,1,0:T(8,128)}, bf16[2,192,1536]{2,1,0:T(8,128)(2,1)}, f32[2,192,2048]{2,1,0:T(8,128)}, ...) custom-call(s32[1]{0:T(128)} %bitcast.1.host, s32[6]{0:T(128)S(1)} %stack.73.refs_0_.refs_1_, ...), custom_call_target="tpu_custom_call" | custom-call | flops 4831838208 | bytes 20971520 | tf_op jit(solution)/shard_map/project/pallas_call | solution.py:704
  100.9 6.2 %collective-permute-done.9.refs_7_.new_theirs = bf16[96,2048]{1,0:T(8,128)(2,1)S(1)} collective-permute-done((bf16[96,2048]{1,0:T(8,128)(2,1)S(1)}, bf16[96,2048]{1,0:T(8,128)(2,1)S(1)}, u32[]{:S(2)}, u32[]{:S(2)}) %collective-permute-start.9) | collective-permute-done | bytes 393248 | tf_op jit(solution)/shard_map/ppermute | solution.py:561
  107.1 1.8 pack.1
  108.9 3.0 %early.1 = (bf16[192,2048]{1,0:T(8,128)(2,1)S(1)}, f32[192,512]{1,0:T(8,128)}) custom-call(s32[4]{0:T(128)S(1)} %add_multiply_fusion.offs.refs_2_, bf16[3,192,512]{2,1,0:T(8,128)(2,1)S(1)} %get-tuple-element.156.gated, bf16[192,2048]{1,0:T(8,128)(2,1)} %get-tuple-element.117.upstream.refs_3_.up_0, bf16[512,512]{1,0:T(8,128)(2,1)S(1)} %bitcast.72, ...), custom_call_target="tpu_custom_call" | custom-call | tf_op jit(solution)/shard_map/early/pallas_call | solution.py:771
  112.8 2.9 %collective-permute-start.14 = (bf16[2,48,2048]{2,1,0:T(8,128)(2,1)S(1)}, bf16[2,48,2048]{2,1,0:T(8,128)(2,1)S(1)}, u32[]{:S(2)}, u32[]{:S(2)}) collective-permute-start(bf16[2,48,2048]{2,1,0:T(8,128)(2,1)S(1)} %get-tuple-element.114), channel_id=1, source_target_pairs={{0,1},{1,0},{2,3},{3,2},{4,5},{5,4},{6,7},{7,6},{8,9},{9,8},{10,11... | collective-permute-start | bytes 1179656 | tf_op jit(solution)/shard_map/ppermute | solution.py:575
  121.0 1.6 backward.2
  122.7 12.9 %collective-permute-done.16.rest_0_ = bf16[192,1024]{1,0:T(8,128)(2,1)S(1)} collective-permute-done((bf16[192,1024]{1,0:T(8,128)(2,1)S(1)}, bf16[192,1024]{1,0:T(8,128)(2,1)S(1)}, u32[]{:S(2)}, u32[]{:S(2)}) %collective-permute-start.16) | collective-permute-done | bytes 393248 | tf_op jit(solution)/shard_map/ppermute | solution.py:564
  138.0 2.4 %settle.1 = (bf16[2,48,2048]{2,1,0:T(8,128)(2,1)}, bf16[2,48,2048]{2,1,0:T(8,128)(2,1)S(1)}) custom-call(s32[1]{0:T(128)} %bitcast.2.core.refs_0_, bf16[96,2048]{1,0:T(8,128)(2,1)} %copy-done, bf16[96,2048]{1,0:T(8,128)(2,1)} %copy-done.11, bf16[2,48,2048]{2,1,0:T(8,128)(2,1)} %get-tuple-element.132.keep, ...), custom_call_target="tpu_custom_call" | custom-call | tf_op jit(solution)/shard_map/settle/pallas_call | solution.py:815
  142.6 2.5 %forward.1 = (bf16[2,48,2048]{2,1,0:T(8,128)(2,1)S(1)}, bf16[2,48,2048]{2,1,0:T(8,128)(2,1)}) custom-call(s32[1]{0:T(128)} %bitcast.1.host, s32[1]{0:T(128)} %bitcast.2.core.refs_0_, s32[6]{0:T(128)S(1)} %stack.73.refs_0_.refs_1_, s32[4]{0:T(128)S(1)} %add_multiply_fusion.offs.refs_2_, s32[1]{0:T(128)} %bitcast.33.refs_3_.fresh, ...), custom_call_target="tpu_custom_call" | custom-call | flops 3221225472 | bytes 20971520 | tf_op jit(solution)/shard_map/forward/pallas_call | solution.py:828
  145.0 10.7 %collective-permute-done.21.rest_2_ = bf16[192,1536]{1,0:T(8,128)(2,1)} collective-permute-done((bf16[192,1536]{1,0:T(8,128)(2,1)}, bf16[192,1536]{1,0:T(8,128)(2,1)}, u32[]{:S(2)}, u32[]{:S(2)}) %collective-permute-start.21) | collective-permute-done | bytes 589856 | tf_op jit(solution)/shard_map/ppermute | solution.py:570
  161.4 1.6 message.1
  164.4 1.7 backward.3
  166.1 7.6 %collective-permute-done.23.given = bf16[2,48,2048]{2,1,0:T(8,128)(2,1)S(1)} collective-permute-done((bf16[2,48,2048]{2,1,0:T(8,128)(2,1)S(1)}, bf16[2,48,2048]{2,1,0:T(8,128)(2,1)S(1)}, u32[]{:S(2)}, u32[]{:S(2)}) %collective-permute-start.23) | collective-permute-done | bytes 393248 | tf_op jit(solution)/shard_map/ppermute | solution.py:564
  173.7 6.3 %collective-permute-done.27.message = bf16[96,1536]{1,0:T(8,128)(2,1)S(1)} collective-permute-done((bf16[96,1536]{1,0:T(8,128)(2,1)S(1)}, bf16[96,1536]{1,0:T(8,128)(2,1)S(1)}, u32[]{:S(2)}, u32[]{:S(2)}) %collective-permute-start.27) | collective-permute-done | bytes 294944 | tf_op jit(solution)/shard_map/ppermute | solution.py:564
  184.9 1.8 finish.1
  186.7 3.1 %grads.1 = f32[512,512]{1,0:T(8,128)} custom-call(s32[1]{0:T(128)} %bitcast.1.host, s32[1]{0:T(128)} %bitcast.2.core.refs_0_, s32[4]{0:T(128)S(1)} %add_multiply_fusion.offs.refs_2_, bf16[3,192,512]{2,1,0:T(8,128)(2,1)S(1)} %get-tuple-element.156.gated, bf16[192,2048]{1,0:T(8,128)(2,1)S(1)} %copy-done.2, bf16[96,2048]{1,0:T(8,128)(2,1)S(1)} %copy-done.1, ...), custom_call_target="tpu_custom_call" | custom-call | flops 402653184 | bytes 2621440 | tf_op jit(solution)/shard_map/grads/pallas_call | solution.py:917
  189.8 1.8 collective-permute-done.29
  (128 shorter events, 38.8 us)
Async XLA Ops:
  0.7 67.1 %copy-start.19 = (bf16[1,96,2048]{2,1,0:T(8,128)(2,1)S(1)}, bf16[1,96,2048]{2,1,0:T(8,128)(2,1)}, u32[]{:S(2)}) copy-start(bf16[1,96,2048]{2,1,0:T(8,128)(2,1)} %param.13) | copy-start | bytes 1179652
  0.7 54.0 %collective-permute-start = (bf16[512,2048]{1,0:T(8,128)(2,1)}, bf16[512,2048]{1,0:T(8,128)(2,1)S(1)}, u32[]{:S(2)}, u32[]{:S(2)}) collective-permute-start(bf16[512,2048]{1,0:T(8,128)(2,1)} %bitcast.76), channel_id=1, source_target_pairs={{4,2},{2,4},{5,3},{3,5},{12,10},{10,12},{13,11},{11,13},{20,18},{1... | collective-permute-start | bytes 6291464 | tf_op jit(solution)/shard_map/ppermute | solution.py:567
  4.8 27.4 %collective-permute-start.1 = (bf16[256,2048]{1,0:T(8,128)(2,1)}, bf16[256,2048]{1,0:T(8,128)(2,1)}, u32[]{:S(2)}, u32[]{:S(2)}) collective-permute-start(bf16[256,2048]{1,0:T(8,128)(2,1)} %get-tuple-element.164), channel_id=1, source_target_pairs={{0,2},{6,4},{1,3},{7,5},{8,10},{14,12},{9,11},{15,13},{16,18},{22,... | collective-permute-start | bytes 3145736 | tf_op jit(solution)/shard_map/ppermute | solution.py:561
  11.4 43.3 %collective-permute-start.2 = (bf16[256,2048]{1,0:T(8,128)(2,1)}, bf16[256,2048]{1,0:T(8,128)(2,1)}, u32[]{:S(2)}, u32[]{:S(2)}) collective-permute-start(bf16[256,2048]{1,0:T(8,128)(2,1)} %get-tuple-element.163), channel_id=1, source_target_pairs={{0,2},{6,4},{1,3},{7,5},{8,10},{14,12},{9,11},{15,13},{16,18},{22,... | collective-permute-start | bytes 3145736 | tf_op jit(solution)/shard_map/ppermute | solution.py:561
  13.6 56.6 %collective-permute-start.5 = (bf16[512,512]{1,0:T(8,128)(2,1)S(1)}, bf16[512,512]{1,0:T(8,128)(2,1)S(1)}, u32[]{:S(2)}, u32[]{:S(2)}) collective-permute-start(bf16[512,512]{1,0:T(8,128)(2,1)S(1)} %bitcast.70), channel_id=1, source_target_pairs={{0,2},{6,4},{1,3},{7,5},{8,10},{14,12},{9,11},{15,13},{16,18},{22,... | collective-permute-start | bytes 1572872 | tf_op jit(solution)/shard_map/ppermute | solution.py:561
  32.2 50.5 %collective-permute-start.7 = (bf16[256,2048]{1,0:T(8,128)(2,1)}, bf16[256,2048]{1,0:T(8,128)(2,1)}, u32[]{:S(2)}, u32[]{:S(2)}) collective-permute-start(bf16[256,2048]{1,0:T(8,128)(2,1)} %collective-permute-done.1.refs_8_.refs_16_.refs_11_.refs_19_), channel_id=1, source_target_pairs={{4,2},{2,4},{5,3},{3,5},{12,10},{10,12},{13,11},{11,13},{20,18},{1... | collective-permute-start | bytes 3145736 | tf_op jit(solution)/shard_map/ppermute | solution.py:567
  59.8 12.4 %collective-permute-start.6 = (s32[2,5,17]{2,0,1:T(2,128)S(1)}, s32[2,5,17]{2,0,1:T(2,128)S(1)}, u32[]{:S(2)}, u32[]{:S(2)}) collective-permute-start(s32[2,5,17]{2,0,1:T(2,128)S(1)} %add_add_fusion), channel_id=1, source_target_pairs={{0,2},{6,4},{1,3},{7,5},{8,10},{14,12},{9,11},{15,13},{16,18},{22,... | collective-permute-start | bytes 2048 | tf_op jit(solution)/shard_map/ppermute | solution.py:561
  63.9 18.0 %collective-permute-start.4 = (bf16[2,96,2048]{2,1,0:T(8,128)(2,1)}, bf16[2,96,2048]{2,1,0:T(8,128)(2,1)}, u32[]{:S(2)}, u32[]{:S(2)}) collective-permute-start(bf16[2,96,2048]{2,1,0:T(8,128)(2,1)} %bitcast.12.refs_3_.refs_11_), channel_id=1, source_target_pairs={{0,2},{6,4},{1,3},{7,5},{8,10},{14,12},{9,11},{15,13},{16,18},{22,... | collective-permute-start | bytes 2359304 | tf_op jit(solution)/shard_map/ppermute | solution.py:561
  66.1 25.5 %collective-permute-start.8 = (bf16[256,2048]{1,0:T(8,128)(2,1)}, bf16[256,2048]{1,0:T(8,128)(2,1)}, u32[]{:S(2)}, u32[]{:S(2)}) collective-permute-start(bf16[256,2048]{1,0:T(8,128)(2,1)} %collective-permute-done.2.refs_9_.refs_17_.refs_12_.refs_20_), channel_id=1, source_target_pairs={{4,2},{2,4},{5,3},{3,5},{12,10},{10,12},{13,11},{11,13},{20,18},{1... | collective-permute-start | bytes 3145736 | tf_op jit(solution)/shard_map/ppermute | solution.py:567
  70.2 20.1 %collective-permute-start.3 = (bf16[96,2048]{1,0:T(8,128)(2,1)S(1)}, bf16[96,2048]{1,0:T(8,128)(2,1)}, u32[]{:S(2)}, u32[]{:S(2)}) collective-permute-start(bf16[96,2048]{1,0:T(8,128)(2,1)S(1)} %get-tuple-element.166.refs_1_.own), channel_id=1, source_target_pairs={{0,2},{6,4},{1,3},{7,5},{8,10},{14,12},{9,11},{15,13},{16,18},{22,... | collective-permute-start | bytes 1179656 | tf_op jit(solution)/shard_map/ppermute | solution.py:561
  73.3 35.6 %collective-permute-start.12 = (bf16[512,512]{1,0:T(8,128)(2,1)S(1)}, bf16[512,512]{1,0:T(8,128)(2,1)S(1)}, u32[]{:S(2)}, u32[]{:S(2)}) collective-permute-start(bf16[512,512]{1,0:T(8,128)(2,1)S(1)} %bitcast.71), channel_id=1, source_target_pairs={{4,2},{2,4},{5,3},{3,5},{12,10},{10,12},{13,11},{11,13},{20,18},{1... | collective-permute-start | bytes 1572872 | tf_op jit(solution)/shard_map/ppermute | solution.py:567
  81.9 30.0 %collective-permute-start.13 = (bf16[512,512]{1,0:T(8,128)(2,1)S(1)}, bf16[512,512]{1,0:T(8,128)(2,1)S(1)}, u32[]{:S(2)}, u32[]{:S(2)}) collective-permute-start(bf16[512,512]{1,0:T(8,128)(2,1)S(1)} %collective-permute-done.5.rest_1_.refs_16_.refs_14_), channel_id=1, source_target_pairs={{4,2},{2,4},{5,3},{3,5},{12,10},{10,12},{13,11},{11,13},{20,18},{1... | collective-permute-start | bytes 1572872 | tf_op jit(solution)/shard_map/ppermute | solution.py:567
  82.7 24.5 %collective-permute-start.11 = (bf16[96,2048]{1,0:T(8,128)(2,1)S(1)}, bf16[96,2048]{1,0:T(8,128)(2,1)S(1)}, u32[]{:S(2)}, u32[]{:S(2)}) collective-permute-start(bf16[96,2048]{1,0:T(8,128)(2,1)S(1)} %get-tuple-element.99.up_own.own), channel_id=1, source_target_pairs={{0,2},{6,4},{1,3},{7,5},{8,10},{14,12},{9,11},{15,13},{16,18},{22,... | collective-permute-start | bytes 1179656 | tf_op jit(solution)/shard_map/ppermute | solution.py:561
  90.3 10.6 %collective-permute-start.10 = (bf16[96,512]{1,0:T(8,128)(2,1)S(1)}, bf16[96,512]{1,0:T(8,128)(2,1)S(1)}, u32[]{:S(2)}, u32[]{:S(2)}) collective-permute-start(bf16[96,512]{1,0:T(8,128)(2,1)S(1)} %constant_dynamic-slice_fusion), channel_id=1, source_target_pairs={{2,0},{4,6},{3,1},{5,7},{10,8},{12,14},{11,9},{13,15},{18,16},{20,... | collective-permute-start | bytes 294920 | tf_op jit(solution)/shard_map/ppermute | solution.py:564
  91.6 15.5 %collective-permute-start.9 = (bf16[96,2048]{1,0:T(8,128)(2,1)S(1)}, bf16[96,2048]{1,0:T(8,128)(2,1)S(1)}, u32[]{:S(2)}, u32[]{:S(2)}) collective-permute-start(bf16[96,2048]{1,0:T(8,128)(2,1)S(1)} %copy-done.15), channel_id=1, source_target_pairs={{0,2},{6,4},{1,3},{7,5},{8,10},{14,12},{9,11},{15,13},{16,18},{22,... | collective-permute-start | bytes 1179656 | tf_op jit(solution)/shard_map/ppermute | solution.py:561
  112.8 4.2 %collective-permute-start.14 = (bf16[2,48,2048]{2,1,0:T(8,128)(2,1)S(1)}, bf16[2,48,2048]{2,1,0:T(8,128)(2,1)S(1)}, u32[]{:S(2)}, u32[]{:S(2)}) collective-permute-start(bf16[2,48,2048]{2,1,0:T(8,128)(2,1)S(1)} %get-tuple-element.114), channel_id=1, source_target_pairs={{0,1},{1,0},{2,3},{3,2},{4,5},{5,4},{6,7},{7,6},{8,9},{9,8},{10,11... | collective-permute-start | bytes 1179656 | tf_op jit(solution)/shard_map/ppermute | solution.py:575
  115.7 7.0 %collective-permute-start.17 = (bf16[192,1536]{1,0:T(8,128)(2,1)S(1)}, bf16[192,1536]{1,0:T(8,128)(2,1)S(1)}, u32[]{:S(2)}, u32[]{:S(2)}) collective-permute-start(bf16[192,1536]{1,0:T(8,128)(2,1)S(1)} %get-tuple-element.128), channel_id=1, source_target_pairs={{4,2},{2,4},{5,3},{3,5},{12,10},{10,12},{13,11},{11,13},{20,18},{1... | collective-permute-start | bytes 1769480 | tf_op jit(solution)/shard_map/ppermute | solution.py:567
  118.3 17.3 %collective-permute-start.16 = (bf16[192,1024]{1,0:T(8,128)(2,1)S(1)}, bf16[192,1024]{1,0:T(8,128)(2,1)S(1)}, u32[]{:S(2)}, u32[]{:S(2)}) collective-permute-start(bf16[192,1024]{1,0:T(8,128)(2,1)S(1)} %get-tuple-element.127), channel_id=1, source_target_pairs={{2,0},{4,6},{3,1},{5,7},{10,8},{12,14},{11,9},{13,15},{18,16},{20,... | collective-permute-start | bytes 1179656 | tf_op jit(solution)/shard_map/ppermute | solution.py:564
  119.6 16.0 %collective-permute-start.15 = (bf16[2,48,2048]{2,1,0:T(8,128)(2,1)S(1)}, bf16[2,48,2048]{2,1,0:T(8,128)(2,1)}, u32[]{:S(2)}, u32[]{:S(2)}) collective-permute-start(bf16[2,48,2048]{2,1,0:T(8,128)(2,1)S(1)} %get-tuple-element.115.earlier.ahead_0), channel_id=1, source_target_pairs={{2,10},{4,12},{10,18},{12,20},{18,26},{20,28},{3,11},{5,13},{11,19... | collective-permute-start | bytes 1179656 | tf_op jit(solution)/shard_map/ppermute | solution.py:584
  135.6 2.3 %collective-permute-start.19 = (bf16[2,48,2048]{2,1,0:T(8,128)(2,1)S(1)}, bf16[2,48,2048]{2,1,0:T(8,128)(2,1)S(1)}, u32[]{:S(2)}, u32[]{:S(2)}) collective-permute-start(bf16[2,48,2048]{2,1,0:T(8,128)(2,1)S(1)} %get-tuple-element.133), channel_id=1, source_target_pairs={{0,1},{1,0},{2,3},{3,2},{4,5},{5,4},{6,7},{7,6},{8,9},{9,8},{10,11... | collective-permute-start | bytes 1179656 | tf_op jit(solution)/shard_map/ppermute | solution.py:575
  136.5 6.1 %collective-permute-start.18 = (bf16[2,48,2048]{2,1,0:T(8,128)(2,1)}, bf16[2,48,2048]{2,1,0:T(8,128)(2,1)S(1)}, u32[]{:S(2)}, u32[]{:S(2)}) collective-permute-start(bf16[2,48,2048]{2,1,0:T(8,128)(2,1)} %collective-permute-done.15.refs_4_.passed), channel_id=1, source_target_pairs={{0,1},{1,0},{2,3},{3,2},{4,5},{5,4},{6,7},{7,6},{8,9},{9,8},{10,11... | collective-permute-start | bytes 1179656 | tf_op jit(solution)/shard_map/ppermute | solution.py:575
  136.5 19.2 %collective-permute-start.21 = (bf16[192,1536]{1,0:T(8,128)(2,1)}, bf16[192,1536]{1,0:T(8,128)(2,1)}, u32[]{:S(2)}, u32[]{:S(2)}) collective-permute-start(bf16[192,1536]{1,0:T(8,128)(2,1)} %get-tuple-element.135), channel_id=1, source_target_pairs={{4,0},{2,6},{5,1},{3,7},{12,8},{10,14},{13,9},{11,15},{20,16},{18,... | collective-permute-start | bytes 1769480 | tf_op jit(solution)/shard_map/ppermute | solution.py:570
  141.1 14.6 %collective-permute-start.20 = (bf16[2,48,2048]{2,1,0:T(8,128)(2,1)}, bf16[2,48,2048]{2,1,0:T(8,128)(2,1)}, u32[]{:S(2)}, u32[]{:S(2)}) collective-permute-start(bf16[2,48,2048]{2,1,0:T(8,128)(2,1)} %get-tuple-element.134.back_0), channel_id=1, source_target_pairs={{10,2},{12,4},{18,10},{20,12},{26,18},{28,20},{11,3},{13,5},{19,11... | collective-permute-start | bytes 1179656 | tf_op jit(solution)/shard_map/ppermute | solution.py:584
  155.7 5.7 %collective-permute-start.22 = (bf16[2,48,2048]{2,1,0:T(8,128)(2,1)S(1)}, bf16[2,48,2048]{2,1,0:T(8,128)(2,1)S(1)}, u32[]{:S(2)}, u32[]{:S(2)}) collective-permute-start(bf16[2,48,2048]{2,1,0:T(8,128)(2,1)S(1)} %get-tuple-element.137), channel_id=1, source_target_pairs={{0,1},{1,0},{2,3},{3,2},{4,5},{5,4},{6,7},{7,6},{8,9},{9,8},{10,11... | collective-permute-start | bytes 1179656 | tf_op jit(solution)/shard_map/ppermute | solution.py:575
  158.1 6.3 %collective-permute-start.24 = (bf16[2,48,2048]{2,1,0:T(8,128)(2,1)S(1)}, bf16[2,48,2048]{2,1,0:T(8,128)(2,1)S(1)}, u32[]{:S(2)}, u32[]{:S(2)}) collective-permute-start(bf16[2,48,2048]{2,1,0:T(8,128)(2,1)S(1)} %get-tuple-element.139.up.refs_3_.mine), channel_id=1, source_target_pairs={{0,1},{1,0},{2,3},{3,2},{4,5},{5,4},{6,7},{7,6},{8,9},{9,8},{10,11... | collective-permute-start | bytes 1179656 | tf_op jit(solution)/shard_map/ppermute | solution.py:575
  158.2 15.5 %collective-permute-start.23 = (bf16[2,48,2048]{2,1,0:T(8,128)(2,1)S(1)}, bf16[2,48,2048]{2,1,0:T(8,128)(2,1)S(1)}, u32[]{:S(2)}, u32[]{:S(2)}) collective-permute-start(bf16[2,48,2048]{2,1,0:T(8,128)(2,1)S(1)} %copy-done.13), channel_id=1, source_target_pairs={{2,0},{4,6},{3,1},{5,7},{10,8},{12,14},{11,9},{13,15},{18,16},{20,... | collective-permute-start | bytes 1179656 | tf_op jit(solution)/shard_map/ppermute | solution.py:564
  159.5 14.2 %collective-permute-start.25 = (bf16[96,512]{1,0:T(8,128)(2,1)S(1)}, bf16[96,512]{1,0:T(8,128)(2,1)S(1)}, u32[]{:S(2)}, u32[]{:S(2)}) collective-permute-start(bf16[96,512]{1,0:T(8,128)(2,1)S(1)} %get-tuple-element.144), channel_id=1, source_target_pairs={{4,2},{2,4},{5,3},{3,5},{12,10},{10,12},{13,11},{11,13},{20,18},{1... | collective-permute-start | bytes 294920 | tf_op jit(solution)/shard_map/ppermute | solution.py:567
  160.1 13.6 %collective-permute-start.26 = (bf16[96,512]{1,0:T(8,128)(2,1)S(1)}, bf16[96,512]{1,0:T(8,128)(2,1)S(1)}, u32[]{:S(2)}, u32[]{:S(2)}) collective-permute-start(bf16[96,512]{1,0:T(8,128)(2,1)S(1)} %get-tuple-element.145), channel_id=1, source_target_pairs={{4,0},{2,6},{5,1},{3,7},{12,8},{10,14},{13,9},{11,15},{20,16},{18,... | collective-permute-start | bytes 294920 | tf_op jit(solution)/shard_map/ppermute | solution.py:570
  163.1 16.9 %collective-permute-start.27 = (bf16[96,1536]{1,0:T(8,128)(2,1)S(1)}, bf16[96,1536]{1,0:T(8,128)(2,1)S(1)}, u32[]{:S(2)}, u32[]{:S(2)}) collective-permute-start(bf16[96,1536]{1,0:T(8,128)(2,1)S(1)} %get-tuple-element.146), channel_id=1, source_target_pairs={{2,0},{4,6},{3,1},{5,7},{10,8},{12,14},{11,9},{13,15},{18,16},{20,... | collective-permute-start | bytes 884744 | tf_op jit(solution)/shard_map/ppermute | solution.py:564
  180.0 2.4 %collective-permute-start.28 = (bf16[2,48,2048]{2,1,0:T(8,128)(2,1)S(1)}, bf16[2,48,2048]{2,1,0:T(8,128)(2,1)S(1)}, u32[]{:S(2)}, u32[]{:S(2)}) collective-permute-start(bf16[2,48,2048]{2,1,0:T(8,128)(2,1)S(1)} %get-tuple-element.149), channel_id=1, source_target_pairs={{0,1},{1,0},{2,3},{3,2},{4,5},{5,4},{6,7},{7,6},{8,9},{9,8},{10,11... | collective-permute-start | bytes 1179656 | tf_op jit(solution)/shard_map/ppermute | solution.py:575
  181.1 5.6 %collective-permute-start.30 = (bf16[2,96,512]{2,1,0:T(8,128)(2,1)S(1)}, bf16[2,96,512]{2,1,0:T(8,128)(2,1)S(1)}, u32[]{:S(2)}, u32[]{:S(2)}) collective-permute-start(bf16[2,96,512]{2,1,0:T(8,128)(2,1)S(1)} %pad_maximum_fusion.halves), channel_id=1, source_target_pairs={{0,1},{1,0},{2,3},{3,2},{4,5},{5,4},{6,7},{7,6},{8,9},{9,8},{10,11... | collective-permute-start | bytes 589832 | tf_op jit(solution)/shard_map/ppermute | solution.py:575
  183.6 8.0 %collective-permute-start.29 = (bf16[48,2048]{1,0:T(8,128)(2,1)S(1)}, bf16[48,2048]{1,0:T(8,128)(2,1)S(1)}, u32[]{:S(2)}, u32[]{:S(2)}) collective-permute-start(bf16[48,2048]{1,0:T(8,128)(2,1)S(1)} %get-tuple-element.155), channel_id=1, source_target_pairs={{2,0},{4,6},{3,1},{5,7},{10,8},{12,14},{11,9},{13,15},{18,16},{20,... | collective-permute-start | bytes 589832 | tf_op jit(solution)/shard_map/ppermute | solution.py:564
  (23 other events, 353.0 us)
